TPU v7x, 32 devices: a whole 2x2x4 slice. The times are simulated.
32 devices in a mesh: group: 2 (over x), expert: 8 (over z, y), dp: 2 (over core).
Axes of the slice: x: 2, y: 2, z: 4, core: 2. Of those that a mesh axis runs over, the one named last changes fastest.
Arguments:
- tokens: bfloat16 [4096, 2048], P(('group', 'expert', 'dp')), parts along dimension 0, may hold values from -6 to 6
- cotangent: bfloat16 [4096, 2048], P(('group', 'expert', 'dp')), parts along dimension 0, may hold values from -6 to 6
- routes: int32 [4096, 2], P(('group', 'expert', 'dp')), parts along dimension 0, may hold values from 0 to 7, all different within a row; in each aligned block of 128 rows (0 to 127, 128 to 255, ...) at most 64 rows name the same one
- route_weight: float32 [4096, 2], P(('group', 'expert', 'dp')), parts along dimension 0, may hold values from 0.1 to 1
- ratio_advantage: float32 [4096], P(('group', 'expert', 'dp')), parts along dimension 0, may hold values from -4 to 4
- clip_mask: int32 [4096], P(('group', 'expert', 'dp')), parts along dimension 0, may hold values 0 or 1
- shadow_plan: int32 [2], P('group'), parts along dimension 0, may hold values from 0 to 7
- gate_up: bfloat16 [8, 2048, 1536], P('expert'), may hold values from -0.125 to 0.125
- down: bfloat16 [8, 768, 2048], P('expert'), may hold values from -0.21875 to 0.21875
Outputs:
- token_grad: bfloat16 [4096, 2048], P(('group', 'expert', 'dp')), parts along dimension 0
- expert_grad: float32 [16, 2048, 2304], P(('group', 'expert'), 'dp'), parts along dimension 0
- shadow_grad: float32 [4096, 2304], P(('group', 'dp'), 'expert'), parts along dimension 0
There are 2 independent parts, one for each index of `group`. A program takes and returns all parts, laid end to end along the dimension named above; an argument that names none is the same for every part. Nothing has to cross between parts.
Inputs may be any that keep to these rules, and one draw needn't show every extreme that they name: `routes`: within the rows of one device's 128 tokens no expert is named more than 64 times, a bound that some block reaches; a token names 2 different experts.
All inputs are finite; a program needn't handle non-finite values. No bound on the sum of `clip_mask` on one device may be relied on, other than what follows from the above.
Results may differ from a plain program's by a relative error of at most 0.012.
Values may be sent and summed in bfloat16 or wider, within the bound.
No kernel may reach another device: no remote copies, remote signals or barrier semaphores. Data moves between devices by JAX's collectives and lax.ppermute only.
A program may use at most 384 MiB of HBM per device.

v0:
```python
import jax
import jax.numpy as jnp
from jax import lax
from jax.sharding import PartitionSpec as P


def broadcast(block, axis, owner):
    block = jnp.where(lax.axis_index(axis) == owner, block, jnp.zeros_like(block))
    return lax.psum(block, axis)


def expert_pass(rows_in, rows_cot, weights_gu, weights_down):
    hidden_units = weights_down.shape[0]
    projected = jnp.dot(rows_in, weights_gu, preferred_element_type=jnp.float32)
    gate_pre = projected[:, :hidden_units]
    up_pre = projected[:, hidden_units:]
    sigmoid_gate = jax.nn.sigmoid(gate_pre)
    activation = gate_pre * sigmoid_gate
    hidden = (activation * up_pre).astype(jnp.bfloat16)
    hidden_grad = lax.dot_general(
        rows_cot, weights_down, (((1,), (1,)), ((), ())), preferred_element_type=jnp.float32
    )
    gate_grad = hidden_grad * up_pre * sigmoid_gate * (1.0 + gate_pre * (1.0 - sigmoid_gate))
    up_grad = hidden_grad * activation
    gate_up_grad = jnp.concatenate([gate_grad, up_grad], axis=1).astype(jnp.bfloat16)
    input_rows = lax.dot_general(
        gate_up_grad, weights_gu, (((1,), (1,)), ((), ())), preferred_element_type=jnp.float32
    )
    return (input_rows.astype(jnp.bfloat16), gate_up_grad, hidden)


def source_sums(rows_in, rows_cot, gate_up_grad, hidden):
    model_width = rows_in.shape[2]
    span_rows = min(model_width, 256)
    pieces = []
    for offset in range(0, model_width, span_rows):
        part_in = rows_in[:, :, offset : offset + span_rows]
        part_cot = rows_cot[:, :, offset : offset + span_rows]
        input_part = jnp.einsum(
            "scd,scf->sdf", part_in, gate_up_grad, preferred_element_type=jnp.float32
        )
        down_part = jnp.einsum("scd,scf->sdf", part_cot, hidden, preferred_element_type=jnp.float32)
        rounded = lax.optimization_barrier(
            jnp.concatenate([input_part, down_part], axis=2).astype(jnp.bfloat16)
        )
        pieces.append(jnp.sum(rounded.astype(jnp.float32), axis=0))
    return jnp.concatenate(pieces, axis=0)


def pick_rows(slot_table, tokens, slot_cot, fanout, slot_count):
    filled = (slot_table < slot_count)[:, None]
    clamped = jnp.minimum(slot_table, slot_count - 1)
    blank = jnp.zeros((), jnp.bfloat16)
    rows_in = jnp.where(filled, tokens[clamped // fanout], blank)
    rows_cot = jnp.where(filled, slot_cot[clamped], blank)
    return (rows_in, rows_cot)


def on_device(
    tokens, cotangent, routes, route_weight, ratio_advantage, clip_mask, shadow_plan, gate_up, down
):
    experts_all = lax.axis_size("expert")
    tok_rows, model_width = tokens.shape
    fanout = routes.shape[1]
    hidden_units = down.shape[1]
    capacity = 2 * tok_rows * fanout // experts_all
    slot_count = tok_rows * fanout
    buffer_rows = experts_all * capacity
    own_index = lax.axis_index("expert")
    flat_routes = routes.reshape(slot_count)
    onehot = (flat_routes[:, None] == jnp.arange(experts_all, dtype=jnp.int32)[None, :]).astype(
        jnp.int32
    )
    hottest = shadow_plan[0]
    position = jnp.sum(jnp.cumsum(onehot, axis=0) * onehot, axis=1) - 1
    slot_weight = route_weight * ratio_advantage[:, None] * clip_mask[:, None].astype(jnp.float32)
    slot_cot = (slot_weight[:, :, None] * cotangent[:, None, :].astype(jnp.float32)).astype(
        jnp.bfloat16
    )
    slot_cot = slot_cot.reshape(slot_count, model_width)
    slot_ids = jnp.arange(slot_count, dtype=jnp.int32)
    leaves = flat_routes != hottest
    target = jnp.where(leaves, flat_routes * capacity + position, buffer_rows)
    slot_table = (
        jnp.full((buffer_rows + 1,), slot_count, jnp.int32).at[target].set(slot_ids)[:buffer_rows]
    )
    send_in, send_cot = pick_rows(slot_table, tokens, slot_cot, fanout, slot_count)
    recv_in, recv_cot = (
        lax.all_to_all(
            send_in.reshape(experts_all, capacity, model_width),
            "expert",
            split_axis=0,
            concat_axis=0,
            tiled=True,
        ),
        lax.all_to_all(
            send_cot.reshape(experts_all, capacity, model_width),
            "expert",
            split_axis=0,
            concat_axis=0,
            tiled=True,
        ),
    )
    input_rows, gate_up_grad, hidden = expert_pass(
        recv_in.reshape(buffer_rows, model_width),
        recv_cot.reshape(buffer_rows, model_width),
        gate_up[0],
        down[0],
    )
    returned = lax.all_to_all(
        input_rows.reshape(experts_all, capacity, model_width),
        "expert",
        split_axis=0,
        concat_axis=0,
        tiled=True,
    )
    returned = returned.reshape(buffer_rows, model_width)
    grad_blocks = gate_up_grad.reshape(experts_all, capacity, 2 * hidden_units)
    hidden_blocks = hidden.reshape(experts_all, capacity, hidden_units)
    own_part = source_sums(recv_in, recv_cot, grad_blocks, hidden_blocks)
    own_half = lax.psum_scatter(
        own_part.astype(jnp.bfloat16), "dp", scatter_dimension=0, tiled=True
    ).astype(jnp.float32)
    is_hot = own_index == hottest
    expert_grad = jnp.where(is_hot, jnp.zeros_like(own_half), own_half)[None]
    back_rows = returned[jnp.minimum(target, buffer_rows - 1)]
    hot_gate_up, hot_down = (
        broadcast(gate_up, "expert", hottest),
        broadcast(down, "expert", hottest),
    )
    hot_target = jnp.where(leaves, capacity, position)
    hot_table = (
        jnp.full((capacity + 1,), slot_count, jnp.int32).at[hot_target].set(slot_ids)[:capacity]
    )
    hot_in, hot_cot = pick_rows(hot_table, tokens, slot_cot, fanout, slot_count)
    hot_rows, hot_grad_rows, hot_hidden = expert_pass(hot_in, hot_cot, hot_gate_up[0], hot_down[0])
    hot_part = source_sums(hot_in[None], hot_cot[None], hot_grad_rows[None], hot_hidden[None])
    hot_half = lax.psum_scatter(
        hot_part.astype(jnp.bfloat16), "dp", scatter_dimension=0, tiled=True
    )
    shadow_grad = lax.psum_scatter(hot_half, "expert", scatter_dimension=1, tiled=True).astype(
        jnp.float32
    )
    local_rows = hot_rows[jnp.minimum(position, capacity - 1)]
    slot_rows = jnp.where(leaves[:, None], back_rows, local_rows)
    token_grad = jnp.sum(
        slot_rows.reshape(tok_rows, fanout, model_width).astype(jnp.float32), axis=1
    ).astype(jnp.bfloat16)
    return (token_grad, expert_grad, shadow_grad)


def solution(mesh):
    placed = (
        P(("group", "expert", "dp"), None),
        P(("group", "expert", "dp"), None),
        P(("group", "expert", "dp"), None),
        P(("group", "expert", "dp"), None),
        P(("group", "expert", "dp")),
        P(("group", "expert", "dp")),
        P("group"),
        P("expert", None, None),
        P("expert", None, None),
    )
    return jax.shard_map(
        on_device,
        mesh=mesh,
        in_specs=placed,
        out_specs=(
            P(("group", "expert", "dp"), None),
            P(("group", "expert"), "dp", None),
            P(("group", "dp"), "expert"),
        ),
        check_vma=False,
    )
```

profile of v0, /device:TPU:0, one launch (start us, length us, event | category | flops | bytes accessed | tf_op | source)
XLA Modules:
  0.0 732.2 jit_solution(11504395411394458719)
XLA Ops:
  7.9 3.1 select_bitcast_fusion.1
  19.2 2.4 mul.106
  22.0 3.3 gather_fusion.1
  27.0 3.3 gather_fusion
  30.3 4.6 broadcast_select_fusion
  34.9 7.3 all-to-all-start.1
  46.1 312.8 %all-reduce.3.cloned.1.call-done = (bf16[2048,1536]{1,0:T(8,128)(2,1)}, bf16[768,2048]{1,0:T(8,128)(2,1)}) async-done(((bf16[2048,1536]{1,0:T(8,128)(2,1)}, bf16[768,2048]{1,0:T(8,128)(2,1)}), (bf16[2048,1536]{1,0:T(8,128)(2,1)}, bf16[768,2048]{1,0:T(8,128)(2,1)})) %all-reduce.3.cloned.1.call-update) | async-done | bytes 9437200 | tf_op jit(solution)/shard_map/psum | solution.py:9
  358.9 4.2 fusion.46
  379.3 3.6 all-to-all-start
  383.2 10.0 %fusion.2 = f32[512,1536]{1,0:T(8,128)} fusion(bf16[512,2048]{1,0:T(8,128)(2,1)} %bitcast.9, bf16[1,2048,1536]{2,1,0:T(8,128)(2,1)} %param.16), kind=kOutput, calls=%fused_computation.19 | convolution fusion | flops 3221225472 | bytes 11534336 | tf_op jit(solution)/shard_map/dot_general | solution.py:14
  393.2 38.1 %all-to-all-done = bf16[8,64,2048]{2,1,0:T(8,128)(2,1)S(1)} async-done(((bf16[8,64,2048]{2,1,0:T(8,128)(2,1)}), bf16[8,64,2048]{2,1,0:T(8,128)(2,1)S(1)}, u32[]{:S(2)}, u32[]{:S(2)}) %all-to-all-start) | async-done | bytes 2097184 | tf_op jit(solution)/shard_map/all_to_all | solution.py:96
  432.7 5.8 multiply_convert_fusion.3
  438.4 2.0 convolution_convert_fusion.24
  440.4 2.8 convolution_convert_fusion.7
  443.2 4.4 pad_maximum_fusion
  447.5 2.0 convolution_convert_fusion.23
  449.5 2.8 convolution_convert_fusion.6
  452.3 3.9 pad_maximum_fusion.1
  456.2 6.3 reduce.1
  462.5 6.3 reduce.2
  470.8 2.8 convolution_convert_fusion.5
  473.6 4.1 pad_maximum_fusion.2
  477.7 6.3 reduce.3
  484.0 2.0 convolution_convert_fusion.21
  486.0 2.8 convolution_convert_fusion.4
  488.7 3.9 pad_maximum_fusion.3
  492.7 6.4 reduce.4
  501.0 2.8 convolution_convert_fusion.3
  503.7 4.1 pad_maximum_fusion.4
  507.9 6.3 reduce.5
  516.2 2.8 convolution_convert_fusion.2
  518.9 3.9 pad_maximum_fusion.5
  522.8 6.3 reduce.6
  531.1 2.8 convolution_convert_fusion.1
  533.9 4.1 pad_maximum_fusion.6
  538.0 6.4 reduce.7
  546.4 2.8 convolution_convert_fusion
  549.2 3.9 pad_maximum_fusion.7
  553.1 6.4 reduce.8
  568.9 7.0 copy.28
  575.9 9.1 %fusion.6 = bf16[512,2048]{1,0:T(8,128)(2,1)} fusion(bf16[1,2048,1536]{2,1,0:T(8,128)(2,1)} %param.16, bf16[512,768]{1,0:T(8,128)(2,1)S(1)} %get-tuple-element.15, bf16[512,768]{1,0:T(8,128)(2,1)S(1)} %get-tuple-element.14), kind=kOutput, calls=%fused_computation.33 | convolution fusion | flops 3225419776 | bytes 9961472 | tf_op jit(solution)/shard_map/dot_general | solution.py:26
  585.0 4.0 all-to-all-start.2
  589.1 84.2 %all-to-all-done.2 = bf16[8,64,2048]{2,1,0:T(8,128)(2,1)S(1)} async-done(((bf16[8,64,2048]{2,1,0:T(8,128)(2,1)}), bf16[8,64,2048]{2,1,0:T(8,128)(2,1)S(1)}, u32[]{:S(2)}, u32[]{:S(2)}) %all-to-all-start.2) | async-done | bytes 2097184 | tf_op jit(solution)/shard_map/all_to_all | solution.py:110
  673.3 2.3 gather_fusion.2
  677.4 4.8 convolution_convert_fusion.16
  685.3 4.7 fusion.29
  690.0 6.8 select_bitcast_fusion
  696.8 25.7 %reduce-scatter.10.cloned.1.call-done = bf16[288,1024]{1,0:T(8,128)(2,1)} async-done(((bf16[2304,1024]{1,0:T(8,128)(2,1)}), bf16[288,1024]{1,0:T(8,128)(2,1)}) %reduce-scatter.10.cloned.1.call-update) | async-done | bytes 589840
  (144 shorter events, 58.4 us)
Async XLA Ops:
  7.2 14.8 %copy-start = (bf16[128,2048]{1,0:T(8,128)(2,1)S(1)}, bf16[128,2048]{1,0:T(8,128)(2,1)}, u32[]{:S(2)}) copy-start(bf16[128,2048]{1,0:T(8,128)(2,1)} %param.9) | copy-start | bytes 1572868
  7.2 351.8 %all-reduce.3.cloned.1.call-start = ((), (), s32[]{:S(2)}) async-start(), calls=%async_computation.9 | async-start | bytes 18874368 | tf_op jit(solution)/shard_map/psum | solution.py:9
  7.9 3.1 copy-start.11
  13.0 0.7 copy-start.15
  13.0 5.1 copy-start.12
  14.2 0.6 copy-start.13
  18.1 3.5 copy-start.20
  18.1 3.5 copy-start.17
  18.1 3.5 copy-start.18
  34.9 344.4 %all-to-all-start.1 = ((bf16[8,64,2048]{2,1,0:T(8,128)(2,1)}), bf16[8,64,2048]{2,1,0:T(8,128)(2,1)}, u32[]{:S(2)}, u32[]{:S(2)}) async-start(bf16[8,64,2048]{2,1,0:T(8,128)(2,1)} %get-tuple-element.26), calls=%async_computation.1 | async-start | bytes 4194304 | tf_op jit(solution)/shard_map/all_to_all | solution.py:89
  42.2 526.8 %reduce-scatter.8.cloned.1.call-start = ((), (), s32[]{:S(2)}) async-start(), calls=%async_computation.7 | async-start | bytes 14155776 | tf_op jit(solution)/shard_map/reduce_scatter | solution.py:138
  358.9 4.2 copy-start.19
  379.3 52.0 %all-to-all-start = ((bf16[8,64,2048]{2,1,0:T(8,128)(2,1)}), bf16[8,64,2048]{2,1,0:T(8,128)(2,1)S(1)}, u32[]{:S(2)}, u32[]{:S(2)}) async-start(bf16[8,64,2048]{2,1,0:T(8,128)(2,1)} %get-tuple-element.27), calls=%async_computation | async-start | bytes 4194304 | tf_op jit(solution)/shard_map/all_to_all | solution.py:96
  382.9 307.0 %reduce-scatter.6.cloned.1.call-start = ((), (), s32[]{:S(2)}) async-start(), calls=%async_computation.6 | async-start | bytes 14155776 | tf_op jit(solution)/shard_map/reduce_scatter | solution.py:121
  431.3 1.3 copy-start.2
  553.1 6.4 copy-start.3
  559.5 1.7 copy-start.4
  559.5 2.8 copy-start.5
  559.5 3.9 copy-start.6
  561.2 3.3 copy-start.7
  562.3 3.3 copy-start.8
  563.4 3.3 copy-start.9
  564.5 3.3 copy-start.10
  568.9 153.6 %reduce-scatter.10.cloned.1.call-start = ((), (), s32[]{:S(2)}) async-start(), calls=%async_computation.8 | async-start | bytes 5308416
  585.0 4.0 copy-start.16
  585.0 88.3 %all-to-all-start.2 = ((bf16[8,64,2048]{2,1,0:T(8,128)(2,1)}), bf16[8,64,2048]{2,1,0:T(8,128)(2,1)S(1)}, u32[]{:S(2)}, u32[]{:S(2)}) async-start(bf16[8,64,2048]{2,1,0:T(8,128)(2,1)} %bitcast.193), calls=%async_computation.2 | async-start | bytes 4194304 | tf_op jit(solution)/shard_map/all_to_all | solution.py:110
  682.1 3.2 copy-start.14
  690.0 35.3 %copy-start.1 = (bf16[128,2048]{1,0:T(8,128)(2,1)S(1)}, bf16[128,2048]{1,0:T(8,128)(2,1)}, u32[]{:S(2)}) copy-start(bf16[128,2048]{1,0:T(8,128)(2,1)} %param.9) | copy-start | bytes 1572868
Sparse Core Ops, SparseCore 0:
  13.1 345.7 all-reduce.2
  379.4 16.8 reduce-scatter.7
  569.0 16.7 reduce-scatter.5
  589.3 133.1 reduce-scatter.9
where the time goes:
time: 740 us; the launch traced here: 732 us
  waiting for transfers between devices  461 us (62%)
  other arithmetic  109 us (15%)
  matrix products  78.1 us (11%)
  local copies, waits for them, and re-layouts  53.7 us (7%)
  between operations  15.6 us (2%)
  starting transfers between devices  15.4 us (2%)
    psum x1, waiting for transfers between devices, broadcast(): return lax.psum(block, axis)  313 us
    all_to_all x1, waiting for transfers between devices, on_device(): lax.all_to_all(input_rows.reshape(experts_all, capacity, model_width), 'e...  84.2 us
    reduce_sum x8, other arithmetic, source_sums(): pieces.append(jnp.sum(rounded.astype(jnp.float32), axis=0))  50.7 us
    all_to_all x1, waiting for transfers between devices, on_device(): lax.all_to_all(send_cot.reshape(experts_all, capacity, model_width), 'exp...  38.1 us
    concatenate x16, other arithmetic, source_sums(): jnp.concatenate([input_part, down_part], axis=2).astype(jnp.bfloat16)  33 us
    unnamed x60, local copies, waits for them, and re-layouts  28.3 us
    unnamed x5, waiting for transfers between devices  25.8 us
    dot_general x16, matrix products, source_sums(): jnp.einsum('scd,scf->sdf', part_in, gate_up_grad, preferred_element_type=...  25.2 us
  transfers between devices with their start and end apart: 7, of which 4 were waited for; matrix products, arithmetic and copies ran while one was open for 31% of the time, Pallas kernels for 0%

commit v1 on v0

v1 whole, which is shorter than its diff:
```python
import functools

import jax
import jax.numpy as jnp
from jax import lax
from jax.experimental import pallas as pl
from jax.experimental.pallas import tpu as pltpu
from jax.sharding import PartitionSpec as P

BF16 = jnp.bfloat16
F32 = jnp.float32
VMEM_BYTES = 56 * 1024 * 1024


def snaked(experts):
    return experts <= 8


def to_ring(expert, experts):
    if not snaked(experts):
        return expert
    down = experts - 1 - (expert - 1) // 2
    return jnp.where(expert % 2 == 0, expert // 2, down)


def from_ring(place, experts):
    if not snaked(experts):
        return place
    return jnp.where(place < experts // 2, 2 * place, 2 * (experts - 1 - place) + 1)


def ring_order(experts):
    if not snaked(experts):
        return list(range(experts))
    return list(range(0, experts, 2)) + list(range(experts - 1, 0, -2))


def distances(experts):
    half = experts // 2
    return [[0]] + [[-step, step] for step in range(1, half)] + [[half]]


def slot_place(distance, experts):
    half = experts // 2
    near = jnp.where(distance < half, 2 * distance, 2 * (experts - distance) - 1)
    near = jnp.where(distance == half, experts - 1, near)
    return jnp.where(distance == 0, 0, near)


def dot(a, b, dims):
    return lax.dot_general(a, b, ((dims[:1], dims[1:]), ((), ())), preferred_element_type=F32)


def selection(meta, expert, fanout, capacity):
    tokens = meta.shape[1]
    hit = meta[:fanout] == expert.astype(F32)
    named = jnp.sum(jnp.where(hit, 1.0, 0.0), axis=0, keepdims=True)
    weight = jnp.sum(jnp.where(hit, meta[fanout : 2 * fanout], 0.0), axis=0, keepdims=True)
    upto = lax.broadcasted_iota(jnp.int32, (tokens, tokens), 0) <= lax.broadcasted_iota(
        jnp.int32, (tokens, tokens), 1
    )
    upto = jnp.where(upto, 1.0, 0.0).astype(BF16)
    place = dot(jnp.broadcast_to(named, (8, tokens)).astype(BF16), upto, (1, 0))[:1]
    row = lax.broadcasted_iota(jnp.int32, (capacity, tokens), 0).astype(F32) + 1.0
    onehot = jnp.where((row == place) & (named > 0.5), 1.0, 0.0)
    return onehot, weight


def pick(onehot, weight, tokens, cotangent):
    rows_in = dot(onehot.astype(BF16), tokens, (1, 0)).astype(BF16)
    scale = jnp.sum(onehot * weight, axis=1, keepdims=True)
    rows_cot = (scale * dot(onehot.astype(BF16), cotangent, (1, 0))).astype(BF16)
    return rows_in, rows_cot


def step_kernel(steps, experts, fanout, capacity, local, scal, meta, *refs):
    count = len(steps)
    tok, cot = refs[:count], refs[count : 2 * count]
    gate_up, down = refs[2 * count : 2 * count + 2]
    mine, theirs, grads, hot_in, hot_cot = refs[2 * count + 2 : 2 * count + 7]
    back = refs[2 * count + 7 : 3 * count + 7]
    rows_in, rows_cot = refs[3 * count + 7 :]
    own, half, hottest = scal[0], scal[1], scal[2]
    units = down.shape[0]
    width = down.shape[1]
    for at, step in enumerate(steps):
        rows = pl.ds(at * capacity, capacity)
        if local:
            table = meta[0]
        else:
            place = (to_ring(own, experts) + step + experts) % experts
            table = meta[from_ring(place, experts)]
        onehot, weight = selection(table, own, fanout, capacity)
        rows_in[rows, :], rows_cot[rows, :] = pick(onehot, weight, tok[at][...], cot[at][...])
        onehot, weight = selection(table, hottest, fanout, capacity)
        hot_in[rows, :], hot_cot[rows, :] = pick(onehot, weight, tok[at][...], cot[at][...])
    here = pl.ds(pl.multiple_of(half * (width // 2), width // 2), width // 2)
    there = pl.ds(pl.multiple_of((1 - half) * (width // 2), width // 2), width // 2)
    mine[:, : width // 2] = rows_in[:, here]
    mine[:, width // 2 :] = rows_cot[:, here]
    theirs[:, : width // 2] = rows_in[:, there]
    theirs[:, width // 2 :] = rows_cot[:, there]
    projected = dot(rows_in[...], gate_up[...], (1, 0))
    gate_pre, up_pre = projected[:, :units], projected[:, units:]
    hidden_grad = dot(rows_cot[...], down[...], (1, 1))
    sigmoid_gate = jax.nn.sigmoid(gate_pre)
    activation = gate_pre * sigmoid_gate
    gate_grad = hidden_grad * up_pre * sigmoid_gate * (1.0 + gate_pre * (1.0 - sigmoid_gate))
    grads[:, :units] = gate_grad.astype(BF16)
    grads[:, units : 2 * units] = (hidden_grad * activation).astype(BF16)
    grads[:, 2 * units :] = (activation * up_pre).astype(BF16)
    input_rows = dot(grads[:, : 2 * units], gate_up[...], (1, 1)).astype(BF16)
    for at in range(count):
        back[at][...] = input_rows[at * capacity : (at + 1) * capacity]


def run_step(steps, experts, fanout, capacity, local, scal, meta, tok, cot, gate_up, down):
    count, rows = len(steps), len(steps) * capacity
    width, units = down.shape[1], down.shape[0]
    vmem = pl.BlockSpec(memory_space=pltpu.VMEM)
    shapes = [(rows, width), (rows, width), (rows, 3 * units), (rows, width), (rows, width)]
    shapes += [(capacity, width)] * count
    out = pl.pallas_call(
        functools.partial(step_kernel, steps, experts, fanout, capacity, local),
        out_shape=[jax.ShapeDtypeStruct(shape, BF16) for shape in shapes],
        in_specs=[pl.BlockSpec(memory_space=pltpu.SMEM)] + [vmem] * (2 * count + 3),
        out_specs=[vmem] * len(shapes),
        scratch_shapes=[pltpu.VMEM((rows, width), BF16)] * 2,
        compiler_params=pltpu.CompilerParams(vmem_limit_bytes=VMEM_BYTES),
        cost_estimate=pl.CostEstimate(
            flops=2 * 256 * 5 * width * units, bytes_accessed=3 * 2 * width * units, transcendentals=0
        ),
        name="expert_step",
    )(scal, meta, *tok, *cot, gate_up, down)
    return out[:5], out[5:]


def combine_kernel(experts, fanout, capacity, scal, meta, *refs):
    rows, out = refs[:experts], refs[experts]
    place = to_ring(scal[0], experts)
    total = jnp.zeros(out.shape, F32)
    for step in range(experts):
        expert = from_ring((place - step + experts) % experts, experts)
        onehot, _ = selection(meta[0], expert, fanout, capacity)
        total += dot(onehot.astype(BF16), rows[step][...], (0, 0))
    out[...] = total.astype(BF16)


def combine(experts, fanout, capacity, scal, meta, rows):
    vmem = pl.BlockSpec(memory_space=pltpu.VMEM)
    tokens, width = meta.shape[2], rows[0].shape[1]
    return pl.pallas_call(
        functools.partial(combine_kernel, experts, fanout, capacity),
        out_shape=jax.ShapeDtypeStruct((tokens, width), BF16),
        in_specs=[pl.BlockSpec(memory_space=pltpu.SMEM)] + [vmem] * (experts + 1),
        out_specs=vmem,
        compiler_params=pltpu.CompilerParams(vmem_limit_bytes=VMEM_BYTES),
        cost_estimate=pl.CostEstimate(
            flops=2 * experts * capacity * tokens * width, bytes_accessed=2 * experts * capacity * width, transcendentals=0
        ),
        name="token_sum",
    )(scal, meta, *rows)


def gradient_kernel(units, scal, *refs):
    count = (len(refs) - 1) // 3
    ins, cots, grads = refs[:count], refs[count : 2 * count], refs[2 * count : 3 * count]
    out = refs[3 * count]
    keep = scal[0] != scal[2]
    left = jnp.concatenate([ref[...] for ref in ins], axis=0)
    right = jnp.concatenate([ref[:, : 2 * units] for ref in grads], axis=0)
    out[0, :, : 2 * units] = jnp.where(keep, dot(left, right, (0, 0)), 0.0)
    left = jnp.concatenate([ref[...] for ref in cots], axis=0)
    right = jnp.concatenate([ref[:, 2 * units :] for ref in grads], axis=0)
    out[0, :, 2 * units :] = jnp.where(keep, dot(left, right, (0, 0)), 0.0)


def expert_gradient(scal, rows, grads):
    width, columns = rows[0].shape[1], grads[0].shape[1]
    tile = 256
    tiles = width // 2 // tile
    total = sum(part.shape[0] for part in rows)
    in_specs = [pl.BlockSpec(memory_space=pltpu.SMEM)]
    in_specs += [pl.BlockSpec((part.shape[0], tile), lambda i: (0, i)) for part in rows]
    in_specs += [pl.BlockSpec((part.shape[0], tile), lambda i: (0, i + tiles)) for part in rows]
    in_specs += [pl.BlockSpec(part.shape, lambda i: (0, 0)) for part in grads]
    return pl.pallas_call(
        functools.partial(gradient_kernel, columns // 3),
        grid=(tiles,),
        out_shape=jax.ShapeDtypeStruct((1, width // 2, columns), F32),
        in_specs=in_specs,
        out_specs=pl.BlockSpec((1, tile, columns), lambda i: (0, i, 0)),
        compiler_params=pltpu.CompilerParams(vmem_limit_bytes=VMEM_BYTES),
        cost_estimate=pl.CostEstimate(
            flops=width * columns * total, bytes_accessed=3 * width * columns, transcendentals=0
        ),
        name="expert_gradient",
    )(scal, *rows, *rows, *grads)


def turn_kernel(*refs):
    out, at = refs[-1], 0
    turned = jnp.concatenate([ref[...] for ref in refs[:-1]], axis=0)
    out[...] = turned.T


def turned_grads(grads):
    rows, columns = sum(part.shape[0] for part in grads), grads[0].shape[1]
    vmem = pl.BlockSpec(memory_space=pltpu.VMEM)
    return pl.pallas_call(
        turn_kernel,
        out_shape=jax.ShapeDtypeStruct((columns, rows), BF16),
        in_specs=[vmem] * len(grads),
        out_specs=vmem,
        compiler_params=pltpu.CompilerParams(vmem_limit_bytes=VMEM_BYTES),
        cost_estimate=pl.CostEstimate(flops=0, bytes_accessed=4 * rows * columns, transcendentals=0),
        name="turned_grads",
    )(*grads)


def shadow_kernel(plan, experts, capacity, scal, columns, *refs):
    count = len(plan)
    ins, cots = refs[:count], refs[count : 2 * count]
    mine, theirs, rows_in, rows_cot, total = refs[2 * count :]
    own, half, hottest = scal[0], scal[1], scal[2]
    shift = to_ring(own, experts) - to_ring(hottest, experts)
    for steps, part_in, part_cot in zip(plan, ins, cots):
        for at, step in enumerate(steps):
            place = slot_place((shift + step + 2 * experts) % experts, experts)
            there = pl.ds(pl.multiple_of(place * capacity, capacity), capacity)
            rows_in[there, :] = part_in[at * capacity : (at + 1) * capacity, :]
            rows_cot[there, :] = part_cot[at * capacity : (at + 1) * capacity, :]
    taken = columns.shape[0]
    column = own * taken + lax.broadcasted_iota(jnp.int32, columns.shape, 0)
    gate_part = column < taken * experts * 2 // 3
    blank = jnp.zeros((), BF16)
    total[...] = dot(jnp.where(gate_part, columns[...], blank), rows_in[...], (1, 0)) + dot(
        jnp.where(gate_part, blank, columns[...]), rows_cot[...], (1, 0)
    )
    width = total.shape[1] // 2
    mine[...] = total[:, pl.ds(pl.multiple_of(half * width, width), width)]
    theirs[...] = total[:, pl.ds(pl.multiple_of((1 - half) * width, width), width)].astype(BF16)


def shadow_gradient(plan, experts, capacity, scal, columns, ins, cots):
    vmem = pl.BlockSpec(memory_space=pltpu.VMEM)
    taken, rows = columns.shape
    width = ins[0].shape[1]
    return pl.pallas_call(
        functools.partial(shadow_kernel, plan, experts, capacity),
        out_shape=[
            jax.ShapeDtypeStruct((taken, width // 2), F32),
            jax.ShapeDtypeStruct((taken, width // 2), BF16),
        ],
        in_specs=[pl.BlockSpec(memory_space=pltpu.SMEM)] + [vmem] * (2 * len(ins) + 1),
        out_specs=[vmem] * 2,
        scratch_shapes=[pltpu.VMEM((rows, width), BF16)] * 2 + [pltpu.VMEM((taken, width), F32)],
        compiler_params=pltpu.CompilerParams(vmem_limit_bytes=VMEM_BYTES),
        cost_estimate=pl.CostEstimate(
            flops=4 * taken * rows * width, bytes_accessed=4 * rows * width, transcendentals=0
        ),
        name="shadow_gradient",
    )(scal, columns, *ins, *cots)


def on_device(
    tokens, cotangent, routes, route_weight, ratio_advantage, clip_mask, shadow_plan, gate_up, down
):
    experts = lax.axis_size("expert")
    tok_rows = tokens.shape[0]
    fanout = routes.shape[1]
    units = down.shape[1]
    capacity = 2 * tok_rows * fanout // experts
    gate_up, down = gate_up[0], down[0]
    order = ring_order(experts)
    half = experts // 2

    def shift(block, step):
        pairs = [(order[i], order[(i + step) % experts]) for i in range(experts)]
        return lax.ppermute(block, "expert", pairs)

    def swap(block):
        return lax.ppermute(block, "dp", [(0, 1), (1, 0)])

    own = lax.axis_index("expert")
    hottest = shadow_plan[0]
    scal = jnp.stack([own, lax.axis_index("dp"), hottest]).astype(jnp.int32)
    slot_weight = route_weight * ratio_advantage[:, None] * clip_mask[:, None].astype(F32)
    meta = jnp.concatenate([routes.astype(F32), slot_weight], axis=1).T
    meta = jnp.pad(meta, ((0, -meta.shape[0] % 8), (0, 0)))[None]
    meta_all = lax.all_gather(meta, "expert", axis=0, tiled=True)

    plan = distances(experts)
    rows_mine, rows_other, grads_mine, grads_other, hot_in, hot_cot = [], [], [], [], [], []
    returned = {}

    def work(steps, local, table, tok, cot):
        (mine, theirs, grads, hot_rows, hot_cots), back = run_step(
            steps, experts, fanout, capacity, local, scal, table, tok, cot, gate_up, down
        )
        for step, rows in zip(steps, back):
            returned[step % experts] = shift(rows, step) if step else rows
        rows_mine.append(mine)
        rows_other.append(swap(theirs))
        grads_mine.append(grads)
        grads_other.append(swap(grads))
        hot_in.append(hot_rows)
        hot_cot.append(hot_cots)

    up, below = (tokens, cotangent), (tokens, cotangent)
    held = [(tokens,), (cotangent,)]
    for number, steps in enumerate(plan):
        if number + 1 < half:
            next_up = tuple(shift(block, 1) for block in up)
            next_below = tuple(shift(block, -1) for block in below)
            following = [(next_up[0], next_below[0]), (next_up[1], next_below[1])]
        elif number + 1 == half:
            following = [(shift(up[0], 1),), (shift(below[1], -1),)]
        work(steps, number == 0, meta if number == 0 else meta_all, *held)
        if number + 1 < half:
            up, below = next_up, next_below
        held = following

    expert_grad = expert_gradient(scal, rows_mine + rows_other, grads_mine + grads_other)

    turned = turned_grads(grads_mine)
    taken = 3 * units // experts
    ring_hot = to_ring(hottest, experts)
    is_hot = own == hottest

    def chunk(distance):
        owner = from_ring((ring_hot + distance + experts) % experts, experts)
        return lax.dynamic_slice_in_dim(turned, owner * taken, taken, axis=0)

    ahead, behind = None, None
    for number in range(half):
        mine = chunk(half - number)
        ahead = shift(mine if ahead is None else jnp.where(is_hot, mine, ahead), 1)
        if number < half - 1:
            mine = chunk(number + 1 - half)
            behind = shift(mine if behind is None else jnp.where(is_hot, mine, behind), -1)
    away = (to_ring(own, experts) - ring_hot + experts) % experts
    columns = jnp.where(away == 0, chunk(0), jnp.where(away <= half, ahead, behind))
    shadow_mine, shadow_theirs = shadow_gradient(
        plan, experts, capacity, scal, columns, hot_in, hot_cot
    )
    shadow_grad = (shadow_mine + swap(shadow_theirs).astype(F32)).T

    token_grad = combine(experts, fanout, capacity, scal, meta, [returned[d] for d in range(experts)])
    return (token_grad, expert_grad, shadow_grad)


def solution(mesh):
    placed = (
        P(("group", "expert", "dp"), None),
        P(("group", "expert", "dp"), None),
        P(("group", "expert", "dp"), None),
        P(("group", "expert", "dp"), None),
        P(("group", "expert", "dp")),
        P(("group", "expert", "dp")),
        P("group"),
        P("expert", None, None),
        P("expert", None, None),
    )
    return jax.shard_map(
        on_device,
        mesh=mesh,
        in_specs=placed,
        out_specs=(
            P(("group", "expert", "dp"), None),
            P(("group", "expert"), "dp", None),
            P(("group", "dp"), "expert"),
        ),
        check_vma=False,
    )
```

time: 740 us -> 259 us (0.35)
  waiting for transfers between devices: 461 us -> 85.6 us
  other arithmetic: 109 us -> 14.9 us
  matrix products: 78.1 us -> 0 us
  Pallas kernels: 0 us -> 76.7 us
  local copies, waits for them, and re-layouts: 53.7 us -> 8.15 us
  blocking collectives: 0 us -> 37.4 us
  starting transfers between devices: 15.4 us -> 33.6 us
  between operations: 15.6 us -> 1.61 us
    psum x1 -> x0, waiting for transfers between devices: 313 us -> none  [broadcast(): return lax.psum(block, axis)]
    all_to_all x3 -> x0, waiting for transfers between devices: 122 us -> none  [the longest x1 84.2 us: on_device(): lax.all_to_all(input_rows.reshape(experts_all, capacity, model_width), 'e...]
    ppermute x0 -> x39, waiting for transfers between devices: none -> 85.6 us  [the longest x28 84.4 us: shift(): return lax.ppermute(block, 'expert', pairs)]
    dot_general x38 -> x0, matrix products: 78.1 us -> none  [the longest x16 25.2 us: source_sums(): jnp.einsum('scd,scf->sdf', part_in, gate_up_grad, preferred_element_type=...]
    pallas_call x0 -> x9, Pallas kernels: none -> 76.7 us  [the longest x5 52.3 us: run_step(): pl.pallas_call(functools.partial(step_kernel, steps, experts, fanout, cap...]
    reduce_sum x10 -> x0, other arithmetic: 55.5 us -> none  [the longest x8 50.7 us: source_sums(): pieces.append(jnp.sum(rounded.astype(jnp.float32), axis=0))]
    all_gather x0 -> x1, blocking collectives: none -> 37.4 us  [on_device(): meta_all = lax.all_gather(meta, 'expert', axis=0, tiled=True)]
    ppermute x0 -> x39, starting transfers between devices: none -> 33.6 us  [the longest x28 32 us: shift(): return lax.ppermute(block, 'expert', pairs)]
  transfers between devices with their start and end apart: 7 -> 39, of which waited for: 4 -> 15; matrix products, arithmetic and copies ran while one was open for 31% -> 3% of each run, Pallas kernels for 0% -> 24%
where the time goes in v1:
time: 259 us; the launch traced here: 258 us
  waiting for transfers between devices  85.6 us (33%)
  Pallas kernels  76.7 us (30%)
  blocking collectives  37.4 us (14%)
  starting transfers between devices  33.6 us (13%)
  other arithmetic  14.9 us (6%)
  local copies, waits for them, and re-layouts  8.15 us (3%)
    ppermute x28, waiting for transfers between devices, shift(): return lax.ppermute(block, 'expert', pairs)  84.4 us
    pallas_call x5, Pallas kernels, run_step(): pl.pallas_call(functools.partial(step_kernel, steps, experts, fanout, cap...  52.3 us
    all_gather x1, blocking collectives, on_device(): meta_all = lax.all_gather(meta, 'expert', axis=0, tiled=True)  37.4 us
    ppermute x28, starting transfers between devices, shift(): return lax.ppermute(block, 'expert', pairs)  32 us
    pallas_call x1, Pallas kernels, expert_gradient(): pl.pallas_call(functools.partial(gradient_kernel, columns // 3), grid=(ti...  10.8 us
    unnamed x46, local copies, waits for them, and re-layouts  5.72 us
    select_n x3, other arithmetic, on_device(): ahead = shift(mine if ahead is None else jnp.where(is_hot, mine, ahead), 1)  5.25 us
  transfers between devices with their start and end apart: 39, of which 15 were waited for; matrix products, arithmetic and copies ran while one was open for 3% of the time, Pallas kernels for 24%

profile of v1, /device:TPU:0, one launch (start us, length us, event | category | flops | bytes accessed | tf_op | source)
XLA Modules:
  0.0 257.8 jit_solution(17325018476202790964)
XLA Ops:
  0.6 3.1 %collective-permute-start = (bf16[128,2048]{1,0:T(8,128)(2,1)}, bf16[128,2048]{1,0:T(8,128)(2,1)S(1)}, u32[]{:S(2)}, u32[]{:S(2)}) collective-permute-start(bf16[128,2048]{1,0:T(8,128)(2,1)} %refs_0_.1), channel_id=1, source_target_pairs={{0,4},{4,8},{8,12},{12,14},{14,10},{10,6},{6,2},{2,0},{1,5},{5,9},... | collective-permute-start | bytes 1572872 | tf_op jit(solution)/shard_map/ppermute | solution.py:280
  3.7 2.0 collective-permute-start.1
  7.8 8.9 %collective-permute-done.refs_0_ = bf16[128,2048]{1,0:T(8,128)(2,1)S(1)} collective-permute-done((bf16[128,2048]{1,0:T(8,128)(2,1)}, bf16[128,2048]{1,0:T(8,128)(2,1)S(1)}, u32[]{:S(2)}, u32[]{:S(2)}) %collective-permute-start) | collective-permute-done | bytes 524320 | tf_op jit(solution)/shard_map/ppermute | solution.py:280
  16.6 2.1 collective-permute-start.5
  19.5 10.5 %collective-permute-done.1.refs_1_ = bf16[128,2048]{1,0:T(8,128)(2,1)S(1)} collective-permute-done((bf16[128,2048]{1,0:T(8,128)(2,1)}, bf16[128,2048]{1,0:T(8,128)(2,1)S(1)}, u32[]{:S(2)}, u32[]{:S(2)}) %collective-permute-start.1) | collective-permute-done | bytes 524320 | tf_op jit(solution)/shard_map/ppermute | solution.py:280
  30.0 2.0 collective-permute-start.7
  33.3 5.8 %collective-permute-done.5.refs_0_ = bf16[128,2048]{1,0:T(8,128)(2,1)S(1)} collective-permute-done((bf16[128,2048]{1,0:T(8,128)(2,1)S(1)}, bf16[128,2048]{1,0:T(8,128)(2,1)S(1)}, u32[]{:S(2)}, u32[]{:S(2)}) %collective-permute-start.5) | collective-permute-done | bytes 524320 | tf_op jit(solution)/shard_map/ppermute | solution.py:280
  39.1 2.1 collective-permute-start.10
  41.2 10.0 %expert_step.5 = (bf16[64,2048]{1,0:T(8,128)(2,1)}, bf16[64,2048]{1,0:T(8,128)(2,1)}, bf16[64,2304]{1,0:T(8,128)(2,1)}, bf16[64,2048]{1,0:T(8,128)(2,1)}, bf16[6...) custom-call(s32[3]{0:T(128)} %pad_add_fusion.scal, f32[1,8,128]{2,1,0:T(8,128)} %get-tuple-element.76.meta, ...), custom_call_target="tpu_custom_call" | custom-call | flops 4026531840 | bytes 9437184 | tf_op jit(solution)/shard_map/expert_step/pallas_call | solution.py:123
  51.4 37.4 %all-gather = f32[64,128]{1,0:T(8,128)} all-gather(f32[8,128]{1,0:T(8,128)S(1)} %get-tuple-element.75), channel_id=2, replica_groups=mesh['group'=2,'expert'=8,'dp'=2] {'expert'}, dimensions={0}, use_global_device_ids=true | all-gather | bytes 36864 | tf_op jit(solution)/shard_map/all_gather | solution.py:291
  88.8 2.0 collective-permute-start.12
  90.8 10.8 %expert_step.6 = (bf16[128,2048]{1,0:T(8,128)(2,1)}, bf16[128,2048]{1,0:T(8,128)(2,1)}, bf16[128,2304]{1,0:T(8,128)(2,1)}, bf16[128,2048]{1,0:T(8,128)(2,1)}, bf...) custom-call(s32[3]{0:T(128)} %pad_add_fusion.scal, f32[8,8,128]{2,1,0:T(8,128)} %bitcast.18, ...), custom_call_target="tpu_custom_call" | custom-call | flops 4026531840 | bytes 9437184 | tf_op jit(solution)/shard_map/expert_step/pallas_call | solution.py:123
  101.6 2.0 collective-permute-start.16
  103.6 10.8 %expert_step.7 = (bf16[128,2048]{1,0:T(8,128)(2,1)}, bf16[128,2048]{1,0:T(8,128)(2,1)}, bf16[128,2304]{1,0:T(8,128)(2,1)}, bf16[128,2048]{1,0:T(8,128)(2,1)}, bf...) custom-call(s32[3]{0:T(128)} %pad_add_fusion.scal, f32[8,8,128]{2,1,0:T(8,128)} %bitcast.19, ...), custom_call_target="tpu_custom_call" | custom-call | flops 4026531840 | bytes 9437184 | tf_op jit(solution)/shard_map/expert_step/pallas_call | solution.py:123
  115.2 0.8 copy-done.20
  116.0 10.8 %expert_step.8 = (bf16[128,2048]{1,0:T(8,128)(2,1)}, bf16[128,2048]{1,0:T(8,128)(2,1)}, bf16[128,2304]{1,0:T(8,128)(2,1)}, bf16[128,2048]{1,0:T(8,128)(2,1)}, bf...) custom-call(s32[3]{0:T(128)} %pad_add_fusion.scal, f32[8,8,128]{2,1,0:T(8,128)} %bitcast.20, ...), custom_call_target="tpu_custom_call" | custom-call | flops 4026531840 | bytes 9437184 | tf_op jit(solution)/shard_map/expert_step/pallas_call | solution.py:123
  128.4 9.9 %expert_step.9 = (bf16[64,2048]{1,0:T(8,128)(2,1)}, bf16[64,2048]{1,0:T(8,128)(2,1)}, bf16[64,2304]{1,0:T(8,128)(2,1)}, bf16[64,2048]{1,0:T(8,128)(2,1)}, bf16[6...) custom-call(s32[3]{0:T(128)} %pad_add_fusion.scal, f32[8,8,128]{2,1,0:T(8,128)} %bitcast.21, bf16[128,2048]{1,0:T(8,128)(2,1)} %copy-done.21, ...), custom_call_target="tpu_custom_call" | custom-call | flops 4026531840 | bytes 9437184 | tf_op jit(solution)/shard_map/expert_step/pallas_call | solution.py:123
  138.3 3.6 %turned_grads.1 = bf16[2304,512]{1,0:T(8,128)(2,1)} custom-call(bf16[64,2304]{1,0:T(8,128)(2,1)} %get-tuple-element.56.refs_20_.refs_0_, bf16[128,2304]{1,0:T(8,128)(2,1)} %get-tuple-element.57.refs_21_.refs_1_, bf16[128,2304]{1,0:T(8,128)(2,1)} %get-tuple-element.58.refs_22_.refs_2_, bf16[128,2304]{1,0:T(8,128)(2,1)} %get-tuple-element.59.refs_23_.refs_3_, ...), custom_call_target="tpu_custom_call" | custom-call | bytes 4718592 | tf_op jit(solution)/shard_map/turned_grads/pallas_call | solution.py:210
  141.9 1.8 constant_dynamic-slice_fusion
  143.8 9.0 %collective-permute-done.35 = bf16[288,512]{1,0:T(8,128)(2,1)} collective-permute-done((bf16[288,512]{1,0:T(8,128)(2,1)}, bf16[288,512]{1,0:T(8,128)(2,1)}, u32[]{:S(2)}, u32[]{:S(2)}) %collective-permute-start.35) | collective-permute-done | bytes 294944 | tf_op jit(solution)/shard_map/ppermute | solution.py:280
  152.8 1.8 dynamic-slice_select_fusion
  154.9 6.8 %collective-permute-done.36 = bf16[288,512]{1,0:T(8,128)(2,1)} collective-permute-done((bf16[288,512]{1,0:T(8,128)(2,1)}, bf16[288,512]{1,0:T(8,128)(2,1)}, u32[]{:S(2)}, u32[]{:S(2)}) %collective-permute-start.36) | collective-permute-done | bytes 294944 | tf_op jit(solution)/shard_map/ppermute | solution.py:280
  161.7 2.0 dynamic-slice_select_fusion.1
  164.3 6.7 %collective-permute-done.31 = bf16[288,512]{1,0:T(8,128)(2,1)} collective-permute-done((bf16[288,512]{1,0:T(8,128)(2,1)}, bf16[288,512]{1,0:T(8,128)(2,1)}, u32[]{:S(2)}, u32[]{:S(2)}) %collective-permute-start.31) | collective-permute-done | bytes 294944 | tf_op jit(solution)/shard_map/ppermute | solution.py:280
  171.0 1.8 dynamic-slice_select_fusion.2
  172.7 0.8 collective-permute-start.32
  174.6 1.2 collective-permute-done.21.refs_5_.refs_15_
  176.3 4.3 %collective-permute-done.32 = bf16[288,512]{1,0:T(8,128)(2,1)} collective-permute-done((bf16[288,512]{1,0:T(8,128)(2,1)}, bf16[288,512]{1,0:T(8,128)(2,1)}, u32[]{:S(2)}, u32[]{:S(2)}) %collective-permute-start.32) | collective-permute-done | bytes 294944 | tf_op jit(solution)/shard_map/ppermute | solution.py:280
  180.7 1.8 dynamic-slice_select_fusion.3
  182.4 2.0 collective-permute-start.33
  184.4 1.7 collective-permute-done.4.refs_1_
  186.2 1.1 collective-permute-done.20.refs_7_
  188.0 2.3 collective-permute-start.19
  190.3 1.5 collective-permute-done.33
  191.9 1.7 dynamic-slice_select_fusion.4
  193.7 4.9 %collective-permute-done.9.refs_2_ = bf16[64,2048]{1,0:T(8,128)(2,1)} collective-permute-done((bf16[64,2048]{1,0:T(8,128)(2,1)}, bf16[64,2048]{1,0:T(8,128)(2,1)}, u32[]{:S(2)}, u32[]{:S(2)}) %collective-permute-start.9) | collective-permute-done | bytes 262176 | tf_op jit(solution)/shard_map/ppermute | solution.py:280
  198.6 3.3 %collective-permute-start.34 = (bf16[288,512]{1,0:T(8,128)(2,1)}, bf16[288,512]{1,0:T(8,128)(2,1)}, u32[]{:S(2)}, u32[]{:S(2)}) collective-permute-start(bf16[288,512]{1,0:T(8,128)(2,1)} %dynamic-slice_select_fusion.4), channel_id=1, source_target_pairs={{0,4},{4,8},{8,12},{12,14},{14,10},{10,6},{6,2},{2,0},{1,5},{5,9},... | collective-permute-start | bytes 884744 | tf_op jit(solution)/shard_map/ppermute | solution.py:280
  201.9 1.9 collective-permute-done.19.refs_6_
  203.8 1.8 collective-permute-start.14
  205.7 2.0 collective-permute-start.18
  207.6 18.9 %collective-permute-done.14.refs_3_ = bf16[64,2048]{1,0:T(8,128)(2,1)S(1)} collective-permute-done((bf16[64,2048]{1,0:T(8,128)(2,1)}, bf16[64,2048]{1,0:T(8,128)(2,1)S(1)}, u32[]{:S(2)}, u32[]{:S(2)}) %collective-permute-start.14) | collective-permute-done | bytes 262176 | tf_op jit(solution)/shard_map/ppermute | solution.py:280
  227.8 2.1 collective-permute-start.17
  229.9 1.8 select_select_fusion.columns
  231.7 5.1 %shadow_gradient.1 = (f32[288,1024]{1,0:T(8,128)}, bf16[288,1024]{1,0:T(8,128)(2,1)}) custom-call(s32[3]{0:T(128)} %pad_add_fusion.scal, bf16[288,512]{1,0:T(8,128)(2,1)} %select_select_fusion.columns, bf16[64,2048]{1,0:T(8,128)(2,1)} %get-tuple-element.61.refs_0_, bf16[128,2048]{1,0:T(8,128)(2,1)} %get-tuple-element.62.refs_1_, ...), custom_call_target="tpu_custom_call" | custom-call | flops 1207959552 | bytes 4194304 | tf_op jit(solution)/shard_map/shadow_gradient/pallas_call | solution.py:249
  236.8 2.2 collective-permute-done.17.refs_4_
  239.8 4.8 %token_sum.1 = bf16[128,2048]{1,0:T(8,128)(2,1)} custom-call(s32[3]{0:T(128)} %pad_add_fusion.scal, f32[1,8,128]{2,1,0:T(8,128)} %get-tuple-element.76.meta, bf16[64,2048]{1,0:T(8,128)(2,1)} %get-tuple-element.38.refs_0_, bf16[64,2048]{1,0:T(8,128)(2,1)} %copy-done.8, bf16[64,2048]{1,0:T(8,128)(2,1)} %collective-permute-done.9.refs_2_, ...), custom_call_target="tpu_custom_call" | custom-call | flops 268435456 | bytes 2097152 | tf_op jit(solution)/shard_map/token_sum/pallas_call | solution.py:152
  245.8 10.8 %expert_gradient.1 = f32[1,1024,2304]{2,1,0:T(8,128)} custom-call(s32[3]{0:T(128)} %pad_add_fusion.scal, bf16[64,2048]{1,0:T(8,128)(2,1)} %get-tuple-element.46.refs_0_.refs_10_, bf16[128,2048]{1,0:T(8,128)(2,1)} %get-tuple-element.47.refs_1_.refs_11_, bf16[128,2048]{1,0:T(8,128)(2,1)} %get-tuple-element.48.refs_2_.refs_12_, ...), custom_call_target="tpu_custom_call" | custom-call | flops 4831838208 | bytes 14155776 | tf_op jit(solution)/shard_map/expert_gradient/pallas_call | solution.py:187
  256.6 1.2 add_bitcast_fusion
  (100 shorter events, 12.2 us)
Async XLA Ops:
  0.6 16.0 %collective-permute-start = (bf16[128,2048]{1,0:T(8,128)(2,1)}, bf16[128,2048]{1,0:T(8,128)(2,1)S(1)}, u32[]{:S(2)}, u32[]{:S(2)}) collective-permute-start(bf16[128,2048]{1,0:T(8,128)(2,1)} %refs_0_.1), channel_id=1, source_target_pairs={{0,4},{4,8},{8,12},{12,14},{14,10},{10,6},{6,2},{2,0},{1,5},{5,9},... | collective-permute-start | bytes 1572872 | tf_op jit(solution)/shard_map/ppermute | solution.py:280
  3.7 15.1 %collective-permute-start.3 = (bf16[128,2048]{1,0:T(8,128)(2,1)}, bf16[128,2048]{1,0:T(8,128)(2,1)S(1)}, u32[]{:S(2)}, u32[]{:S(2)}) collective-permute-start(bf16[128,2048]{1,0:T(8,128)(2,1)} %refs_1_.1), channel_id=1, source_target_pairs={{0,2},{4,0},{8,4},{12,8},{14,12},{10,14},{6,10},{2,6},{1,3},{5,1},... | collective-permute-start | bytes 1572872 | tf_op jit(solution)/shard_map/ppermute | solution.py:280
  3.7 26.3 %collective-permute-start.1 = (bf16[128,2048]{1,0:T(8,128)(2,1)}, bf16[128,2048]{1,0:T(8,128)(2,1)S(1)}, u32[]{:S(2)}, u32[]{:S(2)}) collective-permute-start(bf16[128,2048]{1,0:T(8,128)(2,1)} %refs_0_.1), channel_id=1, source_target_pairs={{0,2},{4,0},{8,4},{12,8},{14,12},{10,14},{6,10},{2,6},{1,3},{5,1},... | collective-permute-start | bytes 1572872 | tf_op jit(solution)/shard_map/ppermute | solution.py:280
  5.7 24.3 %collective-permute-start.2 = (bf16[128,2048]{1,0:T(8,128)(2,1)}, bf16[128,2048]{1,0:T(8,128)(2,1)S(1)}, u32[]{:S(2)}, u32[]{:S(2)}) collective-permute-start(bf16[128,2048]{1,0:T(8,128)(2,1)} %refs_1_.1), channel_id=1, source_target_pairs={{0,4},{4,8},{8,12},{12,14},{14,10},{10,6},{6,2},{2,0},{1,5},{5,9},... | collective-permute-start | bytes 1572872 | tf_op jit(solution)/shard_map/ppermute | solution.py:280
  16.6 34.7 %copy-start.13 = (bf16[128,2048]{1,0:T(8,128)(2,1)}, bf16[128,2048]{1,0:T(8,128)(2,1)S(1)}, u32[]{:S(2)}) copy-start(bf16[128,2048]{1,0:T(8,128)(2,1)S(1)} %collective-permute-done.refs_0_) | copy-start | bytes 1572868
  16.6 22.5 %collective-permute-start.5 = (bf16[128,2048]{1,0:T(8,128)(2,1)S(1)}, bf16[128,2048]{1,0:T(8,128)(2,1)S(1)}, u32[]{:S(2)}, u32[]{:S(2)}) collective-permute-start(bf16[128,2048]{1,0:T(8,128)(2,1)S(1)} %collective-permute-done.refs_0_), channel_id=1, source_target_pairs={{0,4},{4,8},{8,12},{12,14},{14,10},{10,6},{6,2},{2,0},{1,5},{5,9},... | collective-permute-start | bytes 1572872 | tf_op jit(solution)/shard_map/ppermute | solution.py:280
  18.8 32.5 %copy-start.14 = (bf16[128,2048]{1,0:T(8,128)(2,1)}, bf16[128,2048]{1,0:T(8,128)(2,1)S(1)}, u32[]{:S(2)}) copy-start(bf16[128,2048]{1,0:T(8,128)(2,1)S(1)} %collective-permute-done.3.refs_3_) | copy-start | bytes 1572868
  18.8 22.5 %collective-permute-start.8 = (bf16[128,2048]{1,0:T(8,128)(2,1)S(1)}, bf16[128,2048]{1,0:T(8,128)(2,1)S(1)}, u32[]{:S(2)}, u32[]{:S(2)}) collective-permute-start(bf16[128,2048]{1,0:T(8,128)(2,1)S(1)} %collective-permute-done.3.refs_3_), channel_id=1, source_target_pairs={{0,2},{4,0},{8,4},{12,8},{14,12},{10,14},{6,10},{2,6},{1,3},{5,1},... | collective-permute-start | bytes 1572872 | tf_op jit(solution)/shard_map/ppermute | solution.py:280
  30.0 21.3 %copy-start.15 = (bf16[128,2048]{1,0:T(8,128)(2,1)}, bf16[128,2048]{1,0:T(8,128)(2,1)S(1)}, u32[]{:S(2)}) copy-start(bf16[128,2048]{1,0:T(8,128)(2,1)S(1)} %collective-permute-done.1.refs_1_) | copy-start | bytes 1572868
  30.0 58.8 %collective-permute-start.6 = (bf16[128,2048]{1,0:T(8,128)(2,1)S(1)}, bf16[128,2048]{1,0:T(8,128)(2,1)}, u32[]{:S(2)}, u32[]{:S(2)}) collective-permute-start(bf16[128,2048]{1,0:T(8,128)(2,1)S(1)} %collective-permute-done.1.refs_1_), channel_id=1, source_target_pairs={{0,2},{4,0},{8,4},{12,8},{14,12},{10,14},{6,10},{2,6},{1,3},{5,1},... | collective-permute-start | bytes 1572872 | tf_op jit(solution)/shard_map/ppermute | solution.py:280
  30.0 21.3 %copy-start.17 = (bf16[128,2048]{1,0:T(8,128)(2,1)}, bf16[128,2048]{1,0:T(8,128)(2,1)S(1)}, u32[]{:S(2)}) copy-start(bf16[128,2048]{1,0:T(8,128)(2,1)S(1)} %collective-permute-done.2.refs_2_) | copy-start | bytes 1572868
  30.0 58.8 %collective-permute-start.7 = (bf16[128,2048]{1,0:T(8,128)(2,1)S(1)}, bf16[128,2048]{1,0:T(8,128)(2,1)}, u32[]{:S(2)}, u32[]{:S(2)}) collective-permute-start(bf16[128,2048]{1,0:T(8,128)(2,1)S(1)} %collective-permute-done.2.refs_2_), channel_id=1, source_target_pairs={{0,4},{4,8},{8,12},{12,14},{14,10},{10,6},{6,2},{2,0},{1,5},{5,9},... | collective-permute-start | bytes 1572872 | tf_op jit(solution)/shard_map/ppermute | solution.py:280
  39.1 12.2 %copy-start.16 = (bf16[128,2048]{1,0:T(8,128)(2,1)}, bf16[128,2048]{1,0:T(8,128)(2,1)S(1)}, u32[]{:S(2)}) copy-start(bf16[128,2048]{1,0:T(8,128)(2,1)S(1)} %collective-permute-done.5.refs_0_) | copy-start | bytes 1572868
  39.1 62.5 %collective-permute-start.10 = (bf16[128,2048]{1,0:T(8,128)(2,1)S(1)}, bf16[128,2048]{1,0:T(8,128)(2,1)}, u32[]{:S(2)}, u32[]{:S(2)}) collective-permute-start(bf16[128,2048]{1,0:T(8,128)(2,1)S(1)} %collective-permute-done.5.refs_0_), channel_id=1, source_target_pairs={{0,4},{4,8},{8,12},{12,14},{14,10},{10,6},{6,2},{2,0},{1,5},{5,9},... | collective-permute-start | bytes 1572872 | tf_op jit(solution)/shard_map/ppermute | solution.py:280
  41.2 60.4 %collective-permute-start.13 = (bf16[128,2048]{1,0:T(8,128)(2,1)S(1)}, bf16[128,2048]{1,0:T(8,128)(2,1)}, u32[]{:S(2)}, u32[]{:S(2)}) collective-permute-start(bf16[128,2048]{1,0:T(8,128)(2,1)S(1)} %collective-permute-done.8.refs_3_), channel_id=1, source_target_pairs={{0,2},{4,0},{8,4},{12,8},{14,12},{10,14},{6,10},{2,6},{1,3},{5,1},... | collective-permute-start | bytes 1572872 | tf_op jit(solution)/shard_map/ppermute | solution.py:280
  88.8 25.6 %collective-permute-start.11 = (bf16[128,2048]{1,0:T(8,128)(2,1)}, bf16[128,2048]{1,0:T(8,128)(2,1)S(1)}, u32[]{:S(2)}, u32[]{:S(2)}) collective-permute-start(bf16[128,2048]{1,0:T(8,128)(2,1)} %collective-permute-done.6.refs_1_), channel_id=1, source_target_pairs={{0,2},{4,0},{8,4},{12,8},{14,12},{10,14},{6,10},{2,6},{1,3},{5,1},... | collective-permute-start | bytes 1572872 | tf_op jit(solution)/shard_map/ppermute | solution.py:280
  88.8 25.6 %collective-permute-start.12 = (bf16[128,2048]{1,0:T(8,128)(2,1)}, bf16[128,2048]{1,0:T(8,128)(2,1)S(1)}, u32[]{:S(2)}, u32[]{:S(2)}) collective-permute-start(bf16[128,2048]{1,0:T(8,128)(2,1)} %collective-permute-done.7.refs_2_), channel_id=1, source_target_pairs={{0,4},{4,8},{8,12},{12,14},{14,10},{10,6},{6,2},{2,0},{1,5},{5,9},... | collective-permute-start | bytes 1572872 | tf_op jit(solution)/shard_map/ppermute | solution.py:280
  101.6 25.2 %collective-permute-start.15 = (bf16[128,2048]{1,0:T(8,128)(2,1)}, bf16[128,2048]{1,0:T(8,128)(2,1)S(1)}, u32[]{:S(2)}, u32[]{:S(2)}) collective-permute-start(bf16[128,2048]{1,0:T(8,128)(2,1)} %collective-permute-done.10.refs_0_), channel_id=1, source_target_pairs={{0,4},{4,8},{8,12},{12,14},{14,10},{10,6},{6,2},{2,0},{1,5},{5,9},... | collective-permute-start | bytes 1572872 | tf_op jit(solution)/shard_map/ppermute | solution.py:280
  101.6 25.2 %collective-permute-start.16 = (bf16[128,2048]{1,0:T(8,128)(2,1)}, bf16[128,2048]{1,0:T(8,128)(2,1)S(1)}, u32[]{:S(2)}, u32[]{:S(2)}) collective-permute-start(bf16[128,2048]{1,0:T(8,128)(2,1)} %collective-permute-done.13.refs_3_), channel_id=1, source_target_pairs={{0,2},{4,0},{8,4},{12,8},{14,12},{10,14},{6,10},{2,6},{1,3},{5,1},... | collective-permute-start | bytes 1572872 | tf_op jit(solution)/shard_map/ppermute | solution.py:280
  141.9 29.1 %copy-start = (bf16[2304,512]{1,0:T(8,128)(2,1)S(1)}, bf16[2304,512]{1,0:T(8,128)(2,1)}, u32[]{:S(2)}) copy-start(bf16[2304,512]{1,0:T(8,128)(2,1)} %turned_grads.1) | copy-start | bytes 7077892
  141.9 31.6 %copy-start.1 = (bf16[128,2304]{1,0:T(8,128)(2,1)S(1)}, bf16[128,2304]{1,0:T(8,128)(2,1)}, u32[]{:S(2)}) copy-start(bf16[128,2304]{1,0:T(8,128)(2,1)} %get-tuple-element.57.refs_21_.refs_1_) | copy-start | bytes 1769476
  141.9 45.3 %copy-start.2 = (bf16[128,2304]{1,0:T(8,128)(2,1)S(1)}, bf16[128,2304]{1,0:T(8,128)(2,1)}, u32[]{:S(2)}) copy-start(bf16[128,2304]{1,0:T(8,128)(2,1)} %get-tuple-element.58.refs_22_.refs_2_) | copy-start | bytes 1769476
  143.8 9.0 %collective-permute-start.35 = (bf16[288,512]{1,0:T(8,128)(2,1)}, bf16[288,512]{1,0:T(8,128)(2,1)}, u32[]{:S(2)}, u32[]{:S(2)}) collective-permute-start(bf16[288,512]{1,0:T(8,128)(2,1)} %constant_dynamic-slice_fusion), channel_id=1, source_target_pairs={{0,2},{4,0},{8,4},{12,8},{14,12},{10,14},{6,10},{2,6},{1,3},{5,1},... | collective-permute-start | bytes 884744 | tf_op jit(solution)/shard_map/ppermute | solution.py:280
  154.7 7.0 %collective-permute-start.36 = (bf16[288,512]{1,0:T(8,128)(2,1)}, bf16[288,512]{1,0:T(8,128)(2,1)}, u32[]{:S(2)}, u32[]{:S(2)}) collective-permute-start(bf16[288,512]{1,0:T(8,128)(2,1)} %dynamic-slice_select_fusion), channel_id=1, source_target_pairs={{0,2},{4,0},{8,4},{12,8},{14,12},{10,14},{6,10},{2,6},{1,3},{5,1},... | collective-permute-start | bytes 884744 | tf_op jit(solution)/shard_map/ppermute | solution.py:280
  163.7 7.2 %collective-permute-start.31 = (bf16[288,512]{1,0:T(8,128)(2,1)}, bf16[288,512]{1,0:T(8,128)(2,1)}, u32[]{:S(2)}, u32[]{:S(2)}) collective-permute-start(bf16[288,512]{1,0:T(8,128)(2,1)} %get-tuple-element.74), channel_id=1, source_target_pairs={{0,4},{4,8},{8,12},{12,14},{14,10},{10,6},{6,2},{2,0},{1,5},{5,9},... | collective-permute-start | bytes 884744 | tf_op jit(solution)/shard_map/ppermute | solution.py:280
  172.7 7.9 %collective-permute-start.32 = (bf16[288,512]{1,0:T(8,128)(2,1)}, bf16[288,512]{1,0:T(8,128)(2,1)}, u32[]{:S(2)}, u32[]{:S(2)}) collective-permute-start(bf16[288,512]{1,0:T(8,128)(2,1)} %dynamic-slice_select_fusion.2), channel_id=1, source_target_pairs={{0,4},{4,8},{8,12},{12,14},{14,10},{10,6},{6,2},{2,0},{1,5},{5,9},... | collective-permute-start | bytes 884744 | tf_op jit(solution)/shard_map/ppermute | solution.py:280
  173.6 2.2 collective-permute-start.21
  173.6 14.4 %collective-permute-start.27 = (bf16[128,2304]{1,0:T(8,128)(2,1)S(1)}, bf16[128,2304]{1,0:T(8,128)(2,1)}, u32[]{:S(2)}, u32[]{:S(2)}) collective-permute-start(bf16[128,2304]{1,0:T(8,128)(2,1)S(1)} %copy-done.1), channel_id=1, source_target_pairs={{0,1},{1,0},{2,3},{3,2},{4,5},{5,4},{6,7},{7,6},{8,9},{9,8},{10,11... | collective-permute-start | bytes 1769480 | tf_op jit(solution)/shard_map/ppermute | solution.py:283
  174.1 8.3 %collective-permute-start.26 = (bf16[64,2304]{1,0:T(8,128)(2,1)}, bf16[64,2304]{1,0:T(8,128)(2,1)}, u32[]{:S(2)}, u32[]{:S(2)}) collective-permute-start(bf16[64,2304]{1,0:T(8,128)(2,1)} %get-tuple-element.56.refs_20_.refs_0_), channel_id=1, source_target_pairs={{0,1},{1,0},{2,3},{3,2},{4,5},{5,4},{6,7},{7,6},{8,9},{9,8},{10,11... | collective-permute-start | bytes 884744 | tf_op jit(solution)/shard_map/ppermute | solution.py:283
  174.1 13.2 %collective-permute-start.22 = (bf16[128,2048]{1,0:T(8,128)(2,1)}, bf16[128,2048]{1,0:T(8,128)(2,1)}, u32[]{:S(2)}, u32[]{:S(2)}) collective-permute-start(bf16[128,2048]{1,0:T(8,128)(2,1)} %get-tuple-element.52), channel_id=1, source_target_pairs={{0,1},{1,0},{2,3},{3,2},{4,5},{5,4},{6,7},{7,6},{8,9},{9,8},{10,11... | collective-permute-start | bytes 1572872 | tf_op jit(solution)/shard_map/ppermute | solution.py:283
  175.8 10.4 %collective-permute-start.4 = (bf16[64,2048]{1,0:T(8,128)(2,1)}, bf16[64,2048]{1,0:T(8,128)(2,1)S(1)}, u32[]{:S(2)}, u32[]{:S(2)}) collective-permute-start(bf16[64,2048]{1,0:T(8,128)(2,1)} %get-tuple-element.39), channel_id=1, source_target_pairs={{0,4},{4,8},{8,12},{12,14},{14,10},{10,6},{6,2},{2,0},{1,5},{5,9},... | collective-permute-start | bytes 786440 | tf_op jit(solution)/shard_map/ppermute | solution.py:280
  180.7 6.6 %collective-permute-start.20 = (bf16[64,2048]{1,0:T(8,128)(2,1)}, bf16[64,2048]{1,0:T(8,128)(2,1)S(1)}, u32[]{:S(2)}, u32[]{:S(2)}) collective-permute-start(bf16[64,2048]{1,0:T(8,128)(2,1)} %get-tuple-element.45), channel_id=1, source_target_pairs={{0,2},{4,0},{8,4},{12,8},{14,12},{10,14},{6,10},{2,6},{1,3},{5,1},... | collective-permute-start | bytes 786440 | tf_op jit(solution)/shard_map/ppermute | solution.py:280
  182.4 9.4 %collective-permute-start.33 = (bf16[288,512]{1,0:T(8,128)(2,1)}, bf16[288,512]{1,0:T(8,128)(2,1)}, u32[]{:S(2)}, u32[]{:S(2)}) collective-permute-start(bf16[288,512]{1,0:T(8,128)(2,1)} %dynamic-slice_select_fusion.3), channel_id=1, source_target_pairs={{0,4},{4,8},{8,12},{12,14},{14,10},{10,6},{6,2},{2,0},{1,5},{5,9},... | collective-permute-start | bytes 884744 | tf_op jit(solution)/shard_map/ppermute | solution.py:280
  186.2 19.5 %collective-permute-start.23 = (bf16[128,2048]{1,0:T(8,128)(2,1)}, bf16[128,2048]{1,0:T(8,128)(2,1)}, u32[]{:S(2)}, u32[]{:S(2)}) collective-permute-start(bf16[128,2048]{1,0:T(8,128)(2,1)} %get-tuple-element.53), channel_id=1, source_target_pairs={{0,1},{1,0},{2,3},{3,2},{4,5},{5,4},{6,7},{7,6},{8,9},{9,8},{10,11... | collective-permute-start | bytes 1572872 | tf_op jit(solution)/shard_map/ppermute | solution.py:283
  187.3 20.4 %collective-permute-start.28 = (bf16[128,2304]{1,0:T(8,128)(2,1)S(1)}, bf16[128,2304]{1,0:T(8,128)(2,1)}, u32[]{:S(2)}, u32[]{:S(2)}) collective-permute-start(bf16[128,2304]{1,0:T(8,128)(2,1)S(1)} %copy-done.2), channel_id=1, source_target_pairs={{0,1},{1,0},{2,3},{3,2},{4,5},{5,4},{6,7},{7,6},{8,9},{9,8},{10,11... | collective-permute-start | bytes 1769480 | tf_op jit(solution)/shard_map/ppermute | solution.py:283
  187.3 11.3 %collective-permute-start.9 = (bf16[64,2048]{1,0:T(8,128)(2,1)}, bf16[64,2048]{1,0:T(8,128)(2,1)}, u32[]{:S(2)}, u32[]{:S(2)}) collective-permute-start(bf16[64,2048]{1,0:T(8,128)(2,1)} %get-tuple-element.40), channel_id=1, source_target_pairs={{0,8},{4,12},{8,14},{12,10},{14,6},{10,2},{6,0},{2,4},{1,9},{5,13}... | collective-permute-start | bytes 786440 | tf_op jit(solution)/shard_map/ppermute | solution.py:280
  188.0 15.8 %collective-permute-start.19 = (bf16[64,2048]{1,0:T(8,128)(2,1)}, bf16[64,2048]{1,0:T(8,128)(2,1)S(1)}, u32[]{:S(2)}, u32[]{:S(2)}) collective-permute-start(bf16[64,2048]{1,0:T(8,128)(2,1)} %get-tuple-element.44), channel_id=1, source_target_pairs={{0,6},{4,2},{8,0},{12,4},{14,8},{10,12},{6,14},{2,10},{1,7},{5,3},... | collective-permute-start | bytes 786440 | tf_op jit(solution)/shard_map/ppermute | solution.py:280
  191.8 36.0 %collective-permute-start.37 = (bf16[288,512]{1,0:T(8,128)(2,1)}, bf16[288,512]{1,0:T(8,128)(2,1)}, u32[]{:S(2)}, u32[]{:S(2)}) collective-permute-start(bf16[288,512]{1,0:T(8,128)(2,1)} %get-tuple-element.73), channel_id=1, source_target_pairs={{0,2},{4,0},{8,4},{12,8},{14,12},{10,14},{6,10},{2,6},{1,3},{5,1},... | collective-permute-start | bytes 884744 | tf_op jit(solution)/shard_map/ppermute | solution.py:280
  198.6 31.3 %collective-permute-start.34 = (bf16[288,512]{1,0:T(8,128)(2,1)}, bf16[288,512]{1,0:T(8,128)(2,1)}, u32[]{:S(2)}, u32[]{:S(2)}) collective-permute-start(bf16[288,512]{1,0:T(8,128)(2,1)} %dynamic-slice_select_fusion.4), channel_id=1, source_target_pairs={{0,4},{4,8},{8,12},{12,14},{14,10},{10,6},{6,2},{2,0},{1,5},{5,9},... | collective-permute-start | bytes 884744 | tf_op jit(solution)/shard_map/ppermute | solution.py:280
  203.8 22.8 %collective-permute-start.14 = (bf16[64,2048]{1,0:T(8,128)(2,1)}, bf16[64,2048]{1,0:T(8,128)(2,1)S(1)}, u32[]{:S(2)}, u32[]{:S(2)}) collective-permute-start(bf16[64,2048]{1,0:T(8,128)(2,1)} %get-tuple-element.41), channel_id=1, source_target_pairs={{0,12},{4,14},{8,10},{12,6},{14,2},{10,0},{6,4},{2,8},{1,13},{5,15... | collective-permute-start | bytes 786440 | tf_op jit(solution)/shard_map/ppermute | solution.py:280
  205.7 21.6 %collective-permute-start.18 = (bf16[64,2048]{1,0:T(8,128)(2,1)}, bf16[64,2048]{1,0:T(8,128)(2,1)}, u32[]{:S(2)}, u32[]{:S(2)}) collective-permute-start(bf16[64,2048]{1,0:T(8,128)(2,1)} %get-tuple-element.43), channel_id=1, source_target_pairs={{0,10},{4,6},{8,2},{12,0},{14,4},{10,8},{6,12},{2,14},{1,11},{5,7}... | collective-permute-start | bytes 786440 | tf_op jit(solution)/shard_map/ppermute | solution.py:280
  207.6 37.0 %collective-permute-start.29 = (bf16[128,2304]{1,0:T(8,128)(2,1)}, bf16[128,2304]{1,0:T(8,128)(2,1)S(1)}, u32[]{:S(2)}, u32[]{:S(2)}) collective-permute-start(bf16[128,2304]{1,0:T(8,128)(2,1)} %get-tuple-element.59.refs_23_.refs_3_), channel_id=1, source_target_pairs={{0,1},{1,0},{2,3},{3,2},{4,5},{5,4},{6,7},{7,6},{8,9},{9,8},{10,11... | collective-permute-start | bytes 1769480 | tf_op jit(solution)/shard_map/ppermute | solution.py:283
  227.3 17.4 %collective-permute-start.24 = (bf16[128,2048]{1,0:T(8,128)(2,1)}, bf16[128,2048]{1,0:T(8,128)(2,1)S(1)}, u32[]{:S(2)}, u32[]{:S(2)}) collective-permute-start(bf16[128,2048]{1,0:T(8,128)(2,1)} %get-tuple-element.54), channel_id=1, source_target_pairs={{0,1},{1,0},{2,3},{3,2},{4,5},{5,4},{6,7},{7,6},{8,9},{9,8},{10,11... | collective-permute-start | bytes 1572872 | tf_op jit(solution)/shard_map/ppermute | solution.py:283
  227.3 17.4 %collective-permute-start.30 = (bf16[64,2304]{1,0:T(8,128)(2,1)}, bf16[64,2304]{1,0:T(8,128)(2,1)S(1)}, u32[]{:S(2)}, u32[]{:S(2)}) collective-permute-start(bf16[64,2304]{1,0:T(8,128)(2,1)} %get-tuple-element.60.refs_24_.refs_4_), channel_id=1, source_target_pairs={{0,1},{1,0},{2,3},{3,2},{4,5},{5,4},{6,7},{7,6},{8,9},{9,8},{10,11... | collective-permute-start | bytes 884744 | tf_op jit(solution)/shard_map/ppermute | solution.py:283
  227.8 11.3 %collective-permute-start.17 = (bf16[64,2048]{1,0:T(8,128)(2,1)}, bf16[64,2048]{1,0:T(8,128)(2,1)S(1)}, u32[]{:S(2)}, u32[]{:S(2)}) collective-permute-start(bf16[64,2048]{1,0:T(8,128)(2,1)} %get-tuple-element.42), channel_id=1, source_target_pairs={{0,14},{4,10},{8,6},{12,2},{14,0},{10,4},{6,8},{2,12},{1,15},{5,11... | collective-permute-start | bytes 786440 | tf_op jit(solution)/shard_map/ppermute | solution.py:280
  229.9 14.7 %collective-permute-start.25 = (bf16[64,2048]{1,0:T(8,128)(2,1)}, bf16[64,2048]{1,0:T(8,128)(2,1)S(1)}, u32[]{:S(2)}, u32[]{:S(2)}) collective-permute-start(bf16[64,2048]{1,0:T(8,128)(2,1)} %get-tuple-element.55), channel_id=1, source_target_pairs={{0,1},{1,0},{2,3},{3,2},{4,5},{5,4},{6,7},{7,6},{8,9},{9,8},{10,11... | collective-permute-start | bytes 786440 | tf_op jit(solution)/shard_map/ppermute | solution.py:283
  239.1 17.5 %collective-permute-start.38 = (bf16[288,1024]{1,0:T(8,128)(2,1)}, bf16[288,1024]{1,0:T(8,128)(2,1)S(1)}, u32[]{:S(2)}, u32[]{:S(2)}) collective-permute-start(bf16[288,1024]{1,0:T(8,128)(2,1)} %get-tuple-element.72), channel_id=1, source_target_pairs={{0,1},{1,0},{2,3},{3,2},{4,5},{5,4},{6,7},{7,6},{8,9},{9,8},{10,11... | collective-permute-start | bytes 1769480 | tf_op jit(solution)/shard_map/ppermute | solution.py:283
  245.8 10.8 %copy-start.4 = (f32[288,1024]{1,0:T(8,128)S(1)}, f32[288,1024]{1,0:T(8,128)}, u32[]{:S(2)}) copy-start(f32[288,1024]{1,0:T(8,128)} %get-tuple-element.71) | copy-start | bytes 3538948
  (14 other events, 25.1 us)

commit v2 on v1

v2 whole, which is shorter than its diff:
```python
import functools

import jax
import jax.numpy as jnp
from jax import lax
from jax.experimental import pallas as pl
from jax.experimental.pallas import tpu as pltpu
from jax.sharding import PartitionSpec as P

BF16 = jnp.bfloat16
F32 = jnp.float32
VMEM_BYTES = 56 * 1024 * 1024


def snaked(experts):
    return experts <= 8


def to_ring(expert, experts):
    if not snaked(experts):
        return expert
    down = experts - 1 - (expert - 1) // 2
    return jnp.where(expert % 2 == 0, expert // 2, down)


def from_ring(place, experts):
    if not snaked(experts):
        return place
    return jnp.where(place < experts // 2, 2 * place, 2 * (experts - 1 - place) + 1)


def ring_order(experts):
    if not snaked(experts):
        return list(range(experts))
    return list(range(0, experts, 2)) + list(range(experts - 1, 0, -2))


def distances(experts):
    half = experts // 2
    return [[0]] + [[-step, step] for step in range(1, half)] + [[half]]


def slot_place(distance, experts):
    half = experts // 2
    near = jnp.where(distance < half, 2 * distance - 1, 2 * (experts - distance) - 2)
    near = jnp.where(distance == half, experts - 1, near)
    return jnp.where(distance == 0, experts - 2, near)


def dot(a, b, dims):
    return lax.dot_general(a, b, ((dims[:1], dims[1:]), ((), ())), preferred_element_type=F32)


def selection(table, expert, fanout, capacity):
    tokens = table.shape[1]
    hit = table[:fanout] == expert.astype(F32)
    named = jnp.sum(jnp.where(hit, 1.0, 0.0), axis=0, keepdims=True)
    parts = table[fanout : 4 * fanout]
    weights = parts[:fanout] + parts[fanout : 2 * fanout] + parts[2 * fanout :]
    weight = jnp.sum(jnp.where(hit, weights, 0.0), axis=0, keepdims=True)
    upto = lax.broadcasted_iota(jnp.int32, (tokens, tokens), 0) <= lax.broadcasted_iota(
        jnp.int32, (tokens, tokens), 1
    )
    upto = jnp.where(upto, 1.0, 0.0).astype(BF16)
    place = dot(jnp.broadcast_to(named, (8, tokens)).astype(BF16), upto, (1, 0))[:1]
    row = lax.broadcasted_iota(jnp.int32, (capacity, tokens), 0).astype(F32) + 1.0
    onehot = jnp.where((row == place) & (named > 0.5), 1.0, 0.0)
    return onehot, weight


def step_kernel(steps, fanout, capacity, joined, scal, *refs):
    count = len(steps)
    blocks, refs = refs[: max(count, 1 + joined)], refs[max(count, 1 + joined) :]
    if joined:
        first, refs = refs[0], refs[1:]
        blocks = [jnp.concatenate([block[...] for block in blocks], axis=1)]
    weights_gu, weights_down, mine, pack, hot_in, hot_cot = refs[:6]
    back, refs = refs[6 : 6 + count], refs[6 + count :]
    if len(refs) > 5:
        turned, refs = refs[0], refs[1:]
    else:
        turned = None
    rows_in, rows_cot, gate_up, down, sems = refs
    own, half, hottest = scal[0], scal[1], scal[2]
    units, width = down.shape
    load_gu = pltpu.make_async_copy(weights_gu, gate_up, sems.at[0])
    load_down = pltpu.make_async_copy(weights_down, down, sems.at[1])
    load_gu.start()
    load_down.start()
    for at, block in enumerate(blocks):
        rows = slice(at * capacity, (at + 1) * capacity)
        table = block[:, 2 * width :].astype(F32).T
        own_hot, own_weight = selection(table, own, fanout, capacity)
        all_hot, all_weight = selection(table, hottest, fanout, capacity)
        scale = jnp.concatenate(
            [
                jnp.sum(own_hot * own_weight, axis=1, keepdims=True),
                jnp.sum(all_hot * all_weight, axis=1, keepdims=True),
            ],
            axis=0,
        )
        onehot = jnp.concatenate([own_hot, all_hot], axis=0).astype(BF16)
        picked = dot(onehot, block[:, :width], (1, 0)).astype(BF16)
        rows_in[rows, :] = picked[:capacity]
        hot_in[rows, :] = picked[capacity:]
        picked = (scale * dot(onehot, block[:, width : 2 * width], (1, 0))).astype(BF16)
        rows_cot[rows, :] = picked[:capacity]
        hot_cot[rows, :] = picked[capacity:]
    part = width // 2
    here = pl.ds(pl.multiple_of(half * part, part), part)
    there = pl.ds(pl.multiple_of((1 - half) * part, part), part)
    mine[:, :part] = rows_in[:, here]
    mine[:, part:] = rows_cot[:, here]
    pack[:, :part] = rows_in[:, there]
    pack[:, part:width] = rows_cot[:, there]
    load_gu.wait()
    projected = dot(rows_in[...], gate_up[...], (1, 0))
    gate_pre, up_pre = projected[:, :units], projected[:, units:]
    load_down.wait()
    hidden_grad = dot(rows_cot[...], down[...], (1, 1))
    sigmoid_gate = jax.nn.sigmoid(gate_pre)
    activation = gate_pre * sigmoid_gate
    gate_grad = hidden_grad * up_pre * sigmoid_gate * (1.0 + gate_pre * (1.0 - sigmoid_gate))
    pack[:, width : width + units] = gate_grad.astype(BF16)
    pack[:, width + units : width + 2 * units] = (hidden_grad * activation).astype(BF16)
    pack[:, width + 2 * units :] = (activation * up_pre).astype(BF16)
    input_rows = dot(pack[:, width : width + 2 * units], gate_up[...], (1, 1)).astype(BF16)
    for at in range(count):
        back[at][...] = input_rows[at * capacity : (at + 1) * capacity]
    if turned is not None:
        grads = pack[:, width:]
        if joined:
            grads = jnp.concatenate([first[:, width:], grads], axis=0)
        turned[...] = grads.T


def run_step(steps, fanout, capacity, scal, blocks, first, gate_up, down):
    count, rows = len(steps), len(steps) * capacity
    units, width = down.shape
    vmem = pl.BlockSpec(memory_space=pltpu.VMEM)
    far = pl.BlockSpec(memory_space=pl.ANY)
    shapes = [(rows, width), (rows, width + 3 * units), (rows, width), (rows, width)]
    shapes += [(capacity, width)] * count
    joined = first is not None
    if joined or count > 1:
        shapes += [(3 * units, 2 * capacity)]
    firsts = [first] if joined else []
    out = pl.pallas_call(
        functools.partial(step_kernel, steps, fanout, capacity, joined),
        out_shape=[jax.ShapeDtypeStruct(shape, BF16) for shape in shapes],
        in_specs=[pl.BlockSpec(memory_space=pltpu.SMEM)] + [vmem] * (len(blocks) + len(firsts)) + [far] * 2,
        out_specs=[vmem] * len(shapes),
        scratch_shapes=[pltpu.VMEM((rows, width), BF16)] * 2
        + [
            pltpu.VMEM(gate_up.shape, BF16),
            pltpu.VMEM(down.shape, BF16),
            pltpu.SemaphoreType.DMA((2,)),
        ],
        compiler_params=pltpu.CompilerParams(vmem_limit_bytes=VMEM_BYTES),
        cost_estimate=pl.CostEstimate(
            flops=2 * 256 * 5 * width * units, bytes_accessed=3 * 2 * width * units, transcendentals=0
        ),
        name="expert_step",
    )(scal, *blocks, *firsts, gate_up, down)
    return out[:4], out[4 : 4 + count], out[4 + count :]


def combine_kernel(experts, fanout, capacity, scal, meta, *refs):
    rows, out = refs[:experts], refs[experts]
    place = to_ring(scal[0], experts)
    table = meta[...].astype(F32).T
    picks = []
    for step in range(experts):
        expert = from_ring((place - step + experts) % experts, experts)
        picks.append(selection(table, expert, fanout, capacity)[0])
    onehot = jnp.concatenate(picks, axis=0).astype(BF16)
    out[...] = dot(onehot, jnp.concatenate([part[...] for part in rows], axis=0), (0, 0)).astype(BF16)


def combine(experts, fanout, capacity, scal, meta, rows):
    vmem = pl.BlockSpec(memory_space=pltpu.VMEM)
    tokens, width = meta.shape[0], rows[0].shape[1]
    return pl.pallas_call(
        functools.partial(combine_kernel, experts, fanout, capacity),
        out_shape=jax.ShapeDtypeStruct((tokens, width), BF16),
        in_specs=[pl.BlockSpec(memory_space=pltpu.SMEM)] + [vmem] * (experts + 1),
        out_specs=vmem,
        compiler_params=pltpu.CompilerParams(vmem_limit_bytes=VMEM_BYTES),
        cost_estimate=pl.CostEstimate(
            flops=2 * experts * capacity * tokens * width, bytes_accessed=2 * experts * capacity * width, transcendentals=0
        ),
        name="token_sum",
    )(scal, meta, *rows)


def gradient_kernel(units, count, scal, *refs):
    ins, cots, packs = refs[: 2 * count], refs[2 * count : 4 * count], refs[4 * count : 6 * count]
    out = refs[6 * count]
    keep = scal[0] != scal[2]
    width = packs[0].shape[1] - 3 * units
    left = jnp.concatenate([ref[...] for ref in ins], axis=0)
    right = jnp.concatenate([ref[:, width : width + 2 * units] for ref in packs], axis=0)
    out[0, :, : 2 * units] = jnp.where(keep, dot(left, right, (0, 0)), 0.0)
    left = jnp.concatenate([ref[...] for ref in cots], axis=0)
    right = jnp.concatenate([ref[:, width + 2 * units :] for ref in packs], axis=0)
    out[0, :, 2 * units :] = jnp.where(keep, dot(left, right, (0, 0)), 0.0)


def expert_gradient(units, scal, mine, packs, others):
    width, columns, count = mine[0].shape[1], 3 * units, len(mine)
    tile = 256
    tiles = width // 2 // tile
    total = 2 * sum(part.shape[0] for part in mine)
    rows = mine + others
    in_specs = [pl.BlockSpec(memory_space=pltpu.SMEM)]
    in_specs += [pl.BlockSpec((part.shape[0], tile), lambda i: (0, i)) for part in rows]
    in_specs += [pl.BlockSpec((part.shape[0], tile), lambda i: (0, i + tiles)) for part in rows]
    in_specs += [pl.BlockSpec(part.shape, lambda i: (0, 0)) for part in packs + others]
    return pl.pallas_call(
        functools.partial(gradient_kernel, units, count),
        grid=(tiles,),
        out_shape=jax.ShapeDtypeStruct((1, width // 2, columns), F32),
        in_specs=in_specs,
        out_specs=pl.BlockSpec((1, tile, columns), lambda i: (0, i, 0)),
        compiler_params=pltpu.CompilerParams(vmem_limit_bytes=VMEM_BYTES),
        cost_estimate=pl.CostEstimate(
            flops=width * columns * total, bytes_accessed=3 * width * columns, transcendentals=0
        ),
        name="expert_gradient",
    )(scal, *rows, *rows, *packs, *others)


def shadow_kernel(plan, experts, capacity, scal, columns, *refs):
    count = len(plan)
    ins, cots = refs[:count], refs[count : 2 * count]
    mine, theirs, rows_in, rows_cot, total = refs[2 * count :]
    own, half, hottest = scal[0], scal[1], scal[2]
    shift = to_ring(own, experts) - to_ring(hottest, experts)
    taken = columns.shape[0]
    gates = taken * experts * 2 // 3
    column = own * taken + lax.broadcasted_iota(jnp.int32, columns.shape, 0)
    blank = jnp.zeros((), BF16)

    def in_order(parts, rows):
        for steps, part in zip(plan, parts):
            for at, step in enumerate(steps):
                place = slot_place((shift + step + 2 * experts) % experts, experts)
                there = pl.ds(pl.multiple_of(place * capacity, capacity), capacity)
                rows[there, :] = part[at * capacity : (at + 1) * capacity, :]

    @pl.when(own * taken < gates)
    def _():
        in_order(ins, rows_in)
        total[...] = dot(jnp.where(column < gates, columns[...], blank), rows_in[...], (1, 0))

    @pl.when(own * taken >= gates)
    def _():
        total[...] = jnp.zeros(total.shape, F32)

    @pl.when((own + 1) * taken > gates)
    def _():
        in_order(cots, rows_cot)
        total[...] += dot(jnp.where(column < gates, blank, columns[...]), rows_cot[...], (1, 0))

    width = total.shape[1] // 2
    mine[...] = total[:, pl.ds(pl.multiple_of(half * width, width), width)]
    theirs[...] = total[:, pl.ds(pl.multiple_of((1 - half) * width, width), width)].astype(BF16)


def shadow_gradient(plan, experts, capacity, scal, columns, ins, cots):
    vmem = pl.BlockSpec(memory_space=pltpu.VMEM)
    taken, rows = columns.shape
    width = ins[0].shape[1]
    return pl.pallas_call(
        functools.partial(shadow_kernel, plan, experts, capacity),
        out_shape=[
            jax.ShapeDtypeStruct((taken, width // 2), F32),
            jax.ShapeDtypeStruct((taken, width // 2), BF16),
        ],
        in_specs=[pl.BlockSpec(memory_space=pltpu.SMEM)] + [vmem] * (2 * len(ins) + 1),
        out_specs=[vmem] * 2,
        scratch_shapes=[pltpu.VMEM((rows, width), BF16)] * 2 + [pltpu.VMEM((taken, width), F32)],
        compiler_params=pltpu.CompilerParams(vmem_limit_bytes=VMEM_BYTES),
        cost_estimate=pl.CostEstimate(
            flops=4 * taken * rows * width, bytes_accessed=4 * rows * width, transcendentals=0
        ),
        name="shadow_gradient",
    )(scal, columns, *ins, *cots)


def on_device(
    tokens, cotangent, routes, route_weight, ratio_advantage, clip_mask, shadow_plan, gate_up, down
):
    experts = lax.axis_size("expert")
    tok_rows, width = tokens.shape
    fanout = routes.shape[1]
    units = down.shape[1]
    capacity = 2 * tok_rows * fanout // experts
    gate_up, down = gate_up[0], down[0]
    order = ring_order(experts)
    half = experts // 2

    def shift(block, step):
        pairs = [(order[i], order[(i + step) % experts]) for i in range(experts)]
        return lax.ppermute(block, "expert", pairs)

    def swap(block):
        return lax.ppermute(block, "dp", [(0, 1), (1, 0)])

    own = lax.axis_index("expert")
    hottest = shadow_plan[0]
    scal = jnp.stack([own, lax.axis_index("dp"), hottest]).astype(jnp.int32)
    slot_weight = route_weight * ratio_advantage[:, None] * clip_mask[:, None].astype(F32)
    first = lax.reduce_precision(slot_weight, 8, 7)
    rest = slot_weight - first
    second = lax.reduce_precision(rest, 8, 7)
    meta = jnp.concatenate([routes.astype(F32), first, second, rest - second], axis=1)
    meta = jnp.pad(meta, ((0, 0), (0, 128 - meta.shape[1]))).astype(BF16)
    message = jnp.concatenate([tokens, cotangent, meta], axis=1)

    plan = distances(experts)
    mine, packs, others, hot_in, hot_cot, turned, late = [], [], [], [], [], [], []
    returned = {}
    up, below, held = message, message, [message]
    for number, steps in enumerate(plan):
        if number + 1 < half:
            following = [shift(up, 1), shift(below, -1)]
        elif number + 1 == half:
            following = [shift(up[:, :width], 1), shift(below[:, width:], -1)]
        if number > 1:
            held, late[number - 2] = lax.optimization_barrier((held, late[number - 2]))
        (rows, pack, hot_rows, hot_cots), back, turn = run_step(
            steps, fanout, capacity, scal, held, packs[0] if number == half else None, gate_up, down
        )
        following, back = lax.optimization_barrier((following, back))
        sent = [shift(part, step) if step else part for step, part in zip(steps, back)]
        late.append((sent, swap(pack)))
        mine.append(rows)
        packs.append(pack)
        hot_in.append(hot_rows)
        hot_cot.append(hot_cots)
        turned += turn
        held = following
        if number < half:
            up, below = following
    taken = 3 * units // experts
    ring_hot = to_ring(hottest, experts)
    is_hot = own == hottest

    def chunk(distance):
        owner = from_ring((ring_hot + distance + experts) % experts, experts)
        parts = [lax.dynamic_slice_in_dim(part, owner * taken, taken, axis=0) for part in turned]
        return jnp.concatenate(parts, axis=1)

    ahead, behind = None, None
    for number in range(half):
        part = chunk(half - number)
        if 0 < number < 3:
            at = half - 2 + number
            (ahead, behind), late[at] = lax.optimization_barrier(((ahead, behind), late[at]))
        ahead = shift(part if ahead is None else jnp.where(is_hot, part, ahead), 1)
        if number < half - 1:
            part = chunk(number + 1 - half)
            behind = shift(part if behind is None else jnp.where(is_hot, part, behind), -1)
    for steps, (sent, other) in zip(plan, late):
        others.append(other)
        for step, part in zip(steps, sent):
            returned[step % experts] = part

    expert_grad = expert_gradient(units, scal, mine, packs, others)

    away = (to_ring(own, experts) - ring_hot + experts) % experts
    columns = jnp.where(away == 0, chunk(0), jnp.where(away <= half, ahead, behind))
    columns, expert_grad = lax.optimization_barrier((columns, expert_grad))
    shadow_mine, shadow_theirs = shadow_gradient(
        plan, experts, capacity, scal, columns, hot_in, hot_cot
    )
    shadow_grad = (shadow_mine + swap(shadow_theirs).astype(F32)).T

    token_grad = combine(experts, fanout, capacity, scal, meta, [returned[d] for d in range(experts)])
    return (token_grad, expert_grad, shadow_grad)


def solution(mesh):
    placed = (
        P(("group", "expert", "dp"), None),
        P(("group", "expert", "dp"), None),
        P(("group", "expert", "dp"), None),
        P(("group", "expert", "dp"), None),
        P(("group", "expert", "dp")),
        P(("group", "expert", "dp")),
        P("group"),
        P("expert", None, None),
        P("expert", None, None),
    )
    return jax.shard_map(
        on_device,
        mesh=mesh,
        in_specs=placed,
        out_specs=(
            P(("group", "expert", "dp"), None),
            P(("group", "expert"), "dp", None),
            P(("group", "dp"), "expert"),
        ),
        check_vma=False,
    )
```

time: 259 us -> 213 us (0.82)
  blocking collectives: 37.4 us -> 0 us
  Pallas kernels: 76.7 us -> 68.9 us
  starting transfers between devices: 33.6 us -> 36.9 us
  other arithmetic: 14.9 us -> 12 us
  local copies, waits for them, and re-layouts: 8.15 us -> 5.52 us
    all_gather x1 -> x0, blocking collectives: 37.4 us -> none  [on_device(): meta_all = lax.all_gather(meta, 'expert', axis=0, tiled=True)]
    pallas_call x7 -> x6, Pallas kernels: 66.7 us -> 61.2 us  [the longest x5 49.2 us: run_step(): pl.pallas_call(functools.partial(step_kernel, steps, fanout, capacity, jo...]
    unnamed x46 -> x62, local copies, waits for them, and re-layouts: 5.72 us -> 0.81 us
    select_n x5, other arithmetic: 9.12 us -> 4.5 us  [the longest x3 2.38 us: on_device(): ahead = shift(part if ahead is None else jnp.where(is_hot, part, ahead), 1)]
    ppermute x28 -> x22, starting transfers between devices: 32 us -> 36.6 us  [shift(): return lax.ppermute(block, 'expert', pairs)]
    concatenate x0 -> x4, other arithmetic: none -> 2.81 us  [the longest x2 1.5 us: chunk(): return jnp.concatenate(parts, axis=1)]
    ppermute x28 -> x22, waiting for transfers between devices: 84.4 us -> 85.9 us  [shift(): return lax.ppermute(block, 'expert', pairs)]
  transfers between devices with their start and end apart: 39 -> 28, of which waited for: 15 -> 13; matrix products, arithmetic and copies ran while one was open for 3% -> 5% of each run, Pallas kernels for 24% -> 30%
where the time goes in v2:
time: 213 us; the launch traced here: 211 us
  waiting for transfers between devices  85.9 us (40%)
  Pallas kernels  68.9 us (32%)
  starting transfers between devices  36.9 us (17%)
  other arithmetic  12 us (6%)
  local copies, waits for them, and re-layouts  5.52 us (3%)
    ppermute x22, waiting for transfers between devices, shift(): return lax.ppermute(block, 'expert', pairs)  85.9 us
    pallas_call x5, Pallas kernels, run_step(): pl.pallas_call(functools.partial(step_kernel, steps, fanout, capacity, jo...  49.2 us
    ppermute x22, starting transfers between devices, shift(): return lax.ppermute(block, 'expert', pairs)  36.6 us
    pallas_call x1, Pallas kernels, expert_gradient(): pl.pallas_call(functools.partial(gradient_kernel, units, count), grid=(ti...  12 us
    pallas_call x1, Pallas kernels, shadow_gradient(): pl.pallas_call(functools.partial(shadow_kernel, plan, experts, capacity),...  4.55 us
  transfers between devices with their start and end apart: 28, of which 13 were waited for; matrix products, arithmetic and copies ran while one was open for 5% of the time, Pallas kernels for 30%

profile of v2, /device:TPU:0, one launch (start us, length us, event | category | flops | bytes accessed | tf_op | source)
XLA Modules:
  0.0 210.9 jit_solution(17060803152089168638)
XLA Ops:
  2.0 0.7 reduce-precision_convert_fusion.1
  2.8 1.3 pad_maximum_fusion.refs_0_
  4.1 3.1 %collective-permute-start = (bf16[128,4224]{1,0:T(8,128)(2,1)S(1)}, bf16[128,4224]{1,0:T(8,128)(2,1)S(1)}, u32[]{:S(2)}, u32[]{:S(2)}) collective-permute-start(bf16[128,4224]{1,0:T(8,128)(2,1)S(1)} %pad_maximum_fusion.refs_0_), channel_id=1, source_target_pairs={{0,4},{4,8},{8,12},{12,14},{14,10},{10,6},{6,2},{2,0},{1,5},{5,9},... | collective-permute-start | bytes 3244040 | tf_op jit(solution)/shard_map/ppermute | solution.py:305
  8.5 9.4 %expert_step.5 = (bf16[64,2048]{1,0:T(8,128)(2,1)}, bf16[64,4352]{1,0:T(8,128)(2,1)}, bf16[64,2048]{1,0:T(8,128)(2,1)}, bf16[64,2048]{1,0:T(8,128)(2,1)}, bf16[64,2048]{1,0:T(8,128)(2,1)}) custom-call(s32[3]{0:T(128)} %pad_add_fusion.scal, bf16[128,4224]{1,0:T(8,128)(2,1)} %copy-done.6, bf16[2048,1536]{1,0:T(8,128)(2,1)} %bitcast.13, bf16[768,2048]{1,0:T(8,128)(2,1)} %bitcast.18), custom_call_target="tpu_custom_call" | custom-call | flops 4026531840 | bytes 9437184 | tf_op jit(solution)/shard_map/expert_step/pallas_call | solution.py:148
  17.9 13.1 %collective-permute-done.refs_0_ = bf16[128,4224]{1,0:T(8,128)(2,1)S(1)} collective-permute-done((bf16[128,4224]{1,0:T(8,128)(2,1)S(1)}, bf16[128,4224]{1,0:T(8,128)(2,1)S(1)}, u32[]{:S(2)}, u32[]{:S(2)}) %collective-permute-start) | collective-permute-done | bytes 1081376 | tf_op jit(solution)/shard_map/ppermute | solution.py:305
  31.0 1.6 collective-permute-done.1.refs_1_
  32.6 1.6 collective-permute-start.2
  34.7 9.9 %expert_step.6 = (bf16[128,2048]{1,0:T(8,128)(2,1)}, bf16[128,4352]{1,0:T(8,128)(2,1)}, bf16[128,2048]{1,0:T(8,128)(2,1)}, bf16[128,2048]{1,0:T(8,128)(2,1)}, bf...) custom-call(s32[3]{0:T(128)} %pad_add_fusion.scal, bf16[128,4224]{1,0:T(8,128)(2,1)} %copy-done.26, ...), custom_call_target="tpu_custom_call" | custom-call | flops 4026531840 | bytes 9437184 | tf_op jit(solution)/shard_map/expert_step/pallas_call | solution.py:148
  44.6 12.5 %collective-permute-done.2.refs_0_ = bf16[128,4224]{1,0:T(8,128)(2,1)S(1)} collective-permute-done((bf16[128,4224]{1,0:T(8,128)(2,1)S(1)}, bf16[128,4224]{1,0:T(8,128)(2,1)S(1)}, u32[]{:S(2)}, u32[]{:S(2)}) %collective-permute-start.2) | collective-permute-done | bytes 1081376 | tf_op jit(solution)/shard_map/ppermute | solution.py:305
  57.1 1.5 collective-permute-done.3.refs_1_
  58.6 1.6 collective-permute-start.5
  60.6 10.2 %expert_step.7 = (bf16[128,2048]{1,0:T(8,128)(2,1)}, bf16[128,4352]{1,0:T(8,128)(2,1)}, bf16[128,2048]{1,0:T(8,128)(2,1)}, bf16[128,2048]{1,0:T(8,128)(2,1)}, bf...) custom-call(s32[3]{0:T(128)} %pad_add_fusion.scal, bf16[128,4224]{1,0:T(8,128)(2,1)} %copy-done.25, ...), custom_call_target="tpu_custom_call" | custom-call | flops 4026531840 | bytes 9437184 | tf_op jit(solution)/shard_map/expert_step/pallas_call | solution.py:148
  71.5 10.7 %collective-permute-done.5.refs_0_ = bf16[128,4224]{1,0:T(8,128)(2,1)S(1)} collective-permute-done((bf16[128,4224]{1,0:T(8,128)(2,1)S(1)}, bf16[128,4224]{1,0:T(8,128)(2,1)S(1)}, u32[]{:S(2)}, u32[]{:S(2)}) %collective-permute-start.5) | collective-permute-done | bytes 1081376 | tf_op jit(solution)/shard_map/ppermute | solution.py:305
  82.3 1.6 collective-permute-start.8
  83.9 3.1 %collective-permute-done.6.refs_1_ = bf16[128,4224]{1,0:T(8,128)(2,1)} collective-permute-done((bf16[128,4224]{1,0:T(8,128)(2,1)S(1)}, bf16[128,4224]{1,0:T(8,128)(2,1)}, u32[]{:S(2)}, u32[]{:S(2)}) %collective-permute-start.6) | collective-permute-done | bytes 1081376 | tf_op jit(solution)/shard_map/ppermute | solution.py:305
  87.0 1.8 collective-permute-start.10
  88.7 1.2 slice.7
  90.5 0.7 constant_dynamic-slice_fusion.3
  91.2 1.3 collective-permute-done.7.refs_7_
  92.8 2.7 %collective-permute-start.13 = (bf16[64,2048]{1,0:T(8,128)(2,1)S(1)}, bf16[64,2048]{1,0:T(8,128)(2,1)S(1)}, u32[]{:S(2)}, u32[]{:S(2)}) collective-permute-start(bf16[64,2048]{1,0:T(8,128)(2,1)S(1)} %copy-done.28), channel_id=1, source_target_pairs={{0,8},{4,12},{8,14},{12,10},{14,6},{10,2},{6,0},{2,4},{1,9},{5,13}... | collective-permute-start | bytes 786440 | tf_op jit(solution)/shard_map/ppermute | solution.py:305
  95.5 9.9 %expert_step.8 = (bf16[128,2048]{1,0:T(8,128)(2,1)}, bf16[128,4352]{1,0:T(8,128)(2,1)}, bf16[128,2048]{1,0:T(8,128)(2,1)}, bf16[128,2048]{1,0:T(8,128)(2,1)}, bf...) custom-call(s32[3]{0:T(128)} %pad_add_fusion.scal, bf16[128,4224]{1,0:T(8,128)(2,1)} %copy-done.23, ...), custom_call_target="tpu_custom_call" | custom-call | flops 4026531840 | bytes 9437184 | tf_op jit(solution)/shard_map/expert_step/pallas_call | solution.py:148
  105.5 0.7 constant_dynamic-slice_fusion.2
  106.2 10.0 %collective-permute-done.12.refs_6_ = bf16[64,2048]{1,0:T(8,128)(2,1)S(1)} collective-permute-done((bf16[64,2048]{1,0:T(8,128)(2,1)S(1)}, bf16[64,2048]{1,0:T(8,128)(2,1)S(1)}, u32[]{:S(2)}, u32[]{:S(2)}) %collective-permute-start.12) | collective-permute-done | bytes 262176 | tf_op jit(solution)/shard_map/ppermute | solution.py:305
  116.2 9.8 %expert_step.9 = (bf16[64,2048]{1,0:T(8,128)(2,1)}, bf16[64,4352]{1,0:T(8,128)(2,1)}, bf16[64,2048]{1,0:T(8,128)(2,1)}, bf16[64,2048]{1,0:T(8,128)(2,1)}, bf16[6...) custom-call(s32[3]{0:T(128)} %pad_add_fusion.scal, bf16[128,2048]{1,0:T(8,128)(2,1)} %collective-permute-done.10.refs_0_, ...), custom_call_target="tpu_custom_call" | custom-call | flops 4026531840 | bytes 9437184 | tf_op jit(solution)/shard_map/expert_step/pallas_call | solution.py:148
  126.1 1.9 constant_dynamic-slice_fusion
  128.0 0.7 pad_maximum_fusion.1
  128.8 0.7 pad_maximum_fusion.2
  129.5 2.0 collective-permute-start.16
  131.6 1.4 collective-permute-start.17
  133.0 2.4 %collective-permute-start.18 = (bf16[64,2048]{1,0:T(8,128)(2,1)}, bf16[64,2048]{1,0:T(8,128)(2,1)}, u32[]{:S(2)}, u32[]{:S(2)}) collective-permute-start(bf16[64,2048]{1,0:T(8,128)(2,1)} %get-tuple-element.115), channel_id=1, source_target_pairs={{0,12},{4,14},{8,10},{12,6},{14,2},{10,0},{6,4},{2,8},{1,13},{5,15... | collective-permute-start | bytes 786440 | tf_op jit(solution)/shard_map/ppermute | solution.py:305
  135.4 9.6 %collective-permute-done.17.refs_5_ = bf16[64,2048]{1,0:T(8,128)(2,1)S(1)} collective-permute-done((bf16[64,2048]{1,0:T(8,128)(2,1)S(1)}, bf16[64,2048]{1,0:T(8,128)(2,1)S(1)}, u32[]{:S(2)}, u32[]{:S(2)}) %collective-permute-start.17) | collective-permute-done | bytes 262176 | tf_op jit(solution)/shard_map/ppermute | solution.py:305
  144.9 0.7 copy-done.21
  145.6 8.6 %collective-permute-done.18.refs_3_ = bf16[64,2048]{1,0:T(8,128)(2,1)} collective-permute-done((bf16[64,2048]{1,0:T(8,128)(2,1)}, bf16[64,2048]{1,0:T(8,128)(2,1)}, u32[]{:S(2)}, u32[]{:S(2)}) %collective-permute-start.18) | collective-permute-done | bytes 262176 | tf_op jit(solution)/shard_map/ppermute | solution.py:305
  154.2 1.5 maximum_select_fusion
  155.8 1.1 maximum_select_fusion.1
  156.9 2.0 collective-permute-start.21
  158.8 3.6 %collective-permute-start.22 = (bf16[64,2048]{1,0:T(8,128)(2,1)}, bf16[64,2048]{1,0:T(8,128)(2,1)S(1)}, u32[]{:S(2)}, u32[]{:S(2)}) collective-permute-start(bf16[64,2048]{1,0:T(8,128)(2,1)} %get-tuple-element.121), channel_id=1, source_target_pairs={{0,14},{4,10},{8,6},{12,2},{14,0},{10,4},{6,8},{2,12},{1,15},{5,11... | collective-permute-start | bytes 786440 | tf_op jit(solution)/shard_map/ppermute | solution.py:305
  162.4 7.9 %collective-permute-done.22.refs_4_ = bf16[64,2048]{1,0:T(8,128)(2,1)S(1)} collective-permute-done((bf16[64,2048]{1,0:T(8,128)(2,1)}, bf16[64,2048]{1,0:T(8,128)(2,1)S(1)}, u32[]{:S(2)}, u32[]{:S(2)}) %collective-permute-start.22) | collective-permute-done | bytes 262176 | tf_op jit(solution)/shard_map/ppermute | solution.py:305
  171.0 0.8 maximum_select_fusion.4
  171.8 7.3 %collective-permute-start.24 = (bf16[288,512]{1,0:T(8,128)(2,1)}, bf16[288,512]{1,0:T(8,128)(2,1)S(1)}, u32[]{:S(2)}, u32[]{:S(2)}) collective-permute-start(bf16[288,512]{1,0:T(8,128)(2,1)} %maximum_select_fusion.4), channel_id=1, source_target_pairs={{0,4},{4,8},{8,12},{12,14},{14,10},{10,6},{6,2},{2,0},{1,5},{5,9},... | collective-permute-start | bytes 884744 | tf_op jit(solution)/shard_map/ppermute | solution.py:305
  179.1 1.0 maximum_select_fusion.5
  180.2 5.3 %collective-permute-done.24 = bf16[288,512]{1,0:T(8,128)(2,1)S(1)} collective-permute-done((bf16[288,512]{1,0:T(8,128)(2,1)}, bf16[288,512]{1,0:T(8,128)(2,1)S(1)}, u32[]{:S(2)}, u32[]{:S(2)}) %collective-permute-start.24) | collective-permute-done | bytes 294944 | tf_op jit(solution)/shard_map/ppermute | solution.py:305
  185.7 3.4 %collective-permute-start.25 = (bf16[288,512]{1,0:T(8,128)(2,1)S(1)}, bf16[288,512]{1,0:T(8,128)(2,1)S(1)}, u32[]{:S(2)}, u32[]{:S(2)}) collective-permute-start(bf16[288,512]{1,0:T(8,128)(2,1)S(1)} %maximum_select_fusion.3), channel_id=1, source_target_pairs={{0,4},{4,8},{8,12},{12,14},{14,10},{10,6},{6,2},{2,0},{1,5},{5,9},... | collective-permute-start | bytes 884744 | tf_op jit(solution)/shard_map/ppermute | solution.py:305
  189.1 12.0 %expert_gradient.1 = f32[1,1024,2304]{2,1,0:T(8,128)} custom-call(s32[3]{0:T(128)} %pad_add_fusion.scal, bf16[64,2048]{1,0:T(8,128)(2,1)} %get-tuple-element.129.refs_0_.refs_10_, bf16[128,2048]{1,0:T(8,128)(2,1)} %get-tuple-element.130.refs_1_.refs_11_, bf16[128,2048]{1,0:T(8,128)(2,1)} %get-tuple-element.131.refs_2_.refs_12_, ...), custom_call_target="tpu_custom_call" | custom-call | flops 4831838208 | bytes 14155776 | tf_op jit(solution)/shard_map/expert_gradient/pallas_call | solution.py:219
  201.1 0.8 maximum_select_fusion.2.columns
  202.0 4.6 %shadow_gradient.1 = (f32[288,1024]{1,0:T(8,128)}, bf16[288,1024]{1,0:T(8,128)(2,1)}) custom-call(s32[3]{0:T(128)} %pad_add_fusion.scal, bf16[288,512]{1,0:T(8,128)(2,1)} %maximum_select_fusion.2.columns, bf16[64,2048]{1,0:T(8,128)(2,1)} %get-tuple-element.141.refs_0_, bf16[128,2048]{1,0:T(8,128)(2,1)} %get-tuple-element.142.refs_1_, ...), custom_call_target="tpu_custom_call" | custom-call | flops 1207959552 | bytes 4194304 | tf_op jit(solution)/shard_map/shadow_gradient/pallas_call | solution.py:274
  206.6 3.1 %token_sum.1 = bf16[128,2048]{1,0:T(8,128)(2,1)} custom-call(s32[3]{0:T(128)} %pad_add_fusion.scal, bf16[128,128]{1,0:T(8,128)(2,1)} %copy-done.11, bf16[64,2048]{1,0:T(8,128)(2,1)} %get-tuple-element.87.refs_0_, bf16[64,2048]{1,0:T(8,128)(2,1)} %collective-permute-done.8.refs_1_, bf16[64,2048]{1,0:T(8,128)(2,1)} %copy-done.20, ...), custom_call_target="tpu_custom_call" | custom-call | flops 268435456 | bytes 2097152 | tf_op jit(solution)/shard_map/token_sum/pallas_call | solution.py:183
  209.7 1.2 add_bitcast_fusion
  (100 shorter events, 5.7 us)
Async XLA Ops:
  2.8 15.1 %copy-start.11 = (bf16[128,128]{1,0:T(8,128)(2,1)}, bf16[128,128]{1,0:T(8,128)(2,1)S(1)}, u32[]{:S(2)}) copy-start(bf16[128,128]{1,0:T(8,128)(2,1)S(1)} %pad.5.meta) | copy-start | bytes 98308
  4.1 26.9 %collective-permute-start = (bf16[128,4224]{1,0:T(8,128)(2,1)S(1)}, bf16[128,4224]{1,0:T(8,128)(2,1)S(1)}, u32[]{:S(2)}, u32[]{:S(2)}) collective-permute-start(bf16[128,4224]{1,0:T(8,128)(2,1)S(1)} %pad_maximum_fusion.refs_0_), channel_id=1, source_target_pairs={{0,4},{4,8},{8,12},{12,14},{14,10},{10,6},{6,2},{2,0},{1,5},{5,9},... | collective-permute-start | bytes 3244040 | tf_op jit(solution)/shard_map/ppermute | solution.py:305
  7.2 25.4 %collective-permute-start.1 = (bf16[128,4224]{1,0:T(8,128)(2,1)S(1)}, bf16[128,4224]{1,0:T(8,128)(2,1)}, u32[]{:S(2)}, u32[]{:S(2)}) collective-permute-start(bf16[128,4224]{1,0:T(8,128)(2,1)S(1)} %pad_maximum_fusion.refs_0_), channel_id=1, source_target_pairs={{0,2},{4,0},{8,4},{12,8},{14,12},{10,14},{6,10},{2,6},{1,3},{5,1},... | collective-permute-start | bytes 3244040 | tf_op jit(solution)/shard_map/ppermute | solution.py:305
  32.6 24.4 %collective-permute-start.2 = (bf16[128,4224]{1,0:T(8,128)(2,1)S(1)}, bf16[128,4224]{1,0:T(8,128)(2,1)S(1)}, u32[]{:S(2)}, u32[]{:S(2)}) collective-permute-start(bf16[128,4224]{1,0:T(8,128)(2,1)S(1)} %collective-permute-done.refs_0_), channel_id=1, source_target_pairs={{0,4},{4,8},{8,12},{12,14},{14,10},{10,6},{6,2},{2,0},{1,5},{5,9},... | collective-permute-start | bytes 3244040 | tf_op jit(solution)/shard_map/ppermute | solution.py:305
  34.2 24.3 %collective-permute-start.3 = (bf16[128,4224]{1,0:T(8,128)(2,1)}, bf16[128,4224]{1,0:T(8,128)(2,1)S(1)}, u32[]{:S(2)}, u32[]{:S(2)}) collective-permute-start(bf16[128,4224]{1,0:T(8,128)(2,1)} %collective-permute-done.1.refs_1_), channel_id=1, source_target_pairs={{0,2},{4,0},{8,4},{12,8},{14,12},{10,14},{6,10},{2,6},{1,3},{5,1},... | collective-permute-start | bytes 3244040 | tf_op jit(solution)/shard_map/ppermute | solution.py:305
  34.7 25.9 %collective-permute-start.4 = (bf16[64,4352]{1,0:T(8,128)(2,1)}, bf16[64,4352]{1,0:T(8,128)(2,1)S(1)}, u32[]{:S(2)}, u32[]{:S(2)}) collective-permute-start(bf16[64,4352]{1,0:T(8,128)(2,1)} %get-tuple-element.86.refs_2_.refs_20_), channel_id=1, source_target_pairs={{0,1},{1,0},{2,3},{3,2},{4,5},{5,4},{6,7},{7,6},{8,9},{9,8},{10,11... | collective-permute-start | bytes 1671176 | tf_op jit(solution)/shard_map/ppermute | solution.py:308
  58.6 23.7 %collective-permute-start.5 = (bf16[128,4224]{1,0:T(8,128)(2,1)S(1)}, bf16[128,4224]{1,0:T(8,128)(2,1)S(1)}, u32[]{:S(2)}, u32[]{:S(2)}) collective-permute-start(bf16[128,4224]{1,0:T(8,128)(2,1)S(1)} %collective-permute-done.2.refs_0_), channel_id=1, source_target_pairs={{0,4},{4,8},{8,12},{12,14},{14,10},{10,6},{6,2},{2,0},{1,5},{5,9},... | collective-permute-start | bytes 3244040 | tf_op jit(solution)/shard_map/ppermute | solution.py:305
  60.1 29.7 %collective-permute-start.9 = (bf16[128,4352]{1,0:T(8,128)(2,1)}, bf16[128,4352]{1,0:T(8,128)(2,1)S(1)}, u32[]{:S(2)}, u32[]{:S(2)}) collective-permute-start(bf16[128,4352]{1,0:T(8,128)(2,1)} %get-tuple-element.96.refs_21_), channel_id=1, source_target_pairs={{0,1},{1,0},{2,3},{3,2},{4,5},{5,4},{6,7},{7,6},{8,9},{9,8},{10,11... | collective-permute-start | bytes 3342344 | tf_op jit(solution)/shard_map/ppermute | solution.py:308
  60.1 26.8 %collective-permute-start.6 = (bf16[128,4224]{1,0:T(8,128)(2,1)S(1)}, bf16[128,4224]{1,0:T(8,128)(2,1)}, u32[]{:S(2)}, u32[]{:S(2)}) collective-permute-start(bf16[128,4224]{1,0:T(8,128)(2,1)S(1)} %collective-permute-done.3.refs_1_), channel_id=1, source_target_pairs={{0,2},{4,0},{8,4},{12,8},{14,12},{10,14},{6,10},{2,6},{1,3},{5,1},... | collective-permute-start | bytes 3244040 | tf_op jit(solution)/shard_map/ppermute | solution.py:305
  60.6 10.2 %copy-start.3 = (bf16[64,4352]{1,0:T(8,128)(2,1)}, bf16[64,4352]{1,0:T(8,128)(2,1)S(1)}, u32[]{:S(2)}) copy-start(bf16[64,4352]{1,0:T(8,128)(2,1)S(1)} %collective-permute-done.4.refs_5_.refs_15_.refs_25_) | copy-start | bytes 1671172
  70.8 35.4 %collective-permute-start.14 = (bf16[128,4352]{1,0:T(8,128)(2,1)}, bf16[128,4352]{1,0:T(8,128)(2,1)S(1)}, u32[]{:S(2)}, u32[]{:S(2)}) collective-permute-start(bf16[128,4352]{1,0:T(8,128)(2,1)} %get-tuple-element.106.refs_22_), channel_id=1, source_target_pairs={{0,1},{1,0},{2,3},{3,2},{4,5},{5,4},{6,7},{7,6},{8,9},{9,8},{10,11... | collective-permute-start | bytes 3342344 | tf_op jit(solution)/shard_map/ppermute | solution.py:308
  71.1 21.4 %collective-permute-start.7 = (bf16[64,2048]{1,0:T(8,128)(2,1)}, bf16[64,2048]{1,0:T(8,128)(2,1)}, u32[]{:S(2)}, u32[]{:S(2)}) collective-permute-start(bf16[64,2048]{1,0:T(8,128)(2,1)} %get-tuple-element.94), channel_id=1, source_target_pairs={{0,2},{4,0},{8,4},{12,8},{14,12},{10,14},{6,10},{2,6},{1,3},{5,1},... | collective-permute-start | bytes 786440 | tf_op jit(solution)/shard_map/ppermute | solution.py:305
  82.3 6.4 %copy-start.23 = (bf16[128,4224]{1,0:T(8,128)(2,1)}, bf16[128,4224]{1,0:T(8,128)(2,1)S(1)}, u32[]{:S(2)}) copy-start(bf16[128,4224]{1,0:T(8,128)(2,1)S(1)} %collective-permute-done.5.refs_0_) | copy-start | bytes 3244036
  82.3 10.3 %collective-permute-start.8 = (bf16[64,2048]{1,0:T(8,128)(2,1)}, bf16[64,2048]{1,0:T(8,128)(2,1)}, u32[]{:S(2)}, u32[]{:S(2)}) collective-permute-start(bf16[64,2048]{1,0:T(8,128)(2,1)} %get-tuple-element.95), channel_id=1, source_target_pairs={{0,4},{4,8},{8,12},{12,14},{14,10},{10,6},{6,2},{2,0},{1,5},{5,9},... | collective-permute-start | bytes 786440 | tf_op jit(solution)/shard_map/ppermute | solution.py:305
  87.0 18.4 %collective-permute-start.10 = (bf16[128,2048]{1,0:T(8,128)(2,1)S(1)}, bf16[128,2048]{1,0:T(8,128)(2,1)}, u32[]{:S(2)}, u32[]{:S(2)}) collective-permute-start(bf16[128,2048]{1,0:T(8,128)(2,1)S(1)} %slice.6), channel_id=1, source_target_pairs={{0,4},{4,8},{8,12},{12,14},{14,10},{10,6},{6,2},{2,0},{1,5},{5,9},... | collective-permute-start | bytes 1572872 | tf_op jit(solution)/shard_map/ppermute | solution.py:305
  89.9 15.5 %copy-start = (bf16[128,4352]{1,0:T(8,128)(2,1)}, bf16[128,4352]{1,0:T(8,128)(2,1)S(1)}, u32[]{:S(2)}) copy-start(bf16[128,4352]{1,0:T(8,128)(2,1)S(1)} %collective-permute-done.9.refs_6_.refs_16_.refs_26_) | copy-start | bytes 3342340
  89.9 16.3 %collective-permute-start.11 = (bf16[128,2176]{1,0:T(8,128)(2,1)S(1)}, bf16[128,2176]{1,0:T(8,128)(2,1)S(1)}, u32[]{:S(2)}, u32[]{:S(2)}) collective-permute-start(bf16[128,2176]{1,0:T(8,128)(2,1)S(1)} %slice.7), channel_id=1, source_target_pairs={{0,2},{4,0},{8,4},{12,8},{14,12},{10,14},{6,10},{2,6},{1,3},{5,1},... | collective-permute-start | bytes 1671176 | tf_op jit(solution)/shard_map/ppermute | solution.py:305
  91.2 14.3 %copy-start.7 = (bf16[2304,128]{1,0:T(8,128)(2,1)S(1)}, bf16[2304,128]{1,0:T(8,128)(2,1)}, u32[]{:S(2)}) copy-start(bf16[2304,128]{1,0:T(8,128)(2,1)} %get-tuple-element.109) | copy-start | bytes 1769476
  92.5 23.6 %collective-permute-start.12 = (bf16[64,2048]{1,0:T(8,128)(2,1)S(1)}, bf16[64,2048]{1,0:T(8,128)(2,1)S(1)}, u32[]{:S(2)}, u32[]{:S(2)}) collective-permute-start(bf16[64,2048]{1,0:T(8,128)(2,1)S(1)} %copy-done.29), channel_id=1, source_target_pairs={{0,6},{4,2},{8,0},{12,4},{14,8},{10,12},{6,14},{2,10},{1,7},{5,3},... | collective-permute-start | bytes 786440 | tf_op jit(solution)/shard_map/ppermute | solution.py:305
  92.8 23.4 %collective-permute-start.13 = (bf16[64,2048]{1,0:T(8,128)(2,1)S(1)}, bf16[64,2048]{1,0:T(8,128)(2,1)S(1)}, u32[]{:S(2)}, u32[]{:S(2)}) collective-permute-start(bf16[64,2048]{1,0:T(8,128)(2,1)S(1)} %copy-done.28), channel_id=1, source_target_pairs={{0,8},{4,12},{8,14},{12,10},{14,6},{10,2},{6,0},{2,4},{1,9},{5,13}... | collective-permute-start | bytes 786440 | tf_op jit(solution)/shard_map/ppermute | solution.py:305
  105.4 48.8 %collective-permute-start.19 = (bf16[128,4352]{1,0:T(8,128)(2,1)}, bf16[128,4352]{1,0:T(8,128)(2,1)S(1)}, u32[]{:S(2)}, u32[]{:S(2)}) collective-permute-start(bf16[128,4352]{1,0:T(8,128)(2,1)} %get-tuple-element.116.refs_23_), channel_id=1, source_target_pairs={{0,1},{1,0},{2,3},{3,2},{4,5},{5,4},{6,7},{7,6},{8,9},{9,8},{10,11... | collective-permute-start | bytes 3342344 | tf_op jit(solution)/shard_map/ppermute | solution.py:308
  106.2 10.0 %copy-start.27 = (bf16[128,2176]{1,0:T(8,128)(2,1)}, bf16[128,2176]{1,0:T(8,128)(2,1)S(1)}, u32[]{:S(2)}) copy-start(bf16[128,2176]{1,0:T(8,128)(2,1)S(1)} %collective-permute-done.11.refs_1_) | copy-start | bytes 1671172
  106.2 19.9 %copy-start.9 = (bf16[2304,128]{1,0:T(8,128)(2,1)S(1)}, bf16[2304,128]{1,0:T(8,128)(2,1)}, u32[]{:S(2)}) copy-start(bf16[2304,128]{1,0:T(8,128)(2,1)} %get-tuple-element.110) | copy-start | bytes 1769476
  106.2 19.9 %copy-start.1 = (bf16[128,4352]{1,0:T(8,128)(2,1)}, bf16[128,4352]{1,0:T(8,128)(2,1)S(1)}, u32[]{:S(2)}) copy-start(bf16[128,4352]{1,0:T(8,128)(2,1)S(1)} %collective-permute-done.14.refs_7_.refs_17_.refs_27_) | copy-start | bytes 3342340
  116.2 9.9 %copy-start.19 = (bf16[64,2048]{1,0:T(8,128)(2,1)}, bf16[64,2048]{1,0:T(8,128)(2,1)S(1)}, u32[]{:S(2)}) copy-start(bf16[64,2048]{1,0:T(8,128)(2,1)S(1)} %collective-permute-done.12.refs_6_) | copy-start | bytes 786436
  116.2 9.9 %copy-start.20 = (bf16[64,2048]{1,0:T(8,128)(2,1)}, bf16[64,2048]{1,0:T(8,128)(2,1)S(1)}, u32[]{:S(2)}) copy-start(bf16[64,2048]{1,0:T(8,128)(2,1)S(1)} %collective-permute-done.13.refs_2_) | copy-start | bytes 786436
  128.0 17.6 %copy-start.10 = (bf16[64,4352]{1,0:T(8,128)(2,1)S(1)}, bf16[64,4352]{1,0:T(8,128)(2,1)}, u32[]{:S(2)}) copy-start(bf16[64,4352]{1,0:T(8,128)(2,1)} %get-tuple-element.122.refs_24_) | copy-start | bytes 1671172
  128.0 26.2 %copy-start.14 = (bf16[288,128]{1,0:T(8,128)(2,1)S(1)}, bf16[288,128]{1,0:T(8,128)(2,1)}, u32[]{:S(2)}) copy-start(bf16[288,128]{1,0:T(8,128)(2,1)} %get-tuple-element.158) | copy-start | bytes 221188
  128.0 27.8 %copy-start.13 = (bf16[288,128]{1,0:T(8,128)(2,1)S(1)}, bf16[288,128]{1,0:T(8,128)(2,1)}, u32[]{:S(2)}) copy-start(bf16[288,128]{1,0:T(8,128)(2,1)} %get-tuple-element.157) | copy-start | bytes 221188
  128.8 25.4 %collective-permute-start.15 = (bf16[288,512]{1,0:T(8,128)(2,1)}, bf16[288,512]{1,0:T(8,128)(2,1)}, u32[]{:S(2)}, u32[]{:S(2)}) collective-permute-start(bf16[288,512]{1,0:T(8,128)(2,1)} %pad_maximum_fusion.1), channel_id=1, source_target_pairs={{0,4},{4,8},{8,12},{12,14},{14,10},{10,6},{6,2},{2,0},{1,5},{5,9},... | collective-permute-start | bytes 884744 | tf_op jit(solution)/shard_map/ppermute | solution.py:305
  128.8 42.2 %copy-start.12 = (bf16[288,128]{1,0:T(8,128)(2,1)S(1)}, bf16[288,128]{1,0:T(8,128)(2,1)}, u32[]{:S(2)}) copy-start(bf16[288,128]{1,0:T(8,128)(2,1)} %get-tuple-element.154) | copy-start | bytes 221188
  129.5 24.7 %collective-permute-start.16 = (bf16[288,512]{1,0:T(8,128)(2,1)}, bf16[288,512]{1,0:T(8,128)(2,1)}, u32[]{:S(2)}, u32[]{:S(2)}) collective-permute-start(bf16[288,512]{1,0:T(8,128)(2,1)} %pad_maximum_fusion.2), channel_id=1, source_target_pairs={{0,2},{4,0},{8,4},{12,8},{14,12},{10,14},{6,10},{2,6},{1,3},{5,1},... | collective-permute-start | bytes 884744 | tf_op jit(solution)/shard_map/ppermute | solution.py:305
  131.6 13.4 %collective-permute-start.17 = (bf16[64,2048]{1,0:T(8,128)(2,1)S(1)}, bf16[64,2048]{1,0:T(8,128)(2,1)S(1)}, u32[]{:S(2)}, u32[]{:S(2)}) collective-permute-start(bf16[64,2048]{1,0:T(8,128)(2,1)S(1)} %copy-done.30), channel_id=1, source_target_pairs={{0,10},{4,6},{8,2},{12,0},{14,4},{10,8},{6,12},{2,14},{1,11},{5,7}... | collective-permute-start | bytes 786440 | tf_op jit(solution)/shard_map/ppermute | solution.py:305
  133.0 21.2 %collective-permute-start.18 = (bf16[64,2048]{1,0:T(8,128)(2,1)}, bf16[64,2048]{1,0:T(8,128)(2,1)}, u32[]{:S(2)}, u32[]{:S(2)}) collective-permute-start(bf16[64,2048]{1,0:T(8,128)(2,1)} %get-tuple-element.115), channel_id=1, source_target_pairs={{0,12},{4,14},{8,10},{12,6},{14,2},{10,0},{6,4},{2,8},{1,13},{5,15... | collective-permute-start | bytes 786440 | tf_op jit(solution)/shard_map/ppermute | solution.py:305
  145.6 24.7 %collective-permute-start.23 = (bf16[64,4352]{1,0:T(8,128)(2,1)S(1)}, bf16[64,4352]{1,0:T(8,128)(2,1)S(1)}, u32[]{:S(2)}, u32[]{:S(2)}) collective-permute-start(bf16[64,4352]{1,0:T(8,128)(2,1)S(1)} %copy-done.10), channel_id=1, source_target_pairs={{0,1},{1,0},{2,3},{3,2},{4,5},{5,4},{6,7},{7,6},{8,9},{9,8},{10,11... | collective-permute-start | bytes 1671176 | tf_op jit(solution)/shard_map/ppermute | solution.py:308
  154.2 17.6 %copy-start.2 = (bf16[128,4352]{1,0:T(8,128)(2,1)}, bf16[128,4352]{1,0:T(8,128)(2,1)S(1)}, u32[]{:S(2)}) copy-start(bf16[128,4352]{1,0:T(8,128)(2,1)S(1)} %collective-permute-done.19.refs_8_.refs_18_.refs_28_) | copy-start | bytes 3342340
  155.7 15.3 %collective-permute-start.20 = (bf16[288,512]{1,0:T(8,128)(2,1)S(1)}, bf16[288,512]{1,0:T(8,128)(2,1)S(1)}, u32[]{:S(2)}, u32[]{:S(2)}) collective-permute-start(bf16[288,512]{1,0:T(8,128)(2,1)S(1)} %maximum_select_fusion), channel_id=1, source_target_pairs={{0,4},{4,8},{8,12},{12,14},{14,10},{10,6},{6,2},{2,0},{1,5},{5,9},... | collective-permute-start | bytes 884744 | tf_op jit(solution)/shard_map/ppermute | solution.py:305
  156.9 14.1 %collective-permute-start.21 = (bf16[288,512]{1,0:T(8,128)(2,1)S(1)}, bf16[288,512]{1,0:T(8,128)(2,1)}, u32[]{:S(2)}, u32[]{:S(2)}) collective-permute-start(bf16[288,512]{1,0:T(8,128)(2,1)S(1)} %maximum_select_fusion.1), channel_id=1, source_target_pairs={{0,2},{4,0},{8,4},{12,8},{14,12},{10,14},{6,10},{2,6},{1,3},{5,1},... | collective-permute-start | bytes 884744 | tf_op jit(solution)/shard_map/ppermute | solution.py:305
  158.8 11.5 %collective-permute-start.22 = (bf16[64,2048]{1,0:T(8,128)(2,1)}, bf16[64,2048]{1,0:T(8,128)(2,1)S(1)}, u32[]{:S(2)}, u32[]{:S(2)}) collective-permute-start(bf16[64,2048]{1,0:T(8,128)(2,1)} %get-tuple-element.121), channel_id=1, source_target_pairs={{0,14},{4,10},{8,6},{12,2},{14,0},{10,4},{6,8},{2,12},{1,15},{5,11... | collective-permute-start | bytes 786440 | tf_op jit(solution)/shard_map/ppermute | solution.py:305
  170.3 15.3 %copy-start.4 = (bf16[64,4352]{1,0:T(8,128)(2,1)}, bf16[64,4352]{1,0:T(8,128)(2,1)S(1)}, u32[]{:S(2)}) copy-start(bf16[64,4352]{1,0:T(8,128)(2,1)S(1)} %collective-permute-done.23.refs_9_.refs_19_.refs_29_) | copy-start | bytes 1671172
  171.8 13.7 %collective-permute-start.24 = (bf16[288,512]{1,0:T(8,128)(2,1)}, bf16[288,512]{1,0:T(8,128)(2,1)S(1)}, u32[]{:S(2)}, u32[]{:S(2)}) collective-permute-start(bf16[288,512]{1,0:T(8,128)(2,1)} %maximum_select_fusion.4), channel_id=1, source_target_pairs={{0,4},{4,8},{8,12},{12,14},{14,10},{10,6},{6,2},{2,0},{1,5},{5,9},... | collective-permute-start | bytes 884744 | tf_op jit(solution)/shard_map/ppermute | solution.py:305
  180.2 20.9 %collective-permute-start.26 = (bf16[288,512]{1,0:T(8,128)(2,1)S(1)}, bf16[288,512]{1,0:T(8,128)(2,1)S(1)}, u32[]{:S(2)}, u32[]{:S(2)}) collective-permute-start(bf16[288,512]{1,0:T(8,128)(2,1)S(1)} %maximum_select_fusion.5), channel_id=1, source_target_pairs={{0,2},{4,0},{8,4},{12,8},{14,12},{10,14},{6,10},{2,6},{1,3},{5,1},... | collective-permute-start | bytes 884744 | tf_op jit(solution)/shard_map/ppermute | solution.py:305
  185.7 15.4 %collective-permute-start.25 = (bf16[288,512]{1,0:T(8,128)(2,1)S(1)}, bf16[288,512]{1,0:T(8,128)(2,1)S(1)}, u32[]{:S(2)}, u32[]{:S(2)}) collective-permute-start(bf16[288,512]{1,0:T(8,128)(2,1)S(1)} %maximum_select_fusion.3), channel_id=1, source_target_pairs={{0,4},{4,8},{8,12},{12,14},{14,10},{10,6},{6,2},{2,0},{1,5},{5,9},... | collective-permute-start | bytes 884744 | tf_op jit(solution)/shard_map/ppermute | solution.py:305
  189.1 12.0 %copy-start.15 = (bf16[288,128]{1,0:T(8,128)(2,1)S(1)}, bf16[288,128]{1,0:T(8,128)(2,1)}, u32[]{:S(2)}) copy-start(bf16[288,128]{1,0:T(8,128)(2,1)} %get-tuple-element.156) | copy-start | bytes 221188
  189.1 12.1 %copy-start.16 = (bf16[288,128]{1,0:T(8,128)(2,1)S(1)}, bf16[288,128]{1,0:T(8,128)(2,1)}, u32[]{:S(2)}) copy-start(bf16[288,128]{1,0:T(8,128)(2,1)} %get-tuple-element.164) | copy-start | bytes 221188
  189.1 12.1 %copy-start.17 = (bf16[288,128]{1,0:T(8,128)(2,1)S(1)}, bf16[288,128]{1,0:T(8,128)(2,1)}, u32[]{:S(2)}) copy-start(bf16[288,128]{1,0:T(8,128)(2,1)} %get-tuple-element.180) | copy-start | bytes 221188
  189.1 12.1 %copy-start.18 = (bf16[288,128]{1,0:T(8,128)(2,1)S(1)}, bf16[288,128]{1,0:T(8,128)(2,1)}, u32[]{:S(2)}) copy-start(bf16[288,128]{1,0:T(8,128)(2,1)} %get-tuple-element.192) | copy-start | bytes 221188
  206.5 3.1 %collective-permute-start.27 = (bf16[288,1024]{1,0:T(8,128)(2,1)}, bf16[288,1024]{1,0:T(8,128)(2,1)S(1)}, u32[]{:S(2)}, u32[]{:S(2)}) collective-permute-start(bf16[288,1024]{1,0:T(8,128)(2,1)} %get-tuple-element.152), channel_id=1, source_target_pairs={{0,1},{1,0},{2,3},{3,2},{4,5},{5,4},{6,7},{7,6},{8,9},{9,8},{10,11... | collective-permute-start | bytes 1769480 | tf_op jit(solution)/shard_map/ppermute | solution.py:308
  (11 other events, 33.1 us)

commit v3 on v2

--- a/solution.py
+++ b/solution.py
@@ -230,16 +230,19 @@
     )(scal, *rows, *rows, *packs, *others)
 
 
-def shadow_kernel(plan, experts, capacity, scal, columns, *refs):
+def shadow_kernel(plan, experts, capacity, scal, kept, ahead, behind, *refs):
     count = len(plan)
     ins, cots = refs[:count], refs[count : 2 * count]
     mine, theirs, rows_in, rows_cot, total = refs[2 * count :]
     own, half, hottest = scal[0], scal[1], scal[2]
     shift = to_ring(own, experts) - to_ring(hottest, experts)
-    taken = columns.shape[0]
+    taken = kept.shape[0]
     gates = taken * experts * 2 // 3
-    column = own * taken + lax.broadcasted_iota(jnp.int32, columns.shape, 0)
+    column = own * taken + lax.broadcasted_iota(jnp.int32, kept.shape, 0)
     blank = jnp.zeros((), BF16)
+    away = (shift + experts) % experts
+    received = jnp.where(away <= experts // 2, ahead[...], behind[...])
+    columns = jnp.where(away == 0, kept[...], received)
 
     def in_order(parts, rows):
         for steps, part in zip(plan, parts):
@@ -251,7 +254,7 @@
     @pl.when(own * taken < gates)
     def _():
         in_order(ins, rows_in)
-        total[...] = dot(jnp.where(column < gates, columns[...], blank), rows_in[...], (1, 0))
+        total[...] = dot(jnp.where(column < gates, columns, blank), rows_in[...], (1, 0))
 
     @pl.when(own * taken >= gates)
     def _():
@@ -260,7 +263,7 @@
     @pl.when((own + 1) * taken > gates)
     def _():
         in_order(cots, rows_cot)
-        total[...] += dot(jnp.where(column < gates, blank, columns[...]), rows_cot[...], (1, 0))
+        total[...] += dot(jnp.where(column < gates, blank, columns), rows_cot[...], (1, 0))
 
     width = total.shape[1] // 2
     mine[...] = total[:, pl.ds(pl.multiple_of(half * width, width), width)]
@@ -269,7 +272,7 @@
 
 def shadow_gradient(plan, experts, capacity, scal, columns, ins, cots):
     vmem = pl.BlockSpec(memory_space=pltpu.VMEM)
-    taken, rows = columns.shape
+    taken, rows = columns[0].shape
     width = ins[0].shape[1]
     return pl.pallas_call(
         functools.partial(shadow_kernel, plan, experts, capacity),
@@ -277,7 +280,7 @@
             jax.ShapeDtypeStruct((taken, width // 2), F32),
             jax.ShapeDtypeStruct((taken, width // 2), BF16),
         ],
-        in_specs=[pl.BlockSpec(memory_space=pltpu.SMEM)] + [vmem] * (2 * len(ins) + 1),
+        in_specs=[pl.BlockSpec(memory_space=pltpu.SMEM)] + [vmem] * (2 * len(ins) + 3),
         out_specs=[vmem] * 2,
         scratch_shapes=[pltpu.VMEM((rows, width), BF16)] * 2 + [pltpu.VMEM((taken, width), F32)],
         compiler_params=pltpu.CompilerParams(vmem_limit_bytes=VMEM_BYTES),
@@ -285,7 +288,7 @@
             flops=4 * taken * rows * width, bytes_accessed=4 * rows * width, transcendentals=0
         ),
         name="shadow_gradient",
-    )(scal, columns, *ins, *cots)
+    )(scal, *columns, *ins, *cots)
 
 
 def on_device(
@@ -327,8 +330,8 @@
             following = [shift(up, 1), shift(below, -1)]
         elif number + 1 == half:
             following = [shift(up[:, :width], 1), shift(below[:, width:], -1)]
-        if number > 1:
-            held, late[number - 2] = lax.optimization_barrier((held, late[number - 2]))
+        if 0 < number < half:
+            held, late[number - 1] = lax.optimization_barrier((held, late[number - 1]))
         (rows, pack, hot_rows, hot_cots), back, turn = run_step(
             steps, fanout, capacity, scal, held, packs[0] if number == half else None, gate_up, down
         )
@@ -352,32 +355,32 @@
         parts = [lax.dynamic_slice_in_dim(part, owner * taken, taken, axis=0) for part in turned]
         return jnp.concatenate(parts, axis=1)
 
-    ahead, behind = None, None
-    for number in range(half):
-        part = chunk(half - number)
-        if 0 < number < 3:
-            at = half - 2 + number
-            (ahead, behind), late[at] = lax.optimization_barrier(((ahead, behind), late[at]))
-        ahead = shift(part if ahead is None else jnp.where(is_hot, part, ahead), 1)
+    own_part = chunk(0)
+    first_parts = [chunk(half), chunk(1 - half)]
+    first_parts, late[half - 1] = lax.optimization_barrier((first_parts, late[half - 1]))
+    around = [shift(first_parts[0], 1), shift(first_parts[1], -1)]
+    for number in range(1, half):
+        if number == 1:
+            around, late[half] = lax.optimization_barrier((around, (late[half][0], late[half][1])))
+            others = [other for _, other in late]
+            expert_grad = expert_gradient(units, scal, mine, packs, others)
+        if number == 2:
+            around, expert_grad = lax.optimization_barrier((around, expert_grad))
+        ahead = jnp.where(is_hot, chunk(half - number), around[0])
         if number < half - 1:
-            part = chunk(number + 1 - half)
-            behind = shift(part if behind is None else jnp.where(is_hot, part, behind), -1)
-    for steps, (sent, other) in zip(plan, late):
-        others.append(other)
+            behind = jnp.where(is_hot, chunk(number + 1 - half), around[1])
+            around = [shift(ahead, 1), shift(behind, -1)]
+        else:
+            around = [shift(ahead, 1), around[1]]
+    for steps, (sent, _) in zip(plan, late):
         for step, part in zip(steps, sent):
             returned[step % experts] = part
-
-    expert_grad = expert_gradient(units, scal, mine, packs, others)
-
-    away = (to_ring(own, experts) - ring_hot + experts) % experts
-    columns = jnp.where(away == 0, chunk(0), jnp.where(away <= half, ahead, behind))
-    columns, expert_grad = lax.optimization_barrier((columns, expert_grad))
+    token_grad = combine(experts, fanout, capacity, scal, meta, [returned[d] for d in range(experts)])
+    around, token_grad = lax.optimization_barrier((around, token_grad))
     shadow_mine, shadow_theirs = shadow_gradient(
-        plan, experts, capacity, scal, columns, hot_in, hot_cot
+        plan, experts, capacity, scal, [own_part] + around, hot_in, hot_cot
     )
     shadow_grad = (shadow_mine + swap(shadow_theirs).astype(F32)).T
-
-    token_grad = combine(experts, fanout, capacity, scal, meta, [returned[d] for d in range(experts)])
     return (token_grad, expert_grad, shadow_grad)
 
 

time: 213 us -> 199 us (0.934)
  starting transfers between devices: 36.9 us -> 31.5 us
  waiting for transfers between devices: 85.9 us -> 80.9 us
  other arithmetic: 12 us -> 9.67 us
    ppermute x22, waiting for transfers between devices: 85.9 us -> 78.7 us  [shift(): return lax.ppermute(block, 'expert', pairs)]
    ppermute x22, starting transfers between devices: 36.6 us -> 31.2 us  [shift(): return lax.ppermute(block, 'expert', pairs)]
    select_n x6 -> x5, other arithmetic: 5.34 us -> 1.56 us  [the longest x2 1.31 us: on_device(): behind = jnp.where(is_hot, chunk(number + 1 - half), around[1])]
    unnamed x62 -> x70, local copies, waits for them, and re-layouts: 0.81 us -> 3.13 us
    ppermute x6, waiting for transfers between devices: 0.02 us -> 2.22 us  [swap(): return lax.ppermute(block, 'dp', [(0, 1), (1, 0)])]
  transfers between devices with their start and end apart: 28 -> 28, of which waited for: 13 -> 14; matrix products, arithmetic and copies ran while one was open for 5% -> 2% of each run, Pallas kernels for 30% -> 32%
where the time goes in v3:
time: 199 us; the launch traced here: 198 us
  waiting for transfers between devices  80.9 us (41%)
  Pallas kernels  69.3 us (35%)
  starting transfers between devices  31.5 us (16%)
  other arithmetic  9.67 us (5%)
  local copies, waits for them, and re-layouts  4.98 us (3%)
  between operations  2.01 us (1%)
    ppermute x22, waiting for transfers between devices, shift(): return lax.ppermute(block, 'expert', pairs)  78.7 us
    pallas_call x5, Pallas kernels, run_step(): pl.pallas_call(functools.partial(step_kernel, steps, fanout, capacity, jo...  49.4 us
    ppermute x22, starting transfers between devices, shift(): return lax.ppermute(block, 'expert', pairs)  31.2 us
    pallas_call x1, Pallas kernels, expert_gradient(): pl.pallas_call(functools.partial(gradient_kernel, units, count), grid=(ti...  12 us
    pallas_call x1, Pallas kernels, shadow_gradient(): pl.pallas_call(functools.partial(shadow_kernel, plan, experts, capacity),...  4.84 us
  transfers between devices with their start and end apart: 28, of which 14 were waited for; matrix products, arithmetic and copies ran while one was open for 2% of the time, Pallas kernels for 32%

profile of v3, /device:TPU:0, one launch (start us, length us, event | category | flops | bytes accessed | tf_op | source)
XLA Modules:
  0.0 198.4 jit_solution(5424478650177789613)
XLA Ops:
  0.6 0.7 convert_convert_fusion
  1.3 0.7 convert_element_type.14
  2.0 0.7 reduce-precision_convert_fusion.1
  2.8 1.3 pad_maximum_fusion.refs_0_
  4.1 3.0 %collective-permute-start.1 = (bf16[128,4224]{1,0:T(8,128)(2,1)S(1)}, bf16[128,4224]{1,0:T(8,128)(2,1)}, u32[]{:S(2)}, u32[]{:S(2)}) collective-permute-start(bf16[128,4224]{1,0:T(8,128)(2,1)S(1)} %pad_maximum_fusion.refs_0_), channel_id=1, source_target_pairs={{0,2},{4,0},{8,4},{12,8},{14,12},{10,14},{6,10},{2,6},{1,3},{5,1},... | collective-permute-start | bytes 3244040 | tf_op jit(solution)/shard_map/ppermute | solution.py:308
  8.6 9.4 %expert_step.5 = (bf16[64,2048]{1,0:T(8,128)(2,1)}, bf16[64,4352]{1,0:T(8,128)(2,1)}, bf16[64,2048]{1,0:T(8,128)(2,1)}, bf16[64,2048]{1,0:T(8,128)(2,1)}, bf16[64,2048]{1,0:T(8,128)(2,1)}) custom-call(s32[3]{0:T(128)} %pad_add_fusion.scal, bf16[128,4224]{1,0:T(8,128)(2,1)} %copy-done.5, bf16[2048,1536]{1,0:T(8,128)(2,1)} %bitcast.13, bf16[768,2048]{1,0:T(8,128)(2,1)} %bitcast.18), custom_call_target="tpu_custom_call" | custom-call | flops 4026531840 | bytes 9437184 | tf_op jit(solution)/shard_map/expert_step/pallas_call | solution.py:148
  18.1 13.1 %collective-permute-done.1.refs_1_ = bf16[128,4224]{1,0:T(8,128)(2,1)} collective-permute-done((bf16[128,4224]{1,0:T(8,128)(2,1)S(1)}, bf16[128,4224]{1,0:T(8,128)(2,1)}, u32[]{:S(2)}, u32[]{:S(2)}) %collective-permute-start.1) | collective-permute-done | bytes 1081376 | tf_op jit(solution)/shard_map/ppermute | solution.py:308
  31.2 1.4 collective-permute-done.refs_0_
  33.0 1.6 collective-permute-start.4
  34.6 10.1 %expert_step.6 = (bf16[128,2048]{1,0:T(8,128)(2,1)}, bf16[128,4352]{1,0:T(8,128)(2,1)}, bf16[128,2048]{1,0:T(8,128)(2,1)}, bf16[128,2048]{1,0:T(8,128)(2,1)}, bf...) custom-call(s32[3]{0:T(128)} %pad_add_fusion.scal, ...), custom_call_target="tpu_custom_call" | custom-call | flops 4026531840 | bytes 9437184 | tf_op jit(solution)/shard_map/expert_step/pallas_call | solution.py:148
  44.8 12.4 %collective-permute-done.3.refs_0_ = bf16[128,4224]{1,0:T(8,128)(2,1)S(1)} collective-permute-done((bf16[128,4224]{1,0:T(8,128)(2,1)}, bf16[128,4224]{1,0:T(8,128)(2,1)S(1)}, u32[]{:S(2)}, u32[]{:S(2)}) %collective-permute-start.3) | collective-permute-done | bytes 1081376 | tf_op jit(solution)/shard_map/ppermute | solution.py:308
  57.7 1.3 collective-permute-start.5
  59.0 0.7 collective-permute-start.6
  59.7 1.5 collective-permute-start.8
  61.7 5.4 %collective-permute-done.5.refs_7_ = bf16[64,2048]{1,0:T(8,128)(2,1)S(1)} collective-permute-done((bf16[64,2048]{1,0:T(8,128)(2,1)}, bf16[64,2048]{1,0:T(8,128)(2,1)S(1)}, u32[]{:S(2)}, u32[]{:S(2)}) %collective-permute-start.5) | collective-permute-done | bytes 262176 | tf_op jit(solution)/shard_map/ppermute | solution.py:308
  67.1 1.3 collective-permute-done.6.refs_1_
  68.4 10.0 %expert_step.7 = (bf16[128,2048]{1,0:T(8,128)(2,1)}, bf16[128,4352]{1,0:T(8,128)(2,1)}, bf16[128,2048]{1,0:T(8,128)(2,1)}, bf16[128,2048]{1,0:T(8,128)(2,1)}, bf...) custom-call(s32[3]{0:T(128)} %pad_add_fusion.scal, bf16[128,4224]{1,0:T(8,128)(2,1)} %copy-done.31, ...), custom_call_target="tpu_custom_call" | custom-call | flops 4026531840 | bytes 9437184 | tf_op jit(solution)/shard_map/expert_step/pallas_call | solution.py:148
  78.5 9.4 %collective-permute-done.8.refs_0_ = bf16[128,4224]{1,0:T(8,128)(2,1)S(1)} collective-permute-done((bf16[128,4224]{1,0:T(8,128)(2,1)S(1)}, bf16[128,4224]{1,0:T(8,128)(2,1)S(1)}, u32[]{:S(2)}, u32[]{:S(2)}) %collective-permute-start.8) | collective-permute-done | bytes 1081376 | tf_op jit(solution)/shard_map/ppermute | solution.py:308
  87.9 2.6 %collective-permute-start.10 = (bf16[64,2048]{1,0:T(8,128)(2,1)}, bf16[64,2048]{1,0:T(8,128)(2,1)S(1)}, u32[]{:S(2)}, u32[]{:S(2)}) collective-permute-start(bf16[64,2048]{1,0:T(8,128)(2,1)} %get-tuple-element.104), channel_id=1, source_target_pairs={{0,6},{4,2},{8,0},{12,4},{14,8},{10,12},{6,14},{2,10},{1,7},{5,3},... | collective-permute-start | bytes 786440 | tf_op jit(solution)/shard_map/ppermute | solution.py:308
  90.9 1.1 collective-permute-start.13
  92.1 1.8 collective-permute-start.14
  93.9 7.3 %collective-permute-done.10.refs_6_ = bf16[64,2048]{1,0:T(8,128)(2,1)S(1)} collective-permute-done((bf16[64,2048]{1,0:T(8,128)(2,1)}, bf16[64,2048]{1,0:T(8,128)(2,1)S(1)}, u32[]{:S(2)}, u32[]{:S(2)}) %collective-permute-start.10) | collective-permute-done | bytes 262176 | tf_op jit(solution)/shard_map/ppermute | solution.py:308
  101.1 2.1 %collective-permute-done.11.refs_2_ = bf16[64,2048]{1,0:T(8,128)(2,1)S(1)} collective-permute-done((bf16[64,2048]{1,0:T(8,128)(2,1)}, bf16[64,2048]{1,0:T(8,128)(2,1)S(1)}, u32[]{:S(2)}, u32[]{:S(2)}) %collective-permute-start.11) | collective-permute-done | bytes 262176 | tf_op jit(solution)/shard_map/ppermute | solution.py:308
  103.2 0.7 copy-done.27
  103.9 10.4 %expert_step.8 = (bf16[128,2048]{1,0:T(8,128)(2,1)}, bf16[128,4352]{1,0:T(8,128)(2,1)}, bf16[128,2048]{1,0:T(8,128)(2,1)}, bf16[128,2048]{1,0:T(8,128)(2,1)}, bf...) custom-call(s32[3]{0:T(128)} %pad_add_fusion.scal, bf16[128,4224]{1,0:T(8,128)(2,1)} %copy-done.30, ...), custom_call_target="tpu_custom_call" | custom-call | flops 4026531840 | bytes 9437184 | tf_op jit(solution)/shard_map/expert_step/pallas_call | solution.py:148
  114.7 0.8 constant_dynamic-slice_fusion.3
  115.5 0.8 constant_dynamic-slice_fusion.2
  116.2 3.2 %collective-permute-start.15 = (bf16[64,2048]{1,0:T(8,128)(2,1)S(1)}, bf16[64,2048]{1,0:T(8,128)(2,1)S(1)}, u32[]{:S(2)}, u32[]{:S(2)}) collective-permute-start(bf16[64,2048]{1,0:T(8,128)(2,1)S(1)} %copy-done.34), channel_id=1, source_target_pairs={{0,10},{4,6},{8,2},{12,0},{14,4},{10,8},{6,12},{2,14},{1,11},{5,7}... | collective-permute-start | bytes 786440 | tf_op jit(solution)/shard_map/ppermute | solution.py:308
  120.1 9.6 %expert_step.9 = (bf16[64,2048]{1,0:T(8,128)(2,1)}, bf16[64,4352]{1,0:T(8,128)(2,1)}, bf16[64,2048]{1,0:T(8,128)(2,1)}, bf16[64,2048]{1,0:T(8,128)(2,1)}, bf16[6...) custom-call(s32[3]{0:T(128)} %pad_add_fusion.scal, bf16[128,2048]{1,0:T(8,128)(2,1)} %collective-permute-done.13.refs_0_, ...), custom_call_target="tpu_custom_call" | custom-call | flops 4026531840 | bytes 9437184 | tf_op jit(solution)/shard_map/expert_step/pallas_call | solution.py:148
  129.9 0.9 copy-done.9
  130.9 0.9 pad_maximum_fusion.1
  131.8 8.8 %collective-permute-done.16.refs_3_ = bf16[64,2048]{1,0:T(8,128)(2,1)S(1)} collective-permute-done((bf16[64,2048]{1,0:T(8,128)(2,1)S(1)}, bf16[64,2048]{1,0:T(8,128)(2,1)S(1)}, u32[]{:S(2)}, u32[]{:S(2)}) %collective-permute-start.16) | collective-permute-done | bytes 262176 | tf_op jit(solution)/shard_map/ppermute | solution.py:308
  140.6 0.7 copy-done.29
  141.3 2.0 %collective-permute-start.19 = (bf16[288,512]{1,0:T(8,128)(2,1)}, bf16[288,512]{1,0:T(8,128)(2,1)}, u32[]{:S(2)}, u32[]{:S(2)}) collective-permute-start(bf16[288,512]{1,0:T(8,128)(2,1)} %get-tuple-element.119), channel_id=1, source_target_pairs={{0,2},{4,0},{8,4},{12,8},{14,12},{10,14},{6,10},{2,6},{1,3},{5,1},... | collective-permute-start | bytes 884744 | tf_op jit(solution)/shard_map/ppermute | solution.py:308
  143.4 1.2 collective-permute-start.20
  144.6 11.2 %collective-permute-done.20.refs_4_ = bf16[64,2048]{1,0:T(8,128)(2,1)} collective-permute-done((bf16[64,2048]{1,0:T(8,128)(2,1)}, bf16[64,2048]{1,0:T(8,128)(2,1)}, u32[]{:S(2)}, u32[]{:S(2)}) %collective-permute-start.20) | collective-permute-done | bytes 262176 | tf_op jit(solution)/shard_map/ppermute | solution.py:308
  155.8 1.2 maximum_select_fusion.3
  157.1 1.8 collective-permute-start.23
  159.6 12.0 %expert_gradient.1 = f32[1,1024,2304]{2,1,0:T(8,128)} custom-call(s32[3]{0:T(128)} %pad_add_fusion.scal, bf16[64,2048]{1,0:T(8,128)(2,1)} %get-tuple-element.125.refs_0_.refs_10_, bf16[128,2048]{1,0:T(8,128)(2,1)} %get-tuple-element.126.refs_1_.refs_11_, bf16[128,2048]{1,0:T(8,128)(2,1)} %get-tuple-element.127.refs_2_.refs_12_, ...), custom_call_target="tpu_custom_call" | custom-call | flops 4831838208 | bytes 14155776 | tf_op jit(solution)/shard_map/expert_gradient/pallas_call | solution.py:219
  171.8 3.9 %collective-permute-start.24 = (bf16[288,512]{1,0:T(8,128)(2,1)S(1)}, bf16[288,512]{1,0:T(8,128)(2,1)S(1)}, u32[]{:S(2)}, u32[]{:S(2)}) collective-permute-start(bf16[288,512]{1,0:T(8,128)(2,1)S(1)} %maximum_select_fusion.1), channel_id=1, source_target_pairs={{0,4},{4,8},{8,12},{12,14},{14,10},{10,6},{6,2},{2,0},{1,5},{5,9},... | collective-permute-start | bytes 884744 | tf_op jit(solution)/shard_map/ppermute | solution.py:308
  175.9 5.2 %collective-permute-done.24 = bf16[288,512]{1,0:T(8,128)(2,1)S(1)} collective-permute-done((bf16[288,512]{1,0:T(8,128)(2,1)S(1)}, bf16[288,512]{1,0:T(8,128)(2,1)S(1)}, u32[]{:S(2)}, u32[]{:S(2)}) %collective-permute-start.24) | collective-permute-done | bytes 294944 | tf_op jit(solution)/shard_map/ppermute | solution.py:308
  181.2 2.5 %collective-permute-start.25 = (bf16[288,512]{1,0:T(8,128)(2,1)S(1)}, bf16[288,512]{1,0:T(8,128)(2,1)S(1)}, u32[]{:S(2)}, u32[]{:S(2)}) collective-permute-start(bf16[288,512]{1,0:T(8,128)(2,1)S(1)} %maximum_select_fusion), channel_id=1, source_target_pairs={{0,4},{4,8},{8,12},{12,14},{14,10},{10,6},{6,2},{2,0},{1,5},{5,9},... | collective-permute-start | bytes 884744 | tf_op jit(solution)/shard_map/ppermute | solution.py:308
  183.7 0.7 pad_maximum_fusion.3.kept
  184.5 3.0 %token_sum.1 = bf16[128,2048]{1,0:T(8,128)(2,1)} custom-call(s32[3]{0:T(128)} %pad_add_fusion.scal, bf16[128,128]{1,0:T(8,128)(2,1)} %copy-done.10, bf16[64,2048]{1,0:T(8,128)(2,1)} %get-tuple-element.137.refs_0_, bf16[64,2048]{1,0:T(8,128)(2,1)} %copy-done.25, bf16[64,2048]{1,0:T(8,128)(2,1)} %copy-done.27, bf16[64,2048]{1,0:T(8,128)(2,1)} %copy-done.29, ...), custom_call_target="tpu_custom_call" | custom-call | flops 268435456 | bytes 2097152 | tf_op jit(solution)/shard_map/token_sum/pallas_call | solution.py:183
  188.2 0.7 copy-done.22
  188.9 4.8 %shadow_gradient.1 = (f32[288,1024]{1,0:T(8,128)}, bf16[288,1024]{1,0:T(8,128)(2,1)}) custom-call(s32[3]{0:T(128)} %pad_add_fusion.scal, bf16[288,512]{1,0:T(8,128)(2,1)} %pad_maximum_fusion.3.kept, bf16[288,512]{1,0:T(8,128)(2,1)} %copy-done.22, bf16[288,512]{1,0:T(8,128)(2,1)} %copy-done.21, bf16[64,2048]{1,0:T(8,128)(2,1)} %get-tuple-element.149.refs_0_, ...), custom_call_target="tpu_custom_call" | custom-call | flops 1207959552 | bytes 4194304 | tf_op jit(solution)/shard_map/shadow_gradient/pallas_call | solution.py:277
  193.7 2.2 %collective-permute-done.27 = bf16[288,1024]{1,0:T(8,128)(2,1)S(1)} collective-permute-done((bf16[288,1024]{1,0:T(8,128)(2,1)}, bf16[288,1024]{1,0:T(8,128)(2,1)S(1)}, u32[]{:S(2)}, u32[]{:S(2)}) %collective-permute-start.27) | collective-permute-done | bytes 589856 | tf_op jit(solution)/shard_map/ppermute | solution.py:311
  195.9 2.5 %add_bitcast_fusion = f32[1024,288]{0,1:T(8,128)} fusion(f32[288,1024]{1,0:T(8,128)} %get-tuple-element.159, bf16[288,1024]{1,0:T(8,128)(2,1)S(1)} %collective-permute-done.27), kind=kLoop, calls=%fused_computation | loop fusion | flops 589824 | bytes 2949120 | tf_op jit(solution)/shard_map/transpose | solution.py:383
  (108 shorter events, 5.7 us)
Async XLA Ops:
  2.8 15.2 %copy-start.10 = (bf16[128,128]{1,0:T(8,128)(2,1)}, bf16[128,128]{1,0:T(8,128)(2,1)S(1)}, u32[]{:S(2)}) copy-start(bf16[128,128]{1,0:T(8,128)(2,1)S(1)} %pad.5.meta) | copy-start | bytes 98308
  4.1 27.0 %collective-permute-start.1 = (bf16[128,4224]{1,0:T(8,128)(2,1)S(1)}, bf16[128,4224]{1,0:T(8,128)(2,1)}, u32[]{:S(2)}, u32[]{:S(2)}) collective-permute-start(bf16[128,4224]{1,0:T(8,128)(2,1)S(1)} %pad_maximum_fusion.refs_0_), channel_id=1, source_target_pairs={{0,2},{4,0},{8,4},{12,8},{14,12},{10,14},{6,10},{2,6},{1,3},{5,1},... | collective-permute-start | bytes 3244040 | tf_op jit(solution)/shard_map/ppermute | solution.py:308
  7.2 25.4 %collective-permute-start = (bf16[128,4224]{1,0:T(8,128)(2,1)S(1)}, bf16[128,4224]{1,0:T(8,128)(2,1)}, u32[]{:S(2)}, u32[]{:S(2)}) collective-permute-start(bf16[128,4224]{1,0:T(8,128)(2,1)S(1)} %pad_maximum_fusion.refs_0_), channel_id=1, source_target_pairs={{0,4},{4,8},{8,12},{12,14},{14,10},{10,6},{6,2},{2,0},{1,5},{5,9},... | collective-permute-start | bytes 3244040 | tf_op jit(solution)/shard_map/ppermute | solution.py:308
  18.0 16.6 %collective-permute-start.2 = (bf16[64,4352]{1,0:T(8,128)(2,1)}, bf16[64,4352]{1,0:T(8,128)(2,1)S(1)}, u32[]{:S(2)}, u32[]{:S(2)}) collective-permute-start(bf16[64,4352]{1,0:T(8,128)(2,1)} %get-tuple-element.86.refs_2_.refs_20_), channel_id=1, source_target_pairs={{0,1},{1,0},{2,3},{3,2},{4,5},{5,4},{6,7},{7,6},{8,9},{9,8},{10,11... | collective-permute-start | bytes 1671176 | tf_op jit(solution)/shard_map/ppermute | solution.py:311
  32.6 24.6 %collective-permute-start.3 = (bf16[128,4224]{1,0:T(8,128)(2,1)}, bf16[128,4224]{1,0:T(8,128)(2,1)S(1)}, u32[]{:S(2)}, u32[]{:S(2)}) collective-permute-start(bf16[128,4224]{1,0:T(8,128)(2,1)} %collective-permute-done.refs_0_), channel_id=1, source_target_pairs={{0,4},{4,8},{8,12},{12,14},{14,10},{10,6},{6,2},{2,0},{1,5},{5,9},... | collective-permute-start | bytes 3244040 | tf_op jit(solution)/shard_map/ppermute | solution.py:308
  33.0 24.7 %collective-permute-start.4 = (bf16[128,4224]{1,0:T(8,128)(2,1)}, bf16[128,4224]{1,0:T(8,128)(2,1)S(1)}, u32[]{:S(2)}, u32[]{:S(2)}) collective-permute-start(bf16[128,4224]{1,0:T(8,128)(2,1)} %collective-permute-done.1.refs_1_), channel_id=1, source_target_pairs={{0,2},{4,0},{8,4},{12,8},{14,12},{10,14},{6,10},{2,6},{1,3},{5,1},... | collective-permute-start | bytes 3244040 | tf_op jit(solution)/shard_map/ppermute | solution.py:308
  34.6 10.1 %copy-start.3 = (bf16[64,4352]{1,0:T(8,128)(2,1)}, bf16[64,4352]{1,0:T(8,128)(2,1)S(1)}, u32[]{:S(2)}) copy-start(bf16[64,4352]{1,0:T(8,128)(2,1)S(1)} %collective-permute-done.2.refs_5_.refs_15_.refs_25_) | copy-start | bytes 1671172
  44.7 17.0 %collective-permute-start.7 = (bf16[128,4352]{1,0:T(8,128)(2,1)}, bf16[128,4352]{1,0:T(8,128)(2,1)S(1)}, u32[]{:S(2)}, u32[]{:S(2)}) collective-permute-start(bf16[128,4352]{1,0:T(8,128)(2,1)} %get-tuple-element.96.refs_21_), channel_id=1, source_target_pairs={{0,1},{1,0},{2,3},{3,2},{4,5},{5,4},{6,7},{7,6},{8,9},{9,8},{10,11... | collective-permute-start | bytes 3342344 | tf_op jit(solution)/shard_map/ppermute | solution.py:311
  57.2 11.2 %copy-start.31 = (bf16[128,4224]{1,0:T(8,128)(2,1)}, bf16[128,4224]{1,0:T(8,128)(2,1)S(1)}, u32[]{:S(2)}) copy-start(bf16[128,4224]{1,0:T(8,128)(2,1)S(1)} %collective-permute-done.3.refs_0_) | copy-start | bytes 3244036
  57.7 10.8 %copy-start.32 = (bf16[128,4224]{1,0:T(8,128)(2,1)}, bf16[128,4224]{1,0:T(8,128)(2,1)S(1)}, u32[]{:S(2)}) copy-start(bf16[128,4224]{1,0:T(8,128)(2,1)S(1)} %collective-permute-done.4.refs_1_) | copy-start | bytes 3244036
  57.7 9.5 %collective-permute-start.5 = (bf16[64,2048]{1,0:T(8,128)(2,1)}, bf16[64,2048]{1,0:T(8,128)(2,1)S(1)}, u32[]{:S(2)}, u32[]{:S(2)}) collective-permute-start(bf16[64,2048]{1,0:T(8,128)(2,1)} %get-tuple-element.94), channel_id=1, source_target_pairs={{0,2},{4,0},{8,4},{12,8},{14,12},{10,14},{6,10},{2,6},{1,3},{5,1},... | collective-permute-start | bytes 786440 | tf_op jit(solution)/shard_map/ppermute | solution.py:308
  59.0 9.5 %collective-permute-start.6 = (bf16[64,2048]{1,0:T(8,128)(2,1)}, bf16[64,2048]{1,0:T(8,128)(2,1)S(1)}, u32[]{:S(2)}, u32[]{:S(2)}) collective-permute-start(bf16[64,2048]{1,0:T(8,128)(2,1)} %get-tuple-element.95), channel_id=1, source_target_pairs={{0,4},{4,8},{8,12},{12,14},{14,10},{10,6},{6,2},{2,0},{1,5},{5,9},... | collective-permute-start | bytes 786440 | tf_op jit(solution)/shard_map/ppermute | solution.py:308
  59.7 28.2 %collective-permute-start.8 = (bf16[128,4224]{1,0:T(8,128)(2,1)S(1)}, bf16[128,4224]{1,0:T(8,128)(2,1)S(1)}, u32[]{:S(2)}, u32[]{:S(2)}) collective-permute-start(bf16[128,4224]{1,0:T(8,128)(2,1)S(1)} %collective-permute-done.3.refs_0_), channel_id=1, source_target_pairs={{0,4},{4,8},{8,12},{12,14},{14,10},{10,6},{6,2},{2,0},{1,5},{5,9},... | collective-permute-start | bytes 3244040 | tf_op jit(solution)/shard_map/ppermute | solution.py:308
  61.2 26.7 %collective-permute-start.9 = (bf16[128,4224]{1,0:T(8,128)(2,1)S(1)}, bf16[128,4224]{1,0:T(8,128)(2,1)S(1)}, u32[]{:S(2)}, u32[]{:S(2)}) collective-permute-start(bf16[128,4224]{1,0:T(8,128)(2,1)S(1)} %collective-permute-done.4.refs_1_), channel_id=1, source_target_pairs={{0,2},{4,0},{8,4},{12,8},{14,12},{10,14},{6,10},{2,6},{1,3},{5,1},... | collective-permute-start | bytes 3244040 | tf_op jit(solution)/shard_map/ppermute | solution.py:308
  61.7 16.7 %copy-start = (bf16[128,4352]{1,0:T(8,128)(2,1)}, bf16[128,4352]{1,0:T(8,128)(2,1)S(1)}, u32[]{:S(2)}) copy-start(bf16[128,4352]{1,0:T(8,128)(2,1)S(1)} %collective-permute-done.7.refs_6_.refs_16_.refs_26_) | copy-start | bytes 3342340
  67.1 11.3 %copy-start.24 = (bf16[64,2048]{1,0:T(8,128)(2,1)}, bf16[64,2048]{1,0:T(8,128)(2,1)S(1)}, u32[]{:S(2)}) copy-start(bf16[64,2048]{1,0:T(8,128)(2,1)S(1)} %collective-permute-done.5.refs_7_) | copy-start | bytes 786436
  78.4 24.8 %collective-permute-start.12 = (bf16[128,4352]{1,0:T(8,128)(2,1)}, bf16[128,4352]{1,0:T(8,128)(2,1)S(1)}, u32[]{:S(2)}, u32[]{:S(2)}) collective-permute-start(bf16[128,4352]{1,0:T(8,128)(2,1)} %get-tuple-element.106.refs_22_), channel_id=1, source_target_pairs={{0,1},{1,0},{2,3},{3,2},{4,5},{5,4},{6,7},{7,6},{8,9},{9,8},{10,11... | collective-permute-start | bytes 3342344 | tf_op jit(solution)/shard_map/ppermute | solution.py:311
  87.9 15.4 %copy-start.30 = (bf16[128,4224]{1,0:T(8,128)(2,1)}, bf16[128,4224]{1,0:T(8,128)(2,1)S(1)}, u32[]{:S(2)}) copy-start(bf16[128,4224]{1,0:T(8,128)(2,1)S(1)} %collective-permute-done.8.refs_0_) | copy-start | bytes 3244036
  87.9 15.3 %copy-start.23 = (bf16[128,4224]{1,0:T(8,128)(2,1)}, bf16[128,4224]{1,0:T(8,128)(2,1)S(1)}, u32[]{:S(2)}) copy-start(bf16[128,4224]{1,0:T(8,128)(2,1)S(1)} %collective-permute-done.9.refs_1_) | copy-start | bytes 3244036
  87.9 13.3 %collective-permute-start.10 = (bf16[64,2048]{1,0:T(8,128)(2,1)}, bf16[64,2048]{1,0:T(8,128)(2,1)S(1)}, u32[]{:S(2)}, u32[]{:S(2)}) collective-permute-start(bf16[64,2048]{1,0:T(8,128)(2,1)} %get-tuple-element.104), channel_id=1, source_target_pairs={{0,6},{4,2},{8,0},{12,4},{14,8},{10,12},{6,14},{2,10},{1,7},{5,3},... | collective-permute-start | bytes 786440 | tf_op jit(solution)/shard_map/ppermute | solution.py:308
  90.5 12.7 %collective-permute-start.11 = (bf16[64,2048]{1,0:T(8,128)(2,1)}, bf16[64,2048]{1,0:T(8,128)(2,1)S(1)}, u32[]{:S(2)}, u32[]{:S(2)}) collective-permute-start(bf16[64,2048]{1,0:T(8,128)(2,1)} %get-tuple-element.105), channel_id=1, source_target_pairs={{0,8},{4,12},{8,14},{12,10},{14,6},{10,2},{6,0},{2,4},{1,9},{5,13}... | collective-permute-start | bytes 786440 | tf_op jit(solution)/shard_map/ppermute | solution.py:308
  90.9 25.3 %collective-permute-start.13 = (bf16[128,2048]{1,0:T(8,128)(2,1)S(1)}, bf16[128,2048]{1,0:T(8,128)(2,1)}, u32[]{:S(2)}, u32[]{:S(2)}) collective-permute-start(bf16[128,2048]{1,0:T(8,128)(2,1)S(1)} %slice.6), channel_id=1, source_target_pairs={{0,4},{4,8},{8,12},{12,14},{14,10},{10,6},{6,2},{2,0},{1,5},{5,9},... | collective-permute-start | bytes 1572872 | tf_op jit(solution)/shard_map/ppermute | solution.py:308
  92.1 22.6 %copy-start.6 = (bf16[2304,128]{1,0:T(8,128)(2,1)S(1)}, bf16[2304,128]{1,0:T(8,128)(2,1)}, u32[]{:S(2)}) copy-start(bf16[2304,128]{1,0:T(8,128)(2,1)} %get-tuple-element.89) | copy-start | bytes 1769476
  92.1 24.2 %collective-permute-start.14 = (bf16[128,2176]{1,0:T(8,128)(2,1)S(1)}, bf16[128,2176]{1,0:T(8,128)(2,1)}, u32[]{:S(2)}, u32[]{:S(2)}) collective-permute-start(bf16[128,2176]{1,0:T(8,128)(2,1)S(1)} %slice.7), channel_id=1, source_target_pairs={{0,2},{4,0},{8,4},{12,8},{14,12},{10,14},{6,10},{2,6},{1,3},{5,1},... | collective-permute-start | bytes 1671176 | tf_op jit(solution)/shard_map/ppermute | solution.py:308
  103.9 10.4 %copy-start.1 = (bf16[128,4352]{1,0:T(8,128)(2,1)}, bf16[128,4352]{1,0:T(8,128)(2,1)S(1)}, u32[]{:S(2)}) copy-start(bf16[128,4352]{1,0:T(8,128)(2,1)S(1)} %collective-permute-done.12.refs_7_.refs_17_.refs_27_) | copy-start | bytes 3342340
  114.3 26.3 %collective-permute-start.17 = (bf16[128,4352]{1,0:T(8,128)(2,1)}, bf16[128,4352]{1,0:T(8,128)(2,1)S(1)}, u32[]{:S(2)}, u32[]{:S(2)}) collective-permute-start(bf16[128,4352]{1,0:T(8,128)(2,1)} %get-tuple-element.117.refs_23_), channel_id=1, source_target_pairs={{0,1},{1,0},{2,3},{3,2},{4,5},{5,4},{6,7},{7,6},{8,9},{9,8},{10,11... | collective-permute-start | bytes 3342344 | tf_op jit(solution)/shard_map/ppermute | solution.py:311
  116.2 13.6 %copy-start.8 = (bf16[2304,128]{1,0:T(8,128)(2,1)S(1)}, bf16[2304,128]{1,0:T(8,128)(2,1)}, u32[]{:S(2)}) copy-start(bf16[2304,128]{1,0:T(8,128)(2,1)} %get-tuple-element.109) | copy-start | bytes 1769476
  116.2 15.6 %collective-permute-start.15 = (bf16[64,2048]{1,0:T(8,128)(2,1)S(1)}, bf16[64,2048]{1,0:T(8,128)(2,1)S(1)}, u32[]{:S(2)}, u32[]{:S(2)}) collective-permute-start(bf16[64,2048]{1,0:T(8,128)(2,1)S(1)} %copy-done.34), channel_id=1, source_target_pairs={{0,10},{4,6},{8,2},{12,0},{14,4},{10,8},{6,12},{2,14},{1,11},{5,7}... | collective-permute-start | bytes 786440 | tf_op jit(solution)/shard_map/ppermute | solution.py:308
  119.5 21.1 %collective-permute-start.16 = (bf16[64,2048]{1,0:T(8,128)(2,1)S(1)}, bf16[64,2048]{1,0:T(8,128)(2,1)S(1)}, u32[]{:S(2)}, u32[]{:S(2)}) collective-permute-start(bf16[64,2048]{1,0:T(8,128)(2,1)S(1)} %copy-done.33), channel_id=1, source_target_pairs={{0,12},{4,14},{8,10},{12,6},{14,2},{10,0},{6,4},{2,8},{1,13},{5,15... | collective-permute-start | bytes 786440 | tf_op jit(solution)/shard_map/ppermute | solution.py:308
  129.8 26.0 %collective-permute-start.21 = (bf16[64,4352]{1,0:T(8,128)(2,1)}, bf16[64,4352]{1,0:T(8,128)(2,1)S(1)}, u32[]{:S(2)}, u32[]{:S(2)}) collective-permute-start(bf16[64,4352]{1,0:T(8,128)(2,1)} %get-tuple-element.122.refs_24_), channel_id=1, source_target_pairs={{0,1},{1,0},{2,3},{3,2},{4,5},{5,4},{6,7},{7,6},{8,9},{9,8},{10,11... | collective-permute-start | bytes 1671176 | tf_op jit(solution)/shard_map/ppermute | solution.py:311
  130.8 25.0 %copy-start.18 = (bf16[288,128]{1,0:T(8,128)(2,1)S(1)}, bf16[288,128]{1,0:T(8,128)(2,1)}, u32[]{:S(2)}) copy-start(bf16[288,128]{1,0:T(8,128)(2,1)} %get-tuple-element.163) | copy-start | bytes 221188
  130.9 25.0 %copy-start.20 = (bf16[288,128]{1,0:T(8,128)(2,1)S(1)}, bf16[288,128]{1,0:T(8,128)(2,1)}, u32[]{:S(2)}) copy-start(bf16[288,128]{1,0:T(8,128)(2,1)} %get-tuple-element.171) | copy-start | bytes 221188
  130.9 28.0 %copy-start.17 = (bf16[288,128]{1,0:T(8,128)(2,1)S(1)}, bf16[288,128]{1,0:T(8,128)(2,1)}, u32[]{:S(2)}) copy-start(bf16[288,128]{1,0:T(8,128)(2,1)} %get-tuple-element.166) | copy-start | bytes 221188
  130.9 27.9 %copy-start.19 = (bf16[288,128]{1,0:T(8,128)(2,1)S(1)}, bf16[288,128]{1,0:T(8,128)(2,1)}, u32[]{:S(2)}) copy-start(bf16[288,128]{1,0:T(8,128)(2,1)} %get-tuple-element.174) | copy-start | bytes 221188
  140.6 18.9 %copy-start.2 = (bf16[128,4352]{1,0:T(8,128)(2,1)}, bf16[128,4352]{1,0:T(8,128)(2,1)S(1)}, u32[]{:S(2)}) copy-start(bf16[128,4352]{1,0:T(8,128)(2,1)S(1)} %collective-permute-done.17.refs_8_.refs_18_.refs_28_) | copy-start | bytes 3342340
  141.3 14.5 %collective-permute-start.18 = (bf16[288,512]{1,0:T(8,128)(2,1)}, bf16[288,512]{1,0:T(8,128)(2,1)S(1)}, u32[]{:S(2)}, u32[]{:S(2)}) collective-permute-start(bf16[288,512]{1,0:T(8,128)(2,1)} %get-tuple-element.118), channel_id=1, source_target_pairs={{0,4},{4,8},{8,12},{12,14},{14,10},{10,6},{6,2},{2,0},{1,5},{5,9},... | collective-permute-start | bytes 884744 | tf_op jit(solution)/shard_map/ppermute | solution.py:308
  141.3 14.5 %collective-permute-start.19 = (bf16[288,512]{1,0:T(8,128)(2,1)}, bf16[288,512]{1,0:T(8,128)(2,1)}, u32[]{:S(2)}, u32[]{:S(2)}) collective-permute-start(bf16[288,512]{1,0:T(8,128)(2,1)} %get-tuple-element.119), channel_id=1, source_target_pairs={{0,2},{4,0},{8,4},{12,8},{14,12},{10,14},{6,10},{2,6},{1,3},{5,1},... | collective-permute-start | bytes 884744 | tf_op jit(solution)/shard_map/ppermute | solution.py:308
  143.4 12.4 %collective-permute-start.20 = (bf16[64,2048]{1,0:T(8,128)(2,1)}, bf16[64,2048]{1,0:T(8,128)(2,1)}, u32[]{:S(2)}, u32[]{:S(2)}) collective-permute-start(bf16[64,2048]{1,0:T(8,128)(2,1)} %get-tuple-element.121), channel_id=1, source_target_pairs={{0,14},{4,10},{8,6},{12,2},{14,0},{10,4},{6,8},{2,12},{1,15},{5,11... | collective-permute-start | bytes 786440 | tf_op jit(solution)/shard_map/ppermute | solution.py:308
  157.1 14.6 %collective-permute-start.23 = (bf16[288,512]{1,0:T(8,128)(2,1)S(1)}, bf16[288,512]{1,0:T(8,128)(2,1)S(1)}, u32[]{:S(2)}, u32[]{:S(2)}) collective-permute-start(bf16[288,512]{1,0:T(8,128)(2,1)S(1)} %maximum_select_fusion.3), channel_id=1, source_target_pairs={{0,2},{4,0},{8,4},{12,8},{14,12},{10,14},{6,10},{2,6},{1,3},{5,1},... | collective-permute-start | bytes 884744 | tf_op jit(solution)/shard_map/ppermute | solution.py:308
  158.9 12.7 %collective-permute-start.22 = (bf16[288,512]{1,0:T(8,128)(2,1)S(1)}, bf16[288,512]{1,0:T(8,128)(2,1)S(1)}, u32[]{:S(2)}, u32[]{:S(2)}) collective-permute-start(bf16[288,512]{1,0:T(8,128)(2,1)S(1)} %maximum_select_fusion.2), channel_id=1, source_target_pairs={{0,4},{4,8},{8,12},{12,14},{14,10},{10,6},{6,2},{2,0},{1,5},{5,9},... | collective-permute-start | bytes 884744 | tf_op jit(solution)/shard_map/ppermute | solution.py:308
  159.6 12.1 %copy-start.14 = (bf16[288,128]{1,0:T(8,128)(2,1)S(1)}, bf16[288,128]{1,0:T(8,128)(2,1)}, u32[]{:S(2)}) copy-start(bf16[288,128]{1,0:T(8,128)(2,1)} %get-tuple-element.167) | copy-start | bytes 221188
  159.6 12.1 %copy-start.16 = (bf16[288,128]{1,0:T(8,128)(2,1)S(1)}, bf16[288,128]{1,0:T(8,128)(2,1)}, u32[]{:S(2)}) copy-start(bf16[288,128]{1,0:T(8,128)(2,1)} %get-tuple-element.175) | copy-start | bytes 221188
  159.6 16.1 %copy-start.13 = (bf16[288,128]{1,0:T(8,128)(2,1)S(1)}, bf16[288,128]{1,0:T(8,128)(2,1)}, u32[]{:S(2)}) copy-start(bf16[288,128]{1,0:T(8,128)(2,1)} %get-tuple-element.162) | copy-start | bytes 221188
  159.6 16.1 %copy-start.15 = (bf16[288,128]{1,0:T(8,128)(2,1)S(1)}, bf16[288,128]{1,0:T(8,128)(2,1)}, u32[]{:S(2)}) copy-start(bf16[288,128]{1,0:T(8,128)(2,1)} %get-tuple-element.170) | copy-start | bytes 221188
  171.8 9.3 %collective-permute-start.24 = (bf16[288,512]{1,0:T(8,128)(2,1)S(1)}, bf16[288,512]{1,0:T(8,128)(2,1)S(1)}, u32[]{:S(2)}, u32[]{:S(2)}) collective-permute-start(bf16[288,512]{1,0:T(8,128)(2,1)S(1)} %maximum_select_fusion.1), channel_id=1, source_target_pairs={{0,4},{4,8},{8,12},{12,14},{14,10},{10,6},{6,2},{2,0},{1,5},{5,9},... | collective-permute-start | bytes 884744 | tf_op jit(solution)/shard_map/ppermute | solution.py:308
  175.8 11.7 %collective-permute-start.26 = (bf16[288,512]{1,0:T(8,128)(2,1)S(1)}, bf16[288,512]{1,0:T(8,128)(2,1)S(1)}, u32[]{:S(2)}, u32[]{:S(2)}) collective-permute-start(bf16[288,512]{1,0:T(8,128)(2,1)S(1)} %maximum_select_fusion.4), channel_id=1, source_target_pairs={{0,2},{4,0},{8,4},{12,8},{14,12},{10,14},{6,10},{2,6},{1,3},{5,1},... | collective-permute-start | bytes 884744 | tf_op jit(solution)/shard_map/ppermute | solution.py:308
  181.2 7.0 %collective-permute-start.25 = (bf16[288,512]{1,0:T(8,128)(2,1)S(1)}, bf16[288,512]{1,0:T(8,128)(2,1)S(1)}, u32[]{:S(2)}, u32[]{:S(2)}) collective-permute-start(bf16[288,512]{1,0:T(8,128)(2,1)S(1)} %maximum_select_fusion), channel_id=1, source_target_pairs={{0,4},{4,8},{8,12},{12,14},{14,10},{10,6},{6,2},{2,0},{1,5},{5,9},... | collective-permute-start | bytes 884744 | tf_op jit(solution)/shard_map/ppermute | solution.py:308
  193.7 2.2 %collective-permute-start.27 = (bf16[288,1024]{1,0:T(8,128)(2,1)}, bf16[288,1024]{1,0:T(8,128)(2,1)S(1)}, u32[]{:S(2)}, u32[]{:S(2)}) collective-permute-start(bf16[288,1024]{1,0:T(8,128)(2,1)} %get-tuple-element.160), channel_id=1, source_target_pairs={{0,1},{1,0},{2,3},{3,2},{4,5},{5,4},{6,7},{7,6},{8,9},{9,8},{10,11... | collective-permute-start | bytes 1769480 | tf_op jit(solution)/shard_map/ppermute | solution.py:311
  (15 other events, 59.5 us)

commit v4 on v3

--- a/solution.py
+++ b/solution.py
@@ -230,30 +230,45 @@
     )(scal, *rows, *rows, *packs, *others)
 
 
-def shadow_kernel(plan, experts, capacity, scal, kept, ahead, behind, *refs):
+def order_kernel(plan, experts, capacity, scal, *refs):
     count = len(plan)
-    ins, cots = refs[:count], refs[count : 2 * count]
-    mine, theirs, rows_in, rows_cot, total = refs[2 * count :]
-    own, half, hottest = scal[0], scal[1], scal[2]
-    shift = to_ring(own, experts) - to_ring(hottest, experts)
-    taken = kept.shape[0]
-    gates = taken * experts * 2 // 3
-    column = own * taken + lax.broadcasted_iota(jnp.int32, kept.shape, 0)
-    blank = jnp.zeros((), BF16)
-    away = (shift + experts) % experts
-    received = jnp.where(away <= experts // 2, ahead[...], behind[...])
-    columns = jnp.where(away == 0, kept[...], received)
-
-    def in_order(parts, rows):
+    shift = to_ring(scal[0], experts) - to_ring(scal[2], experts)
+    for parts, out in ((refs[:count], refs[2 * count]), (refs[count : 2 * count], refs[2 * count + 1])):
         for steps, part in zip(plan, parts):
             for at, step in enumerate(steps):
                 place = slot_place((shift + step + 2 * experts) % experts, experts)
                 there = pl.ds(pl.multiple_of(place * capacity, capacity), capacity)
-                rows[there, :] = part[at * capacity : (at + 1) * capacity, :]
+                out[there, :] = part[at * capacity : (at + 1) * capacity, :]
+
+
+def ordered(plan, experts, capacity, scal, ins, cots):
+    vmem = pl.BlockSpec(memory_space=pltpu.VMEM)
+    rows, width = experts * capacity, ins[0].shape[1]
+    return pl.pallas_call(
+        functools.partial(order_kernel, plan, experts, capacity),
+        out_shape=[jax.ShapeDtypeStruct((rows, width), BF16)] * 2,
+        in_specs=[pl.BlockSpec(memory_space=pltpu.SMEM)] + [vmem] * (2 * len(ins)),
+        out_specs=[vmem] * 2,
+        compiler_params=pltpu.CompilerParams(vmem_limit_bytes=VMEM_BYTES),
+        cost_estimate=pl.CostEstimate(flops=0, bytes_accessed=8 * rows * width, transcendentals=0),
+        name="hot_rows_ordered",
+    )(scal, *ins, *cots)
+
+
+def shadow_kernel(experts, scal, kept, ahead, behind, rows_in, rows_cot, out, total):
+    own = scal[0]
+    away = (to_ring(own, experts) - to_ring(scal[2], experts) + experts) % experts
+    taken, rows = kept.shape
+    gates = taken * experts * 2 // 3
+    column = own * taken + lax.broadcasted_iota(jnp.int32, kept.shape, 0)
+    blank = jnp.zeros((), BF16)
+    lane = lax.broadcasted_iota(jnp.int32, kept.shape, 1)
+    reach = jnp.where(lane < rows // 2, experts // 2, experts // 2 - 1)
+    received = jnp.where(away <= reach, ahead[...], behind[...])
+    columns = jnp.where(away == 0, kept[...], received)
 
     @pl.when(own * taken < gates)
     def _():
-        in_order(ins, rows_in)
         total[...] = dot(jnp.where(column < gates, columns, blank), rows_in[...], (1, 0))
 
     @pl.when(own * taken >= gates)
@@ -262,33 +277,33 @@
 
     @pl.when((own + 1) * taken > gates)
     def _():
-        in_order(cots, rows_cot)
         total[...] += dot(jnp.where(column < gates, blank, columns), rows_cot[...], (1, 0))
 
-    width = total.shape[1] // 2
-    mine[...] = total[:, pl.ds(pl.multiple_of(half * width, width), width)]
-    theirs[...] = total[:, pl.ds(pl.multiple_of((1 - half) * width, width), width)].astype(BF16)
-
-
-def shadow_gradient(plan, experts, capacity, scal, columns, ins, cots):
-    vmem = pl.BlockSpec(memory_space=pltpu.VMEM)
+    out[...] = total[...].astype(out.dtype)
+
+
+def shadow_gradient(experts, scal, columns, hot_in, hot_cot, kind):
     taken, rows = columns[0].shape
-    width = ins[0].shape[1]
+    width = hot_in.shape[1] // 2
+    sends = kind == BF16
+    whole = pl.BlockSpec((taken, rows), lambda i, scal: (0, 0))
+    part = pl.BlockSpec((rows, width), lambda i, scal: (0, 1 - scal[1] if sends else scal[1]))
     return pl.pallas_call(
-        functools.partial(shadow_kernel, plan, experts, capacity),
-        out_shape=[
-            jax.ShapeDtypeStruct((taken, width // 2), F32),
-            jax.ShapeDtypeStruct((taken, width // 2), BF16),
-        ],
-        in_specs=[pl.BlockSpec(memory_space=pltpu.SMEM)] + [vmem] * (2 * len(ins) + 3),
-        out_specs=[vmem] * 2,
-        scratch_shapes=[pltpu.VMEM((rows, width), BF16)] * 2 + [pltpu.VMEM((taken, width), F32)],
+        functools.partial(shadow_kernel, experts),
+        out_shape=jax.ShapeDtypeStruct((taken, width), kind),
+        grid_spec=pltpu.PrefetchScalarGridSpec(
+            num_scalar_prefetch=1,
+            grid=(1,),
+            in_specs=[whole] * 3 + [part] * 2,
+            out_specs=pl.BlockSpec((taken, width), lambda i, scal: (0, 0)),
+            scratch_shapes=[pltpu.VMEM((taken, width), F32)],
+        ),
         compiler_params=pltpu.CompilerParams(vmem_limit_bytes=VMEM_BYTES),
         cost_estimate=pl.CostEstimate(
             flops=4 * taken * rows * width, bytes_accessed=4 * rows * width, transcendentals=0
         ),
-        name="shadow_gradient",
-    )(scal, *columns, *ins, *cots)
+        name="shadow_sent" if sends else "shadow_kept",
+    )(scal, *columns, hot_in, hot_cot)
 
 
 def on_device(
@@ -330,7 +345,9 @@
             following = [shift(up, 1), shift(below, -1)]
         elif number + 1 == half:
             following = [shift(up[:, :width], 1), shift(below[:, width:], -1)]
-        if 0 < number < half:
+        if number == half:
+            held, late[half - 2] = lax.optimization_barrier((held, late[half - 2]))
+        elif 0 < number < half - 1:
             held, late[number - 1] = lax.optimization_barrier((held, late[number - 1]))
         (rows, pack, hot_rows, hot_cots), back, turn = run_step(
             steps, fanout, capacity, scal, held, packs[0] if number == half else None, gate_up, down
@@ -346,6 +363,9 @@
         held = following
         if number < half:
             up, below = following
+    (back_behind, back_ahead), other = late[half - 1]
+    turned[-1], back_ahead = lax.optimization_barrier((turned[-1], back_ahead))
+
     taken = 3 * units // experts
     ring_hot = to_ring(hottest, experts)
     is_hot = own == hottest
@@ -355,32 +375,38 @@
         parts = [lax.dynamic_slice_in_dim(part, owner * taken, taken, axis=0) for part in turned]
         return jnp.concatenate(parts, axis=1)
 
-    own_part = chunk(0)
-    first_parts = [chunk(half), chunk(1 - half)]
-    first_parts, late[half - 1] = lax.optimization_barrier((first_parts, late[half - 1]))
-    around = [shift(first_parts[0], 1), shift(first_parts[1], -1)]
+    own_part, far = chunk(0), chunk(half)
+    lanes = far.shape[1] // 2
+    around = [far[:, :lanes], far[:, lanes:]]
+    around, other = lax.optimization_barrier((around, other))
+    around = [shift(around[0], 1), shift(around[1], -1)]
+    others = [part for _, part in late[: half - 1]] + [other, late[half][1]]
+    expert_grad = expert_gradient(units, scal, mine, packs, others)
+    back_far = late[half][0]
     for number in range(1, half):
         if number == 1:
-            around, late[half] = lax.optimization_barrier((around, (late[half][0], late[half][1])))
-            others = [other for _, other in late]
-            expert_grad = expert_gradient(units, scal, mine, packs, others)
+            around, expert_grad, back_behind = lax.optimization_barrier(
+                (around, expert_grad, back_behind)
+            )
+            around = [jnp.concatenate([part, part], axis=1) for part in around]
         if number == 2:
-            around, expert_grad = lax.optimization_barrier((around, expert_grad))
+            around, back_far = lax.optimization_barrier((around, back_far))
         ahead = jnp.where(is_hot, chunk(half - number), around[0])
-        if number < half - 1:
-            behind = jnp.where(is_hot, chunk(number + 1 - half), around[1])
-            around = [shift(ahead, 1), shift(behind, -1)]
-        else:
-            around = [shift(ahead, 1), around[1]]
-    for steps, (sent, _) in zip(plan, late):
-        for step, part in zip(steps, sent):
+        behind = jnp.where(is_hot, chunk(number - half), around[1])
+        around = [shift(ahead, 1), shift(behind, -1)]
+    sent = [rows for rows, _ in late[: half - 1]] + [[back_behind, back_ahead], back_far]
+    for steps, parts in zip(plan, sent):
+        for step, part in zip(steps, parts):
             returned[step % experts] = part
+    hot_in, hot_cot = ordered(plan, experts, capacity, scal, hot_in, hot_cot)
     token_grad = combine(experts, fanout, capacity, scal, meta, [returned[d] for d in range(experts)])
-    around, token_grad = lax.optimization_barrier((around, token_grad))
-    shadow_mine, shadow_theirs = shadow_gradient(
-        plan, experts, capacity, scal, [own_part] + around, hot_in, hot_cot
+    around, token_grad, hot_in, hot_cot = lax.optimization_barrier(
+        (around, token_grad, hot_in, hot_cot)
     )
-    shadow_grad = (shadow_mine + swap(shadow_theirs).astype(F32)).T
+    columns = [own_part] + around
+    theirs = swap(shadow_gradient(experts, scal, columns, hot_in, hot_cot, BF16))
+    kept = shadow_gradient(experts, scal, columns, hot_in, hot_cot, F32)
+    shadow_grad = (kept + theirs.astype(F32)).T
     return (token_grad, expert_grad, shadow_grad)
 
 

time: 199 us -> 196 us (0.985)
  waiting for transfers between devices: 80.9 us -> 69.6 us
  Pallas kernels: 69.3 us -> 76.5 us
  starting transfers between devices: 31.5 us -> 34.9 us
    ppermute x22 -> x23, waiting for transfers between devices: 78.7 us -> 69.6 us  [shift(): return lax.ppermute(block, 'expert', pairs)]
    pallas_call x1 -> x3, Pallas kernels: 4.84 us -> 12.5 us  [the longest x2 8.07 us: shadow_gradient(): pl.pallas_call(functools.partial(shadow_kernel, experts), out_shape=jax.S...]
    ppermute x22 -> x23, starting transfers between devices: 31.2 us -> 34.7 us  [shift(): return lax.ppermute(block, 'expert', pairs)]
    ppermute x6, waiting for transfers between devices: 2.22 us -> 0.02 us  [swap(): return lax.ppermute(block, 'dp', [(0, 1), (1, 0)])]
    unnamed x70 -> x54, local copies, waits for them, and re-layouts: 3.13 us -> 4.27 us
  transfers between devices with their start and end apart: 28 -> 29, of which waited for: 14 -> 11; matrix products, arithmetic and copies ran while one was open for 2% -> 1% of each run, Pallas kernels for 32% -> 37%
where the time goes in v4:
time: 196 us; the launch traced here: 195 us
  Pallas kernels  76.5 us (39%)
  waiting for transfers between devices  69.6 us (36%)
  starting transfers between devices  34.9 us (18%)
  other arithmetic  7.78 us (4%)
  local copies, waits for them, and re-layouts  4.69 us (2%)
    ppermute x23, waiting for transfers between devices, shift(): return lax.ppermute(block, 'expert', pairs)  69.6 us
    pallas_call x5, Pallas kernels, run_step(): pl.pallas_call(functools.partial(step_kernel, steps, fanout, capacity, jo...  49.1 us
    ppermute x23, starting transfers between devices, shift(): return lax.ppermute(block, 'expert', pairs)  34.7 us
    pallas_call x1, Pallas kernels, expert_gradient(): pl.pallas_call(functools.partial(gradient_kernel, units, count), grid=(ti...  11.9 us
    pallas_call x2, Pallas kernels, shadow_gradient(): pl.pallas_call(functools.partial(shadow_kernel, experts), out_shape=jax.S...  8.07 us
    pallas_call x1, Pallas kernels, ordered(): pl.pallas_call(functools.partial(order_kernel, plan, experts, capacity),...  4.47 us
    unnamed x54, local copies, waits for them, and re-layouts  4.27 us
  transfers between devices with their start and end apart: 29, of which 11 were waited for; matrix products, arithmetic and copies ran while one was open for 1% of the time, Pallas kernels for 37%

profile of v4, /device:TPU:0, one launch (start us, length us, event | category | flops | bytes accessed | tf_op | source)
XLA Modules:
  0.0 195.3 jit_solution(7920501563467081943)
XLA Ops:
  0.6 0.7 convert_convert_fusion
  1.3 0.7 convert_element_type.14
  2.0 0.7 reduce-precision_convert_fusion.1
  2.8 1.3 pad_maximum_fusion.refs_0_
  4.1 3.0 %collective-permute-start.1 = (bf16[128,4224]{1,0:T(8,128)(2,1)S(1)}, bf16[128,4224]{1,0:T(8,128)(2,1)}, u32[]{:S(2)}, u32[]{:S(2)}) collective-permute-start(bf16[128,4224]{1,0:T(8,128)(2,1)S(1)} %pad_maximum_fusion.refs_0_), channel_id=1, source_target_pairs={{0,2},{4,0},{8,4},{12,8},{14,12},{10,14},{6,10},{2,6},{1,3},{5,1},... | collective-permute-start | bytes 3244040 | tf_op jit(solution)/shard_map/ppermute | solution.py:323
  7.9 0.6 pad_add_fusion.scal
  8.5 9.3 %expert_step.5 = (bf16[64,2048]{1,0:T(8,128)(2,1)}, bf16[64,4352]{1,0:T(8,128)(2,1)}, bf16[64,2048]{1,0:T(8,128)(2,1)}, bf16[64,2048]{1,0:T(8,128)(2,1)}, bf16[64,2048]{1,0:T(8,128)(2,1)}) custom-call(s32[3]{0:T(128)} %pad_add_fusion.scal, bf16[128,4224]{1,0:T(8,128)(2,1)} %copy-done.7, bf16[2048,1536]{1,0:T(8,128)(2,1)} %bitcast.13, bf16[768,2048]{1,0:T(8,128)(2,1)} %bitcast.18), custom_call_target="tpu_custom_call" | custom-call | flops 4026531840 | bytes 9437184 | tf_op jit(solution)/shard_map/expert_step/pallas_call | solution.py:148
  18.0 13.2 %collective-permute-done.1.refs_1_ = bf16[128,4224]{1,0:T(8,128)(2,1)} collective-permute-done((bf16[128,4224]{1,0:T(8,128)(2,1)S(1)}, bf16[128,4224]{1,0:T(8,128)(2,1)}, u32[]{:S(2)}, u32[]{:S(2)}) %collective-permute-start.1) | collective-permute-done | bytes 1081376 | tf_op jit(solution)/shard_map/ppermute | solution.py:323
  31.2 1.4 collective-permute-done.refs_0_
  33.0 1.6 collective-permute-start.4
  34.6 10.1 %expert_step.6 = (bf16[128,2048]{1,0:T(8,128)(2,1)}, bf16[128,4352]{1,0:T(8,128)(2,1)}, bf16[128,2048]{1,0:T(8,128)(2,1)}, bf16[128,2048]{1,0:T(8,128)(2,1)}, bf...) custom-call(s32[3]{0:T(128)} %pad_add_fusion.scal, ...), custom_call_target="tpu_custom_call" | custom-call | flops 4026531840 | bytes 9437184 | tf_op jit(solution)/shard_map/expert_step/pallas_call | solution.py:148
  44.8 12.4 %collective-permute-done.3.refs_0_ = bf16[128,4224]{1,0:T(8,128)(2,1)S(1)} collective-permute-done((bf16[128,4224]{1,0:T(8,128)(2,1)}, bf16[128,4224]{1,0:T(8,128)(2,1)S(1)}, u32[]{:S(2)}, u32[]{:S(2)}) %collective-permute-start.3) | collective-permute-done | bytes 1081376 | tf_op jit(solution)/shard_map/ppermute | solution.py:323
  57.6 1.3 collective-permute-start.5
  59.0 0.7 collective-permute-start.6
  59.7 1.5 collective-permute-start.8
  61.7 5.4 %collective-permute-done.5.refs_7_ = bf16[64,2048]{1,0:T(8,128)(2,1)S(1)} collective-permute-done((bf16[64,2048]{1,0:T(8,128)(2,1)}, bf16[64,2048]{1,0:T(8,128)(2,1)S(1)}, u32[]{:S(2)}, u32[]{:S(2)}) %collective-permute-start.5) | collective-permute-done | bytes 262176 | tf_op jit(solution)/shard_map/ppermute | solution.py:323
  67.1 1.3 collective-permute-done.6.refs_1_
  68.4 10.0 %expert_step.7 = (bf16[128,2048]{1,0:T(8,128)(2,1)}, bf16[128,4352]{1,0:T(8,128)(2,1)}, bf16[128,2048]{1,0:T(8,128)(2,1)}, bf16[128,2048]{1,0:T(8,128)(2,1)}, bf...) custom-call(s32[3]{0:T(128)} %pad_add_fusion.scal, bf16[128,4224]{1,0:T(8,128)(2,1)} %copy-done.22, ...), custom_call_target="tpu_custom_call" | custom-call | flops 4026531840 | bytes 9437184 | tf_op jit(solution)/shard_map/expert_step/pallas_call | solution.py:148
  78.6 10.1 %collective-permute-done.8.refs_0_ = bf16[128,4224]{1,0:T(8,128)(2,1)S(1)} collective-permute-done((bf16[128,4224]{1,0:T(8,128)(2,1)S(1)}, bf16[128,4224]{1,0:T(8,128)(2,1)S(1)}, u32[]{:S(2)}, u32[]{:S(2)}) %collective-permute-start.8) | collective-permute-done | bytes 1081376 | tf_op jit(solution)/shard_map/ppermute | solution.py:323
  88.8 0.8 collective-permute-start.10
  89.6 1.5 collective-permute-start.11
  91.1 2.6 %collective-permute-start.12 = (bf16[64,2048]{1,0:T(8,128)(2,1)}, bf16[64,2048]{1,0:T(8,128)(2,1)S(1)}, u32[]{:S(2)}, u32[]{:S(2)}) collective-permute-start(bf16[64,2048]{1,0:T(8,128)(2,1)} %get-tuple-element.111), channel_id=1, source_target_pairs={{0,6},{4,2},{8,0},{12,4},{14,8},{10,12},{6,14},{2,10},{1,7},{5,3},... | collective-permute-start | bytes 786440 | tf_op jit(solution)/shard_map/ppermute | solution.py:323
  94.0 9.9 %expert_step.8 = (bf16[128,2048]{1,0:T(8,128)(2,1)}, bf16[128,4352]{1,0:T(8,128)(2,1)}, bf16[128,2048]{1,0:T(8,128)(2,1)}, bf16[128,2048]{1,0:T(8,128)(2,1)}, bf...) custom-call(s32[3]{0:T(128)} %pad_add_fusion.scal, bf16[128,4224]{1,0:T(8,128)(2,1)} %copy-done.21, ...), custom_call_target="tpu_custom_call" | custom-call | flops 4026531840 | bytes 9437184 | tf_op jit(solution)/shard_map/expert_step/pallas_call | solution.py:148
  104.0 0.8 copy-done.24
  104.8 0.9 collective-permute-done.11.refs_1_
  105.7 6.2 %collective-permute-done.12.refs_6_ = bf16[64,2048]{1,0:T(8,128)(2,1)S(1)} collective-permute-done((bf16[64,2048]{1,0:T(8,128)(2,1)}, bf16[64,2048]{1,0:T(8,128)(2,1)S(1)}, u32[]{:S(2)}, u32[]{:S(2)}) %collective-permute-start.12) | collective-permute-done | bytes 262176 | tf_op jit(solution)/shard_map/ppermute | solution.py:323
  111.9 0.8 collective-permute-start.15
  112.7 9.6 %expert_step.9 = (bf16[64,2048]{1,0:T(8,128)(2,1)}, bf16[64,4352]{1,0:T(8,128)(2,1)}, bf16[64,2048]{1,0:T(8,128)(2,1)}, bf16[64,2048]{1,0:T(8,128)(2,1)}, bf16[6...) custom-call(s32[3]{0:T(128)} %pad_add_fusion.scal, bf16[128,2048]{1,0:T(8,128)(2,1)} %copy-done.24, ...), custom_call_target="tpu_custom_call" | custom-call | flops 4026531840 | bytes 9437184 | tf_op jit(solution)/shard_map/expert_step/pallas_call | solution.py:148
  122.6 0.9 copy-done.9
  123.7 0.7 copy-done.25
  124.4 3.1 %collective-permute-start.20 = (bf16[64,2048]{1,0:T(8,128)(2,1)S(1)}, bf16[64,2048]{1,0:T(8,128)(2,1)S(1)}, u32[]{:S(2)}, u32[]{:S(2)}) collective-permute-start(bf16[64,2048]{1,0:T(8,128)(2,1)S(1)} %copy-done.25), channel_id=1, source_target_pairs={{0,10},{4,6},{8,2},{12,0},{14,4},{10,8},{6,12},{2,14},{1,11},{5,7}... | collective-permute-start | bytes 786440 | tf_op jit(solution)/shard_map/ppermute | solution.py:323
  127.7 1.5 collective-permute-start.17
  129.1 0.6 collective-permute-start.18
  129.8 0.8 copy-done.4
  130.6 11.9 %expert_gradient.1 = f32[1,1024,2304]{2,1,0:T(8,128)} custom-call(s32[3]{0:T(128)} %pad_add_fusion.scal, bf16[64,2048]{1,0:T(8,128)(2,1)} %get-tuple-element.122.refs_0_.refs_10_, bf16[128,2048]{1,0:T(8,128)(2,1)} %get-tuple-element.123.refs_1_.refs_11_, bf16[128,2048]{1,0:T(8,128)(2,1)} %get-tuple-element.124.refs_2_.refs_12_, ...), custom_call_target="tpu_custom_call" | custom-call | flops 4831838208 | bytes 14155776 | tf_op jit(solution)/shard_map/expert_gradient/pallas_call | solution.py:219
  142.7 1.8 collective-permute-start.22
  144.9 4.7 %collective-permute-start.23 = (bf16[64,2048]{1,0:T(8,128)(2,1)S(1)}, bf16[64,2048]{1,0:T(8,128)(2,1)S(1)}, u32[]{:S(2)}, u32[]{:S(2)}) collective-permute-start(bf16[64,2048]{1,0:T(8,128)(2,1)S(1)} %copy-done.26), channel_id=1, source_target_pairs={{0,14},{4,10},{8,6},{12,2},{14,0},{10,4},{6,8},{2,12},{1,15},{5,11... | collective-permute-start | bytes 786440 | tf_op jit(solution)/shard_map/ppermute | solution.py:323
  149.6 12.3 %collective-permute-done.23.refs_4_ = bf16[64,2048]{1,0:T(8,128)(2,1)S(1)} collective-permute-done((bf16[64,2048]{1,0:T(8,128)(2,1)S(1)}, bf16[64,2048]{1,0:T(8,128)(2,1)S(1)}, u32[]{:S(2)}, u32[]{:S(2)}) %collective-permute-start.23) | collective-permute-done | bytes 262176 | tf_op jit(solution)/shard_map/ppermute | solution.py:323
  162.2 5.3 %collective-permute-start.24 = (bf16[288,512]{1,0:T(8,128)(2,1)S(1)}, bf16[288,512]{1,0:T(8,128)(2,1)S(1)}, u32[]{:S(2)}, u32[]{:S(2)}) collective-permute-start(bf16[288,512]{1,0:T(8,128)(2,1)S(1)} %maximum_select_fusion.1), channel_id=1, source_target_pairs={{0,4},{4,8},{8,12},{12,14},{14,10},{10,6},{6,2},{2,0},{1,5},{5,9},... | collective-permute-start | bytes 884744 | tf_op jit(solution)/shard_map/ppermute | solution.py:323
  167.5 5.9 %collective-permute-done.26 = bf16[288,512]{1,0:T(8,128)(2,1)S(1)} collective-permute-done((bf16[288,512]{1,0:T(8,128)(2,1)S(1)}, bf16[288,512]{1,0:T(8,128)(2,1)S(1)}, u32[]{:S(2)}, u32[]{:S(2)}) %collective-permute-start.26) | collective-permute-done | bytes 294944 | tf_op jit(solution)/shard_map/ppermute | solution.py:323
  173.6 2.1 %collective-permute-start.25 = (bf16[288,512]{1,0:T(8,128)(2,1)S(1)}, bf16[288,512]{1,0:T(8,128)(2,1)S(1)}, u32[]{:S(2)}, u32[]{:S(2)}) collective-permute-start(bf16[288,512]{1,0:T(8,128)(2,1)S(1)} %maximum_select_fusion), channel_id=1, source_target_pairs={{0,4},{4,8},{8,12},{12,14},{14,10},{10,6},{6,2},{2,0},{1,5},{5,9},... | collective-permute-start | bytes 884744 | tf_op jit(solution)/shard_map/ppermute | solution.py:323
  175.7 4.5 %hot_rows_ordered.1 = (bf16[512,2048]{1,0:T(8,128)(2,1)}, bf16[512,2048]{1,0:T(8,128)(2,1)}) custom-call(s32[3]{0:T(128)} %pad_add_fusion.scal, bf16[64,2048]{1,0:T(8,128)(2,1)} %get-tuple-element.147.refs_0_, bf16[128,2048]{1,0:T(8,128)(2,1)} %get-tuple-element.148.refs_1_, bf16[128,2048]{1,0:T(8,128)(2,1)} %get-tuple-element.149.refs_2_, ...), custom_call_target="tpu_custom_call" | custom-call | bytes 8388608 | tf_op jit(solution)/shard_map/hot_rows_ordered/pallas_call | solution.py:247
  180.2 0.7 pad_maximum_fusion.1.kept
  180.9 3.0 %token_sum.1 = bf16[128,2048]{1,0:T(8,128)(2,1)} custom-call(s32[3]{0:T(128)} %pad_add_fusion.scal, bf16[128,128]{1,0:T(8,128)(2,1)} %copy-done.12, bf16[64,2048]{1,0:T(8,128)(2,1)} %get-tuple-element.139.refs_0_, bf16[64,2048]{1,0:T(8,128)(2,1)} %copy-done.15, bf16[64,2048]{1,0:T(8,128)(2,1)} %copy-done.17, bf16[64,2048]{1,0:T(8,128)(2,1)} %copy-done.18, ...), custom_call_target="tpu_custom_call" | custom-call | flops 268435456 | bytes 2097152 | tf_op jit(solution)/shard_map/token_sum/pallas_call | solution.py:183
  184.0 0.7 copy-done.5
  184.7 3.9 %shadow_sent.1 = bf16[288,1024]{1,0:T(8,128)(2,1)} custom-call(s32[3]{0:T(128)} %pad_add_fusion.scal, bf16[288,512]{1,0:T(8,128)(2,1)} %pad_maximum_fusion.1.kept, bf16[288,512]{1,0:T(8,128)(2,1)} %copy-done.6, bf16[288,512]{1,0:T(8,128)(2,1)} %copy-done.5, bf16[512,2048]{1,0:T(8,128)(2,1)} %get-tuple-element.163.rows_in, ...), custom_call_target="tpu_custom_call" | custom-call | flops 603979776 | bytes 2097152 | tf_op jit(solution)/shard_map/shadow_sent/pallas_call | solution.py:291
  188.7 4.1 %shadow_kept.1 = f32[288,1024]{1,0:T(8,128)} custom-call(s32[3]{0:T(128)} %pad_add_fusion.scal, bf16[288,512]{1,0:T(8,128)(2,1)} %pad_maximum_fusion.1.kept, bf16[288,512]{1,0:T(8,128)(2,1)} %copy-done.6, bf16[288,512]{1,0:T(8,128)(2,1)} %copy-done.5, bf16[512,2048]{1,0:T(8,128)(2,1)} %get-tuple-element.163.rows_in, ...), custom_call_target="tpu_custom_call" | custom-call | flops 603979776 | bytes 2097152 | tf_op jit(solution)/shard_map/shadow_kept/pallas_call | solution.py:291
  192.8 2.5 %add_bitcast_fusion = f32[1024,288]{0,1:T(8,128)} fusion(f32[288,1024]{1,0:T(8,128)} %shadow_kept.1, bf16[288,1024]{1,0:T(8,128)(2,1)S(1)} %collective-permute-done.28), kind=kLoop, calls=%fused_computation | loop fusion | flops 589824 | bytes 2949120 | tf_op jit(solution)/shard_map/transpose | solution.py:409
  (97 shorter events, 4.0 us)
Async XLA Ops:
  2.8 15.1 %copy-start.12 = (bf16[128,128]{1,0:T(8,128)(2,1)}, bf16[128,128]{1,0:T(8,128)(2,1)S(1)}, u32[]{:S(2)}) copy-start(bf16[128,128]{1,0:T(8,128)(2,1)S(1)} %pad.5.meta) | copy-start | bytes 98308
  4.1 4.4 %copy-start.7 = (bf16[128,4224]{1,0:T(8,128)(2,1)}, bf16[128,4224]{1,0:T(8,128)(2,1)S(1)}, u32[]{:S(2)}) copy-start(bf16[128,4224]{1,0:T(8,128)(2,1)S(1)} %pad_maximum_fusion.refs_0_) | copy-start | bytes 3244036
  4.1 27.0 %collective-permute-start.1 = (bf16[128,4224]{1,0:T(8,128)(2,1)S(1)}, bf16[128,4224]{1,0:T(8,128)(2,1)}, u32[]{:S(2)}, u32[]{:S(2)}) collective-permute-start(bf16[128,4224]{1,0:T(8,128)(2,1)S(1)} %pad_maximum_fusion.refs_0_), channel_id=1, source_target_pairs={{0,2},{4,0},{8,4},{12,8},{14,12},{10,14},{6,10},{2,6},{1,3},{5,1},... | collective-permute-start | bytes 3244040 | tf_op jit(solution)/shard_map/ppermute | solution.py:323
  7.2 25.4 %collective-permute-start = (bf16[128,4224]{1,0:T(8,128)(2,1)S(1)}, bf16[128,4224]{1,0:T(8,128)(2,1)}, u32[]{:S(2)}, u32[]{:S(2)}) collective-permute-start(bf16[128,4224]{1,0:T(8,128)(2,1)S(1)} %pad_maximum_fusion.refs_0_), channel_id=1, source_target_pairs={{0,4},{4,8},{8,12},{12,14},{14,10},{10,6},{6,2},{2,0},{1,5},{5,9},... | collective-permute-start | bytes 3244040 | tf_op jit(solution)/shard_map/ppermute | solution.py:323
  17.9 16.7 %collective-permute-start.2 = (bf16[64,4352]{1,0:T(8,128)(2,1)}, bf16[64,4352]{1,0:T(8,128)(2,1)S(1)}, u32[]{:S(2)}, u32[]{:S(2)}) collective-permute-start(bf16[64,4352]{1,0:T(8,128)(2,1)} %get-tuple-element.88.refs_2_.refs_20_), channel_id=1, source_target_pairs={{0,1},{1,0},{2,3},{3,2},{4,5},{5,4},{6,7},{7,6},{8,9},{9,8},{10,11... | collective-permute-start | bytes 1671176 | tf_op jit(solution)/shard_map/ppermute | solution.py:326
  32.6 24.6 %collective-permute-start.3 = (bf16[128,4224]{1,0:T(8,128)(2,1)}, bf16[128,4224]{1,0:T(8,128)(2,1)S(1)}, u32[]{:S(2)}, u32[]{:S(2)}) collective-permute-start(bf16[128,4224]{1,0:T(8,128)(2,1)} %collective-permute-done.refs_0_), channel_id=1, source_target_pairs={{0,4},{4,8},{8,12},{12,14},{14,10},{10,6},{6,2},{2,0},{1,5},{5,9},... | collective-permute-start | bytes 3244040 | tf_op jit(solution)/shard_map/ppermute | solution.py:323
  33.0 24.7 %collective-permute-start.4 = (bf16[128,4224]{1,0:T(8,128)(2,1)}, bf16[128,4224]{1,0:T(8,128)(2,1)S(1)}, u32[]{:S(2)}, u32[]{:S(2)}) collective-permute-start(bf16[128,4224]{1,0:T(8,128)(2,1)} %collective-permute-done.1.refs_1_), channel_id=1, source_target_pairs={{0,2},{4,0},{8,4},{12,8},{14,12},{10,14},{6,10},{2,6},{1,3},{5,1},... | collective-permute-start | bytes 3244040 | tf_op jit(solution)/shard_map/ppermute | solution.py:323
  34.6 10.1 %copy-start.3 = (bf16[64,4352]{1,0:T(8,128)(2,1)}, bf16[64,4352]{1,0:T(8,128)(2,1)S(1)}, u32[]{:S(2)}) copy-start(bf16[64,4352]{1,0:T(8,128)(2,1)S(1)} %collective-permute-done.2.refs_5_.refs_15_.refs_25_) | copy-start | bytes 1671172
  44.8 16.9 %collective-permute-start.7 = (bf16[128,4352]{1,0:T(8,128)(2,1)}, bf16[128,4352]{1,0:T(8,128)(2,1)S(1)}, u32[]{:S(2)}, u32[]{:S(2)}) collective-permute-start(bf16[128,4352]{1,0:T(8,128)(2,1)} %get-tuple-element.98.refs_21_), channel_id=1, source_target_pairs={{0,1},{1,0},{2,3},{3,2},{4,5},{5,4},{6,7},{7,6},{8,9},{9,8},{10,11... | collective-permute-start | bytes 3342344 | tf_op jit(solution)/shard_map/ppermute | solution.py:326
  57.2 11.2 %copy-start.22 = (bf16[128,4224]{1,0:T(8,128)(2,1)}, bf16[128,4224]{1,0:T(8,128)(2,1)S(1)}, u32[]{:S(2)}) copy-start(bf16[128,4224]{1,0:T(8,128)(2,1)S(1)} %collective-permute-done.3.refs_0_) | copy-start | bytes 3244036
  57.6 10.8 %copy-start.23 = (bf16[128,4224]{1,0:T(8,128)(2,1)}, bf16[128,4224]{1,0:T(8,128)(2,1)S(1)}, u32[]{:S(2)}) copy-start(bf16[128,4224]{1,0:T(8,128)(2,1)S(1)} %collective-permute-done.4.refs_1_) | copy-start | bytes 3244036
  57.6 9.5 %collective-permute-start.5 = (bf16[64,2048]{1,0:T(8,128)(2,1)}, bf16[64,2048]{1,0:T(8,128)(2,1)S(1)}, u32[]{:S(2)}, u32[]{:S(2)}) collective-permute-start(bf16[64,2048]{1,0:T(8,128)(2,1)} %get-tuple-element.96), channel_id=1, source_target_pairs={{0,2},{4,0},{8,4},{12,8},{14,12},{10,14},{6,10},{2,6},{1,3},{5,1},... | collective-permute-start | bytes 786440 | tf_op jit(solution)/shard_map/ppermute | solution.py:323
  59.0 9.5 %collective-permute-start.6 = (bf16[64,2048]{1,0:T(8,128)(2,1)}, bf16[64,2048]{1,0:T(8,128)(2,1)S(1)}, u32[]{:S(2)}, u32[]{:S(2)}) collective-permute-start(bf16[64,2048]{1,0:T(8,128)(2,1)} %get-tuple-element.97), channel_id=1, source_target_pairs={{0,4},{4,8},{8,12},{12,14},{14,10},{10,6},{6,2},{2,0},{1,5},{5,9},... | collective-permute-start | bytes 786440 | tf_op jit(solution)/shard_map/ppermute | solution.py:323
  59.7 29.0 %collective-permute-start.8 = (bf16[128,4224]{1,0:T(8,128)(2,1)S(1)}, bf16[128,4224]{1,0:T(8,128)(2,1)S(1)}, u32[]{:S(2)}, u32[]{:S(2)}) collective-permute-start(bf16[128,4224]{1,0:T(8,128)(2,1)S(1)} %collective-permute-done.3.refs_0_), channel_id=1, source_target_pairs={{0,4},{4,8},{8,12},{12,14},{14,10},{10,6},{6,2},{2,0},{1,5},{5,9},... | collective-permute-start | bytes 3244040 | tf_op jit(solution)/shard_map/ppermute | solution.py:323
  61.2 27.5 %collective-permute-start.9 = (bf16[128,4224]{1,0:T(8,128)(2,1)S(1)}, bf16[128,4224]{1,0:T(8,128)(2,1)S(1)}, u32[]{:S(2)}, u32[]{:S(2)}) collective-permute-start(bf16[128,4224]{1,0:T(8,128)(2,1)S(1)} %collective-permute-done.4.refs_1_), channel_id=1, source_target_pairs={{0,2},{4,0},{8,4},{12,8},{14,12},{10,14},{6,10},{2,6},{1,3},{5,1},... | collective-permute-start | bytes 3244040 | tf_op jit(solution)/shard_map/ppermute | solution.py:323
  61.7 16.7 %copy-start = (bf16[128,4352]{1,0:T(8,128)(2,1)}, bf16[128,4352]{1,0:T(8,128)(2,1)S(1)}, u32[]{:S(2)}) copy-start(bf16[128,4352]{1,0:T(8,128)(2,1)S(1)} %collective-permute-done.7.refs_6_.refs_16_.refs_26_) | copy-start | bytes 3342340
  67.1 11.4 %copy-start.14 = (bf16[64,2048]{1,0:T(8,128)(2,1)}, bf16[64,2048]{1,0:T(8,128)(2,1)S(1)}, u32[]{:S(2)}) copy-start(bf16[64,2048]{1,0:T(8,128)(2,1)S(1)} %collective-permute-done.5.refs_7_) | copy-start | bytes 786436
  68.4 10.1 %copy-start.15 = (bf16[64,2048]{1,0:T(8,128)(2,1)}, bf16[64,2048]{1,0:T(8,128)(2,1)S(1)}, u32[]{:S(2)}) copy-start(bf16[64,2048]{1,0:T(8,128)(2,1)S(1)} %collective-permute-done.6.refs_1_) | copy-start | bytes 786436
  78.5 33.4 %collective-permute-start.14 = (bf16[128,4352]{1,0:T(8,128)(2,1)}, bf16[128,4352]{1,0:T(8,128)(2,1)S(1)}, u32[]{:S(2)}, u32[]{:S(2)}) collective-permute-start(bf16[128,4352]{1,0:T(8,128)(2,1)} %get-tuple-element.113.refs_22_), channel_id=1, source_target_pairs={{0,1},{1,0},{2,3},{3,2},{4,5},{5,4},{6,7},{7,6},{8,9},{9,8},{10,11... | collective-permute-start | bytes 3342344 | tf_op jit(solution)/shard_map/ppermute | solution.py:326
  88.7 5.3 %copy-start.21 = (bf16[128,4224]{1,0:T(8,128)(2,1)}, bf16[128,4224]{1,0:T(8,128)(2,1)S(1)}, u32[]{:S(2)}) copy-start(bf16[128,4224]{1,0:T(8,128)(2,1)S(1)} %collective-permute-done.8.refs_0_) | copy-start | bytes 3244036
  88.7 5.3 %copy-start.13 = (bf16[128,4224]{1,0:T(8,128)(2,1)}, bf16[128,4224]{1,0:T(8,128)(2,1)S(1)}, u32[]{:S(2)}) copy-start(bf16[128,4224]{1,0:T(8,128)(2,1)S(1)} %collective-permute-done.9.refs_1_) | copy-start | bytes 3244036
  88.8 15.2 %collective-permute-start.10 = (bf16[128,2048]{1,0:T(8,128)(2,1)S(1)}, bf16[128,2048]{1,0:T(8,128)(2,1)S(1)}, u32[]{:S(2)}, u32[]{:S(2)}) collective-permute-start(bf16[128,2048]{1,0:T(8,128)(2,1)S(1)} %slice.10), channel_id=1, source_target_pairs={{0,4},{4,8},{8,12},{12,14},{14,10},{10,6},{6,2},{2,0},{1,5},{5,9},... | collective-permute-start | bytes 1572872 | tf_op jit(solution)/shard_map/ppermute | solution.py:323
  89.6 16.1 %collective-permute-start.11 = (bf16[128,2176]{1,0:T(8,128)(2,1)S(1)}, bf16[128,2176]{1,0:T(8,128)(2,1)}, u32[]{:S(2)}, u32[]{:S(2)}) collective-permute-start(bf16[128,2176]{1,0:T(8,128)(2,1)S(1)} %slice.11), channel_id=1, source_target_pairs={{0,2},{4,0},{8,4},{12,8},{14,12},{10,14},{6,10},{2,6},{1,3},{5,1},... | collective-permute-start | bytes 1671176 | tf_op jit(solution)/shard_map/ppermute | solution.py:323
  91.1 20.8 %collective-permute-start.12 = (bf16[64,2048]{1,0:T(8,128)(2,1)}, bf16[64,2048]{1,0:T(8,128)(2,1)S(1)}, u32[]{:S(2)}, u32[]{:S(2)}) collective-permute-start(bf16[64,2048]{1,0:T(8,128)(2,1)} %get-tuple-element.111), channel_id=1, source_target_pairs={{0,6},{4,2},{8,0},{12,4},{14,8},{10,12},{6,14},{2,10},{1,7},{5,3},... | collective-permute-start | bytes 786440 | tf_op jit(solution)/shard_map/ppermute | solution.py:323
  93.7 18.2 %collective-permute-start.13 = (bf16[64,2048]{1,0:T(8,128)(2,1)}, bf16[64,2048]{1,0:T(8,128)(2,1)S(1)}, u32[]{:S(2)}, u32[]{:S(2)}) collective-permute-start(bf16[64,2048]{1,0:T(8,128)(2,1)} %get-tuple-element.112), channel_id=1, source_target_pairs={{0,8},{4,12},{8,14},{12,10},{14,6},{10,2},{6,0},{2,4},{1,9},{5,13}... | collective-permute-start | bytes 786440 | tf_op jit(solution)/shard_map/ppermute | solution.py:323
  104.8 22.9 %collective-permute-start.16 = (bf16[128,4352]{1,0:T(8,128)(2,1)}, bf16[128,4352]{1,0:T(8,128)(2,1)S(1)}, u32[]{:S(2)}, u32[]{:S(2)}) collective-permute-start(bf16[128,4352]{1,0:T(8,128)(2,1)} %get-tuple-element.119.refs_23_), channel_id=1, source_target_pairs={{0,1},{1,0},{2,3},{3,2},{4,5},{5,4},{6,7},{7,6},{8,9},{9,8},{10,11... | collective-permute-start | bytes 3342344 | tf_op jit(solution)/shard_map/ppermute | solution.py:326
  105.7 16.8 %copy-start.8 = (bf16[2304,128]{1,0:T(8,128)(2,1)S(1)}, bf16[2304,128]{1,0:T(8,128)(2,1)}, u32[]{:S(2)}) copy-start(bf16[2304,128]{1,0:T(8,128)(2,1)} %get-tuple-element.91) | copy-start | bytes 1769476
  111.9 10.5 %copy-start.16 = (bf16[64,2048]{1,0:T(8,128)(2,1)}, bf16[64,2048]{1,0:T(8,128)(2,1)S(1)}, u32[]{:S(2)}) copy-start(bf16[64,2048]{1,0:T(8,128)(2,1)S(1)} %collective-permute-done.12.refs_6_) | copy-start | bytes 786436
  111.9 10.5 %copy-start.17 = (bf16[64,2048]{1,0:T(8,128)(2,1)}, bf16[64,2048]{1,0:T(8,128)(2,1)S(1)}, u32[]{:S(2)}) copy-start(bf16[64,2048]{1,0:T(8,128)(2,1)S(1)} %collective-permute-done.13.refs_2_) | copy-start | bytes 786436
  111.9 10.5 %copy-start.1 = (bf16[128,4352]{1,0:T(8,128)(2,1)}, bf16[128,4352]{1,0:T(8,128)(2,1)S(1)}, u32[]{:S(2)}) copy-start(bf16[128,4352]{1,0:T(8,128)(2,1)S(1)} %collective-permute-done.14.refs_7_.refs_17_.refs_27_) | copy-start | bytes 3342340
  111.9 15.6 %collective-permute-start.15 = (bf16[64,2048]{1,0:T(8,128)(2,1)}, bf16[64,2048]{1,0:T(8,128)(2,1)S(1)}, u32[]{:S(2)}, u32[]{:S(2)}) collective-permute-start(bf16[64,2048]{1,0:T(8,128)(2,1)} %get-tuple-element.117), channel_id=1, source_target_pairs={{0,12},{4,14},{8,10},{12,6},{14,2},{10,0},{6,4},{2,8},{1,13},{5,15... | collective-permute-start | bytes 786440 | tf_op jit(solution)/shard_map/ppermute | solution.py:323
  122.4 7.4 %collective-permute-start.19 = (bf16[64,4352]{1,0:T(8,128)(2,1)}, bf16[64,4352]{1,0:T(8,128)(2,1)S(1)}, u32[]{:S(2)}, u32[]{:S(2)}) collective-permute-start(bf16[64,4352]{1,0:T(8,128)(2,1)} %get-tuple-element.131.refs_24_), channel_id=1, source_target_pairs={{0,1},{1,0},{2,3},{3,2},{4,5},{5,4},{6,7},{7,6},{8,9},{9,8},{10,11... | collective-permute-start | bytes 1671176 | tf_op jit(solution)/shard_map/ppermute | solution.py:326
  123.5 4.1 %copy-start.11 = (bf16[2304,128]{1,0:T(8,128)(2,1)S(1)}, bf16[2304,128]{1,0:T(8,128)(2,1)}, u32[]{:S(2)}) copy-start(bf16[2304,128]{1,0:T(8,128)(2,1)} %get-tuple-element.118) | copy-start | bytes 1769476
  124.4 18.1 %collective-permute-start.20 = (bf16[64,2048]{1,0:T(8,128)(2,1)S(1)}, bf16[64,2048]{1,0:T(8,128)(2,1)S(1)}, u32[]{:S(2)}, u32[]{:S(2)}) collective-permute-start(bf16[64,2048]{1,0:T(8,128)(2,1)S(1)} %copy-done.25), channel_id=1, source_target_pairs={{0,10},{4,6},{8,2},{12,0},{14,4},{10,8},{6,12},{2,14},{1,11},{5,7}... | collective-permute-start | bytes 786440 | tf_op jit(solution)/shard_map/ppermute | solution.py:323
  127.5 15.0 %copy-start.18 = (bf16[64,2048]{1,0:T(8,128)(2,1)}, bf16[64,2048]{1,0:T(8,128)(2,1)S(1)}, u32[]{:S(2)}) copy-start(bf16[64,2048]{1,0:T(8,128)(2,1)S(1)} %collective-permute-done.15.refs_3_) | copy-start | bytes 786436
  127.7 14.9 %collective-permute-start.17 = (bf16[288,256]{1,0:T(8,128)(2,1)S(1)}, bf16[288,256]{1,0:T(8,128)(2,1)S(1)}, u32[]{:S(2)}, u32[]{:S(2)}) collective-permute-start(bf16[288,256]{1,0:T(8,128)(2,1)S(1)} %get-tuple-element.120), channel_id=1, source_target_pairs={{0,4},{4,8},{8,12},{12,14},{14,10},{10,6},{6,2},{2,0},{1,5},{5,9},... | collective-permute-start | bytes 442376 | tf_op jit(solution)/shard_map/ppermute | solution.py:323
  129.1 13.4 %collective-permute-start.18 = (bf16[288,256]{1,0:T(8,128)(2,1)S(1)}, bf16[288,256]{1,0:T(8,128)(2,1)S(1)}, u32[]{:S(2)}, u32[]{:S(2)}) collective-permute-start(bf16[288,256]{1,0:T(8,128)(2,1)S(1)} %get-tuple-element.121), channel_id=1, source_target_pairs={{0,2},{4,0},{8,4},{12,8},{14,12},{10,14},{6,10},{2,6},{1,3},{5,1},... | collective-permute-start | bytes 442376 | tf_op jit(solution)/shard_map/ppermute | solution.py:323
  142.5 2.4 %copy-start.26 = (bf16[64,2048]{1,0:T(8,128)(2,1)S(1)}, bf16[64,2048]{1,0:T(8,128)(2,1)}, u32[]{:S(2)}) copy-start(bf16[64,2048]{1,0:T(8,128)(2,1)} %get-tuple-element.136) | copy-start | bytes 786436
  142.5 19.5 %copy-start.19 = (bf16[64,2048]{1,0:T(8,128)(2,1)}, bf16[64,2048]{1,0:T(8,128)(2,1)S(1)}, u32[]{:S(2)}) copy-start(bf16[64,2048]{1,0:T(8,128)(2,1)S(1)} %collective-permute-done.20.refs_5_) | copy-start | bytes 786436
  142.7 19.3 %collective-permute-start.22 = (bf16[288,512]{1,0:T(8,128)(2,1)S(1)}, bf16[288,512]{1,0:T(8,128)(2,1)S(1)}, u32[]{:S(2)}, u32[]{:S(2)}) collective-permute-start(bf16[288,512]{1,0:T(8,128)(2,1)S(1)} %maximum_select_fusion.3), channel_id=1, source_target_pairs={{0,2},{4,0},{8,4},{12,8},{14,12},{10,14},{6,10},{2,6},{1,3},{5,1},... | collective-permute-start | bytes 884744 | tf_op jit(solution)/shard_map/ppermute | solution.py:323
  144.6 17.3 %collective-permute-start.21 = (bf16[288,512]{1,0:T(8,128)(2,1)S(1)}, bf16[288,512]{1,0:T(8,128)(2,1)S(1)}, u32[]{:S(2)}, u32[]{:S(2)}) collective-permute-start(bf16[288,512]{1,0:T(8,128)(2,1)S(1)} %maximum_select_fusion.2), channel_id=1, source_target_pairs={{0,4},{4,8},{8,12},{12,14},{14,10},{10,6},{6,2},{2,0},{1,5},{5,9},... | collective-permute-start | bytes 884744 | tf_op jit(solution)/shard_map/ppermute | solution.py:323
  144.9 17.0 %collective-permute-start.23 = (bf16[64,2048]{1,0:T(8,128)(2,1)S(1)}, bf16[64,2048]{1,0:T(8,128)(2,1)S(1)}, u32[]{:S(2)}, u32[]{:S(2)}) collective-permute-start(bf16[64,2048]{1,0:T(8,128)(2,1)S(1)} %copy-done.26), channel_id=1, source_target_pairs={{0,14},{4,10},{8,6},{12,2},{14,0},{10,4},{6,8},{2,12},{1,15},{5,11... | collective-permute-start | bytes 786440 | tf_op jit(solution)/shard_map/ppermute | solution.py:323
  162.0 11.5 %copy-start.20 = (bf16[64,2048]{1,0:T(8,128)(2,1)}, bf16[64,2048]{1,0:T(8,128)(2,1)S(1)}, u32[]{:S(2)}) copy-start(bf16[64,2048]{1,0:T(8,128)(2,1)S(1)} %collective-permute-done.23.refs_4_) | copy-start | bytes 786436
  162.1 11.3 %collective-permute-start.26 = (bf16[288,512]{1,0:T(8,128)(2,1)S(1)}, bf16[288,512]{1,0:T(8,128)(2,1)S(1)}, u32[]{:S(2)}, u32[]{:S(2)}) collective-permute-start(bf16[288,512]{1,0:T(8,128)(2,1)S(1)} %maximum_select_fusion.5), channel_id=1, source_target_pairs={{0,2},{4,0},{8,4},{12,8},{14,12},{10,14},{6,10},{2,6},{1,3},{5,1},... | collective-permute-start | bytes 884744 | tf_op jit(solution)/shard_map/ppermute | solution.py:323
  162.2 11.3 %collective-permute-start.24 = (bf16[288,512]{1,0:T(8,128)(2,1)S(1)}, bf16[288,512]{1,0:T(8,128)(2,1)S(1)}, u32[]{:S(2)}, u32[]{:S(2)}) collective-permute-start(bf16[288,512]{1,0:T(8,128)(2,1)S(1)} %maximum_select_fusion.1), channel_id=1, source_target_pairs={{0,4},{4,8},{8,12},{12,14},{14,10},{10,6},{6,2},{2,0},{1,5},{5,9},... | collective-permute-start | bytes 884744 | tf_op jit(solution)/shard_map/ppermute | solution.py:323
  173.5 10.5 %collective-permute-start.27 = (bf16[288,512]{1,0:T(8,128)(2,1)S(1)}, bf16[288,512]{1,0:T(8,128)(2,1)S(1)}, u32[]{:S(2)}, u32[]{:S(2)}) collective-permute-start(bf16[288,512]{1,0:T(8,128)(2,1)S(1)} %maximum_select_fusion.4), channel_id=1, source_target_pairs={{0,2},{4,0},{8,4},{12,8},{14,12},{10,14},{6,10},{2,6},{1,3},{5,1},... | collective-permute-start | bytes 884744 | tf_op jit(solution)/shard_map/ppermute | solution.py:323
  173.6 10.3 %collective-permute-start.25 = (bf16[288,512]{1,0:T(8,128)(2,1)S(1)}, bf16[288,512]{1,0:T(8,128)(2,1)S(1)}, u32[]{:S(2)}, u32[]{:S(2)}) collective-permute-start(bf16[288,512]{1,0:T(8,128)(2,1)S(1)} %maximum_select_fusion), channel_id=1, source_target_pairs={{0,4},{4,8},{8,12},{12,14},{14,10},{10,6},{6,2},{2,0},{1,5},{5,9},... | collective-permute-start | bytes 884744 | tf_op jit(solution)/shard_map/ppermute | solution.py:323
  188.7 4.1 %collective-permute-start.28 = (bf16[288,1024]{1,0:T(8,128)(2,1)}, bf16[288,1024]{1,0:T(8,128)(2,1)S(1)}, u32[]{:S(2)}, u32[]{:S(2)}) collective-permute-start(bf16[288,1024]{1,0:T(8,128)(2,1)} %shadow_sent.1), channel_id=1, source_target_pairs={{0,1},{1,0},{2,3},{3,2},{4,5},{5,4},{6,7},{7,6},{8,9},{9,8},{10,11... | collective-permute-start | bytes 1769480 | tf_op jit(solution)/shard_map/ppermute | solution.py:326
  (8 other events, 8.4 us)

commit v5 on v4

--- a/solution.py
+++ b/solution.py
@@ -74,13 +74,13 @@
     if joined:
         first, refs = refs[0], refs[1:]
         blocks = [jnp.concatenate([block[...] for block in blocks], axis=1)]
-    weights_gu, weights_down, mine, pack, hot_in, hot_cot = refs[:6]
-    back, refs = refs[6 : 6 + count], refs[6 + count :]
-    if len(refs) > 5:
+    weights_gu, weights_down, mine, pack, hot = refs[:5]
+    back, refs = refs[5 : 5 + count], refs[5 + count :]
+    if len(refs) > 7:
         turned, refs = refs[0], refs[1:]
     else:
         turned = None
-    rows_in, rows_cot, gate_up, down, sems = refs
+    rows_in, rows_cot, hot_in, hot_cot, gate_up, down, sems = refs
     own, half, hottest = scal[0], scal[1], scal[2]
     units, width = down.shape
     load_gu = pltpu.make_async_copy(weights_gu, gate_up, sems.at[0])
@@ -109,10 +109,13 @@
     part = width // 2
     here = pl.ds(pl.multiple_of(half * part, part), part)
     there = pl.ds(pl.multiple_of((1 - half) * part, part), part)
-    mine[:, :part] = rows_in[:, here]
-    mine[:, part:] = rows_cot[:, here]
-    pack[:, :part] = rows_in[:, there]
-    pack[:, part:width] = rows_cot[:, there]
+    at = 3 * units
+    for kept, rows_x, rows_c in ((mine, rows_in, rows_cot), (hot, hot_in, hot_cot)):
+        kept[:, :part] = rows_x[:, here]
+        kept[:, part:] = rows_c[:, here]
+        pack[:, at : at + part] = rows_x[:, there]
+        pack[:, at + part : at + width] = rows_c[:, there]
+        at += width
     load_gu.wait()
     projected = dot(rows_in[...], gate_up[...], (1, 0))
     gate_pre, up_pre = projected[:, :units], projected[:, units:]
@@ -121,16 +124,16 @@
     sigmoid_gate = jax.nn.sigmoid(gate_pre)
     activation = gate_pre * sigmoid_gate
     gate_grad = hidden_grad * up_pre * sigmoid_gate * (1.0 + gate_pre * (1.0 - sigmoid_gate))
-    pack[:, width : width + units] = gate_grad.astype(BF16)
-    pack[:, width + units : width + 2 * units] = (hidden_grad * activation).astype(BF16)
-    pack[:, width + 2 * units :] = (activation * up_pre).astype(BF16)
-    input_rows = dot(pack[:, width : width + 2 * units], gate_up[...], (1, 1)).astype(BF16)
+    pack[:, :units] = gate_grad.astype(BF16)
+    pack[:, units : 2 * units] = (hidden_grad * activation).astype(BF16)
+    pack[:, 2 * units : 3 * units] = (activation * up_pre).astype(BF16)
+    input_rows = dot(pack[:, : 2 * units], gate_up[...], (1, 1)).astype(BF16)
     for at in range(count):
         back[at][...] = input_rows[at * capacity : (at + 1) * capacity]
     if turned is not None:
-        grads = pack[:, width:]
+        grads = pack[:, : 3 * units]
         if joined:
-            grads = jnp.concatenate([first[:, width:], grads], axis=0)
+            grads = jnp.concatenate([first[:, : 3 * units], grads], axis=0)
         turned[...] = grads.T
 
 
@@ -139,7 +142,7 @@
     units, width = down.shape
     vmem = pl.BlockSpec(memory_space=pltpu.VMEM)
     far = pl.BlockSpec(memory_space=pl.ANY)
-    shapes = [(rows, width), (rows, width + 3 * units), (rows, width), (rows, width)]
+    shapes = [(rows, width), (rows, 3 * units + 2 * width), (rows, width)]
     shapes += [(capacity, width)] * count
     joined = first is not None
     if joined or count > 1:
@@ -150,7 +153,7 @@
         out_shape=[jax.ShapeDtypeStruct(shape, BF16) for shape in shapes],
         in_specs=[pl.BlockSpec(memory_space=pltpu.SMEM)] + [vmem] * (len(blocks) + len(firsts)) + [far] * 2,
         out_specs=[vmem] * len(shapes),
-        scratch_shapes=[pltpu.VMEM((rows, width), BF16)] * 2
+        scratch_shapes=[pltpu.VMEM((rows, width), BF16)] * 4
         + [
             pltpu.VMEM(gate_up.shape, BF16),
             pltpu.VMEM(down.shape, BF16),
@@ -162,7 +165,7 @@
         ),
         name="expert_step",
     )(scal, *blocks, *firsts, gate_up, down)
-    return out[:4], out[4 : 4 + count], out[4 + count :]
+    return out[:3], out[3 : 3 + count], out[3 + count :]
 
 
 def combine_kernel(experts, fanout, capacity, scal, meta, *refs):
@@ -194,28 +197,32 @@
 
 
 def gradient_kernel(units, count, scal, *refs):
-    ins, cots, packs = refs[: 2 * count], refs[2 * count : 4 * count], refs[4 * count : 6 * count]
+    ins, cots, grads = refs[: 2 * count], refs[2 * count : 4 * count], refs[4 * count : 6 * count]
     out = refs[6 * count]
     keep = scal[0] != scal[2]
-    width = packs[0].shape[1] - 3 * units
     left = jnp.concatenate([ref[...] for ref in ins], axis=0)
-    right = jnp.concatenate([ref[:, width : width + 2 * units] for ref in packs], axis=0)
+    right = jnp.concatenate([ref[:, : 2 * units] for ref in grads], axis=0)
     out[0, :, : 2 * units] = jnp.where(keep, dot(left, right, (0, 0)), 0.0)
     left = jnp.concatenate([ref[...] for ref in cots], axis=0)
-    right = jnp.concatenate([ref[:, width + 2 * units :] for ref in packs], axis=0)
+    right = jnp.concatenate([ref[:, 2 * units :] for ref in grads], axis=0)
     out[0, :, 2 * units :] = jnp.where(keep, dot(left, right, (0, 0)), 0.0)
 
 
 def expert_gradient(units, scal, mine, packs, others):
     width, columns, count = mine[0].shape[1], 3 * units, len(mine)
     tile = 256
-    tiles = width // 2 // tile
+    tiles, skip = width // 2 // tile, columns // tile
     total = 2 * sum(part.shape[0] for part in mine)
     rows = mine + others
-    in_specs = [pl.BlockSpec(memory_space=pltpu.SMEM)]
-    in_specs += [pl.BlockSpec((part.shape[0], tile), lambda i: (0, i)) for part in rows]
-    in_specs += [pl.BlockSpec((part.shape[0], tile), lambda i: (0, i + tiles)) for part in rows]
-    in_specs += [pl.BlockSpec(part.shape, lambda i: (0, 0)) for part in packs + others]
+
+    def tiled(first):
+        specs = [pl.BlockSpec((part.shape[0], tile), lambda i: (0, i + first)) for part in mine]
+        return specs + [
+            pl.BlockSpec((part.shape[0], tile), lambda i: (0, i + first + skip)) for part in others
+        ]
+
+    in_specs = [pl.BlockSpec(memory_space=pltpu.SMEM)] + tiled(0) + tiled(tiles)
+    in_specs += [pl.BlockSpec((part.shape[0], columns), lambda i: (0, 0)) for part in packs + others]
     return pl.pallas_call(
         functools.partial(gradient_kernel, units, count),
         grid=(tiles,),
@@ -230,80 +237,120 @@
     )(scal, *rows, *rows, *packs, *others)
 
 
+def message_kernel(fanout, tokens, cotangent, routes, route_weight, ratio, clip, message, meta):
+    count, width = tokens.shape
+    message[:, :width] = tokens[...]
+    message[:, width : 2 * width] = cotangent[...]
+    weight = route_weight[...] * ratio[...] * clip[...].astype(F32)
+    first = weight.astype(BF16).astype(F32)
+    rest = weight - first
+    second = rest.astype(BF16).astype(F32)
+    lines = -(-4 * fanout // 8) * 8
+    row = lax.broadcasted_iota(jnp.int32, (lines, count), 0)
+    table = jnp.zeros((lines, count), F32)
+    for number, part in enumerate([routes[...].astype(F32), first, second, rest - second]):
+        for k in range(fanout):
+            table = jnp.where(row == number * fanout + k, part[k : k + 1], table)
+    table = jnp.concatenate([table, jnp.zeros((128 - lines, count), F32)], axis=0)
+    columns = table.T.astype(BF16)
+    message[:, 2 * width :] = columns
+    meta[...] = columns
+
+
+def build_message(tokens, cotangent, routes, route_weight, ratio, clip):
+    count, width = tokens.shape
+    vmem = pl.BlockSpec(memory_space=pltpu.VMEM)
+    return pl.pallas_call(
+        functools.partial(message_kernel, routes.shape[1]),
+        out_shape=[
+            jax.ShapeDtypeStruct((count, 2 * width + 128), BF16),
+            jax.ShapeDtypeStruct((count, 128), BF16),
+        ],
+        in_specs=[vmem] * 6,
+        out_specs=[vmem] * 2,
+        cost_estimate=pl.CostEstimate(flops=0, bytes_accessed=8 * count * width, transcendentals=0),
+        name="ring_message",
+    )(tokens, cotangent, routes.T, route_weight.T, ratio[None], clip[None])
+
+
 def order_kernel(plan, experts, capacity, scal, *refs):
     count = len(plan)
+    mine, others, out, sems = refs[:count], refs[count : 2 * count], refs[-2], refs[-1]
     shift = to_ring(scal[0], experts) - to_ring(scal[2], experts)
-    for parts, out in ((refs[:count], refs[2 * count]), (refs[count : 2 * count], refs[2 * count + 1])):
+    width = out.shape[1]
+    copies = []
+    for side, parts in enumerate((mine, others)):
         for steps, part in zip(plan, parts):
+            columns = pl.ds(part.shape[1] - width, width)
             for at, step in enumerate(steps):
                 place = slot_place((shift + step + 2 * experts) % experts, experts)
-                there = pl.ds(pl.multiple_of(place * capacity, capacity), capacity)
-                out[there, :] = part[at * capacity : (at + 1) * capacity, :]
-
-
-def ordered(plan, experts, capacity, scal, ins, cots):
-    vmem = pl.BlockSpec(memory_space=pltpu.VMEM)
-    rows, width = experts * capacity, ins[0].shape[1]
+                there = pl.multiple_of((place + side * experts) * capacity, capacity)
+                copies.append(
+                    pltpu.make_async_copy(
+                        part.at[pl.ds(at * capacity, capacity), columns],
+                        out.at[pl.ds(there, capacity)],
+                        sems.at[len(copies)],
+                    )
+                )
+    for copy in copies:
+        copy.start()
+    for copy in copies:
+        copy.wait()
+
+
+def ordered(plan, experts, capacity, scal, mine, others):
+    far = pl.BlockSpec(memory_space=pl.ANY)
+    rows, width = 2 * experts * capacity, mine[0].shape[1]
     return pl.pallas_call(
         functools.partial(order_kernel, plan, experts, capacity),
-        out_shape=[jax.ShapeDtypeStruct((rows, width), BF16)] * 2,
-        in_specs=[pl.BlockSpec(memory_space=pltpu.SMEM)] + [vmem] * (2 * len(ins)),
-        out_specs=[vmem] * 2,
-        compiler_params=pltpu.CompilerParams(vmem_limit_bytes=VMEM_BYTES),
-        cost_estimate=pl.CostEstimate(flops=0, bytes_accessed=8 * rows * width, transcendentals=0),
+        out_shape=jax.ShapeDtypeStruct((rows, width), BF16),
+        in_specs=[pl.BlockSpec(memory_space=pltpu.SMEM)] + [far] * (2 * len(mine)),
+        out_specs=far,
+        scratch_shapes=[pltpu.SemaphoreType.DMA((2 * experts,))],
+        cost_estimate=pl.CostEstimate(flops=0, bytes_accessed=4 * rows * width, transcendentals=0),
         name="hot_rows_ordered",
-    )(scal, *ins, *cots)
-
-
-def shadow_kernel(experts, scal, kept, ahead, behind, rows_in, rows_cot, out, total):
+    )(scal, *mine, *others)
+
+
+def shadow_kernel(experts, scal, mine, theirs, hot, out):
     own = scal[0]
-    away = (to_ring(own, experts) - to_ring(scal[2], experts) + experts) % experts
-    taken, rows = kept.shape
+    taken, rows = mine.shape
+    width = out.shape[1]
     gates = taken * experts * 2 // 3
-    column = own * taken + lax.broadcasted_iota(jnp.int32, kept.shape, 0)
-    blank = jnp.zeros((), BF16)
-    lane = lax.broadcasted_iota(jnp.int32, kept.shape, 1)
-    reach = jnp.where(lane < rows // 2, experts // 2, experts // 2 - 1)
-    received = jnp.where(away <= reach, ahead[...], behind[...])
-    columns = jnp.where(away == 0, kept[...], received)
-
-    @pl.when(own * taken < gates)
+    column = own * taken + lax.broadcasted_iota(jnp.int32, (taken, 1), 0)
+
+    def product(first):
+        columns = pl.ds(first, width)
+        return dot(mine[...], hot[:rows, columns], (1, 0)) + dot(theirs[...], hot[rows:, columns], (1, 0))
+
+    @pl.when((own + 1) * taken <= gates)
     def _():
-        total[...] = dot(jnp.where(column < gates, columns, blank), rows_in[...], (1, 0))
+        out[...] = product(0)
 
     @pl.when(own * taken >= gates)
     def _():
-        total[...] = jnp.zeros(total.shape, F32)
-
-    @pl.when((own + 1) * taken > gates)
+        out[...] = product(width)
+
+    @pl.when((own * taken < gates) & ((own + 1) * taken > gates))
     def _():
-        total[...] += dot(jnp.where(column < gates, blank, columns), rows_cot[...], (1, 0))
-
-    out[...] = total[...].astype(out.dtype)
-
-
-def shadow_gradient(experts, scal, columns, hot_in, hot_cot, kind):
-    taken, rows = columns[0].shape
-    width = hot_in.shape[1] // 2
-    sends = kind == BF16
-    whole = pl.BlockSpec((taken, rows), lambda i, scal: (0, 0))
-    part = pl.BlockSpec((rows, width), lambda i, scal: (0, 1 - scal[1] if sends else scal[1]))
+        out[...] = jnp.where(column < gates, product(0), product(width))
+
+
+def shadow_gradient(experts, scal, mine, theirs, hot):
+    taken, rows = mine.shape
+    width = hot.shape[1] // 2
+    vmem = pl.BlockSpec(memory_space=pltpu.VMEM)
     return pl.pallas_call(
         functools.partial(shadow_kernel, experts),
-        out_shape=jax.ShapeDtypeStruct((taken, width), kind),
-        grid_spec=pltpu.PrefetchScalarGridSpec(
-            num_scalar_prefetch=1,
-            grid=(1,),
-            in_specs=[whole] * 3 + [part] * 2,
-            out_specs=pl.BlockSpec((taken, width), lambda i, scal: (0, 0)),
-            scratch_shapes=[pltpu.VMEM((taken, width), F32)],
-        ),
-        compiler_params=pltpu.CompilerParams(vmem_limit_bytes=VMEM_BYTES),
+        out_shape=jax.ShapeDtypeStruct((taken, width), F32),
+        in_specs=[pl.BlockSpec(memory_space=pltpu.SMEM)] + [vmem] * 3,
+        out_specs=vmem,
+        compiler_params=pltpu.CompilerParams(vmem_limit_bytes=24 * 1024 * 1024),
         cost_estimate=pl.CostEstimate(
             flops=4 * taken * rows * width, bytes_accessed=4 * rows * width, transcendentals=0
         ),
-        name="shadow_sent" if sends else "shadow_kept",
-    )(scal, *columns, hot_in, hot_cot)
+        name="shadow_gradient",
+    )(scal, mine, theirs, hot)
 
 
 def on_device(
@@ -328,16 +375,12 @@
     own = lax.axis_index("expert")
     hottest = shadow_plan[0]
     scal = jnp.stack([own, lax.axis_index("dp"), hottest]).astype(jnp.int32)
-    slot_weight = route_weight * ratio_advantage[:, None] * clip_mask[:, None].astype(F32)
-    first = lax.reduce_precision(slot_weight, 8, 7)
-    rest = slot_weight - first
-    second = lax.reduce_precision(rest, 8, 7)
-    meta = jnp.concatenate([routes.astype(F32), first, second, rest - second], axis=1)
-    meta = jnp.pad(meta, ((0, 0), (0, 128 - meta.shape[1]))).astype(BF16)
-    message = jnp.concatenate([tokens, cotangent, meta], axis=1)
+    message, meta = build_message(
+        tokens, cotangent, routes, route_weight, ratio_advantage, clip_mask
+    )
 
     plan = distances(experts)
-    mine, packs, others, hot_in, hot_cot, turned, late = [], [], [], [], [], [], []
+    mine, packs, hot, turned, late = [], [], [], [], []
     returned = {}
     up, below, held = message, message, [message]
     for number, steps in enumerate(plan):
@@ -349,16 +392,18 @@
             held, late[half - 2] = lax.optimization_barrier((held, late[half - 2]))
         elif 0 < number < half - 1:
             held, late[number - 1] = lax.optimization_barrier((held, late[number - 1]))
-        (rows, pack, hot_rows, hot_cots), back, turn = run_step(
+        (rows, pack, hot_rows), back, turn = run_step(
             steps, fanout, capacity, scal, held, packs[0] if number == half else None, gate_up, down
         )
         following, back = lax.optimization_barrier((following, back))
-        sent = [shift(part, step) if step else part for step, part in zip(steps, back)]
+        if number < half:
+            sent = [shift(part, step) if step else part for step, part in zip(steps, back)]
+        else:
+            sent = back
         late.append((sent, swap(pack)))
         mine.append(rows)
         packs.append(pack)
-        hot_in.append(hot_rows)
-        hot_cot.append(hot_cots)
+        hot.append(hot_rows)
         turned += turn
         held = following
         if number < half:
@@ -375,38 +420,41 @@
         parts = [lax.dynamic_slice_in_dim(part, owner * taken, taken, axis=0) for part in turned]
         return jnp.concatenate(parts, axis=1)
 
-    own_part, far = chunk(0), chunk(half)
+    far = chunk(half)
     lanes = far.shape[1] // 2
     around = [far[:, :lanes], far[:, lanes:]]
     around, other = lax.optimization_barrier((around, other))
     around = [shift(around[0], 1), shift(around[1], -1)]
     others = [part for _, part in late[: half - 1]] + [other, late[half][1]]
     expert_grad = expert_gradient(units, scal, mine, packs, others)
-    back_far = late[half][0]
+    chunks = [chunk(distance) for distance in range(1 - half, half)]
+    (back_far,) = late[half][0]
     for number in range(1, half):
         if number == 1:
-            around, expert_grad, back_behind = lax.optimization_barrier(
-                (around, expert_grad, back_behind)
+            around, expert_grad, back_behind, chunks = lax.optimization_barrier(
+                (around, expert_grad, back_behind, chunks)
             )
             around = [jnp.concatenate([part, part], axis=1) for part in around]
-        if number == 2:
+        if number == half - 1:
             around, back_far = lax.optimization_barrier((around, back_far))
-        ahead = jnp.where(is_hot, chunk(half - number), around[0])
-        behind = jnp.where(is_hot, chunk(number - half), around[1])
+        ahead = jnp.where(is_hot, chunks[2 * half - 1 - number], around[0])
+        behind = jnp.where(is_hot, chunks[number - 1], around[1])
         around = [shift(ahead, 1), shift(behind, -1)]
-    sent = [rows for rows, _ in late[: half - 1]] + [[back_behind, back_ahead], back_far]
+    back_far = shift(back_far, half)
+    hot_rows = ordered(plan, experts, capacity, scal, hot, others)
+    around, hot_rows = lax.optimization_barrier((around, hot_rows))
+    away = (to_ring(own, experts) - ring_hot + experts) % experts
+    lane = lax.broadcasted_iota(jnp.int32, far.shape, 1)
+    reach = jnp.where(lane < lanes, half, half - 1)
+    columns = jnp.where(
+        away == 0, chunks[half - 1], jnp.where(away <= reach, around[0], around[1])
+    )
+    shadow_grad = shadow_gradient(experts, scal, columns, swap(columns), hot_rows).T
+    sent = [rows for rows, _ in late[: half - 1]] + [[back_behind, back_ahead], [back_far]]
     for steps, parts in zip(plan, sent):
         for step, part in zip(steps, parts):
             returned[step % experts] = part
-    hot_in, hot_cot = ordered(plan, experts, capacity, scal, hot_in, hot_cot)
     token_grad = combine(experts, fanout, capacity, scal, meta, [returned[d] for d in range(experts)])
-    around, token_grad, hot_in, hot_cot = lax.optimization_barrier(
-        (around, token_grad, hot_in, hot_cot)
-    )
-    columns = [own_part] + around
-    theirs = swap(shadow_gradient(experts, scal, columns, hot_in, hot_cot, BF16))
-    kept = shadow_gradient(experts, scal, columns, hot_in, hot_cot, F32)
-    shadow_grad = (kept + theirs.astype(F32)).T
     return (token_grad, expert_grad, shadow_grad)
 
 

time: 196 us -> 339 us (1.73)
  Pallas kernels: 76.5 us -> 198 us
  waiting for transfers between devices: 69.6 us -> 86.5 us
  other arithmetic: 7.78 us -> 1.93 us
  local copies, waits for them, and re-layouts: 4.69 us -> 10.4 us
    pallas_call x1, Pallas kernels: 4.47 us -> 129 us  [ordered(): pl.pallas_call(functools.partial(order_kernel, plan, experts, capacity),...]
    ppermute x23, waiting for transfers between devices: 69.6 us -> 86.5 us  [shift(): return lax.ppermute(block, 'expert', pairs)]
    pallas_call x2 -> x1, Pallas kernels: 8.07 us -> 2.34 us  [shadow_gradient(): pl.pallas_call(functools.partial(shadow_kernel, experts), out_shape=jax.S...]
    dynamic_slice x4, local copies, waits for them, and re-layouts: 0.19 us -> 3.74 us  [chunk(): lax.dynamic_slice_in_dim(part, owner * taken, taken, axis=0)]
  transfers between devices with their start and end apart: 29 -> 29, of which waited for: 11 -> 12; matrix products, arithmetic and copies ran while one was open for 1% -> 2% of each run, Pallas kernels for 37% -> 54%
where the time goes in v5:
time: 339 us; the launch traced here: 336 us
  Pallas kernels  198 us (58%)
  waiting for transfers between devices  86.5 us (26%)
  starting transfers between devices  37.8 us (11%)
  local copies, waits for them, and re-layouts  10.4 us (3%)
    pallas_call x1, Pallas kernels, ordered(): pl.pallas_call(functools.partial(order_kernel, plan, experts, capacity),...  129 us
    ppermute x23, waiting for transfers between devices, shift(): return lax.ppermute(block, 'expert', pairs)  86.5 us
    pallas_call x5, Pallas kernels, run_step(): pl.pallas_call(functools.partial(step_kernel, steps, fanout, capacity, jo...  50 us
    ppermute x23, starting transfers between devices, shift(): return lax.ppermute(block, 'expert', pairs)  37.3 us
    pallas_call x1, Pallas kernels, expert_gradient(): pl.pallas_call(functools.partial(gradient_kernel, units, count), grid=(ti...  10.7 us
  transfers between devices with their start and end apart: 29, of which 12 were waited for; matrix products, arithmetic and copies ran while one was open for 2% of the time, Pallas kernels for 54%

profile of v5, /device:TPU:0, one launch (start us, length us, event | category | flops | bytes accessed | tf_op | source)
XLA Modules:
  0.0 336.0 jit_solution(8833674389608312278)
XLA Ops:
  0.6 2.3 ring_message.1
  3.0 3.0 collective-permute-start.1
  7.2 9.4 %expert_step.5 = (bf16[64,2048]{1,0:T(8,128)(2,1)}, bf16[64,6400]{1,0:T(8,128)(2,1)}, bf16[64,2048]{1,0:T(8,128)(2,1)}, bf16[64,2048]{1,0:T(8,128)(2,1)}) custom-call(s32[3]{0:T(128)} %pad_add_fusion.scal, bf16[128,4224]{1,0:T(8,128)(2,1)} %get-tuple-element.85.refs_0_, bf16[2048,1536]{1,0:T(8,128)(2,1)} %bitcast.21, bf16[768,2048]{1,0:T(8,128)(2,1)} %bitcast.26), custom_call_target="tpu_custom_call" | custom-call | flops 4026531840 | bytes 9437184 | tf_op jit(solution)/shard_map/expert_step/pallas_call | solution.py:151
  16.6 13.4 %collective-permute-done.1.refs_1_ = bf16[128,4224]{1,0:T(8,128)(2,1)S(1)} collective-permute-done((bf16[128,4224]{1,0:T(8,128)(2,1)}, bf16[128,4224]{1,0:T(8,128)(2,1)S(1)}, u32[]{:S(2)}, u32[]{:S(2)}) %collective-permute-start.1) | collective-permute-done | bytes 1081376 | tf_op jit(solution)/shard_map/ppermute | solution.py:370
  30.0 1.4 collective-permute-done.refs_0_
  31.5 1.0 copy-done.17
  32.4 9.9 %expert_step.6 = (bf16[128,2048]{1,0:T(8,128)(2,1)}, bf16[128,6400]{1,0:T(8,128)(2,1)}, bf16[128,2048]{1,0:T(8,128)(2,1)}, bf16[64,2048]{1,0:T(8,128)(2,1)}, bf1...) custom-call(s32[3]{0:T(128)} %pad_add_fusion.scal, bf16[128,4224]{1,0:T(8,128)(2,1)} %copy-done.17, ...), custom_call_target="tpu_custom_call" | custom-call | flops 4026531840 | bytes 9437184 | tf_op jit(solution)/shard_map/expert_step/pallas_call | solution.py:151
  42.4 0.7 collective-permute-start.3
  43.1 1.3 collective-permute-start.4
  44.5 24.4 %collective-permute-done.3.refs_0_ = bf16[128,4224]{1,0:T(8,128)(2,1)S(1)} collective-permute-done((bf16[128,4224]{1,0:T(8,128)(2,1)}, bf16[128,4224]{1,0:T(8,128)(2,1)S(1)}, u32[]{:S(2)}, u32[]{:S(2)}) %collective-permute-start.3) | collective-permute-done | bytes 1081376 | tf_op jit(solution)/shard_map/ppermute | solution.py:370
  69.3 1.3 collective-permute-start.5
  70.6 0.7 collective-permute-start.6
  71.3 1.6 collective-permute-start.8
  73.3 5.4 %collective-permute-done.5.refs_7_ = bf16[64,2048]{1,0:T(8,128)(2,1)S(1)} collective-permute-done((bf16[64,2048]{1,0:T(8,128)(2,1)}, bf16[64,2048]{1,0:T(8,128)(2,1)S(1)}, u32[]{:S(2)}, u32[]{:S(2)}) %collective-permute-start.5) | collective-permute-done | bytes 262176 | tf_op jit(solution)/shard_map/ppermute | solution.py:370
  78.7 1.3 collective-permute-done.6.refs_1_
  80.1 10.5 %expert_step.7 = (bf16[128,2048]{1,0:T(8,128)(2,1)}, bf16[128,6400]{1,0:T(8,128)(2,1)}, bf16[128,2048]{1,0:T(8,128)(2,1)}, bf16[64,2048]{1,0:T(8,128)(2,1)}, bf1...) custom-call(s32[3]{0:T(128)} %pad_add_fusion.scal, bf16[128,4224]{1,0:T(8,128)(2,1)} %copy-done.18, ...), custom_call_target="tpu_custom_call" | custom-call | flops 4026531840 | bytes 9437184 | tf_op jit(solution)/shard_map/expert_step/pallas_call | solution.py:151
  90.7 10.7 %collective-permute-done.8.refs_0_ = bf16[128,4224]{1,0:T(8,128)(2,1)S(1)} collective-permute-done((bf16[128,4224]{1,0:T(8,128)(2,1)S(1)}, bf16[128,4224]{1,0:T(8,128)(2,1)S(1)}, u32[]{:S(2)}, u32[]{:S(2)}) %collective-permute-start.8) | collective-permute-done | bytes 1081376 | tf_op jit(solution)/shard_map/ppermute | solution.py:370
  101.5 0.9 slice.10
  102.9 0.9 slice.11
  103.8 1.5 collective-permute-start.11
  105.3 9.8 %expert_step.8 = (bf16[128,2048]{1,0:T(8,128)(2,1)}, bf16[128,6400]{1,0:T(8,128)(2,1)}, bf16[128,2048]{1,0:T(8,128)(2,1)}, bf16[64,2048]{1,0:T(8,128)(2,1)}, bf1...) custom-call(s32[3]{0:T(128)} %pad_add_fusion.scal, bf16[128,4224]{1,0:T(8,128)(2,1)} %copy-done.15, ...), custom_call_target="tpu_custom_call" | custom-call | flops 4026531840 | bytes 9437184 | tf_op jit(solution)/shard_map/expert_step/pallas_call | solution.py:151
  115.3 2.7 collective-permute-start.12
  118.3 1.2 constant_dynamic-slice_fusion.3
  119.5 1.2 constant_dynamic-slice_fusion.2
  120.8 2.6 collective-permute-start.15
  123.3 7.8 %collective-permute-done.12.refs_6_ = bf16[64,2048]{1,0:T(8,128)(2,1)S(1)} collective-permute-done((bf16[64,2048]{1,0:T(8,128)(2,1)}, bf16[64,2048]{1,0:T(8,128)(2,1)S(1)}, u32[]{:S(2)}, u32[]{:S(2)}) %collective-permute-start.12) | collective-permute-done | bytes 262176 | tf_op jit(solution)/shard_map/ppermute | solution.py:370
  131.2 10.5 %expert_step.9 = (bf16[64,2048]{1,0:T(8,128)(2,1)}, bf16[64,6400]{1,0:T(8,128)(2,1)}, bf16[64,2048]{1,0:T(8,128)(2,1)}, bf16[64,2048]{1,0:T(8,128)(2,1)}, bf16[2304,128]{1,0:T(8,128)(2,1)}) custom-call(s32[3]{0:T(128)} %pad_add_fusion.scal, bf16[128,2048]{1,0:T(8,128)(2,1)} %collective-permute-done.10.refs_0_, ...), custom_call_target="tpu_custom_call" | custom-call | flops 4026531840 | bytes 9437184 | tf_op jit(solution)/shard_map/expert_step/pallas_call | solution.py:151
  141.9 8.8 %collective-permute-start.20 = (bf16[64,2048]{1,0:T(8,128)(2,1)S(1)}, bf16[64,2048]{1,0:T(8,128)(2,1)S(1)}, u32[]{:S(2)}, u32[]{:S(2)}) collective-permute-start(bf16[64,2048]{1,0:T(8,128)(2,1)S(1)} %copy-done.20), channel_id=1, source_target_pairs={{0,10},{4,6},{8,2},{12,0},{14,4},{10,8},{6,12},{2,14},{1,11},{5,7}... | collective-permute-start | bytes 786440 | tf_op jit(solution)/shard_map/ppermute | solution.py:370
  150.7 1.3 constant_dynamic-slice_fusion
  152.1 0.8 pad_maximum_fusion.2
  153.1 2.0 collective-permute-start.18
  155.1 0.9 copy-done.5
  156.0 10.7 %expert_gradient.1 = f32[1,1024,2304]{2,1,0:T(8,128)} custom-call(s32[3]{0:T(128)} %pad_add_fusion.scal, bf16[64,2048]{1,0:T(8,128)(2,1)} %get-tuple-element.128.refs_0_.refs_10_, bf16[128,2048]{1,0:T(8,128)(2,1)} %get-tuple-element.129.refs_1_.refs_11_, bf16[128,2048]{1,0:T(8,128)(2,1)} %get-tuple-element.130.refs_2_.refs_12_, ...), custom_call_target="tpu_custom_call" | custom-call | flops 4831838208 | bytes 14155776 | tf_op jit(solution)/shard_map/expert_gradient/pallas_call | solution.py:226
  166.9 1.1 collective-permute-start.23
  168.1 1.0 collective-permute-start.21
  169.1 6.8 %collective-permute-done.23 = bf16[288,512]{1,0:T(8,128)(2,1)S(1)} collective-permute-done((bf16[288,512]{1,0:T(8,128)(2,1)S(1)}, bf16[288,512]{1,0:T(8,128)(2,1)S(1)}, u32[]{:S(2)}, u32[]{:S(2)}) %collective-permute-start.23) | collective-permute-done | bytes 294944 | tf_op jit(solution)/shard_map/ppermute | solution.py:370
  176.0 0.9 collective-permute-start.24
  177.0 1.2 collective-permute-start.22
  178.2 6.0 %collective-permute-done.24 = bf16[288,512]{1,0:T(8,128)(2,1)S(1)} collective-permute-done((bf16[288,512]{1,0:T(8,128)(2,1)S(1)}, bf16[288,512]{1,0:T(8,128)(2,1)S(1)}, u32[]{:S(2)}, u32[]{:S(2)}) %collective-permute-start.24) | collective-permute-done | bytes 294944 | tf_op jit(solution)/shard_map/ppermute | solution.py:370
  184.8 1.4 collective-permute-start.26
  186.2 0.7 collective-permute-start.27
  186.9 129.1 %hot_rows_ordered.1.hot = bf16[1024,2048]{1,0:T(8,128)(2,1)} custom-call(s32[3]{0:T(128)} %pad_add_fusion.scal, bf16[64,2048]{1,0:T(8,128)(2,1)} %get-tuple-element.157.refs_0_, bf16[128,2048]{1,0:T(8,128)(2,1)} %get-tuple-element.158.refs_1_, bf16[128,2048]{1,0:T(8,128)(2,1)} %get-tuple-element.159.refs_2_, bf16[128,2048]{1,0:T(8,128)(2,1)} %get-tuple-element.160.refs_3_, ...), custom_call_target="tpu_custom_call" | custom-call | bytes 8388608 | tf_op jit(solution)/shard_map/hot_rows_ordered/pallas_call | solution.py:304
  316.3 3.3 collective-permute-start.25
  319.6 8.2 %collective-permute-done.25.refs_4_ = bf16[64,2048]{1,0:T(8,128)(2,1)S(1)} collective-permute-done((bf16[64,2048]{1,0:T(8,128)(2,1)S(1)}, bf16[64,2048]{1,0:T(8,128)(2,1)S(1)}, u32[]{:S(2)}, u32[]{:S(2)}) %collective-permute-start.25) | collective-permute-done | bytes 262176 | tf_op jit(solution)/shard_map/ppermute | solution.py:370
  327.8 0.7 copy-done.14
  328.5 3.0 token_sum.1
  331.5 2.2 copy-done
  333.7 2.3 shadow_gradient.1
  (86 shorter events, 4.0 us)
Async XLA Ops:
  3.0 27.1 %collective-permute-start.1 = (bf16[128,4224]{1,0:T(8,128)(2,1)}, bf16[128,4224]{1,0:T(8,128)(2,1)S(1)}, u32[]{:S(2)}, u32[]{:S(2)}) collective-permute-start(bf16[128,4224]{1,0:T(8,128)(2,1)} %get-tuple-element.85.refs_0_), channel_id=1, source_target_pairs={{0,2},{4,0},{8,4},{12,8},{14,12},{10,14},{6,10},{2,6},{1,3},{5,1},... | collective-permute-start | bytes 3244040 | tf_op jit(solution)/shard_map/ppermute | solution.py:370
  5.9 25.5 %collective-permute-start = (bf16[128,4224]{1,0:T(8,128)(2,1)}, bf16[128,4224]{1,0:T(8,128)(2,1)S(1)}, u32[]{:S(2)}, u32[]{:S(2)}) collective-permute-start(bf16[128,4224]{1,0:T(8,128)(2,1)} %get-tuple-element.85.refs_0_), channel_id=1, source_target_pairs={{0,4},{4,8},{8,12},{12,14},{14,10},{10,6},{6,2},{2,0},{1,5},{5,9},... | collective-permute-start | bytes 3244040 | tf_op jit(solution)/shard_map/ppermute | solution.py:370
  16.6 14.9 %collective-permute-start.2 = (bf16[64,6400]{1,0:T(8,128)(2,1)}, bf16[64,6400]{1,0:T(8,128)(2,1)}, u32[]{:S(2)}, u32[]{:S(2)}) collective-permute-start(bf16[64,6400]{1,0:T(8,128)(2,1)} %get-tuple-element.90.refs_2_.refs_20_), channel_id=1, source_target_pairs={{0,1},{1,0},{2,3},{3,2},{4,5},{5,4},{6,7},{7,6},{8,9},{9,8},{10,11... | collective-permute-start | bytes 2457608 | tf_op jit(solution)/shard_map/ppermute | solution.py:373
  42.3 37.8 %collective-permute-start.7 = (bf16[128,6400]{1,0:T(8,128)(2,1)}, bf16[128,6400]{1,0:T(8,128)(2,1)S(1)}, u32[]{:S(2)}, u32[]{:S(2)}) collective-permute-start(bf16[128,6400]{1,0:T(8,128)(2,1)} %get-tuple-element.100.refs_21_), channel_id=1, source_target_pairs={{0,1},{1,0},{2,3},{3,2},{4,5},{5,4},{6,7},{7,6},{8,9},{9,8},{10,11... | collective-permute-start | bytes 4915208 | tf_op jit(solution)/shard_map/ppermute | solution.py:373
  42.4 26.5 %collective-permute-start.3 = (bf16[128,4224]{1,0:T(8,128)(2,1)}, bf16[128,4224]{1,0:T(8,128)(2,1)S(1)}, u32[]{:S(2)}, u32[]{:S(2)}) collective-permute-start(bf16[128,4224]{1,0:T(8,128)(2,1)} %copy-done.17), channel_id=1, source_target_pairs={{0,4},{4,8},{8,12},{12,14},{14,10},{10,6},{6,2},{2,0},{1,5},{5,9},... | collective-permute-start | bytes 3244040 | tf_op jit(solution)/shard_map/ppermute | solution.py:370
  43.1 26.1 %collective-permute-start.4 = (bf16[128,4224]{1,0:T(8,128)(2,1)}, bf16[128,4224]{1,0:T(8,128)(2,1)S(1)}, u32[]{:S(2)}, u32[]{:S(2)}) collective-permute-start(bf16[128,4224]{1,0:T(8,128)(2,1)} %copy-done.16), channel_id=1, source_target_pairs={{0,2},{4,0},{8,4},{12,8},{14,12},{10,14},{6,10},{2,6},{1,3},{5,1},... | collective-permute-start | bytes 3244040 | tf_op jit(solution)/shard_map/ppermute | solution.py:370
  68.9 11.2 %copy-start.18 = (bf16[128,4224]{1,0:T(8,128)(2,1)}, bf16[128,4224]{1,0:T(8,128)(2,1)S(1)}, u32[]{:S(2)}) copy-start(bf16[128,4224]{1,0:T(8,128)(2,1)S(1)} %collective-permute-done.3.refs_0_) | copy-start | bytes 3244036
  69.3 10.8 %copy-start.19 = (bf16[128,4224]{1,0:T(8,128)(2,1)}, bf16[128,4224]{1,0:T(8,128)(2,1)S(1)}, u32[]{:S(2)}) copy-start(bf16[128,4224]{1,0:T(8,128)(2,1)S(1)} %collective-permute-done.4.refs_1_) | copy-start | bytes 3244036
  69.3 9.5 %collective-permute-start.5 = (bf16[64,2048]{1,0:T(8,128)(2,1)}, bf16[64,2048]{1,0:T(8,128)(2,1)S(1)}, u32[]{:S(2)}, u32[]{:S(2)}) collective-permute-start(bf16[64,2048]{1,0:T(8,128)(2,1)} %get-tuple-element.98), channel_id=1, source_target_pairs={{0,2},{4,0},{8,4},{12,8},{14,12},{10,14},{6,10},{2,6},{1,3},{5,1},... | collective-permute-start | bytes 786440 | tf_op jit(solution)/shard_map/ppermute | solution.py:370
  70.6 9.5 %collective-permute-start.6 = (bf16[64,2048]{1,0:T(8,128)(2,1)}, bf16[64,2048]{1,0:T(8,128)(2,1)S(1)}, u32[]{:S(2)}, u32[]{:S(2)}) collective-permute-start(bf16[64,2048]{1,0:T(8,128)(2,1)} %get-tuple-element.99), channel_id=1, source_target_pairs={{0,4},{4,8},{8,12},{12,14},{14,10},{10,6},{6,2},{2,0},{1,5},{5,9},... | collective-permute-start | bytes 786440 | tf_op jit(solution)/shard_map/ppermute | solution.py:370
  71.3 30.2 %collective-permute-start.8 = (bf16[128,4224]{1,0:T(8,128)(2,1)S(1)}, bf16[128,4224]{1,0:T(8,128)(2,1)S(1)}, u32[]{:S(2)}, u32[]{:S(2)}) collective-permute-start(bf16[128,4224]{1,0:T(8,128)(2,1)S(1)} %collective-permute-done.3.refs_0_), channel_id=1, source_target_pairs={{0,4},{4,8},{8,12},{12,14},{14,10},{10,6},{6,2},{2,0},{1,5},{5,9},... | collective-permute-start | bytes 3244040 | tf_op jit(solution)/shard_map/ppermute | solution.py:370
  72.9 28.6 %collective-permute-start.9 = (bf16[128,4224]{1,0:T(8,128)(2,1)S(1)}, bf16[128,4224]{1,0:T(8,128)(2,1)S(1)}, u32[]{:S(2)}, u32[]{:S(2)}) collective-permute-start(bf16[128,4224]{1,0:T(8,128)(2,1)S(1)} %collective-permute-done.4.refs_1_), channel_id=1, source_target_pairs={{0,2},{4,0},{8,4},{12,8},{14,12},{10,14},{6,10},{2,6},{1,3},{5,1},... | collective-permute-start | bytes 3244040 | tf_op jit(solution)/shard_map/ppermute | solution.py:370
  78.7 11.9 %copy-start.9 = (bf16[64,2048]{1,0:T(8,128)(2,1)}, bf16[64,2048]{1,0:T(8,128)(2,1)S(1)}, u32[]{:S(2)}) copy-start(bf16[64,2048]{1,0:T(8,128)(2,1)S(1)} %collective-permute-done.5.refs_7_) | copy-start | bytes 786436
  80.1 10.5 %copy-start.10 = (bf16[64,2048]{1,0:T(8,128)(2,1)}, bf16[64,2048]{1,0:T(8,128)(2,1)S(1)}, u32[]{:S(2)}) copy-start(bf16[64,2048]{1,0:T(8,128)(2,1)S(1)} %collective-permute-done.6.refs_1_) | copy-start | bytes 786436
  80.1 10.5 %copy-start.2 = (bf16[128,6400]{1,0:T(8,128)(2,1)}, bf16[128,6400]{1,0:T(8,128)(2,1)S(1)}, u32[]{:S(2)}) copy-start(bf16[128,6400]{1,0:T(8,128)(2,1)S(1)} %collective-permute-done.7.refs_6_.refs_16_.refs_26_) | copy-start | bytes 4915204
  90.6 40.5 %collective-permute-start.14 = (bf16[128,6400]{1,0:T(8,128)(2,1)}, bf16[128,6400]{1,0:T(8,128)(2,1)S(1)}, u32[]{:S(2)}, u32[]{:S(2)}) collective-permute-start(bf16[128,6400]{1,0:T(8,128)(2,1)} %get-tuple-element.114.refs_22_), channel_id=1, source_target_pairs={{0,1},{1,0},{2,3},{3,2},{4,5},{5,4},{6,7},{7,6},{8,9},{9,8},{10,11... | collective-permute-start | bytes 4915208 | tf_op jit(solution)/shard_map/ppermute | solution.py:373
  101.5 3.9 %copy-start.15 = (bf16[128,4224]{1,0:T(8,128)(2,1)}, bf16[128,4224]{1,0:T(8,128)(2,1)S(1)}, u32[]{:S(2)}) copy-start(bf16[128,4224]{1,0:T(8,128)(2,1)S(1)} %collective-permute-done.8.refs_0_) | copy-start | bytes 3244036
  101.5 3.9 %copy-start.8 = (bf16[128,4224]{1,0:T(8,128)(2,1)}, bf16[128,4224]{1,0:T(8,128)(2,1)S(1)}, u32[]{:S(2)}) copy-start(bf16[128,4224]{1,0:T(8,128)(2,1)S(1)} %collective-permute-done.9.refs_1_) | copy-start | bytes 3244036
  102.4 15.6 %collective-permute-start.10 = (bf16[128,2048]{1,0:T(8,128)(2,1)}, bf16[128,2048]{1,0:T(8,128)(2,1)}, u32[]{:S(2)}, u32[]{:S(2)}) collective-permute-start(bf16[128,2048]{1,0:T(8,128)(2,1)} %slice.10), channel_id=1, source_target_pairs={{0,4},{4,8},{8,12},{12,14},{14,10},{10,6},{6,2},{2,0},{1,5},{5,9},... | collective-permute-start | bytes 1572872 | tf_op jit(solution)/shard_map/ppermute | solution.py:370
  103.8 17.0 %collective-permute-start.11 = (bf16[128,2176]{1,0:T(8,128)(2,1)}, bf16[128,2176]{1,0:T(8,128)(2,1)}, u32[]{:S(2)}, u32[]{:S(2)}) collective-permute-start(bf16[128,2176]{1,0:T(8,128)(2,1)} %slice.11), channel_id=1, source_target_pairs={{0,2},{4,0},{8,4},{12,8},{14,12},{10,14},{6,10},{2,6},{1,3},{5,1},... | collective-permute-start | bytes 1671176 | tf_op jit(solution)/shard_map/ppermute | solution.py:370
  115.2 37.8 %collective-permute-start.16 = (bf16[128,6400]{1,0:T(8,128)(2,1)}, bf16[128,6400]{1,0:T(8,128)(2,1)S(1)}, u32[]{:S(2)}, u32[]{:S(2)}) collective-permute-start(bf16[128,6400]{1,0:T(8,128)(2,1)} %get-tuple-element.125.refs_23_), channel_id=1, source_target_pairs={{0,1},{1,0},{2,3},{3,2},{4,5},{5,4},{6,7},{7,6},{8,9},{9,8},{10,11... | collective-permute-start | bytes 4915208 | tf_op jit(solution)/shard_map/ppermute | solution.py:373
  115.3 15.8 %collective-permute-start.12 = (bf16[64,2048]{1,0:T(8,128)(2,1)}, bf16[64,2048]{1,0:T(8,128)(2,1)S(1)}, u32[]{:S(2)}, u32[]{:S(2)}) collective-permute-start(bf16[64,2048]{1,0:T(8,128)(2,1)} %get-tuple-element.112), channel_id=1, source_target_pairs={{0,6},{4,2},{8,0},{12,4},{14,8},{10,12},{6,14},{2,10},{1,7},{5,3},... | collective-permute-start | bytes 786440 | tf_op jit(solution)/shard_map/ppermute | solution.py:370
  118.0 13.2 %collective-permute-start.13 = (bf16[64,2048]{1,0:T(8,128)(2,1)}, bf16[64,2048]{1,0:T(8,128)(2,1)}, u32[]{:S(2)}, u32[]{:S(2)}) collective-permute-start(bf16[64,2048]{1,0:T(8,128)(2,1)} %get-tuple-element.113), channel_id=1, source_target_pairs={{0,8},{4,12},{8,14},{12,10},{14,6},{10,2},{6,0},{2,4},{1,9},{5,13}... | collective-permute-start | bytes 786440 | tf_op jit(solution)/shard_map/ppermute | solution.py:370
  118.3 2.4 copy-start.21
  120.8 21.0 %copy-start.7 = (bf16[2304,128]{1,0:T(8,128)(2,1)S(1)}, bf16[2304,128]{1,0:T(8,128)(2,1)}, u32[]{:S(2)}) copy-start(bf16[2304,128]{1,0:T(8,128)(2,1)} %get-tuple-element.123) | copy-start | bytes 1769476
  120.8 21.1 %copy-start.20 = (bf16[64,2048]{1,0:T(8,128)(2,1)S(1)}, bf16[64,2048]{1,0:T(8,128)(2,1)}, u32[]{:S(2)}) copy-start(bf16[64,2048]{1,0:T(8,128)(2,1)} %get-tuple-element.138) | copy-start | bytes 786436
  120.8 29.9 %collective-permute-start.15 = (bf16[64,2048]{1,0:T(8,128)(2,1)S(1)}, bf16[64,2048]{1,0:T(8,128)(2,1)S(1)}, u32[]{:S(2)}, u32[]{:S(2)}) collective-permute-start(bf16[64,2048]{1,0:T(8,128)(2,1)S(1)} %copy-done.21), channel_id=1, source_target_pairs={{0,12},{4,14},{8,10},{12,6},{14,2},{10,0},{6,4},{2,8},{1,13},{5,15... | collective-permute-start | bytes 786440 | tf_op jit(solution)/shard_map/ppermute | solution.py:370
  131.2 10.5 %copy-start.11 = (bf16[64,2048]{1,0:T(8,128)(2,1)}, bf16[64,2048]{1,0:T(8,128)(2,1)S(1)}, u32[]{:S(2)}) copy-start(bf16[64,2048]{1,0:T(8,128)(2,1)S(1)} %collective-permute-done.12.refs_6_) | copy-start | bytes 786436
  131.2 10.5 %copy-start.3 = (bf16[128,6400]{1,0:T(8,128)(2,1)}, bf16[128,6400]{1,0:T(8,128)(2,1)S(1)}, u32[]{:S(2)}) copy-start(bf16[128,6400]{1,0:T(8,128)(2,1)S(1)} %collective-permute-done.14.refs_7_.refs_17_.refs_27_) | copy-start | bytes 4915204
  141.7 13.4 %collective-permute-start.19 = (bf16[64,6400]{1,0:T(8,128)(2,1)}, bf16[64,6400]{1,0:T(8,128)(2,1)S(1)}, u32[]{:S(2)}, u32[]{:S(2)}) collective-permute-start(bf16[64,6400]{1,0:T(8,128)(2,1)} %get-tuple-element.137.refs_24_), channel_id=1, source_target_pairs={{0,1},{1,0},{2,3},{3,2},{4,5},{5,4},{6,7},{7,6},{8,9},{9,8},{10,11... | collective-permute-start | bytes 2457608 | tf_op jit(solution)/shard_map/ppermute | solution.py:373
  141.9 24.9 %collective-permute-start.20 = (bf16[64,2048]{1,0:T(8,128)(2,1)S(1)}, bf16[64,2048]{1,0:T(8,128)(2,1)S(1)}, u32[]{:S(2)}, u32[]{:S(2)}) collective-permute-start(bf16[64,2048]{1,0:T(8,128)(2,1)S(1)} %copy-done.20), channel_id=1, source_target_pairs={{0,10},{4,6},{8,2},{12,0},{14,4},{10,8},{6,12},{2,14},{1,11},{5,7}... | collective-permute-start | bytes 786440 | tf_op jit(solution)/shard_map/ppermute | solution.py:370
  150.7 1.4 copy-start.12
  153.0 2.1 copy-start.4
  153.0 13.8 %collective-permute-start.17 = (bf16[288,256]{1,0:T(8,128)(2,1)S(1)}, bf16[288,256]{1,0:T(8,128)(2,1)S(1)}, u32[]{:S(2)}, u32[]{:S(2)}) collective-permute-start(bf16[288,256]{1,0:T(8,128)(2,1)S(1)} %get-tuple-element.126), channel_id=1, source_target_pairs={{0,4},{4,8},{8,12},{12,14},{14,10},{10,6},{6,2},{2,0},{1,5},{5,9},... | collective-permute-start | bytes 442376 | tf_op jit(solution)/shard_map/ppermute | solution.py:370
  153.1 13.7 %collective-permute-start.18 = (bf16[288,256]{1,0:T(8,128)(2,1)S(1)}, bf16[288,256]{1,0:T(8,128)(2,1)S(1)}, u32[]{:S(2)}, u32[]{:S(2)}) collective-permute-start(bf16[288,256]{1,0:T(8,128)(2,1)S(1)} %get-tuple-element.127), channel_id=1, source_target_pairs={{0,2},{4,0},{8,4},{12,8},{14,12},{10,14},{6,10},{2,6},{1,3},{5,1},... | collective-permute-start | bytes 442376 | tf_op jit(solution)/shard_map/ppermute | solution.py:370
  166.8 18.0 %copy-start.13 = (bf16[64,2048]{1,0:T(8,128)(2,1)}, bf16[64,2048]{1,0:T(8,128)(2,1)S(1)}, u32[]{:S(2)}) copy-start(bf16[64,2048]{1,0:T(8,128)(2,1)S(1)} %collective-permute-done.20.refs_5_) | copy-start | bytes 786436
  166.9 9.1 %collective-permute-start.23 = (bf16[288,512]{1,0:T(8,128)(2,1)S(1)}, bf16[288,512]{1,0:T(8,128)(2,1)S(1)}, u32[]{:S(2)}, u32[]{:S(2)}) collective-permute-start(bf16[288,512]{1,0:T(8,128)(2,1)S(1)} %maximum_select_fusion.1), channel_id=1, source_target_pairs={{0,2},{4,0},{8,4},{12,8},{14,12},{10,14},{6,10},{2,6},{1,3},{5,1},... | collective-permute-start | bytes 884744 | tf_op jit(solution)/shard_map/ppermute | solution.py:370
  168.1 8.8 %collective-permute-start.21 = (bf16[288,512]{1,0:T(8,128)(2,1)S(1)}, bf16[288,512]{1,0:T(8,128)(2,1)S(1)}, u32[]{:S(2)}, u32[]{:S(2)}) collective-permute-start(bf16[288,512]{1,0:T(8,128)(2,1)S(1)} %maximum_select_fusion), channel_id=1, source_target_pairs={{0,4},{4,8},{8,12},{12,14},{14,10},{10,6},{6,2},{2,0},{1,5},{5,9},... | collective-permute-start | bytes 884744 | tf_op jit(solution)/shard_map/ppermute | solution.py:370
  176.0 8.2 %collective-permute-start.24 = (bf16[288,512]{1,0:T(8,128)(2,1)S(1)}, bf16[288,512]{1,0:T(8,128)(2,1)S(1)}, u32[]{:S(2)}, u32[]{:S(2)}) collective-permute-start(bf16[288,512]{1,0:T(8,128)(2,1)S(1)} %broadcast_select_fusion.2), channel_id=1, source_target_pairs={{0,2},{4,0},{8,4},{12,8},{14,12},{10,14},{6,10},{2,6},{1,3},{5,1},... | collective-permute-start | bytes 884744 | tf_op jit(solution)/shard_map/ppermute | solution.py:370
  177.0 7.7 %collective-permute-start.22 = (bf16[288,512]{1,0:T(8,128)(2,1)S(1)}, bf16[288,512]{1,0:T(8,128)(2,1)S(1)}, u32[]{:S(2)}, u32[]{:S(2)}) collective-permute-start(bf16[288,512]{1,0:T(8,128)(2,1)S(1)} %broadcast_select_fusion.3), channel_id=1, source_target_pairs={{0,4},{4,8},{8,12},{12,14},{14,10},{10,6},{6,2},{2,0},{1,5},{5,9},... | collective-permute-start | bytes 884744 | tf_op jit(solution)/shard_map/ppermute | solution.py:370
  184.8 131.3 %collective-permute-start.26 = (bf16[288,512]{1,0:T(8,128)(2,1)S(1)}, bf16[288,512]{1,0:T(8,128)(2,1)S(1)}, u32[]{:S(2)}, u32[]{:S(2)}) collective-permute-start(bf16[288,512]{1,0:T(8,128)(2,1)S(1)} %broadcast_select_fusion.1), channel_id=1, source_target_pairs={{0,4},{4,8},{8,12},{12,14},{14,10},{10,6},{6,2},{2,0},{1,5},{5,9},... | collective-permute-start | bytes 884744 | tf_op jit(solution)/shard_map/ppermute | solution.py:370
  186.2 129.9 %collective-permute-start.27 = (bf16[288,512]{1,0:T(8,128)(2,1)S(1)}, bf16[288,512]{1,0:T(8,128)(2,1)S(1)}, u32[]{:S(2)}, u32[]{:S(2)}) collective-permute-start(bf16[288,512]{1,0:T(8,128)(2,1)S(1)} %broadcast_select_fusion), channel_id=1, source_target_pairs={{0,2},{4,0},{8,4},{12,8},{14,12},{10,14},{6,10},{2,6},{1,3},{5,1},... | collective-permute-start | bytes 884744 | tf_op jit(solution)/shard_map/ppermute | solution.py:370
  186.9 129.2 %copy-start.6 = (bf16[288,512]{1,0:T(8,128)(2,1)S(1)}, bf16[288,512]{1,0:T(8,128)(2,1)}, u32[]{:S(2)}) copy-start(bf16[288,512]{1,0:T(8,128)(2,1)} %get-tuple-element.152) | copy-start | bytes 884740
  186.9 129.3 %copy-start.22 = (bf16[64,2048]{1,0:T(8,128)(2,1)S(1)}, bf16[64,2048]{1,0:T(8,128)(2,1)}, u32[]{:S(2)}) copy-start(bf16[64,2048]{1,0:T(8,128)(2,1)} %get-tuple-element.147) | copy-start | bytes 786436
  316.1 15.4 %copy-start.1 = (s32[3]{0:T(128)S(1)}, s32[3]{0:T(128)}, u32[]{:S(2)}) copy-start(s32[3]{0:T(128)} %pad_add_fusion.scal) | copy-start | bytes 40
  316.2 15.3 %collective-permute-start.28 = (bf16[288,512]{1,0:T(8,128)(2,1)S(1)}, bf16[288,512]{1,0:T(8,128)(2,1)S(1)}, u32[]{:S(2)}, u32[]{:S(2)}) collective-permute-start(bf16[288,512]{1,0:T(8,128)(2,1)S(1)} %select_select_fusion.mine), channel_id=1, source_target_pairs={{0,1},{1,0},{2,3},{3,2},{4,5},{5,4},{6,7},{7,6},{8,9},{9,8},{10,11... | collective-permute-start | bytes 884744 | tf_op jit(solution)/shard_map/ppermute | solution.py:373
  316.3 11.5 %collective-permute-start.25 = (bf16[64,2048]{1,0:T(8,128)(2,1)S(1)}, bf16[64,2048]{1,0:T(8,128)(2,1)S(1)}, u32[]{:S(2)}, u32[]{:S(2)}) collective-permute-start(bf16[64,2048]{1,0:T(8,128)(2,1)S(1)} %copy-done.22), channel_id=1, source_target_pairs={{0,14},{4,10},{8,6},{12,2},{14,0},{10,4},{6,8},{2,12},{1,15},{5,11... | collective-permute-start | bytes 786440 | tf_op jit(solution)/shard_map/ppermute | solution.py:370
  331.5 2.2 copy-start
  (4 other events, 4.0 us)

commit v6 on v5

--- a/solution.py
+++ b/solution.py
@@ -109,13 +109,14 @@
     part = width // 2
     here = pl.ds(pl.multiple_of(half * part, part), part)
     there = pl.ds(pl.multiple_of((1 - half) * part, part), part)
-    at = 3 * units
-    for kept, rows_x, rows_c in ((mine, rows_in, rows_cot), (hot, hot_in, hot_cot)):
-        kept[:, :part] = rows_x[:, here]
-        kept[:, part:] = rows_c[:, here]
-        pack[:, at : at + part] = rows_x[:, there]
-        pack[:, at + part : at + width] = rows_c[:, there]
-        at += width
+    mine[:, :part] = rows_in[:, here]
+    mine[:, part:] = rows_cot[:, here]
+    pack[:, 3 * units : 3 * units + part] = rows_in[:, there]
+    pack[:, 3 * units + part :] = rows_cot[:, there]
+    hot[:, :part] = hot_in[:, here]
+    hot[:, part:width] = hot_cot[:, here]
+    hot[:, width : width + part] = hot_in[:, there]
+    hot[:, width + part :] = hot_cot[:, there]
     load_gu.wait()
     projected = dot(rows_in[...], gate_up[...], (1, 0))
     gate_pre, up_pre = projected[:, :units], projected[:, units:]
@@ -142,7 +143,7 @@
     units, width = down.shape
     vmem = pl.BlockSpec(memory_space=pltpu.VMEM)
     far = pl.BlockSpec(memory_space=pl.ANY)
-    shapes = [(rows, width), (rows, 3 * units + 2 * width), (rows, width)]
+    shapes = [(rows, width), (rows, 3 * units + width), (rows, 2 * width)]
     shapes += [(capacity, width)] * count
     joined = first is not None
     if joined or count > 1:
@@ -274,54 +275,41 @@
 
 
 def order_kernel(plan, experts, capacity, scal, *refs):
-    count = len(plan)
-    mine, others, out, sems = refs[:count], refs[count : 2 * count], refs[-2], refs[-1]
+    parts, mine, theirs = refs[:-2], refs[-2], refs[-1]
     shift = to_ring(scal[0], experts) - to_ring(scal[2], experts)
-    width = out.shape[1]
-    copies = []
-    for side, parts in enumerate((mine, others)):
-        for steps, part in zip(plan, parts):
-            columns = pl.ds(part.shape[1] - width, width)
-            for at, step in enumerate(steps):
-                place = slot_place((shift + step + 2 * experts) % experts, experts)
-                there = pl.multiple_of((place + side * experts) * capacity, capacity)
-                copies.append(
-                    pltpu.make_async_copy(
-                        part.at[pl.ds(at * capacity, capacity), columns],
-                        out.at[pl.ds(there, capacity)],
-                        sems.at[len(copies)],
-                    )
-                )
-    for copy in copies:
-        copy.start()
-    for copy in copies:
-        copy.wait()
-
-
-def ordered(plan, experts, capacity, scal, mine, others):
-    far = pl.BlockSpec(memory_space=pl.ANY)
-    rows, width = 2 * experts * capacity, mine[0].shape[1]
+    width = mine.shape[1]
+    for steps, part in zip(plan, parts):
+        for at, step in enumerate(steps):
+            place = slot_place((shift + step + 2 * experts) % experts, experts)
+            there = pl.ds(pl.multiple_of(place * capacity, capacity), capacity)
+            mine[there, :] = part[at * capacity : (at + 1) * capacity, :width]
+            theirs[there, :] = part[at * capacity : (at + 1) * capacity, width:]
+
+
+def ordered(plan, experts, capacity, scal, parts):
+    vmem = pl.BlockSpec(memory_space=pltpu.VMEM)
+    rows, width = experts * capacity, parts[0].shape[1] // 2
     return pl.pallas_call(
         functools.partial(order_kernel, plan, experts, capacity),
-        out_shape=jax.ShapeDtypeStruct((rows, width), BF16),
-        in_specs=[pl.BlockSpec(memory_space=pltpu.SMEM)] + [far] * (2 * len(mine)),
-        out_specs=far,
-        scratch_shapes=[pltpu.SemaphoreType.DMA((2 * experts,))],
-        cost_estimate=pl.CostEstimate(flops=0, bytes_accessed=4 * rows * width, transcendentals=0),
+        out_shape=[jax.ShapeDtypeStruct((rows, width), BF16)] * 2,
+        in_specs=[pl.BlockSpec(memory_space=pltpu.SMEM)] + [vmem] * len(parts),
+        out_specs=[vmem] * 2,
+        compiler_params=pltpu.CompilerParams(vmem_limit_bytes=VMEM_BYTES),
+        cost_estimate=pl.CostEstimate(flops=0, bytes_accessed=8 * rows * width, transcendentals=0),
         name="hot_rows_ordered",
-    )(scal, *mine, *others)
-
-
-def shadow_kernel(experts, scal, mine, theirs, hot, out):
+    )(scal, *parts)
+
+
+def shadow_kernel(experts, scal, mine, theirs, hot_mine, hot_theirs, out):
     own = scal[0]
-    taken, rows = mine.shape
+    taken = mine.shape[0]
     width = out.shape[1]
     gates = taken * experts * 2 // 3
     column = own * taken + lax.broadcasted_iota(jnp.int32, (taken, 1), 0)
 
     def product(first):
         columns = pl.ds(first, width)
-        return dot(mine[...], hot[:rows, columns], (1, 0)) + dot(theirs[...], hot[rows:, columns], (1, 0))
+        return dot(mine[...], hot_mine[:, columns], (1, 0)) + dot(theirs[...], hot_theirs[:, columns], (1, 0))
 
     @pl.when((own + 1) * taken <= gates)
     def _():
@@ -336,21 +324,21 @@
         out[...] = jnp.where(column < gates, product(0), product(width))
 
 
-def shadow_gradient(experts, scal, mine, theirs, hot):
+def shadow_gradient(experts, scal, mine, theirs, hot_mine, hot_theirs):
     taken, rows = mine.shape
-    width = hot.shape[1] // 2
+    width = hot_mine.shape[1] // 2
     vmem = pl.BlockSpec(memory_space=pltpu.VMEM)
     return pl.pallas_call(
         functools.partial(shadow_kernel, experts),
         out_shape=jax.ShapeDtypeStruct((taken, width), F32),
-        in_specs=[pl.BlockSpec(memory_space=pltpu.SMEM)] + [vmem] * 3,
+        in_specs=[pl.BlockSpec(memory_space=pltpu.SMEM)] + [vmem] * 4,
         out_specs=vmem,
         compiler_params=pltpu.CompilerParams(vmem_limit_bytes=24 * 1024 * 1024),
         cost_estimate=pl.CostEstimate(
             flops=4 * taken * rows * width, bytes_accessed=4 * rows * width, transcendentals=0
         ),
         name="shadow_gradient",
-    )(scal, mine, theirs, hot)
+    )(scal, mine, theirs, hot_mine, hot_theirs)
 
 
 def on_device(
@@ -393,13 +381,17 @@
         elif 0 < number < half - 1:
             held, late[number - 1] = lax.optimization_barrier((held, late[number - 1]))
         (rows, pack, hot_rows), back, turn = run_step(
-            steps, fanout, capacity, scal, held, packs[0] if number == half else None, gate_up, down
+            steps,
+            fanout,
+            capacity,
+            scal,
+            held,
+            packs[0] if number == half else None,
+            gate_up,
+            down,
         )
         following, back = lax.optimization_barrier((following, back))
-        if number < half:
-            sent = [shift(part, step) if step else part for step, part in zip(steps, back)]
-        else:
-            sent = back
+        sent = [shift(part, step) if step else part for step, part in zip(steps, back)]
         late.append((sent, swap(pack)))
         mine.append(rows)
         packs.append(pack)
@@ -429,27 +421,30 @@
     expert_grad = expert_gradient(units, scal, mine, packs, others)
     chunks = [chunk(distance) for distance in range(1 - half, half)]
     (back_far,) = late[half][0]
+    hot_mine, hot_theirs = ordered(plan, experts, capacity, scal, hot)
     for number in range(1, half):
         if number == 1:
             around, expert_grad, back_behind, chunks = lax.optimization_barrier(
                 (around, expert_grad, back_behind, chunks)
             )
             around = [jnp.concatenate([part, part], axis=1) for part in around]
+        if number == 2:
+            around, back_far = lax.optimization_barrier((around, back_far))
         if number == half - 1:
-            around, back_far = lax.optimization_barrier((around, back_far))
+            around, hot_mine, hot_theirs = lax.optimization_barrier((around, hot_mine, hot_theirs))
         ahead = jnp.where(is_hot, chunks[2 * half - 1 - number], around[0])
         behind = jnp.where(is_hot, chunks[number - 1], around[1])
         around = [shift(ahead, 1), shift(behind, -1)]
-    back_far = shift(back_far, half)
-    hot_rows = ordered(plan, experts, capacity, scal, hot, others)
-    around, hot_rows = lax.optimization_barrier((around, hot_rows))
+    hot_theirs = swap(hot_theirs)
     away = (to_ring(own, experts) - ring_hot + experts) % experts
     lane = lax.broadcasted_iota(jnp.int32, far.shape, 1)
     reach = jnp.where(lane < lanes, half, half - 1)
     columns = jnp.where(
         away == 0, chunks[half - 1], jnp.where(away <= reach, around[0], around[1])
     )
-    shadow_grad = shadow_gradient(experts, scal, columns, swap(columns), hot_rows).T
+    shadow_grad = shadow_gradient(
+        experts, scal, columns, swap(columns), hot_mine, hot_theirs
+    ).T
     sent = [rows for rows, _ in late[: half - 1]] + [[back_behind, back_ahead], [back_far]]
     for steps, parts in zip(plan, sent):
         for step, part in zip(steps, parts):

time: 339 us -> 198 us (0.58)
  Pallas kernels: 198 us -> 71.9 us
  waiting for transfers between devices: 86.5 us -> 73.1 us
  local copies, waits for them, and re-layouts: 10.4 us -> 5.83 us
  starting transfers between devices: 37.8 us -> 42.1 us
    pallas_call x1, Pallas kernels: 129 us -> 4.5 us  [ordered(): pl.pallas_call(functools.partial(order_kernel, plan, experts, capacity),...]
    ppermute x23, waiting for transfers between devices: 86.5 us -> 73.1 us  [shift(): return lax.ppermute(block, 'expert', pairs)]
    ppermute x23, starting transfers between devices: 37.3 us -> 41.8 us  [shift(): return lax.ppermute(block, 'expert', pairs)]
  transfers between devices with their start and end apart: 29 -> 30, of which waited for: 12 -> 14; matrix products, arithmetic and copies ran while one was open for 2% -> 3% of each run, Pallas kernels for 54% -> 34%
where the time goes in v6:
time: 198 us; the launch traced here: 197 us
  waiting for transfers between devices  73.1 us (37%)
  Pallas kernels  71.9 us (36%)
  starting transfers between devices  42.1 us (21%)
  local copies, waits for them, and re-layouts  5.83 us (3%)
  other arithmetic  2.26 us (1%)
  between operations  2.03 us (1%)
    ppermute x23, waiting for transfers between devices, shift(): return lax.ppermute(block, 'expert', pairs)  73.1 us
    pallas_call x5, Pallas kernels, run_step(): pl.pallas_call(functools.partial(step_kernel, steps, fanout, capacity, jo...  48.9 us
    ppermute x23, starting transfers between devices, shift(): return lax.ppermute(block, 'expert', pairs)  41.8 us
    pallas_call x1, Pallas kernels, expert_gradient(): pl.pallas_call(functools.partial(gradient_kernel, units, count), grid=(ti...  10.7 us
    pallas_call x1, Pallas kernels, ordered(): pl.pallas_call(functools.partial(order_kernel, plan, experts, capacity),...  4.5 us
  transfers between devices with their start and end apart: 30, of which 14 were waited for; matrix products, arithmetic and copies ran while one was open for 3% of the time, Pallas kernels for 34%

profile of v6, /device:TPU:0, one launch (start us, length us, event | category | flops | bytes accessed | tf_op | source)
XLA Modules:
  0.0 197.3 jit_solution(3212584203165107426)
XLA Ops:
  0.6 2.3 %ring_message.1 = (bf16[128,4224]{1,0:T(8,128)(2,1)}, bf16[128,128]{1,0:T(8,128)(2,1)}) custom-call(bf16[128,2048]{1,0:T(8,128)(2,1)} %tokens.1, bf16[128,2048]{1,0:T(8,128)(2,1)} %cotangent.1, s32[2,128]{1,0:T(2,128)} %bitcast.17, f32[2,128]{1,0:T(2,128)} %bitcast.18, f32[1,128]{1,0:T(1,128)} %bitcast.19, s32[1,128]{1,0:T(1,128)} %bitcast.20), custom_call_target="tpu_custom_call" | custom-call | bytes 2097152 | tf_op jit(solution)/shard_map/ring_message/pallas_call | solution.py:264
  3.0 3.0 %collective-permute-start.1 = (bf16[128,4224]{1,0:T(8,128)(2,1)}, bf16[128,4224]{1,0:T(8,128)(2,1)S(1)}, u32[]{:S(2)}, u32[]{:S(2)}) collective-permute-start(bf16[128,4224]{1,0:T(8,128)(2,1)} %get-tuple-element.88.refs_0_), channel_id=1, source_target_pairs={{0,2},{4,0},{8,4},{12,8},{14,12},{10,14},{6,10},{2,6},{1,3},{5,1},... | collective-permute-start | bytes 3244040 | tf_op jit(solution)/shard_map/ppermute | solution.py:358
  6.6 0.7 pad_add_fusion.scal
  7.3 9.4 %expert_step.5 = (bf16[64,2048]{1,0:T(8,128)(2,1)}, bf16[64,4352]{1,0:T(8,128)(2,1)}, bf16[64,4096]{1,0:T(8,128)(2,1)}, bf16[64,2048]{1,0:T(8,128)(2,1)}) custom-call(s32[3]{0:T(128)} %pad_add_fusion.scal, bf16[128,4224]{1,0:T(8,128)(2,1)} %get-tuple-element.88.refs_0_, bf16[2048,1536]{1,0:T(8,128)(2,1)} %bitcast.21, bf16[768,2048]{1,0:T(8,128)(2,1)} %bitcast.26), custom_call_target="tpu_custom_call" | custom-call | flops 4026531840 | bytes 9437184 | tf_op jit(solution)/shard_map/expert_step/pallas_call | solution.py:152
  16.7 13.3 %collective-permute-done.1.refs_1_ = bf16[128,4224]{1,0:T(8,128)(2,1)S(1)} collective-permute-done((bf16[128,4224]{1,0:T(8,128)(2,1)}, bf16[128,4224]{1,0:T(8,128)(2,1)S(1)}, u32[]{:S(2)}, u32[]{:S(2)}) %collective-permute-start.1) | collective-permute-done | bytes 1081376 | tf_op jit(solution)/shard_map/ppermute | solution.py:358
  30.0 1.5 collective-permute-done.refs_0_
  31.6 0.4 collective-permute-start.3
  31.9 1.7 collective-permute-start.4
  33.6 10.0 %expert_step.6 = (bf16[128,2048]{1,0:T(8,128)(2,1)}, bf16[128,4352]{1,0:T(8,128)(2,1)}, bf16[128,4096]{1,0:T(8,128)(2,1)}, bf16[64,2048]{1,0:T(8,128)(2,1)}, bf1...) custom-call(s32[3]{0:T(128)} %pad_add_fusion.scal, bf16[128,4224]{1,0:T(8,128)(2,1)} %collective-permute-done.refs_0_, ...), custom_call_target="tpu_custom_call" | custom-call | flops 4026531840 | bytes 9437184 | tf_op jit(solution)/shard_map/expert_step/pallas_call | solution.py:152
  43.7 12.6 %collective-permute-done.3.refs_0_ = bf16[128,4224]{1,0:T(8,128)(2,1)} collective-permute-done((bf16[128,4224]{1,0:T(8,128)(2,1)}, bf16[128,4224]{1,0:T(8,128)(2,1)}, u32[]{:S(2)}, u32[]{:S(2)}) %collective-permute-start.3) | collective-permute-done | bytes 1081376 | tf_op jit(solution)/shard_map/ppermute | solution.py:358
  56.5 1.4 collective-permute-start.5
  57.9 0.6 collective-permute-start.6
  58.5 1.6 collective-permute-start.8
  60.1 0.4 collective-permute-start.9
  60.5 5.4 %collective-permute-done.5.refs_7_ = bf16[64,2048]{1,0:T(8,128)(2,1)S(1)} collective-permute-done((bf16[64,2048]{1,0:T(8,128)(2,1)}, bf16[64,2048]{1,0:T(8,128)(2,1)S(1)}, u32[]{:S(2)}, u32[]{:S(2)}) %collective-permute-start.5) | collective-permute-done | bytes 262176 | tf_op jit(solution)/shard_map/ppermute | solution.py:358
  65.9 1.4 collective-permute-done.6.refs_1_
  67.3 9.9 %expert_step.7 = (bf16[128,2048]{1,0:T(8,128)(2,1)}, bf16[128,4352]{1,0:T(8,128)(2,1)}, bf16[128,4096]{1,0:T(8,128)(2,1)}, bf16[64,2048]{1,0:T(8,128)(2,1)}, bf1...) custom-call(s32[3]{0:T(128)} %pad_add_fusion.scal, bf16[128,4224]{1,0:T(8,128)(2,1)} %collective-permute-done.3.refs_0_, ...), custom_call_target="tpu_custom_call" | custom-call | flops 4026531840 | bytes 9437184 | tf_op jit(solution)/shard_map/expert_step/pallas_call | solution.py:152
  77.7 9.3 %collective-permute-done.8.refs_0_ = bf16[128,4224]{1,0:T(8,128)(2,1)} collective-permute-done((bf16[128,4224]{1,0:T(8,128)(2,1)}, bf16[128,4224]{1,0:T(8,128)(2,1)}, u32[]{:S(2)}, u32[]{:S(2)}) %collective-permute-start.8) | collective-permute-done | bytes 1081376 | tf_op jit(solution)/shard_map/ppermute | solution.py:358
  87.0 1.4 slice.10
  88.5 0.7 collective-permute-start.10
  89.2 1.4 collective-permute-start.11
  90.7 2.6 %collective-permute-start.12 = (bf16[64,2048]{1,0:T(8,128)(2,1)}, bf16[64,2048]{1,0:T(8,128)(2,1)S(1)}, u32[]{:S(2)}, u32[]{:S(2)}) collective-permute-start(bf16[64,2048]{1,0:T(8,128)(2,1)} %get-tuple-element.115), channel_id=1, source_target_pairs={{0,6},{4,2},{8,0},{12,4},{14,8},{10,12},{6,14},{2,10},{1,7},{5,3},... | collective-permute-start | bytes 786440 | tf_op jit(solution)/shard_map/ppermute | solution.py:358
  93.3 0.3 collective-permute-start.13
  93.7 9.8 %expert_step.8 = (bf16[128,2048]{1,0:T(8,128)(2,1)}, bf16[128,4352]{1,0:T(8,128)(2,1)}, bf16[128,4096]{1,0:T(8,128)(2,1)}, bf16[64,2048]{1,0:T(8,128)(2,1)}, bf1...) custom-call(s32[3]{0:T(128)} %pad_add_fusion.scal, bf16[128,4224]{1,0:T(8,128)(2,1)} %collective-permute-done.8.refs_0_, ...), custom_call_target="tpu_custom_call" | custom-call | flops 4026531840 | bytes 9437184 | tf_op jit(solution)/shard_map/expert_step/pallas_call | solution.py:152
  103.5 1.3 constant_dynamic-slice_fusion.1
  104.8 0.8 copy-done.20
  105.7 6.4 %collective-permute-done.12.refs_6_ = bf16[64,2048]{1,0:T(8,128)(2,1)S(1)} collective-permute-done((bf16[64,2048]{1,0:T(8,128)(2,1)}, bf16[64,2048]{1,0:T(8,128)(2,1)S(1)}, u32[]{:S(2)}, u32[]{:S(2)}) %collective-permute-start.12) | collective-permute-done | bytes 262176 | tf_op jit(solution)/shard_map/ppermute | solution.py:358
  112.1 0.9 collective-permute-start.15
  113.0 3.0 %collective-permute-start.20 = (bf16[64,2048]{1,0:T(8,128)(2,1)}, bf16[64,2048]{1,0:T(8,128)(2,1)S(1)}, u32[]{:S(2)}, u32[]{:S(2)}) collective-permute-start(bf16[64,2048]{1,0:T(8,128)(2,1)} %get-tuple-element.141), channel_id=1, source_target_pairs={{0,10},{4,6},{8,2},{12,0},{14,4},{10,8},{6,12},{2,14},{1,11},{5,7}... | collective-permute-start | bytes 786440 | tf_op jit(solution)/shard_map/ppermute | solution.py:358
  116.0 9.7 %expert_step.9 = (bf16[64,2048]{1,0:T(8,128)(2,1)}, bf16[64,4352]{1,0:T(8,128)(2,1)}, bf16[64,4096]{1,0:T(8,128)(2,1)}, bf16[64,2048]{1,0:T(8,128)(2,1)}, bf16[2304,128]{1,0:T(8,128)(2,1)}) custom-call(s32[3]{0:T(128)} %pad_add_fusion.scal, bf16[128,2048]{1,0:T(8,128)(2,1)} %copy-done.20, bf16[128,2176]{1,0:T(8,128)(2,1)} %copy-done.19, ...), custom_call_target="tpu_custom_call" | custom-call | flops 4026531840 | bytes 9437184 | tf_op jit(solution)/shard_map/expert_step/pallas_call | solution.py:152
  125.9 1.3 constant_dynamic-slice_fusion
  127.5 9.0 %collective-permute-start.17 = (bf16[288,256]{1,0:T(8,128)(2,1)S(1)}, bf16[288,256]{1,0:T(8,128)(2,1)S(1)}, u32[]{:S(2)}, u32[]{:S(2)}) collective-permute-start(bf16[288,256]{1,0:T(8,128)(2,1)S(1)} %get-tuple-element.129), channel_id=1, source_target_pairs={{0,4},{4,8},{8,12},{12,14},{14,10},{10,6},{6,2},{2,0},{1,5},{5,9},... | collective-permute-start | bytes 442376 | tf_op jit(solution)/shard_map/ppermute | solution.py:358
  136.6 0.3 collective-permute-start.18
  136.9 0.8 copy-done.6
  137.7 10.7 %expert_gradient.1 = f32[1,1024,2304]{2,1,0:T(8,128)} custom-call(s32[3]{0:T(128)} %pad_add_fusion.scal, bf16[64,2048]{1,0:T(8,128)(2,1)} %get-tuple-element.131.refs_0_.refs_10_, bf16[128,2048]{1,0:T(8,128)(2,1)} %get-tuple-element.132.refs_1_.refs_11_, bf16[128,2048]{1,0:T(8,128)(2,1)} %get-tuple-element.133.refs_2_.refs_12_, ...), custom_call_target="tpu_custom_call" | custom-call | flops 4831838208 | bytes 14155776 | tf_op jit(solution)/shard_map/expert_gradient/pallas_call | solution.py:227
  148.6 2.0 %collective-permute-start.22 = (bf16[288,512]{1,0:T(8,128)(2,1)S(1)}, bf16[288,512]{1,0:T(8,128)(2,1)S(1)}, u32[]{:S(2)}, u32[]{:S(2)}) collective-permute-start(bf16[288,512]{1,0:T(8,128)(2,1)S(1)} %maximum_select_fusion.1), channel_id=1, source_target_pairs={{0,2},{4,0},{8,4},{12,8},{14,12},{10,14},{6,10},{2,6},{1,3},{5,1},... | collective-permute-start | bytes 884744 | tf_op jit(solution)/shard_map/ppermute | solution.py:358
  150.9 4.9 %collective-permute-start.23 = (bf16[64,2048]{1,0:T(8,128)(2,1)S(1)}, bf16[64,2048]{1,0:T(8,128)(2,1)S(1)}, u32[]{:S(2)}, u32[]{:S(2)}) collective-permute-start(bf16[64,2048]{1,0:T(8,128)(2,1)S(1)} %copy-done.21), channel_id=1, source_target_pairs={{0,14},{4,10},{8,6},{12,2},{14,0},{10,4},{6,8},{2,12},{1,15},{5,11... | collective-permute-start | bytes 786440 | tf_op jit(solution)/shard_map/ppermute | solution.py:358
  155.8 12.2 %collective-permute-done.23.refs_4_ = bf16[64,2048]{1,0:T(8,128)(2,1)S(1)} collective-permute-done((bf16[64,2048]{1,0:T(8,128)(2,1)S(1)}, bf16[64,2048]{1,0:T(8,128)(2,1)S(1)}, u32[]{:S(2)}, u32[]{:S(2)}) %collective-permute-start.23) | collective-permute-done | bytes 262176 | tf_op jit(solution)/shard_map/ppermute | solution.py:358
  168.1 5.0 %collective-permute-start.24 = (bf16[288,512]{1,0:T(8,128)(2,1)S(1)}, bf16[288,512]{1,0:T(8,128)(2,1)S(1)}, u32[]{:S(2)}, u32[]{:S(2)}) collective-permute-start(bf16[288,512]{1,0:T(8,128)(2,1)S(1)} %broadcast_select_fusion.3), channel_id=1, source_target_pairs={{0,4},{4,8},{8,12},{12,14},{14,10},{10,6},{6,2},{2,0},{1,5},{5,9},... | collective-permute-start | bytes 884744 | tf_op jit(solution)/shard_map/ppermute | solution.py:358
  173.2 4.5 %hot_rows_ordered.1 = (bf16[512,2048]{1,0:T(8,128)(2,1)}, bf16[512,2048]{1,0:T(8,128)(2,1)}) custom-call(s32[3]{0:T(128)} %pad_add_fusion.scal, bf16[64,4096]{1,0:T(8,128)(2,1)} %get-tuple-element.159.refs_0_, bf16[128,4096]{1,0:T(8,128)(2,1)} %get-tuple-element.160.refs_1_, bf16[128,4096]{1,0:T(8,128)(2,1)} %get-tuple-element.161.refs_2_, ...), custom_call_target="tpu_custom_call" | custom-call | bytes 8388608 | tf_op jit(solution)/shard_map/hot_rows_ordered/pallas_call | solution.py:292
  177.7 0.9 collective-permute-done.24
  178.6 2.3 %collective-permute-done.25 = bf16[288,512]{1,0:T(8,128)(2,1)S(1)} collective-permute-done((bf16[288,512]{1,0:T(8,128)(2,1)S(1)}, bf16[288,512]{1,0:T(8,128)(2,1)S(1)}, u32[]{:S(2)}, u32[]{:S(2)}) %collective-permute-start.25) | collective-permute-done | bytes 294944 | tf_op jit(solution)/shard_map/ppermute | solution.py:358
  180.9 0.3 collective-permute-start.27
  181.3 1.8 collective-permute-start.26
  183.1 7.3 %collective-permute-done.27 = bf16[288,512]{1,0:T(8,128)(2,1)S(1)} collective-permute-done((bf16[288,512]{1,0:T(8,128)(2,1)S(1)}, bf16[288,512]{1,0:T(8,128)(2,1)S(1)}, u32[]{:S(2)}, u32[]{:S(2)}) %collective-permute-start.27) | collective-permute-done | bytes 294944 | tf_op jit(solution)/shard_map/ppermute | solution.py:358
  190.6 1.0 select_select_fusion.mine
  191.7 3.2 %token_sum.1 = bf16[128,2048]{1,0:T(8,128)(2,1)} custom-call(s32[3]{0:T(128)} %pad_add_fusion.scal, bf16[128,128]{1,0:T(8,128)(2,1)} %get-tuple-element.87.meta, bf16[64,2048]{1,0:T(8,128)(2,1)} %get-tuple-element.94.refs_0_, bf16[64,2048]{1,0:T(8,128)(2,1)} %copy-done.12, bf16[64,2048]{1,0:T(8,128)(2,1)} %copy-done.14, bf16[64,2048]{1,0:T(8,128)(2,1)} %copy-done.15, ...), custom_call_target="tpu_custom_call" | custom-call | flops 268435456 | bytes 2097152 | tf_op jit(solution)/shard_map/token_sum/pallas_call | solution.py:187
  194.9 2.3 %shadow_gradient.1 = f32[288,1024]{1,0:T(8,128)} custom-call(s32[3]{0:T(128)S(1)} %copy-done.1, bf16[288,512]{1,0:T(8,128)(2,1)S(1)} %select_select_fusion.mine, bf16[288,512]{1,0:T(8,128)(2,1)S(1)} %collective-permute-done.28.theirs, bf16[512,2048]{1,0:T(8,128)(2,1)S(1)} %copy-done, bf16[512,2048]{1,0:T(8,128)(2,1)S(1)} %collective-permute-done.29.hot_theirs), custom_call_target="tpu_custom_call" | custom-call | flops 603979776 | bytes 2097152 | tf_op jit(solution)/shard_map/shadow_gradient/pallas_call | solution.py:331
  (86 shorter events, 1.9 us)
Async XLA Ops:
  3.0 27.1 %collective-permute-start.1 = (bf16[128,4224]{1,0:T(8,128)(2,1)}, bf16[128,4224]{1,0:T(8,128)(2,1)S(1)}, u32[]{:S(2)}, u32[]{:S(2)}) collective-permute-start(bf16[128,4224]{1,0:T(8,128)(2,1)} %get-tuple-element.88.refs_0_), channel_id=1, source_target_pairs={{0,2},{4,0},{8,4},{12,8},{14,12},{10,14},{6,10},{2,6},{1,3},{5,1},... | collective-permute-start | bytes 3244040 | tf_op jit(solution)/shard_map/ppermute | solution.py:358
  5.9 25.6 %collective-permute-start = (bf16[128,4224]{1,0:T(8,128)(2,1)}, bf16[128,4224]{1,0:T(8,128)(2,1)}, u32[]{:S(2)}, u32[]{:S(2)}) collective-permute-start(bf16[128,4224]{1,0:T(8,128)(2,1)} %get-tuple-element.88.refs_0_), channel_id=1, source_target_pairs={{0,4},{4,8},{8,12},{12,14},{14,10},{10,6},{6,2},{2,0},{1,5},{5,9},... | collective-permute-start | bytes 3244040 | tf_op jit(solution)/shard_map/ppermute | solution.py:358
  16.7 16.9 %collective-permute-start.2 = (bf16[64,4352]{1,0:T(8,128)(2,1)}, bf16[64,4352]{1,0:T(8,128)(2,1)S(1)}, u32[]{:S(2)}, u32[]{:S(2)}) collective-permute-start(bf16[64,4352]{1,0:T(8,128)(2,1)} %get-tuple-element.93.refs_2_.refs_20_), channel_id=1, source_target_pairs={{0,1},{1,0},{2,3},{3,2},{4,5},{5,4},{6,7},{7,6},{8,9},{9,8},{10,11... | collective-permute-start | bytes 1671176 | tf_op jit(solution)/shard_map/ppermute | solution.py:361
  30.0 3.5 %copy-start.18 = (bf16[128,4224]{1,0:T(8,128)(2,1)}, bf16[128,4224]{1,0:T(8,128)(2,1)S(1)}, u32[]{:S(2)}) copy-start(bf16[128,4224]{1,0:T(8,128)(2,1)S(1)} %collective-permute-done.1.refs_1_) | copy-start | bytes 3244036
  31.6 24.7 %collective-permute-start.3 = (bf16[128,4224]{1,0:T(8,128)(2,1)}, bf16[128,4224]{1,0:T(8,128)(2,1)}, u32[]{:S(2)}, u32[]{:S(2)}) collective-permute-start(bf16[128,4224]{1,0:T(8,128)(2,1)} %collective-permute-done.refs_0_), channel_id=1, source_target_pairs={{0,4},{4,8},{8,12},{12,14},{14,10},{10,6},{6,2},{2,0},{1,5},{5,9},... | collective-permute-start | bytes 3244040 | tf_op jit(solution)/shard_map/ppermute | solution.py:358
  31.9 24.6 %collective-permute-start.4 = (bf16[128,4224]{1,0:T(8,128)(2,1)S(1)}, bf16[128,4224]{1,0:T(8,128)(2,1)}, u32[]{:S(2)}, u32[]{:S(2)}) collective-permute-start(bf16[128,4224]{1,0:T(8,128)(2,1)S(1)} %collective-permute-done.1.refs_1_), channel_id=1, source_target_pairs={{0,2},{4,0},{8,4},{12,8},{14,12},{10,14},{6,10},{2,6},{1,3},{5,1},... | collective-permute-start | bytes 3244040 | tf_op jit(solution)/shard_map/ppermute | solution.py:358
  33.6 10.1 %copy-start.5 = (bf16[64,4352]{1,0:T(8,128)(2,1)}, bf16[64,4352]{1,0:T(8,128)(2,1)S(1)}, u32[]{:S(2)}) copy-start(bf16[64,4352]{1,0:T(8,128)(2,1)S(1)} %collective-permute-done.2.refs_5_.refs_15_.refs_25_) | copy-start | bytes 1671172
  43.6 16.9 %collective-permute-start.7 = (bf16[128,4352]{1,0:T(8,128)(2,1)}, bf16[128,4352]{1,0:T(8,128)(2,1)S(1)}, u32[]{:S(2)}, u32[]{:S(2)}) collective-permute-start(bf16[128,4352]{1,0:T(8,128)(2,1)} %get-tuple-element.103.refs_21_), channel_id=1, source_target_pairs={{0,1},{1,0},{2,3},{3,2},{4,5},{5,4},{6,7},{7,6},{8,9},{9,8},{10,11... | collective-permute-start | bytes 3342344 | tf_op jit(solution)/shard_map/ppermute | solution.py:361
  56.5 21.2 %copy-start.8 = (bf16[2304,128]{1,0:T(8,128)(2,1)S(1)}, bf16[2304,128]{1,0:T(8,128)(2,1)}, u32[]{:S(2)}) copy-start(bf16[2304,128]{1,0:T(8,128)(2,1)} %get-tuple-element.124) | copy-start | bytes 1769476
  56.5 9.5 %collective-permute-start.5 = (bf16[64,2048]{1,0:T(8,128)(2,1)}, bf16[64,2048]{1,0:T(8,128)(2,1)S(1)}, u32[]{:S(2)}, u32[]{:S(2)}) collective-permute-start(bf16[64,2048]{1,0:T(8,128)(2,1)} %get-tuple-element.101), channel_id=1, source_target_pairs={{0,2},{4,0},{8,4},{12,8},{14,12},{10,14},{6,10},{2,6},{1,3},{5,1},... | collective-permute-start | bytes 786440 | tf_op jit(solution)/shard_map/ppermute | solution.py:358
  57.9 9.5 %collective-permute-start.6 = (bf16[64,2048]{1,0:T(8,128)(2,1)}, bf16[64,2048]{1,0:T(8,128)(2,1)S(1)}, u32[]{:S(2)}, u32[]{:S(2)}) collective-permute-start(bf16[64,2048]{1,0:T(8,128)(2,1)} %get-tuple-element.102), channel_id=1, source_target_pairs={{0,4},{4,8},{8,12},{12,14},{14,10},{10,6},{6,2},{2,0},{1,5},{5,9},... | collective-permute-start | bytes 786440 | tf_op jit(solution)/shard_map/ppermute | solution.py:358
  58.5 28.5 %collective-permute-start.8 = (bf16[128,4224]{1,0:T(8,128)(2,1)}, bf16[128,4224]{1,0:T(8,128)(2,1)}, u32[]{:S(2)}, u32[]{:S(2)}) collective-permute-start(bf16[128,4224]{1,0:T(8,128)(2,1)} %collective-permute-done.3.refs_0_), channel_id=1, source_target_pairs={{0,4},{4,8},{8,12},{12,14},{14,10},{10,6},{6,2},{2,0},{1,5},{5,9},... | collective-permute-start | bytes 3244040 | tf_op jit(solution)/shard_map/ppermute | solution.py:358
  60.1 26.9 %collective-permute-start.9 = (bf16[128,4224]{1,0:T(8,128)(2,1)}, bf16[128,4224]{1,0:T(8,128)(2,1)S(1)}, u32[]{:S(2)}, u32[]{:S(2)}) collective-permute-start(bf16[128,4224]{1,0:T(8,128)(2,1)} %collective-permute-done.4.refs_1_), channel_id=1, source_target_pairs={{0,2},{4,0},{8,4},{12,8},{14,12},{10,14},{6,10},{2,6},{1,3},{5,1},... | collective-permute-start | bytes 3244040 | tf_op jit(solution)/shard_map/ppermute | solution.py:358
  60.5 16.7 %copy-start.2 = (bf16[128,4352]{1,0:T(8,128)(2,1)}, bf16[128,4352]{1,0:T(8,128)(2,1)S(1)}, u32[]{:S(2)}) copy-start(bf16[128,4352]{1,0:T(8,128)(2,1)S(1)} %collective-permute-done.7.refs_6_.refs_16_.refs_26_) | copy-start | bytes 3342340
  65.9 11.3 %copy-start.11 = (bf16[64,2048]{1,0:T(8,128)(2,1)}, bf16[64,2048]{1,0:T(8,128)(2,1)S(1)}, u32[]{:S(2)}) copy-start(bf16[64,2048]{1,0:T(8,128)(2,1)S(1)} %collective-permute-done.5.refs_7_) | copy-start | bytes 786436
  67.3 9.9 %copy-start.12 = (bf16[64,2048]{1,0:T(8,128)(2,1)}, bf16[64,2048]{1,0:T(8,128)(2,1)S(1)}, u32[]{:S(2)}) copy-start(bf16[64,2048]{1,0:T(8,128)(2,1)S(1)} %collective-permute-done.6.refs_1_) | copy-start | bytes 786436
  77.3 34.9 %collective-permute-start.14 = (bf16[128,4352]{1,0:T(8,128)(2,1)}, bf16[128,4352]{1,0:T(8,128)(2,1)S(1)}, u32[]{:S(2)}, u32[]{:S(2)}) collective-permute-start(bf16[128,4352]{1,0:T(8,128)(2,1)} %get-tuple-element.117.refs_22_), channel_id=1, source_target_pairs={{0,1},{1,0},{2,3},{3,2},{4,5},{5,4},{6,7},{7,6},{8,9},{9,8},{10,11... | collective-permute-start | bytes 3342344 | tf_op jit(solution)/shard_map/ppermute | solution.py:361
  77.7 12.9 %copy-start.9 = (bf16[2304,128]{1,0:T(8,128)(2,1)S(1)}, bf16[2304,128]{1,0:T(8,128)(2,1)}, u32[]{:S(2)}) copy-start(bf16[2304,128]{1,0:T(8,128)(2,1)} %get-tuple-element.125) | copy-start | bytes 1769476
  87.0 3.7 %copy-start.10 = (bf16[128,4224]{1,0:T(8,128)(2,1)}, bf16[128,4224]{1,0:T(8,128)(2,1)S(1)}, u32[]{:S(2)}) copy-start(bf16[128,4224]{1,0:T(8,128)(2,1)S(1)} %collective-permute-done.9.refs_1_) | copy-start | bytes 3244036
  88.5 16.4 %collective-permute-start.10 = (bf16[128,2048]{1,0:T(8,128)(2,1)S(1)}, bf16[128,2048]{1,0:T(8,128)(2,1)S(1)}, u32[]{:S(2)}, u32[]{:S(2)}) collective-permute-start(bf16[128,2048]{1,0:T(8,128)(2,1)S(1)} %slice.10), channel_id=1, source_target_pairs={{0,4},{4,8},{8,12},{12,14},{14,10},{10,6},{6,2},{2,0},{1,5},{5,9},... | collective-permute-start | bytes 1572872 | tf_op jit(solution)/shard_map/ppermute | solution.py:358
  89.2 16.5 %collective-permute-start.11 = (bf16[128,2176]{1,0:T(8,128)(2,1)S(1)}, bf16[128,2176]{1,0:T(8,128)(2,1)S(1)}, u32[]{:S(2)}, u32[]{:S(2)}) collective-permute-start(bf16[128,2176]{1,0:T(8,128)(2,1)S(1)} %slice.11), channel_id=1, source_target_pairs={{0,2},{4,0},{8,4},{12,8},{14,12},{10,14},{6,10},{2,6},{1,3},{5,1},... | collective-permute-start | bytes 1671176 | tf_op jit(solution)/shard_map/ppermute | solution.py:358
  90.7 21.4 %collective-permute-start.12 = (bf16[64,2048]{1,0:T(8,128)(2,1)}, bf16[64,2048]{1,0:T(8,128)(2,1)S(1)}, u32[]{:S(2)}, u32[]{:S(2)}) collective-permute-start(bf16[64,2048]{1,0:T(8,128)(2,1)} %get-tuple-element.115), channel_id=1, source_target_pairs={{0,6},{4,2},{8,0},{12,4},{14,8},{10,12},{6,14},{2,10},{1,7},{5,3},... | collective-permute-start | bytes 786440 | tf_op jit(solution)/shard_map/ppermute | solution.py:358
  93.3 18.8 %collective-permute-start.13 = (bf16[64,2048]{1,0:T(8,128)(2,1)}, bf16[64,2048]{1,0:T(8,128)(2,1)S(1)}, u32[]{:S(2)}, u32[]{:S(2)}) collective-permute-start(bf16[64,2048]{1,0:T(8,128)(2,1)} %get-tuple-element.116), channel_id=1, source_target_pairs={{0,8},{4,12},{8,14},{12,10},{14,6},{10,2},{6,0},{2,4},{1,9},{5,13}... | collective-permute-start | bytes 786440 | tf_op jit(solution)/shard_map/ppermute | solution.py:358
  105.6 21.9 %collective-permute-start.16 = (bf16[128,4352]{1,0:T(8,128)(2,1)S(1)}, bf16[128,4352]{1,0:T(8,128)(2,1)S(1)}, u32[]{:S(2)}, u32[]{:S(2)}) collective-permute-start(bf16[128,4352]{1,0:T(8,128)(2,1)S(1)} %copy-done.7), channel_id=1, source_target_pairs={{0,1},{1,0},{2,3},{3,2},{4,5},{5,4},{6,7},{7,6},{8,9},{9,8},{10,11... | collective-permute-start | bytes 3342344 | tf_op jit(solution)/shard_map/ppermute | solution.py:361
  105.7 6.4 %copy-start.19 = (bf16[128,2176]{1,0:T(8,128)(2,1)}, bf16[128,2176]{1,0:T(8,128)(2,1)S(1)}, u32[]{:S(2)}) copy-start(bf16[128,2176]{1,0:T(8,128)(2,1)S(1)} %collective-permute-done.11.refs_1_) | copy-start | bytes 1671172
  112.1 13.6 %copy-start.13 = (bf16[64,2048]{1,0:T(8,128)(2,1)}, bf16[64,2048]{1,0:T(8,128)(2,1)S(1)}, u32[]{:S(2)}) copy-start(bf16[64,2048]{1,0:T(8,128)(2,1)S(1)} %collective-permute-done.12.refs_6_) | copy-start | bytes 786436
  112.1 13.6 %copy-start.14 = (bf16[64,2048]{1,0:T(8,128)(2,1)}, bf16[64,2048]{1,0:T(8,128)(2,1)S(1)}, u32[]{:S(2)}) copy-start(bf16[64,2048]{1,0:T(8,128)(2,1)S(1)} %collective-permute-done.13.refs_2_) | copy-start | bytes 786436
  112.1 13.6 %copy-start.3 = (bf16[128,4352]{1,0:T(8,128)(2,1)}, bf16[128,4352]{1,0:T(8,128)(2,1)S(1)}, u32[]{:S(2)}) copy-start(bf16[128,4352]{1,0:T(8,128)(2,1)S(1)} %collective-permute-done.14.refs_7_.refs_17_.refs_27_) | copy-start | bytes 3342340
  112.1 13.7 %collective-permute-start.15 = (bf16[64,2048]{1,0:T(8,128)(2,1)}, bf16[64,2048]{1,0:T(8,128)(2,1)S(1)}, u32[]{:S(2)}, u32[]{:S(2)}) collective-permute-start(bf16[64,2048]{1,0:T(8,128)(2,1)} %get-tuple-element.122), channel_id=1, source_target_pairs={{0,12},{4,14},{8,10},{12,6},{14,2},{10,0},{6,4},{2,8},{1,13},{5,15... | collective-permute-start | bytes 786440 | tf_op jit(solution)/shard_map/ppermute | solution.py:358
  113.0 35.5 %collective-permute-start.20 = (bf16[64,2048]{1,0:T(8,128)(2,1)}, bf16[64,2048]{1,0:T(8,128)(2,1)S(1)}, u32[]{:S(2)}, u32[]{:S(2)}) collective-permute-start(bf16[64,2048]{1,0:T(8,128)(2,1)} %get-tuple-element.141), channel_id=1, source_target_pairs={{0,10},{4,6},{8,2},{12,0},{14,4},{10,8},{6,12},{2,14},{1,11},{5,7}... | collective-permute-start | bytes 786440 | tf_op jit(solution)/shard_map/ppermute | solution.py:358
  125.8 11.1 %collective-permute-start.19 = (bf16[64,4352]{1,0:T(8,128)(2,1)}, bf16[64,4352]{1,0:T(8,128)(2,1)S(1)}, u32[]{:S(2)}, u32[]{:S(2)}) collective-permute-start(bf16[64,4352]{1,0:T(8,128)(2,1)} %get-tuple-element.140.refs_24_), channel_id=1, source_target_pairs={{0,1},{1,0},{2,3},{3,2},{4,5},{5,4},{6,7},{7,6},{8,9},{9,8},{10,11... | collective-permute-start | bytes 1671176 | tf_op jit(solution)/shard_map/ppermute | solution.py:361
  127.5 9.4 %copy-start.4 = (bf16[128,4352]{1,0:T(8,128)(2,1)}, bf16[128,4352]{1,0:T(8,128)(2,1)S(1)}, u32[]{:S(2)}) copy-start(bf16[128,4352]{1,0:T(8,128)(2,1)S(1)} %collective-permute-done.16.refs_8_.refs_18_.refs_28_) | copy-start | bytes 3342340
  127.5 21.0 %collective-permute-start.17 = (bf16[288,256]{1,0:T(8,128)(2,1)S(1)}, bf16[288,256]{1,0:T(8,128)(2,1)S(1)}, u32[]{:S(2)}, u32[]{:S(2)}) collective-permute-start(bf16[288,256]{1,0:T(8,128)(2,1)S(1)} %get-tuple-element.129), channel_id=1, source_target_pairs={{0,4},{4,8},{8,12},{12,14},{14,10},{10,6},{6,2},{2,0},{1,5},{5,9},... | collective-permute-start | bytes 442376 | tf_op jit(solution)/shard_map/ppermute | solution.py:358
  136.6 12.0 %collective-permute-start.18 = (bf16[288,256]{1,0:T(8,128)(2,1)S(1)}, bf16[288,256]{1,0:T(8,128)(2,1)S(1)}, u32[]{:S(2)}, u32[]{:S(2)}) collective-permute-start(bf16[288,256]{1,0:T(8,128)(2,1)S(1)} %get-tuple-element.130), channel_id=1, source_target_pairs={{0,2},{4,0},{8,4},{12,8},{14,12},{10,14},{6,10},{2,6},{1,3},{5,1},... | collective-permute-start | bytes 442376 | tf_op jit(solution)/shard_map/ppermute | solution.py:358
  148.5 2.4 %copy-start.21 = (bf16[64,2048]{1,0:T(8,128)(2,1)S(1)}, bf16[64,2048]{1,0:T(8,128)(2,1)}, u32[]{:S(2)}) copy-start(bf16[64,2048]{1,0:T(8,128)(2,1)} %get-tuple-element.147) | copy-start | bytes 786436
  148.5 19.6 %copy-start.16 = (bf16[64,2048]{1,0:T(8,128)(2,1)}, bf16[64,2048]{1,0:T(8,128)(2,1)S(1)}, u32[]{:S(2)}) copy-start(bf16[64,2048]{1,0:T(8,128)(2,1)S(1)} %collective-permute-done.20.refs_5_) | copy-start | bytes 786436
  148.6 19.4 %collective-permute-start.22 = (bf16[288,512]{1,0:T(8,128)(2,1)S(1)}, bf16[288,512]{1,0:T(8,128)(2,1)S(1)}, u32[]{:S(2)}, u32[]{:S(2)}) collective-permute-start(bf16[288,512]{1,0:T(8,128)(2,1)S(1)} %maximum_select_fusion.1), channel_id=1, source_target_pairs={{0,2},{4,0},{8,4},{12,8},{14,12},{10,14},{6,10},{2,6},{1,3},{5,1},... | collective-permute-start | bytes 884744 | tf_op jit(solution)/shard_map/ppermute | solution.py:358
  150.7 17.3 %collective-permute-start.21 = (bf16[288,512]{1,0:T(8,128)(2,1)S(1)}, bf16[288,512]{1,0:T(8,128)(2,1)S(1)}, u32[]{:S(2)}, u32[]{:S(2)}) collective-permute-start(bf16[288,512]{1,0:T(8,128)(2,1)S(1)} %maximum_select_fusion), channel_id=1, source_target_pairs={{0,4},{4,8},{8,12},{12,14},{14,10},{10,6},{6,2},{2,0},{1,5},{5,9},... | collective-permute-start | bytes 884744 | tf_op jit(solution)/shard_map/ppermute | solution.py:358
  150.9 17.2 %collective-permute-start.23 = (bf16[64,2048]{1,0:T(8,128)(2,1)S(1)}, bf16[64,2048]{1,0:T(8,128)(2,1)S(1)}, u32[]{:S(2)}, u32[]{:S(2)}) collective-permute-start(bf16[64,2048]{1,0:T(8,128)(2,1)S(1)} %copy-done.21), channel_id=1, source_target_pairs={{0,14},{4,10},{8,6},{12,2},{14,0},{10,4},{6,8},{2,12},{1,15},{5,11... | collective-permute-start | bytes 786440 | tf_op jit(solution)/shard_map/ppermute | solution.py:358
  168.0 9.7 %copy-start.17 = (bf16[64,2048]{1,0:T(8,128)(2,1)}, bf16[64,2048]{1,0:T(8,128)(2,1)S(1)}, u32[]{:S(2)}) copy-start(bf16[64,2048]{1,0:T(8,128)(2,1)S(1)} %collective-permute-done.23.refs_4_) | copy-start | bytes 786436
  168.1 10.5 %collective-permute-start.24 = (bf16[288,512]{1,0:T(8,128)(2,1)S(1)}, bf16[288,512]{1,0:T(8,128)(2,1)S(1)}, u32[]{:S(2)}, u32[]{:S(2)}) collective-permute-start(bf16[288,512]{1,0:T(8,128)(2,1)S(1)} %broadcast_select_fusion.3), channel_id=1, source_target_pairs={{0,4},{4,8},{8,12},{12,14},{14,10},{10,6},{6,2},{2,0},{1,5},{5,9},... | collective-permute-start | bytes 884744 | tf_op jit(solution)/shard_map/ppermute | solution.py:358
  173.2 7.7 %collective-permute-start.25 = (bf16[288,512]{1,0:T(8,128)(2,1)S(1)}, bf16[288,512]{1,0:T(8,128)(2,1)S(1)}, u32[]{:S(2)}, u32[]{:S(2)}) collective-permute-start(bf16[288,512]{1,0:T(8,128)(2,1)S(1)} %broadcast_select_fusion.2), channel_id=1, source_target_pairs={{0,2},{4,0},{8,4},{12,8},{14,12},{10,14},{6,10},{2,6},{1,3},{5,1},... | collective-permute-start | bytes 884744 | tf_op jit(solution)/shard_map/ppermute | solution.py:358
  180.9 14.0 %collective-permute-start.29 = (bf16[512,2048]{1,0:T(8,128)(2,1)}, bf16[512,2048]{1,0:T(8,128)(2,1)S(1)}, u32[]{:S(2)}, u32[]{:S(2)}) collective-permute-start(bf16[512,2048]{1,0:T(8,128)(2,1)} %get-tuple-element.170), channel_id=1, source_target_pairs={{0,1},{1,0},{2,3},{3,2},{4,5},{5,4},{6,7},{7,6},{8,9},{9,8},{10,11... | collective-permute-start | bytes 6291464 | tf_op jit(solution)/shard_map/ppermute | solution.py:361
  180.9 9.5 %collective-permute-start.27 = (bf16[288,512]{1,0:T(8,128)(2,1)S(1)}, bf16[288,512]{1,0:T(8,128)(2,1)S(1)}, u32[]{:S(2)}, u32[]{:S(2)}) collective-permute-start(bf16[288,512]{1,0:T(8,128)(2,1)S(1)} %broadcast_select_fusion), channel_id=1, source_target_pairs={{0,2},{4,0},{8,4},{12,8},{14,12},{10,14},{6,10},{2,6},{1,3},{5,1},... | collective-permute-start | bytes 884744 | tf_op jit(solution)/shard_map/ppermute | solution.py:358
  181.3 9.3 %collective-permute-start.26 = (bf16[288,512]{1,0:T(8,128)(2,1)S(1)}, bf16[288,512]{1,0:T(8,128)(2,1)}, u32[]{:S(2)}, u32[]{:S(2)}) collective-permute-start(bf16[288,512]{1,0:T(8,128)(2,1)S(1)} %broadcast_select_fusion.1), channel_id=1, source_target_pairs={{0,4},{4,8},{8,12},{12,14},{14,10},{10,6},{6,2},{2,0},{1,5},{5,9},... | collective-permute-start | bytes 884744 | tf_op jit(solution)/shard_map/ppermute | solution.py:358
  191.6 3.3 %collective-permute-start.28 = (bf16[288,512]{1,0:T(8,128)(2,1)S(1)}, bf16[288,512]{1,0:T(8,128)(2,1)S(1)}, u32[]{:S(2)}, u32[]{:S(2)}) collective-permute-start(bf16[288,512]{1,0:T(8,128)(2,1)S(1)} %select_select_fusion.mine), channel_id=1, source_target_pairs={{0,1},{1,0},{2,3},{3,2},{4,5},{5,4},{6,7},{7,6},{8,9},{9,8},{10,11... | collective-permute-start | bytes 884744 | tf_op jit(solution)/shard_map/ppermute | solution.py:361
  191.7 3.2 %copy-start = (bf16[512,2048]{1,0:T(8,128)(2,1)S(1)}, bf16[512,2048]{1,0:T(8,128)(2,1)}, u32[]{:S(2)}) copy-start(bf16[512,2048]{1,0:T(8,128)(2,1)} %get-tuple-element.169.hot_mine) | copy-start | bytes 6291460
  191.7 3.2 %copy-start.1 = (s32[3]{0:T(128)S(1)}, s32[3]{0:T(128)}, u32[]{:S(2)}) copy-start(s32[3]{0:T(128)} %pad_add_fusion.scal) | copy-start | bytes 40
  (4 other events, 5.1 us)

commit v7 on v6

--- a/solution.py
+++ b/solution.py
@@ -68,14 +68,14 @@
     return onehot, weight
 
 
-def step_kernel(steps, fanout, capacity, joined, scal, *refs):
+def step_kernel(steps, pieces, fanout, capacity, joined, scal, *refs):
     count = len(steps)
     blocks, refs = refs[: max(count, 1 + joined)], refs[max(count, 1 + joined) :]
     if joined:
         first, refs = refs[0], refs[1:]
         blocks = [jnp.concatenate([block[...] for block in blocks], axis=1)]
     weights_gu, weights_down, mine, pack, hot = refs[:5]
-    back, refs = refs[5 : 5 + count], refs[5 + count :]
+    back, refs = refs[5 : 5 + count * pieces], refs[5 + count * pieces :]
     if len(refs) > 7:
         turned, refs = refs[0], refs[1:]
     else:
@@ -129,8 +129,8 @@
     pack[:, units : 2 * units] = (hidden_grad * activation).astype(BF16)
     pack[:, 2 * units : 3 * units] = (activation * up_pre).astype(BF16)
     input_rows = dot(pack[:, : 2 * units], gate_up[...], (1, 1)).astype(BF16)
-    for at in range(count):
-        back[at][...] = input_rows[at * capacity : (at + 1) * capacity]
+    for at, part in enumerate(back):
+        part[...] = input_rows[at * part.shape[0] : (at + 1) * part.shape[0]]
     if turned is not None:
         grads = pack[:, : 3 * units]
         if joined:
@@ -144,13 +144,14 @@
     vmem = pl.BlockSpec(memory_space=pltpu.VMEM)
     far = pl.BlockSpec(memory_space=pl.ANY)
     shapes = [(rows, width), (rows, 3 * units + width), (rows, 2 * width)]
-    shapes += [(capacity, width)] * count
     joined = first is not None
+    pieces = 2 if joined else 1
+    shapes += [(capacity // pieces, width)] * (count * pieces)
     if joined or count > 1:
         shapes += [(3 * units, 2 * capacity)]
     firsts = [first] if joined else []
     out = pl.pallas_call(
-        functools.partial(step_kernel, steps, fanout, capacity, joined),
+        functools.partial(step_kernel, steps, pieces, fanout, capacity, joined),
         out_shape=[jax.ShapeDtypeStruct(shape, BF16) for shape in shapes],
         in_specs=[pl.BlockSpec(memory_space=pltpu.SMEM)] + [vmem] * (len(blocks) + len(firsts)) + [far] * 2,
         out_specs=[vmem] * len(shapes),
@@ -166,11 +167,11 @@
         ),
         name="expert_step",
     )(scal, *blocks, *firsts, gate_up, down)
-    return out[:3], out[3 : 3 + count], out[3 + count :]
+    return out[:3], out[3 : 3 + count * pieces], out[3 + count * pieces :]
 
 
 def combine_kernel(experts, fanout, capacity, scal, meta, *refs):
-    rows, out = refs[:experts], refs[experts]
+    rows, out = refs[:-1], refs[-1]
     place = to_ring(scal[0], experts)
     table = meta[...].astype(F32).T
     picks = []
@@ -187,7 +188,7 @@
     return pl.pallas_call(
         functools.partial(combine_kernel, experts, fanout, capacity),
         out_shape=jax.ShapeDtypeStruct((tokens, width), BF16),
-        in_specs=[pl.BlockSpec(memory_space=pltpu.SMEM)] + [vmem] * (experts + 1),
+        in_specs=[pl.BlockSpec(memory_space=pltpu.SMEM)] + [vmem] * (len(rows) + 1),
         out_specs=vmem,
         compiler_params=pltpu.CompilerParams(vmem_limit_bytes=VMEM_BYTES),
         cost_estimate=pl.CostEstimate(
@@ -376,9 +377,7 @@
             following = [shift(up, 1), shift(below, -1)]
         elif number + 1 == half:
             following = [shift(up[:, :width], 1), shift(below[:, width:], -1)]
-        if number == half:
-            held, late[half - 2] = lax.optimization_barrier((held, late[half - 2]))
-        elif 0 < number < half - 1:
+        if 0 < number < half - 1:
             held, late[number - 1] = lax.optimization_barrier((held, late[number - 1]))
         (rows, pack, hot_rows), back, turn = run_step(
             steps,
@@ -391,6 +390,7 @@
             down,
         )
         following, back = lax.optimization_barrier((following, back))
+        steps = steps * (len(back) // len(steps))
         sent = [shift(part, step) if step else part for step, part in zip(steps, back)]
         late.append((sent, swap(pack)))
         mine.append(rows)
@@ -401,7 +401,7 @@
         if number < half:
             up, below = following
     (back_behind, back_ahead), other = late[half - 1]
-    turned[-1], back_ahead = lax.optimization_barrier((turned[-1], back_ahead))
+    turned[-1], late[half - 2] = lax.optimization_barrier((turned[-1], late[half - 2]))
 
     taken = 3 * units // experts
     ring_hot = to_ring(hottest, experts)
@@ -420,21 +420,24 @@
     others = [part for _, part in late[: half - 1]] + [other, late[half][1]]
     expert_grad = expert_gradient(units, scal, mine, packs, others)
     chunks = [chunk(distance) for distance in range(1 - half, half)]
-    (back_far,) = late[half][0]
+    back_far = list(late[half][0])
     hot_mine, hot_theirs = ordered(plan, experts, capacity, scal, hot)
     for number in range(1, half):
         if number == 1:
-            around, expert_grad, back_behind, chunks = lax.optimization_barrier(
-                (around, expert_grad, back_behind, chunks)
+            around, expert_grad, back_ahead, chunks = lax.optimization_barrier(
+                (around, expert_grad, back_ahead, chunks)
             )
             around = [jnp.concatenate([part, part], axis=1) for part in around]
-        if number == 2:
-            around, back_far = lax.optimization_barrier((around, back_far))
+        if number == half - 2:
+            around, back_behind = lax.optimization_barrier((around, back_behind))
         if number == half - 1:
-            around, hot_mine, hot_theirs = lax.optimization_barrier((around, hot_mine, hot_theirs))
+            around, back_far[0], hot_mine, hot_theirs = lax.optimization_barrier(
+                (around, back_far[0], hot_mine, hot_theirs)
+            )
         ahead = jnp.where(is_hot, chunks[2 * half - 1 - number], around[0])
         behind = jnp.where(is_hot, chunks[number - 1], around[1])
         around = [shift(ahead, 1), shift(behind, -1)]
+    around, back_far[1] = lax.optimization_barrier((around, back_far[1]))
     hot_theirs = swap(hot_theirs)
     away = (to_ring(own, experts) - ring_hot + experts) % experts
     lane = lax.broadcasted_iota(jnp.int32, far.shape, 1)
@@ -445,11 +448,13 @@
     shadow_grad = shadow_gradient(
         experts, scal, columns, swap(columns), hot_mine, hot_theirs
     ).T
-    sent = [rows for rows, _ in late[: half - 1]] + [[back_behind, back_ahead], [back_far]]
+    sent = [rows for rows, _ in late[: half - 1]] + [[back_behind, back_ahead]]
     for steps, parts in zip(plan, sent):
         for step, part in zip(steps, parts):
-            returned[step % experts] = part
-    token_grad = combine(experts, fanout, capacity, scal, meta, [returned[d] for d in range(experts)])
+            returned[step % experts] = [part]
+    returned[half] = back_far
+    rows = [part for distance in range(experts) for part in returned[distance]]
+    token_grad = combine(experts, fanout, capacity, scal, meta, rows)
     return (token_grad, expert_grad, shadow_grad)
 
 

time: 198 us -> 203 us (1.025)
  waiting for transfers between devices: 73.1 us -> 84.3 us
  starting transfers between devices: 42.1 us -> 34.7 us
    ppermute x23 -> x24, waiting for transfers between devices: 73.1 us -> 84.3 us  [shift(): return lax.ppermute(block, 'expert', pairs)]
    ppermute x23 -> x24, starting transfers between devices: 41.8 us -> 34.4 us  [shift(): return lax.ppermute(block, 'expert', pairs)]
  transfers between devices with their start and end apart: 30 -> 31, of which waited for: 14 -> 10; matrix products, arithmetic and copies ran while one was open for 3% -> 3% of each run, Pallas kernels for 34% -> 33%
where the time goes in v7:
time: 203 us; the launch traced here: 202 us
  waiting for transfers between devices  84.3 us (42%)
  Pallas kernels  72 us (35%)
  starting transfers between devices  34.7 us (17%)
  local copies, waits for them, and re-layouts  6.56 us (3%)
  other arithmetic  2.26 us (1%)
    ppermute x24, waiting for transfers between devices, shift(): return lax.ppermute(block, 'expert', pairs)  84.3 us
    pallas_call x5, Pallas kernels, run_step(): pl.pallas_call(functools.partial(step_kernel, steps, pieces, fanout, capa...  48.9 us
    ppermute x24, starting transfers between devices, shift(): return lax.ppermute(block, 'expert', pairs)  34.4 us
    pallas_call x1, Pallas kernels, expert_gradient(): pl.pallas_call(functools.partial(gradient_kernel, units, count), grid=(ti...  10.8 us
    pallas_call x1, Pallas kernels, ordered(): pl.pallas_call(functools.partial(order_kernel, plan, experts, capacity),...  4.49 us
  transfers between devices with their start and end apart: 31, of which 10 were waited for; matrix products, arithmetic and copies ran while one was open for 3% of the time, Pallas kernels for 33%

profile of v7, /device:TPU:0, one launch (start us, length us, event | category | flops | bytes accessed | tf_op | source)
XLA Modules:
  0.0 201.7 jit_solution(3196441702936119616)
XLA Ops:
  0.6 2.3 %ring_message.1 = (bf16[128,4224]{1,0:T(8,128)(2,1)}, bf16[128,128]{1,0:T(8,128)(2,1)}) custom-call(bf16[128,2048]{1,0:T(8,128)(2,1)} %tokens.1, bf16[128,2048]{1,0:T(8,128)(2,1)} %cotangent.1, s32[2,128]{1,0:T(2,128)} %bitcast.17, f32[2,128]{1,0:T(2,128)} %bitcast.18, f32[1,128]{1,0:T(1,128)} %bitcast.19, s32[1,128]{1,0:T(1,128)} %bitcast.20), custom_call_target="tpu_custom_call" | custom-call | bytes 2097152 | tf_op jit(solution)/shard_map/ring_message/pallas_call | solution.py:265
  3.0 3.0 %collective-permute-start.1 = (bf16[128,4224]{1,0:T(8,128)(2,1)}, bf16[128,4224]{1,0:T(8,128)(2,1)S(1)}, u32[]{:S(2)}, u32[]{:S(2)}) collective-permute-start(bf16[128,4224]{1,0:T(8,128)(2,1)} %get-tuple-element.91.refs_0_), channel_id=1, source_target_pairs={{0,2},{4,0},{8,4},{12,8},{14,12},{10,14},{6,10},{2,6},{1,3},{5,1},... | collective-permute-start | bytes 3244040 | tf_op jit(solution)/shard_map/ppermute | solution.py:359
  6.6 0.6 pad_add_fusion.scal
  7.2 9.4 %expert_step.5 = (bf16[64,2048]{1,0:T(8,128)(2,1)}, bf16[64,4352]{1,0:T(8,128)(2,1)}, bf16[64,4096]{1,0:T(8,128)(2,1)}, bf16[64,2048]{1,0:T(8,128)(2,1)}) custom-call(s32[3]{0:T(128)} %pad_add_fusion.scal, bf16[128,4224]{1,0:T(8,128)(2,1)} %get-tuple-element.91.refs_0_, bf16[2048,1536]{1,0:T(8,128)(2,1)} %bitcast.21, bf16[768,2048]{1,0:T(8,128)(2,1)} %bitcast.26), custom_call_target="tpu_custom_call" | custom-call | flops 4026531840 | bytes 9437184 | tf_op jit(solution)/shard_map/expert_step/pallas_call | solution.py:153
  16.7 13.4 %collective-permute-done.1.refs_1_ = bf16[128,4224]{1,0:T(8,128)(2,1)S(1)} collective-permute-done((bf16[128,4224]{1,0:T(8,128)(2,1)}, bf16[128,4224]{1,0:T(8,128)(2,1)S(1)}, u32[]{:S(2)}, u32[]{:S(2)}) %collective-permute-start.1) | collective-permute-done | bytes 1081376 | tf_op jit(solution)/shard_map/ppermute | solution.py:359
  30.0 1.5 collective-permute-done.refs_0_
  31.6 0.4 collective-permute-start.3
  31.9 1.7 collective-permute-start.4
  33.6 10.1 %expert_step.6 = (bf16[128,2048]{1,0:T(8,128)(2,1)}, bf16[128,4352]{1,0:T(8,128)(2,1)}, bf16[128,4096]{1,0:T(8,128)(2,1)}, bf16[64,2048]{1,0:T(8,128)(2,1)}, bf1...) custom-call(s32[3]{0:T(128)} %pad_add_fusion.scal, bf16[128,4224]{1,0:T(8,128)(2,1)} %collective-permute-done.refs_0_, ...), custom_call_target="tpu_custom_call" | custom-call | flops 4026531840 | bytes 9437184 | tf_op jit(solution)/shard_map/expert_step/pallas_call | solution.py:153
  43.7 12.5 %collective-permute-done.3.refs_0_ = bf16[128,4224]{1,0:T(8,128)(2,1)} collective-permute-done((bf16[128,4224]{1,0:T(8,128)(2,1)}, bf16[128,4224]{1,0:T(8,128)(2,1)}, u32[]{:S(2)}, u32[]{:S(2)}) %collective-permute-start.3) | collective-permute-done | bytes 1081376 | tf_op jit(solution)/shard_map/ppermute | solution.py:359
  56.5 1.6 collective-permute-start.8
  58.0 0.5 collective-permute-start.9
  58.5 1.4 collective-permute-start.5
  59.9 0.6 collective-permute-start.6
  60.5 26.4 %collective-permute-done.5.refs_8_ = bf16[64,2048]{1,0:T(8,128)(2,1)S(1)} collective-permute-done((bf16[64,2048]{1,0:T(8,128)(2,1)}, bf16[64,2048]{1,0:T(8,128)(2,1)S(1)}, u32[]{:S(2)}, u32[]{:S(2)}) %collective-permute-start.5) | collective-permute-done | bytes 262176 | tf_op jit(solution)/shard_map/ppermute | solution.py:359
  87.0 10.0 %expert_step.7 = (bf16[128,2048]{1,0:T(8,128)(2,1)}, bf16[128,4352]{1,0:T(8,128)(2,1)}, bf16[128,4096]{1,0:T(8,128)(2,1)}, bf16[64,2048]{1,0:T(8,128)(2,1)}, bf1...) custom-call(s32[3]{0:T(128)} %pad_add_fusion.scal, bf16[128,4224]{1,0:T(8,128)(2,1)} %collective-permute-done.3.refs_0_, ...), custom_call_target="tpu_custom_call" | custom-call | flops 4026531840 | bytes 9437184 | tf_op jit(solution)/shard_map/expert_step/pallas_call | solution.py:153
  97.2 1.5 slice.10
  98.7 1.6 collective-permute-start.10
  100.4 0.5 collective-permute-start.11
  101.0 1.5 collective-permute-start.12
  102.4 1.5 collective-permute-start.13
  103.9 9.8 %expert_step.8 = (bf16[128,2048]{1,0:T(8,128)(2,1)}, bf16[128,4352]{1,0:T(8,128)(2,1)}, bf16[128,4096]{1,0:T(8,128)(2,1)}, bf16[64,2048]{1,0:T(8,128)(2,1)}, bf1...) custom-call(s32[3]{0:T(128)} %pad_add_fusion.scal, bf16[128,4224]{1,0:T(8,128)(2,1)} %collective-permute-done.8.refs_0_, ...), custom_call_target="tpu_custom_call" | custom-call | flops 4026531840 | bytes 9437184 | tf_op jit(solution)/shard_map/expert_step/pallas_call | solution.py:153
  113.8 1.3 constant_dynamic-slice_fusion.1
  115.1 0.2 copy-done.7
  115.3 1.0 collective-permute-done.11.refs_1_
  116.4 6.1 %collective-permute-start.19 = (bf16[64,2048]{1,0:T(8,128)(2,1)}, bf16[64,2048]{1,0:T(8,128)(2,1)S(1)}, u32[]{:S(2)}, u32[]{:S(2)}) collective-permute-start(bf16[64,2048]{1,0:T(8,128)(2,1)} %get-tuple-element.140), channel_id=1, source_target_pairs={{0,12},{4,14},{8,10},{12,6},{14,2},{10,0},{6,4},{2,8},{1,13},{5,15... | collective-permute-start | bytes 786440 | tf_op jit(solution)/shard_map/ppermute | solution.py:359
  122.4 9.6 %expert_step.9 = (bf16[64,2048]{1,0:T(8,128)(2,1)}, bf16[64,4352]{1,0:T(8,128)(2,1)}, bf16[64,4096]{1,0:T(8,128)(2,1)}, bf16[32,2048]{1,0:T(8,128)(2,1)}, bf16[3...) custom-call(s32[3]{0:T(128)} %pad_add_fusion.scal, bf16[128,2048]{1,0:T(8,128)(2,1)} %copy-done.21, ...), custom_call_target="tpu_custom_call" | custom-call | flops 4026531840 | bytes 9437184 | tf_op jit(solution)/shard_map/expert_step/pallas_call | solution.py:153
  132.2 0.7 copy-done.14
  132.9 1.2 constant_dynamic-slice_fusion
  134.5 2.0 collective-permute-start.17
  136.5 0.8 copy-done.6
  137.3 10.8 %expert_gradient.1 = f32[1,1024,2304]{2,1,0:T(8,128)} custom-call(s32[3]{0:T(128)} %pad_add_fusion.scal, bf16[64,2048]{1,0:T(8,128)(2,1)} %get-tuple-element.130.refs_0_.refs_10_, bf16[128,2048]{1,0:T(8,128)(2,1)} %get-tuple-element.131.refs_1_.refs_11_, bf16[128,2048]{1,0:T(8,128)(2,1)} %get-tuple-element.132.refs_2_.refs_12_, ...), custom_call_target="tpu_custom_call" | custom-call | flops 4831838208 | bytes 14155776 | tf_op jit(solution)/shard_map/expert_gradient/pallas_call | solution.py:228
  148.4 2.1 %collective-permute-start.20 = (bf16[288,512]{1,0:T(8,128)(2,1)S(1)}, bf16[288,512]{1,0:T(8,128)(2,1)S(1)}, u32[]{:S(2)}, u32[]{:S(2)}) collective-permute-start(bf16[288,512]{1,0:T(8,128)(2,1)S(1)} %maximum_select_fusion), channel_id=1, source_target_pairs={{0,4},{4,8},{8,12},{12,14},{14,10},{10,6},{6,2},{2,0},{1,5},{5,9},... | collective-permute-start | bytes 884744 | tf_op jit(solution)/shard_map/ppermute | solution.py:359
  150.4 1.1 collective-permute-start.22
  151.5 11.7 %collective-permute-done.22.refs_6_ = bf16[64,2048]{1,0:T(8,128)(2,1)S(1)} collective-permute-done((bf16[64,2048]{1,0:T(8,128)(2,1)S(1)}, bf16[64,2048]{1,0:T(8,128)(2,1)S(1)}, u32[]{:S(2)}, u32[]{:S(2)}) %collective-permute-start.22) | collective-permute-done | bytes 262176 | tf_op jit(solution)/shard_map/ppermute | solution.py:359
  163.2 5.3 %collective-permute-done.21 = bf16[288,512]{1,0:T(8,128)(2,1)S(1)} collective-permute-done((bf16[288,512]{1,0:T(8,128)(2,1)S(1)}, bf16[288,512]{1,0:T(8,128)(2,1)S(1)}, u32[]{:S(2)}, u32[]{:S(2)}) %collective-permute-start.21) | collective-permute-done | bytes 294944 | tf_op jit(solution)/shard_map/ppermute | solution.py:359
  168.5 1.3 collective-permute-start.24
  169.8 0.9 collective-permute-start.23
  170.7 1.8 collective-permute-start.25
  172.5 4.5 %hot_rows_ordered.1 = (bf16[512,2048]{1,0:T(8,128)(2,1)}, bf16[512,2048]{1,0:T(8,128)(2,1)}) custom-call(s32[3]{0:T(128)} %pad_add_fusion.scal, bf16[64,4096]{1,0:T(8,128)(2,1)} %get-tuple-element.154.refs_0_, bf16[128,4096]{1,0:T(8,128)(2,1)} %get-tuple-element.155.refs_1_, bf16[128,4096]{1,0:T(8,128)(2,1)} %get-tuple-element.156.refs_2_, ...), custom_call_target="tpu_custom_call" | custom-call | bytes 8388608 | tf_op jit(solution)/shard_map/hot_rows_ordered/pallas_call | solution.py:293
  177.0 3.8 %collective-permute-done.25.refs_4_ = bf16[32,2048]{1,0:T(8,128)(2,1)S(1)} collective-permute-done((bf16[32,2048]{1,0:T(8,128)(2,1)S(1)}, bf16[32,2048]{1,0:T(8,128)(2,1)S(1)}, u32[]{:S(2)}, u32[]{:S(2)}) %collective-permute-start.25) | collective-permute-done | bytes 131104 | tf_op jit(solution)/shard_map/ppermute | solution.py:359
  180.8 0.6 copy-done.17
  181.6 2.1 %collective-permute-start.27 = (bf16[288,512]{1,0:T(8,128)(2,1)S(1)}, bf16[288,512]{1,0:T(8,128)(2,1)}, u32[]{:S(2)}, u32[]{:S(2)}) collective-permute-start(bf16[288,512]{1,0:T(8,128)(2,1)S(1)} %broadcast_select_fusion), channel_id=1, source_target_pairs={{0,2},{4,0},{8,4},{12,8},{14,12},{10,14},{6,10},{2,6},{1,3},{5,1},... | collective-permute-start | bytes 884744 | tf_op jit(solution)/shard_map/ppermute | solution.py:359
  183.7 2.8 %collective-permute-start.28 = (bf16[32,2048]{1,0:T(8,128)(2,1)}, bf16[32,2048]{1,0:T(8,128)(2,1)S(1)}, u32[]{:S(2)}, u32[]{:S(2)}) collective-permute-start(bf16[32,2048]{1,0:T(8,128)(2,1)} %get-tuple-element.166), channel_id=1, source_target_pairs={{0,14},{4,10},{8,6},{12,2},{14,0},{10,4},{6,8},{2,12},{1,15},{5,11... | collective-permute-start | bytes 393224 | tf_op jit(solution)/shard_map/ppermute | solution.py:359
  186.5 8.5 %collective-permute-done.28.refs_5_ = bf16[32,2048]{1,0:T(8,128)(2,1)S(1)} collective-permute-done((bf16[32,2048]{1,0:T(8,128)(2,1)}, bf16[32,2048]{1,0:T(8,128)(2,1)S(1)}, u32[]{:S(2)}, u32[]{:S(2)}) %collective-permute-start.28) | collective-permute-done | bytes 131104 | tf_op jit(solution)/shard_map/ppermute | solution.py:359
  195.0 1.1 select_select_fusion.mine
  196.2 3.2 %token_sum.1 = bf16[128,2048]{1,0:T(8,128)(2,1)} custom-call(s32[3]{0:T(128)} %pad_add_fusion.scal, bf16[128,128]{1,0:T(8,128)(2,1)} %get-tuple-element.90.meta, bf16[64,2048]{1,0:T(8,128)(2,1)} %get-tuple-element.97.refs_0_, bf16[64,2048]{1,0:T(8,128)(2,1)} %copy-done.12, bf16[64,2048]{1,0:T(8,128)(2,1)} %copy-done.14, bf16[64,2048]{1,0:T(8,128)(2,1)} %copy-done.15, ...), custom_call_target="tpu_custom_call" | custom-call | flops 268435456 | bytes 2097152 | tf_op jit(solution)/shard_map/token_sum/pallas_call | solution.py:188
  199.4 2.3 %shadow_gradient.1 = f32[288,1024]{1,0:T(8,128)} custom-call(s32[3]{0:T(128)S(1)} %copy-done.1, bf16[288,512]{1,0:T(8,128)(2,1)S(1)} %select_select_fusion.mine, bf16[288,512]{1,0:T(8,128)(2,1)S(1)} %collective-permute-done.29.theirs, bf16[512,2048]{1,0:T(8,128)(2,1)S(1)} %copy-done, bf16[512,2048]{1,0:T(8,128)(2,1)S(1)} %collective-permute-done.30.hot_theirs), custom_call_target="tpu_custom_call" | custom-call | flops 603979776 | bytes 2097152 | tf_op jit(solution)/shard_map/shadow_gradient/pallas_call | solution.py:332
  (92 shorter events, 1.6 us)
Async XLA Ops:
  3.0 27.1 %collective-permute-start.1 = (bf16[128,4224]{1,0:T(8,128)(2,1)}, bf16[128,4224]{1,0:T(8,128)(2,1)S(1)}, u32[]{:S(2)}, u32[]{:S(2)}) collective-permute-start(bf16[128,4224]{1,0:T(8,128)(2,1)} %get-tuple-element.91.refs_0_), channel_id=1, source_target_pairs={{0,2},{4,0},{8,4},{12,8},{14,12},{10,14},{6,10},{2,6},{1,3},{5,1},... | collective-permute-start | bytes 3244040 | tf_op jit(solution)/shard_map/ppermute | solution.py:359
  5.9 25.6 %collective-permute-start = (bf16[128,4224]{1,0:T(8,128)(2,1)}, bf16[128,4224]{1,0:T(8,128)(2,1)}, u32[]{:S(2)}, u32[]{:S(2)}) collective-permute-start(bf16[128,4224]{1,0:T(8,128)(2,1)} %get-tuple-element.91.refs_0_), channel_id=1, source_target_pairs={{0,4},{4,8},{8,12},{12,14},{14,10},{10,6},{6,2},{2,0},{1,5},{5,9},... | collective-permute-start | bytes 3244040 | tf_op jit(solution)/shard_map/ppermute | solution.py:359
  16.6 17.0 %collective-permute-start.2 = (bf16[64,4352]{1,0:T(8,128)(2,1)}, bf16[64,4352]{1,0:T(8,128)(2,1)S(1)}, u32[]{:S(2)}, u32[]{:S(2)}) collective-permute-start(bf16[64,4352]{1,0:T(8,128)(2,1)} %get-tuple-element.96.refs_2_.refs_20_), channel_id=1, source_target_pairs={{0,1},{1,0},{2,3},{3,2},{4,5},{5,4},{6,7},{7,6},{8,9},{9,8},{10,11... | collective-permute-start | bytes 1671176 | tf_op jit(solution)/shard_map/ppermute | solution.py:362
  30.0 3.5 %copy-start.19 = (bf16[128,4224]{1,0:T(8,128)(2,1)}, bf16[128,4224]{1,0:T(8,128)(2,1)S(1)}, u32[]{:S(2)}) copy-start(bf16[128,4224]{1,0:T(8,128)(2,1)S(1)} %collective-permute-done.1.refs_1_) | copy-start | bytes 3244036
  31.6 24.7 %collective-permute-start.3 = (bf16[128,4224]{1,0:T(8,128)(2,1)}, bf16[128,4224]{1,0:T(8,128)(2,1)}, u32[]{:S(2)}, u32[]{:S(2)}) collective-permute-start(bf16[128,4224]{1,0:T(8,128)(2,1)} %collective-permute-done.refs_0_), channel_id=1, source_target_pairs={{0,4},{4,8},{8,12},{12,14},{14,10},{10,6},{6,2},{2,0},{1,5},{5,9},... | collective-permute-start | bytes 3244040 | tf_op jit(solution)/shard_map/ppermute | solution.py:359
  31.9 24.6 %collective-permute-start.4 = (bf16[128,4224]{1,0:T(8,128)(2,1)S(1)}, bf16[128,4224]{1,0:T(8,128)(2,1)}, u32[]{:S(2)}, u32[]{:S(2)}) collective-permute-start(bf16[128,4224]{1,0:T(8,128)(2,1)S(1)} %collective-permute-done.1.refs_1_), channel_id=1, source_target_pairs={{0,2},{4,0},{8,4},{12,8},{14,12},{10,14},{6,10},{2,6},{1,3},{5,1},... | collective-permute-start | bytes 3244040 | tf_op jit(solution)/shard_map/ppermute | solution.py:359
  33.6 10.1 %copy-start.5 = (bf16[64,4352]{1,0:T(8,128)(2,1)}, bf16[64,4352]{1,0:T(8,128)(2,1)S(1)}, u32[]{:S(2)}) copy-start(bf16[64,4352]{1,0:T(8,128)(2,1)S(1)} %collective-permute-done.2.refs_5_.refs_15_.refs_25_) | copy-start | bytes 1671172
  43.7 16.9 %collective-permute-start.7 = (bf16[128,4352]{1,0:T(8,128)(2,1)}, bf16[128,4352]{1,0:T(8,128)(2,1)S(1)}, u32[]{:S(2)}, u32[]{:S(2)}) collective-permute-start(bf16[128,4352]{1,0:T(8,128)(2,1)} %get-tuple-element.106.refs_21_), channel_id=1, source_target_pairs={{0,1},{1,0},{2,3},{3,2},{4,5},{5,4},{6,7},{7,6},{8,9},{9,8},{10,11... | collective-permute-start | bytes 3342344 | tf_op jit(solution)/shard_map/ppermute | solution.py:362
  56.5 40.7 %collective-permute-start.8 = (bf16[128,4224]{1,0:T(8,128)(2,1)}, bf16[128,4224]{1,0:T(8,128)(2,1)}, u32[]{:S(2)}, u32[]{:S(2)}) collective-permute-start(bf16[128,4224]{1,0:T(8,128)(2,1)} %collective-permute-done.3.refs_0_), channel_id=1, source_target_pairs={{0,4},{4,8},{8,12},{12,14},{14,10},{10,6},{6,2},{2,0},{1,5},{5,9},... | collective-permute-start | bytes 3244040 | tf_op jit(solution)/shard_map/ppermute | solution.py:359
  58.0 39.2 %collective-permute-start.9 = (bf16[128,4224]{1,0:T(8,128)(2,1)}, bf16[128,4224]{1,0:T(8,128)(2,1)S(1)}, u32[]{:S(2)}, u32[]{:S(2)}) collective-permute-start(bf16[128,4224]{1,0:T(8,128)(2,1)} %collective-permute-done.4.refs_1_), channel_id=1, source_target_pairs={{0,2},{4,0},{8,4},{12,8},{14,12},{10,14},{6,10},{2,6},{1,3},{5,1},... | collective-permute-start | bytes 3244040 | tf_op jit(solution)/shard_map/ppermute | solution.py:359
  58.5 28.5 %collective-permute-start.5 = (bf16[64,2048]{1,0:T(8,128)(2,1)}, bf16[64,2048]{1,0:T(8,128)(2,1)S(1)}, u32[]{:S(2)}, u32[]{:S(2)}) collective-permute-start(bf16[64,2048]{1,0:T(8,128)(2,1)} %get-tuple-element.104), channel_id=1, source_target_pairs={{0,2},{4,0},{8,4},{12,8},{14,12},{10,14},{6,10},{2,6},{1,3},{5,1},... | collective-permute-start | bytes 786440 | tf_op jit(solution)/shard_map/ppermute | solution.py:359
  59.9 27.1 %collective-permute-start.6 = (bf16[64,2048]{1,0:T(8,128)(2,1)}, bf16[64,2048]{1,0:T(8,128)(2,1)S(1)}, u32[]{:S(2)}, u32[]{:S(2)}) collective-permute-start(bf16[64,2048]{1,0:T(8,128)(2,1)} %get-tuple-element.105), channel_id=1, source_target_pairs={{0,4},{4,8},{8,12},{12,14},{14,10},{10,6},{6,2},{2,0},{1,5},{5,9},... | collective-permute-start | bytes 786440 | tf_op jit(solution)/shard_map/ppermute | solution.py:359
  60.5 36.6 %copy-start.8 = (bf16[2304,128]{1,0:T(8,128)(2,1)S(1)}, bf16[2304,128]{1,0:T(8,128)(2,1)}, u32[]{:S(2)}) copy-start(bf16[2304,128]{1,0:T(8,128)(2,1)} %get-tuple-element.123) | copy-start | bytes 1769476
  60.5 36.5 %copy-start.2 = (bf16[128,4352]{1,0:T(8,128)(2,1)}, bf16[128,4352]{1,0:T(8,128)(2,1)S(1)}, u32[]{:S(2)}) copy-start(bf16[128,4352]{1,0:T(8,128)(2,1)S(1)} %collective-permute-done.7.refs_6_.refs_16_.refs_26_) | copy-start | bytes 3342340
  86.9 10.1 %copy-start.11 = (bf16[64,2048]{1,0:T(8,128)(2,1)}, bf16[64,2048]{1,0:T(8,128)(2,1)S(1)}, u32[]{:S(2)}) copy-start(bf16[64,2048]{1,0:T(8,128)(2,1)S(1)} %collective-permute-done.5.refs_8_) | copy-start | bytes 786436
  86.9 10.1 %copy-start.12 = (bf16[64,2048]{1,0:T(8,128)(2,1)}, bf16[64,2048]{1,0:T(8,128)(2,1)S(1)}, u32[]{:S(2)}) copy-start(bf16[64,2048]{1,0:T(8,128)(2,1)S(1)} %collective-permute-done.6.refs_1_) | copy-start | bytes 786436
  97.0 35.1 %collective-permute-start.14 = (bf16[128,4352]{1,0:T(8,128)(2,1)}, bf16[128,4352]{1,0:T(8,128)(2,1)S(1)}, u32[]{:S(2)}, u32[]{:S(2)}) collective-permute-start(bf16[128,4352]{1,0:T(8,128)(2,1)} %get-tuple-element.121.refs_22_), channel_id=1, source_target_pairs={{0,1},{1,0},{2,3},{3,2},{4,5},{5,4},{6,7},{7,6},{8,9},{9,8},{10,11... | collective-permute-start | bytes 3342344 | tf_op jit(solution)/shard_map/ppermute | solution.py:362
  97.2 3.7 %copy-start.9 = (bf16[2304,128]{1,0:T(8,128)(2,1)S(1)}, bf16[2304,128]{1,0:T(8,128)(2,1)}, u32[]{:S(2)}) copy-start(bf16[2304,128]{1,0:T(8,128)(2,1)} %get-tuple-element.124) | copy-start | bytes 1769476
  97.2 3.7 %copy-start.10 = (bf16[128,4224]{1,0:T(8,128)(2,1)}, bf16[128,4224]{1,0:T(8,128)(2,1)S(1)}, u32[]{:S(2)}) copy-start(bf16[128,4224]{1,0:T(8,128)(2,1)S(1)} %collective-permute-done.9.refs_1_) | copy-start | bytes 3244036
  98.7 16.4 %collective-permute-start.10 = (bf16[128,2048]{1,0:T(8,128)(2,1)S(1)}, bf16[128,2048]{1,0:T(8,128)(2,1)S(1)}, u32[]{:S(2)}, u32[]{:S(2)}) collective-permute-start(bf16[128,2048]{1,0:T(8,128)(2,1)S(1)} %slice.10), channel_id=1, source_target_pairs={{0,4},{4,8},{8,12},{12,14},{14,10},{10,6},{6,2},{2,0},{1,5},{5,9},... | collective-permute-start | bytes 1572872 | tf_op jit(solution)/shard_map/ppermute | solution.py:359
  100.4 16.0 %collective-permute-start.11 = (bf16[128,2176]{1,0:T(8,128)(2,1)S(1)}, bf16[128,2176]{1,0:T(8,128)(2,1)S(1)}, u32[]{:S(2)}, u32[]{:S(2)}) collective-permute-start(bf16[128,2176]{1,0:T(8,128)(2,1)S(1)} %slice.11), channel_id=1, source_target_pairs={{0,2},{4,0},{8,4},{12,8},{14,12},{10,14},{6,10},{2,6},{1,3},{5,1},... | collective-permute-start | bytes 1671176 | tf_op jit(solution)/shard_map/ppermute | solution.py:359
  101.0 31.1 %collective-permute-start.12 = (bf16[64,2048]{1,0:T(8,128)(2,1)}, bf16[64,2048]{1,0:T(8,128)(2,1)S(1)}, u32[]{:S(2)}, u32[]{:S(2)}) collective-permute-start(bf16[64,2048]{1,0:T(8,128)(2,1)} %get-tuple-element.119), channel_id=1, source_target_pairs={{0,6},{4,2},{8,0},{12,4},{14,8},{10,12},{6,14},{2,10},{1,7},{5,3},... | collective-permute-start | bytes 786440 | tf_op jit(solution)/shard_map/ppermute | solution.py:359
  102.4 29.7 %collective-permute-start.13 = (bf16[64,2048]{1,0:T(8,128)(2,1)}, bf16[64,2048]{1,0:T(8,128)(2,1)S(1)}, u32[]{:S(2)}, u32[]{:S(2)}) collective-permute-start(bf16[64,2048]{1,0:T(8,128)(2,1)} %get-tuple-element.120), channel_id=1, source_target_pairs={{0,8},{4,12},{8,14},{12,10},{14,6},{10,2},{6,0},{2,4},{1,9},{5,13}... | collective-permute-start | bytes 786440 | tf_op jit(solution)/shard_map/ppermute | solution.py:359
  115.1 7.3 %copy-start.21 = (bf16[128,2048]{1,0:T(8,128)(2,1)}, bf16[128,2048]{1,0:T(8,128)(2,1)S(1)}, u32[]{:S(2)}) copy-start(bf16[128,2048]{1,0:T(8,128)(2,1)S(1)} %collective-permute-done.10.refs_0_) | copy-start | bytes 1572868
  115.3 19.1 %collective-permute-start.15 = (bf16[128,4352]{1,0:T(8,128)(2,1)S(1)}, bf16[128,4352]{1,0:T(8,128)(2,1)S(1)}, u32[]{:S(2)}, u32[]{:S(2)}) collective-permute-start(bf16[128,4352]{1,0:T(8,128)(2,1)S(1)} %copy-done.7), channel_id=1, source_target_pairs={{0,1},{1,0},{2,3},{3,2},{4,5},{5,4},{6,7},{7,6},{8,9},{9,8},{10,11... | collective-permute-start | bytes 3342344 | tf_op jit(solution)/shard_map/ppermute | solution.py:362
  116.4 6.1 %copy-start.20 = (bf16[128,2176]{1,0:T(8,128)(2,1)}, bf16[128,2176]{1,0:T(8,128)(2,1)S(1)}, u32[]{:S(2)}) copy-start(bf16[128,2176]{1,0:T(8,128)(2,1)S(1)} %collective-permute-done.11.refs_1_) | copy-start | bytes 1671172
  116.4 31.7 %collective-permute-start.19 = (bf16[64,2048]{1,0:T(8,128)(2,1)}, bf16[64,2048]{1,0:T(8,128)(2,1)S(1)}, u32[]{:S(2)}, u32[]{:S(2)}) collective-permute-start(bf16[64,2048]{1,0:T(8,128)(2,1)} %get-tuple-element.140), channel_id=1, source_target_pairs={{0,12},{4,14},{8,10},{12,6},{14,2},{10,0},{6,4},{2,8},{1,13},{5,15... | collective-permute-start | bytes 786440 | tf_op jit(solution)/shard_map/ppermute | solution.py:359
  132.9 3.6 %collective-permute-start.18 = (bf16[64,4352]{1,0:T(8,128)(2,1)}, bf16[64,4352]{1,0:T(8,128)(2,1)S(1)}, u32[]{:S(2)}, u32[]{:S(2)}) collective-permute-start(bf16[64,4352]{1,0:T(8,128)(2,1)} %get-tuple-element.139.refs_24_), channel_id=1, source_target_pairs={{0,1},{1,0},{2,3},{3,2},{4,5},{5,4},{6,7},{7,6},{8,9},{9,8},{10,11... | collective-permute-start | bytes 1671176 | tf_op jit(solution)/shard_map/ppermute | solution.py:362
  134.4 2.1 %copy-start.4 = (bf16[128,4352]{1,0:T(8,128)(2,1)}, bf16[128,4352]{1,0:T(8,128)(2,1)S(1)}, u32[]{:S(2)}) copy-start(bf16[128,4352]{1,0:T(8,128)(2,1)S(1)} %collective-permute-done.15.refs_8_.refs_18_.refs_28_) | copy-start | bytes 3342340
  134.4 13.7 %collective-permute-start.16 = (bf16[288,256]{1,0:T(8,128)(2,1)S(1)}, bf16[288,256]{1,0:T(8,128)(2,1)S(1)}, u32[]{:S(2)}, u32[]{:S(2)}) collective-permute-start(bf16[288,256]{1,0:T(8,128)(2,1)S(1)} %get-tuple-element.128), channel_id=1, source_target_pairs={{0,4},{4,8},{8,12},{12,14},{14,10},{10,6},{6,2},{2,0},{1,5},{5,9},... | collective-permute-start | bytes 442376 | tf_op jit(solution)/shard_map/ppermute | solution.py:359
  134.5 13.6 %collective-permute-start.17 = (bf16[288,256]{1,0:T(8,128)(2,1)S(1)}, bf16[288,256]{1,0:T(8,128)(2,1)S(1)}, u32[]{:S(2)}, u32[]{:S(2)}) collective-permute-start(bf16[288,256]{1,0:T(8,128)(2,1)S(1)} %get-tuple-element.129), channel_id=1, source_target_pairs={{0,2},{4,0},{8,4},{12,8},{14,12},{10,14},{6,10},{2,6},{1,3},{5,1},... | collective-permute-start | bytes 442376 | tf_op jit(solution)/shard_map/ppermute | solution.py:359
  148.1 2.4 %copy-start.22 = (bf16[64,2048]{1,0:T(8,128)(2,1)S(1)}, bf16[64,2048]{1,0:T(8,128)(2,1)}, u32[]{:S(2)}) copy-start(bf16[64,2048]{1,0:T(8,128)(2,1)} %get-tuple-element.147) | copy-start | bytes 786436
  148.1 20.4 %copy-start.15 = (bf16[64,2048]{1,0:T(8,128)(2,1)}, bf16[64,2048]{1,0:T(8,128)(2,1)S(1)}, u32[]{:S(2)}) copy-start(bf16[64,2048]{1,0:T(8,128)(2,1)S(1)} %collective-permute-done.19.refs_3_) | copy-start | bytes 786436
  148.2 22.5 %copy-start.23 = (bf16[32,2048]{1,0:T(8,128)(2,1)S(1)}, bf16[32,2048]{1,0:T(8,128)(2,1)}, u32[]{:S(2)}) copy-start(bf16[32,2048]{1,0:T(8,128)(2,1)} %get-tuple-element.153) | copy-start | bytes 393220
  148.2 20.3 %collective-permute-start.21 = (bf16[288,512]{1,0:T(8,128)(2,1)S(1)}, bf16[288,512]{1,0:T(8,128)(2,1)S(1)}, u32[]{:S(2)}, u32[]{:S(2)}) collective-permute-start(bf16[288,512]{1,0:T(8,128)(2,1)S(1)} %maximum_select_fusion.1), channel_id=1, source_target_pairs={{0,2},{4,0},{8,4},{12,8},{14,12},{10,14},{6,10},{2,6},{1,3},{5,1},... | collective-permute-start | bytes 884744 | tf_op jit(solution)/shard_map/ppermute | solution.py:359
  148.4 20.1 %collective-permute-start.20 = (bf16[288,512]{1,0:T(8,128)(2,1)S(1)}, bf16[288,512]{1,0:T(8,128)(2,1)S(1)}, u32[]{:S(2)}, u32[]{:S(2)}) collective-permute-start(bf16[288,512]{1,0:T(8,128)(2,1)S(1)} %maximum_select_fusion), channel_id=1, source_target_pairs={{0,4},{4,8},{8,12},{12,14},{14,10},{10,6},{6,2},{2,0},{1,5},{5,9},... | collective-permute-start | bytes 884744 | tf_op jit(solution)/shard_map/ppermute | solution.py:359
  150.4 12.7 %collective-permute-start.22 = (bf16[64,2048]{1,0:T(8,128)(2,1)S(1)}, bf16[64,2048]{1,0:T(8,128)(2,1)S(1)}, u32[]{:S(2)}, u32[]{:S(2)}) collective-permute-start(bf16[64,2048]{1,0:T(8,128)(2,1)S(1)} %copy-done.22), channel_id=1, source_target_pairs={{0,10},{4,6},{8,2},{12,0},{14,4},{10,8},{6,12},{2,14},{1,11},{5,7}... | collective-permute-start | bytes 786440 | tf_op jit(solution)/shard_map/ppermute | solution.py:359
  163.2 13.8 %copy-start.16 = (bf16[64,2048]{1,0:T(8,128)(2,1)}, bf16[64,2048]{1,0:T(8,128)(2,1)S(1)}, u32[]{:S(2)}) copy-start(bf16[64,2048]{1,0:T(8,128)(2,1)S(1)} %collective-permute-done.22.refs_6_) | copy-start | bytes 786436
  168.5 12.3 %collective-permute-start.24 = (bf16[288,512]{1,0:T(8,128)(2,1)S(1)}, bf16[288,512]{1,0:T(8,128)(2,1)S(1)}, u32[]{:S(2)}, u32[]{:S(2)}) collective-permute-start(bf16[288,512]{1,0:T(8,128)(2,1)S(1)} %broadcast_select_fusion.2), channel_id=1, source_target_pairs={{0,2},{4,0},{8,4},{12,8},{14,12},{10,14},{6,10},{2,6},{1,3},{5,1},... | collective-permute-start | bytes 884744 | tf_op jit(solution)/shard_map/ppermute | solution.py:359
  169.8 11.0 %collective-permute-start.23 = (bf16[288,512]{1,0:T(8,128)(2,1)S(1)}, bf16[288,512]{1,0:T(8,128)(2,1)S(1)}, u32[]{:S(2)}, u32[]{:S(2)}) collective-permute-start(bf16[288,512]{1,0:T(8,128)(2,1)S(1)} %broadcast_select_fusion.3), channel_id=1, source_target_pairs={{0,4},{4,8},{8,12},{12,14},{14,10},{10,6},{6,2},{2,0},{1,5},{5,9},... | collective-permute-start | bytes 884744 | tf_op jit(solution)/shard_map/ppermute | solution.py:359
  170.7 10.1 %collective-permute-start.25 = (bf16[32,2048]{1,0:T(8,128)(2,1)S(1)}, bf16[32,2048]{1,0:T(8,128)(2,1)S(1)}, u32[]{:S(2)}, u32[]{:S(2)}) collective-permute-start(bf16[32,2048]{1,0:T(8,128)(2,1)S(1)} %copy-done.23), channel_id=1, source_target_pairs={{0,14},{4,10},{8,6},{12,2},{14,0},{10,4},{6,8},{2,12},{1,15},{5,11... | collective-permute-start | bytes 393224 | tf_op jit(solution)/shard_map/ppermute | solution.py:359
  181.5 17.9 %collective-permute-start.30 = (bf16[512,2048]{1,0:T(8,128)(2,1)}, bf16[512,2048]{1,0:T(8,128)(2,1)S(1)}, u32[]{:S(2)}, u32[]{:S(2)}) collective-permute-start(bf16[512,2048]{1,0:T(8,128)(2,1)} %get-tuple-element.176), channel_id=1, source_target_pairs={{0,1},{1,0},{2,3},{3,2},{4,5},{5,4},{6,7},{7,6},{8,9},{9,8},{10,11... | collective-permute-start | bytes 6291464 | tf_op jit(solution)/shard_map/ppermute | solution.py:362
  181.5 13.5 %collective-permute-start.26 = (bf16[288,512]{1,0:T(8,128)(2,1)S(1)}, bf16[288,512]{1,0:T(8,128)(2,1)S(1)}, u32[]{:S(2)}, u32[]{:S(2)}) collective-permute-start(bf16[288,512]{1,0:T(8,128)(2,1)S(1)} %broadcast_select_fusion.1), channel_id=1, source_target_pairs={{0,4},{4,8},{8,12},{12,14},{14,10},{10,6},{6,2},{2,0},{1,5},{5,9},... | collective-permute-start | bytes 884744 | tf_op jit(solution)/shard_map/ppermute | solution.py:359
  181.6 13.4 %collective-permute-start.27 = (bf16[288,512]{1,0:T(8,128)(2,1)S(1)}, bf16[288,512]{1,0:T(8,128)(2,1)}, u32[]{:S(2)}, u32[]{:S(2)}) collective-permute-start(bf16[288,512]{1,0:T(8,128)(2,1)S(1)} %broadcast_select_fusion), channel_id=1, source_target_pairs={{0,2},{4,0},{8,4},{12,8},{14,12},{10,14},{6,10},{2,6},{1,3},{5,1},... | collective-permute-start | bytes 884744 | tf_op jit(solution)/shard_map/ppermute | solution.py:359
  183.7 11.3 %collective-permute-start.28 = (bf16[32,2048]{1,0:T(8,128)(2,1)}, bf16[32,2048]{1,0:T(8,128)(2,1)S(1)}, u32[]{:S(2)}, u32[]{:S(2)}) collective-permute-start(bf16[32,2048]{1,0:T(8,128)(2,1)} %get-tuple-element.166), channel_id=1, source_target_pairs={{0,14},{4,10},{8,6},{12,2},{14,0},{10,4},{6,8},{2,12},{1,15},{5,11... | collective-permute-start | bytes 393224 | tf_op jit(solution)/shard_map/ppermute | solution.py:359
  196.1 3.3 %collective-permute-start.29 = (bf16[288,512]{1,0:T(8,128)(2,1)S(1)}, bf16[288,512]{1,0:T(8,128)(2,1)S(1)}, u32[]{:S(2)}, u32[]{:S(2)}) collective-permute-start(bf16[288,512]{1,0:T(8,128)(2,1)S(1)} %select_select_fusion.mine), channel_id=1, source_target_pairs={{0,1},{1,0},{2,3},{3,2},{4,5},{5,4},{6,7},{7,6},{8,9},{9,8},{10,11... | collective-permute-start | bytes 884744 | tf_op jit(solution)/shard_map/ppermute | solution.py:362
  196.1 3.2 %copy-start = (bf16[512,2048]{1,0:T(8,128)(2,1)S(1)}, bf16[512,2048]{1,0:T(8,128)(2,1)}, u32[]{:S(2)}) copy-start(bf16[512,2048]{1,0:T(8,128)(2,1)} %get-tuple-element.175.hot_mine) | copy-start | bytes 6291460
  196.2 3.2 %copy-start.1 = (s32[3]{0:T(128)S(1)}, s32[3]{0:T(128)}, u32[]{:S(2)}) copy-start(s32[3]{0:T(128)} %pad_add_fusion.scal) | copy-start | bytes 40
  (7 other events, 8.9 us)

commit v8 on v7

--- a/solution.py
+++ b/solution.py
@@ -377,8 +377,12 @@
             following = [shift(up, 1), shift(below, -1)]
         elif number + 1 == half:
             following = [shift(up[:, :width], 1), shift(below[:, width:], -1)]
-        if 0 < number < half - 1:
-            held, late[number - 1] = lax.optimization_barrier((held, late[number - 1]))
+        if number > 1:
+            sent, other = late[number - 2]
+            held, other = lax.optimization_barrier((held, other))
+            late[number - 2] = (sent, other)
+        if number == half - 1:
+            held, late[: half - 2] = lax.optimization_barrier((held, late[: half - 2]))
         (rows, pack, hot_rows), back, turn = run_step(
             steps,
             fanout,
@@ -424,20 +428,19 @@
     hot_mine, hot_theirs = ordered(plan, experts, capacity, scal, hot)
     for number in range(1, half):
         if number == 1:
-            around, expert_grad, back_ahead, chunks = lax.optimization_barrier(
-                (around, expert_grad, back_ahead, chunks)
+            around, expert_grad, back_ahead, back_behind, chunks = lax.optimization_barrier(
+                (around, expert_grad, back_ahead, back_behind, chunks)
             )
             around = [jnp.concatenate([part, part], axis=1) for part in around]
         if number == half - 2:
-            around, back_behind = lax.optimization_barrier((around, back_behind))
+            around, back_far[0] = lax.optimization_barrier((around, back_far[0]))
         if number == half - 1:
-            around, back_far[0], hot_mine, hot_theirs = lax.optimization_barrier(
-                (around, back_far[0], hot_mine, hot_theirs)
+            around, back_far[1], hot_mine, hot_theirs = lax.optimization_barrier(
+                (around, back_far[1], hot_mine, hot_theirs)
             )
         ahead = jnp.where(is_hot, chunks[2 * half - 1 - number], around[0])
         behind = jnp.where(is_hot, chunks[number - 1], around[1])
         around = [shift(ahead, 1), shift(behind, -1)]
-    around, back_far[1] = lax.optimization_barrier((around, back_far[1]))
     hot_theirs = swap(hot_theirs)
     away = (to_ring(own, experts) - ring_hot + experts) % experts
     lane = lax.broadcasted_iota(jnp.int32, far.shape, 1)

time: 203 us -> 190 us (0.936)
  waiting for transfers between devices: 84.3 us -> 72 us
    ppermute x24, waiting for transfers between devices: 84.3 us -> 72 us  [shift(): return lax.ppermute(block, 'expert', pairs)]
  transfers between devices with their start and end apart: 31 -> 31, of which waited for: 10 -> 13; matrix products, arithmetic and copies ran while one was open for 3% -> 4% of each run, Pallas kernels for 33% -> 35%
where the time goes in v8:
time: 190 us; the launch traced here: 189 us
  waiting for transfers between devices  72 us (38%)
  Pallas kernels  71.7 us (38%)
  starting transfers between devices  34.7 us (18%)
  local copies, waits for them, and re-layouts  6.51 us (3%)
  other arithmetic  2.24 us (1%)
    ppermute x24, waiting for transfers between devices, shift(): return lax.ppermute(block, 'expert', pairs)  72 us
    pallas_call x5, Pallas kernels, run_step(): pl.pallas_call(functools.partial(step_kernel, steps, pieces, fanout, capa...  48.7 us
    ppermute x24, starting transfers between devices, shift(): return lax.ppermute(block, 'expert', pairs)  34.2 us
    pallas_call x1, Pallas kernels, expert_gradient(): pl.pallas_call(functools.partial(gradient_kernel, units, count), grid=(ti...  10.8 us
    pallas_call x1, Pallas kernels, ordered(): pl.pallas_call(functools.partial(order_kernel, plan, experts, capacity),...  4.49 us
  transfers between devices with their start and end apart: 31, of which 13 were waited for; matrix products, arithmetic and copies ran while one was open for 4% of the time, Pallas kernels for 35%

profile of v8, /device:TPU:0, one launch (start us, length us, event | category | flops | bytes accessed | tf_op | source)
XLA Modules:
  0.0 189.0 jit_solution(1017116999691697496)
XLA Ops:
  0.6 2.3 %ring_message.1 = (bf16[128,4224]{1,0:T(8,128)(2,1)}, bf16[128,128]{1,0:T(8,128)(2,1)}) custom-call(bf16[128,2048]{1,0:T(8,128)(2,1)} %tokens.1, bf16[128,2048]{1,0:T(8,128)(2,1)} %cotangent.1, s32[2,128]{1,0:T(2,128)} %bitcast.17, f32[2,128]{1,0:T(2,128)} %bitcast.18, f32[1,128]{1,0:T(1,128)} %bitcast.19, s32[1,128]{1,0:T(1,128)} %bitcast.20), custom_call_target="tpu_custom_call" | custom-call | bytes 2097152 | tf_op jit(solution)/shard_map/ring_message/pallas_call | solution.py:265
  3.0 3.0 %collective-permute-start.1 = (bf16[128,4224]{1,0:T(8,128)(2,1)}, bf16[128,4224]{1,0:T(8,128)(2,1)S(1)}, u32[]{:S(2)}, u32[]{:S(2)}) collective-permute-start(bf16[128,4224]{1,0:T(8,128)(2,1)} %get-tuple-element.96.refs_0_), channel_id=1, source_target_pairs={{0,2},{4,0},{8,4},{12,8},{14,12},{10,14},{6,10},{2,6},{1,3},{5,1},... | collective-permute-start | bytes 3244040 | tf_op jit(solution)/shard_map/ppermute | solution.py:359
  6.6 0.6 pad_add_fusion.scal
  7.3 9.4 %expert_step.5 = (bf16[64,2048]{1,0:T(8,128)(2,1)}, bf16[64,4352]{1,0:T(8,128)(2,1)}, bf16[64,4096]{1,0:T(8,128)(2,1)}, bf16[64,2048]{1,0:T(8,128)(2,1)}) custom-call(s32[3]{0:T(128)} %pad_add_fusion.scal, bf16[128,4224]{1,0:T(8,128)(2,1)} %get-tuple-element.96.refs_0_, bf16[2048,1536]{1,0:T(8,128)(2,1)} %bitcast.21, bf16[768,2048]{1,0:T(8,128)(2,1)} %bitcast.26), custom_call_target="tpu_custom_call" | custom-call | flops 4026531840 | bytes 9437184 | tf_op jit(solution)/shard_map/expert_step/pallas_call | solution.py:153
  16.6 13.4 %collective-permute-done.1.refs_1_ = bf16[128,4224]{1,0:T(8,128)(2,1)S(1)} collective-permute-done((bf16[128,4224]{1,0:T(8,128)(2,1)}, bf16[128,4224]{1,0:T(8,128)(2,1)S(1)}, u32[]{:S(2)}, u32[]{:S(2)}) %collective-permute-start.1) | collective-permute-done | bytes 1081376 | tf_op jit(solution)/shard_map/ppermute | solution.py:359
  30.0 1.4 collective-permute-done.refs_0_
  31.8 1.6 collective-permute-start.3
  33.5 9.8 %expert_step.6 = (bf16[128,2048]{1,0:T(8,128)(2,1)}, bf16[128,4352]{1,0:T(8,128)(2,1)}, bf16[128,4096]{1,0:T(8,128)(2,1)}, bf16[64,2048]{1,0:T(8,128)(2,1)}, bf1...) custom-call(s32[3]{0:T(128)} %pad_add_fusion.scal, bf16[128,4224]{1,0:T(8,128)(2,1)} %copy-done.17, ...), custom_call_target="tpu_custom_call" | custom-call | flops 4026531840 | bytes 9437184 | tf_op jit(solution)/shard_map/expert_step/pallas_call | solution.py:153
  43.3 12.6 %collective-permute-done.2.refs_0_ = bf16[128,4224]{1,0:T(8,128)(2,1)} collective-permute-done((bf16[128,4224]{1,0:T(8,128)(2,1)S(1)}, bf16[128,4224]{1,0:T(8,128)(2,1)}, u32[]{:S(2)}, u32[]{:S(2)}) %collective-permute-start.2) | collective-permute-done | bytes 1081376 | tf_op jit(solution)/shard_map/ppermute | solution.py:359
  56.4 1.6 collective-permute-start.4
  58.0 0.4 collective-permute-start.5
  58.4 10.0 %expert_step.7 = (bf16[128,2048]{1,0:T(8,128)(2,1)}, bf16[128,4352]{1,0:T(8,128)(2,1)}, bf16[128,4096]{1,0:T(8,128)(2,1)}, bf16[64,2048]{1,0:T(8,128)(2,1)}, bf1...) custom-call(s32[3]{0:T(128)} %pad_add_fusion.scal, bf16[128,4224]{1,0:T(8,128)(2,1)} %collective-permute-done.2.refs_0_, ...), custom_call_target="tpu_custom_call" | custom-call | flops 4026531840 | bytes 9437184 | tf_op jit(solution)/shard_map/expert_step/pallas_call | solution.py:153
  68.8 1.3 collective-permute-start.8
  70.1 10.3 %collective-permute-done.4.refs_0_ = bf16[128,4224]{1,0:T(8,128)(2,1)} collective-permute-done((bf16[128,4224]{1,0:T(8,128)(2,1)}, bf16[128,4224]{1,0:T(8,128)(2,1)}, u32[]{:S(2)}, u32[]{:S(2)}) %collective-permute-start.4) | collective-permute-done | bytes 1081376 | tf_op jit(solution)/shard_map/ppermute | solution.py:359
  80.4 1.6 collective-permute-start.9
  82.1 2.9 %collective-permute-done.5.refs_1_ = bf16[128,4224]{1,0:T(8,128)(2,1)} collective-permute-done((bf16[128,4224]{1,0:T(8,128)(2,1)}, bf16[128,4224]{1,0:T(8,128)(2,1)}, u32[]{:S(2)}, u32[]{:S(2)}) %collective-permute-start.5) | collective-permute-done | bytes 1081376 | tf_op jit(solution)/shard_map/ppermute | solution.py:359
  85.0 1.1 slice.10
  86.0 1.6 collective-permute-start.10
  87.7 1.1 slice.11
  88.8 0.5 collective-permute-start.11
  89.3 0.9 collective-permute-done.8.refs_8_
  90.2 1.6 collective-permute-start.13
  91.8 1.3 collective-permute-start.14
  93.1 9.8 %expert_step.8 = (bf16[128,2048]{1,0:T(8,128)(2,1)}, bf16[128,4352]{1,0:T(8,128)(2,1)}, bf16[128,4096]{1,0:T(8,128)(2,1)}, bf16[64,2048]{1,0:T(8,128)(2,1)}, bf1...) custom-call(s32[3]{0:T(128)} %pad_add_fusion.scal, bf16[128,4224]{1,0:T(8,128)(2,1)} %collective-permute-done.4.refs_0_, ...), custom_call_target="tpu_custom_call" | custom-call | flops 4026531840 | bytes 9437184 | tf_op jit(solution)/shard_map/expert_step/pallas_call | solution.py:153
  103.0 1.3 constant_dynamic-slice_fusion.1
  104.3 0.8 copy-done.19
  105.1 0.6 collective-permute-done.11.refs_1_
  105.7 4.9 %collective-permute-start.19 = (bf16[64,2048]{1,0:T(8,128)(2,1)}, bf16[64,2048]{1,0:T(8,128)(2,1)S(1)}, u32[]{:S(2)}, u32[]{:S(2)}) collective-permute-start(bf16[64,2048]{1,0:T(8,128)(2,1)} %get-tuple-element.152), channel_id=1, source_target_pairs={{0,12},{4,14},{8,10},{12,6},{14,2},{10,0},{6,4},{2,8},{1,13},{5,15... | collective-permute-start | bytes 786440 | tf_op jit(solution)/shard_map/ppermute | solution.py:359
  110.6 0.4 collective-permute-start.20
  111.0 9.6 %expert_step.9 = (bf16[64,2048]{1,0:T(8,128)(2,1)}, bf16[64,4352]{1,0:T(8,128)(2,1)}, bf16[64,4096]{1,0:T(8,128)(2,1)}, bf16[32,2048]{1,0:T(8,128)(2,1)}, bf16[3...) custom-call(s32[3]{0:T(128)} %pad_add_fusion.scal, bf16[128,2048]{1,0:T(8,128)(2,1)} %copy-done.19, ...), custom_call_target="tpu_custom_call" | custom-call | flops 4026531840 | bytes 9437184 | tf_op jit(solution)/shard_map/expert_step/pallas_call | solution.py:153
  120.7 6.8 %collective-permute-done.13.refs_7_ = bf16[64,2048]{1,0:T(8,128)(2,1)S(1)} collective-permute-done((bf16[64,2048]{1,0:T(8,128)(2,1)}, bf16[64,2048]{1,0:T(8,128)(2,1)S(1)}, u32[]{:S(2)}, u32[]{:S(2)}) %collective-permute-start.13) | collective-permute-done | bytes 262176 | tf_op jit(solution)/shard_map/ppermute | solution.py:359
  127.5 1.3 constant_dynamic-slice_fusion
  129.2 2.0 %collective-permute-start.17 = (bf16[288,256]{1,0:T(8,128)(2,1)S(1)}, bf16[288,256]{1,0:T(8,128)(2,1)S(1)}, u32[]{:S(2)}, u32[]{:S(2)}) collective-permute-start(bf16[288,256]{1,0:T(8,128)(2,1)S(1)} %get-tuple-element.141), channel_id=1, source_target_pairs={{0,2},{4,0},{8,4},{12,8},{14,12},{10,14},{6,10},{2,6},{1,3},{5,1},... | collective-permute-start | bytes 442376 | tf_op jit(solution)/shard_map/ppermute | solution.py:359
  131.3 0.8 copy-done.6
  132.1 10.8 %expert_gradient.1 = f32[1,1024,2304]{2,1,0:T(8,128)} custom-call(s32[3]{0:T(128)} %pad_add_fusion.scal, bf16[64,2048]{1,0:T(8,128)(2,1)} %get-tuple-element.142.refs_0_.refs_10_, bf16[128,2048]{1,0:T(8,128)(2,1)} %get-tuple-element.143.refs_1_.refs_11_, bf16[128,2048]{1,0:T(8,128)(2,1)} %get-tuple-element.144.refs_2_.refs_12_, ...), custom_call_target="tpu_custom_call" | custom-call | flops 4831838208 | bytes 14155776 | tf_op jit(solution)/shard_map/expert_gradient/pallas_call | solution.py:228
  143.2 2.1 %collective-permute-start.21 = (bf16[288,512]{1,0:T(8,128)(2,1)S(1)}, bf16[288,512]{1,0:T(8,128)(2,1)S(1)}, u32[]{:S(2)}, u32[]{:S(2)}) collective-permute-start(bf16[288,512]{1,0:T(8,128)(2,1)S(1)} %maximum_select_fusion), channel_id=1, source_target_pairs={{0,4},{4,8},{8,12},{12,14},{14,10},{10,6},{6,2},{2,0},{1,5},{5,9},... | collective-permute-start | bytes 884744 | tf_op jit(solution)/shard_map/ppermute | solution.py:359
  145.2 1.3 collective-permute-start.23
  146.5 9.3 %collective-permute-done.23.refs_4_ = bf16[32,2048]{1,0:T(8,128)(2,1)S(1)} collective-permute-done((bf16[32,2048]{1,0:T(8,128)(2,1)S(1)}, bf16[32,2048]{1,0:T(8,128)(2,1)S(1)}, u32[]{:S(2)}, u32[]{:S(2)}) %collective-permute-start.23) | collective-permute-done | bytes 131104 | tf_op jit(solution)/shard_map/ppermute | solution.py:359
  155.9 2.2 %collective-permute-start.24 = (bf16[288,512]{1,0:T(8,128)(2,1)S(1)}, bf16[288,512]{1,0:T(8,128)(2,1)S(1)}, u32[]{:S(2)}, u32[]{:S(2)}) collective-permute-start(bf16[288,512]{1,0:T(8,128)(2,1)S(1)} %broadcast_select_fusion.3), channel_id=1, source_target_pairs={{0,4},{4,8},{8,12},{12,14},{14,10},{10,6},{6,2},{2,0},{1,5},{5,9},... | collective-permute-start | bytes 884744 | tf_op jit(solution)/shard_map/ppermute | solution.py:359
  158.2 3.5 %collective-permute-start.26 = (bf16[32,2048]{1,0:T(8,128)(2,1)S(1)}, bf16[32,2048]{1,0:T(8,128)(2,1)S(1)}, u32[]{:S(2)}, u32[]{:S(2)}) collective-permute-start(bf16[32,2048]{1,0:T(8,128)(2,1)S(1)} %copy-done.20), channel_id=1, source_target_pairs={{0,14},{4,10},{8,6},{12,2},{14,0},{10,4},{6,8},{2,12},{1,15},{5,11... | collective-permute-start | bytes 393224 | tf_op jit(solution)/shard_map/ppermute | solution.py:359
  161.7 4.5 %hot_rows_ordered.1 = (bf16[512,2048]{1,0:T(8,128)(2,1)}, bf16[512,2048]{1,0:T(8,128)(2,1)}) custom-call(s32[3]{0:T(128)} %pad_add_fusion.scal, bf16[64,4096]{1,0:T(8,128)(2,1)} %get-tuple-element.168.refs_0_, bf16[128,4096]{1,0:T(8,128)(2,1)} %get-tuple-element.169.refs_1_, bf16[128,4096]{1,0:T(8,128)(2,1)} %get-tuple-element.170.refs_2_, ...), custom_call_target="tpu_custom_call" | custom-call | bytes 8388608 | tf_op jit(solution)/shard_map/hot_rows_ordered/pallas_call | solution.py:293
  166.2 4.1 %collective-permute-done.26.refs_5_ = bf16[32,2048]{1,0:T(8,128)(2,1)S(1)} collective-permute-done((bf16[32,2048]{1,0:T(8,128)(2,1)S(1)}, bf16[32,2048]{1,0:T(8,128)(2,1)S(1)}, u32[]{:S(2)}, u32[]{:S(2)}) %collective-permute-start.26) | collective-permute-done | bytes 131104 | tf_op jit(solution)/shard_map/ppermute | solution.py:359
  170.4 2.3 %collective-permute-start.27 = (bf16[288,512]{1,0:T(8,128)(2,1)S(1)}, bf16[288,512]{1,0:T(8,128)(2,1)S(1)}, u32[]{:S(2)}, u32[]{:S(2)}) collective-permute-start(bf16[288,512]{1,0:T(8,128)(2,1)S(1)} %broadcast_select_fusion.1), channel_id=1, source_target_pairs={{0,4},{4,8},{8,12},{12,14},{14,10},{10,6},{6,2},{2,0},{1,5},{5,9},... | collective-permute-start | bytes 884744 | tf_op jit(solution)/shard_map/ppermute | solution.py:359
  173.1 6.7 %collective-permute-done.27 = bf16[288,512]{1,0:T(8,128)(2,1)S(1)} collective-permute-done((bf16[288,512]{1,0:T(8,128)(2,1)S(1)}, bf16[288,512]{1,0:T(8,128)(2,1)S(1)}, u32[]{:S(2)}, u32[]{:S(2)}) %collective-permute-start.27) | collective-permute-done | bytes 294944 | tf_op jit(solution)/shard_map/ppermute | solution.py:359
  179.9 2.5 %collective-permute-done.28 = bf16[288,512]{1,0:T(8,128)(2,1)} collective-permute-done((bf16[288,512]{1,0:T(8,128)(2,1)S(1)}, bf16[288,512]{1,0:T(8,128)(2,1)}, u32[]{:S(2)}, u32[]{:S(2)}) %collective-permute-start.28) | collective-permute-done | bytes 294944 | tf_op jit(solution)/shard_map/ppermute | solution.py:359
  182.4 1.0 select_select_fusion.mine
  183.5 3.2 %token_sum.1 = bf16[128,2048]{1,0:T(8,128)(2,1)} custom-call(s32[3]{0:T(128)} %pad_add_fusion.scal, bf16[128,128]{1,0:T(8,128)(2,1)} %get-tuple-element.95.meta, bf16[64,2048]{1,0:T(8,128)(2,1)} %get-tuple-element.119.refs_0_, bf16[64,2048]{1,0:T(8,128)(2,1)} %collective-permute-done.9.refs_1_, bf16[64,2048]{1,0:T(8,128)(2,1)} %copy-done.11, ...), custom_call_target="tpu_custom_call" | custom-call | flops 268435456 | bytes 2097152 | tf_op jit(solution)/shard_map/token_sum/pallas_call | solution.py:188
  186.7 2.3 %shadow_gradient.1 = f32[288,1024]{1,0:T(8,128)} custom-call(s32[3]{0:T(128)S(1)} %copy-done.1, bf16[288,512]{1,0:T(8,128)(2,1)S(1)} %select_select_fusion.mine, bf16[288,512]{1,0:T(8,128)(2,1)S(1)} %collective-permute-done.29.theirs, bf16[512,2048]{1,0:T(8,128)(2,1)S(1)} %copy-done, bf16[512,2048]{1,0:T(8,128)(2,1)S(1)} %collective-permute-done.30.hot_theirs), custom_call_target="tpu_custom_call" | custom-call | flops 603979776 | bytes 2097152 | tf_op jit(solution)/shard_map/shadow_gradient/pallas_call | solution.py:332
  (88 shorter events, 2.7 us)
Async XLA Ops:
  3.0 27.1 %collective-permute-start.1 = (bf16[128,4224]{1,0:T(8,128)(2,1)}, bf16[128,4224]{1,0:T(8,128)(2,1)S(1)}, u32[]{:S(2)}, u32[]{:S(2)}) collective-permute-start(bf16[128,4224]{1,0:T(8,128)(2,1)} %get-tuple-element.96.refs_0_), channel_id=1, source_target_pairs={{0,2},{4,0},{8,4},{12,8},{14,12},{10,14},{6,10},{2,6},{1,3},{5,1},... | collective-permute-start | bytes 3244040 | tf_op jit(solution)/shard_map/ppermute | solution.py:359
  5.9 25.5 %collective-permute-start = (bf16[128,4224]{1,0:T(8,128)(2,1)}, bf16[128,4224]{1,0:T(8,128)(2,1)S(1)}, u32[]{:S(2)}, u32[]{:S(2)}) collective-permute-start(bf16[128,4224]{1,0:T(8,128)(2,1)} %get-tuple-element.96.refs_0_), channel_id=1, source_target_pairs={{0,4},{4,8},{8,12},{12,14},{14,10},{10,6},{6,2},{2,0},{1,5},{5,9},... | collective-permute-start | bytes 3244040 | tf_op jit(solution)/shard_map/ppermute | solution.py:359
  30.0 3.4 %copy-start.16 = (bf16[128,4224]{1,0:T(8,128)(2,1)}, bf16[128,4224]{1,0:T(8,128)(2,1)S(1)}, u32[]{:S(2)}) copy-start(bf16[128,4224]{1,0:T(8,128)(2,1)S(1)} %collective-permute-done.1.refs_1_) | copy-start | bytes 3244036
  31.5 24.5 %collective-permute-start.2 = (bf16[128,4224]{1,0:T(8,128)(2,1)S(1)}, bf16[128,4224]{1,0:T(8,128)(2,1)}, u32[]{:S(2)}, u32[]{:S(2)}) collective-permute-start(bf16[128,4224]{1,0:T(8,128)(2,1)S(1)} %collective-permute-done.refs_0_), channel_id=1, source_target_pairs={{0,4},{4,8},{8,12},{12,14},{14,10},{10,6},{6,2},{2,0},{1,5},{5,9},... | collective-permute-start | bytes 3244040 | tf_op jit(solution)/shard_map/ppermute | solution.py:359
  31.8 24.6 %collective-permute-start.3 = (bf16[128,4224]{1,0:T(8,128)(2,1)S(1)}, bf16[128,4224]{1,0:T(8,128)(2,1)}, u32[]{:S(2)}, u32[]{:S(2)}) collective-permute-start(bf16[128,4224]{1,0:T(8,128)(2,1)S(1)} %collective-permute-done.1.refs_1_), channel_id=1, source_target_pairs={{0,2},{4,0},{8,4},{12,8},{14,12},{10,14},{6,10},{2,6},{1,3},{5,1},... | collective-permute-start | bytes 3244040 | tf_op jit(solution)/shard_map/ppermute | solution.py:359
  33.5 25.0 %collective-permute-start.6 = (bf16[64,4352]{1,0:T(8,128)(2,1)}, bf16[64,4352]{1,0:T(8,128)(2,1)S(1)}, u32[]{:S(2)}, u32[]{:S(2)}) collective-permute-start(bf16[64,4352]{1,0:T(8,128)(2,1)} %get-tuple-element.104.refs_2_.refs_20_), channel_id=1, source_target_pairs={{0,1},{1,0},{2,3},{3,2},{4,5},{5,4},{6,7},{7,6},{8,9},{9,8},{10,11... | collective-permute-start | bytes 1671176 | tf_op jit(solution)/shard_map/ppermute | solution.py:362
  56.4 24.0 %collective-permute-start.4 = (bf16[128,4224]{1,0:T(8,128)(2,1)}, bf16[128,4224]{1,0:T(8,128)(2,1)}, u32[]{:S(2)}, u32[]{:S(2)}) collective-permute-start(bf16[128,4224]{1,0:T(8,128)(2,1)} %collective-permute-done.2.refs_0_), channel_id=1, source_target_pairs={{0,4},{4,8},{8,12},{12,14},{14,10},{10,6},{6,2},{2,0},{1,5},{5,9},... | collective-permute-start | bytes 3244040 | tf_op jit(solution)/shard_map/ppermute | solution.py:359
  58.0 24.0 %copy-start.8 = (bf16[2304,128]{1,0:T(8,128)(2,1)S(1)}, bf16[2304,128]{1,0:T(8,128)(2,1)}, u32[]{:S(2)}) copy-start(bf16[2304,128]{1,0:T(8,128)(2,1)} %get-tuple-element.135) | copy-start | bytes 1769476
  58.0 30.8 %collective-permute-start.7 = (bf16[128,4352]{1,0:T(8,128)(2,1)}, bf16[128,4352]{1,0:T(8,128)(2,1)S(1)}, u32[]{:S(2)}, u32[]{:S(2)}) collective-permute-start(bf16[128,4352]{1,0:T(8,128)(2,1)} %get-tuple-element.111.refs_21_), channel_id=1, source_target_pairs={{0,1},{1,0},{2,3},{3,2},{4,5},{5,4},{6,7},{7,6},{8,9},{9,8},{10,11... | collective-permute-start | bytes 3342344 | tf_op jit(solution)/shard_map/ppermute | solution.py:362
  58.0 27.0 %collective-permute-start.5 = (bf16[128,4224]{1,0:T(8,128)(2,1)}, bf16[128,4224]{1,0:T(8,128)(2,1)}, u32[]{:S(2)}, u32[]{:S(2)}) collective-permute-start(bf16[128,4224]{1,0:T(8,128)(2,1)} %collective-permute-done.3.refs_1_), channel_id=1, source_target_pairs={{0,2},{4,0},{8,4},{12,8},{14,12},{10,14},{6,10},{2,6},{1,3},{5,1},... | collective-permute-start | bytes 3244040 | tf_op jit(solution)/shard_map/ppermute | solution.py:359
  58.4 10.0 %copy-start.5 = (bf16[64,4352]{1,0:T(8,128)(2,1)}, bf16[64,4352]{1,0:T(8,128)(2,1)S(1)}, u32[]{:S(2)}) copy-start(bf16[64,4352]{1,0:T(8,128)(2,1)S(1)} %collective-permute-done.6.refs_5_.refs_15_.refs_25_) | copy-start | bytes 1671172
  68.5 37.2 %collective-permute-start.12 = (bf16[128,4352]{1,0:T(8,128)(2,1)}, bf16[128,4352]{1,0:T(8,128)(2,1)S(1)}, u32[]{:S(2)}, u32[]{:S(2)}) collective-permute-start(bf16[128,4352]{1,0:T(8,128)(2,1)} %get-tuple-element.127.refs_22_), channel_id=1, source_target_pairs={{0,1},{1,0},{2,3},{3,2},{4,5},{5,4},{6,7},{7,6},{8,9},{9,8},{10,11... | collective-permute-start | bytes 3342344 | tf_op jit(solution)/shard_map/ppermute | solution.py:362
  68.8 21.4 %collective-permute-start.8 = (bf16[64,2048]{1,0:T(8,128)(2,1)}, bf16[64,2048]{1,0:T(8,128)(2,1)}, u32[]{:S(2)}, u32[]{:S(2)}) collective-permute-start(bf16[64,2048]{1,0:T(8,128)(2,1)} %get-tuple-element.116), channel_id=1, source_target_pairs={{0,2},{4,0},{8,4},{12,8},{14,12},{10,14},{6,10},{2,6},{1,3},{5,1},... | collective-permute-start | bytes 786440 | tf_op jit(solution)/shard_map/ppermute | solution.py:359
  80.4 9.8 %collective-permute-start.9 = (bf16[64,2048]{1,0:T(8,128)(2,1)}, bf16[64,2048]{1,0:T(8,128)(2,1)}, u32[]{:S(2)}, u32[]{:S(2)}) collective-permute-start(bf16[64,2048]{1,0:T(8,128)(2,1)} %get-tuple-element.117), channel_id=1, source_target_pairs={{0,4},{4,8},{8,12},{12,14},{14,10},{10,6},{6,2},{2,0},{1,5},{5,9},... | collective-permute-start | bytes 786440 | tf_op jit(solution)/shard_map/ppermute | solution.py:359
  82.0 7.2 %copy-start.9 = (bf16[2304,128]{1,0:T(8,128)(2,1)S(1)}, bf16[2304,128]{1,0:T(8,128)(2,1)}, u32[]{:S(2)}) copy-start(bf16[2304,128]{1,0:T(8,128)(2,1)} %get-tuple-element.136) | copy-start | bytes 1769476
  86.0 18.2 %collective-permute-start.10 = (bf16[128,2048]{1,0:T(8,128)(2,1)S(1)}, bf16[128,2048]{1,0:T(8,128)(2,1)S(1)}, u32[]{:S(2)}, u32[]{:S(2)}) collective-permute-start(bf16[128,2048]{1,0:T(8,128)(2,1)S(1)} %slice.10), channel_id=1, source_target_pairs={{0,4},{4,8},{8,12},{12,14},{14,10},{10,6},{6,2},{2,0},{1,5},{5,9},... | collective-permute-start | bytes 1572872 | tf_op jit(solution)/shard_map/ppermute | solution.py:359
  88.8 14.2 %copy-start.2 = (bf16[128,4352]{1,0:T(8,128)(2,1)}, bf16[128,4352]{1,0:T(8,128)(2,1)S(1)}, u32[]{:S(2)}) copy-start(bf16[128,4352]{1,0:T(8,128)(2,1)S(1)} %collective-permute-done.7.refs_6_.refs_16_.refs_26_) | copy-start | bytes 3342340
  88.8 16.9 %collective-permute-start.11 = (bf16[128,2176]{1,0:T(8,128)(2,1)S(1)}, bf16[128,2176]{1,0:T(8,128)(2,1)S(1)}, u32[]{:S(2)}, u32[]{:S(2)}) collective-permute-start(bf16[128,2176]{1,0:T(8,128)(2,1)S(1)} %slice.11), channel_id=1, source_target_pairs={{0,2},{4,0},{8,4},{12,8},{14,12},{10,14},{6,10},{2,6},{1,3},{5,1},... | collective-permute-start | bytes 1671176 | tf_op jit(solution)/shard_map/ppermute | solution.py:359
  90.2 37.2 %collective-permute-start.13 = (bf16[64,2048]{1,0:T(8,128)(2,1)}, bf16[64,2048]{1,0:T(8,128)(2,1)S(1)}, u32[]{:S(2)}, u32[]{:S(2)}) collective-permute-start(bf16[64,2048]{1,0:T(8,128)(2,1)} %get-tuple-element.131), channel_id=1, source_target_pairs={{0,6},{4,2},{8,0},{12,4},{14,8},{10,12},{6,14},{2,10},{1,7},{5,3},... | collective-permute-start | bytes 786440 | tf_op jit(solution)/shard_map/ppermute | solution.py:359
  91.8 35.7 %collective-permute-start.14 = (bf16[64,2048]{1,0:T(8,128)(2,1)}, bf16[64,2048]{1,0:T(8,128)(2,1)S(1)}, u32[]{:S(2)}, u32[]{:S(2)}) collective-permute-start(bf16[64,2048]{1,0:T(8,128)(2,1)} %get-tuple-element.132), channel_id=1, source_target_pairs={{0,8},{4,12},{8,14},{12,10},{14,6},{10,2},{6,0},{2,4},{1,9},{5,13}... | collective-permute-start | bytes 786440 | tf_op jit(solution)/shard_map/ppermute | solution.py:359
  103.0 2.1 %copy-start.7 = (bf16[128,4352]{1,0:T(8,128)(2,1)S(1)}, bf16[128,4352]{1,0:T(8,128)(2,1)}, u32[]{:S(2)}) copy-start(bf16[128,4352]{1,0:T(8,128)(2,1)} %get-tuple-element.139.refs_23_) | copy-start | bytes 3342340
  105.1 24.1 %collective-permute-start.15 = (bf16[128,4352]{1,0:T(8,128)(2,1)S(1)}, bf16[128,4352]{1,0:T(8,128)(2,1)S(1)}, u32[]{:S(2)}, u32[]{:S(2)}) collective-permute-start(bf16[128,4352]{1,0:T(8,128)(2,1)S(1)} %copy-done.7), channel_id=1, source_target_pairs={{0,1},{1,0},{2,3},{3,2},{4,5},{5,4},{6,7},{7,6},{8,9},{9,8},{10,11... | collective-permute-start | bytes 3342344 | tf_op jit(solution)/shard_map/ppermute | solution.py:362
  105.7 5.4 %copy-start.18 = (bf16[128,2176]{1,0:T(8,128)(2,1)}, bf16[128,2176]{1,0:T(8,128)(2,1)S(1)}, u32[]{:S(2)}) copy-start(bf16[128,2176]{1,0:T(8,128)(2,1)S(1)} %collective-permute-done.11.refs_1_) | copy-start | bytes 1671172
  105.7 15.0 %copy-start.3 = (bf16[128,4352]{1,0:T(8,128)(2,1)}, bf16[128,4352]{1,0:T(8,128)(2,1)S(1)}, u32[]{:S(2)}) copy-start(bf16[128,4352]{1,0:T(8,128)(2,1)S(1)} %collective-permute-done.12.refs_7_.refs_17_.refs_27_) | copy-start | bytes 3342340
  105.7 37.2 %collective-permute-start.19 = (bf16[64,2048]{1,0:T(8,128)(2,1)}, bf16[64,2048]{1,0:T(8,128)(2,1)S(1)}, u32[]{:S(2)}, u32[]{:S(2)}) collective-permute-start(bf16[64,2048]{1,0:T(8,128)(2,1)} %get-tuple-element.152), channel_id=1, source_target_pairs={{0,12},{4,14},{8,10},{12,6},{14,2},{10,0},{6,4},{2,8},{1,13},{5,15... | collective-permute-start | bytes 786440 | tf_op jit(solution)/shard_map/ppermute | solution.py:359
  110.6 32.3 %collective-permute-start.20 = (bf16[64,2048]{1,0:T(8,128)(2,1)}, bf16[64,2048]{1,0:T(8,128)(2,1)S(1)}, u32[]{:S(2)}, u32[]{:S(2)}) collective-permute-start(bf16[64,2048]{1,0:T(8,128)(2,1)} %get-tuple-element.153), channel_id=1, source_target_pairs={{0,10},{4,6},{8,2},{12,0},{14,4},{10,8},{6,12},{2,14},{1,11},{5,7}... | collective-permute-start | bytes 786440 | tf_op jit(solution)/shard_map/ppermute | solution.py:359
  127.4 3.8 %collective-permute-start.18 = (bf16[64,4352]{1,0:T(8,128)(2,1)}, bf16[64,4352]{1,0:T(8,128)(2,1)S(1)}, u32[]{:S(2)}, u32[]{:S(2)}) collective-permute-start(bf16[64,4352]{1,0:T(8,128)(2,1)} %get-tuple-element.151.refs_24_), channel_id=1, source_target_pairs={{0,1},{1,0},{2,3},{3,2},{4,5},{5,4},{6,7},{7,6},{8,9},{9,8},{10,11... | collective-permute-start | bytes 1671176 | tf_op jit(solution)/shard_map/ppermute | solution.py:362
  129.2 2.1 %copy-start.4 = (bf16[128,4352]{1,0:T(8,128)(2,1)}, bf16[128,4352]{1,0:T(8,128)(2,1)S(1)}, u32[]{:S(2)}) copy-start(bf16[128,4352]{1,0:T(8,128)(2,1)S(1)} %collective-permute-done.15.refs_8_.refs_18_.refs_28_) | copy-start | bytes 3342340
  129.2 13.7 %collective-permute-start.16 = (bf16[288,256]{1,0:T(8,128)(2,1)S(1)}, bf16[288,256]{1,0:T(8,128)(2,1)S(1)}, u32[]{:S(2)}, u32[]{:S(2)}) collective-permute-start(bf16[288,256]{1,0:T(8,128)(2,1)S(1)} %get-tuple-element.140), channel_id=1, source_target_pairs={{0,4},{4,8},{8,12},{12,14},{14,10},{10,6},{6,2},{2,0},{1,5},{5,9},... | collective-permute-start | bytes 442376 | tf_op jit(solution)/shard_map/ppermute | solution.py:359
  129.2 13.7 %collective-permute-start.17 = (bf16[288,256]{1,0:T(8,128)(2,1)S(1)}, bf16[288,256]{1,0:T(8,128)(2,1)S(1)}, u32[]{:S(2)}, u32[]{:S(2)}) collective-permute-start(bf16[288,256]{1,0:T(8,128)(2,1)S(1)} %get-tuple-element.141), channel_id=1, source_target_pairs={{0,2},{4,0},{8,4},{12,8},{14,12},{10,14},{6,10},{2,6},{1,3},{5,1},... | collective-permute-start | bytes 442376 | tf_op jit(solution)/shard_map/ppermute | solution.py:359
  142.8 2.4 %copy-start.21 = (bf16[32,2048]{1,0:T(8,128)(2,1)S(1)}, bf16[32,2048]{1,0:T(8,128)(2,1)}, u32[]{:S(2)}) copy-start(bf16[32,2048]{1,0:T(8,128)(2,1)} %get-tuple-element.161) | copy-start | bytes 393220
  142.9 13.0 %copy-start.12 = (bf16[64,2048]{1,0:T(8,128)(2,1)}, bf16[64,2048]{1,0:T(8,128)(2,1)S(1)}, u32[]{:S(2)}) copy-start(bf16[64,2048]{1,0:T(8,128)(2,1)S(1)} %collective-permute-done.19.refs_3_) | copy-start | bytes 786436
  142.9 13.0 %copy-start.13 = (bf16[64,2048]{1,0:T(8,128)(2,1)}, bf16[64,2048]{1,0:T(8,128)(2,1)S(1)}, u32[]{:S(2)}) copy-start(bf16[64,2048]{1,0:T(8,128)(2,1)S(1)} %collective-permute-done.20.refs_6_) | copy-start | bytes 786436
  143.0 15.2 %copy-start.20 = (bf16[32,2048]{1,0:T(8,128)(2,1)S(1)}, bf16[32,2048]{1,0:T(8,128)(2,1)}, u32[]{:S(2)}) copy-start(bf16[32,2048]{1,0:T(8,128)(2,1)} %get-tuple-element.167) | copy-start | bytes 393220
  143.0 12.8 %collective-permute-start.22 = (bf16[288,512]{1,0:T(8,128)(2,1)S(1)}, bf16[288,512]{1,0:T(8,128)(2,1)S(1)}, u32[]{:S(2)}, u32[]{:S(2)}) collective-permute-start(bf16[288,512]{1,0:T(8,128)(2,1)S(1)} %maximum_select_fusion.1), channel_id=1, source_target_pairs={{0,2},{4,0},{8,4},{12,8},{14,12},{10,14},{6,10},{2,6},{1,3},{5,1},... | collective-permute-start | bytes 884744 | tf_op jit(solution)/shard_map/ppermute | solution.py:359
  143.2 12.7 %collective-permute-start.21 = (bf16[288,512]{1,0:T(8,128)(2,1)S(1)}, bf16[288,512]{1,0:T(8,128)(2,1)S(1)}, u32[]{:S(2)}, u32[]{:S(2)}) collective-permute-start(bf16[288,512]{1,0:T(8,128)(2,1)S(1)} %maximum_select_fusion), channel_id=1, source_target_pairs={{0,4},{4,8},{8,12},{12,14},{14,10},{10,6},{6,2},{2,0},{1,5},{5,9},... | collective-permute-start | bytes 884744 | tf_op jit(solution)/shard_map/ppermute | solution.py:359
  145.2 10.6 %collective-permute-start.23 = (bf16[32,2048]{1,0:T(8,128)(2,1)S(1)}, bf16[32,2048]{1,0:T(8,128)(2,1)S(1)}, u32[]{:S(2)}, u32[]{:S(2)}) collective-permute-start(bf16[32,2048]{1,0:T(8,128)(2,1)S(1)} %copy-done.21), channel_id=1, source_target_pairs={{0,14},{4,10},{8,6},{12,2},{14,0},{10,4},{6,8},{2,12},{1,15},{5,11... | collective-permute-start | bytes 393224 | tf_op jit(solution)/shard_map/ppermute | solution.py:359
  155.8 10.4 %copy-start.14 = (bf16[32,2048]{1,0:T(8,128)(2,1)}, bf16[32,2048]{1,0:T(8,128)(2,1)S(1)}, u32[]{:S(2)}) copy-start(bf16[32,2048]{1,0:T(8,128)(2,1)S(1)} %collective-permute-done.23.refs_4_) | copy-start | bytes 393220
  155.9 14.4 %collective-permute-start.24 = (bf16[288,512]{1,0:T(8,128)(2,1)S(1)}, bf16[288,512]{1,0:T(8,128)(2,1)S(1)}, u32[]{:S(2)}, u32[]{:S(2)}) collective-permute-start(bf16[288,512]{1,0:T(8,128)(2,1)S(1)} %broadcast_select_fusion.3), channel_id=1, source_target_pairs={{0,4},{4,8},{8,12},{12,14},{14,10},{10,6},{6,2},{2,0},{1,5},{5,9},... | collective-permute-start | bytes 884744 | tf_op jit(solution)/shard_map/ppermute | solution.py:359
  158.2 12.1 %collective-permute-start.25 = (bf16[288,512]{1,0:T(8,128)(2,1)S(1)}, bf16[288,512]{1,0:T(8,128)(2,1)S(1)}, u32[]{:S(2)}, u32[]{:S(2)}) collective-permute-start(bf16[288,512]{1,0:T(8,128)(2,1)S(1)} %broadcast_select_fusion.2), channel_id=1, source_target_pairs={{0,2},{4,0},{8,4},{12,8},{14,12},{10,14},{6,10},{2,6},{1,3},{5,1},... | collective-permute-start | bytes 884744 | tf_op jit(solution)/shard_map/ppermute | solution.py:359
  158.2 12.1 %collective-permute-start.26 = (bf16[32,2048]{1,0:T(8,128)(2,1)S(1)}, bf16[32,2048]{1,0:T(8,128)(2,1)S(1)}, u32[]{:S(2)}, u32[]{:S(2)}) collective-permute-start(bf16[32,2048]{1,0:T(8,128)(2,1)S(1)} %copy-done.20), channel_id=1, source_target_pairs={{0,14},{4,10},{8,6},{12,2},{14,0},{10,4},{6,8},{2,12},{1,15},{5,11... | collective-permute-start | bytes 393224 | tf_op jit(solution)/shard_map/ppermute | solution.py:359
  170.3 13.1 %copy-start.15 = (bf16[32,2048]{1,0:T(8,128)(2,1)}, bf16[32,2048]{1,0:T(8,128)(2,1)S(1)}, u32[]{:S(2)}) copy-start(bf16[32,2048]{1,0:T(8,128)(2,1)S(1)} %collective-permute-done.26.refs_5_) | copy-start | bytes 393220
  170.3 16.4 %collective-permute-start.30 = (bf16[512,2048]{1,0:T(8,128)(2,1)}, bf16[512,2048]{1,0:T(8,128)(2,1)S(1)}, u32[]{:S(2)}, u32[]{:S(2)}) collective-permute-start(bf16[512,2048]{1,0:T(8,128)(2,1)} %get-tuple-element.186), channel_id=1, source_target_pairs={{0,1},{1,0},{2,3},{3,2},{4,5},{5,4},{6,7},{7,6},{8,9},{9,8},{10,11... | collective-permute-start | bytes 6291464 | tf_op jit(solution)/shard_map/ppermute | solution.py:362
  170.4 9.5 %collective-permute-start.27 = (bf16[288,512]{1,0:T(8,128)(2,1)S(1)}, bf16[288,512]{1,0:T(8,128)(2,1)S(1)}, u32[]{:S(2)}, u32[]{:S(2)}) collective-permute-start(bf16[288,512]{1,0:T(8,128)(2,1)S(1)} %broadcast_select_fusion.1), channel_id=1, source_target_pairs={{0,4},{4,8},{8,12},{12,14},{14,10},{10,6},{6,2},{2,0},{1,5},{5,9},... | collective-permute-start | bytes 884744 | tf_op jit(solution)/shard_map/ppermute | solution.py:359
  172.8 9.6 %collective-permute-start.28 = (bf16[288,512]{1,0:T(8,128)(2,1)S(1)}, bf16[288,512]{1,0:T(8,128)(2,1)}, u32[]{:S(2)}, u32[]{:S(2)}) collective-permute-start(bf16[288,512]{1,0:T(8,128)(2,1)S(1)} %broadcast_select_fusion), channel_id=1, source_target_pairs={{0,2},{4,0},{8,4},{12,8},{14,12},{10,14},{6,10},{2,6},{1,3},{5,1},... | collective-permute-start | bytes 884744 | tf_op jit(solution)/shard_map/ppermute | solution.py:359
  183.4 3.3 %collective-permute-start.29 = (bf16[288,512]{1,0:T(8,128)(2,1)S(1)}, bf16[288,512]{1,0:T(8,128)(2,1)S(1)}, u32[]{:S(2)}, u32[]{:S(2)}) collective-permute-start(bf16[288,512]{1,0:T(8,128)(2,1)S(1)} %select_select_fusion.mine), channel_id=1, source_target_pairs={{0,1},{1,0},{2,3},{3,2},{4,5},{5,4},{6,7},{7,6},{8,9},{9,8},{10,11... | collective-permute-start | bytes 884744 | tf_op jit(solution)/shard_map/ppermute | solution.py:362
  183.5 3.2 %copy-start = (bf16[512,2048]{1,0:T(8,128)(2,1)S(1)}, bf16[512,2048]{1,0:T(8,128)(2,1)}, u32[]{:S(2)}) copy-start(bf16[512,2048]{1,0:T(8,128)(2,1)} %get-tuple-element.185.hot_mine) | copy-start | bytes 6291460
  183.5 3.2 %copy-start.1 = (s32[3]{0:T(128)S(1)}, s32[3]{0:T(128)}, u32[]{:S(2)}) copy-start(s32[3]{0:T(128)} %pad_add_fusion.scal) | copy-start | bytes 40
  (5 other events, 6.6 us)

commit v9 on v8

--- a/solution.py
+++ b/solution.py
@@ -68,14 +68,13 @@
     return onehot, weight
 
 
-def step_kernel(steps, pieces, fanout, capacity, joined, scal, *refs):
+def step_kernel(steps, fanout, capacity, joined, scal, *refs):
     count = len(steps)
-    blocks, refs = refs[: max(count, 1 + joined)], refs[max(count, 1 + joined) :]
+    messages, cotangents, refs = refs[:count], refs[count : 2 * count], refs[2 * count :]
     if joined:
         first, refs = refs[0], refs[1:]
-        blocks = [jnp.concatenate([block[...] for block in blocks], axis=1)]
     weights_gu, weights_down, mine, pack, hot = refs[:5]
-    back, refs = refs[5 : 5 + count * pieces], refs[5 + count * pieces :]
+    back, refs = refs[5 : 5 + count], refs[5 + count :]
     if len(refs) > 7:
         turned, refs = refs[0], refs[1:]
     else:
@@ -87,9 +86,9 @@
     load_down = pltpu.make_async_copy(weights_down, down, sems.at[1])
     load_gu.start()
     load_down.start()
-    for at, block in enumerate(blocks):
+    for at, (message, cotangent) in enumerate(zip(messages, cotangents)):
         rows = slice(at * capacity, (at + 1) * capacity)
-        table = block[:, 2 * width :].astype(F32).T
+        table = message[:, width:].astype(F32).T
         own_hot, own_weight = selection(table, own, fanout, capacity)
         all_hot, all_weight = selection(table, hottest, fanout, capacity)
         scale = jnp.concatenate(
@@ -100,10 +99,10 @@
             axis=0,
         )
         onehot = jnp.concatenate([own_hot, all_hot], axis=0).astype(BF16)
-        picked = dot(onehot, block[:, :width], (1, 0)).astype(BF16)
+        picked = dot(onehot, message[:, :width], (1, 0)).astype(BF16)
         rows_in[rows, :] = picked[:capacity]
         hot_in[rows, :] = picked[capacity:]
-        picked = (scale * dot(onehot, block[:, width : 2 * width], (1, 0))).astype(BF16)
+        picked = (scale * dot(onehot, cotangent[...], (1, 0))).astype(BF16)
         rows_cot[rows, :] = picked[:capacity]
         hot_cot[rows, :] = picked[capacity:]
     part = width // 2
@@ -138,22 +137,21 @@
         turned[...] = grads.T
 
 
-def run_step(steps, fanout, capacity, scal, blocks, first, gate_up, down):
+def run_step(steps, fanout, capacity, scal, messages, cotangents, first, gate_up, down):
     count, rows = len(steps), len(steps) * capacity
     units, width = down.shape
     vmem = pl.BlockSpec(memory_space=pltpu.VMEM)
     far = pl.BlockSpec(memory_space=pl.ANY)
     shapes = [(rows, width), (rows, 3 * units + width), (rows, 2 * width)]
     joined = first is not None
-    pieces = 2 if joined else 1
-    shapes += [(capacity // pieces, width)] * (count * pieces)
+    shapes += [(capacity, width)] * count
     if joined or count > 1:
         shapes += [(3 * units, 2 * capacity)]
     firsts = [first] if joined else []
     out = pl.pallas_call(
-        functools.partial(step_kernel, steps, pieces, fanout, capacity, joined),
+        functools.partial(step_kernel, steps, fanout, capacity, joined),
         out_shape=[jax.ShapeDtypeStruct(shape, BF16) for shape in shapes],
-        in_specs=[pl.BlockSpec(memory_space=pltpu.SMEM)] + [vmem] * (len(blocks) + len(firsts)) + [far] * 2,
+        in_specs=[pl.BlockSpec(memory_space=pltpu.SMEM)] + [vmem] * (2 * count + len(firsts)) + [far] * 2,
         out_specs=[vmem] * len(shapes),
         scratch_shapes=[pltpu.VMEM((rows, width), BF16)] * 4
         + [
@@ -166,8 +164,8 @@
             flops=2 * 256 * 5 * width * units, bytes_accessed=3 * 2 * width * units, transcendentals=0
         ),
         name="expert_step",
-    )(scal, *blocks, *firsts, gate_up, down)
-    return out[:3], out[3 : 3 + count * pieces], out[3 + count * pieces :]
+    )(scal, *messages, *cotangents, *firsts, gate_up, down)
+    return out[:3], out[3 : 3 + count], out[3 + count :]
 
 
 def combine_kernel(experts, fanout, capacity, scal, meta, *refs):
@@ -239,10 +237,9 @@
     )(scal, *rows, *rows, *packs, *others)
 
 
-def message_kernel(fanout, tokens, cotangent, routes, route_weight, ratio, clip, message, meta):
+def message_kernel(fanout, tokens, routes, route_weight, ratio, clip, message, meta):
     count, width = tokens.shape
     message[:, :width] = tokens[...]
-    message[:, width : 2 * width] = cotangent[...]
     weight = route_weight[...] * ratio[...] * clip[...].astype(F32)
     first = weight.astype(BF16).astype(F32)
     rest = weight - first
@@ -255,24 +252,24 @@
             table = jnp.where(row == number * fanout + k, part[k : k + 1], table)
     table = jnp.concatenate([table, jnp.zeros((128 - lines, count), F32)], axis=0)
     columns = table.T.astype(BF16)
-    message[:, 2 * width :] = columns
+    message[:, width:] = columns
     meta[...] = columns
 
 
-def build_message(tokens, cotangent, routes, route_weight, ratio, clip):
+def build_message(tokens, routes, route_weight, ratio, clip):
     count, width = tokens.shape
     vmem = pl.BlockSpec(memory_space=pltpu.VMEM)
     return pl.pallas_call(
         functools.partial(message_kernel, routes.shape[1]),
         out_shape=[
-            jax.ShapeDtypeStruct((count, 2 * width + 128), BF16),
+            jax.ShapeDtypeStruct((count, width + 128), BF16),
             jax.ShapeDtypeStruct((count, 128), BF16),
         ],
-        in_specs=[vmem] * 6,
+        in_specs=[vmem] * 5,
         out_specs=[vmem] * 2,
-        cost_estimate=pl.CostEstimate(flops=0, bytes_accessed=8 * count * width, transcendentals=0),
+        cost_estimate=pl.CostEstimate(flops=0, bytes_accessed=4 * count * width, transcendentals=0),
         name="ring_message",
-    )(tokens, cotangent, routes.T, route_weight.T, ratio[None], clip[None])
+    )(tokens, routes.T, route_weight.T, ratio[None], clip[None])
 
 
 def order_kernel(plan, experts, capacity, scal, *refs):
@@ -364,19 +361,18 @@
     own = lax.axis_index("expert")
     hottest = shadow_plan[0]
     scal = jnp.stack([own, lax.axis_index("dp"), hottest]).astype(jnp.int32)
-    message, meta = build_message(
-        tokens, cotangent, routes, route_weight, ratio_advantage, clip_mask
-    )
+    message, meta = build_message(tokens, routes, route_weight, ratio_advantage, clip_mask)
 
     plan = distances(experts)
     mine, packs, hot, turned, late = [], [], [], [], []
     returned = {}
-    up, below, held = message, message, [message]
+    up, below, held = [message, cotangent], [message, cotangent], [[message], [cotangent]]
     for number, steps in enumerate(plan):
         if number + 1 < half:
-            following = [shift(up, 1), shift(below, -1)]
+            up, below = [shift(part, 1) for part in up], [shift(part, -1) for part in below]
+            following = [[up[0], below[0]], [up[1], below[1]]]
         elif number + 1 == half:
-            following = [shift(up[:, :width], 1), shift(below[:, width:], -1)]
+            following = [[shift(up[0], 1)], [shift(below[1], -1)]]
         if number > 1:
             sent, other = late[number - 2]
             held, other = lax.optimization_barrier((held, other))
@@ -388,13 +384,14 @@
             fanout,
             capacity,
             scal,
-            held,
+            *held,
             packs[0] if number == half else None,
             gate_up,
             down,
         )
-        following, back = lax.optimization_barrier((following, back))
-        steps = steps * (len(back) // len(steps))
+        following[1], back = lax.optimization_barrier((following[1], back))
+        if number + 1 < half:
+            up, below = [[part[k] for part in following] for k in range(2)]
         sent = [shift(part, step) if step else part for step, part in zip(steps, back)]
         late.append((sent, swap(pack)))
         mine.append(rows)
@@ -402,8 +399,6 @@
         hot.append(hot_rows)
         turned += turn
         held = following
-        if number < half:
-            up, below = following
     (back_behind, back_ahead), other = late[half - 1]
     turned[-1], late[half - 2] = lax.optimization_barrier((turned[-1], late[half - 2]))
 
@@ -424,24 +419,28 @@
     others = [part for _, part in late[: half - 1]] + [other, late[half][1]]
     expert_grad = expert_gradient(units, scal, mine, packs, others)
     chunks = [chunk(distance) for distance in range(1 - half, half)]
-    back_far = list(late[half][0])
+    (back_far,) = late[half][0]
     hot_mine, hot_theirs = ordered(plan, experts, capacity, scal, hot)
     for number in range(1, half):
         if number == 1:
-            around, expert_grad, back_ahead, back_behind, chunks = lax.optimization_barrier(
-                (around, expert_grad, back_ahead, back_behind, chunks)
+            around, expert_grad, back_ahead, back_behind, back_far, chunks = (
+                lax.optimization_barrier(
+                    (around, expert_grad, back_ahead, back_behind, back_far, chunks)
+                )
             )
             around = [jnp.concatenate([part, part], axis=1) for part in around]
-        if number == half - 2:
-            around, back_far[0] = lax.optimization_barrier((around, back_far[0]))
         if number == half - 1:
-            around, back_far[1], hot_mine, hot_theirs = lax.optimization_barrier(
-                (around, back_far[1], hot_mine, hot_theirs)
-            )
+            around, hot_mine, hot_theirs = lax.optimization_barrier((around, hot_mine, hot_theirs))
         ahead = jnp.where(is_hot, chunks[2 * half - 1 - number], around[0])
         behind = jnp.where(is_hot, chunks[number - 1], around[1])
         around = [shift(ahead, 1), shift(behind, -1)]
     hot_theirs = swap(hot_theirs)
+    sent = [rows for rows, _ in late[: half - 1]] + [[back_behind, back_ahead], [back_far]]
+    for steps, parts in zip(plan, sent):
+        for step, part in zip(steps, parts):
+            returned[step % experts] = part
+    token_grad = combine(experts, fanout, capacity, scal, meta, [returned[d] for d in range(experts)])
+    around, token_grad = lax.optimization_barrier((around, token_grad))
     away = (to_ring(own, experts) - ring_hot + experts) % experts
     lane = lax.broadcasted_iota(jnp.int32, far.shape, 1)
     reach = jnp.where(lane < lanes, half, half - 1)
@@ -451,13 +450,6 @@
     shadow_grad = shadow_gradient(
         experts, scal, columns, swap(columns), hot_mine, hot_theirs
     ).T
-    sent = [rows for rows, _ in late[: half - 1]] + [[back_behind, back_ahead]]
-    for steps, parts in zip(plan, sent):
-        for step, part in zip(steps, parts):
-            returned[step % experts] = [part]
-    returned[half] = back_far
-    rows = [part for distance in range(experts) for part in returned[distance]]
-    token_grad = combine(experts, fanout, capacity, scal, meta, rows)
     return (token_grad, expert_grad, shadow_grad)
 
 

time: 190 us -> 176 us (0.926)
  waiting for transfers between devices: 72 us -> 50.8 us
  starting transfers between devices: 34.7 us -> 45.4 us
  local copies, waits for them, and re-layouts: 6.51 us -> 3.63 us
    ppermute x24 -> x29, waiting for transfers between devices: 72 us -> 49.2 us  [shift(): return lax.ppermute(block, 'expert', pairs)]
    ppermute x24 -> x29, starting transfers between devices: 34.2 us -> 45.3 us  [shift(): return lax.ppermute(block, 'expert', pairs)]
    slice x2 -> x0, local copies, waits for them, and re-layouts: 2.17 us -> none  [on_device(): following = [shift(up[:, :width], 1), shift(below[:, width:], -1)]]
  transfers between devices with their start and end apart: 31 -> 36, of which waited for: 13 -> 12; matrix products, arithmetic and copies ran while one was open for 4% -> 3% of each run, Pallas kernels for 35% -> 39%
where the time goes in v9:
time: 176 us; the launch traced here: 175 us
  Pallas kernels  71.6 us (41%)
  waiting for transfers between devices  50.8 us (29%)
  starting transfers between devices  45.4 us (26%)
  local copies, waits for them, and re-layouts  3.63 us (2%)
  other arithmetic  2.29 us (1%)
  between operations  1.77 us (1%)
    ppermute x29, waiting for transfers between devices, shift(): return lax.ppermute(block, 'expert', pairs)  49.2 us
    pallas_call x5, Pallas kernels, run_step(): pl.pallas_call(functools.partial(step_kernel, steps, fanout, capacity, jo...  48.8 us
    ppermute x29, starting transfers between devices, shift(): return lax.ppermute(block, 'expert', pairs)  45.3 us
    pallas_call x1, Pallas kernels, expert_gradient(): pl.pallas_call(functools.partial(gradient_kernel, units, count), grid=(ti...  10.8 us
    pallas_call x1, Pallas kernels, ordered(): pl.pallas_call(functools.partial(order_kernel, plan, experts, capacity),...  4.49 us
  transfers between devices with their start and end apart: 36, of which 12 were waited for; matrix products, arithmetic and copies ran while one was open for 3% of the time, Pallas kernels for 39%

profile of v9, /device:TPU:0, one launch (start us, length us, event | category | flops | bytes accessed | tf_op | source)
XLA Modules:
  0.0 175.5 jit_solution(14586045881335797607)
XLA Ops:
  0.6 3.1 %collective-permute-start.2 = (bf16[128,2048]{1,0:T(8,128)(2,1)}, bf16[128,2048]{1,0:T(8,128)(2,1)S(1)}, u32[]{:S(2)}, u32[]{:S(2)}) collective-permute-start(bf16[128,2048]{1,0:T(8,128)(2,1)} %refs_1_.1), channel_id=1, source_target_pairs={{0,4},{4,8},{8,12},{12,14},{14,10},{10,6},{6,2},{2,0},{1,5},{5,9},... | collective-permute-start | bytes 1572872 | tf_op jit(solution)/shard_map/ppermute | solution.py:356
  3.7 2.0 %ring_message.1 = (bf16[128,2176]{1,0:T(8,128)(2,1)}, bf16[128,128]{1,0:T(8,128)(2,1)}) custom-call(bf16[128,2048]{1,0:T(8,128)(2,1)} %tokens.1, s32[2,128]{1,0:T(2,128)} %bitcast.17, f32[2,128]{1,0:T(2,128)} %bitcast.18, f32[1,128]{1,0:T(1,128)} %bitcast.19, s32[1,128]{1,0:T(1,128)} %bitcast.20), custom_call_target="tpu_custom_call" | custom-call | bytes 1048576 | tf_op jit(solution)/shard_map/ring_message/pallas_call | solution.py:262
  5.7 2.0 %collective-permute-start.1 = (bf16[128,2176]{1,0:T(8,128)(2,1)}, bf16[128,2176]{1,0:T(8,128)(2,1)S(1)}, u32[]{:S(2)}, u32[]{:S(2)}) collective-permute-start(bf16[128,2176]{1,0:T(8,128)(2,1)} %get-tuple-element.98.refs_0_), channel_id=1, source_target_pairs={{0,2},{4,0},{8,4},{12,8},{14,12},{10,14},{6,10},{2,6},{1,3},{5,1},... | collective-permute-start | bytes 1671176 | tf_op jit(solution)/shard_map/ppermute | solution.py:356
  8.4 0.7 pad_add_fusion.scal
  9.1 9.3 %expert_step.5 = (bf16[64,2048]{1,0:T(8,128)(2,1)}, bf16[64,4352]{1,0:T(8,128)(2,1)}, bf16[64,4096]{1,0:T(8,128)(2,1)}, bf16[64,2048]{1,0:T(8,128)(2,1)}) custom-call(s32[3]{0:T(128)} %pad_add_fusion.scal, bf16[128,2176]{1,0:T(8,128)(2,1)} %get-tuple-element.98.refs_0_, bf16[128,2048]{1,0:T(8,128)(2,1)} %refs_1_.1, bf16[2048,1536]{1,0:T(8,128)(2,1)} %bitcast.21, ...), custom_call_target="tpu_custom_call" | custom-call | flops 4026531840 | bytes 9437184 | tf_op jit(solution)/shard_map/expert_step/pallas_call | solution.py:151
  18.8 1.7 collective-permute-start.6
  20.8 9.9 %collective-permute-done.1.refs_1_ = bf16[128,2176]{1,0:T(8,128)(2,1)S(1)} collective-permute-done((bf16[128,2176]{1,0:T(8,128)(2,1)}, bf16[128,2176]{1,0:T(8,128)(2,1)S(1)}, u32[]{:S(2)}, u32[]{:S(2)}) %collective-permute-start.1) | collective-permute-done | bytes 557088 | tf_op jit(solution)/shard_map/ppermute | solution.py:356
  30.7 2.0 %collective-permute-start.4 = (bf16[128,2176]{1,0:T(8,128)(2,1)S(1)}, bf16[128,2176]{1,0:T(8,128)(2,1)}, u32[]{:S(2)}, u32[]{:S(2)}) collective-permute-start(bf16[128,2176]{1,0:T(8,128)(2,1)S(1)} %collective-permute-done.refs_0_), channel_id=1, source_target_pairs={{0,4},{4,8},{8,12},{12,14},{14,10},{10,6},{6,2},{2,0},{1,5},{5,9},... | collective-permute-start | bytes 1671176 | tf_op jit(solution)/shard_map/ppermute | solution.py:356
  32.8 9.8 %expert_step.6 = (bf16[128,2048]{1,0:T(8,128)(2,1)}, bf16[128,4352]{1,0:T(8,128)(2,1)}, bf16[128,4096]{1,0:T(8,128)(2,1)}, bf16[64,2048]{1,0:T(8,128)(2,1)}, bf1...) custom-call(s32[3]{0:T(128)} %pad_add_fusion.scal, bf16[128,2176]{1,0:T(8,128)(2,1)} %copy-done.16, ...), custom_call_target="tpu_custom_call" | custom-call | flops 4026531840 | bytes 9437184 | tf_op jit(solution)/shard_map/expert_step/pallas_call | solution.py:151
  42.7 1.6 collective-permute-start.11
  44.3 0.4 collective-permute-start.12
  44.8 9.2 %collective-permute-done.5.refs_1_ = bf16[128,2176]{1,0:T(8,128)(2,1)} collective-permute-done((bf16[128,2176]{1,0:T(8,128)(2,1)S(1)}, bf16[128,2176]{1,0:T(8,128)(2,1)}, u32[]{:S(2)}, u32[]{:S(2)}) %collective-permute-start.5) | collective-permute-done | bytes 557088 | tf_op jit(solution)/shard_map/ppermute | solution.py:356
  54.0 2.0 %collective-permute-start.9 = (bf16[128,2176]{1,0:T(8,128)(2,1)}, bf16[128,2176]{1,0:T(8,128)(2,1)}, u32[]{:S(2)}, u32[]{:S(2)}) collective-permute-start(bf16[128,2176]{1,0:T(8,128)(2,1)} %collective-permute-done.4.refs_0_), channel_id=1, source_target_pairs={{0,4},{4,8},{8,12},{12,14},{14,10},{10,6},{6,2},{2,0},{1,5},{5,9},... | collective-permute-start | bytes 1671176 | tf_op jit(solution)/shard_map/ppermute | solution.py:356
  56.0 9.8 %expert_step.7 = (bf16[128,2048]{1,0:T(8,128)(2,1)}, bf16[128,4352]{1,0:T(8,128)(2,1)}, bf16[128,4096]{1,0:T(8,128)(2,1)}, bf16[64,2048]{1,0:T(8,128)(2,1)}, bf1...) custom-call(s32[3]{0:T(128)} %pad_add_fusion.scal, bf16[128,2176]{1,0:T(8,128)(2,1)} %collective-permute-done.4.refs_0_, ...), custom_call_target="tpu_custom_call" | custom-call | flops 4026531840 | bytes 9437184 | tf_op jit(solution)/shard_map/expert_step/pallas_call | solution.py:151
  65.8 0.8 copy-done.18
  66.6 10.5 %collective-permute-done.10.refs_1_ = bf16[128,2176]{1,0:T(8,128)(2,1)} collective-permute-done((bf16[128,2176]{1,0:T(8,128)(2,1)}, bf16[128,2176]{1,0:T(8,128)(2,1)}, u32[]{:S(2)}, u32[]{:S(2)}) %collective-permute-start.10) | collective-permute-done | bytes 557088 | tf_op jit(solution)/shard_map/ppermute | solution.py:356
  77.2 1.6 collective-permute-start.15
  78.8 0.5 collective-permute-start.17
  79.3 1.6 collective-permute-start.16
  80.9 1.9 %collective-permute-done.14.refs_7_ = bf16[64,2048]{1,0:T(8,128)(2,1)} collective-permute-done((bf16[64,2048]{1,0:T(8,128)(2,1)}, bf16[64,2048]{1,0:T(8,128)(2,1)}, u32[]{:S(2)}, u32[]{:S(2)}) %collective-permute-start.14) | collective-permute-done | bytes 262176 | tf_op jit(solution)/shard_map/ppermute | solution.py:356
  82.8 1.4 collective-permute-start.19
  84.2 2.5 %collective-permute-done.15.refs_1_ = bf16[64,2048]{1,0:T(8,128)(2,1)} collective-permute-done((bf16[64,2048]{1,0:T(8,128)(2,1)}, bf16[64,2048]{1,0:T(8,128)(2,1)}, u32[]{:S(2)}, u32[]{:S(2)}) %collective-permute-start.15) | collective-permute-done | bytes 262176 | tf_op jit(solution)/shard_map/ppermute | solution.py:356
  86.7 2.6 %collective-permute-start.20 = (bf16[64,2048]{1,0:T(8,128)(2,1)}, bf16[64,2048]{1,0:T(8,128)(2,1)S(1)}, u32[]{:S(2)}, u32[]{:S(2)}) collective-permute-start(bf16[64,2048]{1,0:T(8,128)(2,1)} %get-tuple-element.140), channel_id=1, source_target_pairs={{0,8},{4,12},{8,14},{12,10},{14,6},{10,2},{6,0},{2,4},{1,9},{5,13}... | collective-permute-start | bytes 786440 | tf_op jit(solution)/shard_map/ppermute | solution.py:356
  89.3 9.8 %expert_step.8 = (bf16[128,2048]{1,0:T(8,128)(2,1)}, bf16[128,4352]{1,0:T(8,128)(2,1)}, bf16[128,4096]{1,0:T(8,128)(2,1)}, bf16[64,2048]{1,0:T(8,128)(2,1)}, bf1...) custom-call(s32[3]{0:T(128)} %pad_add_fusion.scal, bf16[128,2176]{1,0:T(8,128)(2,1)} %collective-permute-done.9.refs_0_, ...), custom_call_target="tpu_custom_call" | custom-call | flops 4026531840 | bytes 9437184 | tf_op jit(solution)/shard_map/expert_step/pallas_call | solution.py:151
  99.1 1.3 constant_dynamic-slice_fusion.1
  100.7 4.9 %collective-permute-start.25 = (bf16[64,2048]{1,0:T(8,128)(2,1)}, bf16[64,2048]{1,0:T(8,128)(2,1)S(1)}, u32[]{:S(2)}, u32[]{:S(2)}) collective-permute-start(bf16[64,2048]{1,0:T(8,128)(2,1)} %get-tuple-element.156), channel_id=1, source_target_pairs={{0,12},{4,14},{8,10},{12,6},{14,2},{10,0},{6,4},{2,8},{1,13},{5,15... | collective-permute-start | bytes 786440 | tf_op jit(solution)/shard_map/ppermute | solution.py:356
  105.6 10.1 %expert_step.9 = (bf16[64,2048]{1,0:T(8,128)(2,1)}, bf16[64,4352]{1,0:T(8,128)(2,1)}, bf16[64,4096]{1,0:T(8,128)(2,1)}, bf16[64,2048]{1,0:T(8,128)(2,1)}, bf16[2304,128]{1,0:T(8,128)(2,1)}) custom-call(s32[3]{0:T(128)} %pad_add_fusion.scal, bf16[128,2176]{1,0:T(8,128)(2,1)} %copy-done.17, bf16[128,2048]{1,0:T(8,128)(2,1)} %copy-done.19, ...), custom_call_target="tpu_custom_call" | custom-call | flops 4026531840 | bytes 9437184 | tf_op jit(solution)/shard_map/expert_step/pallas_call | solution.py:151
  115.7 0.8 collective-permute-start.27
  116.5 1.2 constant_dynamic-slice_fusion
  118.0 7.6 %collective-permute-start.22 = (bf16[288,256]{1,0:T(8,128)(2,1)S(1)}, bf16[288,256]{1,0:T(8,128)(2,1)S(1)}, u32[]{:S(2)}, u32[]{:S(2)}) collective-permute-start(bf16[288,256]{1,0:T(8,128)(2,1)S(1)} %get-tuple-element.144), channel_id=1, source_target_pairs={{0,4},{4,8},{8,12},{12,14},{14,10},{10,6},{6,2},{2,0},{1,5},{5,9},... | collective-permute-start | bytes 442376 | tf_op jit(solution)/shard_map/ppermute | solution.py:356
  125.6 4.8 %collective-permute-start.23 = (bf16[288,256]{1,0:T(8,128)(2,1)S(1)}, bf16[288,256]{1,0:T(8,128)(2,1)S(1)}, u32[]{:S(2)}, u32[]{:S(2)}) collective-permute-start(bf16[288,256]{1,0:T(8,128)(2,1)S(1)} %get-tuple-element.145), channel_id=1, source_target_pairs={{0,2},{4,0},{8,4},{12,8},{14,12},{10,14},{6,10},{2,6},{1,3},{5,1},... | collective-permute-start | bytes 442376 | tf_op jit(solution)/shard_map/ppermute | solution.py:356
  130.4 10.8 %expert_gradient.1 = f32[1,1024,2304]{2,1,0:T(8,128)} custom-call(s32[3]{0:T(128)} %pad_add_fusion.scal, bf16[64,2048]{1,0:T(8,128)(2,1)} %get-tuple-element.146.refs_0_.refs_10_, bf16[128,2048]{1,0:T(8,128)(2,1)} %get-tuple-element.147.refs_1_.refs_11_, bf16[128,2048]{1,0:T(8,128)(2,1)} %get-tuple-element.148.refs_2_.refs_12_, ...), custom_call_target="tpu_custom_call" | custom-call | flops 4831838208 | bytes 14155776 | tf_op jit(solution)/shard_map/expert_gradient/pallas_call | solution.py:226
  141.3 1.5 collective-permute-start.30
  142.9 0.6 collective-permute-start.28
  143.6 6.6 %collective-permute-done.30 = bf16[288,512]{1,0:T(8,128)(2,1)S(1)} collective-permute-done((bf16[288,512]{1,0:T(8,128)(2,1)S(1)}, bf16[288,512]{1,0:T(8,128)(2,1)S(1)}, u32[]{:S(2)}, u32[]{:S(2)}) %collective-permute-start.30) | collective-permute-done | bytes 294944 | tf_op jit(solution)/shard_map/ppermute | solution.py:356
  150.2 1.6 collective-permute-start.31
  151.9 0.5 collective-permute-start.29
  152.4 4.5 %hot_rows_ordered.1 = (bf16[512,2048]{1,0:T(8,128)(2,1)}, bf16[512,2048]{1,0:T(8,128)(2,1)}) custom-call(s32[3]{0:T(128)} %pad_add_fusion.scal, bf16[64,4096]{1,0:T(8,128)(2,1)} %get-tuple-element.167.refs_0_, bf16[128,4096]{1,0:T(8,128)(2,1)} %get-tuple-element.168.refs_1_, bf16[128,4096]{1,0:T(8,128)(2,1)} %get-tuple-element.169.refs_2_, ...), custom_call_target="tpu_custom_call" | custom-call | bytes 8388608 | tf_op jit(solution)/shard_map/hot_rows_ordered/pallas_call | solution.py:290
  156.9 1.3 collective-permute-done.31
  158.2 1.5 collective-permute-done.29
  159.7 1.4 collective-permute-start.33
  161.1 0.7 collective-permute-start.32
  161.8 3.2 %token_sum.1 = bf16[128,2048]{1,0:T(8,128)(2,1)} custom-call(s32[3]{0:T(128)} %pad_add_fusion.scal, bf16[128,128]{1,0:T(8,128)(2,1)} %get-tuple-element.177.meta, bf16[64,2048]{1,0:T(8,128)(2,1)} %get-tuple-element.178.refs_0_, bf16[64,2048]{1,0:T(8,128)(2,1)} %collective-permute-done.15.refs_1_, bf16[64,2048]{1,0:T(8,128)(2,1)} %copy-done.11, ...), custom_call_target="tpu_custom_call" | custom-call | flops 268435456 | bytes 2097152 | tf_op jit(solution)/shard_map/token_sum/pallas_call | solution.py:186
  165.0 4.1 %collective-permute-done.33 = bf16[288,512]{1,0:T(8,128)(2,1)S(1)} collective-permute-done((bf16[288,512]{1,0:T(8,128)(2,1)S(1)}, bf16[288,512]{1,0:T(8,128)(2,1)S(1)}, u32[]{:S(2)}, u32[]{:S(2)}) %collective-permute-start.33) | collective-permute-done | bytes 294944 | tf_op jit(solution)/shard_map/ppermute | solution.py:356
  169.1 1.3 collective-permute-done.32
  170.4 1.0 select_select_fusion.mine
  171.5 1.6 collective-permute-done.34.theirs
  173.1 2.4 %shadow_gradient.1 = f32[288,1024]{1,0:T(8,128)} custom-call(s32[3]{0:T(128)S(1)} %copy-done.1, bf16[288,512]{1,0:T(8,128)(2,1)S(1)} %select_select_fusion.mine, bf16[288,512]{1,0:T(8,128)(2,1)S(1)} %collective-permute-done.34.theirs, bf16[512,2048]{1,0:T(8,128)(2,1)S(1)} %copy-done, bf16[512,2048]{1,0:T(8,128)(2,1)S(1)} %collective-permute-done.35.hot_theirs), custom_call_target="tpu_custom_call" | custom-call | flops 603979776 | bytes 2097152 | tf_op jit(solution)/shard_map/shadow_gradient/pallas_call | solution.py:329
  (98 shorter events, 2.0 us)
Async XLA Ops:
  0.6 17.8 %collective-permute-start.2 = (bf16[128,2048]{1,0:T(8,128)(2,1)}, bf16[128,2048]{1,0:T(8,128)(2,1)S(1)}, u32[]{:S(2)}, u32[]{:S(2)}) collective-permute-start(bf16[128,2048]{1,0:T(8,128)(2,1)} %refs_1_.1), channel_id=1, source_target_pairs={{0,4},{4,8},{8,12},{12,14},{14,10},{10,6},{6,2},{2,0},{1,5},{5,9},... | collective-permute-start | bytes 1572872 | tf_op jit(solution)/shard_map/ppermute | solution.py:356
  3.7 15.1 %collective-permute-start.3 = (bf16[128,2048]{1,0:T(8,128)(2,1)}, bf16[128,2048]{1,0:T(8,128)(2,1)S(1)}, u32[]{:S(2)}, u32[]{:S(2)}) collective-permute-start(bf16[128,2048]{1,0:T(8,128)(2,1)} %refs_1_.1), channel_id=1, source_target_pairs={{0,2},{4,0},{8,4},{12,8},{14,12},{10,14},{6,10},{2,6},{1,3},{5,1},... | collective-permute-start | bytes 1572872 | tf_op jit(solution)/shard_map/ppermute | solution.py:356
  5.7 25.0 %collective-permute-start.1 = (bf16[128,2176]{1,0:T(8,128)(2,1)}, bf16[128,2176]{1,0:T(8,128)(2,1)S(1)}, u32[]{:S(2)}, u32[]{:S(2)}) collective-permute-start(bf16[128,2176]{1,0:T(8,128)(2,1)} %get-tuple-element.98.refs_0_), channel_id=1, source_target_pairs={{0,2},{4,0},{8,4},{12,8},{14,12},{10,14},{6,10},{2,6},{1,3},{5,1},... | collective-permute-start | bytes 1671176 | tf_op jit(solution)/shard_map/ppermute | solution.py:356
  7.7 23.0 %collective-permute-start = (bf16[128,2176]{1,0:T(8,128)(2,1)}, bf16[128,2176]{1,0:T(8,128)(2,1)S(1)}, u32[]{:S(2)}, u32[]{:S(2)}) collective-permute-start(bf16[128,2176]{1,0:T(8,128)(2,1)} %get-tuple-element.98.refs_0_), channel_id=1, source_target_pairs={{0,4},{4,8},{8,12},{12,14},{14,10},{10,6},{6,2},{2,0},{1,5},{5,9},... | collective-permute-start | bytes 1671176 | tf_op jit(solution)/shard_map/ppermute | solution.py:356
  18.4 14.3 %copy-start.22 = (bf16[128,2048]{1,0:T(8,128)(2,1)}, bf16[128,2048]{1,0:T(8,128)(2,1)S(1)}, u32[]{:S(2)}) copy-start(bf16[128,2048]{1,0:T(8,128)(2,1)S(1)} %collective-permute-done.2.refs_2_) | copy-start | bytes 1572868
  18.8 14.0 %copy-start.20 = (bf16[128,2048]{1,0:T(8,128)(2,1)}, bf16[128,2048]{1,0:T(8,128)(2,1)S(1)}, u32[]{:S(2)}) copy-start(bf16[128,2048]{1,0:T(8,128)(2,1)S(1)} %collective-permute-done.3.refs_3_) | copy-start | bytes 1572868
  18.8 23.8 %collective-permute-start.6 = (bf16[128,2048]{1,0:T(8,128)(2,1)S(1)}, bf16[128,2048]{1,0:T(8,128)(2,1)S(1)}, u32[]{:S(2)}, u32[]{:S(2)}) collective-permute-start(bf16[128,2048]{1,0:T(8,128)(2,1)S(1)} %collective-permute-done.2.refs_2_), channel_id=1, source_target_pairs={{0,4},{4,8},{8,12},{12,14},{14,10},{10,6},{6,2},{2,0},{1,5},{5,9},... | collective-permute-start | bytes 1572872 | tf_op jit(solution)/shard_map/ppermute | solution.py:356
  20.5 22.2 %collective-permute-start.7 = (bf16[128,2048]{1,0:T(8,128)(2,1)S(1)}, bf16[128,2048]{1,0:T(8,128)(2,1)}, u32[]{:S(2)}, u32[]{:S(2)}) collective-permute-start(bf16[128,2048]{1,0:T(8,128)(2,1)S(1)} %collective-permute-done.3.refs_3_), channel_id=1, source_target_pairs={{0,2},{4,0},{8,4},{12,8},{14,12},{10,14},{6,10},{2,6},{1,3},{5,1},... | collective-permute-start | bytes 1572872 | tf_op jit(solution)/shard_map/ppermute | solution.py:356
  20.8 23.5 %collective-permute-start.8 = (bf16[64,4352]{1,0:T(8,128)(2,1)}, bf16[64,4352]{1,0:T(8,128)(2,1)S(1)}, u32[]{:S(2)}, u32[]{:S(2)}) collective-permute-start(bf16[64,4352]{1,0:T(8,128)(2,1)} %get-tuple-element.107.refs_2_.refs_20_), channel_id=1, source_target_pairs={{0,1},{1,0},{2,3},{3,2},{4,5},{5,4},{6,7},{7,6},{8,9},{9,8},{10,11... | collective-permute-start | bytes 1671176 | tf_op jit(solution)/shard_map/ppermute | solution.py:359
  30.7 23.3 %collective-permute-start.5 = (bf16[128,2176]{1,0:T(8,128)(2,1)S(1)}, bf16[128,2176]{1,0:T(8,128)(2,1)}, u32[]{:S(2)}, u32[]{:S(2)}) collective-permute-start(bf16[128,2176]{1,0:T(8,128)(2,1)S(1)} %collective-permute-done.1.refs_1_), channel_id=1, source_target_pairs={{0,2},{4,0},{8,4},{12,8},{14,12},{10,14},{6,10},{2,6},{1,3},{5,1},... | collective-permute-start | bytes 1671176 | tf_op jit(solution)/shard_map/ppermute | solution.py:356
  30.7 23.3 %collective-permute-start.4 = (bf16[128,2176]{1,0:T(8,128)(2,1)S(1)}, bf16[128,2176]{1,0:T(8,128)(2,1)}, u32[]{:S(2)}, u32[]{:S(2)}) collective-permute-start(bf16[128,2176]{1,0:T(8,128)(2,1)S(1)} %collective-permute-done.refs_0_), channel_id=1, source_target_pairs={{0,4},{4,8},{8,12},{12,14},{14,10},{10,6},{6,2},{2,0},{1,5},{5,9},... | collective-permute-start | bytes 1671176 | tf_op jit(solution)/shard_map/ppermute | solution.py:356
  42.6 13.5 %copy-start.21 = (bf16[128,2048]{1,0:T(8,128)(2,1)}, bf16[128,2048]{1,0:T(8,128)(2,1)S(1)}, u32[]{:S(2)}) copy-start(bf16[128,2048]{1,0:T(8,128)(2,1)S(1)} %collective-permute-done.6.refs_2_) | copy-start | bytes 1572868
  42.6 36.7 %collective-permute-start.13 = (bf16[128,4352]{1,0:T(8,128)(2,1)}, bf16[128,4352]{1,0:T(8,128)(2,1)S(1)}, u32[]{:S(2)}, u32[]{:S(2)}) collective-permute-start(bf16[128,4352]{1,0:T(8,128)(2,1)} %get-tuple-element.117.refs_21_), channel_id=1, source_target_pairs={{0,1},{1,0},{2,3},{3,2},{4,5},{5,4},{6,7},{7,6},{8,9},{9,8},{10,11... | collective-permute-start | bytes 3342344 | tf_op jit(solution)/shard_map/ppermute | solution.py:359
  42.7 36.1 %copy-start.8 = (bf16[2304,128]{1,0:T(8,128)(2,1)S(1)}, bf16[2304,128]{1,0:T(8,128)(2,1)}, u32[]{:S(2)}) copy-start(bf16[2304,128]{1,0:T(8,128)(2,1)} %get-tuple-element.102) | copy-start | bytes 1769476
  42.7 23.2 %collective-permute-start.11 = (bf16[128,2048]{1,0:T(8,128)(2,1)S(1)}, bf16[128,2048]{1,0:T(8,128)(2,1)S(1)}, u32[]{:S(2)}, u32[]{:S(2)}) collective-permute-start(bf16[128,2048]{1,0:T(8,128)(2,1)S(1)} %collective-permute-done.6.refs_2_), channel_id=1, source_target_pairs={{0,4},{4,8},{8,12},{12,14},{14,10},{10,6},{6,2},{2,0},{1,5},{5,9},... | collective-permute-start | bytes 1572872 | tf_op jit(solution)/shard_map/ppermute | solution.py:356
  44.3 21.5 %copy-start.5 = (bf16[64,4352]{1,0:T(8,128)(2,1)}, bf16[64,4352]{1,0:T(8,128)(2,1)S(1)}, u32[]{:S(2)}) copy-start(bf16[64,4352]{1,0:T(8,128)(2,1)S(1)} %collective-permute-done.8.refs_5_.refs_15_.refs_25_) | copy-start | bytes 1671172
  44.3 22.3 %collective-permute-start.12 = (bf16[128,2048]{1,0:T(8,128)(2,1)}, bf16[128,2048]{1,0:T(8,128)(2,1)}, u32[]{:S(2)}, u32[]{:S(2)}) collective-permute-start(bf16[128,2048]{1,0:T(8,128)(2,1)} %collective-permute-done.7.refs_3_), channel_id=1, source_target_pairs={{0,2},{4,0},{8,4},{12,8},{14,12},{10,14},{6,10},{2,6},{1,3},{5,1},... | collective-permute-start | bytes 1572872 | tf_op jit(solution)/shard_map/ppermute | solution.py:356
  54.0 23.2 %collective-permute-start.10 = (bf16[128,2176]{1,0:T(8,128)(2,1)}, bf16[128,2176]{1,0:T(8,128)(2,1)}, u32[]{:S(2)}, u32[]{:S(2)}) collective-permute-start(bf16[128,2176]{1,0:T(8,128)(2,1)} %collective-permute-done.5.refs_1_), channel_id=1, source_target_pairs={{0,2},{4,0},{8,4},{12,8},{14,12},{10,14},{6,10},{2,6},{1,3},{5,1},... | collective-permute-start | bytes 1671176 | tf_op jit(solution)/shard_map/ppermute | solution.py:356
  54.0 24.8 %collective-permute-start.9 = (bf16[128,2176]{1,0:T(8,128)(2,1)}, bf16[128,2176]{1,0:T(8,128)(2,1)}, u32[]{:S(2)}, u32[]{:S(2)}) collective-permute-start(bf16[128,2176]{1,0:T(8,128)(2,1)} %collective-permute-done.4.refs_0_), channel_id=1, source_target_pairs={{0,4},{4,8},{8,12},{12,14},{14,10},{10,6},{6,2},{2,0},{1,5},{5,9},... | collective-permute-start | bytes 1671176 | tf_op jit(solution)/shard_map/ppermute | solution.py:356
  66.6 38.9 %collective-permute-start.18 = (bf16[128,4352]{1,0:T(8,128)(2,1)}, bf16[128,4352]{1,0:T(8,128)(2,1)S(1)}, u32[]{:S(2)}, u32[]{:S(2)}) collective-permute-start(bf16[128,4352]{1,0:T(8,128)(2,1)} %get-tuple-element.135.refs_22_), channel_id=1, source_target_pairs={{0,1},{1,0},{2,3},{3,2},{4,5},{5,4},{6,7},{7,6},{8,9},{9,8},{10,11... | collective-permute-start | bytes 3342344 | tf_op jit(solution)/shard_map/ppermute | solution.py:359
  66.6 16.1 %collective-permute-start.14 = (bf16[64,2048]{1,0:T(8,128)(2,1)}, bf16[64,2048]{1,0:T(8,128)(2,1)}, u32[]{:S(2)}, u32[]{:S(2)}) collective-permute-start(bf16[64,2048]{1,0:T(8,128)(2,1)} %get-tuple-element.124), channel_id=1, source_target_pairs={{0,2},{4,0},{8,4},{12,8},{14,12},{10,14},{6,10},{2,6},{1,3},{5,1},... | collective-permute-start | bytes 786440 | tf_op jit(solution)/shard_map/ppermute | solution.py:356
  77.2 9.6 %collective-permute-start.15 = (bf16[64,2048]{1,0:T(8,128)(2,1)}, bf16[64,2048]{1,0:T(8,128)(2,1)}, u32[]{:S(2)}, u32[]{:S(2)}) collective-permute-start(bf16[64,2048]{1,0:T(8,128)(2,1)} %get-tuple-element.125), channel_id=1, source_target_pairs={{0,4},{4,8},{8,12},{12,14},{14,10},{10,6},{6,2},{2,0},{1,5},{5,9},... | collective-permute-start | bytes 786440 | tf_op jit(solution)/shard_map/ppermute | solution.py:356
  78.8 21.6 %collective-permute-start.17 = (bf16[128,2048]{1,0:T(8,128)(2,1)}, bf16[128,2048]{1,0:T(8,128)(2,1)S(1)}, u32[]{:S(2)}, u32[]{:S(2)}) collective-permute-start(bf16[128,2048]{1,0:T(8,128)(2,1)} %collective-permute-done.12.refs_3_), channel_id=1, source_target_pairs={{0,2},{4,0},{8,4},{12,8},{14,12},{10,14},{6,10},{2,6},{1,3},{5,1},... | collective-permute-start | bytes 1572872 | tf_op jit(solution)/shard_map/ppermute | solution.py:356
  79.3 19.8 %copy-start.2 = (bf16[128,4352]{1,0:T(8,128)(2,1)}, bf16[128,4352]{1,0:T(8,128)(2,1)S(1)}, u32[]{:S(2)}) copy-start(bf16[128,4352]{1,0:T(8,128)(2,1)S(1)} %collective-permute-done.13.refs_6_.refs_16_.refs_26_) | copy-start | bytes 3342340
  79.3 21.4 %collective-permute-start.16 = (bf16[128,2176]{1,0:T(8,128)(2,1)}, bf16[128,2176]{1,0:T(8,128)(2,1)S(1)}, u32[]{:S(2)}, u32[]{:S(2)}) collective-permute-start(bf16[128,2176]{1,0:T(8,128)(2,1)} %collective-permute-done.9.refs_0_), channel_id=1, source_target_pairs={{0,4},{4,8},{8,12},{12,14},{14,10},{10,6},{6,2},{2,0},{1,5},{5,9},... | collective-permute-start | bytes 1671176 | tf_op jit(solution)/shard_map/ppermute | solution.py:356
  82.8 32.9 %collective-permute-start.19 = (bf16[64,2048]{1,0:T(8,128)(2,1)}, bf16[64,2048]{1,0:T(8,128)(2,1)S(1)}, u32[]{:S(2)}, u32[]{:S(2)}) collective-permute-start(bf16[64,2048]{1,0:T(8,128)(2,1)} %get-tuple-element.139), channel_id=1, source_target_pairs={{0,6},{4,2},{8,0},{12,4},{14,8},{10,12},{6,14},{2,10},{1,7},{5,3},... | collective-permute-start | bytes 786440 | tf_op jit(solution)/shard_map/ppermute | solution.py:356
  86.7 29.0 %collective-permute-start.20 = (bf16[64,2048]{1,0:T(8,128)(2,1)}, bf16[64,2048]{1,0:T(8,128)(2,1)S(1)}, u32[]{:S(2)}, u32[]{:S(2)}) collective-permute-start(bf16[64,2048]{1,0:T(8,128)(2,1)} %get-tuple-element.140), channel_id=1, source_target_pairs={{0,8},{4,12},{8,14},{12,10},{14,6},{10,2},{6,0},{2,4},{1,9},{5,13}... | collective-permute-start | bytes 786440 | tf_op jit(solution)/shard_map/ppermute | solution.py:356
  100.7 17.4 %collective-permute-start.21 = (bf16[128,4352]{1,0:T(8,128)(2,1)S(1)}, bf16[128,4352]{1,0:T(8,128)(2,1)S(1)}, u32[]{:S(2)}, u32[]{:S(2)}) collective-permute-start(bf16[128,4352]{1,0:T(8,128)(2,1)S(1)} %copy-done.7), channel_id=1, source_target_pairs={{0,1},{1,0},{2,3},{3,2},{4,5},{5,4},{6,7},{7,6},{8,9},{9,8},{10,11... | collective-permute-start | bytes 3342344 | tf_op jit(solution)/shard_map/ppermute | solution.py:359
  100.7 40.5 %collective-permute-start.25 = (bf16[64,2048]{1,0:T(8,128)(2,1)}, bf16[64,2048]{1,0:T(8,128)(2,1)S(1)}, u32[]{:S(2)}, u32[]{:S(2)}) collective-permute-start(bf16[64,2048]{1,0:T(8,128)(2,1)} %get-tuple-element.156), channel_id=1, source_target_pairs={{0,12},{4,14},{8,10},{12,6},{14,2},{10,0},{6,4},{2,8},{1,13},{5,15... | collective-permute-start | bytes 786440 | tf_op jit(solution)/shard_map/ppermute | solution.py:356
  105.5 10.1 %copy-start.3 = (bf16[128,4352]{1,0:T(8,128)(2,1)}, bf16[128,4352]{1,0:T(8,128)(2,1)S(1)}, u32[]{:S(2)}) copy-start(bf16[128,4352]{1,0:T(8,128)(2,1)S(1)} %collective-permute-done.18.refs_7_.refs_17_.refs_27_) | copy-start | bytes 3342340
  105.5 35.6 %collective-permute-start.26 = (bf16[64,2048]{1,0:T(8,128)(2,1)}, bf16[64,2048]{1,0:T(8,128)(2,1)S(1)}, u32[]{:S(2)}, u32[]{:S(2)}) collective-permute-start(bf16[64,2048]{1,0:T(8,128)(2,1)} %get-tuple-element.157), channel_id=1, source_target_pairs={{0,10},{4,6},{8,2},{12,0},{14,4},{10,8},{6,12},{2,14},{1,11},{5,7}... | collective-permute-start | bytes 786440 | tf_op jit(solution)/shard_map/ppermute | solution.py:356
  115.7 25.5 %collective-permute-start.27 = (bf16[64,2048]{1,0:T(8,128)(2,1)}, bf16[64,2048]{1,0:T(8,128)(2,1)S(1)}, u32[]{:S(2)}, u32[]{:S(2)}) collective-permute-start(bf16[64,2048]{1,0:T(8,128)(2,1)} %get-tuple-element.159), channel_id=1, source_target_pairs={{0,14},{4,10},{8,6},{12,2},{14,0},{10,4},{6,8},{2,12},{1,15},{5,11... | collective-permute-start | bytes 786440 | tf_op jit(solution)/shard_map/ppermute | solution.py:356
  116.5 9.1 %collective-permute-start.24 = (bf16[64,4352]{1,0:T(8,128)(2,1)}, bf16[64,4352]{1,0:T(8,128)(2,1)S(1)}, u32[]{:S(2)}, u32[]{:S(2)}) collective-permute-start(bf16[64,4352]{1,0:T(8,128)(2,1)} %get-tuple-element.155.refs_24_), channel_id=1, source_target_pairs={{0,1},{1,0},{2,3},{3,2},{4,5},{5,4},{6,7},{7,6},{8,9},{9,8},{10,11... | collective-permute-start | bytes 1671176 | tf_op jit(solution)/shard_map/ppermute | solution.py:359
  118.0 12.4 %copy-start.4 = (bf16[128,4352]{1,0:T(8,128)(2,1)}, bf16[128,4352]{1,0:T(8,128)(2,1)S(1)}, u32[]{:S(2)}) copy-start(bf16[128,4352]{1,0:T(8,128)(2,1)S(1)} %collective-permute-done.21.refs_8_.refs_18_.refs_28_) | copy-start | bytes 3342340
  118.0 23.2 %collective-permute-start.22 = (bf16[288,256]{1,0:T(8,128)(2,1)S(1)}, bf16[288,256]{1,0:T(8,128)(2,1)S(1)}, u32[]{:S(2)}, u32[]{:S(2)}) collective-permute-start(bf16[288,256]{1,0:T(8,128)(2,1)S(1)} %get-tuple-element.144), channel_id=1, source_target_pairs={{0,4},{4,8},{8,12},{12,14},{14,10},{10,6},{6,2},{2,0},{1,5},{5,9},... | collective-permute-start | bytes 442376 | tf_op jit(solution)/shard_map/ppermute | solution.py:356
  125.6 15.6 %collective-permute-start.23 = (bf16[288,256]{1,0:T(8,128)(2,1)S(1)}, bf16[288,256]{1,0:T(8,128)(2,1)S(1)}, u32[]{:S(2)}, u32[]{:S(2)}) collective-permute-start(bf16[288,256]{1,0:T(8,128)(2,1)S(1)} %get-tuple-element.145), channel_id=1, source_target_pairs={{0,2},{4,0},{8,4},{12,8},{14,12},{10,14},{6,10},{2,6},{1,3},{5,1},... | collective-permute-start | bytes 442376 | tf_op jit(solution)/shard_map/ppermute | solution.py:356
  141.2 9.0 %copy-start.12 = (bf16[64,2048]{1,0:T(8,128)(2,1)}, bf16[64,2048]{1,0:T(8,128)(2,1)S(1)}, u32[]{:S(2)}) copy-start(bf16[64,2048]{1,0:T(8,128)(2,1)S(1)} %collective-permute-done.25.refs_3_) | copy-start | bytes 786436
  141.2 9.0 %copy-start.13 = (bf16[64,2048]{1,0:T(8,128)(2,1)}, bf16[64,2048]{1,0:T(8,128)(2,1)S(1)}, u32[]{:S(2)}) copy-start(bf16[64,2048]{1,0:T(8,128)(2,1)S(1)} %collective-permute-done.26.refs_5_) | copy-start | bytes 786436
  141.2 9.0 %copy-start.14 = (bf16[64,2048]{1,0:T(8,128)(2,1)}, bf16[64,2048]{1,0:T(8,128)(2,1)S(1)}, u32[]{:S(2)}) copy-start(bf16[64,2048]{1,0:T(8,128)(2,1)S(1)} %collective-permute-done.27.refs_4_) | copy-start | bytes 786436
  141.3 8.8 %collective-permute-start.30 = (bf16[288,512]{1,0:T(8,128)(2,1)S(1)}, bf16[288,512]{1,0:T(8,128)(2,1)S(1)}, u32[]{:S(2)}, u32[]{:S(2)}) collective-permute-start(bf16[288,512]{1,0:T(8,128)(2,1)S(1)} %maximum_select_fusion.1), channel_id=1, source_target_pairs={{0,2},{4,0},{8,4},{12,8},{14,12},{10,14},{6,10},{2,6},{1,3},{5,1},... | collective-permute-start | bytes 884744 | tf_op jit(solution)/shard_map/ppermute | solution.py:356
  142.9 8.9 %collective-permute-start.28 = (bf16[288,512]{1,0:T(8,128)(2,1)S(1)}, bf16[288,512]{1,0:T(8,128)(2,1)S(1)}, u32[]{:S(2)}, u32[]{:S(2)}) collective-permute-start(bf16[288,512]{1,0:T(8,128)(2,1)S(1)} %maximum_select_fusion), channel_id=1, source_target_pairs={{0,4},{4,8},{8,12},{12,14},{14,10},{10,6},{6,2},{2,0},{1,5},{5,9},... | collective-permute-start | bytes 884744 | tf_op jit(solution)/shard_map/ppermute | solution.py:356
  150.2 7.9 %collective-permute-start.31 = (bf16[288,512]{1,0:T(8,128)(2,1)S(1)}, bf16[288,512]{1,0:T(8,128)(2,1)S(1)}, u32[]{:S(2)}, u32[]{:S(2)}) collective-permute-start(bf16[288,512]{1,0:T(8,128)(2,1)S(1)} %broadcast_select_fusion.2), channel_id=1, source_target_pairs={{0,2},{4,0},{8,4},{12,8},{14,12},{10,14},{6,10},{2,6},{1,3},{5,1},... | collective-permute-start | bytes 884744 | tf_op jit(solution)/shard_map/ppermute | solution.py:356
  151.9 7.8 %collective-permute-start.29 = (bf16[288,512]{1,0:T(8,128)(2,1)S(1)}, bf16[288,512]{1,0:T(8,128)(2,1)S(1)}, u32[]{:S(2)}, u32[]{:S(2)}) collective-permute-start(bf16[288,512]{1,0:T(8,128)(2,1)S(1)} %broadcast_select_fusion.3), channel_id=1, source_target_pairs={{0,4},{4,8},{8,12},{12,14},{14,10},{10,6},{6,2},{2,0},{1,5},{5,9},... | collective-permute-start | bytes 884744 | tf_op jit(solution)/shard_map/ppermute | solution.py:356
  159.6 13.5 %collective-permute-start.35 = (bf16[512,2048]{1,0:T(8,128)(2,1)}, bf16[512,2048]{1,0:T(8,128)(2,1)S(1)}, u32[]{:S(2)}, u32[]{:S(2)}) collective-permute-start(bf16[512,2048]{1,0:T(8,128)(2,1)} %get-tuple-element.192), channel_id=1, source_target_pairs={{0,1},{1,0},{2,3},{3,2},{4,5},{5,4},{6,7},{7,6},{8,9},{9,8},{10,11... | collective-permute-start | bytes 6291464 | tf_op jit(solution)/shard_map/ppermute | solution.py:359
  159.7 9.5 %collective-permute-start.33 = (bf16[288,512]{1,0:T(8,128)(2,1)S(1)}, bf16[288,512]{1,0:T(8,128)(2,1)S(1)}, u32[]{:S(2)}, u32[]{:S(2)}) collective-permute-start(bf16[288,512]{1,0:T(8,128)(2,1)S(1)} %broadcast_select_fusion), channel_id=1, source_target_pairs={{0,2},{4,0},{8,4},{12,8},{14,12},{10,14},{6,10},{2,6},{1,3},{5,1},... | collective-permute-start | bytes 884744 | tf_op jit(solution)/shard_map/ppermute | solution.py:356
  161.1 9.3 %collective-permute-start.32 = (bf16[288,512]{1,0:T(8,128)(2,1)S(1)}, bf16[288,512]{1,0:T(8,128)(2,1)}, u32[]{:S(2)}, u32[]{:S(2)}) collective-permute-start(bf16[288,512]{1,0:T(8,128)(2,1)S(1)} %broadcast_select_fusion.1), channel_id=1, source_target_pairs={{0,4},{4,8},{8,12},{12,14},{14,10},{10,6},{6,2},{2,0},{1,5},{5,9},... | collective-permute-start | bytes 884744 | tf_op jit(solution)/shard_map/ppermute | solution.py:356
  161.8 11.3 %copy-start = (bf16[512,2048]{1,0:T(8,128)(2,1)S(1)}, bf16[512,2048]{1,0:T(8,128)(2,1)}, u32[]{:S(2)}) copy-start(bf16[512,2048]{1,0:T(8,128)(2,1)} %get-tuple-element.191.hot_mine) | copy-start | bytes 6291460
  171.5 1.6 collective-permute-start.34
  (11 other events, 35.5 us)

commit v10 on v9

--- a/solution.py
+++ b/solution.py
@@ -68,13 +68,18 @@
     return onehot, weight
 
 
+def back_sections(capacity):
+    return [capacity // 2] * 2
+
+
 def step_kernel(steps, fanout, capacity, joined, scal, *refs):
     count = len(steps)
     messages, cotangents, refs = refs[:count], refs[count : 2 * count], refs[2 * count :]
     if joined:
         first, refs = refs[0], refs[1:]
     weights_gu, weights_down, mine, pack, hot = refs[:5]
-    back, refs = refs[5 : 5 + count], refs[5 + count :]
+    sections = len(back_sections(capacity)) if joined else count
+    back, refs = refs[5 : 5 + sections], refs[5 + sections :]
     if len(refs) > 7:
         turned, refs = refs[0], refs[1:]
     else:
@@ -128,8 +133,10 @@
     pack[:, units : 2 * units] = (hidden_grad * activation).astype(BF16)
     pack[:, 2 * units : 3 * units] = (activation * up_pre).astype(BF16)
     input_rows = dot(pack[:, : 2 * units], gate_up[...], (1, 1)).astype(BF16)
-    for at, part in enumerate(back):
-        part[...] = input_rows[at * part.shape[0] : (at + 1) * part.shape[0]]
+    at = 0
+    for part in back:
+        part[...] = input_rows[at : at + part.shape[0]]
+        at += part.shape[0]
     if turned is not None:
         grads = pack[:, : 3 * units]
         if joined:
@@ -144,7 +151,8 @@
     far = pl.BlockSpec(memory_space=pl.ANY)
     shapes = [(rows, width), (rows, 3 * units + width), (rows, 2 * width)]
     joined = first is not None
-    shapes += [(capacity, width)] * count
+    sections = back_sections(capacity) if first is not None else [capacity] * count
+    shapes += [(size, width) for size in sections]
     if joined or count > 1:
         shapes += [(3 * units, 2 * capacity)]
     firsts = [first] if joined else []
@@ -165,7 +173,7 @@
         ),
         name="expert_step",
     )(scal, *messages, *cotangents, *firsts, gate_up, down)
-    return out[:3], out[3 : 3 + count], out[3 + count :]
+    return out[:3], out[3 : 3 + len(sections)], out[3 + len(sections) :]
 
 
 def combine_kernel(experts, fanout, capacity, scal, meta, *refs):
@@ -373,12 +381,10 @@
             following = [[up[0], below[0]], [up[1], below[1]]]
         elif number + 1 == half:
             following = [[shift(up[0], 1)], [shift(below[1], -1)]]
-        if number > 1:
-            sent, other = late[number - 2]
+        if number > 2:
+            sent, other = late[number - 3]
             held, other = lax.optimization_barrier((held, other))
-            late[number - 2] = (sent, other)
-        if number == half - 1:
-            held, late[: half - 2] = lax.optimization_barrier((held, late[: half - 2]))
+            late[number - 3] = (sent, other)
         (rows, pack, hot_rows), back, turn = run_step(
             steps,
             fanout,
@@ -392,6 +398,7 @@
         following[1], back = lax.optimization_barrier((following[1], back))
         if number + 1 < half:
             up, below = [[part[k] for part in following] for k in range(2)]
+        steps = steps if number < half else steps * len(back)
         sent = [shift(part, step) if step else part for step, part in zip(steps, back)]
         late.append((sent, swap(pack)))
         mine.append(rows)
@@ -400,7 +407,7 @@
         turned += turn
         held = following
     (back_behind, back_ahead), other = late[half - 1]
-    turned[-1], late[half - 2] = lax.optimization_barrier((turned[-1], late[half - 2]))
+    turned[-1], late[: half - 1] = lax.optimization_barrier((turned[-1], late[: half - 1]))
 
     taken = 3 * units // experts
     ring_hot = to_ring(hottest, experts)
@@ -419,28 +426,31 @@
     others = [part for _, part in late[: half - 1]] + [other, late[half][1]]
     expert_grad = expert_gradient(units, scal, mine, packs, others)
     chunks = [chunk(distance) for distance in range(1 - half, half)]
-    (back_far,) = late[half][0]
+    back_far = list(late[half][0])
     hot_mine, hot_theirs = ordered(plan, experts, capacity, scal, hot)
     for number in range(1, half):
         if number == 1:
-            around, expert_grad, back_ahead, back_behind, back_far, chunks = (
-                lax.optimization_barrier(
-                    (around, expert_grad, back_ahead, back_behind, back_far, chunks)
-                )
+            around, expert_grad, back_ahead, back_behind, chunks = lax.optimization_barrier(
+                (around, expert_grad, back_ahead, back_behind, chunks)
             )
             around = [jnp.concatenate([part, part], axis=1) for part in around]
+        if number == 2:
+            around, back_far[0] = lax.optimization_barrier((around, back_far[0]))
         if number == half - 1:
-            around, hot_mine, hot_theirs = lax.optimization_barrier((around, hot_mine, hot_theirs))
+            around, back_far[1], hot_mine, hot_theirs = lax.optimization_barrier(
+                (around, back_far[1], hot_mine, hot_theirs)
+            )
         ahead = jnp.where(is_hot, chunks[2 * half - 1 - number], around[0])
         behind = jnp.where(is_hot, chunks[number - 1], around[1])
         around = [shift(ahead, 1), shift(behind, -1)]
     hot_theirs = swap(hot_theirs)
-    sent = [rows for rows, _ in late[: half - 1]] + [[back_behind, back_ahead], [back_far]]
+    sent = [rows for rows, _ in late[: half - 1]] + [[back_behind, back_ahead]]
     for steps, parts in zip(plan, sent):
         for step, part in zip(steps, parts):
-            returned[step % experts] = part
-    token_grad = combine(experts, fanout, capacity, scal, meta, [returned[d] for d in range(experts)])
-    around, token_grad = lax.optimization_barrier((around, token_grad))
+            returned[step % experts] = [part]
+    returned[half] = back_far
+    rows = [part for distance in range(experts) for part in returned[distance]]
+    token_grad = combine(experts, fanout, capacity, scal, meta, rows)
     away = (to_ring(own, experts) - ring_hot + experts) % experts
     lane = lax.broadcasted_iota(jnp.int32, far.shape, 1)
     reach = jnp.where(lane < lanes, half, half - 1)

time: 176 us -> 183 us (1.040)
  waiting for transfers between devices: 50.8 us -> 55.6 us
  starting transfers between devices: 45.4 us -> 47.5 us
    ppermute x29 -> x30, waiting for transfers between devices: 49.2 us -> 55.6 us  [shift(): return lax.ppermute(block, 'expert', pairs)]
    ppermute x29 -> x30, starting transfers between devices: 45.3 us -> 47 us  [shift(): return lax.ppermute(block, 'expert', pairs)]
  transfers between devices with their start and end apart: 36 -> 37, of which waited for: 12 -> 11; matrix products, arithmetic and copies ran while one was open for 3% -> 3% of each run, Pallas kernels for 39% -> 38%
where the time goes in v10:
time: 183 us
  Pallas kernels  71.3 us (39%)
  waiting for transfers between devices  55.6 us (30%)
  starting transfers between devices  47.5 us (26%)
  local copies, waits for them, and re-layouts  4.11 us (2%)
  other arithmetic  2.2 us (1%)
  between operations  1.91 us (1%)
    ppermute x30, waiting for transfers between devices, shift(): return lax.ppermute(block, 'expert', pairs)  55.6 us
    pallas_call x5, Pallas kernels, run_step(): pl.pallas_call(functools.partial(step_kernel, steps, fanout, capacity, jo...  48.5 us
    ppermute x30, starting transfers between devices, shift(): return lax.ppermute(block, 'expert', pairs)  47 us
    pallas_call x1, Pallas kernels, expert_gradient(): pl.pallas_call(functools.partial(gradient_kernel, units, count), grid=(ti...  10.7 us
    pallas_call x1, Pallas kernels, ordered(): pl.pallas_call(functools.partial(order_kernel, plan, experts, capacity),...  4.5 us
  transfers between devices with their start and end apart: 37, of which 11 were waited for; matrix products, arithmetic and copies ran while one was open for 3% of the time, Pallas kernels for 38%

profile of v10, /device:TPU:0, one launch (start us, length us, event | category | flops | bytes accessed | tf_op | source)
XLA Modules:
  0.0 182.6 jit_solution(8402295285080876136)
XLA Ops:
  0.6 3.1 %collective-permute-start.4 = (bf16[128,2048]{1,0:T(8,128)(2,1)}, bf16[128,2048]{1,0:T(8,128)(2,1)S(1)}, u32[]{:S(2)}, u32[]{:S(2)}) collective-permute-start(bf16[128,2048]{1,0:T(8,128)(2,1)} %refs_1_.1), channel_id=1, source_target_pairs={{0,4},{4,8},{8,12},{12,14},{14,10},{10,6},{6,2},{2,0},{1,5},{5,9},... | collective-permute-start | bytes 1572872 | tf_op jit(solution)/shard_map/ppermute | solution.py:364
  3.7 2.0 %ring_message.1 = (bf16[128,2176]{1,0:T(8,128)(2,1)}, bf16[128,128]{1,0:T(8,128)(2,1)}) custom-call(bf16[128,2048]{1,0:T(8,128)(2,1)} %tokens.1, s32[2,128]{1,0:T(2,128)} %bitcast.17, f32[2,128]{1,0:T(2,128)} %bitcast.18, f32[1,128]{1,0:T(1,128)} %bitcast.19, s32[1,128]{1,0:T(1,128)} %bitcast.20), custom_call_target="tpu_custom_call" | custom-call | bytes 1048576 | tf_op jit(solution)/shard_map/ring_message/pallas_call | solution.py:270
  5.7 2.0 %collective-permute-start.8 = (bf16[128,2176]{1,0:T(8,128)(2,1)}, bf16[128,2176]{1,0:T(8,128)(2,1)S(1)}, u32[]{:S(2)}, u32[]{:S(2)}) collective-permute-start(bf16[128,2176]{1,0:T(8,128)(2,1)} %get-tuple-element.92.refs_0_), channel_id=1, source_target_pairs={{0,2},{4,0},{8,4},{12,8},{14,12},{10,14},{6,10},{2,6},{1,3},{5,1},... | collective-permute-start | bytes 1671176 | tf_op jit(solution)/shard_map/ppermute | solution.py:364
  8.4 0.6 pad_add_fusion.scal
  9.0 9.3 %expert_step.5 = (bf16[64,2048]{1,0:T(8,128)(2,1)}, bf16[64,4352]{1,0:T(8,128)(2,1)}, bf16[64,4096]{1,0:T(8,128)(2,1)}, bf16[64,2048]{1,0:T(8,128)(2,1)}) custom-call(s32[3]{0:T(128)} %pad_add_fusion.scal, bf16[128,2176]{1,0:T(8,128)(2,1)} %get-tuple-element.92.refs_0_, bf16[128,2048]{1,0:T(8,128)(2,1)} %refs_1_.1, bf16[2048,1536]{1,0:T(8,128)(2,1)} %bitcast.21, ...), custom_call_target="tpu_custom_call" | custom-call | flops 4026531840 | bytes 9437184 | tf_op jit(solution)/shard_map/expert_step/pallas_call | solution.py:159
  18.4 0.5 collective-permute-done.5.refs_3_
  18.9 1.6 collective-permute-start.6
  20.5 0.4 collective-permute-start.7
  20.9 9.8 %collective-permute-done.8.refs_1_ = bf16[128,2176]{1,0:T(8,128)(2,1)S(1)} collective-permute-done((bf16[128,2176]{1,0:T(8,128)(2,1)}, bf16[128,2176]{1,0:T(8,128)(2,1)S(1)}, u32[]{:S(2)}, u32[]{:S(2)}) %collective-permute-start.8) | collective-permute-done | bytes 557088 | tf_op jit(solution)/shard_map/ppermute | solution.py:364
  30.7 2.0 %collective-permute-start.1 = (bf16[128,2176]{1,0:T(8,128)(2,1)S(1)}, bf16[128,2176]{1,0:T(8,128)(2,1)S(1)}, u32[]{:S(2)}, u32[]{:S(2)}) collective-permute-start(bf16[128,2176]{1,0:T(8,128)(2,1)S(1)} %collective-permute-done.refs_0_), channel_id=1, source_target_pairs={{0,4},{4,8},{8,12},{12,14},{14,10},{10,6},{6,2},{2,0},{1,5},{5,9},... | collective-permute-start | bytes 1671176 | tf_op jit(solution)/shard_map/ppermute | solution.py:364
  32.7 9.8 %expert_step.6 = (bf16[128,2048]{1,0:T(8,128)(2,1)}, bf16[128,4352]{1,0:T(8,128)(2,1)}, bf16[128,4096]{1,0:T(8,128)(2,1)}, bf16[64,2048]{1,0:T(8,128)(2,1)}, bf1...) custom-call(s32[3]{0:T(128)} %pad_add_fusion.scal, bf16[128,2176]{1,0:T(8,128)(2,1)} %copy-done.22, ...), custom_call_target="tpu_custom_call" | custom-call | flops 4026531840 | bytes 9437184 | tf_op jit(solution)/shard_map/expert_step/pallas_call | solution.py:159
  42.6 1.6 collective-permute-start.9
  44.2 0.5 collective-permute-start.10
  44.7 7.1 %collective-permute-done.1.refs_0_ = bf16[128,2176]{1,0:T(8,128)(2,1)S(1)} collective-permute-done((bf16[128,2176]{1,0:T(8,128)(2,1)S(1)}, bf16[128,2176]{1,0:T(8,128)(2,1)S(1)}, u32[]{:S(2)}, u32[]{:S(2)}) %collective-permute-start.1) | collective-permute-done | bytes 557088 | tf_op jit(solution)/shard_map/ppermute | solution.py:364
  51.7 2.1 %collective-permute-start.2 = (bf16[128,2176]{1,0:T(8,128)(2,1)S(1)}, bf16[128,2176]{1,0:T(8,128)(2,1)}, u32[]{:S(2)}, u32[]{:S(2)}) collective-permute-start(bf16[128,2176]{1,0:T(8,128)(2,1)S(1)} %collective-permute-done.1.refs_0_), channel_id=1, source_target_pairs={{0,4},{4,8},{8,12},{12,14},{14,10},{10,6},{6,2},{2,0},{1,5},{5,9},... | collective-permute-start | bytes 1671176 | tf_op jit(solution)/shard_map/ppermute | solution.py:364
  53.9 9.2 %collective-permute-done.9.refs_2_ = bf16[128,2048]{1,0:T(8,128)(2,1)} collective-permute-done((bf16[128,2048]{1,0:T(8,128)(2,1)}, bf16[128,2048]{1,0:T(8,128)(2,1)}, u32[]{:S(2)}, u32[]{:S(2)}) %collective-permute-start.9) | collective-permute-done | bytes 524320 | tf_op jit(solution)/shard_map/ppermute | solution.py:364
  63.1 2.1 %collective-permute-start.13 = (bf16[128,2176]{1,0:T(8,128)(2,1)S(1)}, bf16[128,2176]{1,0:T(8,128)(2,1)S(1)}, u32[]{:S(2)}, u32[]{:S(2)}) collective-permute-start(bf16[128,2176]{1,0:T(8,128)(2,1)S(1)} %collective-permute-done.11.refs_1_), channel_id=1, source_target_pairs={{0,2},{4,0},{8,4},{12,8},{14,12},{10,14},{6,10},{2,6},{1,3},{5,1},... | collective-permute-start | bytes 1671176 | tf_op jit(solution)/shard_map/ppermute | solution.py:364
  65.1 9.8 %expert_step.7 = (bf16[128,2048]{1,0:T(8,128)(2,1)}, bf16[128,4352]{1,0:T(8,128)(2,1)}, bf16[128,4096]{1,0:T(8,128)(2,1)}, bf16[64,2048]{1,0:T(8,128)(2,1)}, bf1...) custom-call(s32[3]{0:T(128)} %pad_add_fusion.scal, bf16[128,2176]{1,0:T(8,128)(2,1)} %copy-done.21, ...), custom_call_target="tpu_custom_call" | custom-call | flops 4026531840 | bytes 9437184 | tf_op jit(solution)/shard_map/expert_step/pallas_call | solution.py:159
  75.2 1.6 collective-permute-start.12
  76.8 0.4 collective-permute-start.3
  77.3 1.6 collective-permute-start.16
  79.0 9.8 %expert_step.8 = (bf16[128,2048]{1,0:T(8,128)(2,1)}, bf16[128,4352]{1,0:T(8,128)(2,1)}, bf16[128,4096]{1,0:T(8,128)(2,1)}, bf16[64,2048]{1,0:T(8,128)(2,1)}, bf1...) custom-call(s32[3]{0:T(128)} %pad_add_fusion.scal, bf16[128,2176]{1,0:T(8,128)(2,1)} %collective-permute-done.2.refs_0_, ...), custom_call_target="tpu_custom_call" | custom-call | flops 4026531840 | bytes 9437184 | tf_op jit(solution)/shard_map/expert_step/pallas_call | solution.py:159
  88.8 1.3 constant_dynamic-slice_fusion.1
  90.2 0.4 collective-permute-start.17
  90.6 0.4 copy-done.25
  91.0 2.6 %collective-permute-start.18 = (bf16[64,2048]{1,0:T(8,128)(2,1)}, bf16[64,2048]{1,0:T(8,128)(2,1)S(1)}, u32[]{:S(2)}, u32[]{:S(2)}) collective-permute-start(bf16[64,2048]{1,0:T(8,128)(2,1)} %get-tuple-element.121), channel_id=1, source_target_pairs={{0,6},{4,2},{8,0},{12,4},{14,8},{10,12},{6,14},{2,10},{1,7},{5,3},... | collective-permute-start | bytes 786440 | tf_op jit(solution)/shard_map/ppermute | solution.py:364
  93.6 0.3 collective-permute-start.19
  93.9 3.2 %collective-permute-done.16.refs_8_ = bf16[64,2048]{1,0:T(8,128)(2,1)S(1)} collective-permute-done((bf16[64,2048]{1,0:T(8,128)(2,1)}, bf16[64,2048]{1,0:T(8,128)(2,1)S(1)}, u32[]{:S(2)}, u32[]{:S(2)}) %collective-permute-start.16) | collective-permute-done | bytes 262176 | tf_op jit(solution)/shard_map/ppermute | solution.py:364
  97.1 9.7 %expert_step.9 = (bf16[64,2048]{1,0:T(8,128)(2,1)}, bf16[64,4352]{1,0:T(8,128)(2,1)}, bf16[64,4096]{1,0:T(8,128)(2,1)}, bf16[32,2048]{1,0:T(8,128)(2,1)}, bf16[3...) custom-call(s32[3]{0:T(128)} %pad_add_fusion.scal, bf16[128,2176]{1,0:T(8,128)(2,1)} %copy-done.23, ...), custom_call_target="tpu_custom_call" | custom-call | flops 4026531840 | bytes 9437184 | tf_op jit(solution)/shard_map/expert_step/pallas_call | solution.py:159
  106.9 0.9 collective-permute-start.25
  107.8 7.4 %collective-permute-start.26 = (bf16[64,2048]{1,0:T(8,128)(2,1)}, bf16[64,2048]{1,0:T(8,128)(2,1)S(1)}, u32[]{:S(2)}, u32[]{:S(2)}) collective-permute-start(bf16[64,2048]{1,0:T(8,128)(2,1)} %get-tuple-element.145), channel_id=1, source_target_pairs={{0,10},{4,6},{8,2},{12,0},{14,4},{10,8},{6,12},{2,14},{1,11},{5,7}... | collective-permute-start | bytes 786440 | tf_op jit(solution)/shard_map/ppermute | solution.py:364
  115.4 1.4 constant_dynamic-slice_fusion
  117.3 2.0 %collective-permute-start.23 = (bf16[288,256]{1,0:T(8,128)(2,1)S(1)}, bf16[288,256]{1,0:T(8,128)(2,1)S(1)}, u32[]{:S(2)}, u32[]{:S(2)}) collective-permute-start(bf16[288,256]{1,0:T(8,128)(2,1)S(1)} %get-tuple-element.133), channel_id=1, source_target_pairs={{0,2},{4,0},{8,4},{12,8},{14,12},{10,14},{6,10},{2,6},{1,3},{5,1},... | collective-permute-start | bytes 442376 | tf_op jit(solution)/shard_map/ppermute | solution.py:364
  119.3 0.8 copy-done.6
  120.1 10.7 %expert_gradient.1 = f32[1,1024,2304]{2,1,0:T(8,128)} custom-call(s32[3]{0:T(128)} %pad_add_fusion.scal, bf16[64,2048]{1,0:T(8,128)(2,1)} %get-tuple-element.134.refs_0_.refs_10_, bf16[128,2048]{1,0:T(8,128)(2,1)} %get-tuple-element.135.refs_1_.refs_11_, bf16[128,2048]{1,0:T(8,128)(2,1)} %get-tuple-element.136.refs_2_.refs_12_, ...), custom_call_target="tpu_custom_call" | custom-call | flops 4831838208 | bytes 14155776 | tf_op jit(solution)/shard_map/expert_gradient/pallas_call | solution.py:234
  130.9 3.4 %collective-permute-done.23 = bf16[288,256]{1,0:T(8,128)(2,1)S(1)} collective-permute-done((bf16[288,256]{1,0:T(8,128)(2,1)S(1)}, bf16[288,256]{1,0:T(8,128)(2,1)S(1)}, u32[]{:S(2)}, u32[]{:S(2)}) %collective-permute-start.23) | collective-permute-done | bytes 147488 | tf_op jit(solution)/shard_map/ppermute | solution.py:364
  134.9 2.3 %collective-permute-start.27 = (bf16[288,512]{1,0:T(8,128)(2,1)S(1)}, bf16[288,512]{1,0:T(8,128)(2,1)S(1)}, u32[]{:S(2)}, u32[]{:S(2)}) collective-permute-start(bf16[288,512]{1,0:T(8,128)(2,1)S(1)} %maximum_select_fusion), channel_id=1, source_target_pairs={{0,4},{4,8},{8,12},{12,14},{14,10},{10,6},{6,2},{2,0},{1,5},{5,9},... | collective-permute-start | bytes 884744 | tf_op jit(solution)/shard_map/ppermute | solution.py:364
  137.1 9.3 %collective-permute-done.29.refs_4_ = bf16[32,2048]{1,0:T(8,128)(2,1)S(1)} collective-permute-done((bf16[32,2048]{1,0:T(8,128)(2,1)S(1)}, bf16[32,2048]{1,0:T(8,128)(2,1)S(1)}, u32[]{:S(2)}, u32[]{:S(2)}) %collective-permute-start.29) | collective-permute-done | bytes 131104 | tf_op jit(solution)/shard_map/ppermute | solution.py:364
  146.5 4.9 %collective-permute-start.30 = (bf16[288,512]{1,0:T(8,128)(2,1)S(1)}, bf16[288,512]{1,0:T(8,128)(2,1)S(1)}, u32[]{:S(2)}, u32[]{:S(2)}) collective-permute-start(bf16[288,512]{1,0:T(8,128)(2,1)S(1)} %broadcast_select_fusion.3), channel_id=1, source_target_pairs={{0,4},{4,8},{8,12},{12,14},{14,10},{10,6},{6,2},{2,0},{1,5},{5,9},... | collective-permute-start | bytes 884744 | tf_op jit(solution)/shard_map/ppermute | solution.py:364
  151.5 4.4 %collective-permute-start.32 = (bf16[32,2048]{1,0:T(8,128)(2,1)S(1)}, bf16[32,2048]{1,0:T(8,128)(2,1)S(1)}, u32[]{:S(2)}, u32[]{:S(2)}) collective-permute-start(bf16[32,2048]{1,0:T(8,128)(2,1)S(1)} %copy-done.27), channel_id=1, source_target_pairs={{0,14},{4,10},{8,6},{12,2},{14,0},{10,4},{6,8},{2,12},{1,15},{5,11... | collective-permute-start | bytes 393224 | tf_op jit(solution)/shard_map/ppermute | solution.py:364
  155.9 4.5 %hot_rows_ordered.1 = (bf16[512,2048]{1,0:T(8,128)(2,1)}, bf16[512,2048]{1,0:T(8,128)(2,1)}) custom-call(s32[3]{0:T(128)} %pad_add_fusion.scal, bf16[64,4096]{1,0:T(8,128)(2,1)} %get-tuple-element.160.refs_0_, bf16[128,4096]{1,0:T(8,128)(2,1)} %get-tuple-element.161.refs_1_, bf16[128,4096]{1,0:T(8,128)(2,1)} %get-tuple-element.162.refs_2_, ...), custom_call_target="tpu_custom_call" | custom-call | bytes 8388608 | tf_op jit(solution)/shard_map/hot_rows_ordered/pallas_call | solution.py:298
  160.4 3.7 %collective-permute-done.32.refs_5_ = bf16[32,2048]{1,0:T(8,128)(2,1)S(1)} collective-permute-done((bf16[32,2048]{1,0:T(8,128)(2,1)S(1)}, bf16[32,2048]{1,0:T(8,128)(2,1)S(1)}, u32[]{:S(2)}, u32[]{:S(2)}) %collective-permute-start.32) | collective-permute-done | bytes 131104 | tf_op jit(solution)/shard_map/ppermute | solution.py:364
  164.2 2.3 %collective-permute-start.33 = (bf16[288,512]{1,0:T(8,128)(2,1)S(1)}, bf16[288,512]{1,0:T(8,128)(2,1)S(1)}, u32[]{:S(2)}, u32[]{:S(2)}) collective-permute-start(bf16[288,512]{1,0:T(8,128)(2,1)S(1)} %broadcast_select_fusion.1), channel_id=1, source_target_pairs={{0,4},{4,8},{8,12},{12,14},{14,10},{10,6},{6,2},{2,0},{1,5},{5,9},... | collective-permute-start | bytes 884744 | tf_op jit(solution)/shard_map/ppermute | solution.py:364
  166.7 7.0 %collective-permute-done.33 = bf16[288,512]{1,0:T(8,128)(2,1)S(1)} collective-permute-done((bf16[288,512]{1,0:T(8,128)(2,1)S(1)}, bf16[288,512]{1,0:T(8,128)(2,1)S(1)}, u32[]{:S(2)}, u32[]{:S(2)}) %collective-permute-start.33) | collective-permute-done | bytes 294944 | tf_op jit(solution)/shard_map/ppermute | solution.py:364
  173.7 2.3 %collective-permute-done.34 = bf16[288,512]{1,0:T(8,128)(2,1)} collective-permute-done((bf16[288,512]{1,0:T(8,128)(2,1)S(1)}, bf16[288,512]{1,0:T(8,128)(2,1)}, u32[]{:S(2)}, u32[]{:S(2)}) %collective-permute-start.34) | collective-permute-done | bytes 294944 | tf_op jit(solution)/shard_map/ppermute | solution.py:364
  175.9 1.0 select_select_fusion.mine
  177.1 3.2 %token_sum.1 = bf16[128,2048]{1,0:T(8,128)(2,1)} custom-call(s32[3]{0:T(128)} %pad_add_fusion.scal, bf16[128,128]{1,0:T(8,128)(2,1)} %get-tuple-element.91.meta, bf16[64,2048]{1,0:T(8,128)(2,1)} %get-tuple-element.124.refs_0_, bf16[64,2048]{1,0:T(8,128)(2,1)} %copy-done.12, bf16[64,2048]{1,0:T(8,128)(2,1)} %copy-done.14, bf16[64,2048]{1,0:T(8,128)(2,1)} %copy-done.15, ...), custom_call_target="tpu_custom_call" | custom-call | flops 268435456 | bytes 2097152 | tf_op jit(solution)/shard_map/token_sum/pallas_call | solution.py:194
  180.2 2.3 %shadow_gradient.1 = f32[288,1024]{1,0:T(8,128)} custom-call(s32[3]{0:T(128)S(1)} %copy-done.1, bf16[288,512]{1,0:T(8,128)(2,1)S(1)} %select_select_fusion.mine, bf16[288,512]{1,0:T(8,128)(2,1)S(1)} %collective-permute-done.35.theirs, bf16[512,2048]{1,0:T(8,128)(2,1)S(1)} %copy-done, bf16[512,2048]{1,0:T(8,128)(2,1)S(1)} %collective-permute-done.36.hot_theirs), custom_call_target="tpu_custom_call" | custom-call | flops 603979776 | bytes 2097152 | tf_op jit(solution)/shard_map/shadow_gradient/pallas_call | solution.py:337
  (112 shorter events, 2.0 us)
Async XLA Ops:
  0.6 17.7 %collective-permute-start.4 = (bf16[128,2048]{1,0:T(8,128)(2,1)}, bf16[128,2048]{1,0:T(8,128)(2,1)S(1)}, u32[]{:S(2)}, u32[]{:S(2)}) collective-permute-start(bf16[128,2048]{1,0:T(8,128)(2,1)} %refs_1_.1), channel_id=1, source_target_pairs={{0,4},{4,8},{8,12},{12,14},{14,10},{10,6},{6,2},{2,0},{1,5},{5,9},... | collective-permute-start | bytes 1572872 | tf_op jit(solution)/shard_map/ppermute | solution.py:364
  3.7 15.2 %collective-permute-start.5 = (bf16[128,2048]{1,0:T(8,128)(2,1)}, bf16[128,2048]{1,0:T(8,128)(2,1)}, u32[]{:S(2)}, u32[]{:S(2)}) collective-permute-start(bf16[128,2048]{1,0:T(8,128)(2,1)} %refs_1_.1), channel_id=1, source_target_pairs={{0,2},{4,0},{8,4},{12,8},{14,12},{10,14},{6,10},{2,6},{1,3},{5,1},... | collective-permute-start | bytes 1572872 | tf_op jit(solution)/shard_map/ppermute | solution.py:364
  5.7 25.0 %collective-permute-start.8 = (bf16[128,2176]{1,0:T(8,128)(2,1)}, bf16[128,2176]{1,0:T(8,128)(2,1)S(1)}, u32[]{:S(2)}, u32[]{:S(2)}) collective-permute-start(bf16[128,2176]{1,0:T(8,128)(2,1)} %get-tuple-element.92.refs_0_), channel_id=1, source_target_pairs={{0,2},{4,0},{8,4},{12,8},{14,12},{10,14},{6,10},{2,6},{1,3},{5,1},... | collective-permute-start | bytes 1671176 | tf_op jit(solution)/shard_map/ppermute | solution.py:364
  7.7 23.0 %collective-permute-start = (bf16[128,2176]{1,0:T(8,128)(2,1)}, bf16[128,2176]{1,0:T(8,128)(2,1)S(1)}, u32[]{:S(2)}, u32[]{:S(2)}) collective-permute-start(bf16[128,2176]{1,0:T(8,128)(2,1)} %get-tuple-element.92.refs_0_), channel_id=1, source_target_pairs={{0,4},{4,8},{8,12},{12,14},{14,10},{10,6},{6,2},{2,0},{1,5},{5,9},... | collective-permute-start | bytes 1671176 | tf_op jit(solution)/shard_map/ppermute | solution.py:364
  18.4 14.4 %copy-start.26 = (bf16[128,2048]{1,0:T(8,128)(2,1)}, bf16[128,2048]{1,0:T(8,128)(2,1)S(1)}, u32[]{:S(2)}) copy-start(bf16[128,2048]{1,0:T(8,128)(2,1)S(1)} %collective-permute-done.4.refs_2_) | copy-start | bytes 1572868
  18.9 25.8 %copy-start.10 = (bf16[64,4352]{1,0:T(8,128)(2,1)S(1)}, bf16[64,4352]{1,0:T(8,128)(2,1)}, u32[]{:S(2)}) copy-start(bf16[64,4352]{1,0:T(8,128)(2,1)} %get-tuple-element.104.refs_2_.refs_20_) | copy-start | bytes 1671172
  18.9 23.7 %collective-permute-start.6 = (bf16[128,2048]{1,0:T(8,128)(2,1)S(1)}, bf16[128,2048]{1,0:T(8,128)(2,1)}, u32[]{:S(2)}, u32[]{:S(2)}) collective-permute-start(bf16[128,2048]{1,0:T(8,128)(2,1)S(1)} %collective-permute-done.4.refs_2_), channel_id=1, source_target_pairs={{0,4},{4,8},{8,12},{12,14},{14,10},{10,6},{6,2},{2,0},{1,5},{5,9},... | collective-permute-start | bytes 1572872 | tf_op jit(solution)/shard_map/ppermute | solution.py:364
  20.5 22.1 %collective-permute-start.7 = (bf16[128,2048]{1,0:T(8,128)(2,1)}, bf16[128,2048]{1,0:T(8,128)(2,1)}, u32[]{:S(2)}, u32[]{:S(2)}) collective-permute-start(bf16[128,2048]{1,0:T(8,128)(2,1)} %collective-permute-done.5.refs_3_), channel_id=1, source_target_pairs={{0,2},{4,0},{8,4},{12,8},{14,12},{10,14},{6,10},{2,6},{1,3},{5,1},... | collective-permute-start | bytes 1572872 | tf_op jit(solution)/shard_map/ppermute | solution.py:364
  30.7 23.2 %collective-permute-start.11 = (bf16[128,2176]{1,0:T(8,128)(2,1)S(1)}, bf16[128,2176]{1,0:T(8,128)(2,1)S(1)}, u32[]{:S(2)}, u32[]{:S(2)}) collective-permute-start(bf16[128,2176]{1,0:T(8,128)(2,1)S(1)} %collective-permute-done.8.refs_1_), channel_id=1, source_target_pairs={{0,2},{4,0},{8,4},{12,8},{14,12},{10,14},{6,10},{2,6},{1,3},{5,1},... | collective-permute-start | bytes 1671176 | tf_op jit(solution)/shard_map/ppermute | solution.py:364
  30.7 21.0 %collective-permute-start.1 = (bf16[128,2176]{1,0:T(8,128)(2,1)S(1)}, bf16[128,2176]{1,0:T(8,128)(2,1)S(1)}, u32[]{:S(2)}, u32[]{:S(2)}) collective-permute-start(bf16[128,2176]{1,0:T(8,128)(2,1)S(1)} %collective-permute-done.refs_0_), channel_id=1, source_target_pairs={{0,4},{4,8},{8,12},{12,14},{14,10},{10,6},{6,2},{2,0},{1,5},{5,9},... | collective-permute-start | bytes 1671176 | tf_op jit(solution)/shard_map/ppermute | solution.py:364
  42.6 20.5 %collective-permute-start.9 = (bf16[128,2048]{1,0:T(8,128)(2,1)}, bf16[128,2048]{1,0:T(8,128)(2,1)}, u32[]{:S(2)}, u32[]{:S(2)}) collective-permute-start(bf16[128,2048]{1,0:T(8,128)(2,1)} %collective-permute-done.6.refs_2_), channel_id=1, source_target_pairs={{0,4},{4,8},{8,12},{12,14},{14,10},{10,6},{6,2},{2,0},{1,5},{5,9},... | collective-permute-start | bytes 1572872 | tf_op jit(solution)/shard_map/ppermute | solution.py:364
  44.2 30.8 %collective-permute-start.10 = (bf16[128,2048]{1,0:T(8,128)(2,1)}, bf16[128,2048]{1,0:T(8,128)(2,1)}, u32[]{:S(2)}, u32[]{:S(2)}) collective-permute-start(bf16[128,2048]{1,0:T(8,128)(2,1)} %collective-permute-done.7.refs_3_), channel_id=1, source_target_pairs={{0,2},{4,0},{8,4},{12,8},{14,12},{10,14},{6,10},{2,6},{1,3},{5,1},... | collective-permute-start | bytes 1572872 | tf_op jit(solution)/shard_map/ppermute | solution.py:364
  44.7 30.5 %collective-permute-start.14 = (bf16[64,4352]{1,0:T(8,128)(2,1)S(1)}, bf16[64,4352]{1,0:T(8,128)(2,1)S(1)}, u32[]{:S(2)}, u32[]{:S(2)}) collective-permute-start(bf16[64,4352]{1,0:T(8,128)(2,1)S(1)} %copy-done.10), channel_id=1, source_target_pairs={{0,1},{1,0},{2,3},{3,2},{4,5},{5,4},{6,7},{7,6},{8,9},{9,8},{10,11... | collective-permute-start | bytes 1671176 | tf_op jit(solution)/shard_map/ppermute | solution.py:367
  51.7 13.4 %copy-start.21 = (bf16[128,2176]{1,0:T(8,128)(2,1)}, bf16[128,2176]{1,0:T(8,128)(2,1)S(1)}, u32[]{:S(2)}) copy-start(bf16[128,2176]{1,0:T(8,128)(2,1)S(1)} %collective-permute-done.1.refs_0_) | copy-start | bytes 1671172
  51.7 25.1 %collective-permute-start.2 = (bf16[128,2176]{1,0:T(8,128)(2,1)S(1)}, bf16[128,2176]{1,0:T(8,128)(2,1)}, u32[]{:S(2)}, u32[]{:S(2)}) collective-permute-start(bf16[128,2176]{1,0:T(8,128)(2,1)S(1)} %collective-permute-done.1.refs_0_), channel_id=1, source_target_pairs={{0,4},{4,8},{8,12},{12,14},{14,10},{10,6},{6,2},{2,0},{1,5},{5,9},... | collective-permute-start | bytes 1671176 | tf_op jit(solution)/shard_map/ppermute | solution.py:364
  53.9 21.2 %copy-start.8 = (bf16[2304,128]{1,0:T(8,128)(2,1)S(1)}, bf16[2304,128]{1,0:T(8,128)(2,1)}, u32[]{:S(2)}) copy-start(bf16[2304,128]{1,0:T(8,128)(2,1)} %get-tuple-element.127) | copy-start | bytes 1769476
  53.9 37.1 %collective-permute-start.15 = (bf16[128,4352]{1,0:T(8,128)(2,1)}, bf16[128,4352]{1,0:T(8,128)(2,1)S(1)}, u32[]{:S(2)}, u32[]{:S(2)}) collective-permute-start(bf16[128,4352]{1,0:T(8,128)(2,1)} %get-tuple-element.112.refs_21_), channel_id=1, source_target_pairs={{0,1},{1,0},{2,3},{3,2},{4,5},{5,4},{6,7},{7,6},{8,9},{9,8},{10,11... | collective-permute-start | bytes 3342344 | tf_op jit(solution)/shard_map/ppermute | solution.py:367
  63.1 14.2 %collective-permute-start.13 = (bf16[128,2176]{1,0:T(8,128)(2,1)S(1)}, bf16[128,2176]{1,0:T(8,128)(2,1)S(1)}, u32[]{:S(2)}, u32[]{:S(2)}) collective-permute-start(bf16[128,2176]{1,0:T(8,128)(2,1)S(1)} %collective-permute-done.11.refs_1_), channel_id=1, source_target_pairs={{0,2},{4,0},{8,4},{12,8},{14,12},{10,14},{6,10},{2,6},{1,3},{5,1},... | collective-permute-start | bytes 1671176 | tf_op jit(solution)/shard_map/ppermute | solution.py:364
  75.0 40.2 %collective-permute-start.20 = (bf16[128,4352]{1,0:T(8,128)(2,1)}, bf16[128,4352]{1,0:T(8,128)(2,1)S(1)}, u32[]{:S(2)}, u32[]{:S(2)}) collective-permute-start(bf16[128,4352]{1,0:T(8,128)(2,1)} %get-tuple-element.123.refs_22_), channel_id=1, source_target_pairs={{0,1},{1,0},{2,3},{3,2},{4,5},{5,4},{6,7},{7,6},{8,9},{9,8},{10,11... | collective-permute-start | bytes 3342344 | tf_op jit(solution)/shard_map/ppermute | solution.py:367
  75.2 13.6 %copy-start.5 = (bf16[64,4352]{1,0:T(8,128)(2,1)}, bf16[64,4352]{1,0:T(8,128)(2,1)S(1)}, u32[]{:S(2)}) copy-start(bf16[64,4352]{1,0:T(8,128)(2,1)S(1)} %collective-permute-done.14.refs_5_.refs_15_.refs_25_) | copy-start | bytes 1671172
  75.2 15.0 %collective-permute-start.12 = (bf16[128,2048]{1,0:T(8,128)(2,1)}, bf16[128,2048]{1,0:T(8,128)(2,1)S(1)}, u32[]{:S(2)}, u32[]{:S(2)}) collective-permute-start(bf16[128,2048]{1,0:T(8,128)(2,1)} %collective-permute-done.10.refs_3_), channel_id=1, source_target_pairs={{0,2},{4,0},{8,4},{12,8},{14,12},{10,14},{6,10},{2,6},{1,3},{5,1},... | collective-permute-start | bytes 1572872 | tf_op jit(solution)/shard_map/ppermute | solution.py:364
  76.8 16.7 %collective-permute-start.3 = (bf16[128,2176]{1,0:T(8,128)(2,1)}, bf16[128,2176]{1,0:T(8,128)(2,1)S(1)}, u32[]{:S(2)}, u32[]{:S(2)}) collective-permute-start(bf16[128,2176]{1,0:T(8,128)(2,1)} %collective-permute-done.2.refs_0_), channel_id=1, source_target_pairs={{0,4},{4,8},{8,12},{12,14},{14,10},{10,6},{6,2},{2,0},{1,5},{5,9},... | collective-permute-start | bytes 1671176 | tf_op jit(solution)/shard_map/ppermute | solution.py:364
  77.3 19.7 %collective-permute-start.16 = (bf16[64,2048]{1,0:T(8,128)(2,1)}, bf16[64,2048]{1,0:T(8,128)(2,1)S(1)}, u32[]{:S(2)}, u32[]{:S(2)}) collective-permute-start(bf16[64,2048]{1,0:T(8,128)(2,1)} %get-tuple-element.118), channel_id=1, source_target_pairs={{0,2},{4,0},{8,4},{12,8},{14,12},{10,14},{6,10},{2,6},{1,3},{5,1},... | collective-permute-start | bytes 786440 | tf_op jit(solution)/shard_map/ppermute | solution.py:364
  90.2 16.7 %collective-permute-start.17 = (bf16[64,2048]{1,0:T(8,128)(2,1)}, bf16[64,2048]{1,0:T(8,128)(2,1)S(1)}, u32[]{:S(2)}, u32[]{:S(2)}) collective-permute-start(bf16[64,2048]{1,0:T(8,128)(2,1)} %get-tuple-element.119), channel_id=1, source_target_pairs={{0,4},{4,8},{8,12},{12,14},{14,10},{10,6},{6,2},{2,0},{1,5},{5,9},... | collective-permute-start | bytes 786440 | tf_op jit(solution)/shard_map/ppermute | solution.py:364
  91.0 15.9 %copy-start.2 = (bf16[128,4352]{1,0:T(8,128)(2,1)}, bf16[128,4352]{1,0:T(8,128)(2,1)S(1)}, u32[]{:S(2)}) copy-start(bf16[128,4352]{1,0:T(8,128)(2,1)S(1)} %collective-permute-done.15.refs_6_.refs_16_.refs_26_) | copy-start | bytes 3342340
  91.0 16.8 %collective-permute-start.18 = (bf16[64,2048]{1,0:T(8,128)(2,1)}, bf16[64,2048]{1,0:T(8,128)(2,1)S(1)}, u32[]{:S(2)}, u32[]{:S(2)}) collective-permute-start(bf16[64,2048]{1,0:T(8,128)(2,1)} %get-tuple-element.121), channel_id=1, source_target_pairs={{0,6},{4,2},{8,0},{12,4},{14,8},{10,12},{6,14},{2,10},{1,7},{5,3},... | collective-permute-start | bytes 786440 | tf_op jit(solution)/shard_map/ppermute | solution.py:364
  93.6 21.6 %collective-permute-start.19 = (bf16[64,2048]{1,0:T(8,128)(2,1)}, bf16[64,2048]{1,0:T(8,128)(2,1)S(1)}, u32[]{:S(2)}, u32[]{:S(2)}) collective-permute-start(bf16[64,2048]{1,0:T(8,128)(2,1)} %get-tuple-element.122), channel_id=1, source_target_pairs={{0,8},{4,12},{8,14},{12,10},{14,6},{10,2},{6,0},{2,4},{1,9},{5,13}... | collective-permute-start | bytes 786440 | tf_op jit(solution)/shard_map/ppermute | solution.py:364
  97.1 20.1 %collective-permute-start.21 = (bf16[128,4352]{1,0:T(8,128)(2,1)S(1)}, bf16[128,4352]{1,0:T(8,128)(2,1)S(1)}, u32[]{:S(2)}, u32[]{:S(2)}) collective-permute-start(bf16[128,4352]{1,0:T(8,128)(2,1)S(1)} %copy-done.7), channel_id=1, source_target_pairs={{0,1},{1,0},{2,3},{3,2},{4,5},{5,4},{6,7},{7,6},{8,9},{9,8},{10,11... | collective-permute-start | bytes 3342344 | tf_op jit(solution)/shard_map/ppermute | solution.py:367
  106.9 24.0 %collective-permute-start.25 = (bf16[64,2048]{1,0:T(8,128)(2,1)}, bf16[64,2048]{1,0:T(8,128)(2,1)S(1)}, u32[]{:S(2)}, u32[]{:S(2)}) collective-permute-start(bf16[64,2048]{1,0:T(8,128)(2,1)} %get-tuple-element.144), channel_id=1, source_target_pairs={{0,12},{4,14},{8,10},{12,6},{14,2},{10,0},{6,4},{2,8},{1,13},{5,15... | collective-permute-start | bytes 786440 | tf_op jit(solution)/shard_map/ppermute | solution.py:364
  107.8 23.1 %collective-permute-start.26 = (bf16[64,2048]{1,0:T(8,128)(2,1)}, bf16[64,2048]{1,0:T(8,128)(2,1)S(1)}, u32[]{:S(2)}, u32[]{:S(2)}) collective-permute-start(bf16[64,2048]{1,0:T(8,128)(2,1)} %get-tuple-element.145), channel_id=1, source_target_pairs={{0,10},{4,6},{8,2},{12,0},{14,4},{10,8},{6,12},{2,14},{1,11},{5,7}... | collective-permute-start | bytes 786440 | tf_op jit(solution)/shard_map/ppermute | solution.py:364
  115.2 4.1 %collective-permute-start.24 = (bf16[64,4352]{1,0:T(8,128)(2,1)}, bf16[64,4352]{1,0:T(8,128)(2,1)S(1)}, u32[]{:S(2)}, u32[]{:S(2)}) collective-permute-start(bf16[64,4352]{1,0:T(8,128)(2,1)} %get-tuple-element.143.refs_24_), channel_id=1, source_target_pairs={{0,1},{1,0},{2,3},{3,2},{4,5},{5,4},{6,7},{7,6},{8,9},{9,8},{10,11... | collective-permute-start | bytes 1671176 | tf_op jit(solution)/shard_map/ppermute | solution.py:367
  117.2 13.7 %collective-permute-start.22 = (bf16[288,256]{1,0:T(8,128)(2,1)S(1)}, bf16[288,256]{1,0:T(8,128)(2,1)S(1)}, u32[]{:S(2)}, u32[]{:S(2)}) collective-permute-start(bf16[288,256]{1,0:T(8,128)(2,1)S(1)} %get-tuple-element.132), channel_id=1, source_target_pairs={{0,4},{4,8},{8,12},{12,14},{14,10},{10,6},{6,2},{2,0},{1,5},{5,9},... | collective-permute-start | bytes 442376 | tf_op jit(solution)/shard_map/ppermute | solution.py:364
  117.3 17.1 %collective-permute-start.23 = (bf16[288,256]{1,0:T(8,128)(2,1)S(1)}, bf16[288,256]{1,0:T(8,128)(2,1)S(1)}, u32[]{:S(2)}, u32[]{:S(2)}) collective-permute-start(bf16[288,256]{1,0:T(8,128)(2,1)S(1)} %get-tuple-element.133), channel_id=1, source_target_pairs={{0,2},{4,0},{8,4},{12,8},{14,12},{10,14},{6,10},{2,6},{1,3},{5,1},... | collective-permute-start | bytes 442376 | tf_op jit(solution)/shard_map/ppermute | solution.py:364
  130.9 15.6 %copy-start.15 = (bf16[64,2048]{1,0:T(8,128)(2,1)}, bf16[64,2048]{1,0:T(8,128)(2,1)S(1)}, u32[]{:S(2)}) copy-start(bf16[64,2048]{1,0:T(8,128)(2,1)S(1)} %collective-permute-done.25.refs_3_) | copy-start | bytes 786436
  130.9 15.6 %copy-start.16 = (bf16[64,2048]{1,0:T(8,128)(2,1)}, bf16[64,2048]{1,0:T(8,128)(2,1)S(1)}, u32[]{:S(2)}) copy-start(bf16[64,2048]{1,0:T(8,128)(2,1)S(1)} %collective-permute-done.26.refs_6_) | copy-start | bytes 786436
  134.5 17.1 %copy-start.27 = (bf16[32,2048]{1,0:T(8,128)(2,1)S(1)}, bf16[32,2048]{1,0:T(8,128)(2,1)}, u32[]{:S(2)}) copy-start(bf16[32,2048]{1,0:T(8,128)(2,1)} %get-tuple-element.159) | copy-start | bytes 393220
  134.5 12.0 %collective-permute-start.28 = (bf16[288,512]{1,0:T(8,128)(2,1)S(1)}, bf16[288,512]{1,0:T(8,128)(2,1)S(1)}, u32[]{:S(2)}, u32[]{:S(2)}) collective-permute-start(bf16[288,512]{1,0:T(8,128)(2,1)S(1)} %maximum_select_fusion.1), channel_id=1, source_target_pairs={{0,2},{4,0},{8,4},{12,8},{14,12},{10,14},{6,10},{2,6},{1,3},{5,1},... | collective-permute-start | bytes 884744 | tf_op jit(solution)/shard_map/ppermute | solution.py:364
  134.9 11.6 %collective-permute-start.27 = (bf16[288,512]{1,0:T(8,128)(2,1)S(1)}, bf16[288,512]{1,0:T(8,128)(2,1)S(1)}, u32[]{:S(2)}, u32[]{:S(2)}) collective-permute-start(bf16[288,512]{1,0:T(8,128)(2,1)S(1)} %maximum_select_fusion), channel_id=1, source_target_pairs={{0,4},{4,8},{8,12},{12,14},{14,10},{10,6},{6,2},{2,0},{1,5},{5,9},... | collective-permute-start | bytes 884744 | tf_op jit(solution)/shard_map/ppermute | solution.py:364
  137.1 9.4 %collective-permute-start.29 = (bf16[32,2048]{1,0:T(8,128)(2,1)S(1)}, bf16[32,2048]{1,0:T(8,128)(2,1)S(1)}, u32[]{:S(2)}, u32[]{:S(2)}) collective-permute-start(bf16[32,2048]{1,0:T(8,128)(2,1)S(1)} %copy-done.28), channel_id=1, source_target_pairs={{0,14},{4,10},{8,6},{12,2},{14,0},{10,4},{6,8},{2,12},{1,15},{5,11... | collective-permute-start | bytes 393224 | tf_op jit(solution)/shard_map/ppermute | solution.py:364
  146.5 13.9 %copy-start.17 = (bf16[32,2048]{1,0:T(8,128)(2,1)}, bf16[32,2048]{1,0:T(8,128)(2,1)S(1)}, u32[]{:S(2)}) copy-start(bf16[32,2048]{1,0:T(8,128)(2,1)S(1)} %collective-permute-done.29.refs_4_) | copy-start | bytes 393220
  146.5 17.5 %collective-permute-start.30 = (bf16[288,512]{1,0:T(8,128)(2,1)S(1)}, bf16[288,512]{1,0:T(8,128)(2,1)S(1)}, u32[]{:S(2)}, u32[]{:S(2)}) collective-permute-start(bf16[288,512]{1,0:T(8,128)(2,1)S(1)} %broadcast_select_fusion.3), channel_id=1, source_target_pairs={{0,4},{4,8},{8,12},{12,14},{14,10},{10,6},{6,2},{2,0},{1,5},{5,9},... | collective-permute-start | bytes 884744 | tf_op jit(solution)/shard_map/ppermute | solution.py:364
  151.5 12.6 %collective-permute-start.31 = (bf16[288,512]{1,0:T(8,128)(2,1)S(1)}, bf16[288,512]{1,0:T(8,128)(2,1)S(1)}, u32[]{:S(2)}, u32[]{:S(2)}) collective-permute-start(bf16[288,512]{1,0:T(8,128)(2,1)S(1)} %broadcast_select_fusion.2), channel_id=1, source_target_pairs={{0,2},{4,0},{8,4},{12,8},{14,12},{10,14},{6,10},{2,6},{1,3},{5,1},... | collective-permute-start | bytes 884744 | tf_op jit(solution)/shard_map/ppermute | solution.py:364
  151.5 12.5 %collective-permute-start.32 = (bf16[32,2048]{1,0:T(8,128)(2,1)S(1)}, bf16[32,2048]{1,0:T(8,128)(2,1)S(1)}, u32[]{:S(2)}, u32[]{:S(2)}) collective-permute-start(bf16[32,2048]{1,0:T(8,128)(2,1)S(1)} %copy-done.27), channel_id=1, source_target_pairs={{0,14},{4,10},{8,6},{12,2},{14,0},{10,4},{6,8},{2,12},{1,15},{5,11... | collective-permute-start | bytes 393224 | tf_op jit(solution)/shard_map/ppermute | solution.py:364
  164.1 12.9 %copy-start.18 = (bf16[32,2048]{1,0:T(8,128)(2,1)}, bf16[32,2048]{1,0:T(8,128)(2,1)S(1)}, u32[]{:S(2)}) copy-start(bf16[32,2048]{1,0:T(8,128)(2,1)S(1)} %collective-permute-done.32.refs_5_) | copy-start | bytes 393220
  164.1 16.1 %collective-permute-start.36 = (bf16[512,2048]{1,0:T(8,128)(2,1)}, bf16[512,2048]{1,0:T(8,128)(2,1)S(1)}, u32[]{:S(2)}, u32[]{:S(2)}) collective-permute-start(bf16[512,2048]{1,0:T(8,128)(2,1)} %get-tuple-element.178), channel_id=1, source_target_pairs={{0,1},{1,0},{2,3},{3,2},{4,5},{5,4},{6,7},{7,6},{8,9},{9,8},{10,11... | collective-permute-start | bytes 6291464 | tf_op jit(solution)/shard_map/ppermute | solution.py:367
  164.2 9.5 %collective-permute-start.33 = (bf16[288,512]{1,0:T(8,128)(2,1)S(1)}, bf16[288,512]{1,0:T(8,128)(2,1)S(1)}, u32[]{:S(2)}, u32[]{:S(2)}) collective-permute-start(bf16[288,512]{1,0:T(8,128)(2,1)S(1)} %broadcast_select_fusion.1), channel_id=1, source_target_pairs={{0,4},{4,8},{8,12},{12,14},{14,10},{10,6},{6,2},{2,0},{1,5},{5,9},... | collective-permute-start | bytes 884744 | tf_op jit(solution)/shard_map/ppermute | solution.py:364
  166.6 9.4 %collective-permute-start.34 = (bf16[288,512]{1,0:T(8,128)(2,1)S(1)}, bf16[288,512]{1,0:T(8,128)(2,1)}, u32[]{:S(2)}, u32[]{:S(2)}) collective-permute-start(bf16[288,512]{1,0:T(8,128)(2,1)S(1)} %broadcast_select_fusion), channel_id=1, source_target_pairs={{0,2},{4,0},{8,4},{12,8},{14,12},{10,14},{6,10},{2,6},{1,3},{5,1},... | collective-permute-start | bytes 884744 | tf_op jit(solution)/shard_map/ppermute | solution.py:364
  177.0 3.3 %collective-permute-start.35 = (bf16[288,512]{1,0:T(8,128)(2,1)S(1)}, bf16[288,512]{1,0:T(8,128)(2,1)S(1)}, u32[]{:S(2)}, u32[]{:S(2)}) collective-permute-start(bf16[288,512]{1,0:T(8,128)(2,1)S(1)} %select_select_fusion.mine), channel_id=1, source_target_pairs={{0,1},{1,0},{2,3},{3,2},{4,5},{5,4},{6,7},{7,6},{8,9},{9,8},{10,11... | collective-permute-start | bytes 884744 | tf_op jit(solution)/shard_map/ppermute | solution.py:367
  (18 other events, 79.9 us)

commit v11 on v9

--- a/solution.py
+++ b/solution.py
@@ -411,42 +411,45 @@
         parts = [lax.dynamic_slice_in_dim(part, owner * taken, taken, axis=0) for part in turned]
         return jnp.concatenate(parts, axis=1)
 
-    far = chunk(half)
-    lanes = far.shape[1] // 2
-    around = [far[:, :lanes], far[:, lanes:]]
-    around, other = lax.optimization_barrier((around, other))
-    around = [shift(around[0], 1), shift(around[1], -1)]
+    lanes = experts * capacity // 2
+
+    def halves(distance):
+        columns = chunk(distance)
+        return [columns[:, :lanes], columns[:, lanes:]]
+
+    hot_mine, hot_theirs = ordered(plan, experts, capacity, scal, hot)
+    far = halves(half)
+    far, other, hot_mine, hot_theirs = lax.optimization_barrier((far, other, hot_mine, hot_theirs))
+    hot_theirs = swap(hot_theirs)
+    far = [shift(far[0], 1), shift(far[1], -1)]
     others = [part for _, part in late[: half - 1]] + [other, late[half][1]]
     expert_grad = expert_gradient(units, scal, mine, packs, others)
-    chunks = [chunk(distance) for distance in range(1 - half, half)]
+    chunks = {distance: halves(distance) for distance in range(1 - half, half)}
     (back_far,) = late[half][0]
-    hot_mine, hot_theirs = ordered(plan, experts, capacity, scal, hot)
+    far, expert_grad, back_ahead, back_behind, back_far, chunks = lax.optimization_barrier(
+        (far, expert_grad, back_ahead, back_behind, back_far, chunks)
+    )
+    ahead, behind = [far[0], None], [None, far[1]]
+
+    def onward(kept, received, step):
+        return shift(kept if received is None else jnp.where(is_hot, kept, received), step)
+
     for number in range(1, half):
-        if number == 1:
-            around, expert_grad, back_ahead, back_behind, back_far, chunks = (
-                lax.optimization_barrier(
-                    (around, expert_grad, back_ahead, back_behind, back_far, chunks)
-                )
-            )
-            around = [jnp.concatenate([part, part], axis=1) for part in around]
-        if number == half - 1:
-            around, hot_mine, hot_theirs = lax.optimization_barrier((around, hot_mine, hot_theirs))
-        ahead = jnp.where(is_hot, chunks[2 * half - 1 - number], around[0])
-        behind = jnp.where(is_hot, chunks[number - 1], around[1])
-        around = [shift(ahead, 1), shift(behind, -1)]
-    hot_theirs = swap(hot_theirs)
+        for k in range(2):
+            ahead[k] = onward(chunks[half - number][k], ahead[k], 1)
+            behind[k] = onward(chunks[number - half][k], behind[k], -1)
     sent = [rows for rows, _ in late[: half - 1]] + [[back_behind, back_ahead], [back_far]]
     for steps, parts in zip(plan, sent):
         for step, part in zip(steps, parts):
             returned[step % experts] = part
     token_grad = combine(experts, fanout, capacity, scal, meta, [returned[d] for d in range(experts)])
-    around, token_grad = lax.optimization_barrier((around, token_grad))
+    ahead, behind, token_grad = lax.optimization_barrier((ahead, behind, token_grad))
     away = (to_ring(own, experts) - ring_hot + experts) % experts
-    lane = lax.broadcasted_iota(jnp.int32, far.shape, 1)
-    reach = jnp.where(lane < lanes, half, half - 1)
-    columns = jnp.where(
-        away == 0, chunks[half - 1], jnp.where(away <= reach, around[0], around[1])
-    )
+    columns = [
+        jnp.where(away == 0, chunks[0][k], jnp.where(away <= half - k, ahead[k], behind[k]))
+        for k in range(2)
+    ]
+    columns = jnp.concatenate(columns, axis=1)
     shadow_grad = shadow_gradient(
         experts, scal, columns, swap(columns), hot_mine, hot_theirs
     ).T

time: 176 us -> 180 us (1.023)
  starting transfers between devices: 45.4 us -> 61.7 us
  waiting for transfers between devices: 50.8 us -> 38.8 us
    ppermute x29 -> x35, starting transfers between devices: 45.3 us -> 61.1 us  [shift(): return lax.ppermute(block, 'expert', pairs)]
    ppermute x29 -> x35, waiting for transfers between devices: 49.2 us -> 37.2 us  [shift(): return lax.ppermute(block, 'expert', pairs)]
  transfers between devices with their start and end apart: 36 -> 42, of which waited for: 12 -> 16; matrix products, arithmetic and copies ran while one was open for 3% -> 2% of each run, Pallas kernels for 39% -> 39%
where the time goes in v11:
time: 180 us; the launch traced here: 179 us
  Pallas kernels  71.5 us (40%)
  starting transfers between devices  61.7 us (34%)
  waiting for transfers between devices  38.8 us (22%)
  local copies, waits for them, and re-layouts  2.98 us (2%)
  other arithmetic  2.1 us (1%)
  between operations  1.85 us (1%)
    ppermute x35, starting transfers between devices, shift(): return lax.ppermute(block, 'expert', pairs)  61.1 us
    pallas_call x5, Pallas kernels, run_step(): pl.pallas_call(functools.partial(step_kernel, steps, fanout, capacity, jo...  48.6 us
    ppermute x35, waiting for transfers between devices, shift(): return lax.ppermute(block, 'expert', pairs)  37.2 us
    pallas_call x1, Pallas kernels, expert_gradient(): pl.pallas_call(functools.partial(gradient_kernel, units, count), grid=(ti...  10.8 us
    pallas_call x1, Pallas kernels, ordered(): pl.pallas_call(functools.partial(order_kernel, plan, experts, capacity),...  4.61 us
  transfers between devices with their start and end apart: 42, of which 16 were waited for; matrix products, arithmetic and copies ran while one was open for 2% of the time, Pallas kernels for 39%

profile of v11, /device:TPU:0, one launch (start us, length us, event | category | flops | bytes accessed | tf_op | source)
XLA Modules:
  0.0 178.9 jit_solution(3744180822400642482)
XLA Ops:
  0.6 3.1 %collective-permute-start.2 = (bf16[128,2048]{1,0:T(8,128)(2,1)}, bf16[128,2048]{1,0:T(8,128)(2,1)S(1)}, u32[]{:S(2)}, u32[]{:S(2)}) collective-permute-start(bf16[128,2048]{1,0:T(8,128)(2,1)} %refs_1_.1), channel_id=1, source_target_pairs={{0,4},{4,8},{8,12},{12,14},{14,10},{10,6},{6,2},{2,0},{1,5},{5,9},... | collective-permute-start | bytes 1572872 | tf_op jit(solution)/shard_map/ppermute | solution.py:356
  3.7 2.0 %ring_message.1 = (bf16[128,2176]{1,0:T(8,128)(2,1)}, bf16[128,128]{1,0:T(8,128)(2,1)}) custom-call(bf16[128,2048]{1,0:T(8,128)(2,1)} %tokens.1, s32[2,128]{1,0:T(2,128)} %bitcast.17, f32[2,128]{1,0:T(2,128)} %bitcast.18, f32[1,128]{1,0:T(1,128)} %bitcast.19, s32[1,128]{1,0:T(1,128)} %bitcast.20), custom_call_target="tpu_custom_call" | custom-call | bytes 1048576 | tf_op jit(solution)/shard_map/ring_message/pallas_call | solution.py:262
  5.7 2.0 %collective-permute-start = (bf16[128,2176]{1,0:T(8,128)(2,1)}, bf16[128,2176]{1,0:T(8,128)(2,1)S(1)}, u32[]{:S(2)}, u32[]{:S(2)}) collective-permute-start(bf16[128,2176]{1,0:T(8,128)(2,1)} %get-tuple-element.105.refs_0_), channel_id=1, source_target_pairs={{0,4},{4,8},{8,12},{12,14},{14,10},{10,6},{6,2},{2,0},{1,5},{5,9},... | collective-permute-start | bytes 1671176 | tf_op jit(solution)/shard_map/ppermute | solution.py:356
  9.0 9.4 %expert_step.5 = (bf16[64,2048]{1,0:T(8,128)(2,1)}, bf16[64,4352]{1,0:T(8,128)(2,1)}, bf16[64,4096]{1,0:T(8,128)(2,1)}, bf16[64,2048]{1,0:T(8,128)(2,1)}) custom-call(s32[3]{0:T(128)} %pad_add_fusion.scal, bf16[128,2176]{1,0:T(8,128)(2,1)} %get-tuple-element.105.refs_0_, bf16[128,2048]{1,0:T(8,128)(2,1)} %refs_1_.1, bf16[2048,1536]{1,0:T(8,128)(2,1)} %bitcast.21, ...), custom_call_target="tpu_custom_call" | custom-call | flops 4026531840 | bytes 9437184 | tf_op jit(solution)/shard_map/expert_step/pallas_call | solution.py:151
  18.9 1.6 collective-permute-start.6
  20.9 7.7 %collective-permute-done.refs_0_ = bf16[128,2176]{1,0:T(8,128)(2,1)S(1)} collective-permute-done((bf16[128,2176]{1,0:T(8,128)(2,1)}, bf16[128,2176]{1,0:T(8,128)(2,1)S(1)}, u32[]{:S(2)}, u32[]{:S(2)}) %collective-permute-start) | collective-permute-done | bytes 557088 | tf_op jit(solution)/shard_map/ppermute | solution.py:356
  28.6 2.1 %collective-permute-start.4 = (bf16[128,2176]{1,0:T(8,128)(2,1)S(1)}, bf16[128,2176]{1,0:T(8,128)(2,1)S(1)}, u32[]{:S(2)}, u32[]{:S(2)}) collective-permute-start(bf16[128,2176]{1,0:T(8,128)(2,1)S(1)} %collective-permute-done.refs_0_), channel_id=1, source_target_pairs={{0,4},{4,8},{8,12},{12,14},{14,10},{10,6},{6,2},{2,0},{1,5},{5,9},... | collective-permute-start | bytes 1671176 | tf_op jit(solution)/shard_map/ppermute | solution.py:356
  30.8 9.8 %expert_step.6 = (bf16[128,2048]{1,0:T(8,128)(2,1)}, bf16[128,4352]{1,0:T(8,128)(2,1)}, bf16[128,4096]{1,0:T(8,128)(2,1)}, bf16[64,2048]{1,0:T(8,128)(2,1)}, bf1...) custom-call(s32[3]{0:T(128)} %pad_add_fusion.scal, bf16[128,2176]{1,0:T(8,128)(2,1)} %copy-done.19, ...), custom_call_target="tpu_custom_call" | custom-call | flops 4026531840 | bytes 9437184 | tf_op jit(solution)/shard_map/expert_step/pallas_call | solution.py:151
  40.7 1.3 collective-permute-done.7.refs_3_
  42.0 1.6 collective-permute-start.11
  44.1 7.6 %collective-permute-done.4.refs_0_ = bf16[128,2176]{1,0:T(8,128)(2,1)S(1)} collective-permute-done((bf16[128,2176]{1,0:T(8,128)(2,1)S(1)}, bf16[128,2176]{1,0:T(8,128)(2,1)S(1)}, u32[]{:S(2)}, u32[]{:S(2)}) %collective-permute-start.4) | collective-permute-done | bytes 557088 | tf_op jit(solution)/shard_map/ppermute | solution.py:356
  51.7 2.1 %collective-permute-done.5.refs_1_ = bf16[128,2176]{1,0:T(8,128)(2,1)S(1)} collective-permute-done((bf16[128,2176]{1,0:T(8,128)(2,1)}, bf16[128,2176]{1,0:T(8,128)(2,1)S(1)}, u32[]{:S(2)}, u32[]{:S(2)}) %collective-permute-start.5) | collective-permute-done | bytes 557088 | tf_op jit(solution)/shard_map/ppermute | solution.py:356
  53.9 1.6 collective-permute-start.9
  55.9 9.8 %expert_step.7 = (bf16[128,2048]{1,0:T(8,128)(2,1)}, bf16[128,4352]{1,0:T(8,128)(2,1)}, bf16[128,4096]{1,0:T(8,128)(2,1)}, bf16[64,2048]{1,0:T(8,128)(2,1)}, bf1...) custom-call(s32[3]{0:T(128)} %pad_add_fusion.scal, bf16[128,2176]{1,0:T(8,128)(2,1)} %copy-done.17, ...), custom_call_target="tpu_custom_call" | custom-call | flops 4026531840 | bytes 9437184 | tf_op jit(solution)/shard_map/expert_step/pallas_call | solution.py:151
  65.9 0.9 copy-done.9
  67.0 2.0 %collective-permute-start.15 = (bf16[64,2048]{1,0:T(8,128)(2,1)S(1)}, bf16[64,2048]{1,0:T(8,128)(2,1)S(1)}, u32[]{:S(2)}, u32[]{:S(2)}) collective-permute-start(bf16[64,2048]{1,0:T(8,128)(2,1)S(1)} %copy-done.24), channel_id=1, source_target_pairs={{0,4},{4,8},{8,12},{12,14},{14,10},{10,6},{6,2},{2,0},{1,5},{5,9},... | collective-permute-start | bytes 786440 | tf_op jit(solution)/shard_map/ppermute | solution.py:356
  69.1 5.8 %collective-permute-done.9.refs_0_ = bf16[128,2176]{1,0:T(8,128)(2,1)S(1)} collective-permute-done((bf16[128,2176]{1,0:T(8,128)(2,1)S(1)}, bf16[128,2176]{1,0:T(8,128)(2,1)S(1)}, u32[]{:S(2)}, u32[]{:S(2)}) %collective-permute-start.9) | collective-permute-done | bytes 557088 | tf_op jit(solution)/shard_map/ppermute | solution.py:356
  74.9 2.1 %collective-permute-start.17 = (bf16[128,2048]{1,0:T(8,128)(2,1)}, bf16[128,2048]{1,0:T(8,128)(2,1)}, u32[]{:S(2)}, u32[]{:S(2)}) collective-permute-start(bf16[128,2048]{1,0:T(8,128)(2,1)} %collective-permute-done.12.refs_3_), channel_id=1, source_target_pairs={{0,2},{4,0},{8,4},{12,8},{14,12},{10,14},{6,10},{2,6},{1,3},{5,1},... | collective-permute-start | bytes 1572872 | tf_op jit(solution)/shard_map/ppermute | solution.py:356
  77.1 1.6 collective-permute-start.16
  78.7 4.0 %collective-permute-done.14.refs_7_ = bf16[64,2048]{1,0:T(8,128)(2,1)S(1)} collective-permute-done((bf16[64,2048]{1,0:T(8,128)(2,1)S(1)}, bf16[64,2048]{1,0:T(8,128)(2,1)S(1)}, u32[]{:S(2)}, u32[]{:S(2)}) %collective-permute-start.14) | collective-permute-done | bytes 262176 | tf_op jit(solution)/shard_map/ppermute | solution.py:356
  82.7 1.4 collective-permute-start.19
  84.1 9.9 %expert_step.8 = (bf16[128,2048]{1,0:T(8,128)(2,1)}, bf16[128,4352]{1,0:T(8,128)(2,1)}, bf16[128,4096]{1,0:T(8,128)(2,1)}, bf16[64,2048]{1,0:T(8,128)(2,1)}, bf1...) custom-call(s32[3]{0:T(128)} %pad_add_fusion.scal, bf16[128,2176]{1,0:T(8,128)(2,1)} %copy-done.20, ...), custom_call_target="tpu_custom_call" | custom-call | flops 4026531840 | bytes 9437184 | tf_op jit(solution)/shard_map/expert_step/pallas_call | solution.py:151
  94.2 1.3 constant_dynamic-slice_fusion.1
  95.5 1.6 collective-permute-start.20
  97.1 6.5 %collective-permute-start.25 = (bf16[64,2048]{1,0:T(8,128)(2,1)S(1)}, bf16[64,2048]{1,0:T(8,128)(2,1)S(1)}, u32[]{:S(2)}, u32[]{:S(2)}) collective-permute-start(bf16[64,2048]{1,0:T(8,128)(2,1)S(1)} %copy-done.27), channel_id=1, source_target_pairs={{0,12},{4,14},{8,10},{12,6},{14,2},{10,0},{6,4},{2,8},{1,13},{5,15... | collective-permute-start | bytes 786440 | tf_op jit(solution)/shard_map/ppermute | solution.py:356
  104.4 9.7 %expert_step.9 = (bf16[64,2048]{1,0:T(8,128)(2,1)}, bf16[64,4352]{1,0:T(8,128)(2,1)}, bf16[64,4096]{1,0:T(8,128)(2,1)}, bf16[64,2048]{1,0:T(8,128)(2,1)}, bf16[2304,128]{1,0:T(8,128)(2,1)}) custom-call(s32[3]{0:T(128)} %pad_add_fusion.scal, bf16[128,2176]{1,0:T(8,128)(2,1)} %copy-done.22, bf16[128,2048]{1,0:T(8,128)(2,1)} %collective-permute-done.17.refs_1_, ...), custom_call_target="tpu_custom_call" | custom-call | flops 4026531840 | bytes 9437184 | tf_op jit(solution)/shard_map/expert_step/pallas_call | solution.py:151
  114.2 5.6 %collective-permute-start.27 = (bf16[64,2048]{1,0:T(8,128)(2,1)}, bf16[64,2048]{1,0:T(8,128)(2,1)S(1)}, u32[]{:S(2)}, u32[]{:S(2)}) collective-permute-start(bf16[64,2048]{1,0:T(8,128)(2,1)} %get-tuple-element.173), channel_id=1, source_target_pairs={{0,14},{4,10},{8,6},{12,2},{14,0},{10,4},{6,8},{2,12},{1,15},{5,11... | collective-permute-start | bytes 786440 | tf_op jit(solution)/shard_map/ppermute | solution.py:356
  119.8 4.6 %hot_rows_ordered.1 = (bf16[512,2048]{1,0:T(8,128)(2,1)}, bf16[512,2048]{1,0:T(8,128)(2,1)}) custom-call(s32[3]{0:T(128)} %pad_add_fusion.scal, bf16[64,4096]{1,0:T(8,128)(2,1)} %get-tuple-element.151.refs_0_, bf16[128,4096]{1,0:T(8,128)(2,1)} %get-tuple-element.152.refs_1_, bf16[128,4096]{1,0:T(8,128)(2,1)} %get-tuple-element.153.refs_2_, ...), custom_call_target="tpu_custom_call" | custom-call | bytes 8388608 | tf_op jit(solution)/shard_map/hot_rows_ordered/pallas_call | solution.py:290
  124.7 10.1 %collective-permute-start.22 = (bf16[288,256]{1,0:T(8,128)(2,1)S(1)}, bf16[288,256]{1,0:T(8,128)(2,1)S(1)}, u32[]{:S(2)}, u32[]{:S(2)}) collective-permute-start(bf16[288,256]{1,0:T(8,128)(2,1)S(1)} %get-tuple-element.158), channel_id=1, source_target_pairs={{0,4},{4,8},{8,12},{12,14},{14,10},{10,6},{6,2},{2,0},{1,5},{5,9},... | collective-permute-start | bytes 442376 | tf_op jit(solution)/shard_map/ppermute | solution.py:356
  134.8 1.8 %collective-permute-start.23 = (bf16[288,256]{1,0:T(8,128)(2,1)S(1)}, bf16[288,256]{1,0:T(8,128)(2,1)S(1)}, u32[]{:S(2)}, u32[]{:S(2)}) collective-permute-start(bf16[288,256]{1,0:T(8,128)(2,1)S(1)} %get-tuple-element.159), channel_id=1, source_target_pairs={{0,2},{4,0},{8,4},{12,8},{14,12},{10,14},{6,10},{2,6},{1,3},{5,1},... | collective-permute-start | bytes 442376 | tf_op jit(solution)/shard_map/ppermute | solution.py:356
  136.6 10.8 %expert_gradient.1 = f32[1,1024,2304]{2,1,0:T(8,128)} custom-call(s32[3]{0:T(128)} %pad_add_fusion.scal, bf16[64,2048]{1,0:T(8,128)(2,1)} %get-tuple-element.160.refs_0_.refs_10_, bf16[128,2048]{1,0:T(8,128)(2,1)} %get-tuple-element.161.refs_1_.refs_11_, bf16[128,2048]{1,0:T(8,128)(2,1)} %get-tuple-element.162.refs_2_.refs_12_, ...), custom_call_target="tpu_custom_call" | custom-call | flops 4831838208 | bytes 14155776 | tf_op jit(solution)/shard_map/expert_gradient/pallas_call | solution.py:226
  147.8 1.8 %collective-permute-start.37 = (bf16[288,256]{1,0:T(8,128)(2,1)S(1)}, bf16[288,256]{1,0:T(8,128)(2,1)S(1)}, u32[]{:S(2)}, u32[]{:S(2)}) collective-permute-start(bf16[288,256]{1,0:T(8,128)(2,1)S(1)} %broadcast_select_fusion.2), channel_id=1, source_target_pairs={{0,2},{4,0},{8,4},{12,8},{14,12},{10,14},{6,10},{2,6},{1,3},{5,1},... | collective-permute-start | bytes 442376 | tf_op jit(solution)/shard_map/ppermute | solution.py:356
  149.6 1.0 collective-permute-start.34
  150.6 1.0 collective-permute-start.31
  152.0 2.5 %collective-permute-done.37 = bf16[288,256]{1,0:T(8,128)(2,1)S(1)} collective-permute-done((bf16[288,256]{1,0:T(8,128)(2,1)S(1)}, bf16[288,256]{1,0:T(8,128)(2,1)S(1)}, u32[]{:S(2)}, u32[]{:S(2)}) %collective-permute-start.37) | collective-permute-done | bytes 147488 | tf_op jit(solution)/shard_map/ppermute | solution.py:356
  154.5 1.8 collective-permute-start.38
  156.3 1.0 collective-permute-done.34
  157.3 2.1 %collective-permute-start.35 = (bf16[288,256]{1,0:T(8,128)(2,1)S(1)}, bf16[288,256]{1,0:T(8,128)(2,1)S(1)}, u32[]{:S(2)}, u32[]{:S(2)}) collective-permute-start(bf16[288,256]{1,0:T(8,128)(2,1)S(1)} %broadcast_select_fusion.4), channel_id=1, source_target_pairs={{0,2},{4,0},{8,4},{12,8},{14,12},{10,14},{6,10},{2,6},{1,3},{5,1},... | collective-permute-start | bytes 442376 | tf_op jit(solution)/shard_map/ppermute | solution.py:356
  159.6 2.1 %collective-permute-start.29 = (bf16[288,256]{1,0:T(8,128)(2,1)S(1)}, bf16[288,256]{1,0:T(8,128)(2,1)S(1)}, u32[]{:S(2)}, u32[]{:S(2)}) collective-permute-start(bf16[288,256]{1,0:T(8,128)(2,1)S(1)} %broadcast_select_fusion.8), channel_id=1, source_target_pairs={{0,4},{4,8},{8,12},{12,14},{14,10},{10,6},{6,2},{2,0},{1,5},{5,9},... | collective-permute-start | bytes 442376 | tf_op jit(solution)/shard_map/ppermute | solution.py:356
  161.8 1.1 collective-permute-start.39
  162.9 0.8 collective-permute-done.35
  163.8 2.5 %collective-permute-start.36 = (bf16[288,256]{1,0:T(8,128)(2,1)S(1)}, bf16[288,256]{1,0:T(8,128)(2,1)S(1)}, u32[]{:S(2)}, u32[]{:S(2)}) collective-permute-start(bf16[288,256]{1,0:T(8,128)(2,1)S(1)} %broadcast_select_fusion.3), channel_id=1, source_target_pairs={{0,2},{4,0},{8,4},{12,8},{14,12},{10,14},{6,10},{2,6},{1,3},{5,1},... | collective-permute-start | bytes 442376 | tf_op jit(solution)/shard_map/ppermute | solution.py:356
  166.5 1.4 collective-permute-done.29
  168.6 3.2 %token_sum.1 = bf16[128,2048]{1,0:T(8,128)(2,1)} custom-call(s32[3]{0:T(128)} %pad_add_fusion.scal, bf16[128,128]{1,0:T(8,128)(2,1)} %get-tuple-element.188.meta, bf16[64,2048]{1,0:T(8,128)(2,1)} %get-tuple-element.189.refs_0_, bf16[64,2048]{1,0:T(8,128)(2,1)} %copy-done.11, bf16[64,2048]{1,0:T(8,128)(2,1)} %copy-done.13, bf16[64,2048]{1,0:T(8,128)(2,1)} %copy-done.14, ...), custom_call_target="tpu_custom_call" | custom-call | flops 268435456 | bytes 2097152 | tf_op jit(solution)/shard_map/token_sum/pallas_call | solution.py:186
  172.2 1.7 collective-permute-done.30
  173.9 0.9 select_select_fusion.1
  174.9 1.6 collective-permute-done.40.theirs
  176.5 2.3 %shadow_gradient.1 = f32[288,1024]{1,0:T(8,128)} custom-call(s32[3]{0:T(128)S(1)} %copy-done.1, bf16[288,512]{1,0:T(8,128)(2,1)S(1)} %pad_maximum_fusion.mine, bf16[288,512]{1,0:T(8,128)(2,1)S(1)} %collective-permute-done.40.theirs, bf16[512,2048]{1,0:T(8,128)(2,1)S(1)} %copy-done, bf16[512,2048]{1,0:T(8,128)(2,1)S(1)} %collective-permute-done.41.hot_theirs), custom_call_target="tpu_custom_call" | custom-call | flops 603979776 | bytes 2097152 | tf_op jit(solution)/shard_map/shadow_gradient/pallas_call | solution.py:329
  (130 shorter events, 6.6 us)
Async XLA Ops:
  0.6 17.8 %collective-permute-start.2 = (bf16[128,2048]{1,0:T(8,128)(2,1)}, bf16[128,2048]{1,0:T(8,128)(2,1)S(1)}, u32[]{:S(2)}, u32[]{:S(2)}) collective-permute-start(bf16[128,2048]{1,0:T(8,128)(2,1)} %refs_1_.1), channel_id=1, source_target_pairs={{0,4},{4,8},{8,12},{12,14},{14,10},{10,6},{6,2},{2,0},{1,5},{5,9},... | collective-permute-start | bytes 1572872 | tf_op jit(solution)/shard_map/ppermute | solution.py:356
  3.7 15.2 %collective-permute-start.3 = (bf16[128,2048]{1,0:T(8,128)(2,1)}, bf16[128,2048]{1,0:T(8,128)(2,1)}, u32[]{:S(2)}, u32[]{:S(2)}) collective-permute-start(bf16[128,2048]{1,0:T(8,128)(2,1)} %refs_1_.1), channel_id=1, source_target_pairs={{0,2},{4,0},{8,4},{12,8},{14,12},{10,14},{6,10},{2,6},{1,3},{5,1},... | collective-permute-start | bytes 1572872 | tf_op jit(solution)/shard_map/ppermute | solution.py:356
  5.7 22.8 %collective-permute-start = (bf16[128,2176]{1,0:T(8,128)(2,1)}, bf16[128,2176]{1,0:T(8,128)(2,1)S(1)}, u32[]{:S(2)}, u32[]{:S(2)}) collective-permute-start(bf16[128,2176]{1,0:T(8,128)(2,1)} %get-tuple-element.105.refs_0_), channel_id=1, source_target_pairs={{0,4},{4,8},{8,12},{12,14},{14,10},{10,6},{6,2},{2,0},{1,5},{5,9},... | collective-permute-start | bytes 1671176 | tf_op jit(solution)/shard_map/ppermute | solution.py:356
  7.7 23.1 %collective-permute-start.1 = (bf16[128,2176]{1,0:T(8,128)(2,1)}, bf16[128,2176]{1,0:T(8,128)(2,1)}, u32[]{:S(2)}, u32[]{:S(2)}) collective-permute-start(bf16[128,2176]{1,0:T(8,128)(2,1)} %get-tuple-element.105.refs_0_), channel_id=1, source_target_pairs={{0,2},{4,0},{8,4},{12,8},{14,12},{10,14},{6,10},{2,6},{1,3},{5,1},... | collective-permute-start | bytes 1671176 | tf_op jit(solution)/shard_map/ppermute | solution.py:356
  18.4 12.4 %copy-start.23 = (bf16[128,2048]{1,0:T(8,128)(2,1)}, bf16[128,2048]{1,0:T(8,128)(2,1)S(1)}, u32[]{:S(2)}) copy-start(bf16[128,2048]{1,0:T(8,128)(2,1)S(1)} %collective-permute-done.2.refs_2_) | copy-start | bytes 1572868
  18.9 21.7 %collective-permute-start.6 = (bf16[128,2048]{1,0:T(8,128)(2,1)S(1)}, bf16[128,2048]{1,0:T(8,128)(2,1)}, u32[]{:S(2)}, u32[]{:S(2)}) collective-permute-start(bf16[128,2048]{1,0:T(8,128)(2,1)S(1)} %collective-permute-done.2.refs_2_), channel_id=1, source_target_pairs={{0,4},{4,8},{8,12},{12,14},{14,10},{10,6},{6,2},{2,0},{1,5},{5,9},... | collective-permute-start | bytes 1572872 | tf_op jit(solution)/shard_map/ppermute | solution.py:356
  20.5 23.1 %collective-permute-start.8 = (bf16[64,4352]{1,0:T(8,128)(2,1)}, bf16[64,4352]{1,0:T(8,128)(2,1)S(1)}, u32[]{:S(2)}, u32[]{:S(2)}) collective-permute-start(bf16[64,4352]{1,0:T(8,128)(2,1)} %get-tuple-element.114.refs_2_.refs_20_), channel_id=1, source_target_pairs={{0,1},{1,0},{2,3},{3,2},{4,5},{5,4},{6,7},{7,6},{8,9},{9,8},{10,11... | collective-permute-start | bytes 1671176 | tf_op jit(solution)/shard_map/ppermute | solution.py:359
  20.5 21.5 %collective-permute-start.7 = (bf16[128,2048]{1,0:T(8,128)(2,1)}, bf16[128,2048]{1,0:T(8,128)(2,1)}, u32[]{:S(2)}, u32[]{:S(2)}) collective-permute-start(bf16[128,2048]{1,0:T(8,128)(2,1)} %collective-permute-done.3.refs_3_), channel_id=1, source_target_pairs={{0,2},{4,0},{8,4},{12,8},{14,12},{10,14},{6,10},{2,6},{1,3},{5,1},... | collective-permute-start | bytes 1572872 | tf_op jit(solution)/shard_map/ppermute | solution.py:356
  28.6 23.2 %collective-permute-start.4 = (bf16[128,2176]{1,0:T(8,128)(2,1)S(1)}, bf16[128,2176]{1,0:T(8,128)(2,1)S(1)}, u32[]{:S(2)}, u32[]{:S(2)}) collective-permute-start(bf16[128,2176]{1,0:T(8,128)(2,1)S(1)} %collective-permute-done.refs_0_), channel_id=1, source_target_pairs={{0,4},{4,8},{8,12},{12,14},{14,10},{10,6},{6,2},{2,0},{1,5},{5,9},... | collective-permute-start | bytes 1671176 | tf_op jit(solution)/shard_map/ppermute | solution.py:356
  30.8 23.1 %collective-permute-start.5 = (bf16[128,2176]{1,0:T(8,128)(2,1)}, bf16[128,2176]{1,0:T(8,128)(2,1)S(1)}, u32[]{:S(2)}, u32[]{:S(2)}) collective-permute-start(bf16[128,2176]{1,0:T(8,128)(2,1)} %collective-permute-done.1.refs_1_), channel_id=1, source_target_pairs={{0,2},{4,0},{8,4},{12,8},{14,12},{10,14},{6,10},{2,6},{1,3},{5,1},... | collective-permute-start | bytes 1671176 | tf_op jit(solution)/shard_map/ppermute | solution.py:356
  40.6 26.3 %collective-permute-start.13 = (bf16[128,4352]{1,0:T(8,128)(2,1)}, bf16[128,4352]{1,0:T(8,128)(2,1)S(1)}, u32[]{:S(2)}, u32[]{:S(2)}) collective-permute-start(bf16[128,4352]{1,0:T(8,128)(2,1)} %get-tuple-element.124.refs_21_), channel_id=1, source_target_pairs={{0,1},{1,0},{2,3},{3,2},{4,5},{5,4},{6,7},{7,6},{8,9},{9,8},{10,11... | collective-permute-start | bytes 3342344 | tf_op jit(solution)/shard_map/ppermute | solution.py:359
  42.0 23.7 %collective-permute-start.11 = (bf16[128,2048]{1,0:T(8,128)(2,1)}, bf16[128,2048]{1,0:T(8,128)(2,1)}, u32[]{:S(2)}, u32[]{:S(2)}) collective-permute-start(bf16[128,2048]{1,0:T(8,128)(2,1)} %collective-permute-done.6.refs_2_), channel_id=1, source_target_pairs={{0,4},{4,8},{8,12},{12,14},{14,10},{10,6},{6,2},{2,0},{1,5},{5,9},... | collective-permute-start | bytes 1572872 | tf_op jit(solution)/shard_map/ppermute | solution.py:356
  43.6 22.2 %copy-start.7 = (bf16[2304,128]{1,0:T(8,128)(2,1)S(1)}, bf16[2304,128]{1,0:T(8,128)(2,1)}, u32[]{:S(2)}) copy-start(bf16[2304,128]{1,0:T(8,128)(2,1)} %get-tuple-element.109) | copy-start | bytes 1769476
  43.6 22.1 %copy-start.5 = (bf16[64,4352]{1,0:T(8,128)(2,1)}, bf16[64,4352]{1,0:T(8,128)(2,1)S(1)}, u32[]{:S(2)}) copy-start(bf16[64,4352]{1,0:T(8,128)(2,1)S(1)} %collective-permute-done.8.refs_5_.refs_15_.refs_25_) | copy-start | bytes 1671172
  43.6 23.2 %collective-permute-start.12 = (bf16[128,2048]{1,0:T(8,128)(2,1)}, bf16[128,2048]{1,0:T(8,128)(2,1)}, u32[]{:S(2)}, u32[]{:S(2)}) collective-permute-start(bf16[128,2048]{1,0:T(8,128)(2,1)} %collective-permute-done.7.refs_3_), channel_id=1, source_target_pairs={{0,2},{4,0},{8,4},{12,8},{14,12},{10,14},{6,10},{2,6},{1,3},{5,1},... | collective-permute-start | bytes 1572872 | tf_op jit(solution)/shard_map/ppermute | solution.py:356
  53.9 21.0 %collective-permute-start.9 = (bf16[128,2176]{1,0:T(8,128)(2,1)S(1)}, bf16[128,2176]{1,0:T(8,128)(2,1)S(1)}, u32[]{:S(2)}, u32[]{:S(2)}) collective-permute-start(bf16[128,2176]{1,0:T(8,128)(2,1)S(1)} %collective-permute-done.4.refs_0_), channel_id=1, source_target_pairs={{0,4},{4,8},{8,12},{12,14},{14,10},{10,6},{6,2},{2,0},{1,5},{5,9},... | collective-permute-start | bytes 1671176 | tf_op jit(solution)/shard_map/ppermute | solution.py:356
  55.5 21.6 %collective-permute-start.10 = (bf16[128,2176]{1,0:T(8,128)(2,1)S(1)}, bf16[128,2176]{1,0:T(8,128)(2,1)S(1)}, u32[]{:S(2)}, u32[]{:S(2)}) collective-permute-start(bf16[128,2176]{1,0:T(8,128)(2,1)S(1)} %collective-permute-done.5.refs_1_), channel_id=1, source_target_pairs={{0,2},{4,0},{8,4},{12,8},{14,12},{10,14},{6,10},{2,6},{1,3},{5,1},... | collective-permute-start | bytes 1671176 | tf_op jit(solution)/shard_map/ppermute | solution.py:356
  65.8 31.3 %collective-permute-start.18 = (bf16[128,4352]{1,0:T(8,128)(2,1)}, bf16[128,4352]{1,0:T(8,128)(2,1)S(1)}, u32[]{:S(2)}, u32[]{:S(2)}) collective-permute-start(bf16[128,4352]{1,0:T(8,128)(2,1)} %get-tuple-element.142.refs_22_), channel_id=1, source_target_pairs={{0,1},{1,0},{2,3},{3,2},{4,5},{5,4},{6,7},{7,6},{8,9},{9,8},{10,11... | collective-permute-start | bytes 3342344 | tf_op jit(solution)/shard_map/ppermute | solution.py:359
  66.9 15.8 %collective-permute-start.14 = (bf16[64,2048]{1,0:T(8,128)(2,1)S(1)}, bf16[64,2048]{1,0:T(8,128)(2,1)S(1)}, u32[]{:S(2)}, u32[]{:S(2)}) collective-permute-start(bf16[64,2048]{1,0:T(8,128)(2,1)S(1)} %copy-done.25), channel_id=1, source_target_pairs={{0,2},{4,0},{8,4},{12,8},{14,12},{10,14},{6,10},{2,6},{1,3},{5,1},... | collective-permute-start | bytes 786440 | tf_op jit(solution)/shard_map/ppermute | solution.py:356
  67.0 27.1 %copy-start.2 = (bf16[128,4352]{1,0:T(8,128)(2,1)}, bf16[128,4352]{1,0:T(8,128)(2,1)S(1)}, u32[]{:S(2)}) copy-start(bf16[128,4352]{1,0:T(8,128)(2,1)S(1)} %collective-permute-done.13.refs_6_.refs_16_.refs_26_) | copy-start | bytes 3342340
  67.0 17.1 %collective-permute-start.15 = (bf16[64,2048]{1,0:T(8,128)(2,1)S(1)}, bf16[64,2048]{1,0:T(8,128)(2,1)S(1)}, u32[]{:S(2)}, u32[]{:S(2)}) collective-permute-start(bf16[64,2048]{1,0:T(8,128)(2,1)S(1)} %copy-done.24), channel_id=1, source_target_pairs={{0,4},{4,8},{8,12},{12,14},{14,10},{10,6},{6,2},{2,0},{1,5},{5,9},... | collective-permute-start | bytes 786440 | tf_op jit(solution)/shard_map/ppermute | solution.py:356
  74.9 20.6 %collective-permute-start.17 = (bf16[128,2048]{1,0:T(8,128)(2,1)}, bf16[128,2048]{1,0:T(8,128)(2,1)}, u32[]{:S(2)}, u32[]{:S(2)}) collective-permute-start(bf16[128,2048]{1,0:T(8,128)(2,1)} %collective-permute-done.12.refs_3_), channel_id=1, source_target_pairs={{0,2},{4,0},{8,4},{12,8},{14,12},{10,14},{6,10},{2,6},{1,3},{5,1},... | collective-permute-start | bytes 1572872 | tf_op jit(solution)/shard_map/ppermute | solution.py:356
  77.1 26.5 %collective-permute-start.16 = (bf16[128,2176]{1,0:T(8,128)(2,1)S(1)}, bf16[128,2176]{1,0:T(8,128)(2,1)S(1)}, u32[]{:S(2)}, u32[]{:S(2)}) collective-permute-start(bf16[128,2176]{1,0:T(8,128)(2,1)S(1)} %collective-permute-done.9.refs_0_), channel_id=1, source_target_pairs={{0,4},{4,8},{8,12},{12,14},{14,10},{10,6},{6,2},{2,0},{1,5},{5,9},... | collective-permute-start | bytes 1671176 | tf_op jit(solution)/shard_map/ppermute | solution.py:356
  82.7 31.5 %collective-permute-start.19 = (bf16[64,2048]{1,0:T(8,128)(2,1)}, bf16[64,2048]{1,0:T(8,128)(2,1)S(1)}, u32[]{:S(2)}, u32[]{:S(2)}) collective-permute-start(bf16[64,2048]{1,0:T(8,128)(2,1)} %get-tuple-element.146), channel_id=1, source_target_pairs={{0,6},{4,2},{8,0},{12,4},{14,8},{10,12},{6,14},{2,10},{1,7},{5,3},... | collective-permute-start | bytes 786440 | tf_op jit(solution)/shard_map/ppermute | solution.py:356
  94.1 30.6 %collective-permute-start.21 = (bf16[128,4352]{1,0:T(8,128)(2,1)}, bf16[128,4352]{1,0:T(8,128)(2,1)S(1)}, u32[]{:S(2)}, u32[]{:S(2)}) collective-permute-start(bf16[128,4352]{1,0:T(8,128)(2,1)} %get-tuple-element.150.refs_23_), channel_id=1, source_target_pairs={{0,1},{1,0},{2,3},{3,2},{4,5},{5,4},{6,7},{7,6},{8,9},{9,8},{10,11... | collective-permute-start | bytes 3342344 | tf_op jit(solution)/shard_map/ppermute | solution.py:359
  95.5 18.7 %collective-permute-start.20 = (bf16[64,2048]{1,0:T(8,128)(2,1)S(1)}, bf16[64,2048]{1,0:T(8,128)(2,1)S(1)}, u32[]{:S(2)}, u32[]{:S(2)}) collective-permute-start(bf16[64,2048]{1,0:T(8,128)(2,1)S(1)} %copy-done.28), channel_id=1, source_target_pairs={{0,8},{4,12},{8,14},{12,10},{14,6},{10,2},{6,0},{2,4},{1,9},{5,13}... | collective-permute-start | bytes 786440 | tf_op jit(solution)/shard_map/ppermute | solution.py:356
  97.1 17.1 %copy-start.3 = (bf16[128,4352]{1,0:T(8,128)(2,1)}, bf16[128,4352]{1,0:T(8,128)(2,1)S(1)}, u32[]{:S(2)}) copy-start(bf16[128,4352]{1,0:T(8,128)(2,1)S(1)} %collective-permute-done.18.refs_7_.refs_17_.refs_27_) | copy-start | bytes 3342340
  97.1 50.3 %collective-permute-start.25 = (bf16[64,2048]{1,0:T(8,128)(2,1)S(1)}, bf16[64,2048]{1,0:T(8,128)(2,1)S(1)}, u32[]{:S(2)}, u32[]{:S(2)}) collective-permute-start(bf16[64,2048]{1,0:T(8,128)(2,1)S(1)} %copy-done.27), channel_id=1, source_target_pairs={{0,12},{4,14},{8,10},{12,6},{14,2},{10,0},{6,4},{2,8},{1,13},{5,15... | collective-permute-start | bytes 786440 | tf_op jit(solution)/shard_map/ppermute | solution.py:356
  103.6 44.1 %collective-permute-start.26 = (bf16[64,2048]{1,0:T(8,128)(2,1)S(1)}, bf16[64,2048]{1,0:T(8,128)(2,1)S(1)}, u32[]{:S(2)}, u32[]{:S(2)}) collective-permute-start(bf16[64,2048]{1,0:T(8,128)(2,1)S(1)} %copy-done.26), channel_id=1, source_target_pairs={{0,10},{4,6},{8,2},{12,0},{14,4},{10,8},{6,12},{2,14},{1,11},{5,7}... | collective-permute-start | bytes 786440 | tf_op jit(solution)/shard_map/ppermute | solution.py:356
  114.2 33.5 %collective-permute-start.27 = (bf16[64,2048]{1,0:T(8,128)(2,1)}, bf16[64,2048]{1,0:T(8,128)(2,1)S(1)}, u32[]{:S(2)}, u32[]{:S(2)}) collective-permute-start(bf16[64,2048]{1,0:T(8,128)(2,1)} %get-tuple-element.173), channel_id=1, source_target_pairs={{0,14},{4,10},{8,6},{12,2},{14,0},{10,4},{6,8},{2,12},{1,15},{5,11... | collective-permute-start | bytes 786440 | tf_op jit(solution)/shard_map/ppermute | solution.py:356
  119.8 15.0 %collective-permute-start.24 = (bf16[64,4352]{1,0:T(8,128)(2,1)}, bf16[64,4352]{1,0:T(8,128)(2,1)S(1)}, u32[]{:S(2)}, u32[]{:S(2)}) collective-permute-start(bf16[64,4352]{1,0:T(8,128)(2,1)} %get-tuple-element.169.refs_24_), channel_id=1, source_target_pairs={{0,1},{1,0},{2,3},{3,2},{4,5},{5,4},{6,7},{7,6},{8,9},{9,8},{10,11... | collective-permute-start | bytes 1671176 | tf_op jit(solution)/shard_map/ppermute | solution.py:359
  124.7 23.0 %collective-permute-start.22 = (bf16[288,256]{1,0:T(8,128)(2,1)S(1)}, bf16[288,256]{1,0:T(8,128)(2,1)S(1)}, u32[]{:S(2)}, u32[]{:S(2)}) collective-permute-start(bf16[288,256]{1,0:T(8,128)(2,1)S(1)} %get-tuple-element.158), channel_id=1, source_target_pairs={{0,4},{4,8},{8,12},{12,14},{14,10},{10,6},{6,2},{2,0},{1,5},{5,9},... | collective-permute-start | bytes 442376 | tf_op jit(solution)/shard_map/ppermute | solution.py:356
  134.8 12.9 %collective-permute-start.23 = (bf16[288,256]{1,0:T(8,128)(2,1)S(1)}, bf16[288,256]{1,0:T(8,128)(2,1)S(1)}, u32[]{:S(2)}, u32[]{:S(2)}) collective-permute-start(bf16[288,256]{1,0:T(8,128)(2,1)S(1)} %get-tuple-element.159), channel_id=1, source_target_pairs={{0,2},{4,0},{8,4},{12,8},{14,12},{10,14},{6,10},{2,6},{1,3},{5,1},... | collective-permute-start | bytes 442376 | tf_op jit(solution)/shard_map/ppermute | solution.py:356
  147.4 12.2 %copy-start.14 = (bf16[64,2048]{1,0:T(8,128)(2,1)}, bf16[64,2048]{1,0:T(8,128)(2,1)S(1)}, u32[]{:S(2)}) copy-start(bf16[64,2048]{1,0:T(8,128)(2,1)S(1)} %collective-permute-done.25.refs_3_) | copy-start | bytes 786436
  147.4 29.1 %collective-permute-start.41 = (bf16[512,2048]{1,0:T(8,128)(2,1)}, bf16[512,2048]{1,0:T(8,128)(2,1)S(1)}, u32[]{:S(2)}, u32[]{:S(2)}) collective-permute-start(bf16[512,2048]{1,0:T(8,128)(2,1)} %get-tuple-element.206), channel_id=1, source_target_pairs={{0,1},{1,0},{2,3},{3,2},{4,5},{5,4},{6,7},{7,6},{8,9},{9,8},{10,11... | collective-permute-start | bytes 6291464 | tf_op jit(solution)/shard_map/ppermute | solution.py:359
  147.8 6.7 %collective-permute-start.37 = (bf16[288,256]{1,0:T(8,128)(2,1)S(1)}, bf16[288,256]{1,0:T(8,128)(2,1)S(1)}, u32[]{:S(2)}, u32[]{:S(2)}) collective-permute-start(bf16[288,256]{1,0:T(8,128)(2,1)S(1)} %broadcast_select_fusion.2), channel_id=1, source_target_pairs={{0,2},{4,0},{8,4},{12,8},{14,12},{10,14},{6,10},{2,6},{1,3},{5,1},... | collective-permute-start | bytes 442376 | tf_op jit(solution)/shard_map/ppermute | solution.py:356
  149.6 7.7 %collective-permute-start.34 = (bf16[288,256]{1,0:T(8,128)(2,1)S(1)}, bf16[288,256]{1,0:T(8,128)(2,1)S(1)}, u32[]{:S(2)}, u32[]{:S(2)}) collective-permute-start(bf16[288,256]{1,0:T(8,128)(2,1)S(1)} %get-tuple-element.183), channel_id=1, source_target_pairs={{0,2},{4,0},{8,4},{12,8},{14,12},{10,14},{6,10},{2,6},{1,3},{5,1},... | collective-permute-start | bytes 442376 | tf_op jit(solution)/shard_map/ppermute | solution.py:356
  150.6 8.9 %collective-permute-start.31 = (bf16[288,256]{1,0:T(8,128)(2,1)S(1)}, bf16[288,256]{1,0:T(8,128)(2,1)S(1)}, u32[]{:S(2)}, u32[]{:S(2)}) collective-permute-start(bf16[288,256]{1,0:T(8,128)(2,1)S(1)} %get-tuple-element.180), channel_id=1, source_target_pairs={{0,4},{4,8},{8,12},{12,14},{14,10},{10,6},{6,2},{2,0},{1,5},{5,9},... | collective-permute-start | bytes 442376 | tf_op jit(solution)/shard_map/ppermute | solution.py:356
  151.6 8.0 %collective-permute-start.28 = (bf16[288,256]{1,0:T(8,128)(2,1)S(1)}, bf16[288,256]{1,0:T(8,128)(2,1)S(1)}, u32[]{:S(2)}, u32[]{:S(2)}) collective-permute-start(bf16[288,256]{1,0:T(8,128)(2,1)S(1)} %broadcast_select_fusion.9), channel_id=1, source_target_pairs={{0,4},{4,8},{8,12},{12,14},{14,10},{10,6},{6,2},{2,0},{1,5},{5,9},... | collective-permute-start | bytes 442376 | tf_op jit(solution)/shard_map/ppermute | solution.py:356
  154.5 7.3 %collective-permute-start.38 = (bf16[288,256]{1,0:T(8,128)(2,1)S(1)}, bf16[288,256]{1,0:T(8,128)(2,1)S(1)}, u32[]{:S(2)}, u32[]{:S(2)}) collective-permute-start(bf16[288,256]{1,0:T(8,128)(2,1)S(1)} %broadcast_select_fusion.1), channel_id=1, source_target_pairs={{0,2},{4,0},{8,4},{12,8},{14,12},{10,14},{6,10},{2,6},{1,3},{5,1},... | collective-permute-start | bytes 442376 | tf_op jit(solution)/shard_map/ppermute | solution.py:356
  157.3 6.4 %collective-permute-start.35 = (bf16[288,256]{1,0:T(8,128)(2,1)S(1)}, bf16[288,256]{1,0:T(8,128)(2,1)S(1)}, u32[]{:S(2)}, u32[]{:S(2)}) collective-permute-start(bf16[288,256]{1,0:T(8,128)(2,1)S(1)} %broadcast_select_fusion.4), channel_id=1, source_target_pairs={{0,2},{4,0},{8,4},{12,8},{14,12},{10,14},{6,10},{2,6},{1,3},{5,1},... | collective-permute-start | bytes 442376 | tf_op jit(solution)/shard_map/ppermute | solution.py:356
  159.5 6.8 %collective-permute-start.32 = (bf16[288,256]{1,0:T(8,128)(2,1)S(1)}, bf16[288,256]{1,0:T(8,128)(2,1)S(1)}, u32[]{:S(2)}, u32[]{:S(2)}) collective-permute-start(bf16[288,256]{1,0:T(8,128)(2,1)S(1)} %broadcast_select_fusion.6), channel_id=1, source_target_pairs={{0,4},{4,8},{8,12},{12,14},{14,10},{10,6},{6,2},{2,0},{1,5},{5,9},... | collective-permute-start | bytes 442376 | tf_op jit(solution)/shard_map/ppermute | solution.py:356
  159.6 8.3 %collective-permute-start.29 = (bf16[288,256]{1,0:T(8,128)(2,1)S(1)}, bf16[288,256]{1,0:T(8,128)(2,1)S(1)}, u32[]{:S(2)}, u32[]{:S(2)}) collective-permute-start(bf16[288,256]{1,0:T(8,128)(2,1)S(1)} %broadcast_select_fusion.8), channel_id=1, source_target_pairs={{0,4},{4,8},{8,12},{12,14},{14,10},{10,6},{6,2},{2,0},{1,5},{5,9},... | collective-permute-start | bytes 442376 | tf_op jit(solution)/shard_map/ppermute | solution.py:356
  161.8 10.0 %collective-permute-start.39 = (bf16[288,256]{1,0:T(8,128)(2,1)S(1)}, bf16[288,256]{1,0:T(8,128)(2,1)S(1)}, u32[]{:S(2)}, u32[]{:S(2)}) collective-permute-start(bf16[288,256]{1,0:T(8,128)(2,1)S(1)} %broadcast_select_fusion), channel_id=1, source_target_pairs={{0,2},{4,0},{8,4},{12,8},{14,12},{10,14},{6,10},{2,6},{1,3},{5,1},... | collective-permute-start | bytes 442376 | tf_op jit(solution)/shard_map/ppermute | solution.py:356
  163.8 8.0 %collective-permute-start.36 = (bf16[288,256]{1,0:T(8,128)(2,1)S(1)}, bf16[288,256]{1,0:T(8,128)(2,1)S(1)}, u32[]{:S(2)}, u32[]{:S(2)}) collective-permute-start(bf16[288,256]{1,0:T(8,128)(2,1)S(1)} %broadcast_select_fusion.3), channel_id=1, source_target_pairs={{0,2},{4,0},{8,4},{12,8},{14,12},{10,14},{6,10},{2,6},{1,3},{5,1},... | collective-permute-start | bytes 442376 | tf_op jit(solution)/shard_map/ppermute | solution.py:356
  166.3 5.8 %collective-permute-start.33 = (bf16[288,256]{1,0:T(8,128)(2,1)S(1)}, bf16[288,256]{1,0:T(8,128)(2,1)S(1)}, u32[]{:S(2)}, u32[]{:S(2)}) collective-permute-start(bf16[288,256]{1,0:T(8,128)(2,1)S(1)} %broadcast_select_fusion.5), channel_id=1, source_target_pairs={{0,4},{4,8},{8,12},{12,14},{14,10},{10,6},{6,2},{2,0},{1,5},{5,9},... | collective-permute-start | bytes 442376 | tf_op jit(solution)/shard_map/ppermute | solution.py:356
  167.9 5.9 %collective-permute-start.30 = (bf16[288,256]{1,0:T(8,128)(2,1)S(1)}, bf16[288,256]{1,0:T(8,128)(2,1)}, u32[]{:S(2)}, u32[]{:S(2)}) collective-permute-start(bf16[288,256]{1,0:T(8,128)(2,1)S(1)} %broadcast_select_fusion.7), channel_id=1, source_target_pairs={{0,4},{4,8},{8,12},{12,14},{14,10},{10,6},{6,2},{2,0},{1,5},{5,9},... | collective-permute-start | bytes 442376 | tf_op jit(solution)/shard_map/ppermute | solution.py:356
  174.9 1.6 collective-permute-start.40
  (23 other events, 139.3 us)

commit v12 on v11

--- a/solution.py
+++ b/solution.py
@@ -400,7 +400,6 @@
         turned += turn
         held = following
     (back_behind, back_ahead), other = late[half - 1]
-    turned[-1], late[half - 2] = lax.optimization_barrier((turned[-1], late[half - 2]))
 
     taken = 3 * units // experts
     ring_hot = to_ring(hottest, experts)
@@ -426,8 +425,10 @@
     expert_grad = expert_gradient(units, scal, mine, packs, others)
     chunks = {distance: halves(distance) for distance in range(1 - half, half)}
     (back_far,) = late[half][0]
-    far, expert_grad, back_ahead, back_behind, back_far, chunks = lax.optimization_barrier(
-        (far, expert_grad, back_ahead, back_behind, back_far, chunks)
+    far, expert_grad, back_ahead, back_behind, chunks, late[half - 2] = (
+        lax.optimization_barrier(
+            (far, expert_grad, back_ahead, back_behind, chunks, late[half - 2])
+        )
     )
     ahead, behind = [far[0], None], [None, far[1]]
 

time: 180 us -> 180 us (level)
  starting transfers between devices: 61.7 us -> 52.6 us
  waiting for transfers between devices: 38.8 us -> 45.4 us
  local copies, waits for them, and re-layouts: 2.98 us -> 4.98 us
    ppermute x35, starting transfers between devices: 61.1 us -> 52.2 us  [shift(): return lax.ppermute(block, 'expert', pairs)]
    ppermute x35, waiting for transfers between devices: 37.2 us -> 43.8 us  [shift(): return lax.ppermute(block, 'expert', pairs)]
  transfers between devices with their start and end apart: 42 -> 42, of which waited for: 16 -> 17; matrix products, arithmetic and copies ran while one was open for 2% -> 3% of each run, Pallas kernels for 39% -> 39%
where the time goes in v12:
time: 180 us; the launch traced here: 179 us
  Pallas kernels  71.5 us (40%)
  starting transfers between devices  52.6 us (29%)
  waiting for transfers between devices  45.4 us (25%)
  local copies, waits for them, and re-layouts  4.98 us (3%)
  other arithmetic  2.51 us (1%)
  between operations  1.96 us (1%)
    ppermute x35, starting transfers between devices, shift(): return lax.ppermute(block, 'expert', pairs)  52.2 us
    pallas_call x5, Pallas kernels, run_step(): pl.pallas_call(functools.partial(step_kernel, steps, fanout, capacity, jo...  48.7 us
    ppermute x35, waiting for transfers between devices, shift(): return lax.ppermute(block, 'expert', pairs)  43.8 us
    pallas_call x1, Pallas kernels, expert_gradient(): pl.pallas_call(functools.partial(gradient_kernel, units, count), grid=(ti...  10.8 us
    pallas_call x1, Pallas kernels, ordered(): pl.pallas_call(functools.partial(order_kernel, plan, experts, capacity),...  4.55 us
  transfers between devices with their start and end apart: 42, of which 17 were waited for; matrix products, arithmetic and copies ran while one was open for 3% of the time, Pallas kernels for 39%

profile of v12, /device:TPU:0, one launch (start us, length us, event | category | flops | bytes accessed | tf_op | source)
XLA Modules:
  0.0 178.9 jit_solution(12080597350788348254)
XLA Ops:
  0.6 3.1 %collective-permute-start.2 = (bf16[128,2048]{1,0:T(8,128)(2,1)}, bf16[128,2048]{1,0:T(8,128)(2,1)S(1)}, u32[]{:S(2)}, u32[]{:S(2)}) collective-permute-start(bf16[128,2048]{1,0:T(8,128)(2,1)} %refs_1_.1), channel_id=1, source_target_pairs={{0,4},{4,8},{8,12},{12,14},{14,10},{10,6},{6,2},{2,0},{1,5},{5,9},... | collective-permute-start | bytes 1572872 | tf_op jit(solution)/shard_map/ppermute | solution.py:356
  3.7 2.0 %ring_message.1 = (bf16[128,2176]{1,0:T(8,128)(2,1)}, bf16[128,128]{1,0:T(8,128)(2,1)}) custom-call(bf16[128,2048]{1,0:T(8,128)(2,1)} %tokens.1, s32[2,128]{1,0:T(2,128)} %bitcast.17, f32[2,128]{1,0:T(2,128)} %bitcast.18, f32[1,128]{1,0:T(1,128)} %bitcast.19, s32[1,128]{1,0:T(1,128)} %bitcast.20), custom_call_target="tpu_custom_call" | custom-call | bytes 1048576 | tf_op jit(solution)/shard_map/ring_message/pallas_call | solution.py:262
  5.7 2.0 %collective-permute-start = (bf16[128,2176]{1,0:T(8,128)(2,1)}, bf16[128,2176]{1,0:T(8,128)(2,1)S(1)}, u32[]{:S(2)}, u32[]{:S(2)}) collective-permute-start(bf16[128,2176]{1,0:T(8,128)(2,1)} %get-tuple-element.102.refs_0_), channel_id=1, source_target_pairs={{0,4},{4,8},{8,12},{12,14},{14,10},{10,6},{6,2},{2,0},{1,5},{5,9},... | collective-permute-start | bytes 1671176 | tf_op jit(solution)/shard_map/ppermute | solution.py:356
  9.0 9.3 %expert_step.5 = (bf16[64,2048]{1,0:T(8,128)(2,1)}, bf16[64,4352]{1,0:T(8,128)(2,1)}, bf16[64,4096]{1,0:T(8,128)(2,1)}, bf16[64,2048]{1,0:T(8,128)(2,1)}) custom-call(s32[3]{0:T(128)} %pad_add_fusion.scal, bf16[128,2176]{1,0:T(8,128)(2,1)} %get-tuple-element.102.refs_0_, bf16[128,2048]{1,0:T(8,128)(2,1)} %refs_1_.1, bf16[2048,1536]{1,0:T(8,128)(2,1)} %bitcast.21, ...), custom_call_target="tpu_custom_call" | custom-call | flops 4026531840 | bytes 9437184 | tf_op jit(solution)/shard_map/expert_step/pallas_call | solution.py:151
  18.9 1.6 collective-permute-start.6
  20.9 7.7 %collective-permute-done.refs_0_ = bf16[128,2176]{1,0:T(8,128)(2,1)S(1)} collective-permute-done((bf16[128,2176]{1,0:T(8,128)(2,1)}, bf16[128,2176]{1,0:T(8,128)(2,1)S(1)}, u32[]{:S(2)}, u32[]{:S(2)}) %collective-permute-start) | collective-permute-done | bytes 557088 | tf_op jit(solution)/shard_map/ppermute | solution.py:356
  28.6 2.1 %collective-permute-start.4 = (bf16[128,2176]{1,0:T(8,128)(2,1)S(1)}, bf16[128,2176]{1,0:T(8,128)(2,1)S(1)}, u32[]{:S(2)}, u32[]{:S(2)}) collective-permute-start(bf16[128,2176]{1,0:T(8,128)(2,1)S(1)} %collective-permute-done.refs_0_), channel_id=1, source_target_pairs={{0,4},{4,8},{8,12},{12,14},{14,10},{10,6},{6,2},{2,0},{1,5},{5,9},... | collective-permute-start | bytes 1671176 | tf_op jit(solution)/shard_map/ppermute | solution.py:356
  30.8 9.8 %expert_step.6 = (bf16[128,2048]{1,0:T(8,128)(2,1)}, bf16[128,4352]{1,0:T(8,128)(2,1)}, bf16[128,4096]{1,0:T(8,128)(2,1)}, bf16[64,2048]{1,0:T(8,128)(2,1)}, bf1...) custom-call(s32[3]{0:T(128)} %pad_add_fusion.scal, bf16[128,2176]{1,0:T(8,128)(2,1)} %copy-done.18, ...), custom_call_target="tpu_custom_call" | custom-call | flops 4026531840 | bytes 9437184 | tf_op jit(solution)/shard_map/expert_step/pallas_call | solution.py:151
  40.8 1.3 collective-permute-done.7.refs_3_
  42.0 1.6 collective-permute-start.11
  44.1 7.6 %collective-permute-done.4.refs_0_ = bf16[128,2176]{1,0:T(8,128)(2,1)S(1)} collective-permute-done((bf16[128,2176]{1,0:T(8,128)(2,1)S(1)}, bf16[128,2176]{1,0:T(8,128)(2,1)S(1)}, u32[]{:S(2)}, u32[]{:S(2)}) %collective-permute-start.4) | collective-permute-done | bytes 557088 | tf_op jit(solution)/shard_map/ppermute | solution.py:356
  51.7 2.1 %collective-permute-done.5.refs_1_ = bf16[128,2176]{1,0:T(8,128)(2,1)S(1)} collective-permute-done((bf16[128,2176]{1,0:T(8,128)(2,1)}, bf16[128,2176]{1,0:T(8,128)(2,1)S(1)}, u32[]{:S(2)}, u32[]{:S(2)}) %collective-permute-start.5) | collective-permute-done | bytes 557088 | tf_op jit(solution)/shard_map/ppermute | solution.py:356
  53.9 1.6 collective-permute-start.9
  55.9 9.8 %expert_step.7 = (bf16[128,2048]{1,0:T(8,128)(2,1)}, bf16[128,4352]{1,0:T(8,128)(2,1)}, bf16[128,4096]{1,0:T(8,128)(2,1)}, bf16[64,2048]{1,0:T(8,128)(2,1)}, bf1...) custom-call(s32[3]{0:T(128)} %pad_add_fusion.scal, bf16[128,2176]{1,0:T(8,128)(2,1)} %copy-done.16, ...), custom_call_target="tpu_custom_call" | custom-call | flops 4026531840 | bytes 9437184 | tf_op jit(solution)/shard_map/expert_step/pallas_call | solution.py:151
  65.9 0.9 copy-done.8
  67.0 2.1 %collective-permute-start.15 = (bf16[64,2048]{1,0:T(8,128)(2,1)S(1)}, bf16[64,2048]{1,0:T(8,128)(2,1)S(1)}, u32[]{:S(2)}, u32[]{:S(2)}) collective-permute-start(bf16[64,2048]{1,0:T(8,128)(2,1)S(1)} %copy-done.23), channel_id=1, source_target_pairs={{0,4},{4,8},{8,12},{12,14},{14,10},{10,6},{6,2},{2,0},{1,5},{5,9},... | collective-permute-start | bytes 786440 | tf_op jit(solution)/shard_map/ppermute | solution.py:356
  69.1 5.8 %collective-permute-done.9.refs_0_ = bf16[128,2176]{1,0:T(8,128)(2,1)S(1)} collective-permute-done((bf16[128,2176]{1,0:T(8,128)(2,1)S(1)}, bf16[128,2176]{1,0:T(8,128)(2,1)S(1)}, u32[]{:S(2)}, u32[]{:S(2)}) %collective-permute-start.9) | collective-permute-done | bytes 557088 | tf_op jit(solution)/shard_map/ppermute | solution.py:356
  74.9 2.1 %collective-permute-start.17 = (bf16[128,2048]{1,0:T(8,128)(2,1)}, bf16[128,2048]{1,0:T(8,128)(2,1)}, u32[]{:S(2)}, u32[]{:S(2)}) collective-permute-start(bf16[128,2048]{1,0:T(8,128)(2,1)} %collective-permute-done.12.refs_3_), channel_id=1, source_target_pairs={{0,2},{4,0},{8,4},{12,8},{14,12},{10,14},{6,10},{2,6},{1,3},{5,1},... | collective-permute-start | bytes 1572872 | tf_op jit(solution)/shard_map/ppermute | solution.py:356
  77.1 1.6 collective-permute-start.16
  78.7 4.0 %collective-permute-done.14.refs_7_ = bf16[64,2048]{1,0:T(8,128)(2,1)S(1)} collective-permute-done((bf16[64,2048]{1,0:T(8,128)(2,1)S(1)}, bf16[64,2048]{1,0:T(8,128)(2,1)S(1)}, u32[]{:S(2)}, u32[]{:S(2)}) %collective-permute-start.14) | collective-permute-done | bytes 262176 | tf_op jit(solution)/shard_map/ppermute | solution.py:356
  82.7 1.4 collective-permute-start.25
  84.1 10.0 %expert_step.8 = (bf16[128,2048]{1,0:T(8,128)(2,1)}, bf16[128,4352]{1,0:T(8,128)(2,1)}, bf16[128,4096]{1,0:T(8,128)(2,1)}, bf16[64,2048]{1,0:T(8,128)(2,1)}, bf1...) custom-call(s32[3]{0:T(128)} %pad_add_fusion.scal, bf16[128,2176]{1,0:T(8,128)(2,1)} %copy-done.19, ...), custom_call_target="tpu_custom_call" | custom-call | flops 4026531840 | bytes 9437184 | tf_op jit(solution)/shard_map/expert_step/pallas_call | solution.py:151
  94.2 1.2 constant_dynamic-slice_fusion.1
  95.5 1.6 collective-permute-start.26
  97.0 6.7 %collective-permute-start.23 = (bf16[64,2048]{1,0:T(8,128)(2,1)S(1)}, bf16[64,2048]{1,0:T(8,128)(2,1)S(1)}, u32[]{:S(2)}, u32[]{:S(2)}) collective-permute-start(bf16[64,2048]{1,0:T(8,128)(2,1)S(1)} %copy-done.28), channel_id=1, source_target_pairs={{0,12},{4,14},{8,10},{12,6},{14,2},{10,0},{6,4},{2,8},{1,13},{5,15... | collective-permute-start | bytes 786440 | tf_op jit(solution)/shard_map/ppermute | solution.py:356
  104.6 9.7 %expert_step.9 = (bf16[64,2048]{1,0:T(8,128)(2,1)}, bf16[64,4352]{1,0:T(8,128)(2,1)}, bf16[64,4096]{1,0:T(8,128)(2,1)}, bf16[64,2048]{1,0:T(8,128)(2,1)}, bf16[2304,128]{1,0:T(8,128)(2,1)}) custom-call(s32[3]{0:T(128)} %pad_add_fusion.scal, bf16[128,2176]{1,0:T(8,128)(2,1)} %copy-done.21, bf16[128,2048]{1,0:T(8,128)(2,1)} %collective-permute-done.17.refs_1_, ...), custom_call_target="tpu_custom_call" | custom-call | flops 4026531840 | bytes 9437184 | tf_op jit(solution)/shard_map/expert_step/pallas_call | solution.py:151
  114.4 1.2 constant_dynamic-slice_fusion
  115.8 4.5 %hot_rows_ordered.1 = (bf16[512,2048]{1,0:T(8,128)(2,1)}, bf16[512,2048]{1,0:T(8,128)(2,1)}) custom-call(s32[3]{0:T(128)} %pad_add_fusion.scal, bf16[64,4096]{1,0:T(8,128)(2,1)} %get-tuple-element.144.refs_0_, bf16[128,4096]{1,0:T(8,128)(2,1)} %get-tuple-element.145.refs_1_, bf16[128,4096]{1,0:T(8,128)(2,1)} %get-tuple-element.146.refs_2_, ...), custom_call_target="tpu_custom_call" | custom-call | bytes 8388608 | tf_op jit(solution)/shard_map/hot_rows_ordered/pallas_call | solution.py:290
  120.6 2.9 %collective-permute-start.21 = (bf16[288,256]{1,0:T(8,128)(2,1)S(1)}, bf16[288,256]{1,0:T(8,128)(2,1)S(1)}, u32[]{:S(2)}, u32[]{:S(2)}) collective-permute-start(bf16[288,256]{1,0:T(8,128)(2,1)S(1)} %get-tuple-element.152), channel_id=1, source_target_pairs={{0,2},{4,0},{8,4},{12,8},{14,12},{10,14},{6,10},{2,6},{1,3},{5,1},... | collective-permute-start | bytes 442376 | tf_op jit(solution)/shard_map/ppermute | solution.py:356
  123.6 10.8 %expert_gradient.1 = f32[1,1024,2304]{2,1,0:T(8,128)} custom-call(s32[3]{0:T(128)} %pad_add_fusion.scal, bf16[64,2048]{1,0:T(8,128)(2,1)} %get-tuple-element.153.refs_0_.refs_10_, bf16[128,2048]{1,0:T(8,128)(2,1)} %get-tuple-element.154.refs_1_.refs_11_, bf16[128,2048]{1,0:T(8,128)(2,1)} %get-tuple-element.155.refs_2_.refs_12_, ...), custom_call_target="tpu_custom_call" | custom-call | flops 4831838208 | bytes 14155776 | tf_op jit(solution)/shard_map/expert_gradient/pallas_call | solution.py:226
  134.4 2.4 %collective-permute-start.39 = (bf16[64,2048]{1,0:T(8,128)(2,1)S(1)}, bf16[64,2048]{1,0:T(8,128)(2,1)S(1)}, u32[]{:S(2)}, u32[]{:S(2)}) collective-permute-start(bf16[64,2048]{1,0:T(8,128)(2,1)S(1)} %copy-done.25), channel_id=1, source_target_pairs={{0,14},{4,10},{8,6},{12,2},{14,0},{10,4},{6,8},{2,12},{1,15},{5,11... | collective-permute-start | bytes 786440 | tf_op jit(solution)/shard_map/ppermute | solution.py:356
  136.8 1.0 collective-permute-done.21
  137.8 1.0 collective-permute-start.36
  138.9 2.0 %collective-permute-start.30 = (bf16[288,256]{1,0:T(8,128)(2,1)S(1)}, bf16[288,256]{1,0:T(8,128)(2,1)S(1)}, u32[]{:S(2)}, u32[]{:S(2)}) collective-permute-start(bf16[288,256]{1,0:T(8,128)(2,1)S(1)} %get-tuple-element.173), channel_id=1, source_target_pairs={{0,4},{4,8},{8,12},{12,14},{14,10},{10,6},{6,2},{2,0},{1,5},{5,9},... | collective-permute-start | bytes 442376 | tf_op jit(solution)/shard_map/ppermute | solution.py:356
  140.9 7.9 %collective-permute-done.36 = bf16[288,256]{1,0:T(8,128)(2,1)S(1)} collective-permute-done((bf16[288,256]{1,0:T(8,128)(2,1)S(1)}, bf16[288,256]{1,0:T(8,128)(2,1)S(1)}, u32[]{:S(2)}, u32[]{:S(2)}) %collective-permute-start.36) | collective-permute-done | bytes 147488 | tf_op jit(solution)/shard_map/ppermute | solution.py:356
  148.8 5.8 %collective-permute-start.27 = (bf16[288,256]{1,0:T(8,128)(2,1)S(1)}, bf16[288,256]{1,0:T(8,128)(2,1)S(1)}, u32[]{:S(2)}, u32[]{:S(2)}) collective-permute-start(bf16[288,256]{1,0:T(8,128)(2,1)S(1)} %broadcast_select_fusion.9), channel_id=1, source_target_pairs={{0,4},{4,8},{8,12},{12,14},{14,10},{10,6},{6,2},{2,0},{1,5},{5,9},... | collective-permute-start | bytes 442376 | tf_op jit(solution)/shard_map/ppermute | solution.py:356
  154.7 1.5 collective-permute-start.34
  156.3 1.3 collective-permute-done.27
  157.5 2.5 %collective-permute-start.31 = (bf16[288,256]{1,0:T(8,128)(2,1)S(1)}, bf16[288,256]{1,0:T(8,128)(2,1)S(1)}, u32[]{:S(2)}, u32[]{:S(2)}) collective-permute-start(bf16[288,256]{1,0:T(8,128)(2,1)S(1)} %broadcast_select_fusion.6), channel_id=1, source_target_pairs={{0,4},{4,8},{8,12},{12,14},{14,10},{10,6},{6,2},{2,0},{1,5},{5,9},... | collective-permute-start | bytes 442376 | tf_op jit(solution)/shard_map/ppermute | solution.py:356
  160.1 1.3 collective-permute-done.37
  161.3 1.7 collective-permute-start.28
  163.7 0.9 collective-permute-start.35
  165.3 1.3 collective-permute-done.28
  166.6 2.1 %collective-permute-start.32 = (bf16[288,256]{1,0:T(8,128)(2,1)}, bf16[288,256]{1,0:T(8,128)(2,1)S(1)}, u32[]{:S(2)}, u32[]{:S(2)}) collective-permute-start(bf16[288,256]{1,0:T(8,128)(2,1)} %broadcast_select_fusion.5), channel_id=1, source_target_pairs={{0,4},{4,8},{8,12},{12,14},{14,10},{10,6},{6,2},{2,0},{1,5},{5,9},... | collective-permute-start | bytes 442376 | tf_op jit(solution)/shard_map/ppermute | solution.py:356
  170.1 3.2 %token_sum.1 = bf16[128,2048]{1,0:T(8,128)(2,1)} custom-call(s32[3]{0:T(128)} %pad_add_fusion.scal, bf16[128,128]{1,0:T(8,128)(2,1)} %get-tuple-element.181.meta, bf16[64,2048]{1,0:T(8,128)(2,1)} %get-tuple-element.182.refs_0_, bf16[64,2048]{1,0:T(8,128)(2,1)} %copy-done.10, bf16[64,2048]{1,0:T(8,128)(2,1)} %copy-done.12, bf16[64,2048]{1,0:T(8,128)(2,1)} %copy-done.13, ...), custom_call_target="tpu_custom_call" | custom-call | flops 268435456 | bytes 2097152 | tf_op jit(solution)/shard_map/token_sum/pallas_call | solution.py:186
  173.3 1.6 collective-permute-done.29
  175.0 1.6 collective-permute-done.40.theirs
  176.6 2.3 %shadow_gradient.1 = f32[288,1024]{1,0:T(8,128)} custom-call(s32[3]{0:T(128)S(1)} %copy-done.1, bf16[288,512]{1,0:T(8,128)(2,1)S(1)} %pad_maximum_fusion.mine, bf16[288,512]{1,0:T(8,128)(2,1)S(1)} %collective-permute-done.40.theirs, bf16[512,2048]{1,0:T(8,128)(2,1)S(1)} %copy-done, bf16[512,2048]{1,0:T(8,128)(2,1)S(1)} %collective-permute-done.41.hot_theirs), custom_call_target="tpu_custom_call" | custom-call | flops 603979776 | bytes 2097152 | tf_op jit(solution)/shard_map/shadow_gradient/pallas_call | solution.py:329
  (130 shorter events, 7.6 us)
Async XLA Ops:
  0.6 17.8 %collective-permute-start.2 = (bf16[128,2048]{1,0:T(8,128)(2,1)}, bf16[128,2048]{1,0:T(8,128)(2,1)S(1)}, u32[]{:S(2)}, u32[]{:S(2)}) collective-permute-start(bf16[128,2048]{1,0:T(8,128)(2,1)} %refs_1_.1), channel_id=1, source_target_pairs={{0,4},{4,8},{8,12},{12,14},{14,10},{10,6},{6,2},{2,0},{1,5},{5,9},... | collective-permute-start | bytes 1572872 | tf_op jit(solution)/shard_map/ppermute | solution.py:356
  3.7 15.2 %collective-permute-start.3 = (bf16[128,2048]{1,0:T(8,128)(2,1)}, bf16[128,2048]{1,0:T(8,128)(2,1)}, u32[]{:S(2)}, u32[]{:S(2)}) collective-permute-start(bf16[128,2048]{1,0:T(8,128)(2,1)} %refs_1_.1), channel_id=1, source_target_pairs={{0,2},{4,0},{8,4},{12,8},{14,12},{10,14},{6,10},{2,6},{1,3},{5,1},... | collective-permute-start | bytes 1572872 | tf_op jit(solution)/shard_map/ppermute | solution.py:356
  5.7 22.8 %collective-permute-start = (bf16[128,2176]{1,0:T(8,128)(2,1)}, bf16[128,2176]{1,0:T(8,128)(2,1)S(1)}, u32[]{:S(2)}, u32[]{:S(2)}) collective-permute-start(bf16[128,2176]{1,0:T(8,128)(2,1)} %get-tuple-element.102.refs_0_), channel_id=1, source_target_pairs={{0,4},{4,8},{8,12},{12,14},{14,10},{10,6},{6,2},{2,0},{1,5},{5,9},... | collective-permute-start | bytes 1671176 | tf_op jit(solution)/shard_map/ppermute | solution.py:356
  7.7 23.1 %collective-permute-start.1 = (bf16[128,2176]{1,0:T(8,128)(2,1)}, bf16[128,2176]{1,0:T(8,128)(2,1)}, u32[]{:S(2)}, u32[]{:S(2)}) collective-permute-start(bf16[128,2176]{1,0:T(8,128)(2,1)} %get-tuple-element.102.refs_0_), channel_id=1, source_target_pairs={{0,2},{4,0},{8,4},{12,8},{14,12},{10,14},{6,10},{2,6},{1,3},{5,1},... | collective-permute-start | bytes 1671176 | tf_op jit(solution)/shard_map/ppermute | solution.py:356
  18.9 21.8 %collective-permute-start.6 = (bf16[128,2048]{1,0:T(8,128)(2,1)S(1)}, bf16[128,2048]{1,0:T(8,128)(2,1)}, u32[]{:S(2)}, u32[]{:S(2)}) collective-permute-start(bf16[128,2048]{1,0:T(8,128)(2,1)S(1)} %collective-permute-done.2.refs_2_), channel_id=1, source_target_pairs={{0,4},{4,8},{8,12},{12,14},{14,10},{10,6},{6,2},{2,0},{1,5},{5,9},... | collective-permute-start | bytes 1572872 | tf_op jit(solution)/shard_map/ppermute | solution.py:356
  20.5 23.1 %collective-permute-start.8 = (bf16[64,4352]{1,0:T(8,128)(2,1)}, bf16[64,4352]{1,0:T(8,128)(2,1)S(1)}, u32[]{:S(2)}, u32[]{:S(2)}) collective-permute-start(bf16[64,4352]{1,0:T(8,128)(2,1)} %get-tuple-element.111.refs_2_.refs_20_), channel_id=1, source_target_pairs={{0,1},{1,0},{2,3},{3,2},{4,5},{5,4},{6,7},{7,6},{8,9},{9,8},{10,11... | collective-permute-start | bytes 1671176 | tf_op jit(solution)/shard_map/ppermute | solution.py:359
  20.5 21.6 %collective-permute-start.7 = (bf16[128,2048]{1,0:T(8,128)(2,1)}, bf16[128,2048]{1,0:T(8,128)(2,1)}, u32[]{:S(2)}, u32[]{:S(2)}) collective-permute-start(bf16[128,2048]{1,0:T(8,128)(2,1)} %collective-permute-done.3.refs_3_), channel_id=1, source_target_pairs={{0,2},{4,0},{8,4},{12,8},{14,12},{10,14},{6,10},{2,6},{1,3},{5,1},... | collective-permute-start | bytes 1572872 | tf_op jit(solution)/shard_map/ppermute | solution.py:356
  28.6 23.2 %collective-permute-start.4 = (bf16[128,2176]{1,0:T(8,128)(2,1)S(1)}, bf16[128,2176]{1,0:T(8,128)(2,1)S(1)}, u32[]{:S(2)}, u32[]{:S(2)}) collective-permute-start(bf16[128,2176]{1,0:T(8,128)(2,1)S(1)} %collective-permute-done.refs_0_), channel_id=1, source_target_pairs={{0,4},{4,8},{8,12},{12,14},{14,10},{10,6},{6,2},{2,0},{1,5},{5,9},... | collective-permute-start | bytes 1671176 | tf_op jit(solution)/shard_map/ppermute | solution.py:356
  30.8 23.1 %collective-permute-start.5 = (bf16[128,2176]{1,0:T(8,128)(2,1)}, bf16[128,2176]{1,0:T(8,128)(2,1)S(1)}, u32[]{:S(2)}, u32[]{:S(2)}) collective-permute-start(bf16[128,2176]{1,0:T(8,128)(2,1)} %collective-permute-done.1.refs_1_), channel_id=1, source_target_pairs={{0,2},{4,0},{8,4},{12,8},{14,12},{10,14},{6,10},{2,6},{1,3},{5,1},... | collective-permute-start | bytes 1671176 | tf_op jit(solution)/shard_map/ppermute | solution.py:356
  40.7 26.3 %collective-permute-start.13 = (bf16[128,4352]{1,0:T(8,128)(2,1)}, bf16[128,4352]{1,0:T(8,128)(2,1)S(1)}, u32[]{:S(2)}, u32[]{:S(2)}) collective-permute-start(bf16[128,4352]{1,0:T(8,128)(2,1)} %get-tuple-element.121.refs_21_), channel_id=1, source_target_pairs={{0,1},{1,0},{2,3},{3,2},{4,5},{5,4},{6,7},{7,6},{8,9},{9,8},{10,11... | collective-permute-start | bytes 3342344 | tf_op jit(solution)/shard_map/ppermute | solution.py:359
  42.0 23.7 %collective-permute-start.11 = (bf16[128,2048]{1,0:T(8,128)(2,1)}, bf16[128,2048]{1,0:T(8,128)(2,1)}, u32[]{:S(2)}, u32[]{:S(2)}) collective-permute-start(bf16[128,2048]{1,0:T(8,128)(2,1)} %collective-permute-done.6.refs_2_), channel_id=1, source_target_pairs={{0,4},{4,8},{8,12},{12,14},{14,10},{10,6},{6,2},{2,0},{1,5},{5,9},... | collective-permute-start | bytes 1572872 | tf_op jit(solution)/shard_map/ppermute | solution.py:356
  43.6 22.2 %copy-start.7 = (bf16[2304,128]{1,0:T(8,128)(2,1)S(1)}, bf16[2304,128]{1,0:T(8,128)(2,1)}, u32[]{:S(2)}) copy-start(bf16[2304,128]{1,0:T(8,128)(2,1)} %get-tuple-element.106) | copy-start | bytes 1769476
  43.6 22.1 %copy-start.5 = (bf16[64,4352]{1,0:T(8,128)(2,1)}, bf16[64,4352]{1,0:T(8,128)(2,1)S(1)}, u32[]{:S(2)}) copy-start(bf16[64,4352]{1,0:T(8,128)(2,1)S(1)} %collective-permute-done.8.refs_5_.refs_15_.refs_25_) | copy-start | bytes 1671172
  43.6 23.2 %collective-permute-start.12 = (bf16[128,2048]{1,0:T(8,128)(2,1)}, bf16[128,2048]{1,0:T(8,128)(2,1)}, u32[]{:S(2)}, u32[]{:S(2)}) collective-permute-start(bf16[128,2048]{1,0:T(8,128)(2,1)} %collective-permute-done.7.refs_3_), channel_id=1, source_target_pairs={{0,2},{4,0},{8,4},{12,8},{14,12},{10,14},{6,10},{2,6},{1,3},{5,1},... | collective-permute-start | bytes 1572872 | tf_op jit(solution)/shard_map/ppermute | solution.py:356
  53.9 21.0 %collective-permute-start.9 = (bf16[128,2176]{1,0:T(8,128)(2,1)S(1)}, bf16[128,2176]{1,0:T(8,128)(2,1)S(1)}, u32[]{:S(2)}, u32[]{:S(2)}) collective-permute-start(bf16[128,2176]{1,0:T(8,128)(2,1)S(1)} %collective-permute-done.4.refs_0_), channel_id=1, source_target_pairs={{0,4},{4,8},{8,12},{12,14},{14,10},{10,6},{6,2},{2,0},{1,5},{5,9},... | collective-permute-start | bytes 1671176 | tf_op jit(solution)/shard_map/ppermute | solution.py:356
  55.5 21.6 %collective-permute-start.10 = (bf16[128,2176]{1,0:T(8,128)(2,1)S(1)}, bf16[128,2176]{1,0:T(8,128)(2,1)S(1)}, u32[]{:S(2)}, u32[]{:S(2)}) collective-permute-start(bf16[128,2176]{1,0:T(8,128)(2,1)S(1)} %collective-permute-done.5.refs_1_), channel_id=1, source_target_pairs={{0,2},{4,0},{8,4},{12,8},{14,12},{10,14},{6,10},{2,6},{1,3},{5,1},... | collective-permute-start | bytes 1671176 | tf_op jit(solution)/shard_map/ppermute | solution.py:356
  65.7 31.3 %collective-permute-start.18 = (bf16[128,4352]{1,0:T(8,128)(2,1)}, bf16[128,4352]{1,0:T(8,128)(2,1)S(1)}, u32[]{:S(2)}, u32[]{:S(2)}) collective-permute-start(bf16[128,4352]{1,0:T(8,128)(2,1)} %get-tuple-element.139.refs_22_), channel_id=1, source_target_pairs={{0,1},{1,0},{2,3},{3,2},{4,5},{5,4},{6,7},{7,6},{8,9},{9,8},{10,11... | collective-permute-start | bytes 3342344 | tf_op jit(solution)/shard_map/ppermute | solution.py:359
  66.9 15.8 %collective-permute-start.14 = (bf16[64,2048]{1,0:T(8,128)(2,1)S(1)}, bf16[64,2048]{1,0:T(8,128)(2,1)S(1)}, u32[]{:S(2)}, u32[]{:S(2)}) collective-permute-start(bf16[64,2048]{1,0:T(8,128)(2,1)S(1)} %copy-done.24), channel_id=1, source_target_pairs={{0,2},{4,0},{8,4},{12,8},{14,12},{10,14},{6,10},{2,6},{1,3},{5,1},... | collective-permute-start | bytes 786440 | tf_op jit(solution)/shard_map/ppermute | solution.py:356
  66.9 27.1 %copy-start.2 = (bf16[128,4352]{1,0:T(8,128)(2,1)}, bf16[128,4352]{1,0:T(8,128)(2,1)S(1)}, u32[]{:S(2)}) copy-start(bf16[128,4352]{1,0:T(8,128)(2,1)S(1)} %collective-permute-done.13.refs_6_.refs_16_.refs_26_) | copy-start | bytes 3342340
  67.0 17.1 %collective-permute-start.15 = (bf16[64,2048]{1,0:T(8,128)(2,1)S(1)}, bf16[64,2048]{1,0:T(8,128)(2,1)S(1)}, u32[]{:S(2)}, u32[]{:S(2)}) collective-permute-start(bf16[64,2048]{1,0:T(8,128)(2,1)S(1)} %copy-done.23), channel_id=1, source_target_pairs={{0,4},{4,8},{8,12},{12,14},{14,10},{10,6},{6,2},{2,0},{1,5},{5,9},... | collective-permute-start | bytes 786440 | tf_op jit(solution)/shard_map/ppermute | solution.py:356
  74.9 20.5 %collective-permute-start.17 = (bf16[128,2048]{1,0:T(8,128)(2,1)}, bf16[128,2048]{1,0:T(8,128)(2,1)}, u32[]{:S(2)}, u32[]{:S(2)}) collective-permute-start(bf16[128,2048]{1,0:T(8,128)(2,1)} %collective-permute-done.12.refs_3_), channel_id=1, source_target_pairs={{0,2},{4,0},{8,4},{12,8},{14,12},{10,14},{6,10},{2,6},{1,3},{5,1},... | collective-permute-start | bytes 1572872 | tf_op jit(solution)/shard_map/ppermute | solution.py:356
  77.1 26.7 %collective-permute-start.16 = (bf16[128,2176]{1,0:T(8,128)(2,1)S(1)}, bf16[128,2176]{1,0:T(8,128)(2,1)S(1)}, u32[]{:S(2)}, u32[]{:S(2)}) collective-permute-start(bf16[128,2176]{1,0:T(8,128)(2,1)S(1)} %collective-permute-done.9.refs_0_), channel_id=1, source_target_pairs={{0,4},{4,8},{8,12},{12,14},{14,10},{10,6},{6,2},{2,0},{1,5},{5,9},... | collective-permute-start | bytes 1671176 | tf_op jit(solution)/shard_map/ppermute | solution.py:356
  82.7 37.8 %collective-permute-start.25 = (bf16[64,2048]{1,0:T(8,128)(2,1)S(1)}, bf16[64,2048]{1,0:T(8,128)(2,1)S(1)}, u32[]{:S(2)}, u32[]{:S(2)}) collective-permute-start(bf16[64,2048]{1,0:T(8,128)(2,1)S(1)} %copy-done.27), channel_id=1, source_target_pairs={{0,6},{4,2},{8,0},{12,4},{14,8},{10,12},{6,14},{2,10},{1,7},{5,3},... | collective-permute-start | bytes 786440 | tf_op jit(solution)/shard_map/ppermute | solution.py:356
  94.1 26.3 %collective-permute-start.19 = (bf16[128,4352]{1,0:T(8,128)(2,1)}, bf16[128,4352]{1,0:T(8,128)(2,1)S(1)}, u32[]{:S(2)}, u32[]{:S(2)}) collective-permute-start(bf16[128,4352]{1,0:T(8,128)(2,1)} %get-tuple-element.143.refs_23_), channel_id=1, source_target_pairs={{0,1},{1,0},{2,3},{3,2},{4,5},{5,4},{6,7},{7,6},{8,9},{9,8},{10,11... | collective-permute-start | bytes 3342344 | tf_op jit(solution)/shard_map/ppermute | solution.py:359
  95.5 38.9 %collective-permute-start.26 = (bf16[64,2048]{1,0:T(8,128)(2,1)S(1)}, bf16[64,2048]{1,0:T(8,128)(2,1)S(1)}, u32[]{:S(2)}, u32[]{:S(2)}) collective-permute-start(bf16[64,2048]{1,0:T(8,128)(2,1)S(1)} %copy-done.26), channel_id=1, source_target_pairs={{0,8},{4,12},{8,14},{12,10},{14,6},{10,2},{6,0},{2,4},{1,9},{5,13}... | collective-permute-start | bytes 786440 | tf_op jit(solution)/shard_map/ppermute | solution.py:356
  97.0 39.7 %collective-permute-start.23 = (bf16[64,2048]{1,0:T(8,128)(2,1)S(1)}, bf16[64,2048]{1,0:T(8,128)(2,1)S(1)}, u32[]{:S(2)}, u32[]{:S(2)}) collective-permute-start(bf16[64,2048]{1,0:T(8,128)(2,1)S(1)} %copy-done.28), channel_id=1, source_target_pairs={{0,12},{4,14},{8,10},{12,6},{14,2},{10,0},{6,4},{2,8},{1,13},{5,15... | collective-permute-start | bytes 786440 | tf_op jit(solution)/shard_map/ppermute | solution.py:356
  114.4 6.2 %collective-permute-start.22 = (bf16[64,4352]{1,0:T(8,128)(2,1)}, bf16[64,4352]{1,0:T(8,128)(2,1)S(1)}, u32[]{:S(2)}, u32[]{:S(2)}) collective-permute-start(bf16[64,4352]{1,0:T(8,128)(2,1)} %get-tuple-element.162.refs_24_), channel_id=1, source_target_pairs={{0,1},{1,0},{2,3},{3,2},{4,5},{5,4},{6,7},{7,6},{8,9},{9,8},{10,11... | collective-permute-start | bytes 1671176 | tf_op jit(solution)/shard_map/ppermute | solution.py:359
  120.4 16.3 %collective-permute-start.24 = (bf16[64,2048]{1,0:T(8,128)(2,1)}, bf16[64,2048]{1,0:T(8,128)(2,1)S(1)}, u32[]{:S(2)}, u32[]{:S(2)}) collective-permute-start(bf16[64,2048]{1,0:T(8,128)(2,1)} %get-tuple-element.164), channel_id=1, source_target_pairs={{0,10},{4,6},{8,2},{12,0},{14,4},{10,8},{6,12},{2,14},{1,11},{5,7}... | collective-permute-start | bytes 786440 | tf_op jit(solution)/shard_map/ppermute | solution.py:356
  120.5 16.3 %collective-permute-start.20 = (bf16[288,256]{1,0:T(8,128)(2,1)S(1)}, bf16[288,256]{1,0:T(8,128)(2,1)S(1)}, u32[]{:S(2)}, u32[]{:S(2)}) collective-permute-start(bf16[288,256]{1,0:T(8,128)(2,1)S(1)} %get-tuple-element.151), channel_id=1, source_target_pairs={{0,4},{4,8},{8,12},{12,14},{14,10},{10,6},{6,2},{2,0},{1,5},{5,9},... | collective-permute-start | bytes 442376 | tf_op jit(solution)/shard_map/ppermute | solution.py:356
  120.6 17.2 %collective-permute-start.21 = (bf16[288,256]{1,0:T(8,128)(2,1)S(1)}, bf16[288,256]{1,0:T(8,128)(2,1)S(1)}, u32[]{:S(2)}, u32[]{:S(2)}) collective-permute-start(bf16[288,256]{1,0:T(8,128)(2,1)S(1)} %get-tuple-element.152), channel_id=1, source_target_pairs={{0,2},{4,0},{8,4},{12,8},{14,12},{10,14},{6,10},{2,6},{1,3},{5,1},... | collective-permute-start | bytes 442376 | tf_op jit(solution)/shard_map/ppermute | solution.py:356
  134.4 25.7 %copy-start.12 = (bf16[64,2048]{1,0:T(8,128)(2,1)}, bf16[64,2048]{1,0:T(8,128)(2,1)S(1)}, u32[]{:S(2)}) copy-start(bf16[64,2048]{1,0:T(8,128)(2,1)S(1)} %collective-permute-done.26.refs_2_) | copy-start | bytes 786436
  134.4 35.0 %collective-permute-start.39 = (bf16[64,2048]{1,0:T(8,128)(2,1)S(1)}, bf16[64,2048]{1,0:T(8,128)(2,1)S(1)}, u32[]{:S(2)}, u32[]{:S(2)}) collective-permute-start(bf16[64,2048]{1,0:T(8,128)(2,1)S(1)} %copy-done.25), channel_id=1, source_target_pairs={{0,14},{4,10},{8,6},{12,2},{14,0},{10,4},{6,8},{2,12},{1,15},{5,11... | collective-permute-start | bytes 786440 | tf_op jit(solution)/shard_map/ppermute | solution.py:356
  136.7 23.3 %copy-start.13 = (bf16[64,2048]{1,0:T(8,128)(2,1)}, bf16[64,2048]{1,0:T(8,128)(2,1)S(1)}, u32[]{:S(2)}) copy-start(bf16[64,2048]{1,0:T(8,128)(2,1)S(1)} %collective-permute-done.23.refs_3_) | copy-start | bytes 786436
  136.7 39.8 %collective-permute-start.41 = (bf16[512,2048]{1,0:T(8,128)(2,1)}, bf16[512,2048]{1,0:T(8,128)(2,1)S(1)}, u32[]{:S(2)}, u32[]{:S(2)}) collective-permute-start(bf16[512,2048]{1,0:T(8,128)(2,1)} %get-tuple-element.200), channel_id=1, source_target_pairs={{0,1},{1,0},{2,3},{3,2},{4,5},{5,4},{6,7},{7,6},{8,9},{9,8},{10,11... | collective-permute-start | bytes 6291464 | tf_op jit(solution)/shard_map/ppermute | solution.py:359
  136.8 23.3 %copy-start.14 = (bf16[64,2048]{1,0:T(8,128)(2,1)}, bf16[64,2048]{1,0:T(8,128)(2,1)S(1)}, u32[]{:S(2)}) copy-start(bf16[64,2048]{1,0:T(8,128)(2,1)S(1)} %collective-permute-done.24.refs_5_) | copy-start | bytes 786436
  137.8 11.0 %collective-permute-start.36 = (bf16[288,256]{1,0:T(8,128)(2,1)S(1)}, bf16[288,256]{1,0:T(8,128)(2,1)S(1)}, u32[]{:S(2)}, u32[]{:S(2)}) collective-permute-start(bf16[288,256]{1,0:T(8,128)(2,1)S(1)} %broadcast_select_fusion.2), channel_id=1, source_target_pairs={{0,2},{4,0},{8,4},{12,8},{14,12},{10,14},{6,10},{2,6},{1,3},{5,1},... | collective-permute-start | bytes 442376 | tf_op jit(solution)/shard_map/ppermute | solution.py:356
  138.8 15.8 %collective-permute-start.33 = (bf16[288,256]{1,0:T(8,128)(2,1)S(1)}, bf16[288,256]{1,0:T(8,128)(2,1)S(1)}, u32[]{:S(2)}, u32[]{:S(2)}) collective-permute-start(bf16[288,256]{1,0:T(8,128)(2,1)S(1)} %get-tuple-element.176), channel_id=1, source_target_pairs={{0,2},{4,0},{8,4},{12,8},{14,12},{10,14},{6,10},{2,6},{1,3},{5,1},... | collective-permute-start | bytes 442376 | tf_op jit(solution)/shard_map/ppermute | solution.py:356
  138.9 15.8 %collective-permute-start.30 = (bf16[288,256]{1,0:T(8,128)(2,1)S(1)}, bf16[288,256]{1,0:T(8,128)(2,1)S(1)}, u32[]{:S(2)}, u32[]{:S(2)}) collective-permute-start(bf16[288,256]{1,0:T(8,128)(2,1)S(1)} %get-tuple-element.173), channel_id=1, source_target_pairs={{0,4},{4,8},{8,12},{12,14},{14,10},{10,6},{6,2},{2,0},{1,5},{5,9},... | collective-permute-start | bytes 442376 | tf_op jit(solution)/shard_map/ppermute | solution.py:356
  148.8 8.7 %collective-permute-start.27 = (bf16[288,256]{1,0:T(8,128)(2,1)S(1)}, bf16[288,256]{1,0:T(8,128)(2,1)S(1)}, u32[]{:S(2)}, u32[]{:S(2)}) collective-permute-start(bf16[288,256]{1,0:T(8,128)(2,1)S(1)} %broadcast_select_fusion.9), channel_id=1, source_target_pairs={{0,4},{4,8},{8,12},{12,14},{14,10},{10,6},{6,2},{2,0},{1,5},{5,9},... | collective-permute-start | bytes 442376 | tf_op jit(solution)/shard_map/ppermute | solution.py:356
  154.6 6.7 %collective-permute-start.37 = (bf16[288,256]{1,0:T(8,128)(2,1)S(1)}, bf16[288,256]{1,0:T(8,128)(2,1)S(1)}, u32[]{:S(2)}, u32[]{:S(2)}) collective-permute-start(bf16[288,256]{1,0:T(8,128)(2,1)S(1)} %broadcast_select_fusion.1), channel_id=1, source_target_pairs={{0,2},{4,0},{8,4},{12,8},{14,12},{10,14},{6,10},{2,6},{1,3},{5,1},... | collective-permute-start | bytes 442376 | tf_op jit(solution)/shard_map/ppermute | solution.py:356
  154.7 8.4 %collective-permute-start.34 = (bf16[288,256]{1,0:T(8,128)(2,1)S(1)}, bf16[288,256]{1,0:T(8,128)(2,1)S(1)}, u32[]{:S(2)}, u32[]{:S(2)}) collective-permute-start(bf16[288,256]{1,0:T(8,128)(2,1)S(1)} %broadcast_select_fusion.4), channel_id=1, source_target_pairs={{0,2},{4,0},{8,4},{12,8},{14,12},{10,14},{6,10},{2,6},{1,3},{5,1},... | collective-permute-start | bytes 442376 | tf_op jit(solution)/shard_map/ppermute | solution.py:356
  157.5 6.2 %collective-permute-start.31 = (bf16[288,256]{1,0:T(8,128)(2,1)S(1)}, bf16[288,256]{1,0:T(8,128)(2,1)S(1)}, u32[]{:S(2)}, u32[]{:S(2)}) collective-permute-start(bf16[288,256]{1,0:T(8,128)(2,1)S(1)} %broadcast_select_fusion.6), channel_id=1, source_target_pairs={{0,4},{4,8},{8,12},{12,14},{14,10},{10,6},{6,2},{2,0},{1,5},{5,9},... | collective-permute-start | bytes 442376 | tf_op jit(solution)/shard_map/ppermute | solution.py:356
  161.3 5.3 %collective-permute-start.28 = (bf16[288,256]{1,0:T(8,128)(2,1)S(1)}, bf16[288,256]{1,0:T(8,128)(2,1)S(1)}, u32[]{:S(2)}, u32[]{:S(2)}) collective-permute-start(bf16[288,256]{1,0:T(8,128)(2,1)S(1)} %broadcast_select_fusion.8), channel_id=1, source_target_pairs={{0,4},{4,8},{8,12},{12,14},{14,10},{10,6},{6,2},{2,0},{1,5},{5,9},... | collective-permute-start | bytes 442376 | tf_op jit(solution)/shard_map/ppermute | solution.py:356
  163.1 10.1 %collective-permute-start.38 = (bf16[288,256]{1,0:T(8,128)(2,1)S(1)}, bf16[288,256]{1,0:T(8,128)(2,1)S(1)}, u32[]{:S(2)}, u32[]{:S(2)}) collective-permute-start(bf16[288,256]{1,0:T(8,128)(2,1)S(1)} %broadcast_select_fusion), channel_id=1, source_target_pairs={{0,2},{4,0},{8,4},{12,8},{14,12},{10,14},{6,10},{2,6},{1,3},{5,1},... | collective-permute-start | bytes 442376 | tf_op jit(solution)/shard_map/ppermute | solution.py:356
  163.7 9.5 %collective-permute-start.35 = (bf16[288,256]{1,0:T(8,128)(2,1)S(1)}, bf16[288,256]{1,0:T(8,128)(2,1)S(1)}, u32[]{:S(2)}, u32[]{:S(2)}) collective-permute-start(bf16[288,256]{1,0:T(8,128)(2,1)S(1)} %broadcast_select_fusion.3), channel_id=1, source_target_pairs={{0,2},{4,0},{8,4},{12,8},{14,12},{10,14},{6,10},{2,6},{1,3},{5,1},... | collective-permute-start | bytes 442376 | tf_op jit(solution)/shard_map/ppermute | solution.py:356
  166.6 6.7 %collective-permute-start.32 = (bf16[288,256]{1,0:T(8,128)(2,1)}, bf16[288,256]{1,0:T(8,128)(2,1)S(1)}, u32[]{:S(2)}, u32[]{:S(2)}) collective-permute-start(bf16[288,256]{1,0:T(8,128)(2,1)} %broadcast_select_fusion.5), channel_id=1, source_target_pairs={{0,4},{4,8},{8,12},{12,14},{14,10},{10,6},{6,2},{2,0},{1,5},{5,9},... | collective-permute-start | bytes 442376 | tf_op jit(solution)/shard_map/ppermute | solution.py:356
  169.4 5.5 %collective-permute-start.29 = (bf16[288,256]{1,0:T(8,128)(2,1)}, bf16[288,256]{1,0:T(8,128)(2,1)}, u32[]{:S(2)}, u32[]{:S(2)}) collective-permute-start(bf16[288,256]{1,0:T(8,128)(2,1)} %broadcast_select_fusion.7), channel_id=1, source_target_pairs={{0,4},{4,8},{8,12},{12,14},{14,10},{10,6},{6,2},{2,0},{1,5},{5,9},... | collective-permute-start | bytes 442376 | tf_op jit(solution)/shard_map/ppermute | solution.py:356
  174.9 1.6 collective-permute-start.40
  (23 other events, 141.3 us)

commit v13 on v11

--- a/solution.py
+++ b/solution.py
@@ -400,7 +400,10 @@
         turned += turn
         held = following
     (back_behind, back_ahead), other = late[half - 1]
-    turned[-1], late[half - 2] = lax.optimization_barrier((turned[-1], late[half - 2]))
+    hot_mine, hot_theirs = ordered(plan, experts, capacity, scal, hot)
+    turned[-1], late[half - 2], hot_mine, hot_theirs = lax.optimization_barrier(
+        (turned[-1], late[half - 2], hot_mine, hot_theirs)
+    )
 
     taken = 3 * units // experts
     ring_hot = to_ring(hottest, experts)
@@ -417,9 +420,8 @@
         columns = chunk(distance)
         return [columns[:, :lanes], columns[:, lanes:]]
 
-    hot_mine, hot_theirs = ordered(plan, experts, capacity, scal, hot)
     far = halves(half)
-    far, other, hot_mine, hot_theirs = lax.optimization_barrier((far, other, hot_mine, hot_theirs))
+    far, other = lax.optimization_barrier((far, other))
     hot_theirs = swap(hot_theirs)
     far = [shift(far[0], 1), shift(far[1], -1)]
     others = [part for _, part in late[: half - 1]] + [other, late[half][1]]

time: 180 us -> 175 us (0.972)
  starting transfers between devices: 61.7 us -> 55.6 us
    ppermute x35, starting transfers between devices: 61.1 us -> 55.2 us  [shift(): return lax.ppermute(block, 'expert', pairs)]
  transfers between devices with their start and end apart: 42 -> 42, of which waited for: 16 -> 16; matrix products, arithmetic and copies ran while one was open for 2% -> 2% of each run, Pallas kernels for 39% -> 40%
where the time goes in v13:
time: 175 us; the launch traced here: 174 us
  Pallas kernels  71.6 us (41%)
  starting transfers between devices  55.6 us (32%)
  waiting for transfers between devices  39.3 us (22%)
  local copies, waits for them, and re-layouts  3.23 us (2%)
  other arithmetic  2.53 us (1%)
  between operations  1.84 us (1%)
    ppermute x35, starting transfers between devices, shift(): return lax.ppermute(block, 'expert', pairs)  55.2 us
    pallas_call x5, Pallas kernels, run_step(): pl.pallas_call(functools.partial(step_kernel, steps, fanout, capacity, jo...  48.6 us
    ppermute x35, waiting for transfers between devices, shift(): return lax.ppermute(block, 'expert', pairs)  37.7 us
    pallas_call x1, Pallas kernels, expert_gradient(): pl.pallas_call(functools.partial(gradient_kernel, units, count), grid=(ti...  10.8 us
    pallas_call x1, Pallas kernels, ordered(): pl.pallas_call(functools.partial(order_kernel, plan, experts, capacity),...  4.64 us
  transfers between devices with their start and end apart: 42, of which 16 were waited for; matrix products, arithmetic and copies ran while one was open for 2% of the time, Pallas kernels for 40%

profile of v13, /device:TPU:0, one launch (start us, length us, event | category | flops | bytes accessed | tf_op | source)
XLA Modules:
  0.0 174.1 jit_solution(1884823278308887204)
XLA Ops:
  0.6 3.1 %collective-permute-start.2 = (bf16[128,2048]{1,0:T(8,128)(2,1)}, bf16[128,2048]{1,0:T(8,128)(2,1)S(1)}, u32[]{:S(2)}, u32[]{:S(2)}) collective-permute-start(bf16[128,2048]{1,0:T(8,128)(2,1)} %refs_1_.1), channel_id=1, source_target_pairs={{0,4},{4,8},{8,12},{12,14},{14,10},{10,6},{6,2},{2,0},{1,5},{5,9},... | collective-permute-start | bytes 1572872 | tf_op jit(solution)/shard_map/ppermute | solution.py:356
  3.7 2.0 %ring_message.1 = (bf16[128,2176]{1,0:T(8,128)(2,1)}, bf16[128,128]{1,0:T(8,128)(2,1)}) custom-call(bf16[128,2048]{1,0:T(8,128)(2,1)} %tokens.1, s32[2,128]{1,0:T(2,128)} %bitcast.17, f32[2,128]{1,0:T(2,128)} %bitcast.18, f32[1,128]{1,0:T(1,128)} %bitcast.19, s32[1,128]{1,0:T(1,128)} %bitcast.20), custom_call_target="tpu_custom_call" | custom-call | bytes 1048576 | tf_op jit(solution)/shard_map/ring_message/pallas_call | solution.py:262
  5.7 2.0 %collective-permute-start = (bf16[128,2176]{1,0:T(8,128)(2,1)}, bf16[128,2176]{1,0:T(8,128)(2,1)S(1)}, u32[]{:S(2)}, u32[]{:S(2)}) collective-permute-start(bf16[128,2176]{1,0:T(8,128)(2,1)} %get-tuple-element.105.refs_0_), channel_id=1, source_target_pairs={{0,4},{4,8},{8,12},{12,14},{14,10},{10,6},{6,2},{2,0},{1,5},{5,9},... | collective-permute-start | bytes 1671176 | tf_op jit(solution)/shard_map/ppermute | solution.py:356
  9.1 9.4 %expert_step.5 = (bf16[64,2048]{1,0:T(8,128)(2,1)}, bf16[64,4352]{1,0:T(8,128)(2,1)}, bf16[64,4096]{1,0:T(8,128)(2,1)}, bf16[64,2048]{1,0:T(8,128)(2,1)}) custom-call(s32[3]{0:T(128)} %pad_add_fusion.scal, bf16[128,2176]{1,0:T(8,128)(2,1)} %get-tuple-element.105.refs_0_, bf16[128,2048]{1,0:T(8,128)(2,1)} %refs_1_.1, bf16[2048,1536]{1,0:T(8,128)(2,1)} %bitcast.21, ...), custom_call_target="tpu_custom_call" | custom-call | flops 4026531840 | bytes 9437184 | tf_op jit(solution)/shard_map/expert_step/pallas_call | solution.py:151
  18.9 1.7 collective-permute-start.6
  20.9 7.7 %collective-permute-done.refs_0_ = bf16[128,2176]{1,0:T(8,128)(2,1)S(1)} collective-permute-done((bf16[128,2176]{1,0:T(8,128)(2,1)}, bf16[128,2176]{1,0:T(8,128)(2,1)S(1)}, u32[]{:S(2)}, u32[]{:S(2)}) %collective-permute-start) | collective-permute-done | bytes 557088 | tf_op jit(solution)/shard_map/ppermute | solution.py:356
  28.6 2.1 %collective-permute-start.4 = (bf16[128,2176]{1,0:T(8,128)(2,1)S(1)}, bf16[128,2176]{1,0:T(8,128)(2,1)S(1)}, u32[]{:S(2)}, u32[]{:S(2)}) collective-permute-start(bf16[128,2176]{1,0:T(8,128)(2,1)S(1)} %collective-permute-done.refs_0_), channel_id=1, source_target_pairs={{0,4},{4,8},{8,12},{12,14},{14,10},{10,6},{6,2},{2,0},{1,5},{5,9},... | collective-permute-start | bytes 1671176 | tf_op jit(solution)/shard_map/ppermute | solution.py:356
  30.8 9.8 %expert_step.6 = (bf16[128,2048]{1,0:T(8,128)(2,1)}, bf16[128,4352]{1,0:T(8,128)(2,1)}, bf16[128,4096]{1,0:T(8,128)(2,1)}, bf16[64,2048]{1,0:T(8,128)(2,1)}, bf1...) custom-call(s32[3]{0:T(128)} %pad_add_fusion.scal, bf16[128,2176]{1,0:T(8,128)(2,1)} %copy-done.21, ...), custom_call_target="tpu_custom_call" | custom-call | flops 4026531840 | bytes 9437184 | tf_op jit(solution)/shard_map/expert_step/pallas_call | solution.py:151
  40.8 1.3 collective-permute-done.7.refs_3_
  42.0 1.6 collective-permute-start.11
  44.1 7.6 %collective-permute-done.4.refs_0_ = bf16[128,2176]{1,0:T(8,128)(2,1)S(1)} collective-permute-done((bf16[128,2176]{1,0:T(8,128)(2,1)S(1)}, bf16[128,2176]{1,0:T(8,128)(2,1)S(1)}, u32[]{:S(2)}, u32[]{:S(2)}) %collective-permute-start.4) | collective-permute-done | bytes 557088 | tf_op jit(solution)/shard_map/ppermute | solution.py:356
  51.7 2.1 %collective-permute-done.5.refs_1_ = bf16[128,2176]{1,0:T(8,128)(2,1)S(1)} collective-permute-done((bf16[128,2176]{1,0:T(8,128)(2,1)}, bf16[128,2176]{1,0:T(8,128)(2,1)S(1)}, u32[]{:S(2)}, u32[]{:S(2)}) %collective-permute-start.5) | collective-permute-done | bytes 557088 | tf_op jit(solution)/shard_map/ppermute | solution.py:356
  53.9 1.6 collective-permute-start.9
  55.9 9.8 %expert_step.7 = (bf16[128,2048]{1,0:T(8,128)(2,1)}, bf16[128,4352]{1,0:T(8,128)(2,1)}, bf16[128,4096]{1,0:T(8,128)(2,1)}, bf16[64,2048]{1,0:T(8,128)(2,1)}, bf1...) custom-call(s32[3]{0:T(128)} %pad_add_fusion.scal, bf16[128,2176]{1,0:T(8,128)(2,1)} %copy-done.19, ...), custom_call_target="tpu_custom_call" | custom-call | flops 4026531840 | bytes 9437184 | tf_op jit(solution)/shard_map/expert_step/pallas_call | solution.py:151
  66.9 2.0 %collective-permute-start.15 = (bf16[64,2048]{1,0:T(8,128)(2,1)S(1)}, bf16[64,2048]{1,0:T(8,128)(2,1)S(1)}, u32[]{:S(2)}, u32[]{:S(2)}) collective-permute-start(bf16[64,2048]{1,0:T(8,128)(2,1)S(1)} %copy-done.25), channel_id=1, source_target_pairs={{0,4},{4,8},{8,12},{12,14},{14,10},{10,6},{6,2},{2,0},{1,5},{5,9},... | collective-permute-start | bytes 786440 | tf_op jit(solution)/shard_map/ppermute | solution.py:356
  69.1 5.8 %collective-permute-done.9.refs_0_ = bf16[128,2176]{1,0:T(8,128)(2,1)S(1)} collective-permute-done((bf16[128,2176]{1,0:T(8,128)(2,1)S(1)}, bf16[128,2176]{1,0:T(8,128)(2,1)S(1)}, u32[]{:S(2)}, u32[]{:S(2)}) %collective-permute-start.9) | collective-permute-done | bytes 557088 | tf_op jit(solution)/shard_map/ppermute | solution.py:356
  74.9 2.1 %collective-permute-start.17 = (bf16[128,2048]{1,0:T(8,128)(2,1)}, bf16[128,2048]{1,0:T(8,128)(2,1)}, u32[]{:S(2)}, u32[]{:S(2)}) collective-permute-start(bf16[128,2048]{1,0:T(8,128)(2,1)} %collective-permute-done.12.refs_3_), channel_id=1, source_target_pairs={{0,2},{4,0},{8,4},{12,8},{14,12},{10,14},{6,10},{2,6},{1,3},{5,1},... | collective-permute-start | bytes 1572872 | tf_op jit(solution)/shard_map/ppermute | solution.py:356
  77.2 1.6 collective-permute-start.16
  79.4 3.2 %collective-permute-done.14.refs_7_ = bf16[64,2048]{1,0:T(8,128)(2,1)S(1)} collective-permute-done((bf16[64,2048]{1,0:T(8,128)(2,1)S(1)}, bf16[64,2048]{1,0:T(8,128)(2,1)S(1)}, u32[]{:S(2)}, u32[]{:S(2)}) %collective-permute-start.14) | collective-permute-done | bytes 262176 | tf_op jit(solution)/shard_map/ppermute | solution.py:356
  82.7 1.4 collective-permute-start.19
  84.1 9.9 %expert_step.8 = (bf16[128,2048]{1,0:T(8,128)(2,1)}, bf16[128,4352]{1,0:T(8,128)(2,1)}, bf16[128,4096]{1,0:T(8,128)(2,1)}, bf16[64,2048]{1,0:T(8,128)(2,1)}, bf1...) custom-call(s32[3]{0:T(128)} %pad_add_fusion.scal, bf16[128,2176]{1,0:T(8,128)(2,1)} %copy-done.22, ...), custom_call_target="tpu_custom_call" | custom-call | flops 4026531840 | bytes 9437184 | tf_op jit(solution)/shard_map/expert_step/pallas_call | solution.py:151
  94.1 1.2 constant_dynamic-slice_fusion.1
  95.4 1.6 collective-permute-start.20
  97.0 6.6 %collective-permute-start.25 = (bf16[64,2048]{1,0:T(8,128)(2,1)S(1)}, bf16[64,2048]{1,0:T(8,128)(2,1)S(1)}, u32[]{:S(2)}, u32[]{:S(2)}) collective-permute-start(bf16[64,2048]{1,0:T(8,128)(2,1)S(1)} %copy-done.27), channel_id=1, source_target_pairs={{0,12},{4,14},{8,10},{12,6},{14,2},{10,0},{6,4},{2,8},{1,13},{5,15... | collective-permute-start | bytes 786440 | tf_op jit(solution)/shard_map/ppermute | solution.py:356
  104.4 9.7 %expert_step.9 = (bf16[64,2048]{1,0:T(8,128)(2,1)}, bf16[64,4352]{1,0:T(8,128)(2,1)}, bf16[64,4096]{1,0:T(8,128)(2,1)}, bf16[64,2048]{1,0:T(8,128)(2,1)}, bf16[2304,128]{1,0:T(8,128)(2,1)}) custom-call(s32[3]{0:T(128)} %pad_add_fusion.scal, bf16[128,2176]{1,0:T(8,128)(2,1)} %copy-done.23, bf16[128,2048]{1,0:T(8,128)(2,1)} %collective-permute-done.17.refs_1_, ...), custom_call_target="tpu_custom_call" | custom-call | flops 4026531840 | bytes 9437184 | tf_op jit(solution)/shard_map/expert_step/pallas_call | solution.py:151
  114.2 4.6 %hot_rows_ordered.1 = (bf16[512,2048]{1,0:T(8,128)(2,1)}, bf16[512,2048]{1,0:T(8,128)(2,1)}) custom-call(s32[3]{0:T(128)} %pad_add_fusion.scal, bf16[64,4096]{1,0:T(8,128)(2,1)} %get-tuple-element.149.refs_0_, bf16[128,4096]{1,0:T(8,128)(2,1)} %get-tuple-element.150.refs_1_, bf16[128,4096]{1,0:T(8,128)(2,1)} %get-tuple-element.151.refs_2_, ...), custom_call_target="tpu_custom_call" | custom-call | bytes 8388608 | tf_op jit(solution)/shard_map/hot_rows_ordered/pallas_call | solution.py:290
  118.8 2.5 %collective-permute-start.27 = (bf16[64,2048]{1,0:T(8,128)(2,1)}, bf16[64,2048]{1,0:T(8,128)(2,1)}, u32[]{:S(2)}, u32[]{:S(2)}) collective-permute-start(bf16[64,2048]{1,0:T(8,128)(2,1)} %get-tuple-element.173), channel_id=1, source_target_pairs={{0,14},{4,10},{8,6},{12,2},{14,0},{10,4},{6,8},{2,12},{1,15},{5,11... | collective-permute-start | bytes 786440 | tf_op jit(solution)/shard_map/ppermute | solution.py:356
  122.3 8.5 %collective-permute-start.22 = (bf16[288,256]{1,0:T(8,128)(2,1)S(1)}, bf16[288,256]{1,0:T(8,128)(2,1)S(1)}, u32[]{:S(2)}, u32[]{:S(2)}) collective-permute-start(bf16[288,256]{1,0:T(8,128)(2,1)S(1)} %get-tuple-element.158), channel_id=1, source_target_pairs={{0,4},{4,8},{8,12},{12,14},{14,10},{10,6},{6,2},{2,0},{1,5},{5,9},... | collective-permute-start | bytes 442376 | tf_op jit(solution)/shard_map/ppermute | solution.py:356
  130.8 2.6 %collective-permute-start.23 = (bf16[288,256]{1,0:T(8,128)(2,1)S(1)}, bf16[288,256]{1,0:T(8,128)(2,1)S(1)}, u32[]{:S(2)}, u32[]{:S(2)}) collective-permute-start(bf16[288,256]{1,0:T(8,128)(2,1)S(1)} %get-tuple-element.159), channel_id=1, source_target_pairs={{0,2},{4,0},{8,4},{12,8},{14,12},{10,14},{6,10},{2,6},{1,3},{5,1},... | collective-permute-start | bytes 442376 | tf_op jit(solution)/shard_map/ppermute | solution.py:356
  133.5 10.8 %expert_gradient.1 = f32[1,1024,2304]{2,1,0:T(8,128)} custom-call(s32[3]{0:T(128)} %pad_add_fusion.scal, bf16[64,2048]{1,0:T(8,128)(2,1)} %get-tuple-element.160.refs_0_.refs_10_, bf16[128,2048]{1,0:T(8,128)(2,1)} %get-tuple-element.161.refs_1_.refs_11_, bf16[128,2048]{1,0:T(8,128)(2,1)} %get-tuple-element.162.refs_2_.refs_12_, ...), custom_call_target="tpu_custom_call" | custom-call | flops 4831838208 | bytes 14155776 | tf_op jit(solution)/shard_map/expert_gradient/pallas_call | solution.py:226
  144.5 1.2 collective-permute-start.37
  146.6 1.1 collective-permute-start.31
  147.7 1.0 collective-permute-start.28
  148.7 2.5 %collective-permute-done.37 = bf16[288,256]{1,0:T(8,128)(2,1)S(1)} collective-permute-done((bf16[288,256]{1,0:T(8,128)(2,1)S(1)}, bf16[288,256]{1,0:T(8,128)(2,1)S(1)}, u32[]{:S(2)}, u32[]{:S(2)}) %collective-permute-start.37) | collective-permute-done | bytes 147488 | tf_op jit(solution)/shard_map/ppermute | solution.py:356
  151.2 1.2 collective-permute-start.38
  152.4 2.0 %collective-permute-done.34 = bf16[288,256]{1,0:T(8,128)(2,1)S(1)} collective-permute-done((bf16[288,256]{1,0:T(8,128)(2,1)S(1)}, bf16[288,256]{1,0:T(8,128)(2,1)S(1)}, u32[]{:S(2)}, u32[]{:S(2)}) %collective-permute-start.34) | collective-permute-done | bytes 147488 | tf_op jit(solution)/shard_map/ppermute | solution.py:356
  154.4 1.2 collective-permute-start.35
  155.6 1.0 collective-permute-start.32
  156.6 1.3 collective-permute-start.29
  157.9 1.1 collective-permute-start.39
  159.0 2.2 %collective-permute-done.35 = bf16[288,256]{1,0:T(8,128)(2,1)S(1)} collective-permute-done((bf16[288,256]{1,0:T(8,128)(2,1)S(1)}, bf16[288,256]{1,0:T(8,128)(2,1)S(1)}, u32[]{:S(2)}, u32[]{:S(2)}) %collective-permute-start.35) | collective-permute-done | bytes 147488 | tf_op jit(solution)/shard_map/ppermute | solution.py:356
  161.2 1.2 collective-permute-start.36
  162.4 1.0 collective-permute-start.33
  164.0 1.0 collective-permute-start.30
  165.0 3.2 %token_sum.1 = bf16[128,2048]{1,0:T(8,128)(2,1)} custom-call(s32[3]{0:T(128)} %pad_add_fusion.scal, bf16[128,128]{1,0:T(8,128)(2,1)} %get-tuple-element.188.meta, bf16[64,2048]{1,0:T(8,128)(2,1)} %get-tuple-element.189.refs_0_, bf16[64,2048]{1,0:T(8,128)(2,1)} %copy-done.12, bf16[64,2048]{1,0:T(8,128)(2,1)} %copy-done.14, bf16[64,2048]{1,0:T(8,128)(2,1)} %copy-done.15, ...), custom_call_target="tpu_custom_call" | custom-call | flops 268435456 | bytes 2097152 | tf_op jit(solution)/shard_map/token_sum/pallas_call | solution.py:186
  168.3 1.7 collective-permute-done.30
  170.1 1.6 collective-permute-done.40.theirs
  171.7 2.4 %shadow_gradient.1 = f32[288,1024]{1,0:T(8,128)} custom-call(s32[3]{0:T(128)S(1)} %copy-done.1, bf16[288,512]{1,0:T(8,128)(2,1)S(1)} %pad_maximum_fusion.mine, bf16[288,512]{1,0:T(8,128)(2,1)S(1)} %collective-permute-done.40.theirs, bf16[512,2048]{1,0:T(8,128)(2,1)S(1)} %copy-done, bf16[512,2048]{1,0:T(8,128)(2,1)S(1)} %collective-permute-done.41.hot_theirs), custom_call_target="tpu_custom_call" | custom-call | flops 603979776 | bytes 2097152 | tf_op jit(solution)/shard_map/shadow_gradient/pallas_call | solution.py:329
  (130 shorter events, 8.7 us)
Async XLA Ops:
  0.6 17.8 %collective-permute-start.2 = (bf16[128,2048]{1,0:T(8,128)(2,1)}, bf16[128,2048]{1,0:T(8,128)(2,1)S(1)}, u32[]{:S(2)}, u32[]{:S(2)}) collective-permute-start(bf16[128,2048]{1,0:T(8,128)(2,1)} %refs_1_.1), channel_id=1, source_target_pairs={{0,4},{4,8},{8,12},{12,14},{14,10},{10,6},{6,2},{2,0},{1,5},{5,9},... | collective-permute-start | bytes 1572872 | tf_op jit(solution)/shard_map/ppermute | solution.py:356
  3.7 15.2 %collective-permute-start.3 = (bf16[128,2048]{1,0:T(8,128)(2,1)}, bf16[128,2048]{1,0:T(8,128)(2,1)}, u32[]{:S(2)}, u32[]{:S(2)}) collective-permute-start(bf16[128,2048]{1,0:T(8,128)(2,1)} %refs_1_.1), channel_id=1, source_target_pairs={{0,2},{4,0},{8,4},{12,8},{14,12},{10,14},{6,10},{2,6},{1,3},{5,1},... | collective-permute-start | bytes 1572872 | tf_op jit(solution)/shard_map/ppermute | solution.py:356
  5.7 22.8 %collective-permute-start = (bf16[128,2176]{1,0:T(8,128)(2,1)}, bf16[128,2176]{1,0:T(8,128)(2,1)S(1)}, u32[]{:S(2)}, u32[]{:S(2)}) collective-permute-start(bf16[128,2176]{1,0:T(8,128)(2,1)} %get-tuple-element.105.refs_0_), channel_id=1, source_target_pairs={{0,4},{4,8},{8,12},{12,14},{14,10},{10,6},{6,2},{2,0},{1,5},{5,9},... | collective-permute-start | bytes 1671176 | tf_op jit(solution)/shard_map/ppermute | solution.py:356
  7.7 23.1 %collective-permute-start.1 = (bf16[128,2176]{1,0:T(8,128)(2,1)}, bf16[128,2176]{1,0:T(8,128)(2,1)}, u32[]{:S(2)}, u32[]{:S(2)}) collective-permute-start(bf16[128,2176]{1,0:T(8,128)(2,1)} %get-tuple-element.105.refs_0_), channel_id=1, source_target_pairs={{0,2},{4,0},{8,4},{12,8},{14,12},{10,14},{6,10},{2,6},{1,3},{5,1},... | collective-permute-start | bytes 1671176 | tf_op jit(solution)/shard_map/ppermute | solution.py:356
  18.4 12.4 %copy-start.24 = (bf16[128,2048]{1,0:T(8,128)(2,1)}, bf16[128,2048]{1,0:T(8,128)(2,1)S(1)}, u32[]{:S(2)}) copy-start(bf16[128,2048]{1,0:T(8,128)(2,1)S(1)} %collective-permute-done.2.refs_2_) | copy-start | bytes 1572868
  18.9 21.8 %collective-permute-start.6 = (bf16[128,2048]{1,0:T(8,128)(2,1)S(1)}, bf16[128,2048]{1,0:T(8,128)(2,1)}, u32[]{:S(2)}, u32[]{:S(2)}) collective-permute-start(bf16[128,2048]{1,0:T(8,128)(2,1)S(1)} %collective-permute-done.2.refs_2_), channel_id=1, source_target_pairs={{0,4},{4,8},{8,12},{12,14},{14,10},{10,6},{6,2},{2,0},{1,5},{5,9},... | collective-permute-start | bytes 1572872 | tf_op jit(solution)/shard_map/ppermute | solution.py:356
  20.5 23.1 %collective-permute-start.8 = (bf16[64,4352]{1,0:T(8,128)(2,1)}, bf16[64,4352]{1,0:T(8,128)(2,1)S(1)}, u32[]{:S(2)}, u32[]{:S(2)}) collective-permute-start(bf16[64,4352]{1,0:T(8,128)(2,1)} %get-tuple-element.114.refs_2_.refs_20_), channel_id=1, source_target_pairs={{0,1},{1,0},{2,3},{3,2},{4,5},{5,4},{6,7},{7,6},{8,9},{9,8},{10,11... | collective-permute-start | bytes 1671176 | tf_op jit(solution)/shard_map/ppermute | solution.py:359
  20.5 21.5 %collective-permute-start.7 = (bf16[128,2048]{1,0:T(8,128)(2,1)}, bf16[128,2048]{1,0:T(8,128)(2,1)}, u32[]{:S(2)}, u32[]{:S(2)}) collective-permute-start(bf16[128,2048]{1,0:T(8,128)(2,1)} %collective-permute-done.3.refs_3_), channel_id=1, source_target_pairs={{0,2},{4,0},{8,4},{12,8},{14,12},{10,14},{6,10},{2,6},{1,3},{5,1},... | collective-permute-start | bytes 1572872 | tf_op jit(solution)/shard_map/ppermute | solution.py:356
  28.6 23.2 %collective-permute-start.4 = (bf16[128,2176]{1,0:T(8,128)(2,1)S(1)}, bf16[128,2176]{1,0:T(8,128)(2,1)S(1)}, u32[]{:S(2)}, u32[]{:S(2)}) collective-permute-start(bf16[128,2176]{1,0:T(8,128)(2,1)S(1)} %collective-permute-done.refs_0_), channel_id=1, source_target_pairs={{0,4},{4,8},{8,12},{12,14},{14,10},{10,6},{6,2},{2,0},{1,5},{5,9},... | collective-permute-start | bytes 1671176 | tf_op jit(solution)/shard_map/ppermute | solution.py:356
  30.8 23.1 %collective-permute-start.5 = (bf16[128,2176]{1,0:T(8,128)(2,1)}, bf16[128,2176]{1,0:T(8,128)(2,1)S(1)}, u32[]{:S(2)}, u32[]{:S(2)}) collective-permute-start(bf16[128,2176]{1,0:T(8,128)(2,1)} %collective-permute-done.1.refs_1_), channel_id=1, source_target_pairs={{0,2},{4,0},{8,4},{12,8},{14,12},{10,14},{6,10},{2,6},{1,3},{5,1},... | collective-permute-start | bytes 1671176 | tf_op jit(solution)/shard_map/ppermute | solution.py:356
  40.7 26.3 %collective-permute-start.13 = (bf16[128,4352]{1,0:T(8,128)(2,1)}, bf16[128,4352]{1,0:T(8,128)(2,1)S(1)}, u32[]{:S(2)}, u32[]{:S(2)}) collective-permute-start(bf16[128,4352]{1,0:T(8,128)(2,1)} %get-tuple-element.124.refs_21_), channel_id=1, source_target_pairs={{0,1},{1,0},{2,3},{3,2},{4,5},{5,4},{6,7},{7,6},{8,9},{9,8},{10,11... | collective-permute-start | bytes 3342344 | tf_op jit(solution)/shard_map/ppermute | solution.py:359
  42.0 23.7 %collective-permute-start.11 = (bf16[128,2048]{1,0:T(8,128)(2,1)}, bf16[128,2048]{1,0:T(8,128)(2,1)}, u32[]{:S(2)}, u32[]{:S(2)}) collective-permute-start(bf16[128,2048]{1,0:T(8,128)(2,1)} %collective-permute-done.6.refs_2_), channel_id=1, source_target_pairs={{0,4},{4,8},{8,12},{12,14},{14,10},{10,6},{6,2},{2,0},{1,5},{5,9},... | collective-permute-start | bytes 1572872 | tf_op jit(solution)/shard_map/ppermute | solution.py:356
  43.6 22.2 %copy-start.7 = (bf16[2304,128]{1,0:T(8,128)(2,1)S(1)}, bf16[2304,128]{1,0:T(8,128)(2,1)}, u32[]{:S(2)}) copy-start(bf16[2304,128]{1,0:T(8,128)(2,1)} %get-tuple-element.109) | copy-start | bytes 1769476
  43.6 22.1 %copy-start.5 = (bf16[64,4352]{1,0:T(8,128)(2,1)}, bf16[64,4352]{1,0:T(8,128)(2,1)S(1)}, u32[]{:S(2)}) copy-start(bf16[64,4352]{1,0:T(8,128)(2,1)S(1)} %collective-permute-done.8.refs_5_.refs_15_.refs_25_) | copy-start | bytes 1671172
  43.6 23.2 %collective-permute-start.12 = (bf16[128,2048]{1,0:T(8,128)(2,1)}, bf16[128,2048]{1,0:T(8,128)(2,1)}, u32[]{:S(2)}, u32[]{:S(2)}) collective-permute-start(bf16[128,2048]{1,0:T(8,128)(2,1)} %collective-permute-done.7.refs_3_), channel_id=1, source_target_pairs={{0,2},{4,0},{8,4},{12,8},{14,12},{10,14},{6,10},{2,6},{1,3},{5,1},... | collective-permute-start | bytes 1572872 | tf_op jit(solution)/shard_map/ppermute | solution.py:356
  53.9 21.0 %collective-permute-start.9 = (bf16[128,2176]{1,0:T(8,128)(2,1)S(1)}, bf16[128,2176]{1,0:T(8,128)(2,1)S(1)}, u32[]{:S(2)}, u32[]{:S(2)}) collective-permute-start(bf16[128,2176]{1,0:T(8,128)(2,1)S(1)} %collective-permute-done.4.refs_0_), channel_id=1, source_target_pairs={{0,4},{4,8},{8,12},{12,14},{14,10},{10,6},{6,2},{2,0},{1,5},{5,9},... | collective-permute-start | bytes 1671176 | tf_op jit(solution)/shard_map/ppermute | solution.py:356
  55.5 21.7 %collective-permute-start.10 = (bf16[128,2176]{1,0:T(8,128)(2,1)S(1)}, bf16[128,2176]{1,0:T(8,128)(2,1)}, u32[]{:S(2)}, u32[]{:S(2)}) collective-permute-start(bf16[128,2176]{1,0:T(8,128)(2,1)S(1)} %collective-permute-done.5.refs_1_), channel_id=1, source_target_pairs={{0,2},{4,0},{8,4},{12,8},{14,12},{10,14},{6,10},{2,6},{1,3},{5,1},... | collective-permute-start | bytes 1671176 | tf_op jit(solution)/shard_map/ppermute | solution.py:356
  65.7 31.3 %collective-permute-start.18 = (bf16[128,4352]{1,0:T(8,128)(2,1)}, bf16[128,4352]{1,0:T(8,128)(2,1)S(1)}, u32[]{:S(2)}, u32[]{:S(2)}) collective-permute-start(bf16[128,4352]{1,0:T(8,128)(2,1)} %get-tuple-element.142.refs_22_), channel_id=1, source_target_pairs={{0,1},{1,0},{2,3},{3,2},{4,5},{5,4},{6,7},{7,6},{8,9},{9,8},{10,11... | collective-permute-start | bytes 3342344 | tf_op jit(solution)/shard_map/ppermute | solution.py:359
  66.9 15.8 %collective-permute-start.14 = (bf16[64,2048]{1,0:T(8,128)(2,1)S(1)}, bf16[64,2048]{1,0:T(8,128)(2,1)S(1)}, u32[]{:S(2)}, u32[]{:S(2)}) collective-permute-start(bf16[64,2048]{1,0:T(8,128)(2,1)S(1)} %copy-done.26), channel_id=1, source_target_pairs={{0,2},{4,0},{8,4},{12,8},{14,12},{10,14},{6,10},{2,6},{1,3},{5,1},... | collective-permute-start | bytes 786440 | tf_op jit(solution)/shard_map/ppermute | solution.py:356
  66.9 27.1 %copy-start.2 = (bf16[128,4352]{1,0:T(8,128)(2,1)}, bf16[128,4352]{1,0:T(8,128)(2,1)S(1)}, u32[]{:S(2)}) copy-start(bf16[128,4352]{1,0:T(8,128)(2,1)S(1)} %collective-permute-done.13.refs_6_.refs_16_.refs_26_) | copy-start | bytes 3342340
  66.9 17.1 %collective-permute-start.15 = (bf16[64,2048]{1,0:T(8,128)(2,1)S(1)}, bf16[64,2048]{1,0:T(8,128)(2,1)S(1)}, u32[]{:S(2)}, u32[]{:S(2)}) collective-permute-start(bf16[64,2048]{1,0:T(8,128)(2,1)S(1)} %copy-done.25), channel_id=1, source_target_pairs={{0,4},{4,8},{8,12},{12,14},{14,10},{10,6},{6,2},{2,0},{1,5},{5,9},... | collective-permute-start | bytes 786440 | tf_op jit(solution)/shard_map/ppermute | solution.py:356
  74.9 20.5 %collective-permute-start.17 = (bf16[128,2048]{1,0:T(8,128)(2,1)}, bf16[128,2048]{1,0:T(8,128)(2,1)}, u32[]{:S(2)}, u32[]{:S(2)}) collective-permute-start(bf16[128,2048]{1,0:T(8,128)(2,1)} %collective-permute-done.12.refs_3_), channel_id=1, source_target_pairs={{0,2},{4,0},{8,4},{12,8},{14,12},{10,14},{6,10},{2,6},{1,3},{5,1},... | collective-permute-start | bytes 1572872 | tf_op jit(solution)/shard_map/ppermute | solution.py:356
  77.2 26.4 %collective-permute-start.16 = (bf16[128,2176]{1,0:T(8,128)(2,1)S(1)}, bf16[128,2176]{1,0:T(8,128)(2,1)S(1)}, u32[]{:S(2)}, u32[]{:S(2)}) collective-permute-start(bf16[128,2176]{1,0:T(8,128)(2,1)S(1)} %collective-permute-done.9.refs_0_), channel_id=1, source_target_pairs={{0,4},{4,8},{8,12},{12,14},{14,10},{10,6},{6,2},{2,0},{1,5},{5,9},... | collective-permute-start | bytes 1671176 | tf_op jit(solution)/shard_map/ppermute | solution.py:356
  82.7 36.1 %collective-permute-start.19 = (bf16[64,2048]{1,0:T(8,128)(2,1)}, bf16[64,2048]{1,0:T(8,128)(2,1)S(1)}, u32[]{:S(2)}, u32[]{:S(2)}) collective-permute-start(bf16[64,2048]{1,0:T(8,128)(2,1)} %get-tuple-element.146), channel_id=1, source_target_pairs={{0,6},{4,2},{8,0},{12,4},{14,8},{10,12},{6,14},{2,10},{1,7},{5,3},... | collective-permute-start | bytes 786440 | tf_op jit(solution)/shard_map/ppermute | solution.py:356
  94.1 28.2 %collective-permute-start.21 = (bf16[128,4352]{1,0:T(8,128)(2,1)}, bf16[128,4352]{1,0:T(8,128)(2,1)S(1)}, u32[]{:S(2)}, u32[]{:S(2)}) collective-permute-start(bf16[128,4352]{1,0:T(8,128)(2,1)} %get-tuple-element.157.refs_23_), channel_id=1, source_target_pairs={{0,1},{1,0},{2,3},{3,2},{4,5},{5,4},{6,7},{7,6},{8,9},{9,8},{10,11... | collective-permute-start | bytes 3342344 | tf_op jit(solution)/shard_map/ppermute | solution.py:359
  95.4 23.4 %collective-permute-start.20 = (bf16[64,2048]{1,0:T(8,128)(2,1)S(1)}, bf16[64,2048]{1,0:T(8,128)(2,1)S(1)}, u32[]{:S(2)}, u32[]{:S(2)}) collective-permute-start(bf16[64,2048]{1,0:T(8,128)(2,1)S(1)} %copy-done.28), channel_id=1, source_target_pairs={{0,8},{4,12},{8,14},{12,10},{14,6},{10,2},{6,0},{2,4},{1,9},{5,13}... | collective-permute-start | bytes 786440 | tf_op jit(solution)/shard_map/ppermute | solution.py:356
  97.0 17.2 %copy-start.3 = (bf16[128,4352]{1,0:T(8,128)(2,1)}, bf16[128,4352]{1,0:T(8,128)(2,1)S(1)}, u32[]{:S(2)}) copy-start(bf16[128,4352]{1,0:T(8,128)(2,1)S(1)} %collective-permute-done.18.refs_7_.refs_17_.refs_27_) | copy-start | bytes 3342340
  97.0 47.3 %collective-permute-start.25 = (bf16[64,2048]{1,0:T(8,128)(2,1)S(1)}, bf16[64,2048]{1,0:T(8,128)(2,1)S(1)}, u32[]{:S(2)}, u32[]{:S(2)}) collective-permute-start(bf16[64,2048]{1,0:T(8,128)(2,1)S(1)} %copy-done.27), channel_id=1, source_target_pairs={{0,12},{4,14},{8,10},{12,6},{14,2},{10,0},{6,4},{2,8},{1,13},{5,15... | collective-permute-start | bytes 786440 | tf_op jit(solution)/shard_map/ppermute | solution.py:356
  103.6 40.8 %collective-permute-start.26 = (bf16[64,2048]{1,0:T(8,128)(2,1)}, bf16[64,2048]{1,0:T(8,128)(2,1)S(1)}, u32[]{:S(2)}, u32[]{:S(2)}) collective-permute-start(bf16[64,2048]{1,0:T(8,128)(2,1)} %get-tuple-element.171), channel_id=1, source_target_pairs={{0,10},{4,6},{8,2},{12,0},{14,4},{10,8},{6,12},{2,14},{1,11},{5,7}... | collective-permute-start | bytes 786440 | tf_op jit(solution)/shard_map/ppermute | solution.py:356
  118.8 25.6 %collective-permute-start.27 = (bf16[64,2048]{1,0:T(8,128)(2,1)}, bf16[64,2048]{1,0:T(8,128)(2,1)}, u32[]{:S(2)}, u32[]{:S(2)}) collective-permute-start(bf16[64,2048]{1,0:T(8,128)(2,1)} %get-tuple-element.173), channel_id=1, source_target_pairs={{0,14},{4,10},{8,6},{12,2},{14,0},{10,4},{6,8},{2,12},{1,15},{5,11... | collective-permute-start | bytes 786440 | tf_op jit(solution)/shard_map/ppermute | solution.py:356
  121.3 9.5 %collective-permute-start.24 = (bf16[64,4352]{1,0:T(8,128)(2,1)S(1)}, bf16[64,4352]{1,0:T(8,128)(2,1)S(1)}, u32[]{:S(2)}, u32[]{:S(2)}) collective-permute-start(bf16[64,4352]{1,0:T(8,128)(2,1)S(1)} %copy-done.10), channel_id=1, source_target_pairs={{0,1},{1,0},{2,3},{3,2},{4,5},{5,4},{6,7},{7,6},{8,9},{9,8},{10,11... | collective-permute-start | bytes 1671176 | tf_op jit(solution)/shard_map/ppermute | solution.py:359
  122.3 22.1 %collective-permute-start.22 = (bf16[288,256]{1,0:T(8,128)(2,1)S(1)}, bf16[288,256]{1,0:T(8,128)(2,1)S(1)}, u32[]{:S(2)}, u32[]{:S(2)}) collective-permute-start(bf16[288,256]{1,0:T(8,128)(2,1)S(1)} %get-tuple-element.158), channel_id=1, source_target_pairs={{0,4},{4,8},{8,12},{12,14},{14,10},{10,6},{6,2},{2,0},{1,5},{5,9},... | collective-permute-start | bytes 442376 | tf_op jit(solution)/shard_map/ppermute | solution.py:356
  130.8 13.6 %collective-permute-start.23 = (bf16[288,256]{1,0:T(8,128)(2,1)S(1)}, bf16[288,256]{1,0:T(8,128)(2,1)S(1)}, u32[]{:S(2)}, u32[]{:S(2)}) collective-permute-start(bf16[288,256]{1,0:T(8,128)(2,1)S(1)} %get-tuple-element.159), channel_id=1, source_target_pairs={{0,2},{4,0},{8,4},{12,8},{14,12},{10,14},{6,10},{2,6},{1,3},{5,1},... | collective-permute-start | bytes 442376 | tf_op jit(solution)/shard_map/ppermute | solution.py:356
  133.5 13.2 %copy-start.18 = (bf16[288,256]{1,0:T(8,128)(2,1)S(1)}, bf16[288,256]{1,0:T(8,128)(2,1)}, u32[]{:S(2)}) copy-start(bf16[288,256]{1,0:T(8,128)(2,1)} %get-tuple-element.180) | copy-start | bytes 442372
  144.3 27.4 %collective-permute-start.41 = (bf16[512,2048]{1,0:T(8,128)(2,1)}, bf16[512,2048]{1,0:T(8,128)(2,1)S(1)}, u32[]{:S(2)}, u32[]{:S(2)}) collective-permute-start(bf16[512,2048]{1,0:T(8,128)(2,1)} %get-tuple-element.206), channel_id=1, source_target_pairs={{0,1},{1,0},{2,3},{3,2},{4,5},{5,4},{6,7},{7,6},{8,9},{9,8},{10,11... | collective-permute-start | bytes 6291464 | tf_op jit(solution)/shard_map/ppermute | solution.py:359
  144.5 6.7 %collective-permute-start.37 = (bf16[288,256]{1,0:T(8,128)(2,1)S(1)}, bf16[288,256]{1,0:T(8,128)(2,1)S(1)}, u32[]{:S(2)}, u32[]{:S(2)}) collective-permute-start(bf16[288,256]{1,0:T(8,128)(2,1)S(1)} %broadcast_select_fusion.2), channel_id=1, source_target_pairs={{0,2},{4,0},{8,4},{12,8},{14,12},{10,14},{6,10},{2,6},{1,3},{5,1},... | collective-permute-start | bytes 442376 | tf_op jit(solution)/shard_map/ppermute | solution.py:356
  145.7 8.7 %collective-permute-start.34 = (bf16[288,256]{1,0:T(8,128)(2,1)S(1)}, bf16[288,256]{1,0:T(8,128)(2,1)S(1)}, u32[]{:S(2)}, u32[]{:S(2)}) collective-permute-start(bf16[288,256]{1,0:T(8,128)(2,1)S(1)} %copy-done.17), channel_id=1, source_target_pairs={{0,2},{4,0},{8,4},{12,8},{14,12},{10,14},{6,10},{2,6},{1,3},{5,1},... | collective-permute-start | bytes 442376 | tf_op jit(solution)/shard_map/ppermute | solution.py:356
  146.6 8.9 %collective-permute-start.31 = (bf16[288,256]{1,0:T(8,128)(2,1)S(1)}, bf16[288,256]{1,0:T(8,128)(2,1)S(1)}, u32[]{:S(2)}, u32[]{:S(2)}) collective-permute-start(bf16[288,256]{1,0:T(8,128)(2,1)S(1)} %copy-done.18), channel_id=1, source_target_pairs={{0,4},{4,8},{8,12},{12,14},{14,10},{10,6},{6,2},{2,0},{1,5},{5,9},... | collective-permute-start | bytes 442376 | tf_op jit(solution)/shard_map/ppermute | solution.py:356
  147.7 8.8 %collective-permute-start.28 = (bf16[288,256]{1,0:T(8,128)(2,1)S(1)}, bf16[288,256]{1,0:T(8,128)(2,1)S(1)}, u32[]{:S(2)}, u32[]{:S(2)}) collective-permute-start(bf16[288,256]{1,0:T(8,128)(2,1)S(1)} %broadcast_select_fusion.9), channel_id=1, source_target_pairs={{0,4},{4,8},{8,12},{12,14},{14,10},{10,6},{6,2},{2,0},{1,5},{5,9},... | collective-permute-start | bytes 442376 | tf_op jit(solution)/shard_map/ppermute | solution.py:356
  151.2 6.6 %collective-permute-start.38 = (bf16[288,256]{1,0:T(8,128)(2,1)S(1)}, bf16[288,256]{1,0:T(8,128)(2,1)S(1)}, u32[]{:S(2)}, u32[]{:S(2)}) collective-permute-start(bf16[288,256]{1,0:T(8,128)(2,1)S(1)} %broadcast_select_fusion.1), channel_id=1, source_target_pairs={{0,2},{4,0},{8,4},{12,8},{14,12},{10,14},{6,10},{2,6},{1,3},{5,1},... | collective-permute-start | bytes 442376 | tf_op jit(solution)/shard_map/ppermute | solution.py:356
  154.4 6.8 %collective-permute-start.35 = (bf16[288,256]{1,0:T(8,128)(2,1)S(1)}, bf16[288,256]{1,0:T(8,128)(2,1)S(1)}, u32[]{:S(2)}, u32[]{:S(2)}) collective-permute-start(bf16[288,256]{1,0:T(8,128)(2,1)S(1)} %broadcast_select_fusion.4), channel_id=1, source_target_pairs={{0,2},{4,0},{8,4},{12,8},{14,12},{10,14},{6,10},{2,6},{1,3},{5,1},... | collective-permute-start | bytes 442376 | tf_op jit(solution)/shard_map/ppermute | solution.py:356
  155.6 6.8 %collective-permute-start.32 = (bf16[288,256]{1,0:T(8,128)(2,1)S(1)}, bf16[288,256]{1,0:T(8,128)(2,1)S(1)}, u32[]{:S(2)}, u32[]{:S(2)}) collective-permute-start(bf16[288,256]{1,0:T(8,128)(2,1)S(1)} %broadcast_select_fusion.6), channel_id=1, source_target_pairs={{0,4},{4,8},{8,12},{12,14},{14,10},{10,6},{6,2},{2,0},{1,5},{5,9},... | collective-permute-start | bytes 442376 | tf_op jit(solution)/shard_map/ppermute | solution.py:356
  156.6 7.4 %collective-permute-start.29 = (bf16[288,256]{1,0:T(8,128)(2,1)S(1)}, bf16[288,256]{1,0:T(8,128)(2,1)S(1)}, u32[]{:S(2)}, u32[]{:S(2)}) collective-permute-start(bf16[288,256]{1,0:T(8,128)(2,1)S(1)} %broadcast_select_fusion.8), channel_id=1, source_target_pairs={{0,4},{4,8},{8,12},{12,14},{14,10},{10,6},{6,2},{2,0},{1,5},{5,9},... | collective-permute-start | bytes 442376 | tf_op jit(solution)/shard_map/ppermute | solution.py:356
  157.9 10.3 %collective-permute-start.39 = (bf16[288,256]{1,0:T(8,128)(2,1)S(1)}, bf16[288,256]{1,0:T(8,128)(2,1)S(1)}, u32[]{:S(2)}, u32[]{:S(2)}) collective-permute-start(bf16[288,256]{1,0:T(8,128)(2,1)S(1)} %broadcast_select_fusion), channel_id=1, source_target_pairs={{0,2},{4,0},{8,4},{12,8},{14,12},{10,14},{6,10},{2,6},{1,3},{5,1},... | collective-permute-start | bytes 442376 | tf_op jit(solution)/shard_map/ppermute | solution.py:356
  161.2 6.9 %collective-permute-start.36 = (bf16[288,256]{1,0:T(8,128)(2,1)S(1)}, bf16[288,256]{1,0:T(8,128)(2,1)S(1)}, u32[]{:S(2)}, u32[]{:S(2)}) collective-permute-start(bf16[288,256]{1,0:T(8,128)(2,1)S(1)} %broadcast_select_fusion.3), channel_id=1, source_target_pairs={{0,2},{4,0},{8,4},{12,8},{14,12},{10,14},{6,10},{2,6},{1,3},{5,1},... | collective-permute-start | bytes 442376 | tf_op jit(solution)/shard_map/ppermute | solution.py:356
  162.4 5.8 %collective-permute-start.33 = (bf16[288,256]{1,0:T(8,128)(2,1)S(1)}, bf16[288,256]{1,0:T(8,128)(2,1)S(1)}, u32[]{:S(2)}, u32[]{:S(2)}) collective-permute-start(bf16[288,256]{1,0:T(8,128)(2,1)S(1)} %broadcast_select_fusion.5), channel_id=1, source_target_pairs={{0,4},{4,8},{8,12},{12,14},{14,10},{10,6},{6,2},{2,0},{1,5},{5,9},... | collective-permute-start | bytes 442376 | tf_op jit(solution)/shard_map/ppermute | solution.py:356
  164.0 5.9 %collective-permute-start.30 = (bf16[288,256]{1,0:T(8,128)(2,1)S(1)}, bf16[288,256]{1,0:T(8,128)(2,1)}, u32[]{:S(2)}, u32[]{:S(2)}) collective-permute-start(bf16[288,256]{1,0:T(8,128)(2,1)S(1)} %broadcast_select_fusion.7), channel_id=1, source_target_pairs={{0,4},{4,8},{8,12},{12,14},{14,10},{10,6},{6,2},{2,0},{1,5},{5,9},... | collective-permute-start | bytes 442376 | tf_op jit(solution)/shard_map/ppermute | solution.py:356
  170.0 1.6 collective-permute-start.40
  (23 other events, 128.9 us)

commit v14 on v13

--- a/solution.py
+++ b/solution.py
@@ -198,14 +198,20 @@
 
 def gradient_kernel(units, count, scal, *refs):
     ins, cots, grads = refs[: 2 * count], refs[2 * count : 4 * count], refs[4 * count : 6 * count]
-    out = refs[6 * count]
+    out, joined = refs[6 * count :]
     keep = scal[0] != scal[2]
+
+    @pl.when(pl.program_id(0) == 0)
+    def _():
+        at = 0
+        for ref in grads:
+            joined[at : at + ref.shape[0], :] = ref[...]
+            at += ref.shape[0]
+
     left = jnp.concatenate([ref[...] for ref in ins], axis=0)
-    right = jnp.concatenate([ref[:, : 2 * units] for ref in grads], axis=0)
-    out[0, :, : 2 * units] = jnp.where(keep, dot(left, right, (0, 0)), 0.0)
+    out[0, :, : 2 * units] = jnp.where(keep, dot(left, joined[:, : 2 * units], (0, 0)), 0.0)
     left = jnp.concatenate([ref[...] for ref in cots], axis=0)
-    right = jnp.concatenate([ref[:, 2 * units :] for ref in grads], axis=0)
-    out[0, :, 2 * units :] = jnp.where(keep, dot(left, right, (0, 0)), 0.0)
+    out[0, :, 2 * units :] = jnp.where(keep, dot(left, joined[:, 2 * units :], (0, 0)), 0.0)
 
 
 def expert_gradient(units, scal, mine, packs, others):
@@ -229,6 +235,7 @@
         out_shape=jax.ShapeDtypeStruct((1, width // 2, columns), F32),
         in_specs=in_specs,
         out_specs=pl.BlockSpec((1, tile, columns), lambda i: (0, i, 0)),
+        scratch_shapes=[pltpu.VMEM((total, columns), BF16)],
         compiler_params=pltpu.CompilerParams(vmem_limit_bytes=VMEM_BYTES),
         cost_estimate=pl.CostEstimate(
             flops=width * columns * total, bytes_accessed=3 * width * columns, transcendentals=0

time: 175 us -> 176 us (level)
  transfers between devices with their start and end apart: 42 -> 42, of which waited for: 16 -> 16; matrix products, arithmetic and copies ran while one was open for 2% -> 3% of each run, Pallas kernels for 40% -> 40%
where the time goes in v14:
time: 176 us; the launch traced here: 175 us
  Pallas kernels  71.9 us (41%)
  starting transfers between devices  55.6 us (32%)
  waiting for transfers between devices  39.3 us (22%)
  other arithmetic  3.43 us (2%)
  local copies, waits for them, and re-layouts  3.23 us (2%)
  between operations  1.84 us (1%)
    ppermute x35, starting transfers between devices, shift(): return lax.ppermute(block, 'expert', pairs)  55.2 us
    pallas_call x5, Pallas kernels, run_step(): pl.pallas_call(functools.partial(step_kernel, steps, fanout, capacity, jo...  48.6 us
    ppermute x35, waiting for transfers between devices, shift(): return lax.ppermute(block, 'expert', pairs)  37.7 us
    pallas_call x1, Pallas kernels, expert_gradient(): pl.pallas_call(functools.partial(gradient_kernel, units, count), grid=(ti...  11.1 us
    pallas_call x1, Pallas kernels, ordered(): pl.pallas_call(functools.partial(order_kernel, plan, experts, capacity),...  4.64 us
  transfers between devices with their start and end apart: 42, of which 16 were waited for; matrix products, arithmetic and copies ran while one was open for 3% of the time, Pallas kernels for 40%

profile of v14, /device:TPU:0, one launch (start us, length us, event | category | flops | bytes accessed | tf_op | source)
XLA Modules:
  0.0 175.3 jit_solution(11473141162861452875)
XLA Ops:
  0.6 3.1 %collective-permute-start.2 = (bf16[128,2048]{1,0:T(8,128)(2,1)}, bf16[128,2048]{1,0:T(8,128)(2,1)S(1)}, u32[]{:S(2)}, u32[]{:S(2)}) collective-permute-start(bf16[128,2048]{1,0:T(8,128)(2,1)} %refs_1_.1), channel_id=1, source_target_pairs={{0,4},{4,8},{8,12},{12,14},{14,10},{10,6},{6,2},{2,0},{1,5},{5,9},... | collective-permute-start | bytes 1572872 | tf_op jit(solution)/shard_map/ppermute | solution.py:363
  3.7 2.0 %ring_message.1 = (bf16[128,2176]{1,0:T(8,128)(2,1)}, bf16[128,128]{1,0:T(8,128)(2,1)}) custom-call(bf16[128,2048]{1,0:T(8,128)(2,1)} %tokens.1, s32[2,128]{1,0:T(2,128)} %bitcast.17, f32[2,128]{1,0:T(2,128)} %bitcast.18, f32[1,128]{1,0:T(1,128)} %bitcast.19, s32[1,128]{1,0:T(1,128)} %bitcast.20), custom_call_target="tpu_custom_call" | custom-call | bytes 1048576 | tf_op jit(solution)/shard_map/ring_message/pallas_call | solution.py:269
  5.7 2.0 %collective-permute-start = (bf16[128,2176]{1,0:T(8,128)(2,1)}, bf16[128,2176]{1,0:T(8,128)(2,1)S(1)}, u32[]{:S(2)}, u32[]{:S(2)}) collective-permute-start(bf16[128,2176]{1,0:T(8,128)(2,1)} %get-tuple-element.105.refs_0_), channel_id=1, source_target_pairs={{0,4},{4,8},{8,12},{12,14},{14,10},{10,6},{6,2},{2,0},{1,5},{5,9},... | collective-permute-start | bytes 1671176 | tf_op jit(solution)/shard_map/ppermute | solution.py:363
  9.1 9.4 %expert_step.5 = (bf16[64,2048]{1,0:T(8,128)(2,1)}, bf16[64,4352]{1,0:T(8,128)(2,1)}, bf16[64,4096]{1,0:T(8,128)(2,1)}, bf16[64,2048]{1,0:T(8,128)(2,1)}) custom-call(s32[3]{0:T(128)} %pad_add_fusion.scal, bf16[128,2176]{1,0:T(8,128)(2,1)} %get-tuple-element.105.refs_0_, bf16[128,2048]{1,0:T(8,128)(2,1)} %refs_1_.1, bf16[2048,1536]{1,0:T(8,128)(2,1)} %bitcast.21, ...), custom_call_target="tpu_custom_call" | custom-call | flops 4026531840 | bytes 9437184 | tf_op jit(solution)/shard_map/expert_step/pallas_call | solution.py:151
  18.9 1.7 collective-permute-start.6
  20.9 7.7 %collective-permute-done.refs_0_ = bf16[128,2176]{1,0:T(8,128)(2,1)S(1)} collective-permute-done((bf16[128,2176]{1,0:T(8,128)(2,1)}, bf16[128,2176]{1,0:T(8,128)(2,1)S(1)}, u32[]{:S(2)}, u32[]{:S(2)}) %collective-permute-start) | collective-permute-done | bytes 557088 | tf_op jit(solution)/shard_map/ppermute | solution.py:363
  28.6 2.1 %collective-permute-start.4 = (bf16[128,2176]{1,0:T(8,128)(2,1)S(1)}, bf16[128,2176]{1,0:T(8,128)(2,1)S(1)}, u32[]{:S(2)}, u32[]{:S(2)}) collective-permute-start(bf16[128,2176]{1,0:T(8,128)(2,1)S(1)} %collective-permute-done.refs_0_), channel_id=1, source_target_pairs={{0,4},{4,8},{8,12},{12,14},{14,10},{10,6},{6,2},{2,0},{1,5},{5,9},... | collective-permute-start | bytes 1671176 | tf_op jit(solution)/shard_map/ppermute | solution.py:363
  30.8 9.8 %expert_step.6 = (bf16[128,2048]{1,0:T(8,128)(2,1)}, bf16[128,4352]{1,0:T(8,128)(2,1)}, bf16[128,4096]{1,0:T(8,128)(2,1)}, bf16[64,2048]{1,0:T(8,128)(2,1)}, bf1...) custom-call(s32[3]{0:T(128)} %pad_add_fusion.scal, bf16[128,2176]{1,0:T(8,128)(2,1)} %copy-done.21, ...), custom_call_target="tpu_custom_call" | custom-call | flops 4026531840 | bytes 9437184 | tf_op jit(solution)/shard_map/expert_step/pallas_call | solution.py:151
  40.8 1.3 collective-permute-done.7.refs_3_
  42.0 1.6 collective-permute-start.11
  44.1 7.6 %collective-permute-done.4.refs_0_ = bf16[128,2176]{1,0:T(8,128)(2,1)S(1)} collective-permute-done((bf16[128,2176]{1,0:T(8,128)(2,1)S(1)}, bf16[128,2176]{1,0:T(8,128)(2,1)S(1)}, u32[]{:S(2)}, u32[]{:S(2)}) %collective-permute-start.4) | collective-permute-done | bytes 557088 | tf_op jit(solution)/shard_map/ppermute | solution.py:363
  51.7 2.1 %collective-permute-done.5.refs_1_ = bf16[128,2176]{1,0:T(8,128)(2,1)S(1)} collective-permute-done((bf16[128,2176]{1,0:T(8,128)(2,1)}, bf16[128,2176]{1,0:T(8,128)(2,1)S(1)}, u32[]{:S(2)}, u32[]{:S(2)}) %collective-permute-start.5) | collective-permute-done | bytes 557088 | tf_op jit(solution)/shard_map/ppermute | solution.py:363
  53.9 1.6 collective-permute-start.9
  55.9 9.8 %expert_step.7 = (bf16[128,2048]{1,0:T(8,128)(2,1)}, bf16[128,4352]{1,0:T(8,128)(2,1)}, bf16[128,4096]{1,0:T(8,128)(2,1)}, bf16[64,2048]{1,0:T(8,128)(2,1)}, bf1...) custom-call(s32[3]{0:T(128)} %pad_add_fusion.scal, bf16[128,2176]{1,0:T(8,128)(2,1)} %copy-done.19, ...), custom_call_target="tpu_custom_call" | custom-call | flops 4026531840 | bytes 9437184 | tf_op jit(solution)/shard_map/expert_step/pallas_call | solution.py:151
  66.9 2.0 %collective-permute-start.15 = (bf16[64,2048]{1,0:T(8,128)(2,1)S(1)}, bf16[64,2048]{1,0:T(8,128)(2,1)S(1)}, u32[]{:S(2)}, u32[]{:S(2)}) collective-permute-start(bf16[64,2048]{1,0:T(8,128)(2,1)S(1)} %copy-done.25), channel_id=1, source_target_pairs={{0,4},{4,8},{8,12},{12,14},{14,10},{10,6},{6,2},{2,0},{1,5},{5,9},... | collective-permute-start | bytes 786440 | tf_op jit(solution)/shard_map/ppermute | solution.py:363
  69.1 5.8 %collective-permute-done.9.refs_0_ = bf16[128,2176]{1,0:T(8,128)(2,1)S(1)} collective-permute-done((bf16[128,2176]{1,0:T(8,128)(2,1)S(1)}, bf16[128,2176]{1,0:T(8,128)(2,1)S(1)}, u32[]{:S(2)}, u32[]{:S(2)}) %collective-permute-start.9) | collective-permute-done | bytes 557088 | tf_op jit(solution)/shard_map/ppermute | solution.py:363
  74.9 2.1 %collective-permute-start.17 = (bf16[128,2048]{1,0:T(8,128)(2,1)}, bf16[128,2048]{1,0:T(8,128)(2,1)}, u32[]{:S(2)}, u32[]{:S(2)}) collective-permute-start(bf16[128,2048]{1,0:T(8,128)(2,1)} %collective-permute-done.12.refs_3_), channel_id=1, source_target_pairs={{0,2},{4,0},{8,4},{12,8},{14,12},{10,14},{6,10},{2,6},{1,3},{5,1},... | collective-permute-start | bytes 1572872 | tf_op jit(solution)/shard_map/ppermute | solution.py:363
  77.2 1.6 collective-permute-start.16
  79.4 3.2 %collective-permute-done.14.refs_7_ = bf16[64,2048]{1,0:T(8,128)(2,1)S(1)} collective-permute-done((bf16[64,2048]{1,0:T(8,128)(2,1)S(1)}, bf16[64,2048]{1,0:T(8,128)(2,1)S(1)}, u32[]{:S(2)}, u32[]{:S(2)}) %collective-permute-start.14) | collective-permute-done | bytes 262176 | tf_op jit(solution)/shard_map/ppermute | solution.py:363
  82.7 1.4 collective-permute-start.19
  84.1 9.9 %expert_step.8 = (bf16[128,2048]{1,0:T(8,128)(2,1)}, bf16[128,4352]{1,0:T(8,128)(2,1)}, bf16[128,4096]{1,0:T(8,128)(2,1)}, bf16[64,2048]{1,0:T(8,128)(2,1)}, bf1...) custom-call(s32[3]{0:T(128)} %pad_add_fusion.scal, bf16[128,2176]{1,0:T(8,128)(2,1)} %copy-done.22, ...), custom_call_target="tpu_custom_call" | custom-call | flops 4026531840 | bytes 9437184 | tf_op jit(solution)/shard_map/expert_step/pallas_call | solution.py:151
  94.1 1.2 constant_dynamic-slice_fusion.1
  95.4 1.6 collective-permute-start.20
  97.0 6.6 %collective-permute-start.25 = (bf16[64,2048]{1,0:T(8,128)(2,1)S(1)}, bf16[64,2048]{1,0:T(8,128)(2,1)S(1)}, u32[]{:S(2)}, u32[]{:S(2)}) collective-permute-start(bf16[64,2048]{1,0:T(8,128)(2,1)S(1)} %copy-done.27), channel_id=1, source_target_pairs={{0,12},{4,14},{8,10},{12,6},{14,2},{10,0},{6,4},{2,8},{1,13},{5,15... | collective-permute-start | bytes 786440 | tf_op jit(solution)/shard_map/ppermute | solution.py:363
  104.4 9.7 %expert_step.9 = (bf16[64,2048]{1,0:T(8,128)(2,1)}, bf16[64,4352]{1,0:T(8,128)(2,1)}, bf16[64,4096]{1,0:T(8,128)(2,1)}, bf16[64,2048]{1,0:T(8,128)(2,1)}, bf16[2304,128]{1,0:T(8,128)(2,1)}) custom-call(s32[3]{0:T(128)} %pad_add_fusion.scal, bf16[128,2176]{1,0:T(8,128)(2,1)} %copy-done.23, bf16[128,2048]{1,0:T(8,128)(2,1)} %collective-permute-done.17.refs_1_, ...), custom_call_target="tpu_custom_call" | custom-call | flops 4026531840 | bytes 9437184 | tf_op jit(solution)/shard_map/expert_step/pallas_call | solution.py:151
  114.2 4.6 %hot_rows_ordered.1 = (bf16[512,2048]{1,0:T(8,128)(2,1)}, bf16[512,2048]{1,0:T(8,128)(2,1)}) custom-call(s32[3]{0:T(128)} %pad_add_fusion.scal, bf16[64,4096]{1,0:T(8,128)(2,1)} %get-tuple-element.149.refs_0_, bf16[128,4096]{1,0:T(8,128)(2,1)} %get-tuple-element.150.refs_1_, bf16[128,4096]{1,0:T(8,128)(2,1)} %get-tuple-element.151.refs_2_, ...), custom_call_target="tpu_custom_call" | custom-call | bytes 8388608 | tf_op jit(solution)/shard_map/hot_rows_ordered/pallas_call | solution.py:297
  118.8 2.5 %collective-permute-start.27 = (bf16[64,2048]{1,0:T(8,128)(2,1)}, bf16[64,2048]{1,0:T(8,128)(2,1)}, u32[]{:S(2)}, u32[]{:S(2)}) collective-permute-start(bf16[64,2048]{1,0:T(8,128)(2,1)} %get-tuple-element.173), channel_id=1, source_target_pairs={{0,14},{4,10},{8,6},{12,2},{14,0},{10,4},{6,8},{2,12},{1,15},{5,11... | collective-permute-start | bytes 786440 | tf_op jit(solution)/shard_map/ppermute | solution.py:363
  122.3 8.5 %collective-permute-start.22 = (bf16[288,256]{1,0:T(8,128)(2,1)S(1)}, bf16[288,256]{1,0:T(8,128)(2,1)S(1)}, u32[]{:S(2)}, u32[]{:S(2)}) collective-permute-start(bf16[288,256]{1,0:T(8,128)(2,1)S(1)} %get-tuple-element.158), channel_id=1, source_target_pairs={{0,4},{4,8},{8,12},{12,14},{14,10},{10,6},{6,2},{2,0},{1,5},{5,9},... | collective-permute-start | bytes 442376 | tf_op jit(solution)/shard_map/ppermute | solution.py:363
  130.8 2.6 %collective-permute-start.23 = (bf16[288,256]{1,0:T(8,128)(2,1)S(1)}, bf16[288,256]{1,0:T(8,128)(2,1)S(1)}, u32[]{:S(2)}, u32[]{:S(2)}) collective-permute-start(bf16[288,256]{1,0:T(8,128)(2,1)S(1)} %get-tuple-element.159), channel_id=1, source_target_pairs={{0,2},{4,0},{8,4},{12,8},{14,12},{10,14},{6,10},{2,6},{1,3},{5,1},... | collective-permute-start | bytes 442376 | tf_op jit(solution)/shard_map/ppermute | solution.py:363
  133.5 11.1 %expert_gradient.1 = f32[1,1024,2304]{2,1,0:T(8,128)} custom-call(s32[3]{0:T(128)} %pad_add_fusion.scal, bf16[64,2048]{1,0:T(8,128)(2,1)} %get-tuple-element.160.refs_0_.refs_10_, bf16[128,2048]{1,0:T(8,128)(2,1)} %get-tuple-element.161.refs_1_.refs_11_, bf16[128,2048]{1,0:T(8,128)(2,1)} %get-tuple-element.162.refs_2_.refs_12_, ...), custom_call_target="tpu_custom_call" | custom-call | flops 4831838208 | bytes 14155776 | tf_op jit(solution)/shard_map/expert_gradient/pallas_call | solution.py:232
  144.8 1.2 collective-permute-start.37
  146.9 1.1 collective-permute-start.31
  148.0 1.0 collective-permute-start.28
  149.0 2.5 %collective-permute-done.37 = bf16[288,256]{1,0:T(8,128)(2,1)S(1)} collective-permute-done((bf16[288,256]{1,0:T(8,128)(2,1)S(1)}, bf16[288,256]{1,0:T(8,128)(2,1)S(1)}, u32[]{:S(2)}, u32[]{:S(2)}) %collective-permute-start.37) | collective-permute-done | bytes 147488 | tf_op jit(solution)/shard_map/ppermute | solution.py:363
  151.5 1.2 collective-permute-start.38
  152.7 2.0 %collective-permute-done.34 = bf16[288,256]{1,0:T(8,128)(2,1)S(1)} collective-permute-done((bf16[288,256]{1,0:T(8,128)(2,1)S(1)}, bf16[288,256]{1,0:T(8,128)(2,1)S(1)}, u32[]{:S(2)}, u32[]{:S(2)}) %collective-permute-start.34) | collective-permute-done | bytes 147488 | tf_op jit(solution)/shard_map/ppermute | solution.py:363
  154.7 1.2 collective-permute-start.35
  155.9 1.0 collective-permute-start.32
  156.9 1.3 collective-permute-start.29
  158.2 1.1 collective-permute-start.39
  159.3 2.2 %collective-permute-done.35 = bf16[288,256]{1,0:T(8,128)(2,1)S(1)} collective-permute-done((bf16[288,256]{1,0:T(8,128)(2,1)S(1)}, bf16[288,256]{1,0:T(8,128)(2,1)S(1)}, u32[]{:S(2)}, u32[]{:S(2)}) %collective-permute-start.35) | collective-permute-done | bytes 147488 | tf_op jit(solution)/shard_map/ppermute | solution.py:363
  161.5 1.2 collective-permute-start.36
  162.7 1.0 collective-permute-start.33
  164.3 1.0 collective-permute-start.30
  165.3 3.2 %token_sum.1 = bf16[128,2048]{1,0:T(8,128)(2,1)} custom-call(s32[3]{0:T(128)} %pad_add_fusion.scal, bf16[128,128]{1,0:T(8,128)(2,1)} %get-tuple-element.188.meta, bf16[64,2048]{1,0:T(8,128)(2,1)} %get-tuple-element.189.refs_0_, bf16[64,2048]{1,0:T(8,128)(2,1)} %copy-done.12, bf16[64,2048]{1,0:T(8,128)(2,1)} %copy-done.14, bf16[64,2048]{1,0:T(8,128)(2,1)} %copy-done.15, ...), custom_call_target="tpu_custom_call" | custom-call | flops 268435456 | bytes 2097152 | tf_op jit(solution)/shard_map/token_sum/pallas_call | solution.py:186
  168.6 1.7 collective-permute-done.30
  171.3 1.6 collective-permute-done.40.theirs
  172.9 2.4 %shadow_gradient.1 = f32[288,1024]{1,0:T(8,128)} custom-call(s32[3]{0:T(128)S(1)} %copy-done.1, bf16[288,512]{1,0:T(8,128)(2,1)S(1)} %pad_maximum_fusion.mine, bf16[288,512]{1,0:T(8,128)(2,1)S(1)} %collective-permute-done.40.theirs, bf16[512,2048]{1,0:T(8,128)(2,1)S(1)} %copy-done, bf16[512,2048]{1,0:T(8,128)(2,1)S(1)} %collective-permute-done.41.hot_theirs), custom_call_target="tpu_custom_call" | custom-call | flops 603979776 | bytes 2097152 | tf_op jit(solution)/shard_map/shadow_gradient/pallas_call | solution.py:336
  (130 shorter events, 9.6 us)
Async XLA Ops:
  0.6 17.8 %collective-permute-start.2 = (bf16[128,2048]{1,0:T(8,128)(2,1)}, bf16[128,2048]{1,0:T(8,128)(2,1)S(1)}, u32[]{:S(2)}, u32[]{:S(2)}) collective-permute-start(bf16[128,2048]{1,0:T(8,128)(2,1)} %refs_1_.1), channel_id=1, source_target_pairs={{0,4},{4,8},{8,12},{12,14},{14,10},{10,6},{6,2},{2,0},{1,5},{5,9},... | collective-permute-start | bytes 1572872 | tf_op jit(solution)/shard_map/ppermute | solution.py:363
  3.7 15.2 %collective-permute-start.3 = (bf16[128,2048]{1,0:T(8,128)(2,1)}, bf16[128,2048]{1,0:T(8,128)(2,1)}, u32[]{:S(2)}, u32[]{:S(2)}) collective-permute-start(bf16[128,2048]{1,0:T(8,128)(2,1)} %refs_1_.1), channel_id=1, source_target_pairs={{0,2},{4,0},{8,4},{12,8},{14,12},{10,14},{6,10},{2,6},{1,3},{5,1},... | collective-permute-start | bytes 1572872 | tf_op jit(solution)/shard_map/ppermute | solution.py:363
  5.7 22.8 %collective-permute-start = (bf16[128,2176]{1,0:T(8,128)(2,1)}, bf16[128,2176]{1,0:T(8,128)(2,1)S(1)}, u32[]{:S(2)}, u32[]{:S(2)}) collective-permute-start(bf16[128,2176]{1,0:T(8,128)(2,1)} %get-tuple-element.105.refs_0_), channel_id=1, source_target_pairs={{0,4},{4,8},{8,12},{12,14},{14,10},{10,6},{6,2},{2,0},{1,5},{5,9},... | collective-permute-start | bytes 1671176 | tf_op jit(solution)/shard_map/ppermute | solution.py:363
  7.7 23.1 %collective-permute-start.1 = (bf16[128,2176]{1,0:T(8,128)(2,1)}, bf16[128,2176]{1,0:T(8,128)(2,1)}, u32[]{:S(2)}, u32[]{:S(2)}) collective-permute-start(bf16[128,2176]{1,0:T(8,128)(2,1)} %get-tuple-element.105.refs_0_), channel_id=1, source_target_pairs={{0,2},{4,0},{8,4},{12,8},{14,12},{10,14},{6,10},{2,6},{1,3},{5,1},... | collective-permute-start | bytes 1671176 | tf_op jit(solution)/shard_map/ppermute | solution.py:363
  18.9 21.8 %collective-permute-start.6 = (bf16[128,2048]{1,0:T(8,128)(2,1)S(1)}, bf16[128,2048]{1,0:T(8,128)(2,1)}, u32[]{:S(2)}, u32[]{:S(2)}) collective-permute-start(bf16[128,2048]{1,0:T(8,128)(2,1)S(1)} %collective-permute-done.2.refs_2_), channel_id=1, source_target_pairs={{0,4},{4,8},{8,12},{12,14},{14,10},{10,6},{6,2},{2,0},{1,5},{5,9},... | collective-permute-start | bytes 1572872 | tf_op jit(solution)/shard_map/ppermute | solution.py:363
  20.5 23.1 %collective-permute-start.8 = (bf16[64,4352]{1,0:T(8,128)(2,1)}, bf16[64,4352]{1,0:T(8,128)(2,1)S(1)}, u32[]{:S(2)}, u32[]{:S(2)}) collective-permute-start(bf16[64,4352]{1,0:T(8,128)(2,1)} %get-tuple-element.114.refs_2_.refs_20_), channel_id=1, source_target_pairs={{0,1},{1,0},{2,3},{3,2},{4,5},{5,4},{6,7},{7,6},{8,9},{9,8},{10,11... | collective-permute-start | bytes 1671176 | tf_op jit(solution)/shard_map/ppermute | solution.py:366
  20.5 21.5 %collective-permute-start.7 = (bf16[128,2048]{1,0:T(8,128)(2,1)}, bf16[128,2048]{1,0:T(8,128)(2,1)}, u32[]{:S(2)}, u32[]{:S(2)}) collective-permute-start(bf16[128,2048]{1,0:T(8,128)(2,1)} %collective-permute-done.3.refs_3_), channel_id=1, source_target_pairs={{0,2},{4,0},{8,4},{12,8},{14,12},{10,14},{6,10},{2,6},{1,3},{5,1},... | collective-permute-start | bytes 1572872 | tf_op jit(solution)/shard_map/ppermute | solution.py:363
  28.6 23.2 %collective-permute-start.4 = (bf16[128,2176]{1,0:T(8,128)(2,1)S(1)}, bf16[128,2176]{1,0:T(8,128)(2,1)S(1)}, u32[]{:S(2)}, u32[]{:S(2)}) collective-permute-start(bf16[128,2176]{1,0:T(8,128)(2,1)S(1)} %collective-permute-done.refs_0_), channel_id=1, source_target_pairs={{0,4},{4,8},{8,12},{12,14},{14,10},{10,6},{6,2},{2,0},{1,5},{5,9},... | collective-permute-start | bytes 1671176 | tf_op jit(solution)/shard_map/ppermute | solution.py:363
  30.8 23.1 %collective-permute-start.5 = (bf16[128,2176]{1,0:T(8,128)(2,1)}, bf16[128,2176]{1,0:T(8,128)(2,1)S(1)}, u32[]{:S(2)}, u32[]{:S(2)}) collective-permute-start(bf16[128,2176]{1,0:T(8,128)(2,1)} %collective-permute-done.1.refs_1_), channel_id=1, source_target_pairs={{0,2},{4,0},{8,4},{12,8},{14,12},{10,14},{6,10},{2,6},{1,3},{5,1},... | collective-permute-start | bytes 1671176 | tf_op jit(solution)/shard_map/ppermute | solution.py:363
  40.7 26.3 %collective-permute-start.13 = (bf16[128,4352]{1,0:T(8,128)(2,1)}, bf16[128,4352]{1,0:T(8,128)(2,1)S(1)}, u32[]{:S(2)}, u32[]{:S(2)}) collective-permute-start(bf16[128,4352]{1,0:T(8,128)(2,1)} %get-tuple-element.124.refs_21_), channel_id=1, source_target_pairs={{0,1},{1,0},{2,3},{3,2},{4,5},{5,4},{6,7},{7,6},{8,9},{9,8},{10,11... | collective-permute-start | bytes 3342344 | tf_op jit(solution)/shard_map/ppermute | solution.py:366
  42.0 23.7 %collective-permute-start.11 = (bf16[128,2048]{1,0:T(8,128)(2,1)}, bf16[128,2048]{1,0:T(8,128)(2,1)}, u32[]{:S(2)}, u32[]{:S(2)}) collective-permute-start(bf16[128,2048]{1,0:T(8,128)(2,1)} %collective-permute-done.6.refs_2_), channel_id=1, source_target_pairs={{0,4},{4,8},{8,12},{12,14},{14,10},{10,6},{6,2},{2,0},{1,5},{5,9},... | collective-permute-start | bytes 1572872 | tf_op jit(solution)/shard_map/ppermute | solution.py:363
  43.6 22.2 %copy-start.7 = (bf16[2304,128]{1,0:T(8,128)(2,1)S(1)}, bf16[2304,128]{1,0:T(8,128)(2,1)}, u32[]{:S(2)}) copy-start(bf16[2304,128]{1,0:T(8,128)(2,1)} %get-tuple-element.109) | copy-start | bytes 1769476
  43.6 22.1 %copy-start.5 = (bf16[64,4352]{1,0:T(8,128)(2,1)}, bf16[64,4352]{1,0:T(8,128)(2,1)S(1)}, u32[]{:S(2)}) copy-start(bf16[64,4352]{1,0:T(8,128)(2,1)S(1)} %collective-permute-done.8.refs_5_.refs_15_.refs_25_) | copy-start | bytes 1671172
  43.6 23.2 %collective-permute-start.12 = (bf16[128,2048]{1,0:T(8,128)(2,1)}, bf16[128,2048]{1,0:T(8,128)(2,1)}, u32[]{:S(2)}, u32[]{:S(2)}) collective-permute-start(bf16[128,2048]{1,0:T(8,128)(2,1)} %collective-permute-done.7.refs_3_), channel_id=1, source_target_pairs={{0,2},{4,0},{8,4},{12,8},{14,12},{10,14},{6,10},{2,6},{1,3},{5,1},... | collective-permute-start | bytes 1572872 | tf_op jit(solution)/shard_map/ppermute | solution.py:363
  53.9 21.0 %collective-permute-start.9 = (bf16[128,2176]{1,0:T(8,128)(2,1)S(1)}, bf16[128,2176]{1,0:T(8,128)(2,1)S(1)}, u32[]{:S(2)}, u32[]{:S(2)}) collective-permute-start(bf16[128,2176]{1,0:T(8,128)(2,1)S(1)} %collective-permute-done.4.refs_0_), channel_id=1, source_target_pairs={{0,4},{4,8},{8,12},{12,14},{14,10},{10,6},{6,2},{2,0},{1,5},{5,9},... | collective-permute-start | bytes 1671176 | tf_op jit(solution)/shard_map/ppermute | solution.py:363
  55.5 21.7 %collective-permute-start.10 = (bf16[128,2176]{1,0:T(8,128)(2,1)S(1)}, bf16[128,2176]{1,0:T(8,128)(2,1)}, u32[]{:S(2)}, u32[]{:S(2)}) collective-permute-start(bf16[128,2176]{1,0:T(8,128)(2,1)S(1)} %collective-permute-done.5.refs_1_), channel_id=1, source_target_pairs={{0,2},{4,0},{8,4},{12,8},{14,12},{10,14},{6,10},{2,6},{1,3},{5,1},... | collective-permute-start | bytes 1671176 | tf_op jit(solution)/shard_map/ppermute | solution.py:363
  65.7 31.3 %collective-permute-start.18 = (bf16[128,4352]{1,0:T(8,128)(2,1)}, bf16[128,4352]{1,0:T(8,128)(2,1)S(1)}, u32[]{:S(2)}, u32[]{:S(2)}) collective-permute-start(bf16[128,4352]{1,0:T(8,128)(2,1)} %get-tuple-element.142.refs_22_), channel_id=1, source_target_pairs={{0,1},{1,0},{2,3},{3,2},{4,5},{5,4},{6,7},{7,6},{8,9},{9,8},{10,11... | collective-permute-start | bytes 3342344 | tf_op jit(solution)/shard_map/ppermute | solution.py:366
  66.9 15.8 %collective-permute-start.14 = (bf16[64,2048]{1,0:T(8,128)(2,1)S(1)}, bf16[64,2048]{1,0:T(8,128)(2,1)S(1)}, u32[]{:S(2)}, u32[]{:S(2)}) collective-permute-start(bf16[64,2048]{1,0:T(8,128)(2,1)S(1)} %copy-done.26), channel_id=1, source_target_pairs={{0,2},{4,0},{8,4},{12,8},{14,12},{10,14},{6,10},{2,6},{1,3},{5,1},... | collective-permute-start | bytes 786440 | tf_op jit(solution)/shard_map/ppermute | solution.py:363
  66.9 27.1 %copy-start.2 = (bf16[128,4352]{1,0:T(8,128)(2,1)}, bf16[128,4352]{1,0:T(8,128)(2,1)S(1)}, u32[]{:S(2)}) copy-start(bf16[128,4352]{1,0:T(8,128)(2,1)S(1)} %collective-permute-done.13.refs_6_.refs_16_.refs_26_) | copy-start | bytes 3342340
  66.9 17.1 %collective-permute-start.15 = (bf16[64,2048]{1,0:T(8,128)(2,1)S(1)}, bf16[64,2048]{1,0:T(8,128)(2,1)S(1)}, u32[]{:S(2)}, u32[]{:S(2)}) collective-permute-start(bf16[64,2048]{1,0:T(8,128)(2,1)S(1)} %copy-done.25), channel_id=1, source_target_pairs={{0,4},{4,8},{8,12},{12,14},{14,10},{10,6},{6,2},{2,0},{1,5},{5,9},... | collective-permute-start | bytes 786440 | tf_op jit(solution)/shard_map/ppermute | solution.py:363
  74.9 20.5 %collective-permute-start.17 = (bf16[128,2048]{1,0:T(8,128)(2,1)}, bf16[128,2048]{1,0:T(8,128)(2,1)}, u32[]{:S(2)}, u32[]{:S(2)}) collective-permute-start(bf16[128,2048]{1,0:T(8,128)(2,1)} %collective-permute-done.12.refs_3_), channel_id=1, source_target_pairs={{0,2},{4,0},{8,4},{12,8},{14,12},{10,14},{6,10},{2,6},{1,3},{5,1},... | collective-permute-start | bytes 1572872 | tf_op jit(solution)/shard_map/ppermute | solution.py:363
  77.2 26.4 %collective-permute-start.16 = (bf16[128,2176]{1,0:T(8,128)(2,1)S(1)}, bf16[128,2176]{1,0:T(8,128)(2,1)S(1)}, u32[]{:S(2)}, u32[]{:S(2)}) collective-permute-start(bf16[128,2176]{1,0:T(8,128)(2,1)S(1)} %collective-permute-done.9.refs_0_), channel_id=1, source_target_pairs={{0,4},{4,8},{8,12},{12,14},{14,10},{10,6},{6,2},{2,0},{1,5},{5,9},... | collective-permute-start | bytes 1671176 | tf_op jit(solution)/shard_map/ppermute | solution.py:363
  82.7 36.1 %collective-permute-start.19 = (bf16[64,2048]{1,0:T(8,128)(2,1)}, bf16[64,2048]{1,0:T(8,128)(2,1)S(1)}, u32[]{:S(2)}, u32[]{:S(2)}) collective-permute-start(bf16[64,2048]{1,0:T(8,128)(2,1)} %get-tuple-element.146), channel_id=1, source_target_pairs={{0,6},{4,2},{8,0},{12,4},{14,8},{10,12},{6,14},{2,10},{1,7},{5,3},... | collective-permute-start | bytes 786440 | tf_op jit(solution)/shard_map/ppermute | solution.py:363
  94.1 28.2 %collective-permute-start.21 = (bf16[128,4352]{1,0:T(8,128)(2,1)}, bf16[128,4352]{1,0:T(8,128)(2,1)S(1)}, u32[]{:S(2)}, u32[]{:S(2)}) collective-permute-start(bf16[128,4352]{1,0:T(8,128)(2,1)} %get-tuple-element.157.refs_23_), channel_id=1, source_target_pairs={{0,1},{1,0},{2,3},{3,2},{4,5},{5,4},{6,7},{7,6},{8,9},{9,8},{10,11... | collective-permute-start | bytes 3342344 | tf_op jit(solution)/shard_map/ppermute | solution.py:366
  95.4 23.4 %collective-permute-start.20 = (bf16[64,2048]{1,0:T(8,128)(2,1)S(1)}, bf16[64,2048]{1,0:T(8,128)(2,1)S(1)}, u32[]{:S(2)}, u32[]{:S(2)}) collective-permute-start(bf16[64,2048]{1,0:T(8,128)(2,1)S(1)} %copy-done.28), channel_id=1, source_target_pairs={{0,8},{4,12},{8,14},{12,10},{14,6},{10,2},{6,0},{2,4},{1,9},{5,13}... | collective-permute-start | bytes 786440 | tf_op jit(solution)/shard_map/ppermute | solution.py:363
  97.0 17.2 %copy-start.3 = (bf16[128,4352]{1,0:T(8,128)(2,1)}, bf16[128,4352]{1,0:T(8,128)(2,1)S(1)}, u32[]{:S(2)}) copy-start(bf16[128,4352]{1,0:T(8,128)(2,1)S(1)} %collective-permute-done.18.refs_7_.refs_17_.refs_27_) | copy-start | bytes 3342340
  97.0 47.6 %collective-permute-start.25 = (bf16[64,2048]{1,0:T(8,128)(2,1)S(1)}, bf16[64,2048]{1,0:T(8,128)(2,1)S(1)}, u32[]{:S(2)}, u32[]{:S(2)}) collective-permute-start(bf16[64,2048]{1,0:T(8,128)(2,1)S(1)} %copy-done.27), channel_id=1, source_target_pairs={{0,12},{4,14},{8,10},{12,6},{14,2},{10,0},{6,4},{2,8},{1,13},{5,15... | collective-permute-start | bytes 786440 | tf_op jit(solution)/shard_map/ppermute | solution.py:363
  103.6 41.2 %collective-permute-start.26 = (bf16[64,2048]{1,0:T(8,128)(2,1)}, bf16[64,2048]{1,0:T(8,128)(2,1)S(1)}, u32[]{:S(2)}, u32[]{:S(2)}) collective-permute-start(bf16[64,2048]{1,0:T(8,128)(2,1)} %get-tuple-element.171), channel_id=1, source_target_pairs={{0,10},{4,6},{8,2},{12,0},{14,4},{10,8},{6,12},{2,14},{1,11},{5,7}... | collective-permute-start | bytes 786440 | tf_op jit(solution)/shard_map/ppermute | solution.py:363
  118.8 25.9 %collective-permute-start.27 = (bf16[64,2048]{1,0:T(8,128)(2,1)}, bf16[64,2048]{1,0:T(8,128)(2,1)}, u32[]{:S(2)}, u32[]{:S(2)}) collective-permute-start(bf16[64,2048]{1,0:T(8,128)(2,1)} %get-tuple-element.173), channel_id=1, source_target_pairs={{0,14},{4,10},{8,6},{12,2},{14,0},{10,4},{6,8},{2,12},{1,15},{5,11... | collective-permute-start | bytes 786440 | tf_op jit(solution)/shard_map/ppermute | solution.py:363
  121.3 9.5 %collective-permute-start.24 = (bf16[64,4352]{1,0:T(8,128)(2,1)S(1)}, bf16[64,4352]{1,0:T(8,128)(2,1)S(1)}, u32[]{:S(2)}, u32[]{:S(2)}) collective-permute-start(bf16[64,4352]{1,0:T(8,128)(2,1)S(1)} %copy-done.10), channel_id=1, source_target_pairs={{0,1},{1,0},{2,3},{3,2},{4,5},{5,4},{6,7},{7,6},{8,9},{9,8},{10,11... | collective-permute-start | bytes 1671176 | tf_op jit(solution)/shard_map/ppermute | solution.py:366
  122.3 22.5 %collective-permute-start.22 = (bf16[288,256]{1,0:T(8,128)(2,1)S(1)}, bf16[288,256]{1,0:T(8,128)(2,1)S(1)}, u32[]{:S(2)}, u32[]{:S(2)}) collective-permute-start(bf16[288,256]{1,0:T(8,128)(2,1)S(1)} %get-tuple-element.158), channel_id=1, source_target_pairs={{0,4},{4,8},{8,12},{12,14},{14,10},{10,6},{6,2},{2,0},{1,5},{5,9},... | collective-permute-start | bytes 442376 | tf_op jit(solution)/shard_map/ppermute | solution.py:363
  130.8 13.9 %collective-permute-start.23 = (bf16[288,256]{1,0:T(8,128)(2,1)S(1)}, bf16[288,256]{1,0:T(8,128)(2,1)S(1)}, u32[]{:S(2)}, u32[]{:S(2)}) collective-permute-start(bf16[288,256]{1,0:T(8,128)(2,1)S(1)} %get-tuple-element.159), channel_id=1, source_target_pairs={{0,2},{4,0},{8,4},{12,8},{14,12},{10,14},{6,10},{2,6},{1,3},{5,1},... | collective-permute-start | bytes 442376 | tf_op jit(solution)/shard_map/ppermute | solution.py:363
  133.5 12.5 %copy-start.17 = (bf16[288,256]{1,0:T(8,128)(2,1)S(1)}, bf16[288,256]{1,0:T(8,128)(2,1)}, u32[]{:S(2)}) copy-start(bf16[288,256]{1,0:T(8,128)(2,1)} %get-tuple-element.183) | copy-start | bytes 442372
  133.5 13.5 %copy-start.18 = (bf16[288,256]{1,0:T(8,128)(2,1)S(1)}, bf16[288,256]{1,0:T(8,128)(2,1)}, u32[]{:S(2)}) copy-start(bf16[288,256]{1,0:T(8,128)(2,1)} %get-tuple-element.180) | copy-start | bytes 442372
  144.6 28.3 %collective-permute-start.41 = (bf16[512,2048]{1,0:T(8,128)(2,1)}, bf16[512,2048]{1,0:T(8,128)(2,1)S(1)}, u32[]{:S(2)}, u32[]{:S(2)}) collective-permute-start(bf16[512,2048]{1,0:T(8,128)(2,1)} %get-tuple-element.206), channel_id=1, source_target_pairs={{0,1},{1,0},{2,3},{3,2},{4,5},{5,4},{6,7},{7,6},{8,9},{9,8},{10,11... | collective-permute-start | bytes 6291464 | tf_op jit(solution)/shard_map/ppermute | solution.py:366
  144.8 6.7 %collective-permute-start.37 = (bf16[288,256]{1,0:T(8,128)(2,1)S(1)}, bf16[288,256]{1,0:T(8,128)(2,1)S(1)}, u32[]{:S(2)}, u32[]{:S(2)}) collective-permute-start(bf16[288,256]{1,0:T(8,128)(2,1)S(1)} %broadcast_select_fusion.2), channel_id=1, source_target_pairs={{0,2},{4,0},{8,4},{12,8},{14,12},{10,14},{6,10},{2,6},{1,3},{5,1},... | collective-permute-start | bytes 442376 | tf_op jit(solution)/shard_map/ppermute | solution.py:363
  146.0 8.7 %collective-permute-start.34 = (bf16[288,256]{1,0:T(8,128)(2,1)S(1)}, bf16[288,256]{1,0:T(8,128)(2,1)S(1)}, u32[]{:S(2)}, u32[]{:S(2)}) collective-permute-start(bf16[288,256]{1,0:T(8,128)(2,1)S(1)} %copy-done.17), channel_id=1, source_target_pairs={{0,2},{4,0},{8,4},{12,8},{14,12},{10,14},{6,10},{2,6},{1,3},{5,1},... | collective-permute-start | bytes 442376 | tf_op jit(solution)/shard_map/ppermute | solution.py:363
  146.9 8.9 %collective-permute-start.31 = (bf16[288,256]{1,0:T(8,128)(2,1)S(1)}, bf16[288,256]{1,0:T(8,128)(2,1)S(1)}, u32[]{:S(2)}, u32[]{:S(2)}) collective-permute-start(bf16[288,256]{1,0:T(8,128)(2,1)S(1)} %copy-done.18), channel_id=1, source_target_pairs={{0,4},{4,8},{8,12},{12,14},{14,10},{10,6},{6,2},{2,0},{1,5},{5,9},... | collective-permute-start | bytes 442376 | tf_op jit(solution)/shard_map/ppermute | solution.py:363
  148.0 8.8 %collective-permute-start.28 = (bf16[288,256]{1,0:T(8,128)(2,1)S(1)}, bf16[288,256]{1,0:T(8,128)(2,1)S(1)}, u32[]{:S(2)}, u32[]{:S(2)}) collective-permute-start(bf16[288,256]{1,0:T(8,128)(2,1)S(1)} %broadcast_select_fusion.9), channel_id=1, source_target_pairs={{0,4},{4,8},{8,12},{12,14},{14,10},{10,6},{6,2},{2,0},{1,5},{5,9},... | collective-permute-start | bytes 442376 | tf_op jit(solution)/shard_map/ppermute | solution.py:363
  151.5 6.6 %collective-permute-start.38 = (bf16[288,256]{1,0:T(8,128)(2,1)S(1)}, bf16[288,256]{1,0:T(8,128)(2,1)S(1)}, u32[]{:S(2)}, u32[]{:S(2)}) collective-permute-start(bf16[288,256]{1,0:T(8,128)(2,1)S(1)} %broadcast_select_fusion.1), channel_id=1, source_target_pairs={{0,2},{4,0},{8,4},{12,8},{14,12},{10,14},{6,10},{2,6},{1,3},{5,1},... | collective-permute-start | bytes 442376 | tf_op jit(solution)/shard_map/ppermute | solution.py:363
  154.7 6.8 %collective-permute-start.35 = (bf16[288,256]{1,0:T(8,128)(2,1)S(1)}, bf16[288,256]{1,0:T(8,128)(2,1)S(1)}, u32[]{:S(2)}, u32[]{:S(2)}) collective-permute-start(bf16[288,256]{1,0:T(8,128)(2,1)S(1)} %broadcast_select_fusion.4), channel_id=1, source_target_pairs={{0,2},{4,0},{8,4},{12,8},{14,12},{10,14},{6,10},{2,6},{1,3},{5,1},... | collective-permute-start | bytes 442376 | tf_op jit(solution)/shard_map/ppermute | solution.py:363
  155.9 6.8 %collective-permute-start.32 = (bf16[288,256]{1,0:T(8,128)(2,1)S(1)}, bf16[288,256]{1,0:T(8,128)(2,1)S(1)}, u32[]{:S(2)}, u32[]{:S(2)}) collective-permute-start(bf16[288,256]{1,0:T(8,128)(2,1)S(1)} %broadcast_select_fusion.6), channel_id=1, source_target_pairs={{0,4},{4,8},{8,12},{12,14},{14,10},{10,6},{6,2},{2,0},{1,5},{5,9},... | collective-permute-start | bytes 442376 | tf_op jit(solution)/shard_map/ppermute | solution.py:363
  156.9 7.4 %collective-permute-start.29 = (bf16[288,256]{1,0:T(8,128)(2,1)S(1)}, bf16[288,256]{1,0:T(8,128)(2,1)S(1)}, u32[]{:S(2)}, u32[]{:S(2)}) collective-permute-start(bf16[288,256]{1,0:T(8,128)(2,1)S(1)} %broadcast_select_fusion.8), channel_id=1, source_target_pairs={{0,4},{4,8},{8,12},{12,14},{14,10},{10,6},{6,2},{2,0},{1,5},{5,9},... | collective-permute-start | bytes 442376 | tf_op jit(solution)/shard_map/ppermute | solution.py:363
  158.2 10.3 %collective-permute-start.39 = (bf16[288,256]{1,0:T(8,128)(2,1)S(1)}, bf16[288,256]{1,0:T(8,128)(2,1)S(1)}, u32[]{:S(2)}, u32[]{:S(2)}) collective-permute-start(bf16[288,256]{1,0:T(8,128)(2,1)S(1)} %broadcast_select_fusion), channel_id=1, source_target_pairs={{0,2},{4,0},{8,4},{12,8},{14,12},{10,14},{6,10},{2,6},{1,3},{5,1},... | collective-permute-start | bytes 442376 | tf_op jit(solution)/shard_map/ppermute | solution.py:363
  161.5 6.9 %collective-permute-start.36 = (bf16[288,256]{1,0:T(8,128)(2,1)S(1)}, bf16[288,256]{1,0:T(8,128)(2,1)S(1)}, u32[]{:S(2)}, u32[]{:S(2)}) collective-permute-start(bf16[288,256]{1,0:T(8,128)(2,1)S(1)} %broadcast_select_fusion.3), channel_id=1, source_target_pairs={{0,2},{4,0},{8,4},{12,8},{14,12},{10,14},{6,10},{2,6},{1,3},{5,1},... | collective-permute-start | bytes 442376 | tf_op jit(solution)/shard_map/ppermute | solution.py:363
  162.7 5.8 %collective-permute-start.33 = (bf16[288,256]{1,0:T(8,128)(2,1)S(1)}, bf16[288,256]{1,0:T(8,128)(2,1)S(1)}, u32[]{:S(2)}, u32[]{:S(2)}) collective-permute-start(bf16[288,256]{1,0:T(8,128)(2,1)S(1)} %broadcast_select_fusion.5), channel_id=1, source_target_pairs={{0,4},{4,8},{8,12},{12,14},{14,10},{10,6},{6,2},{2,0},{1,5},{5,9},... | collective-permute-start | bytes 442376 | tf_op jit(solution)/shard_map/ppermute | solution.py:363
  164.3 5.9 %collective-permute-start.30 = (bf16[288,256]{1,0:T(8,128)(2,1)S(1)}, bf16[288,256]{1,0:T(8,128)(2,1)}, u32[]{:S(2)}, u32[]{:S(2)}) collective-permute-start(bf16[288,256]{1,0:T(8,128)(2,1)S(1)} %broadcast_select_fusion.7), channel_id=1, source_target_pairs={{0,4},{4,8},{8,12},{12,14},{14,10},{10,6},{6,2},{2,0},{1,5},{5,9},... | collective-permute-start | bytes 442376 | tf_op jit(solution)/shard_map/ppermute | solution.py:363
  171.3 1.6 collective-permute-start.40
  (23 other events, 130.9 us)

commit v15 on v13

--- a/solution.py
+++ b/solution.py
@@ -392,7 +392,10 @@
         following[1], back = lax.optimization_barrier((following[1], back))
         if number + 1 < half:
             up, below = [[part[k] for part in following] for k in range(2)]
-        sent = [shift(part, step) if step else part for step, part in zip(steps, back)]
+        if number < half:
+            sent = [shift(part, step) if step else part for step, part in zip(steps, back)]
+        else:
+            sent = back
         late.append((sent, swap(pack)))
         mine.append(rows)
         packs.append(pack)
@@ -421,13 +424,14 @@
         return [columns[:, :lanes], columns[:, lanes:]]
 
     far = halves(half)
-    far, other = lax.optimization_barrier((far, other))
+    (back_far,) = late[half][0]
+    far, other, back_far = lax.optimization_barrier((far, other, back_far))
+    back_far = shift(back_far, half)
     hot_theirs = swap(hot_theirs)
     far = [shift(far[0], 1), shift(far[1], -1)]
     others = [part for _, part in late[: half - 1]] + [other, late[half][1]]
     expert_grad = expert_gradient(units, scal, mine, packs, others)
     chunks = {distance: halves(distance) for distance in range(1 - half, half)}
-    (back_far,) = late[half][0]
     far, expert_grad, back_ahead, back_behind, back_far, chunks = lax.optimization_barrier(
         (far, expert_grad, back_ahead, back_behind, back_far, chunks)
     )

time: 175 us -> 172 us (0.983)
  starting transfers between devices: 55.6 us -> 53.8 us
    ppermute x35, starting transfers between devices: 55.2 us -> 53.4 us  [shift(): return lax.ppermute(block, 'expert', pairs)]
  transfers between devices with their start and end apart: 42 -> 42, of which waited for: 16 -> 15; matrix products, arithmetic and copies ran while one was open for 2% -> 3% of each run, Pallas kernels for 40% -> 40%
where the time goes in v15:
time: 172 us
  Pallas kernels  71.6 us (42%)
  starting transfers between devices  53.8 us (31%)
  waiting for transfers between devices  38 us (22%)
  other arithmetic  3.38 us (2%)
  local copies, waits for them, and re-layouts  3.23 us (2%)
  between operations  1.97 us (1%)
    ppermute x35, starting transfers between devices, shift(): return lax.ppermute(block, 'expert', pairs)  53.4 us
    pallas_call x5, Pallas kernels, run_step(): pl.pallas_call(functools.partial(step_kernel, steps, fanout, capacity, jo...  48.6 us
    ppermute x35, waiting for transfers between devices, shift(): return lax.ppermute(block, 'expert', pairs)  36.4 us
    pallas_call x1, Pallas kernels, expert_gradient(): pl.pallas_call(functools.partial(gradient_kernel, units, count), grid=(ti...  10.8 us
    pallas_call x1, Pallas kernels, ordered(): pl.pallas_call(functools.partial(order_kernel, plan, experts, capacity),...  4.64 us
  transfers between devices with their start and end apart: 42, of which 15 were waited for; matrix products, arithmetic and copies ran while one was open for 3% of the time, Pallas kernels for 40%

profile of v15, /device:TPU:0, one launch (start us, length us, event | category | flops | bytes accessed | tf_op | source)
XLA Modules:
  0.0 172.0 jit_solution(3466999805043257729)
XLA Ops:
  0.6 3.1 %collective-permute-start.2 = (bf16[128,2048]{1,0:T(8,128)(2,1)}, bf16[128,2048]{1,0:T(8,128)(2,1)S(1)}, u32[]{:S(2)}, u32[]{:S(2)}) collective-permute-start(bf16[128,2048]{1,0:T(8,128)(2,1)} %refs_1_.1), channel_id=1, source_target_pairs={{0,4},{4,8},{8,12},{12,14},{14,10},{10,6},{6,2},{2,0},{1,5},{5,9},... | collective-permute-start | bytes 1572872 | tf_op jit(solution)/shard_map/ppermute | solution.py:356
  3.7 2.0 %ring_message.1 = (bf16[128,2176]{1,0:T(8,128)(2,1)}, bf16[128,128]{1,0:T(8,128)(2,1)}) custom-call(bf16[128,2048]{1,0:T(8,128)(2,1)} %tokens.1, s32[2,128]{1,0:T(2,128)} %bitcast.17, f32[2,128]{1,0:T(2,128)} %bitcast.18, f32[1,128]{1,0:T(1,128)} %bitcast.19, s32[1,128]{1,0:T(1,128)} %bitcast.20), custom_call_target="tpu_custom_call" | custom-call | bytes 1048576 | tf_op jit(solution)/shard_map/ring_message/pallas_call | solution.py:262
  5.7 2.0 %collective-permute-start = (bf16[128,2176]{1,0:T(8,128)(2,1)}, bf16[128,2176]{1,0:T(8,128)(2,1)S(1)}, u32[]{:S(2)}, u32[]{:S(2)}) collective-permute-start(bf16[128,2176]{1,0:T(8,128)(2,1)} %get-tuple-element.106.refs_0_), channel_id=1, source_target_pairs={{0,4},{4,8},{8,12},{12,14},{14,10},{10,6},{6,2},{2,0},{1,5},{5,9},... | collective-permute-start | bytes 1671176 | tf_op jit(solution)/shard_map/ppermute | solution.py:356
  9.0 9.4 %expert_step.5 = (bf16[64,2048]{1,0:T(8,128)(2,1)}, bf16[64,4352]{1,0:T(8,128)(2,1)}, bf16[64,4096]{1,0:T(8,128)(2,1)}, bf16[64,2048]{1,0:T(8,128)(2,1)}) custom-call(s32[3]{0:T(128)} %pad_add_fusion.scal, bf16[128,2176]{1,0:T(8,128)(2,1)} %get-tuple-element.106.refs_0_, bf16[128,2048]{1,0:T(8,128)(2,1)} %refs_1_.1, bf16[2048,1536]{1,0:T(8,128)(2,1)} %bitcast.21, ...), custom_call_target="tpu_custom_call" | custom-call | flops 4026531840 | bytes 9437184 | tf_op jit(solution)/shard_map/expert_step/pallas_call | solution.py:151
  18.9 1.6 collective-permute-start.6
  20.9 7.7 %collective-permute-done.refs_0_ = bf16[128,2176]{1,0:T(8,128)(2,1)S(1)} collective-permute-done((bf16[128,2176]{1,0:T(8,128)(2,1)}, bf16[128,2176]{1,0:T(8,128)(2,1)S(1)}, u32[]{:S(2)}, u32[]{:S(2)}) %collective-permute-start) | collective-permute-done | bytes 557088 | tf_op jit(solution)/shard_map/ppermute | solution.py:356
  28.6 2.1 %collective-permute-start.4 = (bf16[128,2176]{1,0:T(8,128)(2,1)S(1)}, bf16[128,2176]{1,0:T(8,128)(2,1)S(1)}, u32[]{:S(2)}, u32[]{:S(2)}) collective-permute-start(bf16[128,2176]{1,0:T(8,128)(2,1)S(1)} %collective-permute-done.refs_0_), channel_id=1, source_target_pairs={{0,4},{4,8},{8,12},{12,14},{14,10},{10,6},{6,2},{2,0},{1,5},{5,9},... | collective-permute-start | bytes 1671176 | tf_op jit(solution)/shard_map/ppermute | solution.py:356
  30.8 9.8 %expert_step.6 = (bf16[128,2048]{1,0:T(8,128)(2,1)}, bf16[128,4352]{1,0:T(8,128)(2,1)}, bf16[128,4096]{1,0:T(8,128)(2,1)}, bf16[64,2048]{1,0:T(8,128)(2,1)}, bf1...) custom-call(s32[3]{0:T(128)} %pad_add_fusion.scal, bf16[128,2176]{1,0:T(8,128)(2,1)} %copy-done.22, ...), custom_call_target="tpu_custom_call" | custom-call | flops 4026531840 | bytes 9437184 | tf_op jit(solution)/shard_map/expert_step/pallas_call | solution.py:151
  40.7 1.3 collective-permute-done.7.refs_3_
  42.0 1.6 collective-permute-start.11
  44.1 7.6 %collective-permute-done.4.refs_0_ = bf16[128,2176]{1,0:T(8,128)(2,1)S(1)} collective-permute-done((bf16[128,2176]{1,0:T(8,128)(2,1)S(1)}, bf16[128,2176]{1,0:T(8,128)(2,1)S(1)}, u32[]{:S(2)}, u32[]{:S(2)}) %collective-permute-start.4) | collective-permute-done | bytes 557088 | tf_op jit(solution)/shard_map/ppermute | solution.py:356
  51.7 2.1 %collective-permute-done.5.refs_1_ = bf16[128,2176]{1,0:T(8,128)(2,1)S(1)} collective-permute-done((bf16[128,2176]{1,0:T(8,128)(2,1)}, bf16[128,2176]{1,0:T(8,128)(2,1)S(1)}, u32[]{:S(2)}, u32[]{:S(2)}) %collective-permute-start.5) | collective-permute-done | bytes 557088 | tf_op jit(solution)/shard_map/ppermute | solution.py:356
  53.9 1.6 collective-permute-start.9
  55.9 9.8 %expert_step.7 = (bf16[128,2048]{1,0:T(8,128)(2,1)}, bf16[128,4352]{1,0:T(8,128)(2,1)}, bf16[128,4096]{1,0:T(8,128)(2,1)}, bf16[64,2048]{1,0:T(8,128)(2,1)}, bf1...) custom-call(s32[3]{0:T(128)} %pad_add_fusion.scal, bf16[128,2176]{1,0:T(8,128)(2,1)} %copy-done.20, ...), custom_call_target="tpu_custom_call" | custom-call | flops 4026531840 | bytes 9437184 | tf_op jit(solution)/shard_map/expert_step/pallas_call | solution.py:151
  65.9 0.9 copy-done.9
  66.9 2.0 %collective-permute-start.15 = (bf16[64,2048]{1,0:T(8,128)(2,1)S(1)}, bf16[64,2048]{1,0:T(8,128)(2,1)S(1)}, u32[]{:S(2)}, u32[]{:S(2)}) collective-permute-start(bf16[64,2048]{1,0:T(8,128)(2,1)S(1)} %copy-done.26), channel_id=1, source_target_pairs={{0,4},{4,8},{8,12},{12,14},{14,10},{10,6},{6,2},{2,0},{1,5},{5,9},... | collective-permute-start | bytes 786440 | tf_op jit(solution)/shard_map/ppermute | solution.py:356
  69.1 5.8 %collective-permute-done.9.refs_0_ = bf16[128,2176]{1,0:T(8,128)(2,1)S(1)} collective-permute-done((bf16[128,2176]{1,0:T(8,128)(2,1)S(1)}, bf16[128,2176]{1,0:T(8,128)(2,1)S(1)}, u32[]{:S(2)}, u32[]{:S(2)}) %collective-permute-start.9) | collective-permute-done | bytes 557088 | tf_op jit(solution)/shard_map/ppermute | solution.py:356
  74.9 2.1 %collective-permute-start.17 = (bf16[128,2048]{1,0:T(8,128)(2,1)}, bf16[128,2048]{1,0:T(8,128)(2,1)}, u32[]{:S(2)}, u32[]{:S(2)}) collective-permute-start(bf16[128,2048]{1,0:T(8,128)(2,1)} %collective-permute-done.12.refs_3_), channel_id=1, source_target_pairs={{0,2},{4,0},{8,4},{12,8},{14,12},{10,14},{6,10},{2,6},{1,3},{5,1},... | collective-permute-start | bytes 1572872 | tf_op jit(solution)/shard_map/ppermute | solution.py:356
  77.2 1.6 collective-permute-start.16
  78.7 0.7 pad_maximum_fusion.3
  79.4 3.2 %collective-permute-done.14.refs_7_ = bf16[64,2048]{1,0:T(8,128)(2,1)S(1)} collective-permute-done((bf16[64,2048]{1,0:T(8,128)(2,1)S(1)}, bf16[64,2048]{1,0:T(8,128)(2,1)S(1)}, u32[]{:S(2)}, u32[]{:S(2)}) %collective-permute-start.14) | collective-permute-done | bytes 262176 | tf_op jit(solution)/shard_map/ppermute | solution.py:356
  82.7 1.4 collective-permute-start.19
  84.1 9.9 %expert_step.8 = (bf16[128,2048]{1,0:T(8,128)(2,1)}, bf16[128,4352]{1,0:T(8,128)(2,1)}, bf16[128,4096]{1,0:T(8,128)(2,1)}, bf16[64,2048]{1,0:T(8,128)(2,1)}, bf1...) custom-call(s32[3]{0:T(128)} %pad_add_fusion.scal, bf16[128,2176]{1,0:T(8,128)(2,1)} %copy-done.23, ...), custom_call_target="tpu_custom_call" | custom-call | flops 4026531840 | bytes 9437184 | tf_op jit(solution)/shard_map/expert_step/pallas_call | solution.py:151
  94.2 1.2 constant_dynamic-slice_fusion.1
  95.4 1.6 collective-permute-start.20
  97.0 6.6 %collective-permute-start.25 = (bf16[64,2048]{1,0:T(8,128)(2,1)S(1)}, bf16[64,2048]{1,0:T(8,128)(2,1)S(1)}, u32[]{:S(2)}, u32[]{:S(2)}) collective-permute-start(bf16[64,2048]{1,0:T(8,128)(2,1)S(1)} %copy-done.28), channel_id=1, source_target_pairs={{0,12},{4,14},{8,10},{12,6},{14,2},{10,0},{6,4},{2,8},{1,13},{5,15... | collective-permute-start | bytes 786440 | tf_op jit(solution)/shard_map/ppermute | solution.py:356
  103.6 0.8 copy-done.24
  104.4 9.7 %expert_step.9 = (bf16[64,2048]{1,0:T(8,128)(2,1)}, bf16[64,4352]{1,0:T(8,128)(2,1)}, bf16[64,4096]{1,0:T(8,128)(2,1)}, bf16[64,2048]{1,0:T(8,128)(2,1)}, bf16[2304,128]{1,0:T(8,128)(2,1)}) custom-call(s32[3]{0:T(128)} %pad_add_fusion.scal, bf16[128,2176]{1,0:T(8,128)(2,1)} %copy-done.24, bf16[128,2048]{1,0:T(8,128)(2,1)} %collective-permute-done.17.refs_1_, ...), custom_call_target="tpu_custom_call" | custom-call | flops 4026531840 | bytes 9437184 | tf_op jit(solution)/shard_map/expert_step/pallas_call | solution.py:151
  114.2 4.6 %hot_rows_ordered.1 = (bf16[512,2048]{1,0:T(8,128)(2,1)}, bf16[512,2048]{1,0:T(8,128)(2,1)}) custom-call(s32[3]{0:T(128)} %pad_add_fusion.scal, bf16[64,4096]{1,0:T(8,128)(2,1)} %get-tuple-element.150.refs_0_, bf16[128,4096]{1,0:T(8,128)(2,1)} %get-tuple-element.151.refs_1_, bf16[128,4096]{1,0:T(8,128)(2,1)} %get-tuple-element.152.refs_2_, ...), custom_call_target="tpu_custom_call" | custom-call | bytes 8388608 | tf_op jit(solution)/shard_map/hot_rows_ordered/pallas_call | solution.py:290
  119.9 2.5 %collective-permute-start.27 = (bf16[64,2048]{1,0:T(8,128)(2,1)}, bf16[64,2048]{1,0:T(8,128)(2,1)S(1)}, u32[]{:S(2)}, u32[]{:S(2)}) collective-permute-start(bf16[64,2048]{1,0:T(8,128)(2,1)} %get-tuple-element.175), channel_id=1, source_target_pairs={{0,14},{4,10},{8,6},{12,2},{14,0},{10,4},{6,8},{2,12},{1,15},{5,11... | collective-permute-start | bytes 786440 | tf_op jit(solution)/shard_map/ppermute | solution.py:356
  122.4 2.8 %collective-permute-start.22 = (bf16[288,256]{1,0:T(8,128)(2,1)S(1)}, bf16[288,256]{1,0:T(8,128)(2,1)S(1)}, u32[]{:S(2)}, u32[]{:S(2)}) collective-permute-start(bf16[288,256]{1,0:T(8,128)(2,1)S(1)} %get-tuple-element.161), channel_id=1, source_target_pairs={{0,4},{4,8},{8,12},{12,14},{14,10},{10,6},{6,2},{2,0},{1,5},{5,9},... | collective-permute-start | bytes 442376 | tf_op jit(solution)/shard_map/ppermute | solution.py:356
  125.2 1.8 %collective-permute-start.23 = (bf16[288,256]{1,0:T(8,128)(2,1)S(1)}, bf16[288,256]{1,0:T(8,128)(2,1)S(1)}, u32[]{:S(2)}, u32[]{:S(2)}) collective-permute-start(bf16[288,256]{1,0:T(8,128)(2,1)S(1)} %get-tuple-element.162), channel_id=1, source_target_pairs={{0,2},{4,0},{8,4},{12,8},{14,12},{10,14},{6,10},{2,6},{1,3},{5,1},... | collective-permute-start | bytes 442376 | tf_op jit(solution)/shard_map/ppermute | solution.py:356
  127.0 10.8 %expert_gradient.1 = f32[1,1024,2304]{2,1,0:T(8,128)} custom-call(s32[3]{0:T(128)} %pad_add_fusion.scal, bf16[64,2048]{1,0:T(8,128)(2,1)} %get-tuple-element.163.refs_0_.refs_10_, bf16[128,2048]{1,0:T(8,128)(2,1)} %get-tuple-element.164.refs_1_.refs_11_, bf16[128,2048]{1,0:T(8,128)(2,1)} %get-tuple-element.165.refs_2_.refs_12_, ...), custom_call_target="tpu_custom_call" | custom-call | flops 4831838208 | bytes 14155776 | tf_op jit(solution)/shard_map/expert_gradient/pallas_call | solution.py:226
  138.0 2.0 %collective-permute-start.37 = (bf16[288,256]{1,0:T(8,128)(2,1)S(1)}, bf16[288,256]{1,0:T(8,128)(2,1)S(1)}, u32[]{:S(2)}, u32[]{:S(2)}) collective-permute-start(bf16[288,256]{1,0:T(8,128)(2,1)S(1)} %broadcast_select_fusion.2), channel_id=1, source_target_pairs={{0,2},{4,0},{8,4},{12,8},{14,12},{10,14},{6,10},{2,6},{1,3},{5,1},... | collective-permute-start | bytes 442376 | tf_op jit(solution)/shard_map/ppermute | solution.py:356
  140.1 4.1 %collective-permute-start.34 = (bf16[288,256]{1,0:T(8,128)(2,1)S(1)}, bf16[288,256]{1,0:T(8,128)(2,1)S(1)}, u32[]{:S(2)}, u32[]{:S(2)}) collective-permute-start(bf16[288,256]{1,0:T(8,128)(2,1)S(1)} %copy-done.18), channel_id=1, source_target_pairs={{0,2},{4,0},{8,4},{12,8},{14,12},{10,14},{6,10},{2,6},{1,3},{5,1},... | collective-permute-start | bytes 442376 | tf_op jit(solution)/shard_map/ppermute | solution.py:356
  144.4 1.9 %collective-permute-done.37 = bf16[288,256]{1,0:T(8,128)(2,1)S(1)} collective-permute-done((bf16[288,256]{1,0:T(8,128)(2,1)S(1)}, bf16[288,256]{1,0:T(8,128)(2,1)S(1)}, u32[]{:S(2)}, u32[]{:S(2)}) %collective-permute-start.37) | collective-permute-done | bytes 147488 | tf_op jit(solution)/shard_map/ppermute | solution.py:356
  146.3 2.2 %collective-permute-start.38 = (bf16[288,256]{1,0:T(8,128)(2,1)S(1)}, bf16[288,256]{1,0:T(8,128)(2,1)S(1)}, u32[]{:S(2)}, u32[]{:S(2)}) collective-permute-start(bf16[288,256]{1,0:T(8,128)(2,1)S(1)} %broadcast_select_fusion.1), channel_id=1, source_target_pairs={{0,2},{4,0},{8,4},{12,8},{14,12},{10,14},{6,10},{2,6},{1,3},{5,1},... | collective-permute-start | bytes 442376 | tf_op jit(solution)/shard_map/ppermute | solution.py:356
  149.1 2.7 %collective-permute-start.35 = (bf16[288,256]{1,0:T(8,128)(2,1)S(1)}, bf16[288,256]{1,0:T(8,128)(2,1)S(1)}, u32[]{:S(2)}, u32[]{:S(2)}) collective-permute-start(bf16[288,256]{1,0:T(8,128)(2,1)S(1)} %broadcast_select_fusion.4), channel_id=1, source_target_pairs={{0,2},{4,0},{8,4},{12,8},{14,12},{10,14},{6,10},{2,6},{1,3},{5,1},... | collective-permute-start | bytes 442376 | tf_op jit(solution)/shard_map/ppermute | solution.py:356
  152.2 2.1 %collective-permute-start.29 = (bf16[288,256]{1,0:T(8,128)(2,1)S(1)}, bf16[288,256]{1,0:T(8,128)(2,1)S(1)}, u32[]{:S(2)}, u32[]{:S(2)}) collective-permute-start(bf16[288,256]{1,0:T(8,128)(2,1)S(1)} %broadcast_select_fusion.8), channel_id=1, source_target_pairs={{0,4},{4,8},{8,12},{12,14},{14,10},{10,6},{6,2},{2,0},{1,5},{5,9},... | collective-permute-start | bytes 442376 | tf_op jit(solution)/shard_map/ppermute | solution.py:356
  154.3 0.9 collective-permute-start.39
  155.2 0.8 collective-permute-done.35
  156.0 2.6 %collective-permute-start.36 = (bf16[288,256]{1,0:T(8,128)(2,1)S(1)}, bf16[288,256]{1,0:T(8,128)(2,1)S(1)}, u32[]{:S(2)}, u32[]{:S(2)}) collective-permute-start(bf16[288,256]{1,0:T(8,128)(2,1)S(1)} %broadcast_select_fusion.3), channel_id=1, source_target_pairs={{0,2},{4,0},{8,4},{12,8},{14,12},{10,14},{6,10},{2,6},{1,3},{5,1},... | collective-permute-start | bytes 442376 | tf_op jit(solution)/shard_map/ppermute | solution.py:356
  159.0 2.3 %collective-permute-done.29 = bf16[288,256]{1,0:T(8,128)(2,1)S(1)} collective-permute-done((bf16[288,256]{1,0:T(8,128)(2,1)S(1)}, bf16[288,256]{1,0:T(8,128)(2,1)S(1)}, u32[]{:S(2)}, u32[]{:S(2)}) %collective-permute-start.29) | collective-permute-done | bytes 147488 | tf_op jit(solution)/shard_map/ppermute | solution.py:356
  161.5 3.2 %token_sum.1 = bf16[128,2048]{1,0:T(8,128)(2,1)} custom-call(s32[3]{0:T(128)} %pad_add_fusion.scal, bf16[128,128]{1,0:T(8,128)(2,1)} %get-tuple-element.190.meta, bf16[64,2048]{1,0:T(8,128)(2,1)} %get-tuple-element.191.refs_0_, bf16[64,2048]{1,0:T(8,128)(2,1)} %copy-done.12, bf16[64,2048]{1,0:T(8,128)(2,1)} %copy-done.14, bf16[64,2048]{1,0:T(8,128)(2,1)} %copy-done.15, ...), custom_call_target="tpu_custom_call" | custom-call | flops 268435456 | bytes 2097152 | tf_op jit(solution)/shard_map/token_sum/pallas_call | solution.py:186
  164.7 2.3 %collective-permute-done.30 = bf16[288,256]{1,0:T(8,128)(2,1)} collective-permute-done((bf16[288,256]{1,0:T(8,128)(2,1)S(1)}, bf16[288,256]{1,0:T(8,128)(2,1)}, u32[]{:S(2)}, u32[]{:S(2)}) %collective-permute-start.30) | collective-permute-done | bytes 147488 | tf_op jit(solution)/shard_map/ppermute | solution.py:356
  167.0 0.9 select_select_fusion.1
  168.1 1.6 collective-permute-done.40.theirs
  169.7 2.4 %shadow_gradient.1 = f32[288,1024]{1,0:T(8,128)} custom-call(s32[3]{0:T(128)S(1)} %copy-done.1, bf16[288,512]{1,0:T(8,128)(2,1)S(1)} %pad_maximum_fusion.mine, bf16[288,512]{1,0:T(8,128)(2,1)S(1)} %collective-permute-done.40.theirs, bf16[512,2048]{1,0:T(8,128)(2,1)S(1)} %copy-done, bf16[512,2048]{1,0:T(8,128)(2,1)S(1)} %collective-permute-done.41.hot_theirs), custom_call_target="tpu_custom_call" | custom-call | flops 603979776 | bytes 2097152 | tf_op jit(solution)/shard_map/shadow_gradient/pallas_call | solution.py:329
  (132 shorter events, 6.2 us)
Async XLA Ops:
  0.6 17.8 %collective-permute-start.2 = (bf16[128,2048]{1,0:T(8,128)(2,1)}, bf16[128,2048]{1,0:T(8,128)(2,1)S(1)}, u32[]{:S(2)}, u32[]{:S(2)}) collective-permute-start(bf16[128,2048]{1,0:T(8,128)(2,1)} %refs_1_.1), channel_id=1, source_target_pairs={{0,4},{4,8},{8,12},{12,14},{14,10},{10,6},{6,2},{2,0},{1,5},{5,9},... | collective-permute-start | bytes 1572872 | tf_op jit(solution)/shard_map/ppermute | solution.py:356
  3.7 15.2 %collective-permute-start.3 = (bf16[128,2048]{1,0:T(8,128)(2,1)}, bf16[128,2048]{1,0:T(8,128)(2,1)}, u32[]{:S(2)}, u32[]{:S(2)}) collective-permute-start(bf16[128,2048]{1,0:T(8,128)(2,1)} %refs_1_.1), channel_id=1, source_target_pairs={{0,2},{4,0},{8,4},{12,8},{14,12},{10,14},{6,10},{2,6},{1,3},{5,1},... | collective-permute-start | bytes 1572872 | tf_op jit(solution)/shard_map/ppermute | solution.py:356
  5.7 22.8 %collective-permute-start = (bf16[128,2176]{1,0:T(8,128)(2,1)}, bf16[128,2176]{1,0:T(8,128)(2,1)S(1)}, u32[]{:S(2)}, u32[]{:S(2)}) collective-permute-start(bf16[128,2176]{1,0:T(8,128)(2,1)} %get-tuple-element.106.refs_0_), channel_id=1, source_target_pairs={{0,4},{4,8},{8,12},{12,14},{14,10},{10,6},{6,2},{2,0},{1,5},{5,9},... | collective-permute-start | bytes 1671176 | tf_op jit(solution)/shard_map/ppermute | solution.py:356
  7.7 23.1 %collective-permute-start.1 = (bf16[128,2176]{1,0:T(8,128)(2,1)}, bf16[128,2176]{1,0:T(8,128)(2,1)}, u32[]{:S(2)}, u32[]{:S(2)}) collective-permute-start(bf16[128,2176]{1,0:T(8,128)(2,1)} %get-tuple-element.106.refs_0_), channel_id=1, source_target_pairs={{0,2},{4,0},{8,4},{12,8},{14,12},{10,14},{6,10},{2,6},{1,3},{5,1},... | collective-permute-start | bytes 1671176 | tf_op jit(solution)/shard_map/ppermute | solution.py:356
  18.9 21.8 %collective-permute-start.6 = (bf16[128,2048]{1,0:T(8,128)(2,1)S(1)}, bf16[128,2048]{1,0:T(8,128)(2,1)}, u32[]{:S(2)}, u32[]{:S(2)}) collective-permute-start(bf16[128,2048]{1,0:T(8,128)(2,1)S(1)} %collective-permute-done.2.refs_2_), channel_id=1, source_target_pairs={{0,4},{4,8},{8,12},{12,14},{14,10},{10,6},{6,2},{2,0},{1,5},{5,9},... | collective-permute-start | bytes 1572872 | tf_op jit(solution)/shard_map/ppermute | solution.py:356
  20.5 23.1 %collective-permute-start.8 = (bf16[64,4352]{1,0:T(8,128)(2,1)}, bf16[64,4352]{1,0:T(8,128)(2,1)S(1)}, u32[]{:S(2)}, u32[]{:S(2)}) collective-permute-start(bf16[64,4352]{1,0:T(8,128)(2,1)} %get-tuple-element.115.refs_2_.refs_20_), channel_id=1, source_target_pairs={{0,1},{1,0},{2,3},{3,2},{4,5},{5,4},{6,7},{7,6},{8,9},{9,8},{10,11... | collective-permute-start | bytes 1671176 | tf_op jit(solution)/shard_map/ppermute | solution.py:359
  20.5 21.6 %collective-permute-start.7 = (bf16[128,2048]{1,0:T(8,128)(2,1)}, bf16[128,2048]{1,0:T(8,128)(2,1)}, u32[]{:S(2)}, u32[]{:S(2)}) collective-permute-start(bf16[128,2048]{1,0:T(8,128)(2,1)} %collective-permute-done.3.refs_3_), channel_id=1, source_target_pairs={{0,2},{4,0},{8,4},{12,8},{14,12},{10,14},{6,10},{2,6},{1,3},{5,1},... | collective-permute-start | bytes 1572872 | tf_op jit(solution)/shard_map/ppermute | solution.py:356
  28.6 23.2 %collective-permute-start.4 = (bf16[128,2176]{1,0:T(8,128)(2,1)S(1)}, bf16[128,2176]{1,0:T(8,128)(2,1)S(1)}, u32[]{:S(2)}, u32[]{:S(2)}) collective-permute-start(bf16[128,2176]{1,0:T(8,128)(2,1)S(1)} %collective-permute-done.refs_0_), channel_id=1, source_target_pairs={{0,4},{4,8},{8,12},{12,14},{14,10},{10,6},{6,2},{2,0},{1,5},{5,9},... | collective-permute-start | bytes 1671176 | tf_op jit(solution)/shard_map/ppermute | solution.py:356
  30.8 23.1 %collective-permute-start.5 = (bf16[128,2176]{1,0:T(8,128)(2,1)}, bf16[128,2176]{1,0:T(8,128)(2,1)S(1)}, u32[]{:S(2)}, u32[]{:S(2)}) collective-permute-start(bf16[128,2176]{1,0:T(8,128)(2,1)} %collective-permute-done.1.refs_1_), channel_id=1, source_target_pairs={{0,2},{4,0},{8,4},{12,8},{14,12},{10,14},{6,10},{2,6},{1,3},{5,1},... | collective-permute-start | bytes 1671176 | tf_op jit(solution)/shard_map/ppermute | solution.py:356
  40.7 26.3 %collective-permute-start.13 = (bf16[128,4352]{1,0:T(8,128)(2,1)}, bf16[128,4352]{1,0:T(8,128)(2,1)S(1)}, u32[]{:S(2)}, u32[]{:S(2)}) collective-permute-start(bf16[128,4352]{1,0:T(8,128)(2,1)} %get-tuple-element.125.refs_21_), channel_id=1, source_target_pairs={{0,1},{1,0},{2,3},{3,2},{4,5},{5,4},{6,7},{7,6},{8,9},{9,8},{10,11... | collective-permute-start | bytes 3342344 | tf_op jit(solution)/shard_map/ppermute | solution.py:359
  42.0 23.7 %collective-permute-start.11 = (bf16[128,2048]{1,0:T(8,128)(2,1)}, bf16[128,2048]{1,0:T(8,128)(2,1)}, u32[]{:S(2)}, u32[]{:S(2)}) collective-permute-start(bf16[128,2048]{1,0:T(8,128)(2,1)} %collective-permute-done.6.refs_2_), channel_id=1, source_target_pairs={{0,4},{4,8},{8,12},{12,14},{14,10},{10,6},{6,2},{2,0},{1,5},{5,9},... | collective-permute-start | bytes 1572872 | tf_op jit(solution)/shard_map/ppermute | solution.py:356
  43.6 22.2 %copy-start.7 = (bf16[2304,128]{1,0:T(8,128)(2,1)S(1)}, bf16[2304,128]{1,0:T(8,128)(2,1)}, u32[]{:S(2)}) copy-start(bf16[2304,128]{1,0:T(8,128)(2,1)} %get-tuple-element.110) | copy-start | bytes 1769476
  43.6 22.1 %copy-start.5 = (bf16[64,4352]{1,0:T(8,128)(2,1)}, bf16[64,4352]{1,0:T(8,128)(2,1)S(1)}, u32[]{:S(2)}) copy-start(bf16[64,4352]{1,0:T(8,128)(2,1)S(1)} %collective-permute-done.8.refs_5_.refs_15_.refs_25_) | copy-start | bytes 1671172
  43.6 23.2 %collective-permute-start.12 = (bf16[128,2048]{1,0:T(8,128)(2,1)}, bf16[128,2048]{1,0:T(8,128)(2,1)}, u32[]{:S(2)}, u32[]{:S(2)}) collective-permute-start(bf16[128,2048]{1,0:T(8,128)(2,1)} %collective-permute-done.7.refs_3_), channel_id=1, source_target_pairs={{0,2},{4,0},{8,4},{12,8},{14,12},{10,14},{6,10},{2,6},{1,3},{5,1},... | collective-permute-start | bytes 1572872 | tf_op jit(solution)/shard_map/ppermute | solution.py:356
  53.9 21.0 %collective-permute-start.9 = (bf16[128,2176]{1,0:T(8,128)(2,1)S(1)}, bf16[128,2176]{1,0:T(8,128)(2,1)S(1)}, u32[]{:S(2)}, u32[]{:S(2)}) collective-permute-start(bf16[128,2176]{1,0:T(8,128)(2,1)S(1)} %collective-permute-done.4.refs_0_), channel_id=1, source_target_pairs={{0,4},{4,8},{8,12},{12,14},{14,10},{10,6},{6,2},{2,0},{1,5},{5,9},... | collective-permute-start | bytes 1671176 | tf_op jit(solution)/shard_map/ppermute | solution.py:356
  55.5 21.7 %collective-permute-start.10 = (bf16[128,2176]{1,0:T(8,128)(2,1)S(1)}, bf16[128,2176]{1,0:T(8,128)(2,1)}, u32[]{:S(2)}, u32[]{:S(2)}) collective-permute-start(bf16[128,2176]{1,0:T(8,128)(2,1)S(1)} %collective-permute-done.5.refs_1_), channel_id=1, source_target_pairs={{0,2},{4,0},{8,4},{12,8},{14,12},{10,14},{6,10},{2,6},{1,3},{5,1},... | collective-permute-start | bytes 1671176 | tf_op jit(solution)/shard_map/ppermute | solution.py:356
  65.7 31.3 %collective-permute-start.18 = (bf16[128,4352]{1,0:T(8,128)(2,1)}, bf16[128,4352]{1,0:T(8,128)(2,1)S(1)}, u32[]{:S(2)}, u32[]{:S(2)}) collective-permute-start(bf16[128,4352]{1,0:T(8,128)(2,1)} %get-tuple-element.143.refs_22_), channel_id=1, source_target_pairs={{0,1},{1,0},{2,3},{3,2},{4,5},{5,4},{6,7},{7,6},{8,9},{9,8},{10,11... | collective-permute-start | bytes 3342344 | tf_op jit(solution)/shard_map/ppermute | solution.py:359
  66.9 15.8 %collective-permute-start.14 = (bf16[64,2048]{1,0:T(8,128)(2,1)S(1)}, bf16[64,2048]{1,0:T(8,128)(2,1)S(1)}, u32[]{:S(2)}, u32[]{:S(2)}) collective-permute-start(bf16[64,2048]{1,0:T(8,128)(2,1)S(1)} %copy-done.27), channel_id=1, source_target_pairs={{0,2},{4,0},{8,4},{12,8},{14,12},{10,14},{6,10},{2,6},{1,3},{5,1},... | collective-permute-start | bytes 786440 | tf_op jit(solution)/shard_map/ppermute | solution.py:356
  66.9 27.1 %copy-start.2 = (bf16[128,4352]{1,0:T(8,128)(2,1)}, bf16[128,4352]{1,0:T(8,128)(2,1)S(1)}, u32[]{:S(2)}) copy-start(bf16[128,4352]{1,0:T(8,128)(2,1)S(1)} %collective-permute-done.13.refs_6_.refs_16_.refs_26_) | copy-start | bytes 3342340
  66.9 17.1 %collective-permute-start.15 = (bf16[64,2048]{1,0:T(8,128)(2,1)S(1)}, bf16[64,2048]{1,0:T(8,128)(2,1)S(1)}, u32[]{:S(2)}, u32[]{:S(2)}) collective-permute-start(bf16[64,2048]{1,0:T(8,128)(2,1)S(1)} %copy-done.26), channel_id=1, source_target_pairs={{0,4},{4,8},{8,12},{12,14},{14,10},{10,6},{6,2},{2,0},{1,5},{5,9},... | collective-permute-start | bytes 786440 | tf_op jit(solution)/shard_map/ppermute | solution.py:356
  74.9 20.5 %collective-permute-start.17 = (bf16[128,2048]{1,0:T(8,128)(2,1)}, bf16[128,2048]{1,0:T(8,128)(2,1)}, u32[]{:S(2)}, u32[]{:S(2)}) collective-permute-start(bf16[128,2048]{1,0:T(8,128)(2,1)} %collective-permute-done.12.refs_3_), channel_id=1, source_target_pairs={{0,2},{4,0},{8,4},{12,8},{14,12},{10,14},{6,10},{2,6},{1,3},{5,1},... | collective-permute-start | bytes 1572872 | tf_op jit(solution)/shard_map/ppermute | solution.py:356
  77.2 26.4 %collective-permute-start.16 = (bf16[128,2176]{1,0:T(8,128)(2,1)S(1)}, bf16[128,2176]{1,0:T(8,128)(2,1)S(1)}, u32[]{:S(2)}, u32[]{:S(2)}) collective-permute-start(bf16[128,2176]{1,0:T(8,128)(2,1)S(1)} %collective-permute-done.9.refs_0_), channel_id=1, source_target_pairs={{0,4},{4,8},{8,12},{12,14},{14,10},{10,6},{6,2},{2,0},{1,5},{5,9},... | collective-permute-start | bytes 1671176 | tf_op jit(solution)/shard_map/ppermute | solution.py:356
  82.7 36.1 %collective-permute-start.19 = (bf16[64,2048]{1,0:T(8,128)(2,1)}, bf16[64,2048]{1,0:T(8,128)(2,1)S(1)}, u32[]{:S(2)}, u32[]{:S(2)}) collective-permute-start(bf16[64,2048]{1,0:T(8,128)(2,1)} %get-tuple-element.147), channel_id=1, source_target_pairs={{0,6},{4,2},{8,0},{12,4},{14,8},{10,12},{6,14},{2,10},{1,7},{5,3},... | collective-permute-start | bytes 786440 | tf_op jit(solution)/shard_map/ppermute | solution.py:356
  94.1 25.8 %collective-permute-start.21 = (bf16[128,4352]{1,0:T(8,128)(2,1)}, bf16[128,4352]{1,0:T(8,128)(2,1)S(1)}, u32[]{:S(2)}, u32[]{:S(2)}) collective-permute-start(bf16[128,4352]{1,0:T(8,128)(2,1)} %get-tuple-element.158.refs_23_), channel_id=1, source_target_pairs={{0,1},{1,0},{2,3},{3,2},{4,5},{5,4},{6,7},{7,6},{8,9},{9,8},{10,11... | collective-permute-start | bytes 3342344 | tf_op jit(solution)/shard_map/ppermute | solution.py:359
  95.4 23.4 %collective-permute-start.20 = (bf16[64,2048]{1,0:T(8,128)(2,1)S(1)}, bf16[64,2048]{1,0:T(8,128)(2,1)S(1)}, u32[]{:S(2)}, u32[]{:S(2)}) collective-permute-start(bf16[64,2048]{1,0:T(8,128)(2,1)S(1)} %copy-done.29), channel_id=1, source_target_pairs={{0,8},{4,12},{8,14},{12,10},{14,6},{10,2},{6,0},{2,4},{1,9},{5,13}... | collective-permute-start | bytes 786440 | tf_op jit(solution)/shard_map/ppermute | solution.py:356
  97.0 17.1 %copy-start.3 = (bf16[128,4352]{1,0:T(8,128)(2,1)}, bf16[128,4352]{1,0:T(8,128)(2,1)S(1)}, u32[]{:S(2)}) copy-start(bf16[128,4352]{1,0:T(8,128)(2,1)S(1)} %collective-permute-done.18.refs_7_.refs_17_.refs_27_) | copy-start | bytes 3342340
  97.0 40.9 %collective-permute-start.25 = (bf16[64,2048]{1,0:T(8,128)(2,1)S(1)}, bf16[64,2048]{1,0:T(8,128)(2,1)S(1)}, u32[]{:S(2)}, u32[]{:S(2)}) collective-permute-start(bf16[64,2048]{1,0:T(8,128)(2,1)S(1)} %copy-done.28), channel_id=1, source_target_pairs={{0,12},{4,14},{8,10},{12,6},{14,2},{10,0},{6,4},{2,8},{1,13},{5,15... | collective-permute-start | bytes 786440 | tf_op jit(solution)/shard_map/ppermute | solution.py:356
  103.6 34.4 %collective-permute-start.26 = (bf16[64,2048]{1,0:T(8,128)(2,1)}, bf16[64,2048]{1,0:T(8,128)(2,1)S(1)}, u32[]{:S(2)}, u32[]{:S(2)}) collective-permute-start(bf16[64,2048]{1,0:T(8,128)(2,1)} %get-tuple-element.174), channel_id=1, source_target_pairs={{0,10},{4,6},{8,2},{12,0},{14,4},{10,8},{6,12},{2,14},{1,11},{5,7}... | collective-permute-start | bytes 786440 | tf_op jit(solution)/shard_map/ppermute | solution.py:356
  118.8 6.4 %collective-permute-start.24 = (bf16[64,4352]{1,0:T(8,128)(2,1)S(1)}, bf16[64,4352]{1,0:T(8,128)(2,1)S(1)}, u32[]{:S(2)}, u32[]{:S(2)}) collective-permute-start(bf16[64,4352]{1,0:T(8,128)(2,1)S(1)} %copy-done.10), channel_id=1, source_target_pairs={{0,1},{1,0},{2,3},{3,2},{4,5},{5,4},{6,7},{7,6},{8,9},{9,8},{10,11... | collective-permute-start | bytes 1671176 | tf_op jit(solution)/shard_map/ppermute | solution.py:359
  119.9 18.1 %collective-permute-start.27 = (bf16[64,2048]{1,0:T(8,128)(2,1)}, bf16[64,2048]{1,0:T(8,128)(2,1)S(1)}, u32[]{:S(2)}, u32[]{:S(2)}) collective-permute-start(bf16[64,2048]{1,0:T(8,128)(2,1)} %get-tuple-element.175), channel_id=1, source_target_pairs={{0,14},{4,10},{8,6},{12,2},{14,0},{10,4},{6,8},{2,12},{1,15},{5,11... | collective-permute-start | bytes 786440 | tf_op jit(solution)/shard_map/ppermute | solution.py:356
  122.4 15.6 %collective-permute-start.22 = (bf16[288,256]{1,0:T(8,128)(2,1)S(1)}, bf16[288,256]{1,0:T(8,128)(2,1)S(1)}, u32[]{:S(2)}, u32[]{:S(2)}) collective-permute-start(bf16[288,256]{1,0:T(8,128)(2,1)S(1)} %get-tuple-element.161), channel_id=1, source_target_pairs={{0,4},{4,8},{8,12},{12,14},{14,10},{10,6},{6,2},{2,0},{1,5},{5,9},... | collective-permute-start | bytes 442376 | tf_op jit(solution)/shard_map/ppermute | solution.py:356
  125.2 12.8 %collective-permute-start.23 = (bf16[288,256]{1,0:T(8,128)(2,1)S(1)}, bf16[288,256]{1,0:T(8,128)(2,1)S(1)}, u32[]{:S(2)}, u32[]{:S(2)}) collective-permute-start(bf16[288,256]{1,0:T(8,128)(2,1)S(1)} %get-tuple-element.162), channel_id=1, source_target_pairs={{0,2},{4,0},{8,4},{12,8},{14,12},{10,14},{6,10},{2,6},{1,3},{5,1},... | collective-permute-start | bytes 442376 | tf_op jit(solution)/shard_map/ppermute | solution.py:356
  127.0 17.2 %copy-start.19 = (bf16[288,256]{1,0:T(8,128)(2,1)S(1)}, bf16[288,256]{1,0:T(8,128)(2,1)}, u32[]{:S(2)}) copy-start(bf16[288,256]{1,0:T(8,128)(2,1)} %get-tuple-element.182) | copy-start | bytes 442372
  137.9 14.3 %copy-start.15 = (bf16[64,2048]{1,0:T(8,128)(2,1)}, bf16[64,2048]{1,0:T(8,128)(2,1)S(1)}, u32[]{:S(2)}) copy-start(bf16[64,2048]{1,0:T(8,128)(2,1)S(1)} %collective-permute-done.25.refs_3_) | copy-start | bytes 786436
  137.9 31.8 %collective-permute-start.41 = (bf16[512,2048]{1,0:T(8,128)(2,1)}, bf16[512,2048]{1,0:T(8,128)(2,1)S(1)}, u32[]{:S(2)}, u32[]{:S(2)}) collective-permute-start(bf16[512,2048]{1,0:T(8,128)(2,1)} %get-tuple-element.208), channel_id=1, source_target_pairs={{0,1},{1,0},{2,3},{3,2},{4,5},{5,4},{6,7},{7,6},{8,9},{9,8},{10,11... | collective-permute-start | bytes 6291464 | tf_op jit(solution)/shard_map/ppermute | solution.py:359
  138.0 8.3 %collective-permute-start.37 = (bf16[288,256]{1,0:T(8,128)(2,1)S(1)}, bf16[288,256]{1,0:T(8,128)(2,1)S(1)}, u32[]{:S(2)}, u32[]{:S(2)}) collective-permute-start(bf16[288,256]{1,0:T(8,128)(2,1)S(1)} %broadcast_select_fusion.2), channel_id=1, source_target_pairs={{0,2},{4,0},{8,4},{12,8},{14,12},{10,14},{6,10},{2,6},{1,3},{5,1},... | collective-permute-start | bytes 442376 | tf_op jit(solution)/shard_map/ppermute | solution.py:356
  140.1 9.0 %collective-permute-start.34 = (bf16[288,256]{1,0:T(8,128)(2,1)S(1)}, bf16[288,256]{1,0:T(8,128)(2,1)S(1)}, u32[]{:S(2)}, u32[]{:S(2)}) collective-permute-start(bf16[288,256]{1,0:T(8,128)(2,1)S(1)} %copy-done.18), channel_id=1, source_target_pairs={{0,2},{4,0},{8,4},{12,8},{14,12},{10,14},{6,10},{2,6},{1,3},{5,1},... | collective-permute-start | bytes 442376 | tf_op jit(solution)/shard_map/ppermute | solution.py:356
  144.2 7.5 %collective-permute-start.31 = (bf16[288,256]{1,0:T(8,128)(2,1)S(1)}, bf16[288,256]{1,0:T(8,128)(2,1)S(1)}, u32[]{:S(2)}, u32[]{:S(2)}) collective-permute-start(bf16[288,256]{1,0:T(8,128)(2,1)S(1)} %copy-done.19), channel_id=1, source_target_pairs={{0,4},{4,8},{8,12},{12,14},{14,10},{10,6},{6,2},{2,0},{1,5},{5,9},... | collective-permute-start | bytes 442376 | tf_op jit(solution)/shard_map/ppermute | solution.py:356
  144.2 7.9 %collective-permute-start.28 = (bf16[288,256]{1,0:T(8,128)(2,1)S(1)}, bf16[288,256]{1,0:T(8,128)(2,1)S(1)}, u32[]{:S(2)}, u32[]{:S(2)}) collective-permute-start(bf16[288,256]{1,0:T(8,128)(2,1)S(1)} %broadcast_select_fusion.9), channel_id=1, source_target_pairs={{0,4},{4,8},{8,12},{12,14},{14,10},{10,6},{6,2},{2,0},{1,5},{5,9},... | collective-permute-start | bytes 442376 | tf_op jit(solution)/shard_map/ppermute | solution.py:356
  146.3 8.0 %collective-permute-start.38 = (bf16[288,256]{1,0:T(8,128)(2,1)S(1)}, bf16[288,256]{1,0:T(8,128)(2,1)S(1)}, u32[]{:S(2)}, u32[]{:S(2)}) collective-permute-start(bf16[288,256]{1,0:T(8,128)(2,1)S(1)} %broadcast_select_fusion.1), channel_id=1, source_target_pairs={{0,2},{4,0},{8,4},{12,8},{14,12},{10,14},{6,10},{2,6},{1,3},{5,1},... | collective-permute-start | bytes 442376 | tf_op jit(solution)/shard_map/ppermute | solution.py:356
  149.1 6.9 %collective-permute-start.35 = (bf16[288,256]{1,0:T(8,128)(2,1)S(1)}, bf16[288,256]{1,0:T(8,128)(2,1)S(1)}, u32[]{:S(2)}, u32[]{:S(2)}) collective-permute-start(bf16[288,256]{1,0:T(8,128)(2,1)S(1)} %broadcast_select_fusion.4), channel_id=1, source_target_pairs={{0,2},{4,0},{8,4},{12,8},{14,12},{10,14},{6,10},{2,6},{1,3},{5,1},... | collective-permute-start | bytes 442376 | tf_op jit(solution)/shard_map/ppermute | solution.py:356
  151.8 6.8 %collective-permute-start.32 = (bf16[288,256]{1,0:T(8,128)(2,1)S(1)}, bf16[288,256]{1,0:T(8,128)(2,1)S(1)}, u32[]{:S(2)}, u32[]{:S(2)}) collective-permute-start(bf16[288,256]{1,0:T(8,128)(2,1)S(1)} %broadcast_select_fusion.6), channel_id=1, source_target_pairs={{0,4},{4,8},{8,12},{12,14},{14,10},{10,6},{6,2},{2,0},{1,5},{5,9},... | collective-permute-start | bytes 442376 | tf_op jit(solution)/shard_map/ppermute | solution.py:356
  152.2 9.2 %collective-permute-start.29 = (bf16[288,256]{1,0:T(8,128)(2,1)S(1)}, bf16[288,256]{1,0:T(8,128)(2,1)S(1)}, u32[]{:S(2)}, u32[]{:S(2)}) collective-permute-start(bf16[288,256]{1,0:T(8,128)(2,1)S(1)} %broadcast_select_fusion.8), channel_id=1, source_target_pairs={{0,4},{4,8},{8,12},{12,14},{14,10},{10,6},{6,2},{2,0},{1,5},{5,9},... | collective-permute-start | bytes 442376 | tf_op jit(solution)/shard_map/ppermute | solution.py:356
  154.3 10.4 %collective-permute-start.39 = (bf16[288,256]{1,0:T(8,128)(2,1)S(1)}, bf16[288,256]{1,0:T(8,128)(2,1)S(1)}, u32[]{:S(2)}, u32[]{:S(2)}) collective-permute-start(bf16[288,256]{1,0:T(8,128)(2,1)S(1)} %broadcast_select_fusion), channel_id=1, source_target_pairs={{0,2},{4,0},{8,4},{12,8},{14,12},{10,14},{6,10},{2,6},{1,3},{5,1},... | collective-permute-start | bytes 442376 | tf_op jit(solution)/shard_map/ppermute | solution.py:356
  156.0 8.7 %collective-permute-start.36 = (bf16[288,256]{1,0:T(8,128)(2,1)S(1)}, bf16[288,256]{1,0:T(8,128)(2,1)S(1)}, u32[]{:S(2)}, u32[]{:S(2)}) collective-permute-start(bf16[288,256]{1,0:T(8,128)(2,1)S(1)} %broadcast_select_fusion.3), channel_id=1, source_target_pairs={{0,2},{4,0},{8,4},{12,8},{14,12},{10,14},{6,10},{2,6},{1,3},{5,1},... | collective-permute-start | bytes 442376 | tf_op jit(solution)/shard_map/ppermute | solution.py:356
  158.6 6.1 %collective-permute-start.33 = (bf16[288,256]{1,0:T(8,128)(2,1)S(1)}, bf16[288,256]{1,0:T(8,128)(2,1)S(1)}, u32[]{:S(2)}, u32[]{:S(2)}) collective-permute-start(bf16[288,256]{1,0:T(8,128)(2,1)S(1)} %broadcast_select_fusion.5), channel_id=1, source_target_pairs={{0,4},{4,8},{8,12},{12,14},{14,10},{10,6},{6,2},{2,0},{1,5},{5,9},... | collective-permute-start | bytes 442376 | tf_op jit(solution)/shard_map/ppermute | solution.py:356
  161.4 5.6 %collective-permute-start.30 = (bf16[288,256]{1,0:T(8,128)(2,1)S(1)}, bf16[288,256]{1,0:T(8,128)(2,1)}, u32[]{:S(2)}, u32[]{:S(2)}) collective-permute-start(bf16[288,256]{1,0:T(8,128)(2,1)S(1)} %broadcast_select_fusion.7), channel_id=1, source_target_pairs={{0,4},{4,8},{8,12},{12,14},{14,10},{10,6},{6,2},{2,0},{1,5},{5,9},... | collective-permute-start | bytes 442376 | tf_op jit(solution)/shard_map/ppermute | solution.py:356
  168.0 1.6 collective-permute-start.40
  (24 other events, 134.5 us)
